TPU v7x, 32 devices: a whole 2x2x4 slice. The times are simulated.
32 devices in a mesh: row: 8 (over z, y), col: 4 (over x, core).
Axes of the slice: x: 2, y: 2, z: 4, core: 2. Of those that a mesh axis runs over, the one named last changes fastest.
Arguments:
- design: float32 [4096, 4096], P('row', 'col'), may hold values from -6 to 6
- sign_bits: int32 [4096], P('row'), may hold values from 0 to 1
- picks: int32 [8, 8, 16], P(None, 'row'), may hold values from 0 to 511
- counts: int32 [8, 8], P(None, 'row'), may hold values from 6 to 16, as said below
- target: float32 [4096], P('row'), may hold values from -6 to 6
- rinv: float32 [4096, 4096], P('col')
Outputs:
- sketch: float32 [1024, 4096], P('row', 'col')
- solution: float32 [4096], P('col')
- basis: float32 [4096], P('row')
Inputs may be any that keep to these rules, and one draw needn't show every extreme that they name: `counts`: some owner takes 16 rows from some block.
All inputs are finite; a program needn't handle non-finite values.
Results may differ from a plain program's by a relative error of at most 0.0003.
Values sent between devices are 32-bit elements; how exact they have to be, the bound alone decides.
No kernel may reach another device: no remote copies, remote signals or barrier semaphores. Data moves between devices by JAX's collectives and lax.ppermute only.
A program may use at most 64 MiB of HBM per device.

v0:
```python
import functools

import jax
import jax.numpy as jnp
import numpy as np
from jax import lax
from jax.experimental import pallas as pl
from jax.experimental.pallas import tpu as pltpu
from jax.sharding import PartitionSpec as P

HB = 256
PAIR = 16
ITERS = 2
LANE = 128
CHUNKS = 2
F32 = jnp.float32
VMEM = pl.BlockSpec(memory_space=pltpu.VMEM)


def swap(array, axis, mask):
    return lax.ppermute(array, axis, [(i, i ^ mask) for i in range(lax.axis_size(axis))])


def gathered(array, axis):
    return [array] + [swap(array, axis, mask) for mask in range(1, lax.axis_size(axis))]


def tree(values):
    while len(values) > 1:
        values = [values[i] + values[i + 1] for i in range(0, len(values), 2)]
    return values[0]


def walsh(size):
    index = np.arange(size)
    common = index[:, None] & index[None, :]
    parity = np.zeros((size, size), np.int64)
    for shift in range(size.bit_length()):
        parity ^= (common >> shift) & 1
    return (1 - 2 * parity).astype(np.float32)


def call(body, out_shape, *operands, megabytes=24, flops=0, size=0):
    return pl.pallas_call(
        body,
        out_shape=out_shape,
        in_specs=[VMEM] * len(operands),
        out_specs=jax.tree.map(lambda _: VMEM, out_shape),
        compiler_params=pltpu.CompilerParams(vmem_limit_bytes=megabytes << 20),
        cost_estimate=pl.CostEstimate(flops=flops, bytes_accessed=size, transcendentals=0),
    )(*operands)


def fold_rows(block):
    return block.reshape(block.shape[0] // 8, 8, LANE).sum(axis=0)


def total(rows):
    return jnp.sum(jnp.sum(rows, axis=0, keepdims=True), axis=1, keepdims=True)


def splat(scalar):
    return jnp.broadcast_to(scalar, (1, LANE))


def left_product(vector, matrix_ref, out_ref):
    blocks, tiles = matrix_ref.shape[0] // LANE, matrix_ref.shape[1] // LANE
    sums = [jnp.zeros((8, LANE), F32) for _ in range(tiles)]
    for block in range(blocks):
        across = jnp.broadcast_to(vector[block : block + 1, :], (LANE, LANE)).T
        for tile in range(tiles):
            part = matrix_ref[block * LANE : (block + 1) * LANE, tile * LANE : (tile + 1) * LANE]
            sums[tile] = sums[tile] + fold_rows(part * across)
    for tile in range(tiles):
        out_ref[tile : tile + 1, :] = jnp.sum(sums[tile], axis=0, keepdims=True)


def left_product_long(vector_ref, matrix_ref, out_ref):
    blocks, tiles = matrix_ref.shape[0] // LANE, matrix_ref.shape[1] // LANE

    def step(block, sums):
        across = jnp.broadcast_to(vector_ref[pl.ds(block, 1), :], (LANE, LANE)).T
        rows = pl.ds(pl.multiple_of(block * LANE, LANE), LANE)
        return tuple(
            sums[tile] + fold_rows(matrix_ref[rows, tile * LANE : (tile + 1) * LANE] * across)
            for tile in range(tiles)
        )

    sums = lax.fori_loop(0, blocks, step, tuple(jnp.zeros((8, LANE), F32) for _ in range(tiles)))
    for tile in range(tiles):
        out_ref[tile : tile + 1, :] = jnp.sum(sums[tile], axis=0, keepdims=True)


def right_product(matrix_ref, vector, out_ref):
    blocks, tiles = matrix_ref.shape[0] // LANE, matrix_ref.shape[1] // LANE

    def step(block, carry):
        rows = pl.ds(pl.multiple_of(block * LANE, LANE), LANE)
        sums = jnp.zeros((LANE, LANE), F32)
        for tile in range(tiles):
            sums = sums + matrix_ref[rows, tile * LANE : (tile + 1) * LANE] * vector[tile : tile + 1, :]
        out_ref[pl.ds(block, 1), :] = jnp.sum(fold_rows(sums.T), axis=0, keepdims=True)
        return carry

    lax.fori_loop(0, blocks, step, 0)


def pack_width(width):
    return -(-(width // LANE + 1) // 8) * 8


def first_body(design_ref, target_ref, out_ref):
    tiles = design_ref.shape[1] // LANE
    target = target_ref[...]
    out_ref[...] = jnp.zeros_like(out_ref)
    left_product(target, design_ref, out_ref)
    out_ref[tiles : tiles + 1, :] = splat(total(target * target))


def back_body(groups, rinv_ref, *refs):
    parts, (term_ref, beta_ref, scratch) = refs[:groups], refs[groups:]
    summed = tree([ref[...] for ref in parts])
    tiles = rinv_ref.shape[0] // LANE
    beta = jnp.sqrt(summed[tiles : tiles + 1, :])
    beta_ref[...] = beta
    scratch[...] = summed[:tiles, :] / beta
    left_product_long(scratch, rinv_ref, term_ref)


def forward_body(groups, first, rinv_ref, design_ref, *refs):
    parts = refs[:groups]
    if first:
        image_ref, right_ref, held_ref, alpha_ref = refs[groups:]
        right = tree([ref[...] for ref in parts])
    else:
        before_ref, beta_ref, image_ref, right_ref, held_ref, alpha_ref = refs[groups:]
        right = tree([ref[...] for ref in parts]) - beta_ref[...] * before_ref[...]
    alpha = jnp.sqrt(total(right * right))
    alpha_ref[...] = splat(alpha)
    right = right / alpha
    right_ref[...] = right
    right_product(rinv_ref, right, held_ref)
    right_product(design_ref, held_ref[...], image_ref)


def turn_body(groups, last, *refs):
    parts, refs = refs[:groups], refs[groups:]
    before_ref, beta_ref, alpha_ref = refs[:3]
    left = tree([ref[...] for ref in parts]) - alpha_ref[...] * (before_ref[...] / beta_ref[...])
    square = splat(total(left * left))
    if last:
        left_ref, out_ref = refs[3:]
        left_ref[...] = left
        out_ref[...] = jnp.broadcast_to(square, out_ref.shape)
    else:
        design_ref, left_ref, out_ref = refs[3:]
        left_ref[...] = left
        tiles = design_ref.shape[1] // LANE
        out_ref[...] = jnp.zeros_like(out_ref)
        left_product(left, design_ref, out_ref)
        out_ref[tiles : tiles + 1, :] = square


def last_body(groups, *refs):
    parts, refs = refs[:groups], refs[groups:]
    left_ref, refs = refs[0], refs[1:]
    betas = [ref[...] for ref in refs[:ITERS]]
    alphas = [ref[...] for ref in refs[ITERS : 2 * ITERS]]
    held = [ref[...] for ref in refs[2 * ITERS : 3 * ITERS]]
    basis_ref, solution_ref = refs[3 * ITERS :]
    last = jnp.sqrt(tree([ref[...] for ref in parts])[:1, :])
    basis_ref[...] = left_ref[...] / last
    betas.append(last)
    phibar, rhobar = betas[0], alphas[0]
    search, iterate = held[0], jnp.zeros_like(held[0])
    for step in range(ITERS):
        beta = betas[step + 1]
        rho = jnp.sqrt(rhobar * rhobar + beta * beta)
        cosine = rhobar / rho
        sine = beta / rho
        phi = cosine * phibar
        phibar = sine * phibar
        iterate = iterate + phi / rho * search
        if step + 1 < ITERS:
            alpha = alphas[step + 1]
            search = held[step + 1] - sine * alpha / rho * search
            rhobar = -cosine * alpha
    solution_ref[...] = iterate


def shape(*dims):
    return jax.ShapeDtypeStruct(dims, F32)


def least_squares(design, target, rinv):
    rows, width = design.shape
    whole = rinv.shape[1]
    row_groups, col_groups = lax.axis_size("row"), lax.axis_size("col")
    packed = shape(pack_width(width), LANE)
    scalar = shape(1, LANE)
    big, small = rinv.size, design.size
    message = call(
        first_body, packed, design, target.reshape(rows // LANE, LANE), flops=2 * small, size=4 * small
    )
    left, alpha, right = target.reshape(rows // LANE, LANE), None, None
    betas, alphas, held = [], [], []
    for step in range(ITERS):
        parts = gathered(message, "row")
        term, beta = pl.pallas_call(
            functools.partial(back_body, row_groups),
            out_shape=(shape(whole // LANE, LANE), scalar),
            in_specs=[VMEM] * (1 + row_groups),
            out_specs=(VMEM, VMEM),
            scratch_shapes=[pltpu.VMEM((width // LANE, LANE), F32)],
            compiler_params=pltpu.CompilerParams(vmem_limit_bytes=24 << 20),
            cost_estimate=pl.CostEstimate(flops=2 * big, bytes_accessed=4 * big, transcendentals=0),
        )(rinv, *parts)
        betas.append(beta)
        parts = gathered(term, "col")
        extra = () if step == 0 else (right, beta)
        image, right, kept, alpha = call(
            functools.partial(forward_body, col_groups, step == 0),
            (shape(rows // LANE, LANE), shape(whole // LANE, LANE), shape(width // LANE, LANE), scalar),
            rinv,
            design,
            *parts,
            *extra,
            flops=2 * big,
            size=4 * big,
        )
        alphas.append(alpha)
        held.append(kept)
        parts = gathered(image, "col")
        last = step + 1 == ITERS
        extra = () if last else (design,)
        left, message = call(
            functools.partial(turn_body, col_groups, last),
            (shape(rows // LANE, LANE), shape(8, LANE) if last else packed),
            *parts,
            left,
            beta,
            alpha,
            *extra,
            flops=2 * small,
            size=0 if last else 4 * small,
        )
    parts = gathered(message, "row")
    basis, solution = call(
        functools.partial(last_body, row_groups),
        (shape(rows // LANE, LANE), shape(width // LANE, LANE)),
        *parts,
        left,
        *betas,
        *alphas,
        *held,
    )
    return solution.reshape(-1), basis.reshape(-1)


def sample_body(own_ref, other_ref, mix_ref, out_ref):
    flip = 1 - 2 * pl.program_id(0).astype(F32)
    both = own_ref[...] + flip * other_ref[...]
    high = both.astype(jnp.bfloat16)
    low = (both - high.astype(F32)).astype(jnp.bfloat16)
    mix = mix_ref[0]
    out_ref[0] = jnp.dot(mix, high, preferred_element_type=F32) + jnp.dot(mix, low, preferred_element_type=F32)


def sample(own, other, mix):
    slots, rows, width = mix.shape[1], own.shape[0], own.shape[1]
    block = min(slots, 256)
    return pl.pallas_call(
        sample_body,
        grid=(2, slots // block),
        out_shape=shape(2, slots, width),
        in_specs=[
            pl.BlockSpec((rows, width), lambda i, j: (0, 0)),
            pl.BlockSpec((rows, width), lambda i, j: (0, 0)),
            pl.BlockSpec((1, block, rows), lambda i, j: (i, j, 0)),
        ],
        out_specs=pl.BlockSpec((1, block, width), lambda i, j: (i, j, 0)),
        compiler_params=pltpu.CompilerParams(vmem_limit_bytes=16 << 20),
        cost_estimate=pl.CostEstimate(
            flops=8 * slots * rows * width, bytes_accessed=4 * slots * (rows + 2 * width), transcendentals=0
        ),
    )(own, other, mix)


def mixers(picks, counts, rows):
    groups = lax.axis_size("row")
    bits = groups.bit_length() - 1
    me = lax.axis_index("row")
    used = jnp.arange(PAIR, dtype=jnp.int32)[None, :] < counts
    coded = jnp.where(used, picks[:, 0, :], -1).reshape(-1, LANE)
    coded = jnp.stack(gathered(coded, "row")).reshape(groups, groups, PAIR)
    order = jnp.arange(groups, dtype=jnp.int32) ^ me
    coded = coded[order][:, order]
    coded = coded.reshape((groups // 2, 2) + (2,) * bits + (PAIR,))
    at = [2 + bits - 1 - bit for bit in range(bits)]
    owner_order = [at[bit] for bit in range(2, bits)] + [at[0]]
    coded = coded.transpose([at[1], 1] + owner_order + [0, 2 + bits])
    coded = coded.reshape(2, 2, groups // 2, groups // 2, PAIR)
    block = jnp.arange(groups // 2, dtype=jnp.int32)
    parity = jnp.zeros_like(block)
    for bit in range(bits - 1):
        parity = parity ^ (jnp.right_shift(block & jnp.right_shift(me, 1), bit) & 1)
    sign = (1 - 2 * parity).astype(F32)
    low = (1 - 2 * (jnp.arange(2, dtype=jnp.int32) * (me & 1))).astype(F32)
    sign = low[:, None] * sign[None, :]
    sign = jnp.broadcast_to(sign[None, :, None, :, None], coded.shape)
    coded, sign = coded.reshape(-1), sign.reshape(-1)
    chosen = coded[:, None] == jnp.arange(rows, dtype=jnp.int32)[None, :]
    chosen = jnp.where(chosen, sign[:, None], 0.0).astype(jnp.bfloat16).reshape(-1, rows // HB, HB)
    mix = jnp.einsum("sqc,cb->sqb", chosen, jnp.asarray(walsh(HB), jnp.bfloat16), preferred_element_type=F32)
    return mix.astype(jnp.bfloat16).reshape(2, 2, -1, rows)


def sketch_rows(design, sign_bits, picks, counts):
    rows, width = design.shape
    groups = lax.axis_size("row")
    bits = groups.bit_length() - 1
    me = lax.axis_index("row")
    low = me & 1
    signs = (2 * sign_bits - 1).astype(F32)[:, None]
    half = width // 2
    piece = half // CHUNKS if half // CHUNKS >= LANE else half
    mix = mixers(picks, counts, rows)
    done_mine, done_other = [], []
    for start in range(0, half, piece):
        mine = jnp.where(low == 1, design[:, half + start : half + start + piece], design[:, start : start + piece])
        away = jnp.where(low == 1, design[:, start : start + piece], design[:, half + start : half + start + piece])
        mine, away = mine * signs, away * signs
        other = swap(away, "row", 1)
        send = sample(mine, other, mix[1])
        keep = sample(mine, other, mix[0])
        slots = send.shape[1]
        for bit in range(1, bits):
            arrived = swap(send, "row", 1 << bit)
            keep = keep + arrived
            slots //= 2
            send = keep[:, slots:]
            keep = keep[:, :slots]
        arrived = swap(send, "row", 1)
        done_mine.append(keep)
        done_other.append(arrived)
    mine, other = jnp.concatenate(done_mine, axis=2), jnp.concatenate(done_other, axis=2)
    left = jnp.where(low == 1, other, mine)
    right = jnp.where(low == 1, mine, other)
    both = jnp.concatenate([left, right], axis=2).reshape(2, groups // 2, PAIR, width)
    both = both.transpose(1, 0, 2, 3).reshape(groups * PAIR, width)
    return both / jnp.sqrt(jnp.float32(rows * groups))


def shards(design, sign_bits, picks, counts, target, rinv):
    sketch = sketch_rows(design, sign_bits, picks, counts)
    answer, basis = least_squares(design, target, rinv)
    return (sketch, answer, basis)


def solution(mesh):
    placed = (
        P("row", "col"),
        P("row"),
        P(None, "row", None),
        P(None, "row"),
        P("row"),
        P("col", None),
    )
    return jax.shard_map(
        shards,
        mesh=mesh,
        in_specs=placed,
        out_specs=(P("row", "col"), P("col"), P("row")),
        check_vma=False,
    )
```

profile of v0, /device:TPU:0, one launch (start us, length us, event | category | flops | bytes accessed | tf_op | source)
XLA Modules:
  0.0 162.2 jit_solution(6843428380153608292)
XLA Ops:
  3.4 3.0 %collective-permute-start.1 = (s32[1,128]{1,0:T(1,128)S(1)}, s32[1,128]{1,0:T(1,128)S(1)}, u32[]{:S(2)}, u32[]{:S(2)}) collective-permute-start(s32[1,128]{1,0:T(1,128)S(1)} %broadcast_select_fusion), channel_id=1, source_target_pairs={{0,4},{4,0},{8,12},{12,8},{16,20},{20,16},{24,28},{28,24},{1,5},{5... | collective-permute-start | bytes 1544 | tf_op jit(solution)/shard_map/ppermute | solution.py:21
  8.0 3.0 %collective-permute-start.4 = (s32[1,128]{1,0:T(1,128)S(1)}, s32[1,128]{1,0:T(1,128)S(1)}, u32[]{:S(2)}, u32[]{:S(2)}) collective-permute-start(s32[1,128]{1,0:T(1,128)S(1)} %broadcast_select_fusion), channel_id=1, source_target_pairs={{0,16},{4,20},{8,24},{12,28},{16,0},{20,4},{24,8},{28,12},{1,17},{... | collective-permute-start | bytes 1544 | tf_op jit(solution)/shard_map/ppermute | solution.py:21
  13.8 2.8 %select_multiply_fusion.2 = (f32[512,256]{1,0:T(8,128)}, f32[512,256]{1,0:T(8,128)S(1)}, f32[512,256]{1,0:T(8,128)}, f32[512,256]{1,0:T(8,128)S(1)}) fusion(f32[512,1024]{1,0:T(8,128)} %design_ref.5, f32[512]{0:T(512)S(1)} %add_convert_fusion, pred[]{:T(512)S(6)} %eq.30), kind=kLoop, calls=%fused_computation.12 | loop fusion | flops 1048576 | bytes 4196353 | tf_op jit(solution)/shard_map/mul | solution.py:332
  16.8 3.7 %collective-permute-start.6 = (s32[1,128]{1,0:T(1,128)S(1)}, s32[1,128]{1,0:T(1,128)S(1)}, u32[]{:S(2)}, u32[]{:S(2)}) collective-permute-start(s32[1,128]{1,0:T(1,128)S(1)} %broadcast_select_fusion), channel_id=1, source_target_pairs={{0,24},{4,28},{8,16},{12,20},{16,8},{20,12},{24,0},{28,4},{1,25},{... | collective-permute-start | bytes 1544 | tf_op jit(solution)/shard_map/ppermute | solution.py:21
  31.8 5.3 %collective-permute-done.11.other_ref = f32[512,256]{1,0:T(8,128)S(1)} collective-permute-done((f32[512,256]{1,0:T(8,128)}, f32[512,256]{1,0:T(8,128)S(1)}, u32[]{:S(2)}, u32[]{:S(2)}) %collective-permute-start.11) | collective-permute-done | bytes 524320 | tf_op jit(solution)/shard_map/ppermute | solution.py:21
  38.5 7.0 %collective-permute-done.other_ref = f32[512,256]{1,0:T(8,128)S(1)} collective-permute-done((f32[512,256]{1,0:T(8,128)}, f32[512,256]{1,0:T(8,128)S(1)}, u32[]{:S(2)}, u32[]{:S(2)}) %collective-permute-start) | collective-permute-done | bytes 524320 | tf_op jit(solution)/shard_map/ppermute | solution.py:21
  50.8 4.1 %collective-permute-start.13 = (f32[2,128,256]{2,1,0:T(8,128)S(1)}, f32[2,128,256]{2,1,0:T(8,128)S(1)}, u32[]{:S(2)}, u32[]{:S(2)}) collective-permute-start(f32[2,128,256]{2,1,0:T(8,128)S(1)} %slice.74), channel_id=1, source_target_pairs={{0,16},{4,20},{8,24},{12,28},{16,0},{20,4},{24,8},{28,12},{1,17},{... | collective-permute-start | bytes 786440 | tf_op jit(solution)/shard_map/ppermute | solution.py:21
  55.5 9.3 %collective-permute-done.8 = f32[2,256,256]{2,1,0:T(8,128)} collective-permute-done((f32[2,256,256]{2,1,0:T(8,128)S(1)}, f32[2,256,256]{2,1,0:T(8,128)}, u32[]{:S(2)}, u32[]{:S(2)}) %collective-permute-start.8) | collective-permute-done | bytes 524320 | tf_op jit(solution)/shard_map/ppermute | solution.py:21
  66.0 1.8 %collective-permute-start.9 = (f32[2,128,256]{2,1,0:T(8,128)S(1)}, f32[2,128,256]{2,1,0:T(8,128)S(1)}, u32[]{:S(2)}, u32[]{:S(2)}) collective-permute-start(f32[2,128,256]{2,1,0:T(8,128)S(1)} %slice.71), channel_id=1, source_target_pairs={{0,16},{4,20},{8,24},{12,28},{16,0},{20,4},{24,8},{28,12},{1,17},{... | collective-permute-start | bytes 786440 | tf_op jit(solution)/shard_map/ppermute | solution.py:21
  67.8 10.7 %collective-permute-done.9 = f32[2,128,256]{2,1,0:T(8,128)S(1)} collective-permute-done((f32[2,128,256]{2,1,0:T(8,128)S(1)}, f32[2,128,256]{2,1,0:T(8,128)S(1)}, u32[]{:S(2)}, u32[]{:S(2)}) %collective-permute-start.9) | collective-permute-done | bytes 262176 | tf_op jit(solution)/shard_map/ppermute | solution.py:21
  82.5 1.9 %collective-permute-start.17 = (f32[16,128]{1,0:T(8,128)S(1)}, f32[16,128]{1,0:T(8,128)S(1)}, u32[]{:S(2)}, u32[]{:S(2)}) collective-permute-start(f32[16,128]{1,0:T(8,128)S(1)} %shard_map.98.refs_0_), channel_id=1, source_target_pairs={{0,12},{4,8},{8,4},{12,0},{16,28},{20,24},{24,20},{28,16},{1,13},{... | collective-permute-start | bytes 24584 | tf_op jit(solution)/shard_map/ppermute | solution.py:21
  84.4 2.3 %collective-permute-done.15.refs_1_ = f32[16,128]{1,0:T(8,128)S(1)} collective-permute-done((f32[16,128]{1,0:T(8,128)S(1)}, f32[16,128]{1,0:T(8,128)S(1)}, u32[]{:S(2)}, u32[]{:S(2)}) %collective-permute-start.15) | collective-permute-done | bytes 8224 | tf_op jit(solution)/shard_map/ppermute | solution.py:21
  86.8 3.9 %collective-permute-start.19 = (f32[16,128]{1,0:T(8,128)S(1)}, f32[16,128]{1,0:T(8,128)S(1)}, u32[]{:S(2)}, u32[]{:S(2)}) collective-permute-start(f32[16,128]{1,0:T(8,128)S(1)} %shard_map.98.refs_0_), channel_id=1, source_target_pairs={{0,20},{4,16},{8,28},{12,24},{16,4},{20,0},{24,12},{28,8},{1,21},{... | collective-permute-start | bytes 24584 | tf_op jit(solution)/shard_map/ppermute | solution.py:21
  91.3 3.1 %collective-permute-start.21 = (f32[16,128]{1,0:T(8,128)S(1)}, f32[16,128]{1,0:T(8,128)S(1)}, u32[]{:S(2)}, u32[]{:S(2)}) collective-permute-start(f32[16,128]{1,0:T(8,128)S(1)} %shard_map.98.refs_0_), channel_id=1, source_target_pairs={{0,28},{4,24},{8,20},{12,16},{16,12},{20,8},{24,4},{28,0},{1,29},{... | collective-permute-start | bytes 24584 | tf_op jit(solution)/shard_map/ppermute | solution.py:21
  97.7 5.8 %copy-done = f32[1024,4096]{1,0:T(8,128)S(1)} copy-done((f32[1024,4096]{1,0:T(8,128)S(1)}, f32[1024,4096]{1,0:T(8,128)}, u32[]{:S(2)}) %copy-start) | copy-done | bytes 16777240
  103.4 2.0 %shard_map.99 = (f32[32,128]{1,0:T(8,128)S(1)}, f32[1,128]{1,0:T(1,128)S(1)}) custom-call(f32[1024,4096]{1,0:T(8,128)S(1)} %copy-done, f32[16,128]{1,0:T(8,128)S(1)} %shard_map.98.refs_0_, f32[16,128]{1,0:T(8,128)S(1)} %collective-permute-done.15.refs_1_, f32[16,128]{1,0:T(8,128)S(1)} %collective-permute-done.16.refs_2_, ...), custom_call_target="tpu_custom_call" | custom-call | flops 8388608 | bytes 16777216 | tf_op jit(solution)/shard_map/pallas_call | solution.py:209
  107.3 1.9 %collective-permute-done.23.refs_2_ = f32[32,128]{1,0:T(8,128)S(1)} collective-permute-done((f32[32,128]{1,0:T(8,128)S(1)}, f32[32,128]{1,0:T(8,128)S(1)}, u32[]{:S(2)}, u32[]{:S(2)}) %collective-permute-start.23) | collective-permute-done | bytes 16416 | tf_op jit(solution)/shard_map/ppermute | solution.py:21
  110.0 2.4 %shard_map.100 = (f32[4,128]{1,0:T(4,128)S(1)}, f32[32,128]{1,0:T(8,128)S(1)}, f32[8,128]{1,0:T(8,128)S(1)}, f32[1,128]{1,0:T(1,128)S(1)}) custom-call(f32[1024,4096]{1,0:T(8,128)S(1)} %copy-done.1, f32[512,1024]{1,0:T(8,128)S(1)} %copy-done.2, f32[32,128]{1,0:T(8,128)S(1)} %get-tuple-element.20.refs_0_, f32[32,128]{1,0:T(8,128)S(1)} %collective-permute-done.22.refs_1_, ...), custom_call_target="tpu_custom_call" | custom-call | flops 8388608 | bytes 16777216 | tf_op jit(solution)/shard_map/pallas_call | solution.py:44
  114.4 1.9 %collective-permute-done.26.refs_2_ = f32[4,128]{1,0:T(4,128)S(1)} collective-permute-done((f32[4,128]{1,0:T(4,128)S(1)}, f32[4,128]{1,0:T(4,128)S(1)}, u32[]{:S(2)}, u32[]{:S(2)}) %collective-permute-start.26) | collective-permute-done | bytes 2080 | tf_op jit(solution)/shard_map/ppermute | solution.py:21
  118.4 1.8 %collective-permute-start.30 = (f32[16,128]{1,0:T(8,128)S(1)}, f32[16,128]{1,0:T(8,128)S(1)}, u32[]{:S(2)}, u32[]{:S(2)}) collective-permute-start(f32[16,128]{1,0:T(8,128)S(1)} %get-tuple-element.24.refs_0_), channel_id=1, source_target_pairs={{0,12},{4,8},{8,4},{12,0},{16,28},{20,24},{24,20},{28,16},{1,13},{... | collective-permute-start | bytes 24584 | tf_op jit(solution)/shard_map/ppermute | solution.py:21
  122.0 2.4 %collective-permute-start.32 = (f32[16,128]{1,0:T(8,128)S(1)}, f32[16,128]{1,0:T(8,128)S(1)}, u32[]{:S(2)}, u32[]{:S(2)}) collective-permute-start(f32[16,128]{1,0:T(8,128)S(1)} %get-tuple-element.24.refs_0_), channel_id=1, source_target_pairs={{0,20},{4,16},{8,28},{12,24},{16,4},{20,0},{24,12},{28,8},{1,21},{... | collective-permute-start | bytes 24584 | tf_op jit(solution)/shard_map/ppermute | solution.py:21
  124.4 2.0 %collective-permute-start.33 = (f32[16,128]{1,0:T(8,128)S(1)}, f32[16,128]{1,0:T(8,128)S(1)}, u32[]{:S(2)}, u32[]{:S(2)}) collective-permute-start(f32[16,128]{1,0:T(8,128)S(1)} %get-tuple-element.24.refs_0_), channel_id=1, source_target_pairs={{0,24},{4,28},{8,16},{12,20},{16,8},{20,12},{24,0},{28,4},{1,25},{... | collective-permute-start | bytes 24584 | tf_op jit(solution)/shard_map/ppermute | solution.py:21
  128.0 1.8 %collective-permute-done.33.refs_6_ = f32[16,128]{1,0:T(8,128)S(1)} collective-permute-done((f32[16,128]{1,0:T(8,128)S(1)}, f32[16,128]{1,0:T(8,128)S(1)}, u32[]{:S(2)}, u32[]{:S(2)}) %collective-permute-start.33) | collective-permute-done | bytes 8224 | tf_op jit(solution)/shard_map/ppermute | solution.py:21
  129.8 2.9 %collective-permute-done.34.refs_7_ = f32[16,128]{1,0:T(8,128)S(1)} collective-permute-done((f32[16,128]{1,0:T(8,128)S(1)}, f32[16,128]{1,0:T(8,128)S(1)}, u32[]{:S(2)}, u32[]{:S(2)}) %collective-permute-start.34) | collective-permute-done | bytes 8224 | tf_op jit(solution)/shard_map/ppermute | solution.py:21
  132.8 1.8 %shard_map.102 = (f32[32,128]{1,0:T(8,128)S(1)}, f32[1,128]{1,0:T(1,128)S(1)}) custom-call(f32[1024,4096]{1,0:T(8,128)S(1)} %copy-done.1, f32[16,128]{1,0:T(8,128)S(1)} %get-tuple-element.24.refs_0_, f32[16,128]{1,0:T(8,128)S(1)} %collective-permute-done.28.refs_1_, f32[16,128]{1,0:T(8,128)S(1)} %collective-permute-done.29.refs_2_, ...), custom_call_target="tpu_custom_call" | custom-call | flops 8388608 | bytes 16777216 | tf_op jit(solution)/shard_map/pallas_call | solution.py:209
  136.5 1.9 %collective-permute-done.36.refs_2_ = f32[32,128]{1,0:T(8,128)S(1)} collective-permute-done((f32[32,128]{1,0:T(8,128)S(1)}, f32[32,128]{1,0:T(8,128)S(1)}, u32[]{:S(2)}, u32[]{:S(2)}) %collective-permute-start.36) | collective-permute-done | bytes 16416 | tf_op jit(solution)/shard_map/ppermute | solution.py:21
  139.2 2.9 %shard_map.103 = (f32[4,128]{1,0:T(4,128)S(1)}, f32[32,128]{1,0:T(8,128)}, f32[8,128]{1,0:T(8,128)S(1)}, f32[1,128]{1,0:T(1,128)S(1)}) custom-call(f32[1024,4096]{1,0:T(8,128)S(1)} %copy-done.1, f32[512,1024]{1,0:T(8,128)S(1)} %copy-done.2, f32[32,128]{1,0:T(8,128)S(1)} %get-tuple-element.25.refs_0_, f32[32,128]{1,0:T(8,128)S(1)} %collective-permute-done.35.refs_1_, ...), custom_call_target="tpu_custom_call" | custom-call | flops 8388608 | bytes 16777216 | tf_op jit(solution)/shard_map/pallas_call | solution.py:44
  144.0 1.9 %collective-permute-done.39.refs_2_ = f32[4,128]{1,0:T(4,128)S(1)} collective-permute-done((f32[4,128]{1,0:T(4,128)S(1)}, f32[4,128]{1,0:T(4,128)S(1)}, u32[]{:S(2)}, u32[]{:S(2)}) %collective-permute-start.39) | collective-permute-done | bytes 2080 | tf_op jit(solution)/shard_map/ppermute | solution.py:21
  147.8 1.8 %collective-permute-start.43 = (f32[8,128]{1,0:T(8,128)S(1)}, f32[8,128]{1,0:T(8,128)S(1)}, u32[]{:S(2)}, u32[]{:S(2)}) collective-permute-start(f32[8,128]{1,0:T(8,128)S(1)} %get-tuple-element.31.refs_0_), channel_id=1, source_target_pairs={{0,12},{4,8},{8,4},{12,0},{16,28},{20,24},{24,20},{28,16},{1,13},{... | collective-permute-start | bytes 12296 | tf_op jit(solution)/shard_map/ppermute | solution.py:21
  151.4 2.4 %collective-permute-start.45 = (f32[8,128]{1,0:T(8,128)S(1)}, f32[8,128]{1,0:T(8,128)S(1)}, u32[]{:S(2)}, u32[]{:S(2)}) collective-permute-start(f32[8,128]{1,0:T(8,128)S(1)} %get-tuple-element.31.refs_0_), channel_id=1, source_target_pairs={{0,20},{4,16},{8,28},{12,24},{16,4},{20,0},{24,12},{28,8},{1,21},{... | collective-permute-start | bytes 12296 | tf_op jit(solution)/shard_map/ppermute | solution.py:21
  154.3 3.1 %collective-permute-start.47 = (f32[8,128]{1,0:T(8,128)S(1)}, f32[8,128]{1,0:T(8,128)S(1)}, u32[]{:S(2)}, u32[]{:S(2)}) collective-permute-start(f32[8,128]{1,0:T(8,128)S(1)} %get-tuple-element.31.refs_0_), channel_id=1, source_target_pairs={{0,28},{4,24},{8,20},{12,16},{16,12},{20,8},{24,4},{28,0},{1,29},{... | collective-permute-start | bytes 12296 | tf_op jit(solution)/shard_map/ppermute | solution.py:21
  157.4 1.8 %collective-permute-done.46.refs_6_ = f32[8,128]{1,0:T(8,128)S(1)} collective-permute-done((f32[8,128]{1,0:T(8,128)S(1)}, f32[8,128]{1,0:T(8,128)S(1)}, u32[]{:S(2)}, u32[]{:S(2)}) %collective-permute-start.46) | collective-permute-done | bytes 4128 | tf_op jit(solution)/shard_map/ppermute | solution.py:21
  (148 shorter events, 56.8 us)
Async XLA Ops:
  3.4 13.4 %collective-permute-start.1 = (s32[1,128]{1,0:T(1,128)S(1)}, s32[1,128]{1,0:T(1,128)S(1)}, u32[]{:S(2)}, u32[]{:S(2)}) collective-permute-start(s32[1,128]{1,0:T(1,128)S(1)} %broadcast_select_fusion), channel_id=1, source_target_pairs={{0,4},{4,0},{8,12},{12,8},{16,20},{20,16},{24,28},{28,24},{1,5},{5... | collective-permute-start | bytes 1544 | tf_op jit(solution)/shard_map/ppermute | solution.py:21
  6.4 14.8 %collective-permute-start.2 = (s32[1,128]{1,0:T(1,128)S(1)}, s32[1,128]{1,0:T(1,128)S(1)}, u32[]{:S(2)}, u32[]{:S(2)}) collective-permute-start(s32[1,128]{1,0:T(1,128)S(1)} %broadcast_select_fusion), channel_id=1, source_target_pairs={{0,8},{4,12},{8,0},{12,4},{16,24},{20,28},{24,16},{28,20},{1,9},{5... | collective-permute-start | bytes 1544 | tf_op jit(solution)/shard_map/ppermute | solution.py:21
  8.0 14.0 %collective-permute-start.3 = (s32[1,128]{1,0:T(1,128)S(1)}, s32[1,128]{1,0:T(1,128)S(1)}, u32[]{:S(2)}, u32[]{:S(2)}) collective-permute-start(s32[1,128]{1,0:T(1,128)S(1)} %broadcast_select_fusion), channel_id=1, source_target_pairs={{0,12},{4,8},{8,4},{12,0},{16,28},{20,24},{24,20},{28,16},{1,13},{... | collective-permute-start | bytes 1544 | tf_op jit(solution)/shard_map/ppermute | solution.py:21
  8.0 16.4 %collective-permute-start.4 = (s32[1,128]{1,0:T(1,128)S(1)}, s32[1,128]{1,0:T(1,128)S(1)}, u32[]{:S(2)}, u32[]{:S(2)}) collective-permute-start(s32[1,128]{1,0:T(1,128)S(1)} %broadcast_select_fusion), channel_id=1, source_target_pairs={{0,16},{4,20},{8,24},{12,28},{16,0},{20,4},{24,8},{28,12},{1,17},{... | collective-permute-start | bytes 1544 | tf_op jit(solution)/shard_map/ppermute | solution.py:21
  11.0 14.6 %collective-permute-start.5 = (s32[1,128]{1,0:T(1,128)S(1)}, s32[1,128]{1,0:T(1,128)S(1)}, u32[]{:S(2)}, u32[]{:S(2)}) collective-permute-start(s32[1,128]{1,0:T(1,128)S(1)} %broadcast_select_fusion), channel_id=1, source_target_pairs={{0,20},{4,16},{8,28},{12,24},{16,4},{20,0},{24,12},{28,8},{1,21},{... | collective-permute-start | bytes 1544 | tf_op jit(solution)/shard_map/ppermute | solution.py:21
  16.8 9.5 %collective-permute-start.6 = (s32[1,128]{1,0:T(1,128)S(1)}, s32[1,128]{1,0:T(1,128)S(1)}, u32[]{:S(2)}, u32[]{:S(2)}) collective-permute-start(s32[1,128]{1,0:T(1,128)S(1)} %broadcast_select_fusion), channel_id=1, source_target_pairs={{0,24},{4,28},{8,16},{12,20},{16,8},{20,12},{24,0},{28,4},{1,25},{... | collective-permute-start | bytes 1544 | tf_op jit(solution)/shard_map/ppermute | solution.py:21
  21.2 6.2 %collective-permute-start.7 = (s32[1,128]{1,0:T(1,128)S(1)}, s32[1,128]{1,0:T(1,128)S(1)}, u32[]{:S(2)}, u32[]{:S(2)}) collective-permute-start(s32[1,128]{1,0:T(1,128)S(1)} %broadcast_select_fusion), channel_id=1, source_target_pairs={{0,28},{4,24},{8,20},{12,16},{16,12},{20,8},{24,4},{28,0},{1,29},{... | collective-permute-start | bytes 1544 | tf_op jit(solution)/shard_map/ppermute | solution.py:21
  22.0 15.1 %collective-permute-start.11 = (f32[512,256]{1,0:T(8,128)}, f32[512,256]{1,0:T(8,128)S(1)}, u32[]{:S(2)}, u32[]{:S(2)}) collective-permute-start(f32[512,256]{1,0:T(8,128)} %get-tuple-element.39), channel_id=1, source_target_pairs={{0,4},{4,0},{8,12},{12,8},{16,20},{20,16},{24,28},{28,24},{1,5},{5... | collective-permute-start | bytes 1572872 | tf_op jit(solution)/shard_map/ppermute | solution.py:21
  24.4 21.0 %collective-permute-start = (f32[512,256]{1,0:T(8,128)}, f32[512,256]{1,0:T(8,128)S(1)}, u32[]{:S(2)}, u32[]{:S(2)}) collective-permute-start(f32[512,256]{1,0:T(8,128)} %get-tuple-element.37), channel_id=1, source_target_pairs={{0,4},{4,0},{8,12},{12,8},{16,20},{20,16},{24,28},{28,24},{1,5},{5... | collective-permute-start | bytes 1572872 | tf_op jit(solution)/shard_map/ppermute | solution.py:21
  38.5 11.2 %collective-permute-start.12 = (f32[2,256,256]{2,1,0:T(8,128)}, f32[2,256,256]{2,1,0:T(8,128)}, u32[]{:S(2)}, u32[]{:S(2)}) collective-permute-start(f32[2,256,256]{2,1,0:T(8,128)} %shard_map.97), channel_id=1, source_target_pairs={{0,8},{4,12},{8,0},{12,4},{16,24},{20,28},{24,16},{28,20},{1,9},{5... | collective-permute-start | bytes 1572872 | tf_op jit(solution)/shard_map/ppermute | solution.py:21
  46.1 18.7 %collective-permute-start.8 = (f32[2,256,256]{2,1,0:T(8,128)S(1)}, f32[2,256,256]{2,1,0:T(8,128)}, u32[]{:S(2)}, u32[]{:S(2)}) collective-permute-start(f32[2,256,256]{2,1,0:T(8,128)S(1)} %shard_map.95), channel_id=1, source_target_pairs={{0,8},{4,12},{8,0},{12,4},{16,24},{20,28},{24,16},{28,20},{1,9},{5... | collective-permute-start | bytes 1572872 | tf_op jit(solution)/shard_map/ppermute | solution.py:21
  50.8 17.0 %collective-permute-start.13 = (f32[2,128,256]{2,1,0:T(8,128)S(1)}, f32[2,128,256]{2,1,0:T(8,128)S(1)}, u32[]{:S(2)}, u32[]{:S(2)}) collective-permute-start(f32[2,128,256]{2,1,0:T(8,128)S(1)} %slice.74), channel_id=1, source_target_pairs={{0,16},{4,20},{8,24},{12,28},{16,0},{20,4},{24,8},{28,12},{1,17},{... | collective-permute-start | bytes 786440 | tf_op jit(solution)/shard_map/ppermute | solution.py:21
  66.0 12.5 %collective-permute-start.9 = (f32[2,128,256]{2,1,0:T(8,128)S(1)}, f32[2,128,256]{2,1,0:T(8,128)S(1)}, u32[]{:S(2)}, u32[]{:S(2)}) collective-permute-start(f32[2,128,256]{2,1,0:T(8,128)S(1)} %slice.71), channel_id=1, source_target_pairs={{0,16},{4,20},{8,24},{12,28},{16,0},{20,4},{24,8},{28,12},{1,17},{... | collective-permute-start | bytes 786440 | tf_op jit(solution)/shard_map/ppermute | solution.py:21
  78.6 82.7 %collective-permute-start.14 = (f32[2,64,256]{2,1,0:T(8,128)S(1)}, f32[2,64,256]{2,1,0:T(8,128)S(1)}, u32[]{:S(2)}, u32[]{:S(2)}) collective-permute-start(f32[2,64,256]{2,1,0:T(8,128)S(1)} %get-tuple-element.47), channel_id=1, source_target_pairs={{0,4},{4,0},{8,12},{12,8},{16,20},{20,16},{24,28},{28,24},{1,5},{5... | collective-permute-start | bytes 393224 | tf_op jit(solution)/shard_map/ppermute | solution.py:21
  80.2 81.1 %collective-permute-start.10 = (f32[2,64,256]{2,1,0:T(8,128)S(1)}, f32[2,64,256]{2,1,0:T(8,128)S(1)}, u32[]{:S(2)}, u32[]{:S(2)}) collective-permute-start(f32[2,64,256]{2,1,0:T(8,128)S(1)} %get-tuple-element.45), channel_id=1, source_target_pairs={{0,4},{4,0},{8,12},{12,8},{16,20},{20,16},{24,28},{28,24},{1,5},{5... | collective-permute-start | bytes 393224 | tf_op jit(solution)/shard_map/ppermute | solution.py:21
  80.9 5.9 %collective-permute-start.15 = (f32[16,128]{1,0:T(8,128)S(1)}, f32[16,128]{1,0:T(8,128)S(1)}, u32[]{:S(2)}, u32[]{:S(2)}) collective-permute-start(f32[16,128]{1,0:T(8,128)S(1)} %shard_map.98.refs_0_), channel_id=1, source_target_pairs={{0,4},{4,0},{8,12},{12,8},{16,20},{20,16},{24,28},{28,24},{1,5},{5... | collective-permute-start | bytes 24584 | tf_op jit(solution)/shard_map/ppermute | solution.py:21
  82.5 4.2 %collective-permute-start.16 = (f32[16,128]{1,0:T(8,128)S(1)}, f32[16,128]{1,0:T(8,128)S(1)}, u32[]{:S(2)}, u32[]{:S(2)}) collective-permute-start(f32[16,128]{1,0:T(8,128)S(1)} %shard_map.98.refs_0_), channel_id=1, source_target_pairs={{0,8},{4,12},{8,0},{12,4},{16,24},{20,28},{24,16},{28,20},{1,9},{5... | collective-permute-start | bytes 24584 | tf_op jit(solution)/shard_map/ppermute | solution.py:21
  82.5 8.1 %collective-permute-start.17 = (f32[16,128]{1,0:T(8,128)S(1)}, f32[16,128]{1,0:T(8,128)S(1)}, u32[]{:S(2)}, u32[]{:S(2)}) collective-permute-start(f32[16,128]{1,0:T(8,128)S(1)} %shard_map.98.refs_0_), channel_id=1, source_target_pairs={{0,12},{4,8},{8,4},{12,0},{16,28},{20,24},{24,20},{28,16},{1,13},{... | collective-permute-start | bytes 24584 | tf_op jit(solution)/shard_map/ppermute | solution.py:21
  86.8 4.5 %collective-permute-start.18 = (f32[16,128]{1,0:T(8,128)S(1)}, f32[16,128]{1,0:T(8,128)S(1)}, u32[]{:S(2)}, u32[]{:S(2)}) collective-permute-start(f32[16,128]{1,0:T(8,128)S(1)} %shard_map.98.refs_0_), channel_id=1, source_target_pairs={{0,16},{4,20},{8,24},{12,28},{16,0},{20,4},{24,8},{28,12},{1,17},{... | collective-permute-start | bytes 24584 | tf_op jit(solution)/shard_map/ppermute | solution.py:21
  86.8 7.7 %collective-permute-start.19 = (f32[16,128]{1,0:T(8,128)S(1)}, f32[16,128]{1,0:T(8,128)S(1)}, u32[]{:S(2)}, u32[]{:S(2)}) collective-permute-start(f32[16,128]{1,0:T(8,128)S(1)} %shard_map.98.refs_0_), channel_id=1, source_target_pairs={{0,20},{4,16},{8,28},{12,24},{16,4},{20,0},{24,12},{28,8},{1,21},{... | collective-permute-start | bytes 24584 | tf_op jit(solution)/shard_map/ppermute | solution.py:21
  90.7 5.4 %collective-permute-start.20 = (f32[16,128]{1,0:T(8,128)S(1)}, f32[16,128]{1,0:T(8,128)S(1)}, u32[]{:S(2)}, u32[]{:S(2)}) collective-permute-start(f32[16,128]{1,0:T(8,128)S(1)} %shard_map.98.refs_0_), channel_id=1, source_target_pairs={{0,24},{4,28},{8,16},{12,20},{16,8},{20,12},{24,0},{28,4},{1,25},{... | collective-permute-start | bytes 24584 | tf_op jit(solution)/shard_map/ppermute | solution.py:21
  91.3 6.3 %collective-permute-start.21 = (f32[16,128]{1,0:T(8,128)S(1)}, f32[16,128]{1,0:T(8,128)S(1)}, u32[]{:S(2)}, u32[]{:S(2)}) collective-permute-start(f32[16,128]{1,0:T(8,128)S(1)} %shard_map.98.refs_0_), channel_id=1, source_target_pairs={{0,28},{4,24},{8,20},{12,16},{16,12},{20,8},{24,4},{28,0},{1,29},{... | collective-permute-start | bytes 24584 | tf_op jit(solution)/shard_map/ppermute | solution.py:21
  118.4 6.0 %collective-permute-start.30 = (f32[16,128]{1,0:T(8,128)S(1)}, f32[16,128]{1,0:T(8,128)S(1)}, u32[]{:S(2)}, u32[]{:S(2)}) collective-permute-start(f32[16,128]{1,0:T(8,128)S(1)} %get-tuple-element.24.refs_0_), channel_id=1, source_target_pairs={{0,12},{4,8},{8,4},{12,0},{16,28},{20,24},{24,20},{28,16},{1,13},{... | collective-permute-start | bytes 24584 | tf_op jit(solution)/shard_map/ppermute | solution.py:21
  120.4 6.0 %collective-permute-start.31 = (f32[16,128]{1,0:T(8,128)S(1)}, f32[16,128]{1,0:T(8,128)S(1)}, u32[]{:S(2)}, u32[]{:S(2)}) collective-permute-start(f32[16,128]{1,0:T(8,128)S(1)} %get-tuple-element.24.refs_0_), channel_id=1, source_target_pairs={{0,16},{4,20},{8,24},{12,28},{16,0},{20,4},{24,8},{28,12},{1,17},{... | collective-permute-start | bytes 24584 | tf_op jit(solution)/shard_map/ppermute | solution.py:21
  122.0 6.0 %collective-permute-start.32 = (f32[16,128]{1,0:T(8,128)S(1)}, f32[16,128]{1,0:T(8,128)S(1)}, u32[]{:S(2)}, u32[]{:S(2)}) collective-permute-start(f32[16,128]{1,0:T(8,128)S(1)} %get-tuple-element.24.refs_0_), channel_id=1, source_target_pairs={{0,20},{4,16},{8,28},{12,24},{16,4},{20,0},{24,12},{28,8},{1,21},{... | collective-permute-start | bytes 24584 | tf_op jit(solution)/shard_map/ppermute | solution.py:21
  124.4 5.4 %collective-permute-start.33 = (f32[16,128]{1,0:T(8,128)S(1)}, f32[16,128]{1,0:T(8,128)S(1)}, u32[]{:S(2)}, u32[]{:S(2)}) collective-permute-start(f32[16,128]{1,0:T(8,128)S(1)} %get-tuple-element.24.refs_0_), channel_id=1, source_target_pairs={{0,24},{4,28},{8,16},{12,20},{16,8},{20,12},{24,0},{28,4},{1,25},{... | collective-permute-start | bytes 24584 | tf_op jit(solution)/shard_map/ppermute | solution.py:21
  126.4 6.3 %collective-permute-start.34 = (f32[16,128]{1,0:T(8,128)S(1)}, f32[16,128]{1,0:T(8,128)S(1)}, u32[]{:S(2)}, u32[]{:S(2)}) collective-permute-start(f32[16,128]{1,0:T(8,128)S(1)} %get-tuple-element.24.refs_0_), channel_id=1, source_target_pairs={{0,28},{4,24},{8,20},{12,16},{16,12},{20,8},{24,4},{28,0},{1,29},{... | collective-permute-start | bytes 24584 | tf_op jit(solution)/shard_map/ppermute | solution.py:21
  147.8 6.0 %collective-permute-start.43 = (f32[8,128]{1,0:T(8,128)S(1)}, f32[8,128]{1,0:T(8,128)S(1)}, u32[]{:S(2)}, u32[]{:S(2)}) collective-permute-start(f32[8,128]{1,0:T(8,128)S(1)} %get-tuple-element.31.refs_0_), channel_id=1, source_target_pairs={{0,12},{4,8},{8,4},{12,0},{16,28},{20,24},{24,20},{28,16},{1,13},{... | collective-permute-start | bytes 12296 | tf_op jit(solution)/shard_map/ppermute | solution.py:21
  149.8 4.5 %collective-permute-start.44 = (f32[8,128]{1,0:T(8,128)S(1)}, f32[8,128]{1,0:T(8,128)S(1)}, u32[]{:S(2)}, u32[]{:S(2)}) collective-permute-start(f32[8,128]{1,0:T(8,128)S(1)} %get-tuple-element.31.refs_0_), channel_id=1, source_target_pairs={{0,16},{4,20},{8,24},{12,28},{16,0},{20,4},{24,8},{28,12},{1,17},{... | collective-permute-start | bytes 12296 | tf_op jit(solution)/shard_map/ppermute | solution.py:21
  151.4 6.0 %collective-permute-start.45 = (f32[8,128]{1,0:T(8,128)S(1)}, f32[8,128]{1,0:T(8,128)S(1)}, u32[]{:S(2)}, u32[]{:S(2)}) collective-permute-start(f32[8,128]{1,0:T(8,128)S(1)} %get-tuple-element.31.refs_0_), channel_id=1, source_target_pairs={{0,20},{4,16},{8,28},{12,24},{16,4},{20,0},{24,12},{28,8},{1,21},{... | collective-permute-start | bytes 12296 | tf_op jit(solution)/shard_map/ppermute | solution.py:21
  153.8 5.4 %collective-permute-start.46 = (f32[8,128]{1,0:T(8,128)S(1)}, f32[8,128]{1,0:T(8,128)S(1)}, u32[]{:S(2)}, u32[]{:S(2)}) collective-permute-start(f32[8,128]{1,0:T(8,128)S(1)} %get-tuple-element.31.refs_0_), channel_id=1, source_target_pairs={{0,24},{4,28},{8,16},{12,20},{16,8},{20,12},{24,0},{28,4},{1,25},{... | collective-permute-start | bytes 12296 | tf_op jit(solution)/shard_map/ppermute | solution.py:21
  154.3 6.3 %collective-permute-start.47 = (f32[8,128]{1,0:T(8,128)S(1)}, f32[8,128]{1,0:T(8,128)S(1)}, u32[]{:S(2)}, u32[]{:S(2)}) collective-permute-start(f32[8,128]{1,0:T(8,128)S(1)} %get-tuple-element.31.refs_0_), channel_id=1, source_target_pairs={{0,28},{4,24},{8,20},{12,16},{16,12},{20,8},{24,4},{28,0},{1,29},{... | collective-permute-start | bytes 12296 | tf_op jit(solution)/shard_map/ppermute | solution.py:21
  (22 other events, 136.9 us)
where the time goes:
time: 163 us; the launch traced here: 162 us
  starting transfers between devices  62.1 us (38%)
  waiting for transfers between devices  57.7 us (35%)
  local copies, waits for them, and re-layouts  13.8 us (8%)
  Pallas kernels  13.6 us (8%)
  other arithmetic  13.5 us (8%)
    ppermute x48, starting transfers between devices, swap(): lax.ppermute(array, axis, [(i, i ^ mask) for i in range(lax.axis_size(axi...  62.1 us
    ppermute x48, waiting for transfers between devices, swap(): lax.ppermute(array, axis, [(i, i ^ mask) for i in range(lax.axis_size(axi...  57.7 us
    pallas_call x6, Pallas kernels, call(): pl.pallas_call(body, out_shape=out_shape, in_specs=[VMEM] * len(operands)...  6.52 us
    unnamed x19, local copies, waits for them, and re-layouts  6.32 us
    ppermute x7, other arithmetic, swap(): lax.ppermute(array, axis, [(i, i ^ mask) for i in range(lax.axis_size(axi...  4.65 us
    pallas_call x2, Pallas kernels, least_squares(): pl.pallas_call(functools.partial(back_body, row_groups), out_shape=(shape...  3.77 us
    pallas_call x4, Pallas kernels, sample(): pl.pallas_call(sample_body, grid=(2, slots // block), out_shape=shape(2,...  3.34 us
  transfers between devices with their start and end apart: 48, of which 24 were waited for; matrix products, arithmetic and copies ran while one was open for 11% of the time, Pallas kernels for 8%

commit v1 on v0

v1 whole, which is shorter than its diff:
```python
import functools

import jax
import jax.numpy as jnp
import numpy as np
from jax import lax
from jax.experimental import pallas as pl
from jax.experimental.pallas import tpu as pltpu
from jax.sharding import PartitionSpec as P

HB = 256
PAIR = 16
ITERS = 2
LANE = 128
CHUNKS = 2
F32 = jnp.float32
VMEM = pl.BlockSpec(memory_space=pltpu.VMEM)


def swap(array, axis, mask):
    return lax.ppermute(array, axis, [(i, i ^ mask) for i in range(lax.axis_size(axis))])


def exchange(copies, axis):
    return lax.all_to_all(copies, axis, split_axis=0, concat_axis=0, tiled=True)


def tree(values):
    while len(values) > 1:
        values = [values[i] + values[i + 1] for i in range(0, len(values), 2)]
    return values[0]


def walsh(size):
    index = np.arange(size)
    common = index[:, None] & index[None, :]
    parity = np.zeros((size, size), np.int64)
    for shift in range(size.bit_length()):
        parity ^= (common >> shift) & 1
    return (1 - 2 * parity).astype(np.float32)


def call(body, out_shape, *operands, scratch=(), flops=0, size=0):
    return pl.pallas_call(
        body,
        out_shape=out_shape,
        in_specs=[VMEM] * len(operands),
        out_specs=jax.tree.map(lambda _: VMEM, out_shape),
        scratch_shapes=scratch,
        compiler_params=pltpu.CompilerParams(vmem_limit_bytes=24 << 20),
        cost_estimate=pl.CostEstimate(flops=flops, bytes_accessed=size, transcendentals=0),
    )(*operands)


def fold_rows(block):
    return block.reshape(block.shape[0] // 8, 8, LANE).sum(axis=0)


def total(rows):
    return jnp.sum(jnp.sum(rows, axis=0, keepdims=True), axis=1, keepdims=True)


def splat(scalar):
    return jnp.broadcast_to(scalar, (1, LANE))


def left_product(vector, matrix_ref, out_ref):
    blocks, tiles = matrix_ref.shape[0] // LANE, matrix_ref.shape[1] // LANE
    sums = [jnp.zeros((8, LANE), F32) for _ in range(tiles)]
    for block in range(blocks):
        across = jnp.broadcast_to(vector[block : block + 1, :], (LANE, LANE)).T
        for tile in range(tiles):
            part = matrix_ref[block * LANE : (block + 1) * LANE, tile * LANE : (tile + 1) * LANE]
            sums[tile] = sums[tile] + fold_rows(part * across)
    for tile in range(tiles):
        out_ref[tile : tile + 1, :] = jnp.sum(sums[tile], axis=0, keepdims=True)


def left_product_long(vector_ref, matrix_ref, out_ref):
    blocks, tiles = matrix_ref.shape[0] // LANE, matrix_ref.shape[1] // LANE

    def step(block, sums):
        across = jnp.broadcast_to(vector_ref[pl.ds(block, 1), :], (LANE, LANE)).T
        rows = pl.ds(pl.multiple_of(block * LANE, LANE), LANE)
        return tuple(
            sums[tile] + fold_rows(matrix_ref[rows, tile * LANE : (tile + 1) * LANE] * across)
            for tile in range(tiles)
        )

    sums = lax.fori_loop(0, blocks, step, tuple(jnp.zeros((8, LANE), F32) for _ in range(tiles)))
    for tile in range(tiles):
        out_ref[tile : tile + 1, :] = jnp.sum(sums[tile], axis=0, keepdims=True)


def right_product(matrix_ref, vector, out_ref):
    blocks, tiles = matrix_ref.shape[0] // LANE, matrix_ref.shape[1] // LANE

    def step(block, carry):
        rows = pl.ds(pl.multiple_of(block * LANE, LANE), LANE)
        sums = jnp.zeros((LANE, LANE), F32)
        for tile in range(tiles):
            sums = sums + matrix_ref[rows, tile * LANE : (tile + 1) * LANE] * vector[tile : tile + 1, :]
        out_ref[pl.ds(block, 1), :] = jnp.sum(fold_rows(sums.T), axis=0, keepdims=True)
        return carry

    lax.fori_loop(0, blocks, step, 0)


def rounded(count, unit):
    return -(-count // unit) * unit


def message_rows(width):
    return rounded(width // LANE + 1, 8)


def copy_out(out_ref):
    first = out_ref[0]
    for index in range(1, out_ref.shape[0]):
        out_ref[index] = first


def signs_across(bits_ref, block):
    signs = (2 * bits_ref[block : block + 1, :] - 1).astype(F32)
    return jnp.broadcast_to(signs, (LANE, LANE)).T


def first_body(design_ref, target_ref, bits_ref, picks_ref, counts_ref, out_ref, *away_refs):
    rows, width = design_ref.shape
    tiles = width // LANE
    target = target_ref[...]
    out_ref[0] = jnp.zeros(out_ref.shape[1:], F32)
    left_product(target, design_ref, out_ref.at[0])
    out_ref[0, tiles : tiles + 1, :] = splat(total(target * target))
    slot = lax.broadcasted_iota(jnp.int32, picks_ref.shape, 1)
    coded = jnp.where(slot < counts_ref[...], picks_ref[...], -1).astype(F32)
    start = message_rows(width)
    out_ref[0, start : start + coded.shape[0], : coded.shape[1]] = coded
    copy_out(out_ref)
    low = lax.axis_index("row") & 1
    half = width // 2
    for chunk, away_ref in enumerate(away_refs):
        piece = away_ref.shape[1]
        for block in range(rows // LANE):
            part = pl.ds(block * LANE, LANE)
            signs = signs_across(bits_ref, block)
            for tile in range(0, piece, LANE):
                column = pl.multiple_of((1 - low) * half + chunk * piece + tile, LANE)
                away_ref[part, tile : tile + LANE] = design_ref[part, pl.ds(column, LANE)] * signs


def back_body(rinv_ref, parts_ref, term_ref, beta_ref, scratch):
    tiles = rinv_ref.shape[0] // LANE
    summed = tree([parts_ref[i, : tiles + 1, :] for i in range(parts_ref.shape[0])])
    beta = jnp.sqrt(summed[tiles : tiles + 1, :])
    beta_ref[...] = beta
    scratch[...] = summed[:tiles, :] / beta
    left_product_long(scratch, rinv_ref, term_ref.at[0])
    copy_out(term_ref)


def forward_body(first, rinv_ref, design_ref, parts_ref, *refs):
    right = tree([parts_ref[i] for i in range(parts_ref.shape[0])])
    if not first:
        before_ref, beta_ref, *refs = refs
        right = right - beta_ref[...] * before_ref[...]
    image_ref, right_ref, held_ref, alpha_ref = refs
    alpha = jnp.sqrt(total(right * right))
    alpha_ref[...] = splat(alpha)
    right = right / alpha
    right_ref[...] = right
    right_product(rinv_ref, right, held_ref)
    right_product(design_ref, held_ref[...], image_ref.at[0])
    copy_out(image_ref)


def turn_body(last, parts_ref, before_ref, beta_ref, alpha_ref, *refs):
    left = tree([parts_ref[i] for i in range(parts_ref.shape[0])])
    left = left - alpha_ref[...] * (before_ref[...] / beta_ref[...])
    square = splat(total(left * left))
    if last:
        left_ref, out_ref = refs
        out_ref[...] = jnp.broadcast_to(square, out_ref.shape)
    else:
        design_ref, left_ref, out_ref = refs
        tiles = design_ref.shape[1] // LANE
        out_ref[0] = jnp.zeros(out_ref.shape[1:], F32)
        left_product(left, design_ref, out_ref.at[0])
        out_ref[0, tiles : tiles + 1, :] = square
        copy_out(out_ref)
    left_ref[...] = left


def last_body(parts_ref, left_ref, *refs):
    betas = [ref[...] for ref in refs[:ITERS]]
    alphas = [ref[...] for ref in refs[ITERS : 2 * ITERS]]
    held = [ref[...] for ref in refs[2 * ITERS : 3 * ITERS]]
    basis_ref, solution_ref = refs[3 * ITERS :]
    last = jnp.sqrt(tree([parts_ref[i] for i in range(parts_ref.shape[0])])[:1, :])
    basis_ref[...] = left_ref[...] / last
    betas.append(last)
    phibar, rhobar = betas[0], alphas[0]
    search, iterate = held[0], jnp.zeros_like(held[0])
    for step in range(ITERS):
        beta = betas[step + 1]
        rho = jnp.sqrt(rhobar * rhobar + beta * beta)
        cosine = rhobar / rho
        sine = beta / rho
        phi = cosine * phibar
        phibar = sine * phibar
        iterate = iterate + phi / rho * search
        if step + 1 < ITERS:
            alpha = alphas[step + 1]
            search = held[step + 1] - sine * alpha / rho * search
            rhobar = -cosine * alpha
    solution_ref[...] = iterate


def shape(*dims):
    return jax.ShapeDtypeStruct(dims, F32)


def mix_body(parts_ref, walsh_ref, order_ref, out_ref):
    groups = parts_ref.shape[0]
    rows = out_ref.shape[3]
    bits = groups.bit_length() - 1
    start = parts_ref.shape[1] - rounded(groups, 8)
    me = lax.axis_index("row")
    local = lax.broadcasted_iota(jnp.int32, (PAIR, rows), 1).astype(F32)

    def step(block, carry):
        coded = parts_ref[block, start : start + rounded(groups, 8), :]
        filler = jnp.zeros((LANE - coded.shape[0], LANE), F32)
        coded = jnp.concatenate([coded, filler], axis=0).T
        parity = jnp.int32(0)
        for bit in range(bits):
            parity = parity ^ ((block & me) >> bit)
        sign = (1 - 2 * (parity & 1)).astype(F32)
        chosen = []
        for owner in range(groups):
            match = jnp.broadcast_to(coded[:PAIR, owner : owner + 1], (PAIR, rows)) == local
            chosen.append(jnp.where(match, sign, 0.0))
        chosen = jnp.concatenate(chosen, axis=0).astype(jnp.bfloat16)
        for part in range(rows // HB):
            columns = slice(part * HB, (part + 1) * HB)
            mixed = jnp.dot(chosen[:, columns], walsh_ref[...], preferred_element_type=F32)
            mixed = mixed.astype(jnp.bfloat16)
            for owner in range(groups):
                apart = owner ^ me
                place = jnp.int32(0)
                for bit in list(range(2, bits)) + [0]:
                    place = 2 * place + ((apart >> bit) & 1)
                place = pl.multiple_of((place * (groups // 2) + (block >> 1)) * PAIR, PAIR)
                rows_here = mixed[owner * PAIR : (owner + 1) * PAIR, :]
                out_ref[(apart >> 1) & 1, block & 1, pl.ds(place, PAIR), columns] = rows_here
        return carry

    lax.fori_loop(0, groups, step, 0)


def sample_body(chunk, design_ref, bits_ref, other_ref, mix_ref, order_ref, send_ref, keep_ref, both):
    rows, piece = other_ref.shape
    half = design_ref.shape[1] // 2
    low = lax.axis_index("row") & 1
    column = pl.multiple_of(low * half + chunk * piece, LANE)
    for block in range(rows // LANE):
        part = slice(block * LANE, (block + 1) * LANE)
        signs = signs_across(bits_ref, block)
        signs = jnp.concatenate([signs] * (piece // LANE), axis=1)
        mine = design_ref[part, pl.ds(column, piece)] * signs
        other = other_ref[part, :]
        for index, value in enumerate((mine + other, mine - other)):
            high = value.astype(jnp.bfloat16)
            both[index, 0, part, :] = high
            both[index, 1, part, :] = (value - high.astype(F32)).astype(jnp.bfloat16)
    slots = mix_ref.shape[2]
    block = min(slots, HB)

    def step(place, carry):
        part = pl.ds(pl.multiple_of(place * block, block), block)
        for apart, out_ref in enumerate((keep_ref, send_ref)):
            for index in range(2):
                mix = mix_ref[apart, index, part, :]
                high = jnp.dot(mix, both[index, 0], preferred_element_type=F32)
                low = jnp.dot(mix, both[index, 1], preferred_element_type=F32)
                out_ref[index, part, :] = high + low
        return carry

    if slots == block:
        step(0, 0)
    else:
        lax.fori_loop(0, slots // block, step, 0)


def halve_body(kept_ref, arrived_ref, order_ref, send_ref, keep_ref):
    slots = keep_ref.shape[1]
    keep_ref[...] = kept_ref[:, :slots, :] + arrived_ref[:, :slots, :]
    send_ref[...] = kept_ref[:, slots:, :] + arrived_ref[:, slots:, :]


def assemble_body(chunks, scale, *refs):
    mine, other, out_ref = refs[:chunks], refs[chunks : 2 * chunks], refs[-1]
    low = lax.axis_index("row") & 1
    half = out_ref.shape[1] // 2
    for chunk in range(chunks):
        piece = mine[chunk].shape[2]
        for refs_here, place in ((mine, low), (other, 1 - low)):
            column = pl.ds(pl.multiple_of(place * half + chunk * piece, LANE), piece)
            for block in range(mine[chunk].shape[1] // PAIR):
                for index in range(2):
                    value = refs_here[chunk][index, block * PAIR : (block + 1) * PAIR, :]
                    out_ref[(2 * block + index) * PAIR : (2 * block + index + 1) * PAIR, column] = value / scale


def shape(*dims, dtype=F32):
    return jax.ShapeDtypeStruct(dims, dtype)


def shards(design, sign_bits, picks, counts, target, rinv):
    rows, width = design.shape
    whole = rinv.shape[1]
    row_groups, col_groups = lax.axis_size("row"), lax.axis_size("col")
    bits = row_groups.bit_length() - 1
    lines, half = rows // LANE, width // 2
    chunks = min(CHUNKS, half // LANE)
    piece = half // chunks
    big, small = rinv.size, design.size
    scalar = shape(1, LANE)
    deep = message_rows(width)
    sign_bits = sign_bits.reshape(lines, LANE)
    left = target.reshape(lines, LANE)

    message, *away = call(
        first_body,
        (shape(row_groups, deep + rounded(row_groups, 8), LANE),) + (shape(rows, piece),) * chunks,
        design,
        left,
        sign_bits,
        picks.reshape(row_groups, PAIR),
        counts,
        flops=2 * small,
        size=4 * small,
    )

    def sample(chunk, order):
        slots = row_groups * row_groups * PAIR // 4
        return call(
            functools.partial(sample_body, chunk),
            (shape(2, slots, piece),) * 2,
            design,
            sign_bits,
            arrived[chunk],
            mix,
            order,
            scratch=[pltpu.VMEM((2, 2, rows, piece), jnp.bfloat16)],
            flops=16 * slots * rows * piece,
            size=8 * rows * piece,
        )

    def halve(kept, arrived, order):
        slots = kept.shape[1] // 2
        return call(halve_body, (shape(2, slots, piece),) * 2, kept, arrived, order, size=12 * kept.size)

    def back(message):
        return call(
            back_body,
            (shape(col_groups, whole // LANE, LANE), scalar),
            rinv,
            message,
            scratch=[pltpu.VMEM((width // LANE, LANE), F32)],
            flops=2 * big,
            size=4 * big,
        )

    def forward(terms, *before):
        return call(
            functools.partial(forward_body, not before),
            (
                shape(col_groups, lines, LANE),
                shape(whole // LANE, LANE),
                shape(width // LANE, LANE),
                scalar,
            ),
            rinv,
            design,
            terms,
            *before,
            flops=2 * big,
            size=4 * big,
        )

    def turn(images, left, beta, alpha, last):
        return call(
            functools.partial(turn_body, last),
            (shape(lines, LANE), shape(row_groups, 8 if last else deep, LANE)),
            images,
            left,
            beta,
            alpha,
            *(() if last else (design,)),
            flops=2 * small,
            size=0 if last else 4 * small,
        )

    betas, alphas, held = [], [], []
    message = exchange(message, "row")
    arrived = [swap(part, "row", 1) for part in away]
    mix, sent, kept = None, [], []
    right = None
    for step in range(ITERS):
        term, beta = back(message)
        betas.append(beta)
        if step == 0:
            mix = call(
                mix_body,
                shape(2, 2, row_groups * row_groups * PAIR // 4, rows, dtype=jnp.bfloat16),
                message,
                jnp.asarray(walsh(HB), jnp.bfloat16),
                beta,
                size=4 * small,
            )
        else:
            for chunk in range(1, chunks):
                send, keep = sample(chunk, beta)
                sent.append(swap(send, "row", 2))
                kept.append(keep)
        terms = exchange(term, "col")
        image, right, part, alpha = forward(terms, *(() if step == 0 else (right, beta)))
        alphas.append(alpha)
        held.append(part)
        if step == 0:
            send, keep = sample(0, alpha)
            sent.append(swap(send, "row", 2))
            kept.append(keep)
        images = exchange(image, "col")
        left, message = turn(images, left, beta, alpha, step + 1 == ITERS)
        message = exchange(message, "row")
    basis, answer = call(
        last_body, (shape(lines, LANE), shape(width // LANE, LANE)), message, left, *betas, *alphas, *held
    )
    mine, other = [], []
    for chunk in range(chunks):
        keep, come = kept[chunk], sent[chunk]
        for bit in range(2, bits):
            send, keep = halve(keep, come, alpha)
            come = swap(send, "row", 1 << bit)
        send, keep = halve(keep, come, alpha)
        mine.append(keep)
        other.append(swap(send, "row", 1))
    scale = float(np.sqrt(np.float32(rows * row_groups)))
    sketch = call(
        functools.partial(assemble_body, chunks, scale), shape(row_groups * PAIR, width), *mine, *other
    )
    return (sketch, answer.reshape(-1), basis.reshape(-1))


def solution(mesh):
    placed = (
        P("row", "col"),
        P("row"),
        P(None, "row", None),
        P(None, "row"),
        P("row"),
        P("col", None),
    )
    return jax.shard_map(
        shards,
        mesh=mesh,
        in_specs=placed,
        out_specs=(P("row", "col"), P("col"), P("row")),
        check_vma=False,
    )
```

time: 163 us -> 141 us (0.87)
  blocking collectives: 0 us -> 61 us
  starting transfers between devices: 62.1 us -> 12.4 us
  waiting for transfers between devices: 57.7 us -> 30.2 us
  other arithmetic: 13.5 us -> 0 us
  Pallas kernels: 13.6 us -> 20.1 us
  local copies, waits for them, and re-layouts: 13.8 us -> 15.9 us
    all_to_all x0 -> x6, blocking collectives: none -> 61 us  [exchange(): return lax.all_to_all(copies, axis, split_axis=0, concat_axis=0, tiled=True)]
    ppermute x48 -> x8, starting transfers between devices: 62.1 us -> 6.54 us  [swap(): lax.ppermute(array, axis, [(i, i ^ mask) for i in range(lax.axis_size(axi...]
    ppermute x48 -> x8, waiting for transfers between devices: 57.7 us -> 25.8 us  [swap(): lax.ppermute(array, axis, [(i, i ^ mask) for i in range(lax.axis_size(axi...]
    pallas_call x6 -> x16, Pallas kernels: 6.52 us -> 20.1 us  [call(): pl.pallas_call(body, out_shape=out_shape, in_specs=[VMEM] * len(operands)...]
    unnamed x19 -> x25, local copies, waits for them, and re-layouts: 6.32 us -> 15.9 us
    pallas_call x6 -> x0, Pallas kernels: 7.1 us -> none  [the longest x2 3.77 us: least_squares(): pl.pallas_call(functools.partial(back_body, row_groups), out_shape=(shape...]
    all_to_all x0 -> x1, starting transfers between devices: none -> 5.9 us  [exchange(): return lax.all_to_all(copies, axis, split_axis=0, concat_axis=0, tiled=True)]
    ppermute x7 -> x0, other arithmetic: 4.65 us -> none  [swap(): lax.ppermute(array, axis, [(i, i ^ mask) for i in range(lax.axis_size(axi...]
  transfers between devices with their start and end apart: 48 -> 9, of which waited for: 24 -> 4; matrix products, arithmetic and copies ran while one was open for 11% -> 0% of each run, Pallas kernels for 8% -> 13%
where the time goes in v1:
time: 141 us; the launch traced here: 140 us
  blocking collectives  61 us (43%)
  waiting for transfers between devices  30.2 us (21%)
  Pallas kernels  20.1 us (14%)
  local copies, waits for them, and re-layouts  15.9 us (11%)
  starting transfers between devices  12.4 us (9%)
    all_to_all x6, blocking collectives, exchange(): return lax.all_to_all(copies, axis, split_axis=0, concat_axis=0, tiled=True)  61 us
    ppermute x8, waiting for transfers between devices, swap(): lax.ppermute(array, axis, [(i, i ^ mask) for i in range(lax.axis_size(axi...  25.8 us
    pallas_call x16, Pallas kernels, call(): pl.pallas_call(body, out_shape=out_shape, in_specs=[VMEM] * len(operands)...  20.1 us
    unnamed x25, local copies, waits for them, and re-layouts  15.9 us
    ppermute x8, starting transfers between devices, swap(): lax.ppermute(array, axis, [(i, i ^ mask) for i in range(lax.axis_size(axi...  6.54 us
    all_to_all x1, starting transfers between devices, exchange(): return lax.all_to_all(copies, axis, split_axis=0, concat_axis=0, tiled=True)  5.9 us
    all_to_all x1, waiting for transfers between devices, exchange(): return lax.all_to_all(copies, axis, split_axis=0, concat_axis=0, tiled=True)  4.42 us
  transfers between devices with their start and end apart: 9, of which 4 were waited for; matrix products, arithmetic and copies ran while one was open for 0% of the time, Pallas kernels for 13%

profile of v1, /device:TPU:0, one launch (start us, length us, event | category | flops | bytes accessed | tf_op | source)
XLA Modules:
  0.0 140.4 jit_solution(10118411321341106754)
XLA Ops:
  0.6 0.7 copy.10.counts_ref
  1.4 1.6 %copy-done.4 = f32[512,1024]{1,0:T(8,128)S(1)} copy-done((f32[512,1024]{1,0:T(8,128)S(1)}, f32[512,1024]{1,0:T(8,128)}, u32[]{:S(2)}) %copy-start.4) | copy-done | bytes 2097176
  3.0 0.7 copy-done.7
  3.6 0.7 copy-done.9
  4.3 0.7 copy-done.11
  5.0 1.3 shard_map.94
  6.3 3.0 %collective-permute-start.3 = (f32[512,256]{1,0:T(8,128)}, f32[512,256]{1,0:T(8,128)}, u32[]{:S(2)}, u32[]{:S(2)}) collective-permute-start(f32[512,256]{1,0:T(8,128)} %get-tuple-element.51), channel_id=1, source_target_pairs={{0,4},{4,0},{8,12},{12,8},{16,20},{20,16},{24,28},{28,24},{1,5},{5... | collective-permute-start | bytes 1572872 | tf_op jit(solution)/shard_map/ppermute | solution.py:21
  9.3 24.4 %all_to_all.35.parts_ref = f32[8,24,128]{2,1,0:T(8,128)S(1)} all-to-all(f32[8,24,128]{2,1,0:T(8,128)S(1)} %get-tuple-element.36), channel_id=1, replica_groups=mesh['row'=8,'col'=4] {'row'}, dimensions={0} | all-to-all | bytes 196608 | tf_op jit(solution)/shard_map/all_to_all | solution.py:25
  33.7 5.8 %copy-done = f32[1024,4096]{1,0:T(8,128)S(1)} copy-done((f32[1024,4096]{1,0:T(8,128)S(1)}, f32[1024,4096]{1,0:T(8,128)}, u32[]{:S(2)}) %copy-start) | copy-done | bytes 16777240
  39.4 1.8 %shard_map.95 = (f32[4,32,128]{2,1,0:T(8,128)S(1)}, f32[1,128]{1,0:T(1,128)S(1)}) custom-call(f32[1024,4096]{1,0:T(8,128)S(1)} %copy-done, f32[8,24,128]{2,1,0:T(8,128)S(1)} %all_to_all.35.parts_ref), custom_call_target="tpu_custom_call" | custom-call | flops 8388608 | bytes 16777216 | tf_op jit(solution)/shard_map/pallas_call | solution.py:44
  41.3 7.2 %all_to_all.36.parts_ref = f32[4,32,128]{2,1,0:T(8,128)S(1)} all-to-all(f32[4,32,128]{2,1,0:T(8,128)S(1)} %get-tuple-element.38), channel_id=1, replica_groups=mesh['row'=8,'col'=4] {'col'}, dimensions={0} | all-to-all | bytes 131072 | tf_op jit(solution)/shard_map/all_to_all | solution.py:25
  48.4 2.4 %shard_map.97 = (f32[4,4,128]{2,1,0:T(4,128)S(1)}, f32[32,128]{1,0:T(8,128)S(1)}, f32[8,128]{1,0:T(8,128)S(1)}, f32[1,128]{1,0:T(1,128)S(1)}) custom-call(f32[1024,4096]{1,0:T(8,128)S(1)} %copy-done.1, f32[512,1024]{1,0:T(8,128)S(1)} %copy-done.5, f32[4,32,128]{2,1,0:T(8,128)S(1)} %all_to_all.36.parts_ref), custom_call_target="tpu_custom_call" | custom-call | flops 8388608 | bytes 16777216 | tf_op jit(solution)/shard_map/pallas_call | solution.py:44
  50.9 6.2 %all_to_all.37.parts_ref = f32[4,4,128]{2,1,0:T(4,128)S(1)} all-to-all(f32[4,4,128]{2,1,0:T(4,128)S(1)} %get-tuple-element.42), channel_id=1, replica_groups=mesh['row'=8,'col'=4] {'col'}, dimensions={0} | all-to-all | bytes 16384 | tf_op jit(solution)/shard_map/all_to_all | solution.py:25
  57.0 0.8 shard_map.99
  57.9 5.9 %all-to-all-start.3 = ((f32[8,16,128]{2,1,0:T(8,128)}), f32[8,16,128]{2,1,0:T(8,128)S(1)}, u32[]{:S(2)}, u32[]{:S(2)}) async-start(f32[8,16,128]{2,1,0:T(8,128)} %get-tuple-element.43), calls=%async_computation.3 | async-start | bytes 131072 | tf_op jit(solution)/shard_map/all_to_all | solution.py:25
  63.8 2.5 %shard_map.96.mix_ref = bf16[2,2,256,512]{3,2,1,0:T(8,128)(2,1)S(1)} custom-call(f32[8,24,128]{2,1,0:T(8,128)S(1)} %all_to_all.35.parts_ref, bf16[256,256]{1,0:T(8,128)(2,1)S(1)} %copy-done.6, f32[1,128]{1,0:T(1,128)S(1)} %get-tuple-element.37.order_ref.beta_ref.refs_0_), custom_call_target="tpu_custom_call" | custom-call | bytes 2097152 | tf_op jit(solution)/shard_map/pallas_call | solution.py:44
  66.2 4.4 %all-to-all-done.3.parts_ref = f32[8,16,128]{2,1,0:T(8,128)S(1)} async-done(((f32[8,16,128]{2,1,0:T(8,128)}), f32[8,16,128]{2,1,0:T(8,128)S(1)}, u32[]{:S(2)}, u32[]{:S(2)}) %all-to-all-start.3) | async-done | bytes 65568 | tf_op jit(solution)/shard_map/all_to_all | solution.py:25
  70.7 5.8 %copy-done.2 = f32[1024,4096]{1,0:T(8,128)S(1)} copy-done((f32[1024,4096]{1,0:T(8,128)S(1)}, f32[1024,4096]{1,0:T(8,128)}, u32[]{:S(2)}) %copy-start.2) | copy-done | bytes 16777240
  76.4 1.8 %shard_map.100 = (f32[4,32,128]{2,1,0:T(8,128)S(1)}, f32[1,128]{1,0:T(1,128)S(1)}) custom-call(f32[1024,4096]{1,0:T(8,128)S(1)} %copy-done.2, f32[8,16,128]{2,1,0:T(8,128)S(1)} %all-to-all-done.3.parts_ref), custom_call_target="tpu_custom_call" | custom-call | flops 8388608 | bytes 16777216 | tf_op jit(solution)/shard_map/pallas_call | solution.py:44
  78.3 2.7 %shard_map.104 = (f32[2,256,256]{2,1,0:T(8,128)S(1)}, f32[2,256,256]{2,1,0:T(8,128)S(1)}) custom-call(f32[512,1024]{1,0:T(8,128)S(1)} %copy-done.5, s32[4,128]{1,0:T(4,128)S(1)} %bitcast.6, f32[512,256]{1,0:T(8,128)} %collective-permute-done.3.other_ref, bf16[2,2,256,512]{3,2,1,0:T(8,128)(2,1)S(1)} %shard_map.96.mix_ref, ...), custom_call_target="tpu_custom_call" | custom-call | flops 536870912 | bytes 1048576 | tf_op jit(solution)/shard_map/pallas_call | solution.py:44
  81.2 2.0 %shard_map.98 = (f32[2,256,256]{2,1,0:T(8,128)S(1)}, f32[2,256,256]{2,1,0:T(8,128)S(1)}) custom-call(f32[512,1024]{1,0:T(8,128)S(1)} %copy-done.5, s32[4,128]{1,0:T(4,128)S(1)} %bitcast.7, f32[512,256]{1,0:T(8,128)} %collective-permute-done.other_ref, bf16[2,2,256,512]{3,2,1,0:T(8,128)(2,1)S(1)} %shard_map.96.mix_ref, ...), custom_call_target="tpu_custom_call" | custom-call | flops 536870912 | bytes 1048576 | tf_op jit(solution)/shard_map/pallas_call | solution.py:44
  83.3 1.7 %collective-permute-start.1 = (f32[2,256,256]{2,1,0:T(8,128)S(1)}, f32[2,256,256]{2,1,0:T(8,128)S(1)}, u32[]{:S(2)}, u32[]{:S(2)}) collective-permute-start(f32[2,256,256]{2,1,0:T(8,128)S(1)} %get-tuple-element.41), channel_id=1, source_target_pairs={{0,8},{4,12},{8,0},{12,4},{16,24},{20,28},{24,16},{28,20},{1,9},{5... | collective-permute-start | bytes 1572872 | tf_op jit(solution)/shard_map/ppermute | solution.py:21
  85.0 6.5 %all_to_all.38.parts_ref = f32[4,32,128]{2,1,0:T(8,128)S(1)} all-to-all(f32[4,32,128]{2,1,0:T(8,128)S(1)} %get-tuple-element.44), channel_id=1, replica_groups=mesh['row'=8,'col'=4] {'col'}, dimensions={0} | all-to-all | bytes 131072 | tf_op jit(solution)/shard_map/all_to_all | solution.py:25
  91.5 3.0 %shard_map.101 = (f32[4,4,128]{2,1,0:T(4,128)S(1)}, f32[32,128]{1,0:T(8,128)}, f32[8,128]{1,0:T(8,128)S(1)}, f32[1,128]{1,0:T(1,128)S(1)}) custom-call(f32[1024,4096]{1,0:T(8,128)S(1)} %copy-done.3, f32[512,1024]{1,0:T(8,128)S(1)} %copy-done.5, f32[4,32,128]{2,1,0:T(8,128)S(1)} %all_to_all.38.parts_ref, f32[32,128]{1,0:T(8,128)S(1)} %get-tuple-element.45.refs_0_, ...), custom_call_target="tpu_custom_call" | custom-call | flops 8388608 | bytes 16777216 | tf_op jit(solution)/shard_map/pallas_call | solution.py:44
  94.5 1.4 collective-permute-done.4.arrived_ref
  95.9 0.5 collective-permute-start.5
  96.5 13.6 %collective-permute-done.1.arrived_ref = f32[2,256,256]{2,1,0:T(8,128)S(1)} collective-permute-done((f32[2,256,256]{2,1,0:T(8,128)S(1)}, f32[2,256,256]{2,1,0:T(8,128)S(1)}, u32[]{:S(2)}, u32[]{:S(2)}) %collective-permute-start.1) | collective-permute-done | bytes 524320 | tf_op jit(solution)/shard_map/ppermute | solution.py:21
  110.7 10.8 %collective-permute-done.2.arrived_ref = f32[2,128,256]{2,1,0:T(8,128)S(1)} collective-permute-done((f32[2,128,256]{2,1,0:T(8,128)S(1)}, f32[2,128,256]{2,1,0:T(8,128)S(1)}, u32[]{:S(2)}, u32[]{:S(2)}) %collective-permute-start.2) | collective-permute-done | bytes 262176 | tf_op jit(solution)/shard_map/ppermute | solution.py:21
  122.0 6.1 %all_to_all.39.parts_ref = f32[4,4,128]{2,1,0:T(4,128)S(1)} all-to-all(f32[4,4,128]{2,1,0:T(4,128)S(1)} %get-tuple-element.59), channel_id=1, replica_groups=mesh['row'=8,'col'=4] {'col'}, dimensions={0} | all-to-all | bytes 16384 | tf_op jit(solution)/shard_map/all_to_all | solution.py:25
  128.2 10.7 %all_to_all.40.parts_ref = f32[8,8,128]{2,1,0:T(8,128)S(1)} all-to-all(f32[8,8,128]{2,1,0:T(8,128)S(1)} %get-tuple-element.61), channel_id=1, replica_groups=mesh['row'=8,'col'=4] {'row'}, dimensions={0} | all-to-all | bytes 65536 | tf_op jit(solution)/shard_map/all_to_all | solution.py:25
  138.9 0.6 shard_map.109
  139.6 0.8 shard_map.107
  (33 shorter events, 1.6 us)
Async XLA Ops:
  1.4 1.6 %copy-start.4 = (f32[512,1024]{1,0:T(8,128)S(1)}, f32[512,1024]{1,0:T(8,128)}, u32[]{:S(2)}) copy-start(f32[512,1024]{1,0:T(8,128)} %design_ref.9) | copy-start | bytes 6291460
  3.0 0.7 copy-start.7
  3.6 0.7 copy-start.9
  4.3 0.7 copy-start.11
  5.0 43.4 %copy-start.5 = (f32[512,1024]{1,0:T(8,128)S(1)}, f32[512,1024]{1,0:T(8,128)}, u32[]{:S(2)}) copy-start(f32[512,1024]{1,0:T(8,128)} %design_ref.9) | copy-start | bytes 6291460
  6.3 72.0 %collective-permute-start.3 = (f32[512,256]{1,0:T(8,128)}, f32[512,256]{1,0:T(8,128)}, u32[]{:S(2)}, u32[]{:S(2)}) collective-permute-start(f32[512,256]{1,0:T(8,128)} %get-tuple-element.51), channel_id=1, source_target_pairs={{0,4},{4,0},{8,12},{12,8},{16,20},{20,16},{24,28},{28,24},{1,5},{5... | collective-permute-start | bytes 1572872 | tf_op jit(solution)/shard_map/ppermute | solution.py:21
  9.2 72.0 %collective-permute-start = (f32[512,256]{1,0:T(8,128)}, f32[512,256]{1,0:T(8,128)}, u32[]{:S(2)}, u32[]{:S(2)}) collective-permute-start(f32[512,256]{1,0:T(8,128)} %get-tuple-element.35), channel_id=1, source_target_pairs={{0,4},{4,0},{8,12},{12,8},{16,20},{20,16},{24,28},{28,24},{1,5},{5... | collective-permute-start | bytes 1572872 | tf_op jit(solution)/shard_map/ppermute | solution.py:21
  33.7 5.8 %copy-start = (f32[1024,4096]{1,0:T(8,128)S(1)}, f32[1024,4096]{1,0:T(8,128)}, u32[]{:S(2)}) copy-start(f32[1024,4096]{1,0:T(8,128)} %rinv_ref.7) | copy-start | bytes 50331652
  39.4 9.0 %copy-start.1 = (f32[1024,4096]{1,0:T(8,128)S(1)}, f32[1024,4096]{1,0:T(8,128)}, u32[]{:S(2)}) copy-start(f32[1024,4096]{1,0:T(8,128)} %rinv_ref.7) | copy-start | bytes 50331652
  39.4 17.6 %copy-start.10 = (f32[512]{0:T(512)S(1)}, f32[512]{0:T(512)}, u32[]{:S(2)}) copy-start(f32[512]{0:T(512)} %param.11) | copy-start | bytes 6148
  39.4 24.3 %copy-start.6 = (bf16[256,256]{1,0:T(8,128)(2,1)S(1)}, bf16[256,256]{1,0:T(8,128)(2,1)}, u32[]{:S(2)}) copy-start(bf16[256,256]{1,0:T(8,128)(2,1)} %constant.2.clone.walsh_ref) | copy-start | bytes 393220
  48.4 29.8 %copy-start.8 = (s32[512]{0:T(512)S(1)}, s32[512]{0:T(512)}, u32[]{:S(2)}) copy-start(s32[512]{0:T(512)} %param.8) | copy-start | bytes 6148
  57.9 12.8 %all-to-all-start.3 = ((f32[8,16,128]{2,1,0:T(8,128)}), f32[8,16,128]{2,1,0:T(8,128)S(1)}, u32[]{:S(2)}, u32[]{:S(2)}) async-start(f32[8,16,128]{2,1,0:T(8,128)} %get-tuple-element.43), calls=%async_computation.3 | async-start | bytes 131072 | tf_op jit(solution)/shard_map/all_to_all | solution.py:25
  70.7 5.8 %copy-start.2 = (f32[1024,4096]{1,0:T(8,128)S(1)}, f32[1024,4096]{1,0:T(8,128)}, u32[]{:S(2)}) copy-start(f32[1024,4096]{1,0:T(8,128)} %rinv_ref.7) | copy-start | bytes 50331652
  76.4 15.1 %copy-start.3 = (f32[1024,4096]{1,0:T(8,128)S(1)}, f32[1024,4096]{1,0:T(8,128)}, u32[]{:S(2)}) copy-start(f32[1024,4096]{1,0:T(8,128)} %rinv_ref.7) | copy-start | bytes 50331652
  80.9 14.9 %collective-permute-start.4 = (f32[2,256,256]{2,1,0:T(8,128)S(1)}, f32[2,256,256]{2,1,0:T(8,128)S(1)}, u32[]{:S(2)}, u32[]{:S(2)}) collective-permute-start(f32[2,256,256]{2,1,0:T(8,128)S(1)} %get-tuple-element.53), channel_id=1, source_target_pairs={{0,8},{4,12},{8,0},{12,4},{16,24},{20,28},{24,16},{28,20},{1,9},{5... | collective-permute-start | bytes 1572872 | tf_op jit(solution)/shard_map/ppermute | solution.py:21
  83.3 26.8 %collective-permute-start.1 = (f32[2,256,256]{2,1,0:T(8,128)S(1)}, f32[2,256,256]{2,1,0:T(8,128)S(1)}, u32[]{:S(2)}, u32[]{:S(2)}) collective-permute-start(f32[2,256,256]{2,1,0:T(8,128)S(1)} %get-tuple-element.41), channel_id=1, source_target_pairs={{0,8},{4,12},{8,0},{12,4},{16,24},{20,28},{24,16},{28,20},{1,9},{5... | collective-permute-start | bytes 1572872 | tf_op jit(solution)/shard_map/ppermute | solution.py:21
  95.9 14.3 %collective-permute-start.5 = (f32[2,128,256]{2,1,0:T(8,128)S(1)}, f32[2,128,256]{2,1,0:T(8,128)S(1)}, u32[]{:S(2)}, u32[]{:S(2)}) collective-permute-start(f32[2,128,256]{2,1,0:T(8,128)S(1)} %get-tuple-element.55), channel_id=1, source_target_pairs={{0,16},{4,20},{8,24},{12,28},{16,0},{20,4},{24,8},{28,12},{1,17},{... | collective-permute-start | bytes 786440 | tf_op jit(solution)/shard_map/ppermute | solution.py:21
  110.1 11.4 %collective-permute-start.2 = (f32[2,128,256]{2,1,0:T(8,128)S(1)}, f32[2,128,256]{2,1,0:T(8,128)S(1)}, u32[]{:S(2)}, u32[]{:S(2)}) collective-permute-start(f32[2,128,256]{2,1,0:T(8,128)S(1)} %get-tuple-element.49), channel_id=1, source_target_pairs={{0,16},{4,20},{8,24},{12,28},{16,0},{20,4},{24,8},{28,12},{1,17},{... | collective-permute-start | bytes 786440 | tf_op jit(solution)/shard_map/ppermute | solution.py:21
  110.2 29.3 %collective-permute-start.7 = (f32[2,64,256]{2,1,0:T(8,128)S(1)}, f32[2,64,256]{2,1,0:T(8,128)S(1)}, u32[]{:S(2)}, u32[]{:S(2)}) collective-permute-start(f32[2,64,256]{2,1,0:T(8,128)S(1)} %get-tuple-element.58), channel_id=1, source_target_pairs={{0,4},{4,0},{8,12},{12,8},{16,20},{20,16},{24,28},{28,24},{1,5},{5... | collective-permute-start | bytes 393224 | tf_op jit(solution)/shard_map/ppermute | solution.py:21
  121.5 18.0 %collective-permute-start.6 = (f32[2,64,256]{2,1,0:T(8,128)S(1)}, f32[2,64,256]{2,1,0:T(8,128)S(1)}, u32[]{:S(2)}, u32[]{:S(2)}) collective-permute-start(f32[2,64,256]{2,1,0:T(8,128)S(1)} %get-tuple-element.57), channel_id=1, source_target_pairs={{0,4},{4,0},{8,12},{12,8},{16,20},{20,16},{24,28},{28,24},{1,5},{5... | collective-permute-start | bytes 393224 | tf_op jit(solution)/shard_map/ppermute | solution.py:21

commit v2 on v1

v2 whole, which is shorter than its diff:
```python
import functools

import jax
import jax.numpy as jnp
import numpy as np
from jax import lax
from jax.experimental import pallas as pl
from jax.experimental.pallas import tpu as pltpu
from jax.sharding import PartitionSpec as P

HB = 256
PAIR = 16
ITERS = 2
LANE = 128
F32 = jnp.float32
VMEM = pl.BlockSpec(memory_space=pltpu.VMEM)


def exchange(copies, axis):
    return lax.all_to_all(copies, axis, split_axis=0, concat_axis=0, tiled=True)


def direct(array, axis):
    size = lax.axis_size(axis)
    return [array] + [
        lax.ppermute(array, axis, [(i, i ^ mask) for i in range(size)]) for mask in range(1, size)
    ]


def tree(values):
    while len(values) > 1:
        values = [values[i] + values[i + 1] for i in range(0, len(values), 2)]
    return values[0]


def walsh(size):
    index = np.arange(size)
    common = index[:, None] & index[None, :]
    parity = np.zeros((size, size), np.int64)
    for shift in range(size.bit_length()):
        parity ^= (common >> shift) & 1
    return (1 - 2 * parity).astype(np.float32)


def call(body, out_shape, *operands, scratch=(), flops=0, size=0):
    return pl.pallas_call(
        body,
        out_shape=out_shape,
        in_specs=[VMEM] * len(operands),
        out_specs=jax.tree.map(lambda _: VMEM, out_shape),
        scratch_shapes=scratch,
        compiler_params=pltpu.CompilerParams(vmem_limit_bytes=24 << 20),
        cost_estimate=pl.CostEstimate(flops=flops, bytes_accessed=size, transcendentals=0),
    )(*operands)


def fold_rows(block):
    return block.reshape(block.shape[0] // 8, 8, LANE).sum(axis=0)


def total(rows):
    return jnp.sum(jnp.sum(rows, axis=0, keepdims=True), axis=1, keepdims=True)


def splat(scalar):
    return jnp.broadcast_to(scalar, (1, LANE))


def left_product(vector, matrix_ref, out_ref):
    blocks, tiles = matrix_ref.shape[0] // LANE, matrix_ref.shape[1] // LANE
    sums = [jnp.zeros((8, LANE), F32) for _ in range(tiles)]
    for block in range(blocks):
        across = jnp.broadcast_to(vector[block : block + 1, :], (LANE, LANE)).T
        for tile in range(tiles):
            part = matrix_ref[block * LANE : (block + 1) * LANE, tile * LANE : (tile + 1) * LANE]
            sums[tile] = sums[tile] + fold_rows(part * across)
    for tile in range(tiles):
        out_ref[tile : tile + 1, :] = jnp.sum(sums[tile], axis=0, keepdims=True)


def left_product_long(vector_ref, matrix_ref, out_ref):
    blocks, tiles = matrix_ref.shape[0] // LANE, matrix_ref.shape[1] // LANE

    def step(block, sums):
        across = jnp.broadcast_to(vector_ref[pl.ds(block, 1), :], (LANE, LANE)).T
        rows = pl.ds(pl.multiple_of(block * LANE, LANE), LANE)
        return tuple(
            sums[tile] + fold_rows(matrix_ref[rows, tile * LANE : (tile + 1) * LANE] * across)
            for tile in range(tiles)
        )

    sums = lax.fori_loop(0, blocks, step, tuple(jnp.zeros((8, LANE), F32) for _ in range(tiles)))
    for tile in range(tiles):
        out_ref[tile : tile + 1, :] = jnp.sum(sums[tile], axis=0, keepdims=True)


def right_product(matrix_ref, vector, out_ref):
    blocks, tiles = matrix_ref.shape[0] // LANE, matrix_ref.shape[1] // LANE

    def step(block, carry):
        rows = pl.ds(pl.multiple_of(block * LANE, LANE), LANE)
        sums = jnp.zeros((LANE, LANE), F32)
        for tile in range(tiles):
            sums = sums + matrix_ref[rows, tile * LANE : (tile + 1) * LANE] * vector[tile : tile + 1, :]
        out_ref[pl.ds(block, 1), :] = jnp.sum(fold_rows(sums.T), axis=0, keepdims=True)
        return carry

    lax.fori_loop(0, blocks, step, 0)


def rounded(count, unit):
    return -(-count // unit) * unit


def message_rows(width):
    return rounded(width // LANE + 1, 8)


def copy_out(out_ref):
    first = out_ref[0]
    for index in range(1, out_ref.shape[0]):
        out_ref[index] = first


def signs_across(bits_ref, block):
    signs = (2 * bits_ref[block : block + 1, :] - 1).astype(F32)
    return jnp.broadcast_to(signs, (LANE, LANE)).T


def first_body(design_ref, target_ref, picks_ref, counts_ref, out_ref):
    width = design_ref.shape[1]
    tiles = width // LANE
    target = target_ref[...]
    out_ref[0] = jnp.zeros(out_ref.shape[1:], F32)
    left_product(target, design_ref, out_ref.at[0])
    out_ref[0, tiles : tiles + 1, :] = splat(total(target * target))
    slot = lax.broadcasted_iota(jnp.int32, picks_ref.shape, 1)
    coded = jnp.where(slot < counts_ref[...], picks_ref[...], -1).astype(F32)
    start = message_rows(width)
    out_ref[0, start : start + coded.shape[0], : coded.shape[1]] = coded
    copy_out(out_ref)


def back_body(rinv_ref, parts_ref, term_ref, beta_ref, scratch):
    tiles = rinv_ref.shape[0] // LANE
    summed = tree([parts_ref[i, : tiles + 1, :] for i in range(parts_ref.shape[0])])
    beta = jnp.sqrt(summed[tiles : tiles + 1, :])
    beta_ref[...] = beta
    scratch[...] = summed[:tiles, :] / beta
    left_product_long(scratch, rinv_ref, term_ref)


def forward_body(groups, first, rinv_ref, design_ref, *refs):
    right = tree([ref[...] for ref in refs[:groups]])
    refs = refs[groups:]
    if not first:
        before_ref, beta_ref, *refs = refs
        right = right - beta_ref[...] * before_ref[...]
    image_ref, right_ref, held_ref, alpha_ref = refs
    alpha = jnp.sqrt(total(right * right))
    alpha_ref[...] = splat(alpha)
    right = right / alpha
    right_ref[...] = right
    right_product(rinv_ref, right, held_ref)
    right_product(design_ref, held_ref[...], image_ref)


def turn_body(groups, last, *refs):
    left = tree([ref[...] for ref in refs[:groups]])
    before_ref, beta_ref, alpha_ref, *refs = refs[groups:]
    left = left - alpha_ref[...] * (before_ref[...] / beta_ref[...])
    square = splat(total(left * left))
    if last:
        left_ref, out_ref = refs
        out_ref[...] = jnp.broadcast_to(square, out_ref.shape)
    else:
        design_ref, left_ref, out_ref = refs
        tiles = design_ref.shape[1] // LANE
        out_ref[0] = jnp.zeros(out_ref.shape[1:], F32)
        left_product(left, design_ref, out_ref.at[0])
        out_ref[0, tiles : tiles + 1, :] = square
        copy_out(out_ref)
    left_ref[...] = left


def last_body(parts_ref, left_ref, *refs):
    betas = [ref[...] for ref in refs[:ITERS]]
    alphas = [ref[...] for ref in refs[ITERS : 2 * ITERS]]
    held = [ref[...] for ref in refs[2 * ITERS : 3 * ITERS]]
    basis_ref, solution_ref = refs[3 * ITERS :]
    last = jnp.sqrt(tree([parts_ref[i] for i in range(parts_ref.shape[0])])[:1, :])
    basis_ref[...] = left_ref[...] / last
    betas.append(last)
    phibar, rhobar = betas[0], alphas[0]
    search, iterate = held[0], jnp.zeros_like(held[0])
    for step in range(ITERS):
        beta = betas[step + 1]
        rho = jnp.sqrt(rhobar * rhobar + beta * beta)
        cosine = rhobar / rho
        sine = beta / rho
        phi = cosine * phibar
        phibar = sine * phibar
        iterate = iterate + phi / rho * search
        if step + 1 < ITERS:
            alpha = alphas[step + 1]
            search = held[step + 1] - sine * alpha / rho * search
            rhobar = -cosine * alpha
    solution_ref[...] = iterate


def sample_body(scale, parts_ref, walsh_ref, design_ref, bits_ref, order_ref, out_ref, high_ref, low_ref):
    groups = out_ref.shape[0]
    rows, width = design_ref.shape
    spread = rounded(groups, 8)
    start = parts_ref.shape[1] - spread
    me, block = lax.axis_index("row"), pl.program_id(0)

    @pl.when(block == 0)
    def _():
        for line in range(rows // LANE):
            part = slice(line * LANE, (line + 1) * LANE)
            signs = signs_across(bits_ref, line)
            for tile in range(0, width, LANE):
                value = design_ref[part, tile : tile + LANE] * signs
                high = value.astype(jnp.bfloat16)
                high_ref[part, tile : tile + LANE] = high
                low_ref[part, tile : tile + LANE] = (value - high.astype(F32)).astype(jnp.bfloat16)

    coded = parts_ref[block, start : start + spread, :]
    filler = jnp.zeros((LANE - spread, LANE), F32)
    coded = jnp.concatenate([coded, filler], axis=0).T
    parity = jnp.int32(0)
    for bit in range(groups.bit_length() - 1):
        parity = parity ^ ((block & me) >> bit)
    sign = (1 - 2 * (parity & 1)).astype(F32)
    local = lax.broadcasted_iota(jnp.int32, (PAIR, rows), 1).astype(F32)
    chosen = []
    for owner in range(groups):
        match = jnp.broadcast_to(coded[:PAIR, owner : owner + 1], (PAIR, rows)) == local
        chosen.append(jnp.where(match, sign, 0.0))
    chosen = jnp.concatenate(chosen, axis=0).astype(jnp.bfloat16)
    mix = []
    for part in range(rows // HB):
        mixed = jnp.dot(chosen[:, part * HB : (part + 1) * HB], walsh_ref[...], preferred_element_type=F32)
        mix.append(mixed.astype(jnp.bfloat16))
    mix = jnp.concatenate(mix, axis=1)
    value = jnp.dot(mix, high_ref[...], preferred_element_type=F32)
    value = value + jnp.dot(mix, low_ref[...], preferred_element_type=F32)
    out_ref[...] = (value / scale).reshape(out_ref.shape)


def shape(*dims, dtype=F32):
    return jax.ShapeDtypeStruct(dims, dtype)


def shards(design, sign_bits, picks, counts, target, rinv):
    rows, width = design.shape
    whole = rinv.shape[1]
    row_groups, col_groups = lax.axis_size("row"), lax.axis_size("col")
    lines = rows // LANE
    big, small = rinv.size, design.size
    scalar = shape(1, LANE)
    deep = message_rows(width)
    left = target.reshape(lines, LANE)

    message = call(
        first_body,
        shape(row_groups, deep + rounded(row_groups, 8), LANE),
        design,
        left,
        picks.reshape(row_groups, PAIR),
        counts,
        flops=2 * small,
        size=4 * small,
    )

    def sample(message, order):
        scale = float(np.sqrt(np.float32(rows * row_groups)))
        signs = jnp.asarray(walsh(HB), jnp.bfloat16)
        operands = (message, signs, design, sign_bits.reshape(lines, LANE), order)
        return pl.pallas_call(
            functools.partial(sample_body, scale),
            grid=(row_groups,),
            out_shape=shape(row_groups, row_groups, PAIR, width),
            in_specs=[VMEM] * len(operands),
            out_specs=pl.BlockSpec((row_groups, 1, PAIR, width), lambda block: (0, block, 0, 0)),
            scratch_shapes=[pltpu.VMEM((rows, width), jnp.bfloat16)] * 2,
            compiler_params=pltpu.CompilerParams(vmem_limit_bytes=20 << 20),
            cost_estimate=pl.CostEstimate(
                flops=4 * row_groups * row_groups * PAIR * small,
                bytes_accessed=4 * row_groups * row_groups * PAIR * width,
                transcendentals=0,
            ),
        )(*operands)

    def back(message):
        return call(
            back_body,
            (shape(whole // LANE, LANE), scalar),
            rinv,
            message,
            scratch=[pltpu.VMEM((width // LANE, LANE), F32)],
            flops=2 * big,
            size=4 * big,
        )

    def forward(terms, *before):
        return call(
            functools.partial(forward_body, col_groups, not before),
            (shape(lines, LANE), shape(whole // LANE, LANE), shape(width // LANE, LANE), scalar),
            rinv,
            design,
            *terms,
            *before,
            flops=2 * big,
            size=4 * big,
        )

    def turn(images, left, beta, alpha, last):
        return call(
            functools.partial(turn_body, col_groups, last),
            (shape(lines, LANE), shape(row_groups, 8 if last else deep, LANE)),
            *images,
            left,
            beta,
            alpha,
            *(() if last else (design,)),
            flops=2 * small,
            size=0 if last else 4 * small,
        )

    betas, alphas, held = [], [], []
    message = exchange(message, "row")
    for step in range(ITERS):
        term, beta = back(message)
        betas.append(beta)
        if step == 0:
            sampled = sample(message, beta).reshape(row_groups * row_groups * PAIR, width)
            sketch = lax.psum_scatter(sampled, "row", scatter_dimension=0, tiled=True)
        terms = direct(term, "col")
        image, right, part, alpha = forward(terms, *(() if step == 0 else (right, beta)))
        alphas.append(alpha)
        held.append(part)
        images = direct(image, "col")
        left, message = turn(images, left, beta, alpha, step + 1 == ITERS)
        message = exchange(message, "row")
    basis, answer = call(
        last_body, (shape(lines, LANE), shape(width // LANE, LANE)), message, left, *betas, *alphas, *held
    )
    return (sketch, answer.reshape(-1), basis.reshape(-1))


def solution(mesh):
    placed = (
        P("row", "col"),
        P("row"),
        P(None, "row", None),
        P(None, "row"),
        P("row"),
        P("col", None),
    )
    return jax.shard_map(
        shards,
        mesh=mesh,
        in_specs=placed,
        out_specs=(P("row", "col"), P("col"), P("row")),
        check_vma=False,
    )
```

time: 141 us -> 136 us (0.965)
  blocking collectives: 61 us -> 34.3 us
  waiting for transfers between devices: 30.2 us -> 45.3 us
  between operations: 0.74 us -> 14.1 us
  starting transfers between devices: 12.4 us -> 8.19 us
  Pallas kernels: 20.1 us -> 16.4 us
  local copies, waits for them, and re-layouts: 15.9 us -> 17.6 us
    reduce_scatter x0 -> x1, waiting for transfers between devices: none -> 36.9 us  [shards(): sketch = lax.psum_scatter(sampled, 'row', scatter_dimension=0, tiled=True)]
    all_to_all x6 -> x3, blocking collectives: 61 us -> 34.3 us  [exchange(): return lax.all_to_all(copies, axis, split_axis=0, concat_axis=0, tiled=True)]
    ppermute x8 -> x12, waiting for transfers between devices: 25.8 us -> 8.31 us  [direct(): lax.ppermute(array, axis, [(i, i ^ mask) for i in range(size)])]
    pallas_call x16 -> x8, Pallas kernels: 20.1 us -> 10.1 us  [call(): pl.pallas_call(body, out_shape=out_shape, in_specs=[VMEM] * len(operands)...]
    pallas_call x0 -> x1, Pallas kernels: none -> 6.3 us  [sample(): pl.pallas_call(functools.partial(sample_body, scale), grid=(row_groups,),...]
    all_to_all x1 -> x0, starting transfers between devices: 5.9 us -> none  [exchange(): return lax.all_to_all(copies, axis, split_axis=0, concat_axis=0, tiled=True)]
    all_to_all x1 -> x0, waiting for transfers between devices: 4.42 us -> none  [exchange(): return lax.all_to_all(copies, axis, split_axis=0, concat_axis=0, tiled=True)]
    unnamed x25 -> x23, local copies, waits for them, and re-layouts: 15.9 us -> 17.6 us
  transfers between devices with their start and end apart: 9 -> 13, of which waited for: 4 -> 9; matrix products, arithmetic and copies ran while one was open for 0% -> 0% of each run, Pallas kernels for 13% -> 6%
where the time goes in v2:
time: 136 us
  waiting for transfers between devices  45.3 us (33%)
  blocking collectives  34.3 us (25%)
  local copies, waits for them, and re-layouts  17.6 us (13%)
  Pallas kernels  16.4 us (12%)
  between operations  14.1 us (10%)
  starting transfers between devices  8.19 us (6%)
    reduce_scatter x1, waiting for transfers between devices, shards(): sketch = lax.psum_scatter(sampled, 'row', scatter_dimension=0, tiled=True)  36.9 us
    all_to_all x3, blocking collectives, exchange(): return lax.all_to_all(copies, axis, split_axis=0, concat_axis=0, tiled=True)  34.3 us
    unnamed x23, local copies, waits for them, and re-layouts  17.6 us
    pallas_call x8, Pallas kernels, call(): pl.pallas_call(body, out_shape=out_shape, in_specs=[VMEM] * len(operands)...  10.1 us
    ppermute x12, waiting for transfers between devices, direct(): lax.ppermute(array, axis, [(i, i ^ mask) for i in range(size)])  8.31 us
    ppermute x12, starting transfers between devices, direct(): lax.ppermute(array, axis, [(i, i ^ mask) for i in range(size)])  8.15 us
    pallas_call x1, Pallas kernels, sample(): pl.pallas_call(functools.partial(sample_body, scale), grid=(row_groups,),...  6.3 us
  transfers between devices with their start and end apart: 13, of which 9 were waited for; matrix products, arithmetic and copies ran while one was open for 0% of the time, Pallas kernels for 6%

profile of v2, /device:TPU:0, one launch (start us, length us, event | category | flops | bytes accessed | tf_op | source)
XLA Modules:
  0.0 135.9 jit_solution(896677029108913147)
XLA Ops:
  7.2 0.7 copy.10.counts_ref
  7.9 1.6 %copy-done.3 = f32[512,1024]{1,0:T(8,128)S(1)} copy-done((f32[512,1024]{1,0:T(8,128)S(1)}, f32[512,1024]{1,0:T(8,128)}, u32[]{:S(2)}) %copy-start.3) | copy-done | bytes 2097176
  9.5 0.7 copy-done.6
  10.2 0.7 copy-done.8
  11.1 14.2 %all_to_all.15.parts_ref = f32[8,24,128]{2,1,0:T(8,128)S(1)} all-to-all(f32[8,24,128]{2,1,0:T(8,128)S(1)} %shard_map.94), channel_id=1, replica_groups=mesh['row'=8,'col'=4] {'row'}, dimensions={0} | all-to-all | bytes 196608 | tf_op jit(solution)/shard_map/all_to_all | solution.py:20
  25.3 5.8 %copy-done = f32[1024,4096]{1,0:T(8,128)S(1)} copy-done((f32[1024,4096]{1,0:T(8,128)S(1)}, f32[1024,4096]{1,0:T(8,128)}, u32[]{:S(2)}) %copy-start) | copy-done | bytes 16777240
  31.1 1.8 %shard_map.95 = (f32[32,128]{1,0:T(8,128)S(1)}, f32[1,128]{1,0:T(1,128)S(1)}) custom-call(f32[1024,4096]{1,0:T(8,128)S(1)} %copy-done, f32[8,24,128]{2,1,0:T(8,128)S(1)} %all_to_all.15.parts_ref), custom_call_target="tpu_custom_call" | custom-call | flops 8388608 | bytes 16777216 | tf_op jit(solution)/shard_map/pallas_call | solution.py:46
  33.0 6.3 %shard_map.96 = f32[8,8,16,1024]{3,2,1,0:T(8,128)S(1)} custom-call(f32[8,24,128]{2,1,0:T(8,128)S(1)} %all_to_all.15.parts_ref, bf16[256,256]{1,0:T(8,128)(2,1)S(1)} %copy-done.10, f32[512,1024]{1,0:T(8,128)S(1)} %copy-done.4, s32[4,128]{1,0:T(4,128)S(1)} %bitcast.10, f32[1,128]{1,0:T(1,128)S(1)} %get-tuple-element.20.order_ref.refs_5_.refs_0_), custom_call_target="tpu_custom_call" | custom-call | flops 2147483648 | bytes 4194304 | tf_op jit(solution)/shard_map/pallas_call | solution.py:281
  39.3 1.9 %copy-done.5 = f32[8,8,16,1024]{3,2,1,0:T(8,128)} copy-done((f32[8,8,16,1024]{3,2,1,0:T(8,128)}, f32[8,8,16,1024]{3,2,1,0:T(8,128)S(1)}, u32[]{:S(2)}) %copy-start.5) | copy-done | bytes 4194328
  41.3 1.6 %collective-permute-start.1 = (f32[32,128]{1,0:T(8,128)S(1)}, f32[32,128]{1,0:T(8,128)S(1)}, u32[]{:S(2)}, u32[]{:S(2)}) collective-permute-start(f32[32,128]{1,0:T(8,128)S(1)} %get-tuple-element.21.refs_0_), channel_id=1, source_target_pairs={{0,2},{1,3},{2,0},{3,1},{4,6},{5,7},{6,4},{7,5},{8,10},{9,11},{10,... | collective-permute-start | bytes 49160 | tf_op jit(solution)/shard_map/ppermute | solution.py:26
  43.2 1.4 %collective-permute-done.2.refs_3_ = f32[32,128]{1,0:T(8,128)S(1)} collective-permute-done((f32[32,128]{1,0:T(8,128)S(1)}, f32[32,128]{1,0:T(8,128)S(1)}, u32[]{:S(2)}, u32[]{:S(2)}) %collective-permute-start.2) | collective-permute-done | bytes 16416 | tf_op jit(solution)/shard_map/ppermute | solution.py:26
  44.6 0.5 collective-permute-done.1.refs_2_
  45.1 6.1 %copy-done.1 = f32[1024,4096]{1,0:T(8,128)S(1)} copy-done((f32[1024,4096]{1,0:T(8,128)S(1)}, f32[1024,4096]{1,0:T(8,128)}, u32[]{:S(2)}) %copy-start.1) | copy-done | bytes 16777240
  51.3 2.4 %shard_map.97 = (f32[4,128]{1,0:T(4,128)S(1)}, f32[32,128]{1,0:T(8,128)S(1)}, f32[8,128]{1,0:T(8,128)S(1)}, f32[1,128]{1,0:T(1,128)S(1)}) custom-call(f32[1024,4096]{1,0:T(8,128)S(1)} %copy-done.1, f32[512,1024]{1,0:T(8,128)S(1)} %copy-done.4, f32[32,128]{1,0:T(8,128)S(1)} %get-tuple-element.21.refs_0_, f32[32,128]{1,0:T(8,128)S(1)} %collective-permute-done.refs_1_, ...), custom_call_target="tpu_custom_call" | custom-call | flops 8388608 | bytes 16777216 | tf_op jit(solution)/shard_map/pallas_call | solution.py:46
  53.7 0.6 collective-permute-start.5
  54.3 1.5 %collective-permute-start.4 = (f32[4,128]{1,0:T(4,128)S(1)}, f32[4,128]{1,0:T(4,128)S(1)}, u32[]{:S(2)}, u32[]{:S(2)}) collective-permute-start(f32[4,128]{1,0:T(4,128)S(1)} %get-tuple-element.22.refs_0_), channel_id=1, source_target_pairs={{0,2},{1,3},{2,0},{3,1},{4,6},{5,7},{6,4},{7,5},{8,10},{9,11},{10,... | collective-permute-start | bytes 6152 | tf_op jit(solution)/shard_map/ppermute | solution.py:26
  55.8 1.0 collective-permute-done.5.refs_3_
  56.8 1.1 collective-permute-done.4.refs_2_
  58.1 10.5 %all_to_all.16.parts_ref = f32[8,16,128]{2,1,0:T(8,128)S(1)} all-to-all(f32[8,16,128]{2,1,0:T(8,128)S(1)} %get-tuple-element.24), channel_id=1, replica_groups=mesh['row'=8,'col'=4] {'row'}, dimensions={0} | all-to-all | bytes 131072 | tf_op jit(solution)/shard_map/all_to_all | solution.py:20
  68.7 1.8 %shard_map.99 = (f32[32,128]{1,0:T(8,128)S(1)}, f32[1,128]{1,0:T(1,128)S(1)}) custom-call(f32[1024,4096]{1,0:T(8,128)S(1)} %copy-done.2, f32[8,16,128]{2,1,0:T(8,128)S(1)} %all_to_all.16.parts_ref), custom_call_target="tpu_custom_call" | custom-call | flops 8388608 | bytes 16777216 | tf_op jit(solution)/shard_map/pallas_call | solution.py:46
  70.6 1.4 %collective-permute-start.7 = (f32[32,128]{1,0:T(8,128)S(1)}, f32[32,128]{1,0:T(8,128)S(1)}, u32[]{:S(2)}, u32[]{:S(2)}) collective-permute-start(f32[32,128]{1,0:T(8,128)S(1)} %get-tuple-element.25.refs_0_), channel_id=1, source_target_pairs={{0,2},{1,3},{2,0},{3,1},{4,6},{5,7},{6,4},{7,5},{8,10},{9,11},{10,... | collective-permute-start | bytes 49160 | tf_op jit(solution)/shard_map/ppermute | solution.py:26
  71.9 0.5 collective-permute-start.6
  72.4 1.3 collective-permute-done.8.refs_3_
  73.8 0.6 collective-permute-done.7.refs_2_
  74.4 2.9 %shard_map.100 = (f32[4,128]{1,0:T(4,128)S(1)}, f32[32,128]{1,0:T(8,128)}, f32[8,128]{1,0:T(8,128)S(1)}, f32[1,128]{1,0:T(1,128)S(1)}) custom-call(f32[1024,4096]{1,0:T(8,128)S(1)} %copy-done.2, f32[512,1024]{1,0:T(8,128)S(1)} %copy-done.4, f32[32,128]{1,0:T(8,128)S(1)} %get-tuple-element.25.refs_0_, f32[32,128]{1,0:T(8,128)S(1)} %collective-permute-done.6.refs_1_, ...), custom_call_target="tpu_custom_call" | custom-call | flops 8388608 | bytes 16777216 | tf_op jit(solution)/shard_map/pallas_call | solution.py:46
  77.3 0.9 collective-permute-start.11
  78.2 1.3 collective-permute-start.10
  79.5 0.8 collective-permute-done.11.refs_3_
  80.3 1.5 %collective-permute-done.10.refs_2_ = f32[4,128]{1,0:T(4,128)S(1)} collective-permute-done((f32[4,128]{1,0:T(4,128)S(1)}, f32[4,128]{1,0:T(4,128)S(1)}, u32[]{:S(2)}, u32[]{:S(2)}) %collective-permute-start.10) | collective-permute-done | bytes 2080 | tf_op jit(solution)/shard_map/ppermute | solution.py:26
  81.9 9.5 %all_to_all.17.parts_ref = f32[8,8,128]{2,1,0:T(8,128)S(1)} all-to-all(f32[8,8,128]{2,1,0:T(8,128)S(1)} %get-tuple-element.31), channel_id=1, replica_groups=mesh['row'=8,'col'=4] {'row'}, dimensions={0} | all-to-all | bytes 65536 | tf_op jit(solution)/shard_map/all_to_all | solution.py:20
  91.5 0.6 shard_map.102
  92.1 36.9 %reduce-scatter.2.cloned.1.call-done = f32[128,1024]{1,0:T(8,128)} async-done(((f32[1024,1024]{1,0:T(8,128)}), f32[128,1024]{1,0:T(8,128)}) %reduce-scatter.2.cloned.1.call-update) | async-done | bytes 524304 | tf_op jit(solution)/shard_map/reduce_scatter | solution.py:339
  (30 shorter events, 1.1 us)
Async XLA Ops:
  7.2 121.9 %reduce-scatter.2.cloned.1.call-start = ((), (), s32[]{:S(2)}) async-start(), calls=%async_computation.4 | async-start | bytes 4718592 | tf_op jit(solution)/shard_map/reduce_scatter | solution.py:339
  7.9 1.6 %copy-start.3 = (f32[512,1024]{1,0:T(8,128)S(1)}, f32[512,1024]{1,0:T(8,128)}, u32[]{:S(2)}) copy-start(f32[512,1024]{1,0:T(8,128)} %design_ref.7) | copy-start | bytes 6291460
  9.5 0.7 copy-start.6
  10.2 0.7 copy-start.8
  25.3 5.8 %copy-start = (f32[1024,4096]{1,0:T(8,128)S(1)}, f32[1024,4096]{1,0:T(8,128)}, u32[]{:S(2)}) copy-start(f32[1024,4096]{1,0:T(8,128)} %rinv_ref.7) | copy-start | bytes 50331652
  31.1 1.8 %copy-start.4 = (f32[512,1024]{1,0:T(8,128)S(1)}, f32[512,1024]{1,0:T(8,128)}, u32[]{:S(2)}) copy-start(f32[512,1024]{1,0:T(8,128)} %design_ref.7) | copy-start | bytes 6291460
  31.1 1.8 %copy-start.9 = (s32[512]{0:T(512)S(1)}, s32[512]{0:T(512)}, u32[]{:S(2)}) copy-start(s32[512]{0:T(512)} %param.8) | copy-start | bytes 6148
  31.1 1.8 %copy-start.10 = (bf16[256,256]{1,0:T(8,128)(2,1)S(1)}, bf16[256,256]{1,0:T(8,128)(2,1)}, u32[]{:S(2)}) copy-start(bf16[256,256]{1,0:T(8,128)(2,1)} %constant.2.clone.walsh_ref) | copy-start | bytes 393220
  39.3 2.0 %copy-start.5 = (f32[8,8,16,1024]{3,2,1,0:T(8,128)}, f32[8,8,16,1024]{3,2,1,0:T(8,128)S(1)}, u32[]{:S(2)}) copy-start(f32[8,8,16,1024]{3,2,1,0:T(8,128)S(1)} %shard_map.96) | copy-start | bytes 12582916
  41.2 16.7 %copy-start.7 = (f32[512]{0:T(512)S(1)}, f32[512]{0:T(512)}, u32[]{:S(2)}) copy-start(f32[512]{0:T(512)} %param.11) | copy-start | bytes 6148
  41.2 3.4 %collective-permute-start.2 = (f32[32,128]{1,0:T(8,128)S(1)}, f32[32,128]{1,0:T(8,128)S(1)}, u32[]{:S(2)}, u32[]{:S(2)}) collective-permute-start(f32[32,128]{1,0:T(8,128)S(1)} %get-tuple-element.21.refs_0_), channel_id=1, source_target_pairs={{0,3},{1,2},{2,1},{3,0},{4,7},{5,6},{6,5},{7,4},{8,11},{9,10},{10,... | collective-permute-start | bytes 49160 | tf_op jit(solution)/shard_map/ppermute | solution.py:26
  41.3 3.8 %collective-permute-start.1 = (f32[32,128]{1,0:T(8,128)S(1)}, f32[32,128]{1,0:T(8,128)S(1)}, u32[]{:S(2)}, u32[]{:S(2)}) collective-permute-start(f32[32,128]{1,0:T(8,128)S(1)} %get-tuple-element.21.refs_0_), channel_id=1, source_target_pairs={{0,2},{1,3},{2,0},{3,1},{4,6},{5,7},{6,4},{7,5},{8,10},{9,11},{10,... | collective-permute-start | bytes 49160 | tf_op jit(solution)/shard_map/ppermute | solution.py:26
  42.9 2.3 %collective-permute-start = (f32[32,128]{1,0:T(8,128)S(1)}, f32[32,128]{1,0:T(8,128)S(1)}, u32[]{:S(2)}, u32[]{:S(2)}) collective-permute-start(f32[32,128]{1,0:T(8,128)S(1)} %get-tuple-element.21.refs_0_), channel_id=1, source_target_pairs={{0,1},{1,0},{2,3},{3,2},{4,5},{5,4},{6,7},{7,6},{8,9},{9,8},{10,11... | collective-permute-start | bytes 49160 | tf_op jit(solution)/shard_map/ppermute | solution.py:26
  45.1 6.1 %copy-start.1 = (f32[1024,4096]{1,0:T(8,128)S(1)}, f32[1024,4096]{1,0:T(8,128)}, u32[]{:S(2)}) copy-start(f32[1024,4096]{1,0:T(8,128)} %rinv_ref.7) | copy-start | bytes 50331652
  51.3 17.4 %copy-start.2 = (f32[1024,4096]{1,0:T(8,128)S(1)}, f32[1024,4096]{1,0:T(8,128)}, u32[]{:S(2)}) copy-start(f32[1024,4096]{1,0:T(8,128)} %rinv_ref.7) | copy-start | bytes 50331652
  53.7 3.1 %collective-permute-start.5 = (f32[4,128]{1,0:T(4,128)S(1)}, f32[4,128]{1,0:T(4,128)S(1)}, u32[]{:S(2)}, u32[]{:S(2)}) collective-permute-start(f32[4,128]{1,0:T(4,128)S(1)} %get-tuple-element.22.refs_0_), channel_id=1, source_target_pairs={{0,3},{1,2},{2,1},{3,0},{4,7},{5,6},{6,5},{7,4},{8,11},{9,10},{10,... | collective-permute-start | bytes 6152 | tf_op jit(solution)/shard_map/ppermute | solution.py:26
  54.3 3.6 %collective-permute-start.4 = (f32[4,128]{1,0:T(4,128)S(1)}, f32[4,128]{1,0:T(4,128)S(1)}, u32[]{:S(2)}, u32[]{:S(2)}) collective-permute-start(f32[4,128]{1,0:T(4,128)S(1)} %get-tuple-element.22.refs_0_), channel_id=1, source_target_pairs={{0,2},{1,3},{2,0},{3,1},{4,6},{5,7},{6,4},{7,5},{8,10},{9,11},{10,... | collective-permute-start | bytes 6152 | tf_op jit(solution)/shard_map/ppermute | solution.py:26
  55.8 2.1 %collective-permute-start.3 = (f32[4,128]{1,0:T(4,128)S(1)}, f32[4,128]{1,0:T(4,128)S(1)}, u32[]{:S(2)}, u32[]{:S(2)}) collective-permute-start(f32[4,128]{1,0:T(4,128)S(1)} %get-tuple-element.22.refs_0_), channel_id=1, source_target_pairs={{0,1},{1,0},{2,3},{3,2},{4,5},{5,4},{6,7},{7,6},{8,9},{9,8},{10,11... | collective-permute-start | bytes 6152 | tf_op jit(solution)/shard_map/ppermute | solution.py:26
  70.5 3.3 %collective-permute-start.8 = (f32[32,128]{1,0:T(8,128)S(1)}, f32[32,128]{1,0:T(8,128)S(1)}, u32[]{:S(2)}, u32[]{:S(2)}) collective-permute-start(f32[32,128]{1,0:T(8,128)S(1)} %get-tuple-element.25.refs_0_), channel_id=1, source_target_pairs={{0,3},{1,2},{2,1},{3,0},{4,7},{5,6},{6,5},{7,4},{8,11},{9,10},{10,... | collective-permute-start | bytes 49160 | tf_op jit(solution)/shard_map/ppermute | solution.py:26
  70.6 3.8 %collective-permute-start.7 = (f32[32,128]{1,0:T(8,128)S(1)}, f32[32,128]{1,0:T(8,128)S(1)}, u32[]{:S(2)}, u32[]{:S(2)}) collective-permute-start(f32[32,128]{1,0:T(8,128)S(1)} %get-tuple-element.25.refs_0_), channel_id=1, source_target_pairs={{0,2},{1,3},{2,0},{3,1},{4,6},{5,7},{6,4},{7,5},{8,10},{9,11},{10,... | collective-permute-start | bytes 49160 | tf_op jit(solution)/shard_map/ppermute | solution.py:26
  71.9 2.4 %collective-permute-start.6 = (f32[32,128]{1,0:T(8,128)S(1)}, f32[32,128]{1,0:T(8,128)S(1)}, u32[]{:S(2)}, u32[]{:S(2)}) collective-permute-start(f32[32,128]{1,0:T(8,128)S(1)} %get-tuple-element.25.refs_0_), channel_id=1, source_target_pairs={{0,1},{1,0},{2,3},{3,2},{4,5},{5,4},{6,7},{7,6},{8,9},{9,8},{10,11... | collective-permute-start | bytes 49160 | tf_op jit(solution)/shard_map/ppermute | solution.py:26
  77.3 3.0 %collective-permute-start.11 = (f32[4,128]{1,0:T(4,128)S(1)}, f32[4,128]{1,0:T(4,128)S(1)}, u32[]{:S(2)}, u32[]{:S(2)}) collective-permute-start(f32[4,128]{1,0:T(4,128)S(1)} %get-tuple-element.28.refs_0_), channel_id=1, source_target_pairs={{0,3},{1,2},{2,1},{3,0},{4,7},{5,6},{6,5},{7,4},{8,11},{9,10},{10,... | collective-permute-start | bytes 6152 | tf_op jit(solution)/shard_map/ppermute | solution.py:26
  78.2 3.6 %collective-permute-start.10 = (f32[4,128]{1,0:T(4,128)S(1)}, f32[4,128]{1,0:T(4,128)S(1)}, u32[]{:S(2)}, u32[]{:S(2)}) collective-permute-start(f32[4,128]{1,0:T(4,128)S(1)} %get-tuple-element.28.refs_0_), channel_id=1, source_target_pairs={{0,2},{1,3},{2,0},{3,1},{4,6},{5,7},{6,4},{7,5},{8,10},{9,11},{10,... | collective-permute-start | bytes 6152 | tf_op jit(solution)/shard_map/ppermute | solution.py:26
  79.5 2.3 %collective-permute-start.9 = (f32[4,128]{1,0:T(4,128)S(1)}, f32[4,128]{1,0:T(4,128)S(1)}, u32[]{:S(2)}, u32[]{:S(2)}) collective-permute-start(f32[4,128]{1,0:T(4,128)S(1)} %get-tuple-element.28.refs_0_), channel_id=1, source_target_pairs={{0,1},{1,0},{2,3},{3,2},{4,5},{5,4},{6,7},{7,6},{8,9},{9,8},{10,11... | collective-permute-start | bytes 6152 | tf_op jit(solution)/shard_map/ppermute | solution.py:26
Sparse Core Ops, SparseCore 0:
  41.4 87.6 reduce-scatter.1

commit v3 on v2

--- a/solution.py
+++ b/solution.py
@@ -12,8 +12,10 @@
 PAIR = 16
 ITERS = 2
 LANE = 128
+CHUNKS = 2
 F32 = jnp.float32
 VMEM = pl.BlockSpec(memory_space=pltpu.VMEM)
+HBM = pl.BlockSpec(memory_space=pltpu.HBM)
 
 
 def exchange(copies, axis):
@@ -127,18 +129,65 @@
     return jnp.broadcast_to(signs, (LANE, LANE)).T
 
 
-def first_body(design_ref, target_ref, picks_ref, counts_ref, out_ref):
-    width = design_ref.shape[1]
-    tiles = width // LANE
-    target = target_ref[...]
+def first_body(design_ref, target_ref, bits_ref, picks_ref, counts_ref, *refs):
+    chunks = len(refs) - 8
+    out_ref, away_refs = refs[0], refs[1 : 1 + chunks]
+    design, target_here, bits, picks, counts, away, sems = refs[1 + chunks :]
+    rows, width = design.shape
+    lines, tiles, half = rows // LANE, width // LANE, width // 2
+    piece = half // chunks
+    small = [
+        pltpu.make_async_copy(source, place, sems.at[index])
+        for index, (source, place) in enumerate(
+            ((target_ref, target_here), (bits_ref, bits), (picks_ref, picks), (counts_ref, counts))
+        )
+    ]
+    parts = [slice(line * LANE, (line + 1) * LANE) for line in range(lines)]
+    large = [
+        pltpu.make_async_copy(design_ref.at[part, :], design.at[part, :], sems.at[4 + line])
+        for line, part in enumerate(parts)
+    ]
+    for copy in small + large:
+        copy.start()
+    for copy in small:
+        copy.wait()
+    low = lax.axis_index("row") & 1
+    sums = [jnp.zeros((8, LANE), F32) for _ in range(tiles)]
+    back = []
+    for line, part in enumerate(parts):
+        across = jnp.broadcast_to(target_here[line : line + 1, :], (LANE, LANE)).T
+        signs = signs_across(bits, line)
+        large[line].wait()
+        for tile in range(tiles):
+            value = design[part, tile * LANE : (tile + 1) * LANE]
+            sums[tile] = sums[tile] + fold_rows(value * across)
+        for tile in range(0, half, LANE):
+            column = pl.multiple_of((1 - low) * half + tile, LANE)
+            away[part, tile : tile + LANE] = design[part, pl.ds(column, LANE)] * signs
+        for chunk in range(chunks):
+            copy = pltpu.make_async_copy(
+                away.at[part, chunk * piece : (chunk + 1) * piece],
+                away_refs[chunk].at[part, :],
+                sems.at[4 + lines * (1 + chunk) + line],
+            )
+            copy.start()
+            back.append(copy)
     out_ref[0] = jnp.zeros(out_ref.shape[1:], F32)
-    left_product(target, design_ref, out_ref.at[0])
+    for tile in range(tiles):
+        out_ref[0, tile : tile + 1, :] = jnp.sum(sums[tile], axis=0, keepdims=True)
+    target = target_here[...]
     out_ref[0, tiles : tiles + 1, :] = splat(total(target * target))
-    slot = lax.broadcasted_iota(jnp.int32, picks_ref.shape, 1)
-    coded = jnp.where(slot < counts_ref[...], picks_ref[...], -1).astype(F32)
+    groups = picks.shape[0]
+    owner = lax.broadcasted_iota(jnp.int32, (groups, groups), 0)
+    same = owner == lax.broadcasted_iota(jnp.int32, (groups, groups), 1)
+    limit = jnp.sum(jnp.where(same, counts[...].astype(F32), 0.0), axis=1, keepdims=True)
+    slot = lax.broadcasted_iota(jnp.int32, picks.shape, 1).astype(F32)
+    coded = jnp.where(slot < limit, picks[...].astype(F32), -1.0)
     start = message_rows(width)
-    out_ref[0, start : start + coded.shape[0], : coded.shape[1]] = coded
+    out_ref[0, start : start + groups, : coded.shape[1]] = coded
     copy_out(out_ref)
+    for copy in back:
+        copy.wait()
 
 
 def back_body(rinv_ref, parts_ref, term_ref, beta_ref, scratch):
@@ -208,23 +257,30 @@
     solution_ref[...] = iterate
 
 
-def sample_body(scale, parts_ref, walsh_ref, design_ref, bits_ref, order_ref, out_ref, high_ref, low_ref):
-    groups = out_ref.shape[0]
+def sample_body(
+    chunk, scale, parts_ref, walsh_ref, design_ref, bits_ref, pair_ref, order_ref, out_ref, both
+):
+    groups, piece = out_ref.shape[0], out_ref.shape[3]
     rows, width = design_ref.shape
     spread = rounded(groups, 8)
     start = parts_ref.shape[1] - spread
     me, block = lax.axis_index("row"), pl.program_id(0)
+    low = me & 1
 
     @pl.when(block == 0)
     def _():
         for line in range(rows // LANE):
             part = slice(line * LANE, (line + 1) * LANE)
+            far = pl.ds(pl.multiple_of((1 - low) * rows + line * LANE, LANE), LANE)
             signs = signs_across(bits_ref, line)
-            for tile in range(0, width, LANE):
-                value = design_ref[part, tile : tile + LANE] * signs
-                high = value.astype(jnp.bfloat16)
-                high_ref[part, tile : tile + LANE] = high
-                low_ref[part, tile : tile + LANE] = (value - high.astype(F32)).astype(jnp.bfloat16)
+            for tile in range(0, piece, LANE):
+                column = pl.multiple_of(low * (width // 2) + chunk * piece + tile, LANE)
+                mine = design_ref[part, pl.ds(column, LANE)] * signs
+                other = pair_ref[far, tile : tile + LANE]
+                for index, value in enumerate((mine + other, mine - other)):
+                    high = value.astype(jnp.bfloat16)
+                    both[index, 0, part, tile : tile + LANE] = high
+                    both[index, 1, part, tile : tile + LANE] = (value - high.astype(F32)).astype(jnp.bfloat16)
 
     coded = parts_ref[block, start : start + spread, :]
     filler = jnp.zeros((LANE - spread, LANE), F32)
@@ -244,9 +300,23 @@
         mixed = jnp.dot(chosen[:, part * HB : (part + 1) * HB], walsh_ref[...], preferred_element_type=F32)
         mix.append(mixed.astype(jnp.bfloat16))
     mix = jnp.concatenate(mix, axis=1)
-    value = jnp.dot(mix, high_ref[...], preferred_element_type=F32)
-    value = value + jnp.dot(mix, low_ref[...], preferred_element_type=F32)
+    value = jnp.dot(mix, both[block & 1, 0], preferred_element_type=F32)
+    value = value + jnp.dot(mix, both[block & 1, 1], preferred_element_type=F32)
     out_ref[...] = (value / scale).reshape(out_ref.shape)
+
+
+def assemble_body(*refs):
+    chunks = len(refs) // 2
+    mine, other, out_ref = refs[:chunks], refs[chunks : 2 * chunks], refs[-1]
+    low = lax.axis_index("row") & 1
+    half = out_ref.shape[1] // 2
+    for chunk in range(chunks):
+        piece = half // chunks
+        for tile in range(0, piece, LANE):
+            near = pl.multiple_of(low * half + chunk * piece + tile, LANE)
+            far = pl.multiple_of((1 - low) * half + chunk * piece + tile, LANE)
+            out_ref[:, pl.ds(near, LANE)] = mine[chunk][:, tile : tile + LANE]
+            out_ref[:, pl.ds(far, LANE)] = other[chunk][:, tile : tile + LANE]
 
 
 def shape(*dims, dtype=F32):
@@ -262,36 +332,59 @@
     scalar = shape(1, LANE)
     deep = message_rows(width)
     left = target.reshape(lines, LANE)
-
-    message = call(
+    bits = sign_bits.reshape(lines, LANE)
+    half = width // 2
+    chunks = min(CHUNKS, half // LANE)
+    piece = half // chunks
+    pairs = [[i, i + 1] for i in range(0, row_groups, 2)]
+    quads = [list(range(i, row_groups, 2)) for i in range(2)]
+
+    message, *away = pl.pallas_call(
         first_body,
-        shape(row_groups, deep + rounded(row_groups, 8), LANE),
-        design,
-        left,
-        picks.reshape(row_groups, PAIR),
-        counts,
-        flops=2 * small,
-        size=4 * small,
-    )
-
-    def sample(message, order):
+        out_shape=(shape(row_groups, deep + rounded(row_groups, 8), LANE),) + (shape(rows, piece),) * chunks,
+        in_specs=[HBM] * 5,
+        out_specs=(VMEM,) + (HBM,) * chunks,
+        scratch_shapes=[
+            pltpu.VMEM((rows, width), F32),
+            pltpu.VMEM((lines, LANE), F32),
+            pltpu.VMEM((lines, LANE), jnp.int32),
+            pltpu.VMEM((row_groups, PAIR), jnp.int32),
+            pltpu.VMEM((1, row_groups), jnp.int32),
+            pltpu.VMEM((rows, half), F32),
+            pltpu.SemaphoreType.DMA((4 + lines * (1 + chunks),)),
+        ],
+        compiler_params=pltpu.CompilerParams(vmem_limit_bytes=58 << 20),
+        cost_estimate=pl.CostEstimate(flops=2 * small, bytes_accessed=6 * small, transcendentals=0),
+    )(design, left, bits, picks.reshape(row_groups, PAIR), counts.reshape(1, row_groups))
+
+    def sample(chunk, pair, order):
         scale = float(np.sqrt(np.float32(rows * row_groups)))
         signs = jnp.asarray(walsh(HB), jnp.bfloat16)
-        operands = (message, signs, design, sign_bits.reshape(lines, LANE), order)
-        return pl.pallas_call(
-            functools.partial(sample_body, scale),
+        operands = (picked, signs, design, bits, pair, order)
+        made = pl.pallas_call(
+            functools.partial(sample_body, chunk, scale),
             grid=(row_groups,),
-            out_shape=shape(row_groups, row_groups, PAIR, width),
+            out_shape=shape(row_groups, row_groups, PAIR, piece),
             in_specs=[VMEM] * len(operands),
-            out_specs=pl.BlockSpec((row_groups, 1, PAIR, width), lambda block: (0, block, 0, 0)),
-            scratch_shapes=[pltpu.VMEM((rows, width), jnp.bfloat16)] * 2,
+            out_specs=pl.BlockSpec((row_groups, 1, PAIR, piece), lambda block: (0, block, 0, 0)),
+            scratch_shapes=[pltpu.VMEM((2, 2, rows, piece), jnp.bfloat16)],
             compiler_params=pltpu.CompilerParams(vmem_limit_bytes=20 << 20),
             cost_estimate=pl.CostEstimate(
-                flops=4 * row_groups * row_groups * PAIR * small,
-                bytes_accessed=4 * row_groups * row_groups * PAIR * width,
+                flops=8 * row_groups * row_groups * PAIR * rows * piece,
+                bytes_accessed=4 * row_groups * row_groups * PAIR * piece,
                 transcendentals=0,
             ),
         )(*operands)
+        made = made.reshape(row_groups * row_groups * PAIR, piece)
+        return lax.psum_scatter(made, "row", scatter_dimension=0, axis_index_groups=quads, tiled=True)
+
+    def finish(summed, order):
+        summed, _ = lax.optimization_barrier((summed, order))
+        low = lax.axis_index("row") & 1
+        summed = summed.reshape(2, row_groups * PAIR, piece)
+        mine = lax.dynamic_index_in_dim(summed, low, 0, keepdims=False)
+        other = lax.dynamic_index_in_dim(summed, 1 - low, 0, keepdims=False)
+        return mine, lax.ppermute(other, "row", [(i, i ^ 1) for i in range(row_groups)])
 
     def back(message):
         return call(
@@ -329,24 +422,28 @@
             size=0 if last else 4 * small,
         )
 
-    betas, alphas, held = [], [], []
-    message = exchange(message, "row")
+    betas, alphas, held, summed = [], [], [], []
+    pair = [lax.all_gather(part, "row", axis=0, axis_index_groups=pairs, tiled=True) for part in away]
+    message = picked = exchange(message, "row")
     for step in range(ITERS):
         term, beta = back(message)
         betas.append(beta)
         if step == 0:
-            sampled = sample(message, beta).reshape(row_groups * row_groups * PAIR, width)
-            sketch = lax.psum_scatter(sampled, "row", scatter_dimension=0, tiled=True)
+            summed.append(sample(0, pair[0], beta))
         terms = direct(term, "col")
         image, right, part, alpha = forward(terms, *(() if step == 0 else (right, beta)))
         alphas.append(alpha)
         held.append(part)
+        if step == 0:
+            summed += [sample(chunk, pair[chunk], alpha) for chunk in range(1, chunks)]
         images = direct(image, "col")
         left, message = turn(images, left, beta, alpha, step + 1 == ITERS)
         message = exchange(message, "row")
     basis, answer = call(
         last_body, (shape(lines, LANE), shape(width // LANE, LANE)), message, left, *betas, *alphas, *held
     )
+    mine, other = zip(*[finish(value, message if i else alpha) for i, value in enumerate(summed)])
+    sketch = call(assemble_body, shape(row_groups * PAIR, width), *mine, *other)
     return (sketch, answer.reshape(-1), basis.reshape(-1))
 
 

time: 136 us -> 135 us (level)
  waiting for transfers between devices: 45.3 us -> 26.8 us
  local copies, waits for them, and re-layouts: 17.6 us -> 27.8 us
  Pallas kernels: 16.4 us -> 25.7 us
  blocking collectives: 34.3 us -> 27.1 us
  starting transfers between devices: 8.19 us -> 13.3 us
    reduce_scatter x1 -> x2, waiting for transfers between devices: 36.9 us -> 0.02 us  [sample(): lax.psum_scatter(made, 'row', scatter_dimension=0, axis_index_groups=quad...]
    unnamed x23 -> x20, local copies, waits for them, and re-layouts: 17.6 us -> 25.8 us
    pallas_call x1 -> x3, Pallas kernels: 6.3 us -> 14.4 us  [the longest x2 11.1 us: sample(): pl.pallas_call(functools.partial(sample_body, chunk, scale), grid=(row_gr...]
    all_to_all x3 -> x2, blocking collectives: 34.3 us -> 27.1 us  [exchange(): return lax.all_to_all(copies, axis, split_axis=0, concat_axis=0, tiled=True)]
    all_to_all x0 -> x1, waiting for transfers between devices: none -> 6.59 us  [exchange(): return lax.all_to_all(copies, axis, split_axis=0, concat_axis=0, tiled=True)]
    ppermute x0 -> x2, waiting for transfers between devices: none -> 4.86 us  [finish(): lax.ppermute(other, 'row', [(i, i ^ 1) for i in range(row_groups)])]
    all_gather x0 -> x2, waiting for transfers between devices: none -> 4.35 us  [shards(): lax.all_gather(part, 'row', axis=0, axis_index_groups=pairs, tiled=True)]
    all_to_all x0 -> x1, starting transfers between devices: none -> 3.34 us  [exchange(): return lax.all_to_all(copies, axis, split_axis=0, concat_axis=0, tiled=True)]
  transfers between devices with their start and end apart: 13 -> 19, of which waited for: 9 -> 12; matrix products, arithmetic and copies ran while one was open for 0% -> 0% of each run, Pallas kernels for 6% -> 16%
where the time goes in v3:
time: 135 us
  local copies, waits for them, and re-layouts  27.8 us (21%)
  blocking collectives  27.1 us (20%)
  waiting for transfers between devices  26.8 us (20%)
  Pallas kernels  25.7 us (19%)
  between operations  13.9 us (10%)
  starting transfers between devices  13.3 us (10%)
    all_to_all x2, blocking collectives, exchange(): return lax.all_to_all(copies, axis, split_axis=0, concat_axis=0, tiled=True)  27.1 us
    unnamed x20, local copies, waits for them, and re-layouts  25.8 us
    pallas_call x8, Pallas kernels, call(): pl.pallas_call(body, out_shape=out_shape, in_specs=[VMEM] * len(operands)...  11.4 us
    pallas_call x2, Pallas kernels, sample(): pl.pallas_call(functools.partial(sample_body, chunk, scale), grid=(row_gr...  11.1 us
    ppermute x12, waiting for transfers between devices, direct(): lax.ppermute(array, axis, [(i, i ^ mask) for i in range(size)])  10.2 us
    ppermute x12, starting transfers between devices, direct(): lax.ppermute(array, axis, [(i, i ^ mask) for i in range(size)])  7.69 us
    all_to_all x1, waiting for transfers between devices, exchange(): return lax.all_to_all(copies, axis, split_axis=0, concat_axis=0, tiled=True)  6.59 us
    ppermute x2, waiting for transfers between devices, finish(): lax.ppermute(other, 'row', [(i, i ^ 1) for i in range(row_groups)])  4.86 us
  transfers between devices with their start and end apart: 19, of which 12 were waited for; matrix products, arithmetic and copies ran while one was open for 0% of the time, Pallas kernels for 16%

profile of v3, /device:TPU:0, one launch (start us, length us, event | category | flops | bytes accessed | tf_op | source)
XLA Modules:
  0.0 134.6 jit_solution(15626006926135861149)
XLA Ops:
  7.2 3.3 %shard_map.103 = (f32[8,24,128]{2,1,0:T(8,128)}, f32[512,256]{1,0:T(8,128)}, f32[512,256]{1,0:T(8,128)}) custom-call(f32[512,1024]{1,0:T(8,128)} %design_ref.9, f32[4,128]{1,0:T(4,128)} %bitcast.21, s32[4,128]{1,0:T(4,128)} %bitcast.18, s32[8,16]{1,0:T(8,128)} %bitcast.25, s32[1,8]{1,0:T(1,128)} %bitcast.26), custom_call_target="tpu_custom_call" | custom-call | flops 1048576 | bytes 3145728 | tf_op jit(solution)/shard_map/pallas_call | solution.py:342
  11.3 14.5 %all_to_all.15.parts_ref = f32[8,24,128]{2,1,0:T(8,128)S(1)} all-to-all(f32[8,24,128]{2,1,0:T(8,128)} %get-tuple-element.25), channel_id=1, replica_groups=mesh['row'=8,'col'=4] {'row'}, dimensions={0} | all-to-all | bytes 196608 | tf_op jit(solution)/shard_map/all_to_all | solution.py:22
  25.9 5.8 %copy-done = f32[1024,4096]{1,0:T(8,128)S(1)} copy-done((f32[1024,4096]{1,0:T(8,128)S(1)}, f32[1024,4096]{1,0:T(8,128)}, u32[]{:S(2)}) %copy-start) | copy-done | bytes 16777240
  31.6 1.8 %shard_map.104 = (f32[32,128]{1,0:T(8,128)S(1)}, f32[1,128]{1,0:T(1,128)S(1)}) custom-call(f32[1024,4096]{1,0:T(8,128)S(1)} %copy-done, f32[8,24,128]{2,1,0:T(8,128)S(1)} %all_to_all.15.parts_ref), custom_call_target="tpu_custom_call" | custom-call | flops 8388608 | bytes 16777216 | tf_op jit(solution)/shard_map/pallas_call | solution.py:48
  33.5 1.8 %all-gather.3.cloned.1.call-done.pair_ref = f32[1024,256]{1,0:T(8,128)} async-done(((f32[512,256]{1,0:T(8,128)}), f32[1024,256]{1,0:T(8,128)}) %all-gather.3.cloned.1.call-update) | async-done | bytes 1048592 | tf_op jit(solution)/shard_map/all_gather | solution.py:426
  35.2 1.2 copy-done.6
  36.5 5.5 %shard_map.105 = f32[8,8,16,256]{3,2,1,0:T(8,128)} custom-call(f32[8,24,128]{2,1,0:T(8,128)S(1)} %all_to_all.15.parts_ref, bf16[256,256]{1,0:T(8,128)(2,1)S(1)} %copy-done.7, f32[512,1024]{1,0:T(8,128)S(1)} %copy-done.4, s32[4,128]{1,0:T(4,128)S(1)} %bitcast.19, f32[1024,256]{1,0:T(8,128)S(1)} %copy-done.6, ...), custom_call_target="tpu_custom_call" | custom-call | flops 1073741824 | bytes 1048576 | tf_op jit(solution)/shard_map/pallas_call | solution.py:364
  42.1 1.5 %collective-permute-start.1 = (f32[32,128]{1,0:T(8,128)S(1)}, f32[32,128]{1,0:T(8,128)S(1)}, u32[]{:S(2)}, u32[]{:S(2)}) collective-permute-start(f32[32,128]{1,0:T(8,128)S(1)} %get-tuple-element.28.refs_0_), channel_id=1, source_target_pairs={{0,2},{1,3},{2,0},{3,1},{4,6},{5,7},{6,4},{7,5},{8,10},{9,11},{10,... | collective-permute-start | bytes 49160 | tf_op jit(solution)/shard_map/ppermute | solution.py:28
  44.0 1.9 %collective-permute-done.1.refs_2_ = f32[32,128]{1,0:T(8,128)S(1)} collective-permute-done((f32[32,128]{1,0:T(8,128)S(1)}, f32[32,128]{1,0:T(8,128)S(1)}, u32[]{:S(2)}, u32[]{:S(2)}) %collective-permute-start.1) | collective-permute-done | bytes 16416 | tf_op jit(solution)/shard_map/ppermute | solution.py:28
  46.8 5.8 %copy-done.1 = f32[1024,4096]{1,0:T(8,128)S(1)} copy-done((f32[1024,4096]{1,0:T(8,128)S(1)}, f32[1024,4096]{1,0:T(8,128)}, u32[]{:S(2)}) %copy-start.1) | copy-done | bytes 16777240
  52.6 2.4 %shard_map.106 = (f32[4,128]{1,0:T(4,128)S(1)}, f32[32,128]{1,0:T(8,128)S(1)}, f32[8,128]{1,0:T(8,128)S(1)}, f32[1,128]{1,0:T(1,128)S(1)}) custom-call(f32[1024,4096]{1,0:T(8,128)S(1)} %copy-done.1, f32[512,1024]{1,0:T(8,128)S(1)} %copy-done.4, f32[32,128]{1,0:T(8,128)S(1)} %get-tuple-element.28.refs_0_, f32[32,128]{1,0:T(8,128)S(1)} %collective-permute-done.refs_1_, ...), custom_call_target="tpu_custom_call" | custom-call | flops 8388608 | bytes 16777216 | tf_op jit(solution)/shard_map/pallas_call | solution.py:48
  55.0 2.6 %all-gather.5.cloned.1.call-done.pair_ref = f32[1024,256]{1,0:T(8,128)} async-done(((f32[512,256]{1,0:T(8,128)}), f32[1024,256]{1,0:T(8,128)}) %all-gather.5.cloned.1.call-update) | async-done | bytes 1048592 | tf_op jit(solution)/shard_map/all_gather | solution.py:426
  57.6 1.2 copy-done.5
  58.8 5.6 %shard_map.110 = f32[8,8,16,256]{3,2,1,0:T(8,128)} custom-call(f32[8,24,128]{2,1,0:T(8,128)S(1)} %all_to_all.15.parts_ref, bf16[256,256]{1,0:T(8,128)(2,1)S(1)} %copy-done.7, f32[512,1024]{1,0:T(8,128)S(1)} %copy-done.4, s32[4,128]{1,0:T(4,128)S(1)} %bitcast.20, f32[1024,256]{1,0:T(8,128)S(1)} %copy-done.5, ...), custom_call_target="tpu_custom_call" | custom-call | flops 1073741824 | bytes 1048576 | tf_op jit(solution)/shard_map/pallas_call | solution.py:364
  64.5 1.5 %collective-permute-start.4 = (f32[4,128]{1,0:T(4,128)S(1)}, f32[4,128]{1,0:T(4,128)S(1)}, u32[]{:S(2)}, u32[]{:S(2)}) collective-permute-start(f32[4,128]{1,0:T(4,128)S(1)} %get-tuple-element.29.refs_0_), channel_id=1, source_target_pairs={{0,2},{1,3},{2,0},{3,1},{4,6},{5,7},{6,4},{7,5},{8,10},{9,11},{10,... | collective-permute-start | bytes 6152 | tf_op jit(solution)/shard_map/ppermute | solution.py:28
  66.4 1.8 %collective-permute-done.4.refs_2_ = f32[4,128]{1,0:T(4,128)S(1)} collective-permute-done((f32[4,128]{1,0:T(4,128)S(1)}, f32[4,128]{1,0:T(4,128)S(1)}, u32[]{:S(2)}, u32[]{:S(2)}) %collective-permute-start.4) | collective-permute-done | bytes 2080 | tf_op jit(solution)/shard_map/ppermute | solution.py:28
  69.3 12.6 %all_to_all.16.parts_ref = f32[8,16,128]{2,1,0:T(8,128)S(1)} all-to-all(f32[8,16,128]{2,1,0:T(8,128)S(1)} %get-tuple-element.31), channel_id=1, replica_groups=mesh['row'=8,'col'=4] {'row'}, dimensions={0} | all-to-all | bytes 131072 | tf_op jit(solution)/shard_map/all_to_all | solution.py:22
  81.8 5.9 %copy-done.2 = f32[1024,4096]{1,0:T(8,128)S(1)} copy-done((f32[1024,4096]{1,0:T(8,128)S(1)}, f32[1024,4096]{1,0:T(8,128)}, u32[]{:S(2)}) %copy-start.2) | copy-done | bytes 16777240
  87.7 1.8 %shard_map.108 = (f32[32,128]{1,0:T(8,128)S(1)}, f32[1,128]{1,0:T(1,128)S(1)}) custom-call(f32[1024,4096]{1,0:T(8,128)S(1)} %copy-done.2, f32[8,16,128]{2,1,0:T(8,128)S(1)} %all_to_all.16.parts_ref), custom_call_target="tpu_custom_call" | custom-call | flops 8388608 | bytes 16777216 | tf_op jit(solution)/shard_map/pallas_call | solution.py:48
  90.2 1.3 collective-permute-start.8
  91.5 2.1 %collective-permute-done.7.refs_2_ = f32[32,128]{1,0:T(8,128)S(1)} collective-permute-done((f32[32,128]{1,0:T(8,128)S(1)}, f32[32,128]{1,0:T(8,128)S(1)}, u32[]{:S(2)}, u32[]{:S(2)}) %collective-permute-start.7) | collective-permute-done | bytes 16416 | tf_op jit(solution)/shard_map/ppermute | solution.py:28
  93.5 6.0 %copy-done.3 = f32[1024,4096]{1,0:T(8,128)S(1)} copy-done((f32[1024,4096]{1,0:T(8,128)S(1)}, f32[1024,4096]{1,0:T(8,128)}, u32[]{:S(2)}) %copy-start.3) | copy-done | bytes 16777240
  99.5 2.9 %shard_map.109 = (f32[4,128]{1,0:T(4,128)S(1)}, f32[32,128]{1,0:T(8,128)}, f32[8,128]{1,0:T(8,128)S(1)}, f32[1,128]{1,0:T(1,128)S(1)}) custom-call(f32[1024,4096]{1,0:T(8,128)S(1)} %copy-done.3, f32[512,1024]{1,0:T(8,128)S(1)} %copy-done.4, f32[32,128]{1,0:T(8,128)S(1)} %get-tuple-element.32.refs_0_, f32[32,128]{1,0:T(8,128)S(1)} %collective-permute-done.6.refs_1_, ...), custom_call_target="tpu_custom_call" | custom-call | flops 8388608 | bytes 16777216 | tf_op jit(solution)/shard_map/pallas_call | solution.py:48
  102.6 1.4 %collective-permute-start.10 = (f32[4,128]{1,0:T(4,128)S(1)}, f32[4,128]{1,0:T(4,128)S(1)}, u32[]{:S(2)}, u32[]{:S(2)}) collective-permute-start(f32[4,128]{1,0:T(4,128)S(1)} %get-tuple-element.38.refs_0_), channel_id=1, source_target_pairs={{0,2},{1,3},{2,0},{3,1},{4,6},{5,7},{6,4},{7,5},{8,10},{9,11},{10,... | collective-permute-start | bytes 6152 | tf_op jit(solution)/shard_map/ppermute | solution.py:28
  104.3 1.8 %collective-permute-done.10.refs_2_ = f32[4,128]{1,0:T(4,128)S(1)} collective-permute-done((f32[4,128]{1,0:T(4,128)S(1)}, f32[4,128]{1,0:T(4,128)S(1)}, u32[]{:S(2)}, u32[]{:S(2)}) %collective-permute-start.10) | collective-permute-done | bytes 2080 | tf_op jit(solution)/shard_map/ppermute | solution.py:28
  107.6 3.3 %all-to-all-start.2 = ((f32[8,8,128]{2,1,0:T(8,128)}), f32[8,8,128]{2,1,0:T(8,128)S(1)}, u32[]{:S(2)}, u32[]{:S(2)}) async-start(f32[8,8,128]{2,1,0:T(8,128)} %get-tuple-element.40), calls=%async_computation.4 | async-start | bytes 65536 | tf_op jit(solution)/shard_map/all_to_all | solution.py:22
  111.0 6.6 %all-to-all-done.2.parts_ref = f32[8,8,128]{2,1,0:T(8,128)S(1)} async-done(((f32[8,8,128]{2,1,0:T(8,128)}), f32[8,8,128]{2,1,0:T(8,128)S(1)}, u32[]{:S(2)}, u32[]{:S(2)}) %all-to-all-start.2) | async-done | bytes 32800 | tf_op jit(solution)/shard_map/all_to_all | solution.py:22
  117.6 1.0 dynamic-slice_bitcast_fusion.1
  118.6 1.0 dynamic-slice_bitcast_fusion
  120.2 1.5 %collective-permute-start.13 = (f32[128,256]{1,0:T(8,128)S(1)}, f32[128,256]{1,0:T(8,128)S(1)}, u32[]{:S(2)}, u32[]{:S(2)}) collective-permute-start(f32[128,256]{1,0:T(8,128)S(1)} %get-tuple-element.47), channel_id=1, source_target_pairs={{0,4},{4,0},{8,12},{12,8},{16,20},{20,16},{24,28},{28,24},{1,5},{5... | collective-permute-start | bytes 393224 | tf_op jit(solution)/shard_map/ppermute | solution.py:387
  122.3 3.5 %collective-permute-done.12.refs_2_ = f32[128,256]{1,0:T(8,128)S(1)} collective-permute-done((f32[128,256]{1,0:T(8,128)S(1)}, f32[128,256]{1,0:T(8,128)S(1)}, u32[]{:S(2)}, u32[]{:S(2)}) %collective-permute-start.12) | collective-permute-done | bytes 131104 | tf_op jit(solution)/shard_map/ppermute | solution.py:387
  125.8 1.4 %collective-permute-done.13.refs_3_ = f32[128,256]{1,0:T(8,128)S(1)} collective-permute-done((f32[128,256]{1,0:T(8,128)S(1)}, f32[128,256]{1,0:T(8,128)S(1)}, u32[]{:S(2)}, u32[]{:S(2)}) %collective-permute-start.13) | collective-permute-done | bytes 131104 | tf_op jit(solution)/shard_map/ppermute | solution.py:387
  (45 shorter events, 8.5 us)
Async XLA Ops:
  7.2 28.1 %copy-start.7 = (bf16[256,256]{1,0:T(8,128)(2,1)S(1)}, bf16[256,256]{1,0:T(8,128)(2,1)}, u32[]{:S(2)}) copy-start(bf16[256,256]{1,0:T(8,128)(2,1)} %constant.24.clone.walsh_ref) | copy-start | bytes 393220
  7.2 28.1 %copy-start.4 = (f32[512,1024]{1,0:T(8,128)S(1)}, f32[512,1024]{1,0:T(8,128)}, u32[]{:S(2)}) copy-start(f32[512,1024]{1,0:T(8,128)} %design_ref.9) | copy-start | bytes 6291460
  7.2 28.1 %copy-start.8 = (s32[512]{0:T(512)S(1)}, s32[512]{0:T(512)}, u32[]{:S(2)}) copy-start(s32[512]{0:T(512)} %param.9) | copy-start | bytes 6148
  7.2 28.0 %all-gather.3.cloned.1.call-start = ((), (), s32[]{:S(2)}) async-start(), calls=%async_computation.5 | async-start | bytes 1572864 | tf_op jit(solution)/shard_map/all_gather | solution.py:426
  10.5 47.0 %all-gather.5.cloned.1.call-start = ((), (), s32[]{:S(2)}) async-start(), calls=%async_computation.7 | async-start | bytes 1572864 | tf_op jit(solution)/shard_map/all_gather | solution.py:426
  11.3 99.7 %reduce-scatter.3.cloned.1.call-start = ((), (), s32[]{:S(2)}) async-start(), calls=%async_computation.6 | async-start | bytes 1310720 | tf_op jit(solution)/shard_map/reduce_scatter | solution.py:379
  25.9 5.8 %copy-start = (f32[1024,4096]{1,0:T(8,128)S(1)}, f32[1024,4096]{1,0:T(8,128)}, u32[]{:S(2)}) copy-start(f32[1024,4096]{1,0:T(8,128)} %rinv_ref.7) | copy-start | bytes 50331652
  31.6 37.4 %copy-start.9 = (f32[512]{0:T(512)S(1)}, f32[512]{0:T(512)}, u32[]{:S(2)}) copy-start(f32[512]{0:T(512)} %param.12) | copy-start | bytes 6148
  35.2 1.2 copy-start.6
  42.0 75.6 %reduce-scatter.5.cloned.1.call-start = ((), (), s32[]{:S(2)}) async-start(), calls=%async_computation.8 | async-start | bytes 1310720 | tf_op jit(solution)/shard_map/reduce_scatter | solution.py:379
  42.1 1.9 %collective-permute-start = (f32[32,128]{1,0:T(8,128)S(1)}, f32[32,128]{1,0:T(8,128)S(1)}, u32[]{:S(2)}, u32[]{:S(2)}) collective-permute-start(f32[32,128]{1,0:T(8,128)S(1)} %get-tuple-element.28.refs_0_), channel_id=1, source_target_pairs={{0,1},{1,0},{2,3},{3,2},{4,5},{5,4},{6,7},{7,6},{8,9},{9,8},{10,11... | collective-permute-start | bytes 49160 | tf_op jit(solution)/shard_map/ppermute | solution.py:28
  42.1 3.8 %collective-permute-start.1 = (f32[32,128]{1,0:T(8,128)S(1)}, f32[32,128]{1,0:T(8,128)S(1)}, u32[]{:S(2)}, u32[]{:S(2)}) collective-permute-start(f32[32,128]{1,0:T(8,128)S(1)} %get-tuple-element.28.refs_0_), channel_id=1, source_target_pairs={{0,2},{1,3},{2,0},{3,1},{4,6},{5,7},{6,4},{7,5},{8,10},{9,11},{10,... | collective-permute-start | bytes 49160 | tf_op jit(solution)/shard_map/ppermute | solution.py:28
  43.7 3.2 %collective-permute-start.2 = (f32[32,128]{1,0:T(8,128)S(1)}, f32[32,128]{1,0:T(8,128)S(1)}, u32[]{:S(2)}, u32[]{:S(2)}) collective-permute-start(f32[32,128]{1,0:T(8,128)S(1)} %get-tuple-element.28.refs_0_), channel_id=1, source_target_pairs={{0,3},{1,2},{2,1},{3,0},{4,7},{5,6},{6,5},{7,4},{8,11},{9,10},{10,... | collective-permute-start | bytes 49160 | tf_op jit(solution)/shard_map/ppermute | solution.py:28
  46.8 5.8 %copy-start.1 = (f32[1024,4096]{1,0:T(8,128)S(1)}, f32[1024,4096]{1,0:T(8,128)}, u32[]{:S(2)}) copy-start(f32[1024,4096]{1,0:T(8,128)} %rinv_ref.7) | copy-start | bytes 50331652
  57.6 1.2 copy-start.5
  64.4 1.9 %collective-permute-start.3 = (f32[4,128]{1,0:T(4,128)S(1)}, f32[4,128]{1,0:T(4,128)S(1)}, u32[]{:S(2)}, u32[]{:S(2)}) collective-permute-start(f32[4,128]{1,0:T(4,128)S(1)} %get-tuple-element.29.refs_0_), channel_id=1, source_target_pairs={{0,1},{1,0},{2,3},{3,2},{4,5},{5,4},{6,7},{7,6},{8,9},{9,8},{10,11... | collective-permute-start | bytes 6152 | tf_op jit(solution)/shard_map/ppermute | solution.py:28
  64.5 3.7 %collective-permute-start.4 = (f32[4,128]{1,0:T(4,128)S(1)}, f32[4,128]{1,0:T(4,128)S(1)}, u32[]{:S(2)}, u32[]{:S(2)}) collective-permute-start(f32[4,128]{1,0:T(4,128)S(1)} %get-tuple-element.29.refs_0_), channel_id=1, source_target_pairs={{0,2},{1,3},{2,0},{3,1},{4,6},{5,7},{6,4},{7,5},{8,10},{9,11},{10,... | collective-permute-start | bytes 6152 | tf_op jit(solution)/shard_map/ppermute | solution.py:28
  66.0 3.0 %collective-permute-start.5 = (f32[4,128]{1,0:T(4,128)S(1)}, f32[4,128]{1,0:T(4,128)S(1)}, u32[]{:S(2)}, u32[]{:S(2)}) collective-permute-start(f32[4,128]{1,0:T(4,128)S(1)} %get-tuple-element.29.refs_0_), channel_id=1, source_target_pairs={{0,3},{1,2},{2,1},{3,0},{4,7},{5,6},{6,5},{7,4},{8,11},{9,10},{10,... | collective-permute-start | bytes 6152 | tf_op jit(solution)/shard_map/ppermute | solution.py:28
  81.8 5.9 %copy-start.2 = (f32[1024,4096]{1,0:T(8,128)S(1)}, f32[1024,4096]{1,0:T(8,128)}, u32[]{:S(2)}) copy-start(f32[1024,4096]{1,0:T(8,128)} %rinv_ref.7) | copy-start | bytes 50331652
  89.5 1.9 %collective-permute-start.6 = (f32[32,128]{1,0:T(8,128)S(1)}, f32[32,128]{1,0:T(8,128)S(1)}, u32[]{:S(2)}, u32[]{:S(2)}) collective-permute-start(f32[32,128]{1,0:T(8,128)S(1)} %get-tuple-element.32.refs_0_), channel_id=1, source_target_pairs={{0,1},{1,0},{2,3},{3,2},{4,5},{5,4},{6,7},{7,6},{8,9},{9,8},{10,11... | collective-permute-start | bytes 49160 | tf_op jit(solution)/shard_map/ppermute | solution.py:28
  89.6 3.9 %collective-permute-start.7 = (f32[32,128]{1,0:T(8,128)S(1)}, f32[32,128]{1,0:T(8,128)S(1)}, u32[]{:S(2)}, u32[]{:S(2)}) collective-permute-start(f32[32,128]{1,0:T(8,128)S(1)} %get-tuple-element.32.refs_0_), channel_id=1, source_target_pairs={{0,2},{1,3},{2,0},{3,1},{4,6},{5,7},{6,4},{7,5},{8,10},{9,11},{10,... | collective-permute-start | bytes 49160 | tf_op jit(solution)/shard_map/ppermute | solution.py:28
  90.2 3.3 %collective-permute-start.8 = (f32[32,128]{1,0:T(8,128)S(1)}, f32[32,128]{1,0:T(8,128)S(1)}, u32[]{:S(2)}, u32[]{:S(2)}) collective-permute-start(f32[32,128]{1,0:T(8,128)S(1)} %get-tuple-element.32.refs_0_), channel_id=1, source_target_pairs={{0,3},{1,2},{2,1},{3,0},{4,7},{5,6},{6,5},{7,4},{8,11},{9,10},{10,... | collective-permute-start | bytes 49160 | tf_op jit(solution)/shard_map/ppermute | solution.py:28
  93.5 6.0 %copy-start.3 = (f32[1024,4096]{1,0:T(8,128)S(1)}, f32[1024,4096]{1,0:T(8,128)}, u32[]{:S(2)}) copy-start(f32[1024,4096]{1,0:T(8,128)} %rinv_ref.7) | copy-start | bytes 50331652
  102.4 1.9 %collective-permute-start.9 = (f32[4,128]{1,0:T(4,128)S(1)}, f32[4,128]{1,0:T(4,128)S(1)}, u32[]{:S(2)}, u32[]{:S(2)}) collective-permute-start(f32[4,128]{1,0:T(4,128)S(1)} %get-tuple-element.38.refs_0_), channel_id=1, source_target_pairs={{0,1},{1,0},{2,3},{3,2},{4,5},{5,4},{6,7},{7,6},{8,9},{9,8},{10,11... | collective-permute-start | bytes 6152 | tf_op jit(solution)/shard_map/ppermute | solution.py:28
  102.6 3.6 %collective-permute-start.10 = (f32[4,128]{1,0:T(4,128)S(1)}, f32[4,128]{1,0:T(4,128)S(1)}, u32[]{:S(2)}, u32[]{:S(2)}) collective-permute-start(f32[4,128]{1,0:T(4,128)S(1)} %get-tuple-element.38.refs_0_), channel_id=1, source_target_pairs={{0,2},{1,3},{2,0},{3,1},{4,6},{5,7},{6,4},{7,5},{8,10},{9,11},{10,... | collective-permute-start | bytes 6152 | tf_op jit(solution)/shard_map/ppermute | solution.py:28
  103.9 3.0 %collective-permute-start.11 = (f32[4,128]{1,0:T(4,128)S(1)}, f32[4,128]{1,0:T(4,128)S(1)}, u32[]{:S(2)}, u32[]{:S(2)}) collective-permute-start(f32[4,128]{1,0:T(4,128)S(1)} %get-tuple-element.38.refs_0_), channel_id=1, source_target_pairs={{0,3},{1,2},{2,1},{3,0},{4,7},{5,6},{6,5},{7,4},{8,11},{9,10},{10,... | collective-permute-start | bytes 6152 | tf_op jit(solution)/shard_map/ppermute | solution.py:28
  107.6 10.0 %all-to-all-start.2 = ((f32[8,8,128]{2,1,0:T(8,128)}), f32[8,8,128]{2,1,0:T(8,128)S(1)}, u32[]{:S(2)}, u32[]{:S(2)}) async-start(f32[8,8,128]{2,1,0:T(8,128)} %get-tuple-element.40), calls=%async_computation.4 | async-start | bytes 65536 | tf_op jit(solution)/shard_map/all_to_all | solution.py:22
  119.6 6.2 %collective-permute-start.12 = (f32[128,256]{1,0:T(8,128)S(1)}, f32[128,256]{1,0:T(8,128)S(1)}, u32[]{:S(2)}, u32[]{:S(2)}) collective-permute-start(f32[128,256]{1,0:T(8,128)S(1)} %get-tuple-element.49), channel_id=1, source_target_pairs={{0,4},{4,0},{8,12},{12,8},{16,20},{20,16},{24,28},{28,24},{1,5},{5... | collective-permute-start | bytes 393224 | tf_op jit(solution)/shard_map/ppermute | solution.py:387
  120.2 7.0 %collective-permute-start.13 = (f32[128,256]{1,0:T(8,128)S(1)}, f32[128,256]{1,0:T(8,128)S(1)}, u32[]{:S(2)}, u32[]{:S(2)}) collective-permute-start(f32[128,256]{1,0:T(8,128)S(1)} %get-tuple-element.47), channel_id=1, source_target_pairs={{0,4},{4,0},{8,12},{12,8},{16,20},{20,16},{24,28},{28,24},{1,5},{5... | collective-permute-start | bytes 393224 | tf_op jit(solution)/shard_map/ppermute | solution.py:387
Sparse Core Ops, SparseCore 0:
  10.7 24.5 all-gather.2
  36.8 20.7 all-gather.4
  59.9 28.1 reduce-scatter.2
  90.4 25.8 reduce-scatter.4

commit v4 on v3

--- a/solution.py
+++ b/solution.py
@@ -12,7 +12,7 @@
 PAIR = 16
 ITERS = 2
 LANE = 128
-CHUNKS = 2
+NEAR = 4
 F32 = jnp.float32
 VMEM = pl.BlockSpec(memory_space=pltpu.VMEM)
 HBM = pl.BlockSpec(memory_space=pltpu.HBM)
@@ -80,7 +80,7 @@
         out_ref[tile : tile + 1, :] = jnp.sum(sums[tile], axis=0, keepdims=True)
 
 
-def left_product_long(vector_ref, matrix_ref, out_ref):
+def left_product_long(vector_ref, matrix_ref, out_ref, copies=()):
     blocks, tiles = matrix_ref.shape[0] // LANE, matrix_ref.shape[1] // LANE
 
     def step(block, sums):
@@ -91,7 +91,13 @@
             for tile in range(tiles)
         )
 
-    sums = lax.fori_loop(0, blocks, step, tuple(jnp.zeros((8, LANE), F32) for _ in range(tiles)))
+    sums = tuple(jnp.zeros((8, LANE), F32) for _ in range(tiles))
+    if copies:
+        for block, copy in enumerate(copies):
+            copy.wait()
+            sums = step(block, sums)
+    else:
+        sums = lax.fori_loop(0, blocks, step, sums)
     for tile in range(tiles):
         out_ref[tile : tile + 1, :] = jnp.sum(sums[tile], axis=0, keepdims=True)
 
@@ -130,12 +136,10 @@
 
 
 def first_body(design_ref, target_ref, bits_ref, picks_ref, counts_ref, *refs):
-    chunks = len(refs) - 8
-    out_ref, away_refs = refs[0], refs[1 : 1 + chunks]
-    design, target_here, bits, picks, counts, away, sems = refs[1 + chunks :]
+    out_ref, away_refs = refs[0], refs[1:NEAR]
+    design, target_here, bits, picks, counts, away, sems = refs[NEAR:]
     rows, width = design.shape
-    lines, tiles, half = rows // LANE, width // LANE, width // 2
-    piece = half // chunks
+    lines, tiles, piece = rows // LANE, width // LANE, width // NEAR
     small = [
         pltpu.make_async_copy(source, place, sems.at[index])
         for index, (source, place) in enumerate(
@@ -151,7 +155,7 @@
         copy.start()
     for copy in small:
         copy.wait()
-    low = lax.axis_index("row") & 1
+    place = lax.axis_index("row") % NEAR
     sums = [jnp.zeros((8, LANE), F32) for _ in range(tiles)]
     back = []
     for line, part in enumerate(parts):
@@ -161,14 +165,12 @@
         for tile in range(tiles):
             value = design[part, tile * LANE : (tile + 1) * LANE]
             sums[tile] = sums[tile] + fold_rows(value * across)
-        for tile in range(0, half, LANE):
-            column = pl.multiple_of((1 - low) * half + tile, LANE)
-            away[part, tile : tile + LANE] = design[part, pl.ds(column, LANE)] * signs
-        for chunk in range(chunks):
+        for mask in range(1, NEAR):
+            for tile in range(0, piece, LANE):
+                column = pl.multiple_of((place ^ mask) * piece + tile, LANE)
+                away[mask - 1, part, tile : tile + LANE] = design[part, pl.ds(column, LANE)] * signs
             copy = pltpu.make_async_copy(
-                away.at[part, chunk * piece : (chunk + 1) * piece],
-                away_refs[chunk].at[part, :],
-                sems.at[4 + lines * (1 + chunk) + line],
+                away.at[mask - 1, part, :], away_refs[mask - 1].at[part, :], sems.at[4 + lines * mask + line]
             )
             copy.start()
             back.append(copy)
@@ -190,13 +192,22 @@
         copy.wait()
 
 
-def back_body(rinv_ref, parts_ref, term_ref, beta_ref, scratch):
+def back_body(first, rinv_ref, parts_ref, term_ref, beta_ref, *refs):
     tiles = rinv_ref.shape[0] // LANE
+    copies = []
+    if first:
+        rinv_here, scratch, sems = refs
+        for block in range(tiles):
+            part = slice(block * LANE, (block + 1) * LANE)
+            copies.append(pltpu.make_async_copy(rinv_ref.at[part, :], rinv_here.at[part, :], sems.at[block]))
+            copies[-1].start()
+    else:
+        rinv_here, (scratch,) = rinv_ref, refs
     summed = tree([parts_ref[i, : tiles + 1, :] for i in range(parts_ref.shape[0])])
     beta = jnp.sqrt(summed[tiles : tiles + 1, :])
     beta_ref[...] = beta
     scratch[...] = summed[:tiles, :] / beta
-    left_product_long(scratch, rinv_ref, term_ref)
+    left_product_long(scratch, rinv_here, term_ref, copies)
 
 
 def forward_body(groups, first, rinv_ref, design_ref, *refs):
@@ -257,66 +268,100 @@
     solution_ref[...] = iterate
 
 
-def sample_body(
-    chunk, scale, parts_ref, walsh_ref, design_ref, bits_ref, pair_ref, order_ref, out_ref, both
-):
-    groups, piece = out_ref.shape[0], out_ref.shape[3]
-    rows, width = design_ref.shape
+def mix_body(parts_ref, walsh_ref, order_ref, out_ref):
+    groups, _, rows = out_ref.shape
     spread = rounded(groups, 8)
     start = parts_ref.shape[1] - spread
-    me, block = lax.axis_index("row"), pl.program_id(0)
-    low = me & 1
-
-    @pl.when(block == 0)
-    def _():
-        for line in range(rows // LANE):
-            part = slice(line * LANE, (line + 1) * LANE)
-            far = pl.ds(pl.multiple_of((1 - low) * rows + line * LANE, LANE), LANE)
-            signs = signs_across(bits_ref, line)
-            for tile in range(0, piece, LANE):
-                column = pl.multiple_of(low * (width // 2) + chunk * piece + tile, LANE)
-                mine = design_ref[part, pl.ds(column, LANE)] * signs
-                other = pair_ref[far, tile : tile + LANE]
-                for index, value in enumerate((mine + other, mine - other)):
-                    high = value.astype(jnp.bfloat16)
-                    both[index, 0, part, tile : tile + LANE] = high
-                    both[index, 1, part, tile : tile + LANE] = (value - high.astype(F32)).astype(jnp.bfloat16)
-
-    coded = parts_ref[block, start : start + spread, :]
-    filler = jnp.zeros((LANE - spread, LANE), F32)
-    coded = jnp.concatenate([coded, filler], axis=0).T
-    parity = jnp.int32(0)
-    for bit in range(groups.bit_length() - 1):
-        parity = parity ^ ((block & me) >> bit)
-    sign = (1 - 2 * (parity & 1)).astype(F32)
+    me = lax.axis_index("row")
     local = lax.broadcasted_iota(jnp.int32, (PAIR, rows), 1).astype(F32)
-    chosen = []
-    for owner in range(groups):
-        match = jnp.broadcast_to(coded[:PAIR, owner : owner + 1], (PAIR, rows)) == local
-        chosen.append(jnp.where(match, sign, 0.0))
-    chosen = jnp.concatenate(chosen, axis=0).astype(jnp.bfloat16)
-    mix = []
-    for part in range(rows // HB):
-        mixed = jnp.dot(chosen[:, part * HB : (part + 1) * HB], walsh_ref[...], preferred_element_type=F32)
-        mix.append(mixed.astype(jnp.bfloat16))
-    mix = jnp.concatenate(mix, axis=1)
-    value = jnp.dot(mix, both[block & 1, 0], preferred_element_type=F32)
-    value = value + jnp.dot(mix, both[block & 1, 1], preferred_element_type=F32)
-    out_ref[...] = (value / scale).reshape(out_ref.shape)
+
+    def step(block, carry):
+        coded = [parts_ref[block, pl.ds(start + (apart ^ me), 1), :] for apart in range(groups)]
+        coded = jnp.concatenate(coded + [jnp.zeros((LANE - groups, LANE), F32)], axis=0).T
+        parity = jnp.int32(0)
+        for bit in range(groups.bit_length() - 1):
+            parity = parity ^ ((block & me) >> bit)
+        sign = (1 - 2 * (parity & 1)).astype(F32)
+        chosen = []
+        for apart in range(groups):
+            match = jnp.broadcast_to(coded[:PAIR, apart : apart + 1], (PAIR, rows)) == local
+            chosen.append(jnp.where(match, sign, 0.0))
+        chosen = jnp.concatenate(chosen, axis=0).astype(jnp.bfloat16)
+        for part in range(rows // HB):
+            columns = slice(part * HB, (part + 1) * HB)
+            mixed = jnp.dot(chosen[:, columns], walsh_ref[...], preferred_element_type=F32)
+            out_ref[block, :, columns] = mixed.astype(jnp.bfloat16)
+        return carry
+
+    if groups <= 8:
+        for block in range(groups):
+            step(block, 0)
+    else:
+        lax.fori_loop(0, groups, step, 0)
+
+
+def sample_body(scale, design_ref, bits_ref, mix_ref, order_ref, *refs):
+    near, (keep_ref, send_ref, both) = refs[: NEAR - 1], refs[NEAR - 1 :]
+    rows, piece = near[0].shape
+    groups = mix_ref.shape[0]
+    place = lax.axis_index("row") % NEAR
+    for line in range(rows // LANE):
+        part = slice(line * LANE, (line + 1) * LANE)
+        signs = signs_across(bits_ref, line)
+        for tile in range(0, piece, LANE):
+            column = pl.multiple_of(place * piece + tile, LANE)
+            here = slice(tile, tile + LANE)
+            values = [design_ref[part, pl.ds(column, LANE)] * signs] + [ref[part, here] for ref in near]
+            apart = 1
+            while apart < NEAR:
+                for first in range(NEAR):
+                    if not first & apart:
+                        one, two = values[first], values[first | apart]
+                        values[first], values[first | apart] = one + two, one - two
+                apart *= 2
+            for index, value in enumerate(values):
+                high = value.astype(jnp.bfloat16)
+                both[index, 0, part, here] = high
+                both[index, 1, part, here] = (value - high.astype(F32)).astype(jnp.bfloat16)
+
+    def step(block, carry):
+        mix = mix_ref[block]
+        value = jnp.dot(mix, both[block % NEAR, 0], preferred_element_type=F32)
+        value = value + jnp.dot(mix, both[block % NEAR, 1], preferred_element_type=F32)
+        value = value / scale
+        slot = pl.ds(block * PAIR, PAIR)
+        for apart in range(groups):
+            far, low = apart // NEAR, apart % NEAR
+            out_ref = send_ref if far >= groups // NEAR // 2 else keep_ref
+            out_ref[far % (groups // NEAR // 2), low, slot, :] = value[apart * PAIR : (apart + 1) * PAIR, :]
+        return carry
+
+    if groups <= 8:
+        for block in range(groups):
+            step(block, 0)
+    else:
+        lax.fori_loop(0, groups, step, 0)
+
+
+def halve_body(kept_ref, arrived_ref, order_ref, keep_ref, send_ref):
+    half = keep_ref.shape[0]
+    keep_ref[...] = kept_ref[:half] + arrived_ref[:half]
+    send_ref[...] = kept_ref[half:] + arrived_ref[half:]
+
+
+def split_body(kept_ref, arrived_ref, order_ref, *out_refs):
+    for index, out_ref in enumerate(out_refs):
+        out_ref[...] = kept_ref[0, index] + arrived_ref[0, index]
 
 
 def assemble_body(*refs):
-    chunks = len(refs) // 2
-    mine, other, out_ref = refs[:chunks], refs[chunks : 2 * chunks], refs[-1]
-    low = lax.axis_index("row") & 1
-    half = out_ref.shape[1] // 2
-    for chunk in range(chunks):
-        piece = half // chunks
+    parts, out_ref = refs[:-1], refs[-1]
+    place = lax.axis_index("row") % NEAR
+    piece = parts[0].shape[1]
+    for mask, part_ref in enumerate(parts):
         for tile in range(0, piece, LANE):
-            near = pl.multiple_of(low * half + chunk * piece + tile, LANE)
-            far = pl.multiple_of((1 - low) * half + chunk * piece + tile, LANE)
-            out_ref[:, pl.ds(near, LANE)] = mine[chunk][:, tile : tile + LANE]
-            out_ref[:, pl.ds(far, LANE)] = other[chunk][:, tile : tile + LANE]
+            column = pl.multiple_of((place ^ mask) * piece + tile, LANE)
+            out_ref[:, pl.ds(column, LANE)] = part_ref[:, tile : tile + LANE]
 
 
 def shape(*dims, dtype=F32):
@@ -333,75 +378,86 @@
     deep = message_rows(width)
     left = target.reshape(lines, LANE)
     bits = sign_bits.reshape(lines, LANE)
-    half = width // 2
-    chunks = min(CHUNKS, half // LANE)
-    piece = half // chunks
-    pairs = [[i, i + 1] for i in range(0, row_groups, 2)]
-    quads = [list(range(i, row_groups, 2)) for i in range(2)]
+    piece = width // NEAR
+    slots = row_groups * PAIR
+    far = row_groups // NEAR
 
     message, *away = pl.pallas_call(
         first_body,
-        out_shape=(shape(row_groups, deep + rounded(row_groups, 8), LANE),) + (shape(rows, piece),) * chunks,
+        out_shape=(shape(row_groups, deep + rounded(row_groups, 8), LANE),) + (shape(rows, piece),) * (NEAR - 1),
         in_specs=[HBM] * 5,
-        out_specs=(VMEM,) + (HBM,) * chunks,
+        out_specs=(VMEM,) + (HBM,) * (NEAR - 1),
         scratch_shapes=[
             pltpu.VMEM((rows, width), F32),
             pltpu.VMEM((lines, LANE), F32),
             pltpu.VMEM((lines, LANE), jnp.int32),
             pltpu.VMEM((row_groups, PAIR), jnp.int32),
             pltpu.VMEM((1, row_groups), jnp.int32),
-            pltpu.VMEM((rows, half), F32),
-            pltpu.SemaphoreType.DMA((4 + lines * (1 + chunks),)),
+            pltpu.VMEM((NEAR - 1, rows, piece), F32),
+            pltpu.SemaphoreType.DMA((4 + lines * NEAR,)),
         ],
         compiler_params=pltpu.CompilerParams(vmem_limit_bytes=58 << 20),
-        cost_estimate=pl.CostEstimate(flops=2 * small, bytes_accessed=6 * small, transcendentals=0),
+        cost_estimate=pl.CostEstimate(flops=2 * small, bytes_accessed=7 * small, transcendentals=0),
     )(design, left, bits, picks.reshape(row_groups, PAIR), counts.reshape(1, row_groups))
 
-    def sample(chunk, pair, order):
+    def swap(array, mask):
+        return lax.ppermute(array, "row", [(i, i ^ mask) for i in range(row_groups)])
+
+    def mix(order):
+        signs = jnp.asarray(walsh(HB), jnp.bfloat16)
+        made = shape(row_groups, slots, rows, dtype=jnp.bfloat16)
+        return call(mix_body, made, picked, signs, order, flops=2 * row_groups * slots * rows * HB)
+
+    def sample(near, mixed, order):
         scale = float(np.sqrt(np.float32(rows * row_groups)))
-        signs = jnp.asarray(walsh(HB), jnp.bfloat16)
-        operands = (picked, signs, design, bits, pair, order)
-        made = pl.pallas_call(
-            functools.partial(sample_body, chunk, scale),
-            grid=(row_groups,),
-            out_shape=shape(row_groups, row_groups, PAIR, piece),
-            in_specs=[VMEM] * len(operands),
-            out_specs=pl.BlockSpec((row_groups, 1, PAIR, piece), lambda block: (0, block, 0, 0)),
-            scratch_shapes=[pltpu.VMEM((2, 2, rows, piece), jnp.bfloat16)],
-            compiler_params=pltpu.CompilerParams(vmem_limit_bytes=20 << 20),
-            cost_estimate=pl.CostEstimate(
-                flops=8 * row_groups * row_groups * PAIR * rows * piece,
-                bytes_accessed=4 * row_groups * row_groups * PAIR * piece,
-                transcendentals=0,
-            ),
-        )(*operands)
-        made = made.reshape(row_groups * row_groups * PAIR, piece)
-        return lax.psum_scatter(made, "row", scatter_dimension=0, axis_index_groups=quads, tiled=True)
-
-    def finish(summed, order):
-        summed, _ = lax.optimization_barrier((summed, order))
-        low = lax.axis_index("row") & 1
-        summed = summed.reshape(2, row_groups * PAIR, piece)
-        mine = lax.dynamic_index_in_dim(summed, low, 0, keepdims=False)
-        other = lax.dynamic_index_in_dim(summed, 1 - low, 0, keepdims=False)
-        return mine, lax.ppermute(other, "row", [(i, i ^ 1) for i in range(row_groups)])
-
-    def back(message):
         return call(
-            back_body,
-            (shape(whole // LANE, LANE), scalar),
-            rinv,
-            message,
-            scratch=[pltpu.VMEM((width // LANE, LANE), F32)],
-            flops=2 * big,
-            size=4 * big,
+            functools.partial(sample_body, scale),
+            (shape(far // 2, NEAR, slots, piece),) * 2,
+            design,
+            bits,
+            mixed,
+            order,
+            *near,
+            scratch=[pltpu.VMEM((NEAR, 2, rows, piece), jnp.bfloat16)],
+            flops=4 * row_groups * slots * rows * piece,
+            size=4 * NEAR * rows * piece,
         )
+
+    def gather_rows(keep, send, order):
+        bit = row_groups // 2
+        come = swap(send, bit)
+        while bit > NEAR:
+            bit //= 2
+            half = keep.shape[0] // 2
+            keep, send = call(halve_body, (shape(half, *keep.shape[1:]),) * 2, keep, come, order)
+            come = swap(send, bit)
+        return keep, come
+
+    def trade(keep, come, order):
+        mine, *others = call(split_body, (shape(slots, piece),) * NEAR, keep, come, order)
+        parts = [mine] + [swap(part, mask + 1) for mask, part in enumerate(others)]
+        return call(assemble_body, shape(slots, width), *parts, size=8 * slots * width)
+
+    def back(rinv, message, first):
+        outs, scratch = (shape(whole // LANE, LANE), scalar), [pltpu.VMEM((width // LANE, LANE), F32)]
+        if first:
+            outs += (shape(*rinv.shape),)
+            scratch += [pltpu.SemaphoreType.DMA((width // LANE,))]
+        return pl.pallas_call(
+            functools.partial(back_body, first),
+            out_shape=outs,
+            in_specs=[HBM if first else VMEM, VMEM],
+            out_specs=(VMEM,) * len(outs),
+            scratch_shapes=scratch,
+            compiler_params=pltpu.CompilerParams(vmem_limit_bytes=(34 if first else 24) << 20),
+            cost_estimate=pl.CostEstimate(flops=2 * big, bytes_accessed=4 * big, transcendentals=0),
+        )(rinv, message)
 
     def forward(terms, *before):
         return call(
             functools.partial(forward_body, col_groups, not before),
             (shape(lines, LANE), shape(whole // LANE, LANE), shape(width // LANE, LANE), scalar),
-            rinv,
+            here,
             design,
             *terms,
             *before,
@@ -422,28 +478,30 @@
             size=0 if last else 4 * small,
         )
 
-    betas, alphas, held, summed = [], [], [], []
-    pair = [lax.all_gather(part, "row", axis=0, axis_index_groups=pairs, tiled=True) for part in away]
+    betas, alphas, held = [], [], []
     message = picked = exchange(message, "row")
     for step in range(ITERS):
-        term, beta = back(message)
+        if step == 0:
+            term, beta, here = back(rinv, message, True)
+            away, _ = lax.optimization_barrier((away, beta))
+            near = [swap(part, mask + 1) for mask, part in enumerate(away)]
+        else:
+            term, beta = back(here, message, False)
+            keep, come = gather_rows(*sample(near, mixed, beta), beta)
         betas.append(beta)
-        if step == 0:
-            summed.append(sample(0, pair[0], beta))
         terms = direct(term, "col")
         image, right, part, alpha = forward(terms, *(() if step == 0 else (right, beta)))
+        if step == 0:
+            mixed = mix(alpha)
         alphas.append(alpha)
         held.append(part)
-        if step == 0:
-            summed += [sample(chunk, pair[chunk], alpha) for chunk in range(1, chunks)]
         images = direct(image, "col")
         left, message = turn(images, left, beta, alpha, step + 1 == ITERS)
         message = exchange(message, "row")
     basis, answer = call(
         last_body, (shape(lines, LANE), shape(width // LANE, LANE)), message, left, *betas, *alphas, *held
     )
-    mine, other = zip(*[finish(value, message if i else alpha) for i, value in enumerate(summed)])
-    sketch = call(assemble_body, shape(row_groups * PAIR, width), *mine, *other)
+    sketch = trade(keep, come, message)
     return (sketch, answer.reshape(-1), basis.reshape(-1))
 
 

time: 135 us -> 104 us (0.77)
  local copies, waits for them, and re-layouts: 27.8 us -> 11.5 us
  between operations: 13.9 us -> 0.76 us
  waiting for transfers between devices: 26.8 us -> 20.3 us
  starting transfers between devices: 13.3 us -> 19.1 us
  Pallas kernels: 25.7 us -> 23.5 us
    unnamed x20 -> x14, local copies, waits for them, and re-layouts: 25.8 us -> 11.5 us
    ppermute x2 -> x7, starting transfers between devices: 2.09 us -> 7.65 us  [swap(): lax.ppermute(array, 'row', [(i, i ^ mask) for i in range(row_groups)])]
    all_gather x2 -> x0, waiting for transfers between devices: 4.35 us -> none  [shards(): lax.all_gather(part, 'row', axis=0, axis_index_groups=pairs, tiled=True)]
    pallas_call x2, Pallas kernels: 11.1 us -> 8.02 us  [back(): pl.pallas_call(functools.partial(back_body, first), out_shape=outs, in_sp...]
    squeeze x2 -> x0, local copies, waits for them, and re-layouts: 1.98 us -> none  [finish(): other = lax.dynamic_index_in_dim(summed, 1 - low, 0, keepdims=False)]
    pallas_call x8 -> x9, Pallas kernels: 11.4 us -> 12.2 us  [call(): pl.pallas_call(body, out_shape=out_shape, in_specs=[VMEM] * len(operands)...]
    ppermute x2 -> x7, waiting for transfers between devices: 4.86 us -> 5.12 us  [swap(): lax.ppermute(array, 'row', [(i, i ^ mask) for i in range(row_groups)])]
  transfers between devices with their start and end apart: 19 -> 20, of which waited for: 12 -> 13; matrix products, arithmetic and copies ran while one was open for 0% -> 0% of each run, Pallas kernels for 16% -> 9%
where the time goes in v4:
time: 104 us
  blocking collectives  28.3 us (27%)
  Pallas kernels  23.5 us (23%)
  waiting for transfers between devices  20.3 us (20%)
  starting transfers between devices  19.1 us (18%)
  local copies, waits for them, and re-layouts  11.5 us (11%)
    all_to_all x2, blocking collectives, exchange(): return lax.all_to_all(copies, axis, split_axis=0, concat_axis=0, tiled=True)  28.3 us
    pallas_call x9, Pallas kernels, call(): pl.pallas_call(body, out_shape=out_shape, in_specs=[VMEM] * len(operands)...  12.2 us
    unnamed x14, local copies, waits for them, and re-layouts  11.5 us
    ppermute x12, waiting for transfers between devices, direct(): lax.ppermute(array, axis, [(i, i ^ mask) for i in range(size)])  9.28 us
    ppermute x12, starting transfers between devices, direct(): lax.ppermute(array, axis, [(i, i ^ mask) for i in range(size)])  8.1 us
    pallas_call x2, Pallas kernels, back(): pl.pallas_call(functools.partial(back_body, first), out_shape=outs, in_sp...  8.02 us
    ppermute x7, starting transfers between devices, swap(): lax.ppermute(array, 'row', [(i, i ^ mask) for i in range(row_groups)])  7.65 us
    all_to_all x1, waiting for transfers between devices, exchange(): return lax.all_to_all(copies, axis, split_axis=0, concat_axis=0, tiled=True)  5.91 us
  transfers between devices with their start and end apart: 20, of which 13 were waited for; matrix products, arithmetic and copies ran while one was open for 0% of the time, Pallas kernels for 9%

profile of v4, /device:TPU:0, one launch (start us, length us, event | category | flops | bytes accessed | tf_op | source)
XLA Modules:
  0.0 103.5 jit_solution(11991838002588759190)
XLA Ops:
  0.6 3.3 %shard_map.94 = (f32[8,24,128]{2,1,0:T(8,128)}, f32[512,256]{1,0:T(8,128)}, f32[512,256]{1,0:T(8,128)}, f32[512,256]{1,0:T(8,128)}) custom-call(f32[512,1024]{1,0:T(8,128)} %design_ref.7, f32[4,128]{1,0:T(4,128)} %bitcast.6, s32[4,128]{1,0:T(4,128)} %bitcast.8, s32[8,16]{1,0:T(8,128)} %bitcast.10, s32[1,8]{1,0:T(1,128)} %bitcast.11), custom_call_target="tpu_custom_call" | custom-call | flops 1048576 | bytes 3670016 | tf_op jit(solution)/shard_map/pallas_call | solution.py:385
  4.0 14.4 %all_to_all.15.parts_ref = f32[8,24,128]{2,1,0:T(8,128)S(1)} all-to-all(f32[8,24,128]{2,1,0:T(8,128)} %get-tuple-element.34), channel_id=1, replica_groups=mesh['row'=8,'col'=4] {'row'}, dimensions={0} | all-to-all | bytes 196608 | tf_op jit(solution)/shard_map/all_to_all | solution.py:22
  18.4 6.2 %shard_map.95 = (f32[32,128]{1,0:T(8,128)S(1)}, f32[1,128]{1,0:T(1,128)S(1)}, f32[1024,4096]{1,0:T(8,128)S(1)}) custom-call(f32[1024,4096]{1,0:T(8,128)} %rinv_ref.1, f32[8,24,128]{2,1,0:T(8,128)S(1)} %all_to_all.15.parts_ref), custom_call_target="tpu_custom_call" | custom-call | flops 8388608 | bytes 16777216 | tf_op jit(solution)/shard_map/pallas_call | solution.py:446
  25.0 1.0 collective-permute-start.7
  25.9 2.2 %collective-permute-start.8 = (f32[512,256]{1,0:T(8,128)}, f32[512,256]{1,0:T(8,128)}, u32[]{:S(2)}, u32[]{:S(2)}) collective-permute-start(f32[512,256]{1,0:T(8,128)} %get-tuple-element.47), channel_id=1, source_target_pairs={{0,12},{4,8},{8,4},{12,0},{16,28},{20,24},{24,20},{28,16},{1,13},{... | collective-permute-start | bytes 1572872 | tf_op jit(solution)/shard_map/ppermute | solution.py:404
  28.2 1.5 %collective-permute-start.1 = (f32[32,128]{1,0:T(8,128)S(1)}, f32[32,128]{1,0:T(8,128)S(1)}, u32[]{:S(2)}, u32[]{:S(2)}) collective-permute-start(f32[32,128]{1,0:T(8,128)S(1)} %get-tuple-element.36.refs_0_), channel_id=1, source_target_pairs={{0,2},{1,3},{2,0},{3,1},{4,6},{5,7},{6,4},{7,5},{8,10},{9,11},{10,... | collective-permute-start | bytes 49160 | tf_op jit(solution)/shard_map/ppermute | solution.py:28
  29.7 1.8 %collective-permute-done.2.refs_3_ = f32[32,128]{1,0:T(8,128)S(1)} collective-permute-done((f32[32,128]{1,0:T(8,128)S(1)}, f32[32,128]{1,0:T(8,128)S(1)}, u32[]{:S(2)}, u32[]{:S(2)}) %collective-permute-start.2) | collective-permute-done | bytes 16416 | tf_op jit(solution)/shard_map/ppermute | solution.py:28
  32.6 2.5 %shard_map.96 = (f32[4,128]{1,0:T(4,128)S(1)}, f32[32,128]{1,0:T(8,128)S(1)}, f32[8,128]{1,0:T(8,128)S(1)}, f32[1,128]{1,0:T(1,128)S(1)}) custom-call(f32[1024,4096]{1,0:T(8,128)S(1)} %get-tuple-element.35.rinv_ref, f32[512,1024]{1,0:T(8,128)S(1)} %copy-done.3, f32[32,128]{1,0:T(8,128)S(1)} %get-tuple-element.36.refs_0_, ...), custom_call_target="tpu_custom_call" | custom-call | flops 8388608 | bytes 16777216 | tf_op jit(solution)/shard_map/pallas_call | solution.py:48
  35.1 5.8 %copy-done = f32[1024,4096]{1,0:T(8,128)} copy-done((f32[1024,4096]{1,0:T(8,128)}, f32[1024,4096]{1,0:T(8,128)S(1)}, u32[]{:S(2)}) %copy-start) | copy-done | bytes 16777240
  40.9 1.1 %collective-permute-start.5 = (f32[4,128]{1,0:T(4,128)S(1)}, f32[4,128]{1,0:T(4,128)S(1)}, u32[]{:S(2)}, u32[]{:S(2)}) collective-permute-start(f32[4,128]{1,0:T(4,128)S(1)} %get-tuple-element.38.refs_0_), channel_id=1, source_target_pairs={{0,3},{1,2},{2,1},{3,0},{4,7},{5,6},{6,5},{7,4},{8,11},{9,10},{10,... | collective-permute-start | bytes 6152 | tf_op jit(solution)/shard_map/ppermute | solution.py:28
  42.8 1.1 %collective-permute-done.5.refs_3_ = f32[4,128]{1,0:T(4,128)S(1)} collective-permute-done((f32[4,128]{1,0:T(4,128)S(1)}, f32[4,128]{1,0:T(4,128)S(1)}, u32[]{:S(2)}, u32[]{:S(2)}) %collective-permute-start.5) | collective-permute-done | bytes 2080 | tf_op jit(solution)/shard_map/ppermute | solution.py:28
  44.6 1.0 %collective-permute-done.4.refs_2_ = f32[4,128]{1,0:T(4,128)S(1)} collective-permute-done((f32[4,128]{1,0:T(4,128)S(1)}, f32[4,128]{1,0:T(4,128)S(1)}, u32[]{:S(2)}, u32[]{:S(2)}) %collective-permute-start.4) | collective-permute-done | bytes 2080 | tf_op jit(solution)/shard_map/ppermute | solution.py:28
  45.6 0.8 shard_map.98
  46.4 3.3 %all-to-all-start.1 = ((f32[8,16,128]{2,1,0:T(8,128)}), f32[8,16,128]{2,1,0:T(8,128)S(1)}, u32[]{:S(2)}, u32[]{:S(2)}) async-start(f32[8,16,128]{2,1,0:T(8,128)} %get-tuple-element.40), calls=%async_computation.1 | async-start | bytes 131072 | tf_op jit(solution)/shard_map/all_to_all | solution.py:22
  49.8 0.9 shard_map.97.mix_ref
  50.7 5.9 %all-to-all-done.1.parts_ref = f32[8,16,128]{2,1,0:T(8,128)S(1)} async-done(((f32[8,16,128]{2,1,0:T(8,128)}), f32[8,16,128]{2,1,0:T(8,128)S(1)}, u32[]{:S(2)}, u32[]{:S(2)}) %all-to-all-start.1) | async-done | bytes 65568 | tf_op jit(solution)/shard_map/all_to_all | solution.py:22
  56.7 5.8 %copy-done.1 = f32[1024,4096]{1,0:T(8,128)S(1)} copy-done((f32[1024,4096]{1,0:T(8,128)S(1)}, f32[1024,4096]{1,0:T(8,128)}, u32[]{:S(2)}) %copy-start.1) | copy-done | bytes 16777240
  62.4 1.8 %shard_map.99 = (f32[32,128]{1,0:T(8,128)S(1)}, f32[1,128]{1,0:T(1,128)S(1)}) custom-call(f32[1024,4096]{1,0:T(8,128)S(1)} %copy-done.1, f32[8,16,128]{2,1,0:T(8,128)S(1)} %all-to-all-done.1.parts_ref), custom_call_target="tpu_custom_call" | custom-call | flops 8388608 | bytes 16777216 | tf_op jit(solution)/shard_map/pallas_call | solution.py:446
  64.3 3.4 %shard_map.100 = (f32[1,4,128,256]{3,2,1,0:T(8,128)S(1)}, f32[1,4,128,256]{3,2,1,0:T(8,128)S(1)}) custom-call(f32[512,1024]{1,0:T(8,128)S(1)} %copy-done.3, s32[4,128]{1,0:T(4,128)S(1)} %bitcast.9, bf16[8,128,512]{2,1,0:T(8,128)(2,1)S(1)} %shard_map.97.mix_ref, f32[1,128]{1,0:T(1,128)S(1)} %get-tuple-element.41.order_ref.refs_5_.refs_1_, ...), custom_call_target="tpu_custom_call" | custom-call | flops 536870912 | bytes 2097152 | tf_op jit(solution)/shard_map/pallas_call | solution.py:48
  68.2 1.1 %collective-permute-start.11 = (f32[32,128]{1,0:T(8,128)S(1)}, f32[32,128]{1,0:T(8,128)S(1)}, u32[]{:S(2)}, u32[]{:S(2)}) collective-permute-start(f32[32,128]{1,0:T(8,128)S(1)} %get-tuple-element.50.refs_0_), channel_id=1, source_target_pairs={{0,2},{1,3},{2,0},{3,1},{4,6},{5,7},{6,4},{7,5},{8,10},{9,11},{10,... | collective-permute-start | bytes 49160 | tf_op jit(solution)/shard_map/ppermute | solution.py:28
  70.1 1.3 %collective-permute-done.12.refs_3_ = f32[32,128]{1,0:T(8,128)S(1)} collective-permute-done((f32[32,128]{1,0:T(8,128)S(1)}, f32[32,128]{1,0:T(8,128)S(1)}, u32[]{:S(2)}, u32[]{:S(2)}) %collective-permute-start.12) | collective-permute-done | bytes 16416 | tf_op jit(solution)/shard_map/ppermute | solution.py:28
  72.0 2.9 %shard_map.101 = (f32[4,128]{1,0:T(4,128)S(1)}, f32[32,128]{1,0:T(8,128)}, f32[8,128]{1,0:T(8,128)S(1)}, f32[1,128]{1,0:T(1,128)S(1)}) custom-call(f32[1024,4096]{1,0:T(8,128)S(1)} %copy-done.2, f32[512,1024]{1,0:T(8,128)S(1)} %copy-done.3, f32[32,128]{1,0:T(8,128)S(1)} %get-tuple-element.50.refs_0_, f32[32,128]{1,0:T(8,128)S(1)} %collective-permute-done.10.refs_1_, ...), custom_call_target="tpu_custom_call" | custom-call | flops 8388608 | bytes 16777216 | tf_op jit(solution)/shard_map/pallas_call | solution.py:48
  75.7 0.9 collective-permute-start.14
  76.8 1.1 %collective-permute-done.15.refs_3_ = f32[4,128]{1,0:T(4,128)S(1)} collective-permute-done((f32[4,128]{1,0:T(4,128)S(1)}, f32[4,128]{1,0:T(4,128)S(1)}, u32[]{:S(2)}, u32[]{:S(2)}) %collective-permute-start.15) | collective-permute-done | bytes 2080 | tf_op jit(solution)/shard_map/ppermute | solution.py:28
  77.9 1.4 %collective-permute-done.14.refs_2_ = f32[4,128]{1,0:T(4,128)S(1)} collective-permute-done((f32[4,128]{1,0:T(4,128)S(1)}, f32[4,128]{1,0:T(4,128)S(1)}, u32[]{:S(2)}, u32[]{:S(2)}) %collective-permute-start.14) | collective-permute-done | bytes 2080 | tf_op jit(solution)/shard_map/ppermute | solution.py:28
  79.4 13.9 %all_to_all.16.order_ref.parts_ref = f32[8,8,128]{2,1,0:T(8,128)S(1)} all-to-all(f32[8,8,128]{2,1,0:T(8,128)S(1)} %get-tuple-element.55), channel_id=1, replica_groups=mesh['row'=8,'col'=4] {'row'}, dimensions={0} | all-to-all | bytes 65536 | tf_op jit(solution)/shard_map/all_to_all | solution.py:22
  93.4 1.3 %collective-permute-start.16 = (f32[128,256]{1,0:T(8,128)S(1)}, f32[128,256]{1,0:T(8,128)S(1)}, u32[]{:S(2)}, u32[]{:S(2)}) collective-permute-start(f32[128,256]{1,0:T(8,128)S(1)} %get-tuple-element.57), channel_id=1, source_target_pairs={{0,4},{4,0},{8,12},{12,8},{16,20},{20,16},{24,28},{28,24},{1,5},{5... | collective-permute-start | bytes 393224 | tf_op jit(solution)/shard_map/ppermute | solution.py:404
  95.1 1.8 %collective-permute-start.18 = (f32[128,256]{1,0:T(8,128)S(1)}, f32[128,256]{1,0:T(8,128)S(1)}, u32[]{:S(2)}, u32[]{:S(2)}) collective-permute-start(f32[128,256]{1,0:T(8,128)S(1)} %get-tuple-element.59), channel_id=1, source_target_pairs={{0,12},{4,8},{8,4},{12,0},{16,28},{20,24},{24,20},{28,16},{1,13},{... | collective-permute-start | bytes 393224 | tf_op jit(solution)/shard_map/ppermute | solution.py:404
  97.6 1.4 %collective-permute-done.16.refs_1_ = f32[128,256]{1,0:T(8,128)S(1)} collective-permute-done((f32[128,256]{1,0:T(8,128)S(1)}, f32[128,256]{1,0:T(8,128)S(1)}, u32[]{:S(2)}, u32[]{:S(2)}) %collective-permute-start.16) | collective-permute-done | bytes 131104 | tf_op jit(solution)/shard_map/ppermute | solution.py:404
  99.0 1.9 %collective-permute-done.17.refs_2_ = f32[128,256]{1,0:T(8,128)S(1)} collective-permute-done((f32[128,256]{1,0:T(8,128)S(1)}, f32[128,256]{1,0:T(8,128)S(1)}, u32[]{:S(2)}, u32[]{:S(2)}) %collective-permute-start.17) | collective-permute-done | bytes 131104 | tf_op jit(solution)/shard_map/ppermute | solution.py:404
  100.9 1.8 %collective-permute-done.18.refs_3_ = f32[128,256]{1,0:T(8,128)S(1)} collective-permute-done((f32[128,256]{1,0:T(8,128)S(1)}, f32[128,256]{1,0:T(8,128)S(1)}, u32[]{:S(2)}, u32[]{:S(2)}) %collective-permute-start.18) | collective-permute-done | bytes 131104 | tf_op jit(solution)/shard_map/ppermute | solution.py:404
  102.7 0.9 shard_map.104
  (36 shorter events, 7.2 us)
Async XLA Ops:
  0.6 32.0 %copy-start.3 = (f32[512,1024]{1,0:T(8,128)S(1)}, f32[512,1024]{1,0:T(8,128)}, u32[]{:S(2)}) copy-start(f32[512,1024]{1,0:T(8,128)} %design_ref.7) | copy-start | bytes 6291460
  18.4 27.2 %copy-start.5 = (f32[512]{0:T(512)S(1)}, f32[512]{0:T(512)}, u32[]{:S(2)}) copy-start(f32[512]{0:T(512)} %param.11) | copy-start | bytes 6148
  18.4 31.4 %copy-start.4 = (bf16[256,256]{1,0:T(8,128)(2,1)S(1)}, bf16[256,256]{1,0:T(8,128)(2,1)}, u32[]{:S(2)}) copy-start(bf16[256,256]{1,0:T(8,128)(2,1)} %constant.2.clone.walsh_ref) | copy-start | bytes 393220
  24.6 39.6 %collective-permute-start.6 = (f32[512,256]{1,0:T(8,128)}, f32[512,256]{1,0:T(8,128)}, u32[]{:S(2)}, u32[]{:S(2)}) collective-permute-start(f32[512,256]{1,0:T(8,128)} %get-tuple-element.45), channel_id=1, source_target_pairs={{0,4},{4,0},{8,12},{12,8},{16,20},{20,16},{24,28},{28,24},{1,5},{5... | collective-permute-start | bytes 1572872 | tf_op jit(solution)/shard_map/ppermute | solution.py:404
  25.0 39.3 %collective-permute-start.7 = (f32[512,256]{1,0:T(8,128)}, f32[512,256]{1,0:T(8,128)}, u32[]{:S(2)}, u32[]{:S(2)}) collective-permute-start(f32[512,256]{1,0:T(8,128)} %get-tuple-element.46), channel_id=1, source_target_pairs={{0,8},{4,12},{8,0},{12,4},{16,24},{20,28},{24,16},{28,20},{1,9},{5... | collective-permute-start | bytes 1572872 | tf_op jit(solution)/shard_map/ppermute | solution.py:404
  25.9 38.3 %collective-permute-start.8 = (f32[512,256]{1,0:T(8,128)}, f32[512,256]{1,0:T(8,128)}, u32[]{:S(2)}, u32[]{:S(2)}) collective-permute-start(f32[512,256]{1,0:T(8,128)} %get-tuple-element.47), channel_id=1, source_target_pairs={{0,12},{4,8},{8,4},{12,0},{16,28},{20,24},{24,20},{28,16},{1,13},{... | collective-permute-start | bytes 1572872 | tf_op jit(solution)/shard_map/ppermute | solution.py:404
  28.2 3.3 %collective-permute-start.2 = (f32[32,128]{1,0:T(8,128)S(1)}, f32[32,128]{1,0:T(8,128)S(1)}, u32[]{:S(2)}, u32[]{:S(2)}) collective-permute-start(f32[32,128]{1,0:T(8,128)S(1)} %get-tuple-element.36.refs_0_), channel_id=1, source_target_pairs={{0,3},{1,2},{2,1},{3,0},{4,7},{5,6},{6,5},{7,4},{8,11},{9,10},{10,... | collective-permute-start | bytes 49160 | tf_op jit(solution)/shard_map/ppermute | solution.py:28
  28.2 3.8 %collective-permute-start.1 = (f32[32,128]{1,0:T(8,128)S(1)}, f32[32,128]{1,0:T(8,128)S(1)}, u32[]{:S(2)}, u32[]{:S(2)}) collective-permute-start(f32[32,128]{1,0:T(8,128)S(1)} %get-tuple-element.36.refs_0_), channel_id=1, source_target_pairs={{0,2},{1,3},{2,0},{3,1},{4,6},{5,7},{6,4},{7,5},{8,10},{9,11},{10,... | collective-permute-start | bytes 49160 | tf_op jit(solution)/shard_map/ppermute | solution.py:28
  31.4 1.2 %collective-permute-start = (f32[32,128]{1,0:T(8,128)S(1)}, f32[32,128]{1,0:T(8,128)S(1)}, u32[]{:S(2)}, u32[]{:S(2)}) collective-permute-start(f32[32,128]{1,0:T(8,128)S(1)} %get-tuple-element.36.refs_0_), channel_id=1, source_target_pairs={{0,1},{1,0},{2,3},{3,2},{4,5},{5,4},{6,7},{7,6},{8,9},{9,8},{10,11... | collective-permute-start | bytes 49160 | tf_op jit(solution)/shard_map/ppermute | solution.py:28
  32.6 31.6 %copy-start.6 = (s32[512]{0:T(512)S(1)}, s32[512]{0:T(512)}, u32[]{:S(2)}) copy-start(s32[512]{0:T(512)} %param.8) | copy-start | bytes 6148
  35.1 5.8 %copy-start = (f32[1024,4096]{1,0:T(8,128)}, f32[1024,4096]{1,0:T(8,128)S(1)}, u32[]{:S(2)}) copy-start(f32[1024,4096]{1,0:T(8,128)S(1)} %get-tuple-element.35.rinv_ref) | copy-start | bytes 50331652
  40.9 3.0 %collective-permute-start.5 = (f32[4,128]{1,0:T(4,128)S(1)}, f32[4,128]{1,0:T(4,128)S(1)}, u32[]{:S(2)}, u32[]{:S(2)}) collective-permute-start(f32[4,128]{1,0:T(4,128)S(1)} %get-tuple-element.38.refs_0_), channel_id=1, source_target_pairs={{0,3},{1,2},{2,1},{3,0},{4,7},{5,6},{6,5},{7,4},{8,11},{9,10},{10,... | collective-permute-start | bytes 6152 | tf_op jit(solution)/shard_map/ppermute | solution.py:28
  42.0 3.6 %collective-permute-start.4 = (f32[4,128]{1,0:T(4,128)S(1)}, f32[4,128]{1,0:T(4,128)S(1)}, u32[]{:S(2)}, u32[]{:S(2)}) collective-permute-start(f32[4,128]{1,0:T(4,128)S(1)} %get-tuple-element.38.refs_0_), channel_id=1, source_target_pairs={{0,2},{1,3},{2,0},{3,1},{4,6},{5,7},{6,4},{7,5},{8,10},{9,11},{10,... | collective-permute-start | bytes 6152 | tf_op jit(solution)/shard_map/ppermute | solution.py:28
  43.9 1.7 %collective-permute-start.3 = (f32[4,128]{1,0:T(4,128)S(1)}, f32[4,128]{1,0:T(4,128)S(1)}, u32[]{:S(2)}, u32[]{:S(2)}) collective-permute-start(f32[4,128]{1,0:T(4,128)S(1)} %get-tuple-element.38.refs_0_), channel_id=1, source_target_pairs={{0,1},{1,0},{2,3},{3,2},{4,5},{5,4},{6,7},{7,6},{8,9},{9,8},{10,11... | collective-permute-start | bytes 6152 | tf_op jit(solution)/shard_map/ppermute | solution.py:28
  46.4 10.2 %all-to-all-start.1 = ((f32[8,16,128]{2,1,0:T(8,128)}), f32[8,16,128]{2,1,0:T(8,128)S(1)}, u32[]{:S(2)}, u32[]{:S(2)}) async-start(f32[8,16,128]{2,1,0:T(8,128)} %get-tuple-element.40), calls=%async_computation.1 | async-start | bytes 131072 | tf_op jit(solution)/shard_map/all_to_all | solution.py:22
  56.6 5.8 %copy-start.1 = (f32[1024,4096]{1,0:T(8,128)S(1)}, f32[1024,4096]{1,0:T(8,128)}, u32[]{:S(2)}) copy-start(f32[1024,4096]{1,0:T(8,128)} %copy-done) | copy-start | bytes 50331652
  62.4 9.6 %copy-start.2 = (f32[1024,4096]{1,0:T(8,128)S(1)}, f32[1024,4096]{1,0:T(8,128)}, u32[]{:S(2)}) copy-start(f32[1024,4096]{1,0:T(8,128)} %copy-done) | copy-start | bytes 50331652
  67.7 25.7 %collective-permute-start.9 = (f32[1,4,128,256]{3,2,1,0:T(8,128)S(1)}, f32[1,4,128,256]{3,2,1,0:T(8,128)S(1)}, u32[]{:S(2)}, u32[]{:S(2)}) collective-permute-start(f32[1,4,128,256]{3,2,1,0:T(8,128)S(1)} %get-tuple-element.49), channel_id=1, source_target_pairs={{0,16},{4,20},{8,24},{12,28},{16,0},{20,4},{24,8},{28,12},{1,17},{... | collective-permute-start | bytes 1572872 | tf_op jit(solution)/shard_map/ppermute | solution.py:404
  68.2 3.2 %collective-permute-start.12 = (f32[32,128]{1,0:T(8,128)S(1)}, f32[32,128]{1,0:T(8,128)S(1)}, u32[]{:S(2)}, u32[]{:S(2)}) collective-permute-start(f32[32,128]{1,0:T(8,128)S(1)} %get-tuple-element.50.refs_0_), channel_id=1, source_target_pairs={{0,3},{1,2},{2,1},{3,0},{4,7},{5,6},{6,5},{7,4},{8,11},{9,10},{10,... | collective-permute-start | bytes 49160 | tf_op jit(solution)/shard_map/ppermute | solution.py:28
  68.2 3.8 %collective-permute-start.11 = (f32[32,128]{1,0:T(8,128)S(1)}, f32[32,128]{1,0:T(8,128)S(1)}, u32[]{:S(2)}, u32[]{:S(2)}) collective-permute-start(f32[32,128]{1,0:T(8,128)S(1)} %get-tuple-element.50.refs_0_), channel_id=1, source_target_pairs={{0,2},{1,3},{2,0},{3,1},{4,6},{5,7},{6,4},{7,5},{8,10},{9,11},{10,... | collective-permute-start | bytes 49160 | tf_op jit(solution)/shard_map/ppermute | solution.py:28
  69.3 2.7 %collective-permute-start.10 = (f32[32,128]{1,0:T(8,128)S(1)}, f32[32,128]{1,0:T(8,128)S(1)}, u32[]{:S(2)}, u32[]{:S(2)}) collective-permute-start(f32[32,128]{1,0:T(8,128)S(1)} %get-tuple-element.50.refs_0_), channel_id=1, source_target_pairs={{0,1},{1,0},{2,3},{3,2},{4,5},{5,4},{6,7},{7,6},{8,9},{9,8},{10,11... | collective-permute-start | bytes 49160 | tf_op jit(solution)/shard_map/ppermute | solution.py:28
  74.9 3.0 %collective-permute-start.15 = (f32[4,128]{1,0:T(4,128)S(1)}, f32[4,128]{1,0:T(4,128)S(1)}, u32[]{:S(2)}, u32[]{:S(2)}) collective-permute-start(f32[4,128]{1,0:T(4,128)S(1)} %get-tuple-element.52.refs_0_), channel_id=1, source_target_pairs={{0,3},{1,2},{2,1},{3,0},{4,7},{5,6},{6,5},{7,4},{8,11},{9,10},{10,... | collective-permute-start | bytes 6152 | tf_op jit(solution)/shard_map/ppermute | solution.py:28
  75.7 3.6 %collective-permute-start.14 = (f32[4,128]{1,0:T(4,128)S(1)}, f32[4,128]{1,0:T(4,128)S(1)}, u32[]{:S(2)}, u32[]{:S(2)}) collective-permute-start(f32[4,128]{1,0:T(4,128)S(1)} %get-tuple-element.52.refs_0_), channel_id=1, source_target_pairs={{0,2},{1,3},{2,0},{3,1},{4,6},{5,7},{6,4},{7,5},{8,10},{9,11},{10,... | collective-permute-start | bytes 6152 | tf_op jit(solution)/shard_map/ppermute | solution.py:28
  76.7 2.6 %collective-permute-start.13 = (f32[4,128]{1,0:T(4,128)S(1)}, f32[4,128]{1,0:T(4,128)S(1)}, u32[]{:S(2)}, u32[]{:S(2)}) collective-permute-start(f32[4,128]{1,0:T(4,128)S(1)} %get-tuple-element.52.refs_0_), channel_id=1, source_target_pairs={{0,1},{1,0},{2,3},{3,2},{4,5},{5,4},{6,7},{7,6},{8,9},{9,8},{10,11... | collective-permute-start | bytes 6152 | tf_op jit(solution)/shard_map/ppermute | solution.py:28
  93.4 5.6 %collective-permute-start.16 = (f32[128,256]{1,0:T(8,128)S(1)}, f32[128,256]{1,0:T(8,128)S(1)}, u32[]{:S(2)}, u32[]{:S(2)}) collective-permute-start(f32[128,256]{1,0:T(8,128)S(1)} %get-tuple-element.57), channel_id=1, source_target_pairs={{0,4},{4,0},{8,12},{12,8},{16,20},{20,16},{24,28},{28,24},{1,5},{5... | collective-permute-start | bytes 393224 | tf_op jit(solution)/shard_map/ppermute | solution.py:404
  94.7 6.2 %collective-permute-start.17 = (f32[128,256]{1,0:T(8,128)S(1)}, f32[128,256]{1,0:T(8,128)S(1)}, u32[]{:S(2)}, u32[]{:S(2)}) collective-permute-start(f32[128,256]{1,0:T(8,128)S(1)} %get-tuple-element.58), channel_id=1, source_target_pairs={{0,8},{4,12},{8,0},{12,4},{16,24},{20,28},{24,16},{28,20},{1,9},{5... | collective-permute-start | bytes 393224 | tf_op jit(solution)/shard_map/ppermute | solution.py:404
  95.1 7.6 %collective-permute-start.18 = (f32[128,256]{1,0:T(8,128)S(1)}, f32[128,256]{1,0:T(8,128)S(1)}, u32[]{:S(2)}, u32[]{:S(2)}) collective-permute-start(f32[128,256]{1,0:T(8,128)S(1)} %get-tuple-element.59), channel_id=1, source_target_pairs={{0,12},{4,8},{8,4},{12,0},{16,28},{20,24},{24,20},{28,16},{1,13},{... | collective-permute-start | bytes 393224 | tf_op jit(solution)/shard_map/ppermute | solution.py:404

commit v5 on v4

--- a/solution.py
+++ b/solution.py
@@ -13,6 +13,7 @@
 ITERS = 2
 LANE = 128
 NEAR = 4
+CHUNKS = 2
 F32 = jnp.float32
 VMEM = pl.BlockSpec(memory_space=pltpu.VMEM)
 HBM = pl.BlockSpec(memory_space=pltpu.HBM)
@@ -136,8 +137,9 @@
 
 
 def first_body(design_ref, target_ref, bits_ref, picks_ref, counts_ref, *refs):
-    out_ref, away_refs = refs[0], refs[1:NEAR]
-    design, target_here, bits, picks, counts, away, sems = refs[NEAR:]
+    out_ref, away_refs = refs[0], refs[1:-7]
+    design, target_here, bits, picks, counts, away, sems = refs[-7:]
+    chunks = len(away_refs) // (NEAR - 1)
     rows, width = design.shape
     lines, tiles, piece = rows // LANE, width // LANE, width // NEAR
     small = [
@@ -169,11 +171,16 @@
             for tile in range(0, piece, LANE):
                 column = pl.multiple_of((place ^ mask) * piece + tile, LANE)
                 away[mask - 1, part, tile : tile + LANE] = design[part, pl.ds(column, LANE)] * signs
-            copy = pltpu.make_async_copy(
-                away.at[mask - 1, part, :], away_refs[mask - 1].at[part, :], sems.at[4 + lines * mask + line]
-            )
-            copy.start()
-            back.append(copy)
+            for chunk in range(chunks):
+                index = chunk * (NEAR - 1) + mask - 1
+                columns = slice(chunk * piece // chunks, (chunk + 1) * piece // chunks)
+                copy = pltpu.make_async_copy(
+                    away.at[mask - 1, part, columns],
+                    away_refs[index].at[part, :],
+                    sems.at[4 + lines * (index + 1) + line],
+                )
+                copy.start()
+                back.append(copy)
     out_ref[0] = jnp.zeros(out_ref.shape[1:], F32)
     for tile in range(tiles):
         out_ref[0, tile : tile + 1, :] = jnp.sum(sums[tile], axis=0, keepdims=True)
@@ -227,7 +234,7 @@
 
 def turn_body(groups, last, *refs):
     left = tree([ref[...] for ref in refs[:groups]])
-    before_ref, beta_ref, alpha_ref, *refs = refs[groups:]
+    before_ref, beta_ref, alpha_ref, token_ref, *refs = refs[groups:]
     left = left - alpha_ref[...] * (before_ref[...] / beta_ref[...])
     square = splat(total(left * left))
     if last:
@@ -268,7 +275,8 @@
     solution_ref[...] = iterate
 
 
-def mix_body(parts_ref, walsh_ref, order_ref, out_ref):
+def mix_body(parts_ref, walsh_ref, order_ref, out_ref, token_ref):
+    token_ref[...] = order_ref[...]
     groups, _, rows = out_ref.shape
     spread = rounded(groups, 8)
     start = parts_ref.shape[1] - spread
@@ -300,16 +308,18 @@
         lax.fori_loop(0, groups, step, 0)
 
 
-def sample_body(scale, design_ref, bits_ref, mix_ref, order_ref, *refs):
-    near, (keep_ref, send_ref, both) = refs[: NEAR - 1], refs[NEAR - 1 :]
+def sample_body(scale, start, design_ref, bits_ref, mix_ref, order_ref, *refs):
+    near, (keep_ref, send_ref, token_ref, both) = refs[: NEAR - 1], refs[NEAR - 1 :]
+    token_ref[...] = order_ref[...]
     rows, piece = near[0].shape
+    quarter = design_ref.shape[1] // NEAR
     groups = mix_ref.shape[0]
     place = lax.axis_index("row") % NEAR
     for line in range(rows // LANE):
         part = slice(line * LANE, (line + 1) * LANE)
         signs = signs_across(bits_ref, line)
         for tile in range(0, piece, LANE):
-            column = pl.multiple_of(place * piece + tile, LANE)
+            column = pl.multiple_of(place * quarter + start + tile, LANE)
             here = slice(tile, tile + LANE)
             values = [design_ref[part, pl.ds(column, LANE)] * signs] + [ref[part, here] for ref in near]
             apart = 1
@@ -349,9 +359,22 @@
     send_ref[...] = kept_ref[half:] + arrived_ref[half:]
 
 
-def split_body(kept_ref, arrived_ref, order_ref, *out_refs):
-    for index, out_ref in enumerate(out_refs):
-        out_ref[...] = kept_ref[0, index] + arrived_ref[0, index]
+def join_body(kept_ref, arrived_ref, order_ref, out_ref, token_ref):
+    token_ref[...] = order_ref[...]
+    out_ref[...] = kept_ref[0] + arrived_ref[0]
+
+
+def split_body(chunks, *refs):
+    joined, (kept_ref, arrived_ref, order_ref, token_ref, *out_refs) = refs[: chunks - 1], refs[chunks - 1 :]
+    token_ref[...] = order_ref[...]
+    piece = kept_ref.shape[3]
+    for chunk in range(chunks):
+        columns = slice(chunk * piece, (chunk + 1) * piece)
+        for index, out_ref in enumerate(out_refs):
+            if chunk < chunks - 1:
+                out_ref[:, columns] = joined[chunk][index]
+            else:
+                out_ref[:, columns] = kept_ref[0, index] + arrived_ref[0, index]
 
 
 def assemble_body(*refs):
@@ -378,23 +401,25 @@
     deep = message_rows(width)
     left = target.reshape(lines, LANE)
     bits = sign_bits.reshape(lines, LANE)
-    piece = width // NEAR
+    chunks = min(CHUNKS, width // NEAR // LANE)
+    piece = width // NEAR // chunks
     slots = row_groups * PAIR
     far = row_groups // NEAR
 
     message, *away = pl.pallas_call(
         first_body,
-        out_shape=(shape(row_groups, deep + rounded(row_groups, 8), LANE),) + (shape(rows, piece),) * (NEAR - 1),
+        out_shape=(shape(row_groups, deep + rounded(row_groups, 8), LANE),)
+        + (shape(rows, piece),) * (chunks * (NEAR - 1)),
         in_specs=[HBM] * 5,
-        out_specs=(VMEM,) + (HBM,) * (NEAR - 1),
+        out_specs=(VMEM,) + (HBM,) * (chunks * (NEAR - 1)),
         scratch_shapes=[
             pltpu.VMEM((rows, width), F32),
             pltpu.VMEM((lines, LANE), F32),
             pltpu.VMEM((lines, LANE), jnp.int32),
             pltpu.VMEM((row_groups, PAIR), jnp.int32),
             pltpu.VMEM((1, row_groups), jnp.int32),
-            pltpu.VMEM((NEAR - 1, rows, piece), F32),
-            pltpu.SemaphoreType.DMA((4 + lines * NEAR,)),
+            pltpu.VMEM((NEAR - 1, rows, width // NEAR), F32),
+            pltpu.SemaphoreType.DMA((4 + lines * (1 + chunks * (NEAR - 1)),)),
         ],
         compiler_params=pltpu.CompilerParams(vmem_limit_bytes=58 << 20),
         cost_estimate=pl.CostEstimate(flops=2 * small, bytes_accessed=7 * small, transcendentals=0),
@@ -405,27 +430,26 @@
 
     def mix(order):
         signs = jnp.asarray(walsh(HB), jnp.bfloat16)
-        made = shape(row_groups, slots, rows, dtype=jnp.bfloat16)
+        made = (shape(row_groups, slots, rows, dtype=jnp.bfloat16), scalar)
         return call(mix_body, made, picked, signs, order, flops=2 * row_groups * slots * rows * HB)
 
-    def sample(near, mixed, order):
+    def sample(chunk, mixed, order):
         scale = float(np.sqrt(np.float32(rows * row_groups)))
         return call(
-            functools.partial(sample_body, scale),
-            (shape(far // 2, NEAR, slots, piece),) * 2,
+            functools.partial(sample_body, scale, chunk * piece),
+            (shape(far // 2, NEAR, slots, piece),) * 2 + (scalar,),
             design,
             bits,
             mixed,
             order,
-            *near,
+            *near[chunk],
             scratch=[pltpu.VMEM((NEAR, 2, rows, piece), jnp.bfloat16)],
             flops=4 * row_groups * slots * rows * piece,
             size=4 * NEAR * rows * piece,
         )
 
-    def gather_rows(keep, send, order):
+    def halve(keep, come, order):
         bit = row_groups // 2
-        come = swap(send, bit)
         while bit > NEAR:
             bit //= 2
             half = keep.shape[0] // 2
@@ -433,10 +457,19 @@
             come = swap(send, bit)
         return keep, come
 
-    def trade(keep, come, order):
-        mine, *others = call(split_body, (shape(slots, piece),) * NEAR, keep, come, order)
-        parts = [mine] + [swap(part, mask + 1) for mask, part in enumerate(others)]
-        return call(assemble_body, shape(slots, width), *parts, size=8 * slots * width)
+    def join(keep, come, order):
+        keep, come = halve(keep, come, order)
+        return call(join_body, (shape(*keep.shape[1:]), scalar), keep, come, order)
+
+    def trade(joined, keep, come, order):
+        token, mine, *others = call(
+            functools.partial(split_body, chunks),
+            (scalar,) + (shape(slots, width // NEAR),) * NEAR,
+            *joined,
+            *halve(keep, come, order),
+            order,
+        )
+        return [mine] + [swap(part, mask + 1) for mask, part in enumerate(others)], token
 
     def back(rinv, message, first):
         outs, scratch = (shape(whole // LANE, LANE), scalar), [pltpu.VMEM((width // LANE, LANE), F32)]
@@ -465,7 +498,7 @@
             size=4 * big,
         )
 
-    def turn(images, left, beta, alpha, last):
+    def turn(images, left, beta, alpha, token, last):
         return call(
             functools.partial(turn_body, col_groups, last),
             (shape(lines, LANE), shape(row_groups, 8 if last else deep, LANE)),
@@ -473,35 +506,55 @@
             left,
             beta,
             alpha,
+            token,
             *(() if last else (design,)),
             flops=2 * small,
             size=0 if last else 4 * small,
         )
 
-    betas, alphas, held = [], [], []
+    def spread(chunk, order):
+        parts = away[chunk * (NEAR - 1) : (chunk + 1) * (NEAR - 1)]
+        parts, _ = lax.optimization_barrier((parts, order))
+        return [swap(part, mask + 1) for mask, part in enumerate(parts)]
+
+    betas, alphas, held, joined = [], [], [], []
     message = picked = exchange(message, "row")
+    near = [spread(0, message)]
     for step in range(ITERS):
+        last = step + 1 == ITERS
         if step == 0:
             term, beta, here = back(rinv, message, True)
-            away, _ = lax.optimization_barrier((away, beta))
-            near = [swap(part, mask + 1) for mask, part in enumerate(away)]
+            mixed, token = mix(beta)
+            near += [spread(chunk, beta) for chunk in range(1, chunks)]
         else:
             term, beta = back(here, message, False)
-            keep, come = gather_rows(*sample(near, mixed, beta), beta)
         betas.append(beta)
         terms = direct(term, "col")
-        image, right, part, alpha = forward(terms, *(() if step == 0 else (right, beta)))
+        image, right, kept, alpha = forward(terms, *(() if step == 0 else (right, beta)))
+        alphas.append(alpha)
+        held.append(kept)
         if step == 0:
-            mixed = mix(alpha)
-        alphas.append(alpha)
-        held.append(part)
+            parts = []
+            token = alpha
+            for chunk in range(chunks):
+                keep, send, token = sample(chunk, mixed, token)
+                if chunk < chunks - 1:
+                    parts.append((keep, swap(send, row_groups // 2)))
+            for part in parts:
+                part, token = join(*part, token)
+                joined.append(part)
         images = direct(image, "col")
-        left, message = turn(images, left, beta, alpha, step + 1 == ITERS)
+        if last:
+            quarters, token = trade(joined, keep, come, alpha)
+        left, message = turn(images, left, beta, alpha, token, last)
         message = exchange(message, "row")
+        if step == 0:
+            send, _ = lax.optimization_barrier((send, message))
+            come = swap(send, row_groups // 2)
     basis, answer = call(
         last_body, (shape(lines, LANE), shape(width // LANE, LANE)), message, left, *betas, *alphas, *held
     )
-    sketch = trade(keep, come, message)
+    sketch = call(assemble_body, shape(slots, width), *quarters, size=8 * slots * width)
     return (sketch, answer.reshape(-1), basis.reshape(-1))
 
 

time: 104 us -> 94.7 us (0.911)
  local copies, waits for them, and re-layouts: 11.5 us -> 0.03 us
  blocking collectives: 28.3 us -> 33.5 us
  Pallas kernels: 23.5 us -> 22 us
    unnamed x14, local copies, waits for them, and re-layouts: 11.5 us -> 0.03 us
    ppermute x7 -> x11, waiting for transfers between devices: 5.12 us -> 14 us  [swap(): lax.ppermute(array, 'row', [(i, i ^ mask) for i in range(row_groups)])]
    all_to_all x1 -> x0, waiting for transfers between devices: 5.91 us -> none  [exchange(): return lax.all_to_all(copies, axis, split_axis=0, concat_axis=0, tiled=True)]
    all_to_all x2 -> x3, blocking collectives: 28.3 us -> 33.5 us  [exchange(): return lax.all_to_all(copies, axis, split_axis=0, concat_axis=0, tiled=True)]
    all_to_all x1 -> x0, starting transfers between devices: 3.35 us -> none  [exchange(): return lax.all_to_all(copies, axis, split_axis=0, concat_axis=0, tiled=True)]
    ppermute x12, waiting for transfers between devices: 9.28 us -> 5.94 us  [direct(): lax.ppermute(array, axis, [(i, i ^ mask) for i in range(size)])]
    ppermute x7 -> x11, starting transfers between devices: 7.65 us -> 11 us  [swap(): lax.ppermute(array, 'row', [(i, i ^ mask) for i in range(row_groups)])]
    pallas_call x9 -> x11, Pallas kernels: 12.2 us -> 10.6 us  [call(): pl.pallas_call(body, out_shape=out_shape, in_specs=[VMEM] * len(operands)...]
  transfers between devices with their start and end apart: 20 -> 23, of which waited for: 13 -> 12; matrix products, arithmetic and copies ran while one was open for 0% -> 0% of each run, Pallas kernels for 9% -> 18%
where the time goes in v5:
time: 94.7 us; the launch traced here: 94.4 us
  blocking collectives  33.5 us (35%)
  Pallas kernels  22 us (23%)
  waiting for transfers between devices  20 us (21%)
  starting transfers between devices  18.1 us (19%)
    all_to_all x3, blocking collectives, exchange(): return lax.all_to_all(copies, axis, split_axis=0, concat_axis=0, tiled=True)  33.5 us
    ppermute x11, waiting for transfers between devices, swap(): lax.ppermute(array, 'row', [(i, i ^ mask) for i in range(row_groups)])  14 us
    ppermute x11, starting transfers between devices, swap(): lax.ppermute(array, 'row', [(i, i ^ mask) for i in range(row_groups)])  11 us
    pallas_call x11, Pallas kernels, call(): pl.pallas_call(body, out_shape=out_shape, in_specs=[VMEM] * len(operands)...  10.6 us
    pallas_call x2, Pallas kernels, back(): pl.pallas_call(functools.partial(back_body, first), out_shape=outs, in_sp...  7.97 us
    ppermute x12, starting transfers between devices, direct(): lax.ppermute(array, axis, [(i, i ^ mask) for i in range(size)])  7.14 us
    ppermute x12, waiting for transfers between devices, direct(): lax.ppermute(array, axis, [(i, i ^ mask) for i in range(size)])  5.94 us
    pallas_call x1, Pallas kernels, shards(): pl.pallas_call(first_body, out_shape=(shape(row_groups, deep + rounded(ro...  3.45 us
  transfers between devices with their start and end apart: 23, of which 12 were waited for; matrix products, arithmetic and copies ran while one was open for 0% of the time, Pallas kernels for 18%

profile of v5, /device:TPU:0, one launch (start us, length us, event | category | flops | bytes accessed | tf_op | source)
XLA Modules:
  0.0 94.4 jit_solution(8688582118021761767)
XLA Ops:
  0.7 3.4 %shard_map.94 = (f32[8,24,128]{2,1,0:T(8,128)}, f32[512,128]{1,0:T(8,128)}, f32[512,128]{1,0:T(8,128)}, f32[512,128]{1,0:T(8,128)}, f32[512,128]{1,0:T(8,128)}, /*index=5*/f32[512,128]{1,0:T(8,128)}, f32[512,128]{1,0:T(8,128)}) custom-call(f32[512,1024]{1,0:T(8,128)} %design_ref.9, f32[4,128]{1,0:T(4,128)} %bitcast.9, s32[4,128]{1,0:T(4,128)} %bitcast.6, ...), custom_call_target="tpu_custom_call" | custom-call | flops 1048576 | bytes 3670016 | tf_op jit(solution)/shard_map/pallas_call | solution.py:409
  4.1 14.5 %all_to_all.15.parts_ref = f32[8,24,128]{2,1,0:T(8,128)S(1)} all-to-all(f32[8,24,128]{2,1,0:T(8,128)} %get-tuple-element.49), channel_id=1, replica_groups=mesh['row'=8,'col'=4] {'row'}, dimensions={0} | all-to-all | bytes 196608 | tf_op jit(solution)/shard_map/all_to_all | solution.py:23
  19.0 1.0 %collective-permute-start.4 = (f32[512,128]{1,0:T(8,128)}, f32[512,128]{1,0:T(8,128)S(1)}, u32[]{:S(2)}, u32[]{:S(2)}) collective-permute-start(f32[512,128]{1,0:T(8,128)} %get-tuple-element.59), channel_id=1, source_target_pairs={{0,8},{4,12},{8,0},{12,4},{16,24},{20,28},{24,16},{28,20},{1,9},{5... | collective-permute-start | bytes 786440 | tf_op jit(solution)/shard_map/ppermute | solution.py:429
  19.9 2.2 %collective-permute-start.5 = (f32[512,128]{1,0:T(8,128)}, f32[512,128]{1,0:T(8,128)S(1)}, u32[]{:S(2)}, u32[]{:S(2)}) collective-permute-start(f32[512,128]{1,0:T(8,128)} %get-tuple-element.60), channel_id=1, source_target_pairs={{0,12},{4,8},{8,4},{12,0},{16,28},{20,24},{24,20},{28,16},{1,13},{... | collective-permute-start | bytes 786440 | tf_op jit(solution)/shard_map/ppermute | solution.py:429
  22.2 6.2 %shard_map.95 = (f32[32,128]{1,0:T(8,128)S(1)}, f32[1,128]{1,0:T(1,128)S(1)}, f32[1024,4096]{1,0:T(8,128)S(1)}) custom-call(f32[1024,4096]{1,0:T(8,128)} %rinv_ref.1, f32[8,24,128]{2,1,0:T(8,128)S(1)} %all_to_all.15.parts_ref), custom_call_target="tpu_custom_call" | custom-call | flops 8388608 | bytes 16777216 | tf_op jit(solution)/shard_map/pallas_call | solution.py:479
  28.4 1.6 %collective-permute-start.1 = (f32[32,128]{1,0:T(8,128)S(1)}, f32[32,128]{1,0:T(8,128)S(1)}, u32[]{:S(2)}, u32[]{:S(2)}) collective-permute-start(f32[32,128]{1,0:T(8,128)S(1)} %get-tuple-element.53.refs_0_), channel_id=1, source_target_pairs={{0,2},{1,3},{2,0},{3,1},{4,6},{5,7},{6,4},{7,5},{8,10},{9,11},{10,... | collective-permute-start | bytes 49160 | tf_op jit(solution)/shard_map/ppermute | solution.py:29
  30.0 0.9 collective-permute-start.2
  30.9 1.3 %shard_map.96 = (bf16[8,128,512]{2,1,0:T(8,128)(2,1)S(1)}, f32[1,128]{1,0:T(1,128)}) custom-call(f32[8,24,128]{2,1,0:T(8,128)S(1)} %all_to_all.15.parts_ref, bf16[256,256]{1,0:T(8,128)(2,1)S(1)} %copy-done.3, f32[1,128]{1,0:T(1,128)S(1)} %get-tuple-element.50.order_ref.refs_5_.refs_0_), custom_call_target="tpu_custom_call" | custom-call | flops 268435456 | tf_op jit(solution)/shard_map/pallas_call | solution.py:49
  32.5 0.6 collective-permute-done.2.refs_3_
  33.5 2.4 %shard_map.97 = (f32[4,128]{1,0:T(4,128)S(1)}, f32[32,128]{1,0:T(8,128)S(1)}, f32[8,128]{1,0:T(8,128)S(1)}, f32[1,128]{1,0:T(1,128)S(1)}) custom-call(f32[1024,4096]{1,0:T(8,128)S(1)} %get-tuple-element.52.rinv_ref, f32[512,1024]{1,0:T(8,128)S(1)} %copy-done, f32[32,128]{1,0:T(8,128)S(1)} %get-tuple-element.53.refs_0_, ...), custom_call_target="tpu_custom_call" | custom-call | flops 8388608 | bytes 16777216 | tf_op jit(solution)/shard_map/pallas_call | solution.py:49
  35.9 2.3 %collective-permute-start.9 = (f32[512,128]{1,0:T(8,128)S(1)}, f32[512,128]{1,0:T(8,128)S(1)}, u32[]{:S(2)}, u32[]{:S(2)}) collective-permute-start(f32[512,128]{1,0:T(8,128)S(1)} %copy-done.4), channel_id=1, source_target_pairs={{0,12},{4,8},{8,4},{12,0},{16,28},{20,24},{24,20},{28,16},{1,13},{... | collective-permute-start | bytes 786440 | tf_op jit(solution)/shard_map/ppermute | solution.py:429
  38.2 1.0 %shard_map.98 = (f32[1,4,128,128]{3,2,1,0:T(8,128)S(1)}, f32[1,4,128,128]{3,2,1,0:T(8,128)S(1)}, f32[1,128]{1,0:T(1,128)S(1)}) custom-call(f32[512,1024]{1,0:T(8,128)S(1)} %copy-done, s32[4,128]{1,0:T(4,128)S(1)} %bitcast.7, bf16[8,128,512]{2,1,0:T(8,128)(2,1)S(1)} %get-tuple-element.51.mix_ref, f32[1,128]{1,0:T(1,128)S(1)} %get-tuple-element.54.order_ref.refs_6_.refs_2_, ...), custom_call_target="tpu_custom_call" | custom-call | flops 268435456 | bytes 1048576 | tf_op jit(solution)/shard_map/pallas_call | solution.py:49
  39.8 1.0 %collective-permute-done.7.refs_0_ = f32[512,128]{1,0:T(8,128)S(1)} collective-permute-done((f32[512,128]{1,0:T(8,128)S(1)}, f32[512,128]{1,0:T(8,128)S(1)}, u32[]{:S(2)}, u32[]{:S(2)}) %collective-permute-start.7) | collective-permute-done | bytes 262176 | tf_op jit(solution)/shard_map/ppermute | solution.py:429
  40.7 1.3 %collective-permute-start.11 = (f32[4,128]{1,0:T(4,128)S(1)}, f32[4,128]{1,0:T(4,128)S(1)}, u32[]{:S(2)}, u32[]{:S(2)}) collective-permute-start(f32[4,128]{1,0:T(4,128)S(1)} %get-tuple-element.74.refs_0_), channel_id=1, source_target_pairs={{0,2},{1,3},{2,0},{3,1},{4,6},{5,7},{6,4},{7,5},{8,10},{9,11},{10,... | collective-permute-start | bytes 6152 | tf_op jit(solution)/shard_map/ppermute | solution.py:29
  42.3 9.9 %collective-permute-done.9.refs_2_ = f32[512,128]{1,0:T(8,128)S(1)} collective-permute-done((f32[512,128]{1,0:T(8,128)S(1)}, f32[512,128]{1,0:T(8,128)S(1)}, u32[]{:S(2)}, u32[]{:S(2)}) %collective-permute-start.9) | collective-permute-done | bytes 262176 | tf_op jit(solution)/shard_map/ppermute | solution.py:429
  52.2 1.0 %shard_map.99 = (f32[1,4,128,128]{3,2,1,0:T(8,128)S(1)}, f32[1,4,128,128]{3,2,1,0:T(8,128)S(1)}, f32[1,128]{1,0:T(1,128)S(1)}) custom-call(f32[512,1024]{1,0:T(8,128)S(1)} %copy-done, s32[4,128]{1,0:T(4,128)S(1)} %bitcast.8, bf16[8,128,512]{2,1,0:T(8,128)(2,1)S(1)} %get-tuple-element.51.mix_ref, f32[1,128]{1,0:T(1,128)S(1)} %get-tuple-element.63.order_ref, ...), custom_call_target="tpu_custom_call" | custom-call | flops 268435456 | bytes 1048576 | tf_op jit(solution)/shard_map/pallas_call | solution.py:49
  53.9 9.7 %all_to_all.16.parts_ref = f32[8,16,128]{2,1,0:T(8,128)S(1)} all-to-all(f32[8,16,128]{2,1,0:T(8,128)S(1)} %get-tuple-element.76), channel_id=1, replica_groups=mesh['row'=8,'col'=4] {'row'}, dimensions={0} | all-to-all | bytes 131072 | tf_op jit(solution)/shard_map/all_to_all | solution.py:23
  64.0 1.8 %shard_map.102 = (f32[32,128]{1,0:T(8,128)S(1)}, f32[1,128]{1,0:T(1,128)S(1)}) custom-call(f32[1024,4096]{1,0:T(8,128)S(1)} %get-tuple-element.52.rinv_ref, f32[8,16,128]{2,1,0:T(8,128)S(1)} %all_to_all.16.parts_ref), custom_call_target="tpu_custom_call" | custom-call | flops 8388608 | bytes 16777216 | tf_op jit(solution)/shard_map/pallas_call | solution.py:479
  65.9 1.2 %collective-permute-start.15 = (f32[32,128]{1,0:T(8,128)S(1)}, f32[32,128]{1,0:T(8,128)S(1)}, u32[]{:S(2)}, u32[]{:S(2)}) collective-permute-start(f32[32,128]{1,0:T(8,128)S(1)} %get-tuple-element.78.refs_0_), channel_id=1, source_target_pairs={{0,2},{1,3},{2,0},{3,1},{4,6},{5,7},{6,4},{7,5},{8,10},{9,11},{10,... | collective-permute-start | bytes 49160 | tf_op jit(solution)/shard_map/ppermute | solution.py:29
  67.1 0.7 collective-permute-start.16
  67.8 1.9 %collective-permute-done.15.refs_2_ = f32[32,128]{1,0:T(8,128)S(1)} collective-permute-done((f32[32,128]{1,0:T(8,128)S(1)}, f32[32,128]{1,0:T(8,128)S(1)}, u32[]{:S(2)}, u32[]{:S(2)}) %collective-permute-start.15) | collective-permute-done | bytes 16416 | tf_op jit(solution)/shard_map/ppermute | solution.py:29
  70.3 2.9 %shard_map.103 = (f32[4,128]{1,0:T(4,128)S(1)}, f32[32,128]{1,0:T(8,128)}, f32[8,128]{1,0:T(8,128)S(1)}, f32[1,128]{1,0:T(1,128)S(1)}) custom-call(f32[1024,4096]{1,0:T(8,128)S(1)} %get-tuple-element.52.rinv_ref, f32[512,1024]{1,0:T(8,128)S(1)} %copy-done, f32[32,128]{1,0:T(8,128)S(1)} %get-tuple-element.78.refs_0_, ...), custom_call_target="tpu_custom_call" | custom-call | flops 8388608 | bytes 16777216 | tf_op jit(solution)/shard_map/pallas_call | solution.py:49
  73.2 2.6 %collective-permute-done.13.refs_2_ = f32[1,4,128,128]{3,2,1,0:T(8,128)S(1)} collective-permute-done((f32[1,4,128,128]{3,2,1,0:T(8,128)S(1)}, f32[1,4,128,128]{3,2,1,0:T(8,128)S(1)}, u32[]{:S(2)}, u32[]{:S(2)}) %collective-permute-start.13) | collective-permute-done | bytes 262176 | tf_op jit(solution)/shard_map/ppermute | solution.py:429
  75.8 0.8 collective-permute-start.17
  76.7 2.7 %collective-permute-start.19 = (f32[128,256]{1,0:T(8,128)S(1)}, f32[128,256]{1,0:T(8,128)S(1)}, u32[]{:S(2)}, u32[]{:S(2)}) collective-permute-start(f32[128,256]{1,0:T(8,128)S(1)} %get-tuple-element.85), channel_id=1, source_target_pairs={{0,12},{4,8},{8,4},{12,0},{16,28},{20,24},{24,20},{28,16},{1,13},{... | collective-permute-start | bytes 393224 | tf_op jit(solution)/shard_map/ppermute | solution.py:429
  79.4 0.7 collective-permute-start.21
  80.6 0.7 collective-permute-start.22
  81.3 1.7 %collective-permute-done.21.refs_2_ = f32[4,128]{1,0:T(4,128)S(1)} collective-permute-done((f32[4,128]{1,0:T(4,128)S(1)}, f32[4,128]{1,0:T(4,128)S(1)}, u32[]{:S(2)}, u32[]{:S(2)}) %collective-permute-start.21) | collective-permute-done | bytes 2080 | tf_op jit(solution)/shard_map/ppermute | solution.py:29
  83.0 0.6 collective-permute-done.22.refs_3_
  83.7 9.2 %all_to_all.17.parts_ref = f32[8,8,128]{2,1,0:T(8,128)S(1)} all-to-all(f32[8,8,128]{2,1,0:T(8,128)S(1)} %get-tuple-element.89), channel_id=1, replica_groups=mesh['row'=8,'col'=4] {'row'}, dimensions={0} | all-to-all | bytes 65536 | tf_op jit(solution)/shard_map/all_to_all | solution.py:23
  92.9 0.6 shard_map.107
  93.5 0.9 shard_map.105
  (45 shorter events, 4.2 us)
Async XLA Ops:
  0.6 30.2 %copy-start.3 = (bf16[256,256]{1,0:T(8,128)(2,1)S(1)}, bf16[256,256]{1,0:T(8,128)(2,1)}, u32[]{:S(2)}) copy-start(bf16[256,256]{1,0:T(8,128)(2,1)} %constant.2.clone.walsh_ref) | copy-start | bytes 393220
  0.6 32.9 %copy-start = (f32[512,1024]{1,0:T(8,128)S(1)}, f32[512,1024]{1,0:T(8,128)}, u32[]{:S(2)}) copy-start(f32[512,1024]{1,0:T(8,128)} %design_ref.9) | copy-start | bytes 6291460
  4.1 28.1 %copy-start.6 = (f32[512,128]{1,0:T(8,128)S(1)}, f32[512,128]{1,0:T(8,128)}, u32[]{:S(2)}) copy-start(f32[512,128]{1,0:T(8,128)} %get-tuple-element.67) | copy-start | bytes 786436
  4.1 29.0 %copy-start.5 = (f32[512,128]{1,0:T(8,128)S(1)}, f32[512,128]{1,0:T(8,128)}, u32[]{:S(2)}) copy-start(f32[512,128]{1,0:T(8,128)} %get-tuple-element.68) | copy-start | bytes 786436
  18.7 17.3 %copy-start.4 = (f32[512,128]{1,0:T(8,128)S(1)}, f32[512,128]{1,0:T(8,128)}, u32[]{:S(2)}) copy-start(f32[512,128]{1,0:T(8,128)} %get-tuple-element.69) | copy-start | bytes 786436
  18.7 19.6 %copy-start.1 = (s32[512]{0:T(512)S(1)}, s32[512]{0:T(512)}, u32[]{:S(2)}) copy-start(s32[512]{0:T(512)} %param.8) | copy-start | bytes 6148
  18.7 17.3 %collective-permute-start.3 = (f32[512,128]{1,0:T(8,128)}, f32[512,128]{1,0:T(8,128)S(1)}, u32[]{:S(2)}, u32[]{:S(2)}) collective-permute-start(f32[512,128]{1,0:T(8,128)} %get-tuple-element.58), channel_id=1, source_target_pairs={{0,4},{4,0},{8,12},{12,8},{16,20},{20,16},{24,28},{28,24},{1,5},{5... | collective-permute-start | bytes 786440 | tf_op jit(solution)/shard_map/ppermute | solution.py:429
  19.0 19.3 %collective-permute-start.4 = (f32[512,128]{1,0:T(8,128)}, f32[512,128]{1,0:T(8,128)S(1)}, u32[]{:S(2)}, u32[]{:S(2)}) collective-permute-start(f32[512,128]{1,0:T(8,128)} %get-tuple-element.59), channel_id=1, source_target_pairs={{0,8},{4,12},{8,0},{12,4},{16,24},{20,28},{24,16},{28,20},{1,9},{5... | collective-permute-start | bytes 786440 | tf_op jit(solution)/shard_map/ppermute | solution.py:429
  19.9 18.3 %collective-permute-start.5 = (f32[512,128]{1,0:T(8,128)}, f32[512,128]{1,0:T(8,128)S(1)}, u32[]{:S(2)}, u32[]{:S(2)}) collective-permute-start(f32[512,128]{1,0:T(8,128)} %get-tuple-element.60), channel_id=1, source_target_pairs={{0,12},{4,8},{8,4},{12,0},{16,28},{20,24},{24,20},{28,16},{1,13},{... | collective-permute-start | bytes 786440 | tf_op jit(solution)/shard_map/ppermute | solution.py:429
  28.3 25.3 %copy-start.2 = (f32[512]{0:T(512)S(1)}, f32[512]{0:T(512)}, u32[]{:S(2)}) copy-start(f32[512]{0:T(512)} %param.11) | copy-start | bytes 6148
  28.3 1.6 %collective-permute-start = (f32[32,128]{1,0:T(8,128)S(1)}, f32[32,128]{1,0:T(8,128)S(1)}, u32[]{:S(2)}, u32[]{:S(2)}) collective-permute-start(f32[32,128]{1,0:T(8,128)S(1)} %get-tuple-element.53.refs_0_), channel_id=1, source_target_pairs={{0,1},{1,0},{2,3},{3,2},{4,5},{5,4},{6,7},{7,6},{8,9},{9,8},{10,11... | collective-permute-start | bytes 49160 | tf_op jit(solution)/shard_map/ppermute | solution.py:29
  28.4 3.8 %collective-permute-start.1 = (f32[32,128]{1,0:T(8,128)S(1)}, f32[32,128]{1,0:T(8,128)S(1)}, u32[]{:S(2)}, u32[]{:S(2)}) collective-permute-start(f32[32,128]{1,0:T(8,128)S(1)} %get-tuple-element.53.refs_0_), channel_id=1, source_target_pairs={{0,2},{1,3},{2,0},{3,1},{4,6},{5,7},{6,4},{7,5},{8,10},{9,11},{10,... | collective-permute-start | bytes 49160 | tf_op jit(solution)/shard_map/ppermute | solution.py:29
  30.0 3.2 %collective-permute-start.2 = (f32[32,128]{1,0:T(8,128)S(1)}, f32[32,128]{1,0:T(8,128)S(1)}, u32[]{:S(2)}, u32[]{:S(2)}) collective-permute-start(f32[32,128]{1,0:T(8,128)S(1)} %get-tuple-element.53.refs_0_), channel_id=1, source_target_pairs={{0,3},{1,2},{2,1},{3,0},{4,7},{5,6},{6,5},{7,4},{8,11},{9,10},{10,... | collective-permute-start | bytes 49160 | tf_op jit(solution)/shard_map/ppermute | solution.py:29
  32.2 8.5 %collective-permute-start.7 = (f32[512,128]{1,0:T(8,128)S(1)}, f32[512,128]{1,0:T(8,128)S(1)}, u32[]{:S(2)}, u32[]{:S(2)}) collective-permute-start(f32[512,128]{1,0:T(8,128)S(1)} %copy-done.6), channel_id=1, source_target_pairs={{0,4},{4,0},{8,12},{12,8},{16,20},{20,16},{24,28},{28,24},{1,5},{5... | collective-permute-start | bytes 786440 | tf_op jit(solution)/shard_map/ppermute | solution.py:429
  33.2 9.2 %collective-permute-start.8 = (f32[512,128]{1,0:T(8,128)S(1)}, f32[512,128]{1,0:T(8,128)S(1)}, u32[]{:S(2)}, u32[]{:S(2)}) collective-permute-start(f32[512,128]{1,0:T(8,128)S(1)} %copy-done.5), channel_id=1, source_target_pairs={{0,8},{4,12},{8,0},{12,4},{16,24},{20,28},{24,16},{28,20},{1,9},{5... | collective-permute-start | bytes 786440 | tf_op jit(solution)/shard_map/ppermute | solution.py:429
  35.9 16.3 %collective-permute-start.9 = (f32[512,128]{1,0:T(8,128)S(1)}, f32[512,128]{1,0:T(8,128)S(1)}, u32[]{:S(2)}, u32[]{:S(2)}) collective-permute-start(f32[512,128]{1,0:T(8,128)S(1)} %copy-done.4), channel_id=1, source_target_pairs={{0,12},{4,8},{8,4},{12,0},{16,28},{20,24},{24,20},{28,16},{1,13},{... | collective-permute-start | bytes 786440 | tf_op jit(solution)/shard_map/ppermute | solution.py:429
  39.3 14.3 %collective-permute-start.6 = (f32[1,4,128,128]{3,2,1,0:T(8,128)S(1)}, f32[1,4,128,128]{3,2,1,0:T(8,128)S(1)}, u32[]{:S(2)}, u32[]{:S(2)}) collective-permute-start(f32[1,4,128,128]{3,2,1,0:T(8,128)S(1)} %get-tuple-element.62), channel_id=1, source_target_pairs={{0,16},{4,20},{8,24},{12,28},{16,0},{20,4},{24,8},{28,12},{1,17},{... | collective-permute-start | bytes 786440 | tf_op jit(solution)/shard_map/ppermute | solution.py:429
  39.8 13.8 %collective-permute-start.10 = (f32[4,128]{1,0:T(4,128)S(1)}, f32[4,128]{1,0:T(4,128)S(1)}, u32[]{:S(2)}, u32[]{:S(2)}) collective-permute-start(f32[4,128]{1,0:T(4,128)S(1)} %get-tuple-element.74.refs_0_), channel_id=1, source_target_pairs={{0,1},{1,0},{2,3},{3,2},{4,5},{5,4},{6,7},{7,6},{8,9},{9,8},{10,11... | collective-permute-start | bytes 6152 | tf_op jit(solution)/shard_map/ppermute | solution.py:29
  40.7 12.9 %collective-permute-start.11 = (f32[4,128]{1,0:T(4,128)S(1)}, f32[4,128]{1,0:T(4,128)S(1)}, u32[]{:S(2)}, u32[]{:S(2)}) collective-permute-start(f32[4,128]{1,0:T(4,128)S(1)} %get-tuple-element.74.refs_0_), channel_id=1, source_target_pairs={{0,2},{1,3},{2,0},{3,1},{4,6},{5,7},{6,4},{7,5},{8,10},{9,11},{10,... | collective-permute-start | bytes 6152 | tf_op jit(solution)/shard_map/ppermute | solution.py:29
  42.3 11.3 %collective-permute-start.12 = (f32[4,128]{1,0:T(4,128)S(1)}, f32[4,128]{1,0:T(4,128)S(1)}, u32[]{:S(2)}, u32[]{:S(2)}) collective-permute-start(f32[4,128]{1,0:T(4,128)S(1)} %get-tuple-element.74.refs_0_), channel_id=1, source_target_pairs={{0,3},{1,2},{2,1},{3,0},{4,7},{5,6},{6,5},{7,4},{8,11},{9,10},{10,... | collective-permute-start | bytes 6152 | tf_op jit(solution)/shard_map/ppermute | solution.py:29
  63.6 12.2 %collective-permute-start.13 = (f32[1,4,128,128]{3,2,1,0:T(8,128)S(1)}, f32[1,4,128,128]{3,2,1,0:T(8,128)S(1)}, u32[]{:S(2)}, u32[]{:S(2)}) collective-permute-start(f32[1,4,128,128]{3,2,1,0:T(8,128)S(1)} %get-tuple-element.77), channel_id=1, source_target_pairs={{0,16},{4,20},{8,24},{12,28},{16,0},{20,4},{24,8},{28,12},{1,17},{... | collective-permute-start | bytes 786440 | tf_op jit(solution)/shard_map/ppermute | solution.py:429
  65.9 1.9 %collective-permute-start.14 = (f32[32,128]{1,0:T(8,128)S(1)}, f32[32,128]{1,0:T(8,128)S(1)}, u32[]{:S(2)}, u32[]{:S(2)}) collective-permute-start(f32[32,128]{1,0:T(8,128)S(1)} %get-tuple-element.78.refs_0_), channel_id=1, source_target_pairs={{0,1},{1,0},{2,3},{3,2},{4,5},{5,4},{6,7},{7,6},{8,9},{9,8},{10,11... | collective-permute-start | bytes 49160 | tf_op jit(solution)/shard_map/ppermute | solution.py:29
  65.9 3.8 %collective-permute-start.15 = (f32[32,128]{1,0:T(8,128)S(1)}, f32[32,128]{1,0:T(8,128)S(1)}, u32[]{:S(2)}, u32[]{:S(2)}) collective-permute-start(f32[32,128]{1,0:T(8,128)S(1)} %get-tuple-element.78.refs_0_), channel_id=1, source_target_pairs={{0,2},{1,3},{2,0},{3,1},{4,6},{5,7},{6,4},{7,5},{8,10},{9,11},{10,... | collective-permute-start | bytes 49160 | tf_op jit(solution)/shard_map/ppermute | solution.py:29
  67.1 3.2 %collective-permute-start.16 = (f32[32,128]{1,0:T(8,128)S(1)}, f32[32,128]{1,0:T(8,128)S(1)}, u32[]{:S(2)}, u32[]{:S(2)}) collective-permute-start(f32[32,128]{1,0:T(8,128)S(1)} %get-tuple-element.78.refs_0_), channel_id=1, source_target_pairs={{0,3},{1,2},{2,1},{3,0},{4,7},{5,6},{6,5},{7,4},{8,11},{9,10},{10,... | collective-permute-start | bytes 49160 | tf_op jit(solution)/shard_map/ppermute | solution.py:29
  75.8 17.7 %collective-permute-start.17 = (f32[128,256]{1,0:T(8,128)S(1)}, f32[128,256]{1,0:T(8,128)S(1)}, u32[]{:S(2)}, u32[]{:S(2)}) collective-permute-start(f32[128,256]{1,0:T(8,128)S(1)} %get-tuple-element.83), channel_id=1, source_target_pairs={{0,4},{4,0},{8,12},{12,8},{16,20},{20,16},{24,28},{28,24},{1,5},{5... | collective-permute-start | bytes 393224 | tf_op jit(solution)/shard_map/ppermute | solution.py:429
  76.7 16.9 %collective-permute-start.18 = (f32[128,256]{1,0:T(8,128)S(1)}, f32[128,256]{1,0:T(8,128)S(1)}, u32[]{:S(2)}, u32[]{:S(2)}) collective-permute-start(f32[128,256]{1,0:T(8,128)S(1)} %get-tuple-element.84), channel_id=1, source_target_pairs={{0,8},{4,12},{8,0},{12,4},{16,24},{20,28},{24,16},{28,20},{1,9},{5... | collective-permute-start | bytes 393224 | tf_op jit(solution)/shard_map/ppermute | solution.py:429
  76.7 16.9 %collective-permute-start.19 = (f32[128,256]{1,0:T(8,128)S(1)}, f32[128,256]{1,0:T(8,128)S(1)}, u32[]{:S(2)}, u32[]{:S(2)}) collective-permute-start(f32[128,256]{1,0:T(8,128)S(1)} %get-tuple-element.85), channel_id=1, source_target_pairs={{0,12},{4,8},{8,4},{12,0},{16,28},{20,24},{24,20},{28,16},{1,13},{... | collective-permute-start | bytes 393224 | tf_op jit(solution)/shard_map/ppermute | solution.py:429
  79.4 1.2 %collective-permute-start.20 = (f32[4,128]{1,0:T(4,128)S(1)}, f32[4,128]{1,0:T(4,128)S(1)}, u32[]{:S(2)}, u32[]{:S(2)}) collective-permute-start(f32[4,128]{1,0:T(4,128)S(1)} %get-tuple-element.86.refs_0_), channel_id=1, source_target_pairs={{0,1},{1,0},{2,3},{3,2},{4,5},{5,4},{6,7},{7,6},{8,9},{9,8},{10,11... | collective-permute-start | bytes 6152 | tf_op jit(solution)/shard_map/ppermute | solution.py:29
  79.4 3.6 %collective-permute-start.21 = (f32[4,128]{1,0:T(4,128)S(1)}, f32[4,128]{1,0:T(4,128)S(1)}, u32[]{:S(2)}, u32[]{:S(2)}) collective-permute-start(f32[4,128]{1,0:T(4,128)S(1)} %get-tuple-element.86.refs_0_), channel_id=1, source_target_pairs={{0,2},{1,3},{2,0},{3,1},{4,6},{5,7},{6,4},{7,5},{8,10},{9,11},{10,... | collective-permute-start | bytes 6152 | tf_op jit(solution)/shard_map/ppermute | solution.py:29
  80.6 3.0 %collective-permute-start.22 = (f32[4,128]{1,0:T(4,128)S(1)}, f32[4,128]{1,0:T(4,128)S(1)}, u32[]{:S(2)}, u32[]{:S(2)}) collective-permute-start(f32[4,128]{1,0:T(4,128)S(1)} %get-tuple-element.86.refs_0_), channel_id=1, source_target_pairs={{0,3},{1,2},{2,1},{3,0},{4,7},{5,6},{6,5},{7,4},{8,11},{9,10},{10,... | collective-permute-start | bytes 6152 | tf_op jit(solution)/shard_map/ppermute | solution.py:29

commit v6 on v5

--- a/solution.py
+++ b/solution.py
@@ -45,7 +45,7 @@
     return (1 - 2 * parity).astype(np.float32)
 
 
-def call(body, out_shape, *operands, scratch=(), flops=0, size=0):
+def call(body, out_shape, *operands, scratch=()):
     return pl.pallas_call(
         body,
         out_shape=out_shape,
@@ -53,7 +53,6 @@
         out_specs=jax.tree.map(lambda _: VMEM, out_shape),
         scratch_shapes=scratch,
         compiler_params=pltpu.CompilerParams(vmem_limit_bytes=24 << 20),
-        cost_estimate=pl.CostEstimate(flops=flops, bytes_accessed=size, transcendentals=0),
     )(*operands)
 
 
@@ -73,10 +72,10 @@
     blocks, tiles = matrix_ref.shape[0] // LANE, matrix_ref.shape[1] // LANE
     sums = [jnp.zeros((8, LANE), F32) for _ in range(tiles)]
     for block in range(blocks):
-        across = jnp.broadcast_to(vector[block : block + 1, :], (LANE, LANE)).T
+        weight = across(vector[block : block + 1, :])
         for tile in range(tiles):
             part = matrix_ref[block * LANE : (block + 1) * LANE, tile * LANE : (tile + 1) * LANE]
-            sums[tile] = sums[tile] + fold_rows(part * across)
+            sums[tile] = sums[tile] + fold_rows(part * weight)
     for tile in range(tiles):
         out_ref[tile : tile + 1, :] = jnp.sum(sums[tile], axis=0, keepdims=True)
 
@@ -85,10 +84,10 @@
     blocks, tiles = matrix_ref.shape[0] // LANE, matrix_ref.shape[1] // LANE
 
     def step(block, sums):
-        across = jnp.broadcast_to(vector_ref[pl.ds(block, 1), :], (LANE, LANE)).T
+        weight = across(vector_ref[pl.ds(block, 1), :])
         rows = pl.ds(pl.multiple_of(block * LANE, LANE), LANE)
         return tuple(
-            sums[tile] + fold_rows(matrix_ref[rows, tile * LANE : (tile + 1) * LANE] * across)
+            sums[tile] + fold_rows(matrix_ref[rows, tile * LANE : (tile + 1) * LANE] * weight)
             for tile in range(tiles)
         )
 
@@ -125,23 +124,29 @@
     return rounded(width // LANE + 1, 8)
 
 
+def picks_at(width):
+    return message_rows(width)
+
+
+def signs_at(width, groups):
+    return message_rows(width) + rounded(groups, 8)
+
+
 def copy_out(out_ref):
     first = out_ref[0]
     for index in range(1, out_ref.shape[0]):
         out_ref[index] = first
 
 
-def signs_across(bits_ref, block):
-    signs = (2 * bits_ref[block : block + 1, :] - 1).astype(F32)
-    return jnp.broadcast_to(signs, (LANE, LANE)).T
+def across(row):
+    return jnp.broadcast_to(row, (LANE, LANE)).T
 
 
 def first_body(design_ref, target_ref, bits_ref, picks_ref, counts_ref, *refs):
-    out_ref, away_refs = refs[0], refs[1:-7]
-    design, target_here, bits, picks, counts, away, sems = refs[-7:]
-    chunks = len(away_refs) // (NEAR - 1)
+    out_ref, away_refs = refs[0], refs[1:-6]
+    design, target_here, bits, picks, counts, sems = refs[-6:]
     rows, width = design.shape
-    lines, tiles, piece = rows // LANE, width // LANE, width // NEAR
+    lines, tiles, quarter = rows // LANE, width // LANE, width // NEAR
     small = [
         pltpu.make_async_copy(source, place, sems.at[index])
         for index, (source, place) in enumerate(
@@ -153,49 +158,41 @@
         pltpu.make_async_copy(design_ref.at[part, :], design.at[part, :], sems.at[4 + line])
         for line, part in enumerate(parts)
     ]
-    for copy in small + large:
+    place = lax.axis_index("row") % NEAR
+    away = []
+    for index, away_ref in enumerate(away_refs):
+        chunk, mask = index // (NEAR - 1), index % (NEAR - 1) + 1
+        piece = away_ref.shape[1]
+        column = pl.multiple_of((place ^ mask) * quarter + chunk * piece, LANE)
+        source = design_ref.at[:, pl.ds(column, piece)]
+        away.append(pltpu.make_async_copy(source, away_ref, sems.at[4 + lines + index]))
+    for copy in small + large + away:
         copy.start()
     for copy in small:
         copy.wait()
-    place = lax.axis_index("row") % NEAR
-    sums = [jnp.zeros((8, LANE), F32) for _ in range(tiles)]
-    back = []
-    for line, part in enumerate(parts):
-        across = jnp.broadcast_to(target_here[line : line + 1, :], (LANE, LANE)).T
-        signs = signs_across(bits, line)
-        large[line].wait()
-        for tile in range(tiles):
-            value = design[part, tile * LANE : (tile + 1) * LANE]
-            sums[tile] = sums[tile] + fold_rows(value * across)
-        for mask in range(1, NEAR):
-            for tile in range(0, piece, LANE):
-                column = pl.multiple_of((place ^ mask) * piece + tile, LANE)
-                away[mask - 1, part, tile : tile + LANE] = design[part, pl.ds(column, LANE)] * signs
-            for chunk in range(chunks):
-                index = chunk * (NEAR - 1) + mask - 1
-                columns = slice(chunk * piece // chunks, (chunk + 1) * piece // chunks)
-                copy = pltpu.make_async_copy(
-                    away.at[mask - 1, part, columns],
-                    away_refs[index].at[part, :],
-                    sems.at[4 + lines * (index + 1) + line],
-                )
-                copy.start()
-                back.append(copy)
     out_ref[0] = jnp.zeros(out_ref.shape[1:], F32)
-    for tile in range(tiles):
-        out_ref[0, tile : tile + 1, :] = jnp.sum(sums[tile], axis=0, keepdims=True)
-    target = target_here[...]
-    out_ref[0, tiles : tiles + 1, :] = splat(total(target * target))
     groups = picks.shape[0]
     owner = lax.broadcasted_iota(jnp.int32, (groups, groups), 0)
     same = owner == lax.broadcasted_iota(jnp.int32, (groups, groups), 1)
     limit = jnp.sum(jnp.where(same, counts[...].astype(F32), 0.0), axis=1, keepdims=True)
     slot = lax.broadcasted_iota(jnp.int32, picks.shape, 1).astype(F32)
     coded = jnp.where(slot < limit, picks[...].astype(F32), -1.0)
-    start = message_rows(width)
+    start = picks_at(width)
     out_ref[0, start : start + groups, : coded.shape[1]] = coded
+    start = signs_at(width, groups)
+    out_ref[0, start : start + lines, :] = (2 * bits[...] - 1).astype(F32)
+    target = target_here[...]
+    out_ref[0, tiles : tiles + 1, :] = splat(total(target * target))
+    sums = [jnp.zeros((8, LANE), F32) for _ in range(tiles)]
+    for line, part in enumerate(parts):
+        weight = across(target[line : line + 1, :])
+        large[line].wait()
+        for tile in range(tiles):
+            sums[tile] = sums[tile] + fold_rows(design[part, tile * LANE : (tile + 1) * LANE] * weight)
+    for tile in range(tiles):
+        out_ref[0, tile : tile + 1, :] = jnp.sum(sums[tile], axis=0, keepdims=True)
     copy_out(out_ref)
-    for copy in back:
+    for copy in away:
         copy.wait()
 
 
@@ -251,10 +248,17 @@
 
 
 def last_body(parts_ref, left_ref, *refs):
+    quarters, sketch_ref, refs = refs[-NEAR - 3 : -3], refs[-1], refs[:-1]
+    place = lax.axis_index("row") % NEAR
+    piece = quarters[0].shape[1]
+    for mask, part_ref in enumerate(quarters):
+        for tile in range(0, piece, LANE):
+            column = pl.multiple_of((place ^ mask) * piece + tile, LANE)
+            sketch_ref[:, pl.ds(column, LANE)] = part_ref[:, tile : tile + LANE]
     betas = [ref[...] for ref in refs[:ITERS]]
     alphas = [ref[...] for ref in refs[ITERS : 2 * ITERS]]
     held = [ref[...] for ref in refs[2 * ITERS : 3 * ITERS]]
-    basis_ref, solution_ref = refs[3 * ITERS :]
+    basis_ref, solution_ref = refs[-2:]
     last = jnp.sqrt(tree([parts_ref[i] for i in range(parts_ref.shape[0])])[:1, :])
     basis_ref[...] = left_ref[...] / last
     betas.append(last)
@@ -275,11 +279,9 @@
     solution_ref[...] = iterate
 
 
-def mix_body(parts_ref, walsh_ref, order_ref, out_ref, token_ref):
+def mix_body(start, parts_ref, walsh_ref, order_ref, out_ref, token_ref):
     token_ref[...] = order_ref[...]
     groups, _, rows = out_ref.shape
-    spread = rounded(groups, 8)
-    start = parts_ref.shape[1] - spread
     me = lax.axis_index("row")
     local = lax.broadcasted_iota(jnp.int32, (PAIR, rows), 1).astype(F32)
 
@@ -308,20 +310,22 @@
         lax.fori_loop(0, groups, step, 0)
 
 
-def sample_body(scale, start, design_ref, bits_ref, mix_ref, order_ref, *refs):
+def sample_body(scale, start, design_ref, parts_ref, mix_ref, order_ref, *refs):
     near, (keep_ref, send_ref, token_ref, both) = refs[: NEAR - 1], refs[NEAR - 1 :]
     token_ref[...] = order_ref[...]
     rows, piece = near[0].shape
     quarter = design_ref.shape[1] // NEAR
     groups = mix_ref.shape[0]
-    place = lax.axis_index("row") % NEAR
+    me = lax.axis_index("row")
+    signs_start = signs_at(design_ref.shape[1], groups)
     for line in range(rows // LANE):
         part = slice(line * LANE, (line + 1) * LANE)
-        signs = signs_across(bits_ref, line)
+        signs = [across(parts_ref[me ^ mask, signs_start + line : signs_start + line + 1, :]) for mask in range(NEAR)]
         for tile in range(0, piece, LANE):
-            column = pl.multiple_of(place * quarter + start + tile, LANE)
+            column = pl.multiple_of(me % NEAR * quarter + start + tile, LANE)
             here = slice(tile, tile + LANE)
-            values = [design_ref[part, pl.ds(column, LANE)] * signs] + [ref[part, here] for ref in near]
+            values = [design_ref[part, pl.ds(column, LANE)]] + [ref[part, here] for ref in near]
+            values = [value * sign for value, sign in zip(values, signs)]
             apart = 1
             while apart < NEAR:
                 for first in range(NEAR):
@@ -366,7 +370,7 @@
 
 def split_body(chunks, *refs):
     joined, (kept_ref, arrived_ref, order_ref, token_ref, *out_refs) = refs[: chunks - 1], refs[chunks - 1 :]
-    token_ref[...] = order_ref[...]
+    token_ref[...] = order_ref[:1, :]
     piece = kept_ref.shape[3]
     for chunk in range(chunks):
         columns = slice(chunk * piece, (chunk + 1) * piece)
@@ -377,16 +381,6 @@
                 out_ref[:, columns] = kept_ref[0, index] + arrived_ref[0, index]
 
 
-def assemble_body(*refs):
-    parts, out_ref = refs[:-1], refs[-1]
-    place = lax.axis_index("row") % NEAR
-    piece = parts[0].shape[1]
-    for mask, part_ref in enumerate(parts):
-        for tile in range(0, piece, LANE):
-            column = pl.multiple_of((place ^ mask) * piece + tile, LANE)
-            out_ref[:, pl.ds(column, LANE)] = part_ref[:, tile : tile + LANE]
-
-
 def shape(*dims, dtype=F32):
     return jax.ShapeDtypeStruct(dims, dtype)
 
@@ -396,7 +390,6 @@
     whole = rinv.shape[1]
     row_groups, col_groups = lax.axis_size("row"), lax.axis_size("col")
     lines = rows // LANE
-    big, small = rinv.size, design.size
     scalar = shape(1, LANE)
     deep = message_rows(width)
     left = target.reshape(lines, LANE)
@@ -408,7 +401,7 @@
 
     message, *away = pl.pallas_call(
         first_body,
-        out_shape=(shape(row_groups, deep + rounded(row_groups, 8), LANE),)
+        out_shape=(shape(row_groups, signs_at(width, row_groups) + rounded(lines, 8), LANE),)
         + (shape(rows, piece),) * (chunks * (NEAR - 1)),
         in_specs=[HBM] * 5,
         out_specs=(VMEM,) + (HBM,) * (chunks * (NEAR - 1)),
@@ -418,11 +411,9 @@
             pltpu.VMEM((lines, LANE), jnp.int32),
             pltpu.VMEM((row_groups, PAIR), jnp.int32),
             pltpu.VMEM((1, row_groups), jnp.int32),
-            pltpu.VMEM((NEAR - 1, rows, width // NEAR), F32),
-            pltpu.SemaphoreType.DMA((4 + lines * (1 + chunks * (NEAR - 1)),)),
+            pltpu.SemaphoreType.DMA((4 + lines + chunks * (NEAR - 1),)),
         ],
         compiler_params=pltpu.CompilerParams(vmem_limit_bytes=58 << 20),
-        cost_estimate=pl.CostEstimate(flops=2 * small, bytes_accessed=7 * small, transcendentals=0),
     )(design, left, bits, picks.reshape(row_groups, PAIR), counts.reshape(1, row_groups))
 
     def swap(array, mask):
@@ -431,7 +422,7 @@
     def mix(order):
         signs = jnp.asarray(walsh(HB), jnp.bfloat16)
         made = (shape(row_groups, slots, rows, dtype=jnp.bfloat16), scalar)
-        return call(mix_body, made, picked, signs, order, flops=2 * row_groups * slots * rows * HB)
+        return call(functools.partial(mix_body, picks_at(width)), made, picked, signs, order)
 
     def sample(chunk, mixed, order):
         scale = float(np.sqrt(np.float32(rows * row_groups)))
@@ -439,13 +430,11 @@
             functools.partial(sample_body, scale, chunk * piece),
             (shape(far // 2, NEAR, slots, piece),) * 2 + (scalar,),
             design,
-            bits,
+            picked,
             mixed,
             order,
             *near[chunk],
             scratch=[pltpu.VMEM((NEAR, 2, rows, piece), jnp.bfloat16)],
-            flops=4 * row_groups * slots * rows * piece,
-            size=4 * NEAR * rows * piece,
         )
 
     def halve(keep, come, order):
@@ -483,8 +472,7 @@
             out_specs=(VMEM,) * len(outs),
             scratch_shapes=scratch,
             compiler_params=pltpu.CompilerParams(vmem_limit_bytes=(34 if first else 24) << 20),
-            cost_estimate=pl.CostEstimate(flops=2 * big, bytes_accessed=4 * big, transcendentals=0),
-        )(rinv, message)
+            )(rinv, message)
 
     def forward(terms, *before):
         return call(
@@ -494,8 +482,6 @@
             design,
             *terms,
             *before,
-            flops=2 * big,
-            size=4 * big,
         )
 
     def turn(images, left, beta, alpha, token, last):
@@ -508,8 +494,6 @@
             alpha,
             token,
             *(() if last else (design,)),
-            flops=2 * small,
-            size=0 if last else 4 * small,
         )
 
     def spread(chunk, order):
@@ -535,9 +519,8 @@
         held.append(kept)
         if step == 0:
             parts = []
-            token = alpha
             for chunk in range(chunks):
-                keep, send, token = sample(chunk, mixed, token)
+                keep, send, token = sample(chunk, mixed, token if chunk == 0 else alpha)
                 if chunk < chunks - 1:
                     parts.append((keep, swap(send, row_groups // 2)))
             for part in parts:
@@ -545,16 +528,22 @@
                 joined.append(part)
         images = direct(image, "col")
         if last:
-            quarters, token = trade(joined, keep, come, alpha)
+            quarters, token = trade(joined, keep, come, images[1])
         left, message = turn(images, left, beta, alpha, token, last)
         message = exchange(message, "row")
         if step == 0:
             send, _ = lax.optimization_barrier((send, message))
             come = swap(send, row_groups // 2)
-    basis, answer = call(
-        last_body, (shape(lines, LANE), shape(width // LANE, LANE)), message, left, *betas, *alphas, *held
+    basis, answer, sketch = call(
+        last_body,
+        (shape(lines, LANE), shape(width // LANE, LANE), shape(slots, width)),
+        message,
+        left,
+        *betas,
+        *alphas,
+        *held,
+        *quarters,
     )
-    sketch = call(assemble_body, shape(slots, width), *quarters, size=8 * slots * width)
     return (sketch, answer.reshape(-1), basis.reshape(-1))
 
 

time: 94.7 us -> 143 us (1.51)
  Pallas kernels: 22 us -> 67.7 us
  waiting for transfers between devices: 20 us -> 21.5 us
    pallas_call x1, Pallas kernels: 3.45 us -> 49.5 us  [shards(): pl.pallas_call(first_body, out_shape=(shape(row_groups, signs_at(width, r...]
    ppermute x12, waiting for transfers between devices: 5.94 us -> 14.2 us  [direct(): lax.ppermute(array, axis, [(i, i ^ mask) for i in range(size)])]
    ppermute x11, waiting for transfers between devices: 14 us -> 7.35 us  [swap(): lax.ppermute(array, 'row', [(i, i ^ mask) for i in range(row_groups)])]
    pallas_call x11 -> x10, Pallas kernels: 10.6 us -> 10.2 us  [call(): pl.pallas_call(body, out_shape=out_shape, in_specs=[VMEM] * len(operands)...]
  transfers between devices with their start and end apart: 23 -> 23, of which waited for: 12 -> 12; matrix products, arithmetic and copies ran while one was open for 0% -> 0% of each run, Pallas kernels for 18% -> 12%
where the time goes in v6:
time: 143 us; the launch traced here: 142 us
  Pallas kernels  67.7 us (47%)
  blocking collectives  34.8 us (24%)
  waiting for transfers between devices  21.5 us (15%)
  starting transfers between devices  17.4 us (12%)
    pallas_call x1, Pallas kernels, shards(): pl.pallas_call(first_body, out_shape=(shape(row_groups, signs_at(width, r...  49.5 us
    all_to_all x3, blocking collectives, exchange(): return lax.all_to_all(copies, axis, split_axis=0, concat_axis=0, tiled=True)  34.8 us
    ppermute x12, waiting for transfers between devices, direct(): lax.ppermute(array, axis, [(i, i ^ mask) for i in range(size)])  14.2 us
    ppermute x11, starting transfers between devices, swap(): lax.ppermute(array, 'row', [(i, i ^ mask) for i in range(row_groups)])  11.1 us
    pallas_call x10, Pallas kernels, call(): pl.pallas_call(body, out_shape=out_shape, in_specs=[VMEM] * len(operands)...  10.2 us
    pallas_call x2, Pallas kernels, back(): pl.pallas_call(functools.partial(back_body, first), out_shape=outs, in_sp...  7.97 us
    ppermute x11, waiting for transfers between devices, swap(): lax.ppermute(array, 'row', [(i, i ^ mask) for i in range(row_groups)])  7.35 us
    ppermute x12, starting transfers between devices, direct(): lax.ppermute(array, axis, [(i, i ^ mask) for i in range(size)])  6.29 us
  transfers between devices with their start and end apart: 23, of which 12 were waited for; matrix products, arithmetic and copies ran while one was open for 0% of the time, Pallas kernels for 12%

profile of v6, /device:TPU:0, one launch (start us, length us, event | category | flops | bytes accessed | tf_op | source)
XLA Modules:
  0.0 142.4 jit_solution(15650366398085522507)
XLA Ops:
  0.7 49.5 %shard_map.94 = (f32[8,32,128]{2,1,0:T(8,128)}, f32[512,128]{1,0:T(8,128)}, f32[512,128]{1,0:T(8,128)}, f32[512,128]{1,0:T(8,128)}, f32[512,128]{1,0:T(8,128)}, /*index=5*/f32[512,128]{1,0:T(8,128)}, f32[512,128]{1,0:T(8,128)}) custom-call(f32[512,1024]{1,0:T(8,128)} %design_ref.9, f32[4,128]{1,0:T(4,128)} %bitcast.6, s32[4,128]{1,0:T(4,128)} %bitcast.9, ...), custom_call_target="tpu_custom_call" | custom-call | tf_op jit(solution)/shard_map/pallas_call | solution.py:402
  50.2 14.8 %all_to_all.15.parts_ref = f32[8,32,128]{2,1,0:T(8,128)S(1)} all-to-all(f32[8,32,128]{2,1,0:T(8,128)} %get-tuple-element.50), channel_id=1, replica_groups=mesh['row'=8,'col'=4] {'row'}, dimensions={0} | all-to-all | bytes 262144 | tf_op jit(solution)/shard_map/all_to_all | solution.py:23
  65.2 1.1 collective-permute-start.7
  66.3 2.2 %collective-permute-start.8 = (f32[512,128]{1,0:T(8,128)}, f32[512,128]{1,0:T(8,128)S(1)}, u32[]{:S(2)}, u32[]{:S(2)}) collective-permute-start(f32[512,128]{1,0:T(8,128)} %get-tuple-element.63), channel_id=1, source_target_pairs={{0,12},{4,8},{8,4},{12,0},{16,28},{20,24},{24,20},{28,16},{1,13},{... | collective-permute-start | bytes 786440 | tf_op jit(solution)/shard_map/ppermute | solution.py:420
  68.5 6.2 %shard_map.95 = (f32[32,128]{1,0:T(8,128)S(1)}, f32[1,128]{1,0:T(1,128)S(1)}, f32[1024,4096]{1,0:T(8,128)S(1)}) custom-call(f32[1024,4096]{1,0:T(8,128)} %rinv_ref.1, f32[8,32,128]{2,1,0:T(8,128)S(1)} %all_to_all.15.parts_ref), custom_call_target="tpu_custom_call" | custom-call | tf_op jit(solution)/shard_map/pallas_call | solution.py:468
  75.0 1.1 collective-permute-start.11
  76.1 0.9 shard_map.97
  77.0 2.2 %collective-permute-start.12 = (f32[512,128]{1,0:T(8,128)S(1)}, f32[512,128]{1,0:T(8,128)S(1)}, u32[]{:S(2)}, u32[]{:S(2)}) collective-permute-start(f32[512,128]{1,0:T(8,128)S(1)} %copy-done.3), channel_id=1, source_target_pairs={{0,12},{4,8},{8,4},{12,0},{16,28},{20,24},{24,20},{28,16},{1,13},{... | collective-permute-start | bytes 786440 | tf_op jit(solution)/shard_map/ppermute | solution.py:420
  79.2 4.7 %collective-permute-done.8.refs_2_ = f32[512,128]{1,0:T(8,128)S(1)} collective-permute-done((f32[512,128]{1,0:T(8,128)}, f32[512,128]{1,0:T(8,128)S(1)}, u32[]{:S(2)}, u32[]{:S(2)}) %collective-permute-start.8) | collective-permute-done | bytes 262176 | tf_op jit(solution)/shard_map/ppermute | solution.py:420
  83.9 1.5 %shard_map.98 = (f32[1,4,128,128]{3,2,1,0:T(8,128)S(1)}, f32[1,4,128,128]{3,2,1,0:T(8,128)S(1)}, f32[1,128]{1,0:T(1,128)}) custom-call(f32[512,1024]{1,0:T(8,128)S(1)} %copy-done, f32[8,32,128]{2,1,0:T(8,128)S(1)} %all_to_all.15.parts_ref, bf16[8,128,512]{2,1,0:T(8,128)(2,1)S(1)} %get-tuple-element.56.mix_ref, f32[1,128]{1,0:T(1,128)S(1)} %get-tuple-element.57.order_ref, ...), custom_call_target="tpu_custom_call" | custom-call | tf_op jit(solution)/shard_map/pallas_call | solution.py:49
  85.5 1.2 collective-permute-done.refs_1_
  86.6 1.5 %collective-permute-start.1 = (f32[32,128]{1,0:T(8,128)S(1)}, f32[32,128]{1,0:T(8,128)S(1)}, u32[]{:S(2)}, u32[]{:S(2)}) collective-permute-start(f32[32,128]{1,0:T(8,128)S(1)} %get-tuple-element.52.refs_0_), channel_id=1, source_target_pairs={{0,2},{1,3},{2,0},{3,1},{4,6},{5,7},{6,4},{7,5},{8,10},{9,11},{10,... | collective-permute-start | bytes 49160 | tf_op jit(solution)/shard_map/ppermute | solution.py:29
  88.1 2.2 %collective-permute-done.1.refs_2_ = f32[32,128]{1,0:T(8,128)S(1)} collective-permute-done((f32[32,128]{1,0:T(8,128)S(1)}, f32[32,128]{1,0:T(8,128)S(1)}, u32[]{:S(2)}, u32[]{:S(2)}) %collective-permute-start.1) | collective-permute-done | bytes 16416 | tf_op jit(solution)/shard_map/ppermute | solution.py:29
  90.5 3.2 %collective-permute-done.2.refs_3_ = f32[32,128]{1,0:T(8,128)S(1)} collective-permute-done((f32[32,128]{1,0:T(8,128)S(1)}, f32[32,128]{1,0:T(8,128)S(1)}, u32[]{:S(2)}, u32[]{:S(2)}) %collective-permute-start.2) | collective-permute-done | bytes 16416 | tf_op jit(solution)/shard_map/ppermute | solution.py:29
  93.7 2.4 %shard_map.96 = (f32[4,128]{1,0:T(4,128)S(1)}, f32[32,128]{1,0:T(8,128)S(1)}, f32[8,128]{1,0:T(8,128)S(1)}, f32[1,128]{1,0:T(1,128)S(1)}) custom-call(f32[1024,4096]{1,0:T(8,128)S(1)} %get-tuple-element.51.rinv_ref, f32[512,1024]{1,0:T(8,128)S(1)} %copy-done, f32[32,128]{1,0:T(8,128)S(1)} %get-tuple-element.52.refs_0_, ...), custom_call_target="tpu_custom_call" | custom-call | tf_op jit(solution)/shard_map/pallas_call | solution.py:49
  96.3 1.3 collective-permute-start.4
  98.0 1.1 shard_map.99
  99.2 0.7 collective-permute-done.4.refs_2_
  99.9 0.7 collective-permute-done.5.refs_3_
  100.9 10.9 %all_to_all.16.parts_ref = f32[8,16,128]{2,1,0:T(8,128)S(1)} all-to-all(f32[8,16,128]{2,1,0:T(8,128)S(1)} %get-tuple-element.74), channel_id=1, replica_groups=mesh['row'=8,'col'=4] {'row'}, dimensions={0} | all-to-all | bytes 131072 | tf_op jit(solution)/shard_map/all_to_all | solution.py:23
  112.2 1.8 %shard_map.102 = (f32[32,128]{1,0:T(8,128)S(1)}, f32[1,128]{1,0:T(1,128)S(1)}) custom-call(f32[1024,4096]{1,0:T(8,128)S(1)} %get-tuple-element.51.rinv_ref, f32[8,16,128]{2,1,0:T(8,128)S(1)} %all_to_all.16.parts_ref), custom_call_target="tpu_custom_call" | custom-call | tf_op jit(solution)/shard_map/pallas_call | solution.py:468
  114.1 0.8 collective-permute-start.14
  114.9 1.1 collective-permute-start.15
  116.0 2.0 %collective-permute-done.14.refs_2_ = f32[32,128]{1,0:T(8,128)S(1)} collective-permute-done((f32[32,128]{1,0:T(8,128)S(1)}, f32[32,128]{1,0:T(8,128)S(1)}, u32[]{:S(2)}, u32[]{:S(2)}) %collective-permute-start.14) | collective-permute-done | bytes 16416 | tf_op jit(solution)/shard_map/ppermute | solution.py:29
  118.1 2.9 %shard_map.103 = (f32[4,128]{1,0:T(4,128)S(1)}, f32[32,128]{1,0:T(8,128)}, f32[8,128]{1,0:T(8,128)S(1)}, f32[1,128]{1,0:T(1,128)S(1)}) custom-call(f32[1024,4096]{1,0:T(8,128)S(1)} %get-tuple-element.51.rinv_ref, f32[512,1024]{1,0:T(8,128)S(1)} %copy-done, f32[32,128]{1,0:T(8,128)S(1)} %get-tuple-element.75.refs_0_, ...), custom_call_target="tpu_custom_call" | custom-call | tf_op jit(solution)/shard_map/pallas_call | solution.py:49
  121.2 1.0 collective-permute-done.16.refs_3_.refs_1_
  122.2 2.7 %collective-permute-done.19.refs_2_ = f32[1,4,128,128]{3,2,1,0:T(8,128)S(1)} collective-permute-done((f32[1,4,128,128]{3,2,1,0:T(8,128)S(1)}, f32[1,4,128,128]{3,2,1,0:T(8,128)S(1)}, u32[]{:S(2)}, u32[]{:S(2)}) %collective-permute-start.19) | collective-permute-done | bytes 262176 | tf_op jit(solution)/shard_map/ppermute | solution.py:420
  124.9 0.8 collective-permute-start.20
  125.7 2.7 %collective-permute-start.22 = (f32[128,256]{1,0:T(8,128)S(1)}, f32[128,256]{1,0:T(8,128)S(1)}, u32[]{:S(2)}, u32[]{:S(2)}) collective-permute-start(f32[128,256]{1,0:T(8,128)S(1)} %get-tuple-element.93), channel_id=1, source_target_pairs={{0,12},{4,8},{8,4},{12,0},{16,28},{20,24},{24,20},{28,16},{1,13},{... | collective-permute-start | bytes 393224 | tf_op jit(solution)/shard_map/ppermute | solution.py:420
  129.2 2.9 %collective-permute-done.17.refs_2_ = f32[4,128]{1,0:T(4,128)S(1)} collective-permute-done((f32[4,128]{1,0:T(4,128)S(1)}, f32[4,128]{1,0:T(4,128)S(1)}, u32[]{:S(2)}, u32[]{:S(2)}) %collective-permute-start.17) | collective-permute-done | bytes 2080 | tf_op jit(solution)/shard_map/ppermute | solution.py:29
  132.3 9.2 %all_to_all.17.parts_ref = f32[8,8,128]{2,1,0:T(8,128)S(1)} all-to-all(f32[8,8,128]{2,1,0:T(8,128)S(1)} %get-tuple-element.86), channel_id=1, replica_groups=mesh['row'=8,'col'=4] {'row'}, dimensions={0} | all-to-all | bytes 65536 | tf_op jit(solution)/shard_map/all_to_all | solution.py:23
  141.5 0.9 shard_map.106
  (42 shorter events, 3.3 us)
Async XLA Ops:
  0.6 75.4 %copy-start.1 = (bf16[256,256]{1,0:T(8,128)(2,1)S(1)}, bf16[256,256]{1,0:T(8,128)(2,1)}, u32[]{:S(2)}) copy-start(bf16[256,256]{1,0:T(8,128)(2,1)} %constant.2.clone.walsh_ref) | copy-start | bytes 393220
  0.6 83.3 %copy-start = (f32[512,1024]{1,0:T(8,128)S(1)}, f32[512,1024]{1,0:T(8,128)}, u32[]{:S(2)}) copy-start(f32[512,1024]{1,0:T(8,128)} %design_ref.9) | copy-start | bytes 6291460
  50.2 24.5 %copy-start.5 = (f32[512,128]{1,0:T(8,128)S(1)}, f32[512,128]{1,0:T(8,128)}, u32[]{:S(2)}) copy-start(f32[512,128]{1,0:T(8,128)} %get-tuple-element.69) | copy-start | bytes 786436
  50.2 24.7 %copy-start.4 = (f32[512,128]{1,0:T(8,128)S(1)}, f32[512,128]{1,0:T(8,128)}, u32[]{:S(2)}) copy-start(f32[512,128]{1,0:T(8,128)} %get-tuple-element.70) | copy-start | bytes 786436
  50.2 26.8 %copy-start.3 = (f32[512,128]{1,0:T(8,128)S(1)}, f32[512,128]{1,0:T(8,128)}, u32[]{:S(2)}) copy-start(f32[512,128]{1,0:T(8,128)} %get-tuple-element.71) | copy-start | bytes 786436
  65.0 12.0 %collective-permute-start.6 = (f32[512,128]{1,0:T(8,128)}, f32[512,128]{1,0:T(8,128)S(1)}, u32[]{:S(2)}, u32[]{:S(2)}) collective-permute-start(f32[512,128]{1,0:T(8,128)} %get-tuple-element.61), channel_id=1, source_target_pairs={{0,4},{4,0},{8,12},{12,8},{16,20},{20,16},{24,28},{28,24},{1,5},{5... | collective-permute-start | bytes 786440 | tf_op jit(solution)/shard_map/ppermute | solution.py:420
  65.2 14.0 %collective-permute-start.7 = (f32[512,128]{1,0:T(8,128)}, f32[512,128]{1,0:T(8,128)S(1)}, u32[]{:S(2)}, u32[]{:S(2)}) collective-permute-start(f32[512,128]{1,0:T(8,128)} %get-tuple-element.62), channel_id=1, source_target_pairs={{0,8},{4,12},{8,0},{12,4},{16,24},{20,28},{24,16},{28,20},{1,9},{5... | collective-permute-start | bytes 786440 | tf_op jit(solution)/shard_map/ppermute | solution.py:420
  66.3 17.6 %collective-permute-start.8 = (f32[512,128]{1,0:T(8,128)}, f32[512,128]{1,0:T(8,128)S(1)}, u32[]{:S(2)}, u32[]{:S(2)}) collective-permute-start(f32[512,128]{1,0:T(8,128)} %get-tuple-element.63), channel_id=1, source_target_pairs={{0,12},{4,8},{8,4},{12,0},{16,28},{20,24},{24,20},{28,16},{1,13},{... | collective-permute-start | bytes 786440 | tf_op jit(solution)/shard_map/ppermute | solution.py:420
  74.7 26.0 %copy-start.2 = (f32[512]{0:T(512)S(1)}, f32[512]{0:T(512)}, u32[]{:S(2)}) copy-start(f32[512]{0:T(512)} %param.11) | copy-start | bytes 6148
  74.7 21.7 %collective-permute-start.10 = (f32[512,128]{1,0:T(8,128)S(1)}, f32[512,128]{1,0:T(8,128)S(1)}, u32[]{:S(2)}, u32[]{:S(2)}) collective-permute-start(f32[512,128]{1,0:T(8,128)S(1)} %copy-done.5), channel_id=1, source_target_pairs={{0,4},{4,0},{8,12},{12,8},{16,20},{20,16},{24,28},{28,24},{1,5},{5... | collective-permute-start | bytes 786440 | tf_op jit(solution)/shard_map/ppermute | solution.py:420
  75.0 22.7 %collective-permute-start.11 = (f32[512,128]{1,0:T(8,128)S(1)}, f32[512,128]{1,0:T(8,128)S(1)}, u32[]{:S(2)}, u32[]{:S(2)}) collective-permute-start(f32[512,128]{1,0:T(8,128)S(1)} %copy-done.4), channel_id=1, source_target_pairs={{0,8},{4,12},{8,0},{12,4},{16,24},{20,28},{24,16},{28,20},{1,9},{5... | collective-permute-start | bytes 786440 | tf_op jit(solution)/shard_map/ppermute | solution.py:420
  77.0 21.0 %collective-permute-start.12 = (f32[512,128]{1,0:T(8,128)S(1)}, f32[512,128]{1,0:T(8,128)S(1)}, u32[]{:S(2)}, u32[]{:S(2)}) collective-permute-start(f32[512,128]{1,0:T(8,128)S(1)} %copy-done.3), channel_id=1, source_target_pairs={{0,12},{4,8},{8,4},{12,0},{16,28},{20,24},{24,20},{28,16},{1,13},{... | collective-permute-start | bytes 786440 | tf_op jit(solution)/shard_map/ppermute | solution.py:420
  85.5 13.7 %collective-permute-start.9 = (f32[1,4,128,128]{3,2,1,0:T(8,128)S(1)}, f32[1,4,128,128]{3,2,1,0:T(8,128)S(1)}, u32[]{:S(2)}, u32[]{:S(2)}) collective-permute-start(f32[1,4,128,128]{3,2,1,0:T(8,128)S(1)} %get-tuple-element.65), channel_id=1, source_target_pairs={{0,16},{4,20},{8,24},{12,28},{16,0},{20,4},{24,8},{28,12},{1,17},{... | collective-permute-start | bytes 786440 | tf_op jit(solution)/shard_map/ppermute | solution.py:420
  85.5 1.2 collective-permute-start
  86.6 3.7 %collective-permute-start.1 = (f32[32,128]{1,0:T(8,128)S(1)}, f32[32,128]{1,0:T(8,128)S(1)}, u32[]{:S(2)}, u32[]{:S(2)}) collective-permute-start(f32[32,128]{1,0:T(8,128)S(1)} %get-tuple-element.52.refs_0_), channel_id=1, source_target_pairs={{0,2},{1,3},{2,0},{3,1},{4,6},{5,7},{6,4},{7,5},{8,10},{9,11},{10,... | collective-permute-start | bytes 49160 | tf_op jit(solution)/shard_map/ppermute | solution.py:29
  90.4 3.3 %collective-permute-start.2 = (f32[32,128]{1,0:T(8,128)S(1)}, f32[32,128]{1,0:T(8,128)S(1)}, u32[]{:S(2)}, u32[]{:S(2)}) collective-permute-start(f32[32,128]{1,0:T(8,128)S(1)} %get-tuple-element.52.refs_0_), channel_id=1, source_target_pairs={{0,3},{1,2},{2,1},{3,0},{4,7},{5,6},{6,5},{7,4},{8,11},{9,10},{10,... | collective-permute-start | bytes 49160 | tf_op jit(solution)/shard_map/ppermute | solution.py:29
  96.1 3.1 %collective-permute-start.3 = (f32[4,128]{1,0:T(4,128)S(1)}, f32[4,128]{1,0:T(4,128)S(1)}, u32[]{:S(2)}, u32[]{:S(2)}) collective-permute-start(f32[4,128]{1,0:T(4,128)S(1)} %get-tuple-element.53.refs_0_), channel_id=1, source_target_pairs={{0,1},{1,0},{2,3},{3,2},{4,5},{5,4},{6,7},{7,6},{8,9},{9,8},{10,11... | collective-permute-start | bytes 6152 | tf_op jit(solution)/shard_map/ppermute | solution.py:29
  96.3 3.6 %collective-permute-start.4 = (f32[4,128]{1,0:T(4,128)S(1)}, f32[4,128]{1,0:T(4,128)S(1)}, u32[]{:S(2)}, u32[]{:S(2)}) collective-permute-start(f32[4,128]{1,0:T(4,128)S(1)} %get-tuple-element.53.refs_0_), channel_id=1, source_target_pairs={{0,2},{1,3},{2,0},{3,1},{4,6},{5,7},{6,4},{7,5},{8,10},{9,11},{10,... | collective-permute-start | bytes 6152 | tf_op jit(solution)/shard_map/ppermute | solution.py:29
  97.6 3.0 %collective-permute-start.5 = (f32[4,128]{1,0:T(4,128)S(1)}, f32[4,128]{1,0:T(4,128)S(1)}, u32[]{:S(2)}, u32[]{:S(2)}) collective-permute-start(f32[4,128]{1,0:T(4,128)S(1)} %get-tuple-element.53.refs_0_), channel_id=1, source_target_pairs={{0,3},{1,2},{2,1},{3,0},{4,7},{5,6},{6,5},{7,4},{8,11},{9,10},{10,... | collective-permute-start | bytes 6152 | tf_op jit(solution)/shard_map/ppermute | solution.py:29
  111.8 13.1 %collective-permute-start.19 = (f32[1,4,128,128]{3,2,1,0:T(8,128)S(1)}, f32[1,4,128,128]{3,2,1,0:T(8,128)S(1)}, u32[]{:S(2)}, u32[]{:S(2)}) collective-permute-start(f32[1,4,128,128]{3,2,1,0:T(8,128)S(1)} %get-tuple-element.84), channel_id=1, source_target_pairs={{0,16},{4,20},{8,24},{12,28},{16,0},{20,4},{24,8},{28,12},{1,17},{... | collective-permute-start | bytes 786440 | tf_op jit(solution)/shard_map/ppermute | solution.py:420
  114.1 1.9 %collective-permute-start.13 = (f32[32,128]{1,0:T(8,128)S(1)}, f32[32,128]{1,0:T(8,128)S(1)}, u32[]{:S(2)}, u32[]{:S(2)}) collective-permute-start(f32[32,128]{1,0:T(8,128)S(1)} %get-tuple-element.75.refs_0_), channel_id=1, source_target_pairs={{0,1},{1,0},{2,3},{3,2},{4,5},{5,4},{6,7},{7,6},{8,9},{9,8},{10,11... | collective-permute-start | bytes 49160 | tf_op jit(solution)/shard_map/ppermute | solution.py:29
  114.1 3.8 %collective-permute-start.14 = (f32[32,128]{1,0:T(8,128)S(1)}, f32[32,128]{1,0:T(8,128)S(1)}, u32[]{:S(2)}, u32[]{:S(2)}) collective-permute-start(f32[32,128]{1,0:T(8,128)S(1)} %get-tuple-element.75.refs_0_), channel_id=1, source_target_pairs={{0,2},{1,3},{2,0},{3,1},{4,6},{5,7},{6,4},{7,5},{8,10},{9,11},{10,... | collective-permute-start | bytes 49160 | tf_op jit(solution)/shard_map/ppermute | solution.py:29
  114.9 3.2 %collective-permute-start.15 = (f32[32,128]{1,0:T(8,128)S(1)}, f32[32,128]{1,0:T(8,128)S(1)}, u32[]{:S(2)}, u32[]{:S(2)}) collective-permute-start(f32[32,128]{1,0:T(8,128)S(1)} %get-tuple-element.75.refs_0_), channel_id=1, source_target_pairs={{0,3},{1,2},{2,1},{3,0},{4,7},{5,6},{6,5},{7,4},{8,11},{9,10},{10,... | collective-permute-start | bytes 49160 | tf_op jit(solution)/shard_map/ppermute | solution.py:29
  121.1 1.2 collective-permute-start.16
  124.9 16.5 %collective-permute-start.20 = (f32[128,256]{1,0:T(8,128)S(1)}, f32[128,256]{1,0:T(8,128)S(1)}, u32[]{:S(2)}, u32[]{:S(2)}) collective-permute-start(f32[128,256]{1,0:T(8,128)S(1)} %get-tuple-element.91), channel_id=1, source_target_pairs={{0,4},{4,0},{8,12},{12,8},{16,20},{20,16},{24,28},{28,24},{1,5},{5... | collective-permute-start | bytes 393224 | tf_op jit(solution)/shard_map/ppermute | solution.py:420
  125.7 15.7 %collective-permute-start.21 = (f32[128,256]{1,0:T(8,128)S(1)}, f32[128,256]{1,0:T(8,128)S(1)}, u32[]{:S(2)}, u32[]{:S(2)}) collective-permute-start(f32[128,256]{1,0:T(8,128)S(1)} %get-tuple-element.92), channel_id=1, source_target_pairs={{0,8},{4,12},{8,0},{12,4},{16,24},{20,28},{24,16},{28,20},{1,9},{5... | collective-permute-start | bytes 393224 | tf_op jit(solution)/shard_map/ppermute | solution.py:420
  125.7 15.7 %collective-permute-start.22 = (f32[128,256]{1,0:T(8,128)S(1)}, f32[128,256]{1,0:T(8,128)S(1)}, u32[]{:S(2)}, u32[]{:S(2)}) collective-permute-start(f32[128,256]{1,0:T(8,128)S(1)} %get-tuple-element.93), channel_id=1, source_target_pairs={{0,12},{4,8},{8,4},{12,0},{16,28},{20,24},{24,20},{28,16},{1,13},{... | collective-permute-start | bytes 393224 | tf_op jit(solution)/shard_map/ppermute | solution.py:420
  128.5 3.6 %collective-permute-start.17 = (f32[4,128]{1,0:T(4,128)S(1)}, f32[4,128]{1,0:T(4,128)S(1)}, u32[]{:S(2)}, u32[]{:S(2)}) collective-permute-start(f32[4,128]{1,0:T(4,128)S(1)} %get-tuple-element.78.refs_0_), channel_id=1, source_target_pairs={{0,2},{1,3},{2,0},{3,1},{4,6},{5,7},{6,4},{7,5},{8,10},{9,11},{10,... | collective-permute-start | bytes 6152 | tf_op jit(solution)/shard_map/ppermute | solution.py:29
  129.2 3.0 %collective-permute-start.18 = (f32[4,128]{1,0:T(4,128)S(1)}, f32[4,128]{1,0:T(4,128)S(1)}, u32[]{:S(2)}, u32[]{:S(2)}) collective-permute-start(f32[4,128]{1,0:T(4,128)S(1)} %get-tuple-element.78.refs_0_), channel_id=1, source_target_pairs={{0,3},{1,2},{2,1},{3,0},{4,7},{5,6},{6,5},{7,4},{8,11},{9,10},{10,... | collective-permute-start | bytes 6152 | tf_op jit(solution)/shard_map/ppermute | solution.py:29

commit v7 on v6

--- a/solution.py
+++ b/solution.py
@@ -23,11 +23,15 @@
     return lax.all_to_all(copies, axis, split_axis=0, concat_axis=0, tiled=True)
 
 
-def direct(array, axis):
+def paired(array, axis):
     size = lax.axis_size(axis)
-    return [array] + [
-        lax.ppermute(array, axis, [(i, i ^ mask) for i in range(size)]) for mask in range(1, size)
-    ]
+    mask = 1
+    while True:
+        come = lax.ppermute(array, axis, [(i, i ^ mask) for i in range(size)])
+        mask *= 2
+        if mask == size:
+            return [array, come]
+        array = array + come
 
 
 def tree(values):
@@ -164,9 +168,9 @@
         chunk, mask = index // (NEAR - 1), index % (NEAR - 1) + 1
         piece = away_ref.shape[1]
         column = pl.multiple_of((place ^ mask) * quarter + chunk * piece, LANE)
-        source = design_ref.at[:, pl.ds(column, piece)]
+        source = design.at[:, pl.ds(column, piece)]
         away.append(pltpu.make_async_copy(source, away_ref, sems.at[4 + lines + index]))
-    for copy in small + large + away:
+    for copy in small + large:
         copy.start()
     for copy in small:
         copy.wait()
@@ -187,6 +191,9 @@
     for line, part in enumerate(parts):
         weight = across(target[line : line + 1, :])
         large[line].wait()
+        if line == lines - 1:
+            for copy in away:
+                copy.start()
         for tile in range(tiles):
             sums[tile] = sums[tile] + fold_rows(design[part, tile * LANE : (tile + 1) * LANE] * weight)
     for tile in range(tiles):
@@ -388,7 +395,7 @@
 def shards(design, sign_bits, picks, counts, target, rinv):
     rows, width = design.shape
     whole = rinv.shape[1]
-    row_groups, col_groups = lax.axis_size("row"), lax.axis_size("col")
+    row_groups = lax.axis_size("row")
     lines = rows // LANE
     scalar = shape(1, LANE)
     deep = message_rows(width)
@@ -476,7 +483,7 @@
 
     def forward(terms, *before):
         return call(
-            functools.partial(forward_body, col_groups, not before),
+            functools.partial(forward_body, 2, not before),
             (shape(lines, LANE), shape(whole // LANE, LANE), shape(width // LANE, LANE), scalar),
             here,
             design,
@@ -486,7 +493,7 @@
 
     def turn(images, left, beta, alpha, token, last):
         return call(
-            functools.partial(turn_body, col_groups, last),
+            functools.partial(turn_body, 2, last),
             (shape(lines, LANE), shape(row_groups, 8 if last else deep, LANE)),
             *images,
             left,
@@ -513,7 +520,7 @@
         else:
             term, beta = back(here, message, False)
         betas.append(beta)
-        terms = direct(term, "col")
+        terms = paired(term, "col")
         image, right, kept, alpha = forward(terms, *(() if step == 0 else (right, beta)))
         alphas.append(alpha)
         held.append(kept)
@@ -526,7 +533,7 @@
             for part in parts:
                 part, token = join(*part, token)
                 joined.append(part)
-        images = direct(image, "col")
+        images = paired(image, "col")
         if last:
             quarters, token = trade(joined, keep, come, images[1])
         left, message = turn(images, left, beta, alpha, token, last)

time: 143 us -> 93.5 us (0.65)
  Pallas kernels: 67.7 us -> 21.8 us
  waiting for transfers between devices: 21.5 us -> 17.2 us
    pallas_call x1, Pallas kernels: 49.5 us -> 3.63 us  [shards(): pl.pallas_call(first_body, out_shape=(shape(row_groups, signs_at(width, r...]
    ppermute x11, waiting for transfers between devices: 7.35 us -> 5.07 us  [swap(): lax.ppermute(array, 'row', [(i, i ^ mask) for i in range(row_groups)])]
    ppermute x12 -> x8, waiting for transfers between devices: 14.2 us -> 12.2 us  [paired(): come = lax.ppermute(array, axis, [(i, i ^ mask) for i in range(size)])]
    ppermute x12 -> x8, starting transfers between devices: 6.29 us -> 6.1 us  [paired(): come = lax.ppermute(array, axis, [(i, i ^ mask) for i in range(size)])]
  transfers between devices with their start and end apart: 23 -> 19, of which waited for: 12 -> 9; matrix products, arithmetic and copies ran while one was open for 0% -> 0% of each run, Pallas kernels for 12% -> 18%
where the time goes in v7:
time: 93.5 us; the launch traced here: 93.1 us
  blocking collectives  36 us (39%)
  Pallas kernels  21.8 us (23%)
  starting transfers between devices  17.2 us (18%)
  waiting for transfers between devices  17.2 us (18%)
    all_to_all x3, blocking collectives, exchange(): return lax.all_to_all(copies, axis, split_axis=0, concat_axis=0, tiled=True)  36 us
    ppermute x8, waiting for transfers between devices, paired(): come = lax.ppermute(array, axis, [(i, i ^ mask) for i in range(size)])  12.2 us
    ppermute x11, starting transfers between devices, swap(): lax.ppermute(array, 'row', [(i, i ^ mask) for i in range(row_groups)])  11.1 us
    pallas_call x10, Pallas kernels, call(): pl.pallas_call(body, out_shape=out_shape, in_specs=[VMEM] * len(operands)...  10.2 us
    pallas_call x2, Pallas kernels, back(): pl.pallas_call(functools.partial(back_body, first), out_shape=outs, in_sp...  7.97 us
    ppermute x8, starting transfers between devices, paired(): come = lax.ppermute(array, axis, [(i, i ^ mask) for i in range(size)])  6.1 us
    ppermute x11, waiting for transfers between devices, swap(): lax.ppermute(array, 'row', [(i, i ^ mask) for i in range(row_groups)])  5.07 us
    pallas_call x1, Pallas kernels, shards(): pl.pallas_call(first_body, out_shape=(shape(row_groups, signs_at(width, r...  3.63 us
  transfers between devices with their start and end apart: 19, of which 9 were waited for; matrix products, arithmetic and copies ran while one was open for 0% of the time, Pallas kernels for 18%

profile of v7, /device:TPU:0, one launch (start us, length us, event | category | flops | bytes accessed | tf_op | source)
XLA Modules:
  0.0 93.1 jit_solution(15339367669218803378)
XLA Ops:
  0.7 3.6 %shard_map.94 = (f32[8,32,128]{2,1,0:T(8,128)}, f32[512,128]{1,0:T(8,128)}, f32[512,128]{1,0:T(8,128)}, f32[512,128]{1,0:T(8,128)}, f32[512,128]{1,0:T(8,128)}, /*index=5*/f32[512,128]{1,0:T(8,128)}, f32[512,128]{1,0:T(8,128)}) custom-call(f32[512,1024]{1,0:T(8,128)} %design_ref.9, f32[4,128]{1,0:T(4,128)} %bitcast.6, s32[4,128]{1,0:T(4,128)} %bitcast.9, ...), custom_call_target="tpu_custom_call" | custom-call | tf_op jit(solution)/shard_map/pallas_call | solution.py:409
  4.3 14.8 %all_to_all.15.parts_ref = f32[8,32,128]{2,1,0:T(8,128)S(1)} all-to-all(f32[8,32,128]{2,1,0:T(8,128)} %get-tuple-element.50), channel_id=1, replica_groups=mesh['row'=8,'col'=4] {'row'}, dimensions={0} | all-to-all | bytes 262144 | tf_op jit(solution)/shard_map/all_to_all | solution.py:23
  19.3 1.1 %collective-permute-start.5 = (f32[512,128]{1,0:T(8,128)}, f32[512,128]{1,0:T(8,128)S(1)}, u32[]{:S(2)}, u32[]{:S(2)}) collective-permute-start(f32[512,128]{1,0:T(8,128)} %get-tuple-element.62), channel_id=1, source_target_pairs={{0,8},{4,12},{8,0},{12,4},{16,24},{20,28},{24,16},{28,20},{1,9},{5... | collective-permute-start | bytes 786440 | tf_op jit(solution)/shard_map/ppermute | solution.py:427
  20.4 2.2 %collective-permute-start.6 = (f32[512,128]{1,0:T(8,128)}, f32[512,128]{1,0:T(8,128)S(1)}, u32[]{:S(2)}, u32[]{:S(2)}) collective-permute-start(f32[512,128]{1,0:T(8,128)} %get-tuple-element.63), channel_id=1, source_target_pairs={{0,12},{4,8},{8,4},{12,0},{16,28},{20,24},{24,20},{28,16},{1,13},{... | collective-permute-start | bytes 786440 | tf_op jit(solution)/shard_map/ppermute | solution.py:427
  22.6 6.2 %shard_map.95 = (f32[32,128]{1,0:T(8,128)S(1)}, f32[1,128]{1,0:T(1,128)S(1)}, f32[1024,4096]{1,0:T(8,128)S(1)}) custom-call(f32[1024,4096]{1,0:T(8,128)} %rinv_ref.1, f32[8,32,128]{2,1,0:T(8,128)S(1)} %all_to_all.15.parts_ref), custom_call_target="tpu_custom_call" | custom-call | tf_op jit(solution)/shard_map/pallas_call | solution.py:475
  28.8 0.8 collective-permute-start.10
  29.6 0.7 collective-permute-start.8
  30.3 0.9 shard_map.97
  31.3 2.1 %collective-permute-start.9 = (f32[512,128]{1,0:T(8,128)S(1)}, f32[512,128]{1,0:T(8,128)S(1)}, u32[]{:S(2)}, u32[]{:S(2)}) collective-permute-start(f32[512,128]{1,0:T(8,128)S(1)} %copy-done.3), channel_id=1, source_target_pairs={{0,8},{4,12},{8,0},{12,4},{16,24},{20,28},{24,16},{28,20},{1,9},{5... | collective-permute-start | bytes 786440 | tf_op jit(solution)/shard_map/ppermute | solution.py:427
  33.3 5.0 %collective-permute-done.6.refs_2_ = f32[512,128]{1,0:T(8,128)S(1)} collective-permute-done((f32[512,128]{1,0:T(8,128)}, f32[512,128]{1,0:T(8,128)S(1)}, u32[]{:S(2)}, u32[]{:S(2)}) %collective-permute-start.6) | collective-permute-done | bytes 262176 | tf_op jit(solution)/shard_map/ppermute | solution.py:427
  38.4 1.5 %shard_map.98 = (f32[1,4,128,128]{3,2,1,0:T(8,128)S(1)}, f32[1,4,128,128]{3,2,1,0:T(8,128)S(1)}, f32[1,128]{1,0:T(1,128)}) custom-call(f32[512,1024]{1,0:T(8,128)S(1)} %copy-done, f32[8,32,128]{2,1,0:T(8,128)S(1)} %all_to_all.15.parts_ref, bf16[8,128,512]{2,1,0:T(8,128)(2,1)S(1)} %get-tuple-element.56.mix_ref, f32[1,128]{1,0:T(1,128)S(1)} %get-tuple-element.57.order_ref, ...), custom_call_target="tpu_custom_call" | custom-call | tf_op jit(solution)/shard_map/pallas_call | solution.py:53
  40.0 1.2 %collective-permute-done = f32[32,128]{1,0:T(8,128)S(1)} collective-permute-done((f32[32,128]{1,0:T(8,128)S(1)}, f32[32,128]{1,0:T(8,128)S(1)}, u32[]{:S(2)}, u32[]{:S(2)}) %collective-permute-start) | collective-permute-done | bytes 16416 | tf_op jit(solution)/shard_map/ppermute | solution.py:30
  41.1 1.5 %collective-permute-start.1 = (f32[32,128]{1,0:T(8,128)S(1)}, f32[32,128]{1,0:T(8,128)S(1)}, u32[]{:S(2)}, u32[]{:S(2)}) collective-permute-start(f32[32,128]{1,0:T(8,128)S(1)} %add.12.refs_0_), channel_id=1, source_target_pairs={{0,2},{1,3},{2,0},{3,1},{4,6},{5,7},{6,4},{7,5},{8,10},{9,11},{10,... | collective-permute-start | bytes 49160 | tf_op jit(solution)/shard_map/ppermute | solution.py:30
  42.6 2.2 %collective-permute-done.1.refs_1_ = f32[32,128]{1,0:T(8,128)S(1)} collective-permute-done((f32[32,128]{1,0:T(8,128)S(1)}, f32[32,128]{1,0:T(8,128)S(1)}, u32[]{:S(2)}, u32[]{:S(2)}) %collective-permute-start.1) | collective-permute-done | bytes 16416 | tf_op jit(solution)/shard_map/ppermute | solution.py:30
  44.9 2.4 %shard_map.96 = (f32[4,128]{1,0:T(4,128)S(1)}, f32[32,128]{1,0:T(8,128)S(1)}, f32[8,128]{1,0:T(8,128)S(1)}, f32[1,128]{1,0:T(1,128)S(1)}) custom-call(f32[1024,4096]{1,0:T(8,128)S(1)} %get-tuple-element.51.rinv_ref, f32[512,1024]{1,0:T(8,128)S(1)} %copy-done, f32[32,128]{1,0:T(8,128)S(1)} %add.12.refs_0_, f32[32,128]{1,0:T(8,128)S(1)} %collective-permute-done.1.refs_1_), custom_call_target="tpu_custom_call" | custom-call | tf_op jit(solution)/shard_map/pallas_call | solution.py:53
  47.4 1.1 %collective-permute-done.2 = f32[4,128]{1,0:T(4,128)S(1)} collective-permute-done((f32[4,128]{1,0:T(4,128)S(1)}, f32[4,128]{1,0:T(4,128)S(1)}, u32[]{:S(2)}, u32[]{:S(2)}) %collective-permute-start.2) | collective-permute-done | bytes 2080 | tf_op jit(solution)/shard_map/ppermute | solution.py:30
  48.5 1.5 %collective-permute-start.3 = (f32[4,128]{1,0:T(4,128)S(1)}, f32[4,128]{1,0:T(4,128)S(1)}, u32[]{:S(2)}, u32[]{:S(2)}) collective-permute-start(f32[4,128]{1,0:T(4,128)S(1)} %add.13.refs_0_), channel_id=1, source_target_pairs={{0,2},{1,3},{2,0},{3,1},{4,6},{5,7},{6,4},{7,5},{8,10},{9,11},{10,... | collective-permute-start | bytes 6152 | tf_op jit(solution)/shard_map/ppermute | solution.py:30
  50.0 1.1 %shard_map.99 = (f32[1,4,128,128]{3,2,1,0:T(8,128)S(1)}, f32[1,4,128,128]{3,2,1,0:T(8,128)S(1)}, f32[1,128]{1,0:T(1,128)S(1)}) custom-call(f32[512,1024]{1,0:T(8,128)S(1)} %copy-done, f32[8,32,128]{2,1,0:T(8,128)S(1)} %all_to_all.15.parts_ref, bf16[8,128,512]{2,1,0:T(8,128)(2,1)S(1)} %get-tuple-element.56.mix_ref, ...), custom_call_target="tpu_custom_call" | custom-call | tf_op jit(solution)/shard_map/pallas_call | solution.py:53
  51.2 0.9 collective-permute-done.3.refs_1_
  52.3 10.9 %all_to_all.16.parts_ref = f32[8,16,128]{2,1,0:T(8,128)S(1)} all-to-all(f32[8,16,128]{2,1,0:T(8,128)S(1)} %get-tuple-element.74), channel_id=1, replica_groups=mesh['row'=8,'col'=4] {'row'}, dimensions={0} | all-to-all | bytes 131072 | tf_op jit(solution)/shard_map/all_to_all | solution.py:23
  63.7 1.8 %shard_map.102 = (f32[32,128]{1,0:T(8,128)S(1)}, f32[1,128]{1,0:T(1,128)S(1)}) custom-call(f32[1024,4096]{1,0:T(8,128)S(1)} %get-tuple-element.51.rinv_ref, f32[8,16,128]{2,1,0:T(8,128)S(1)} %all_to_all.16.parts_ref), custom_call_target="tpu_custom_call" | custom-call | tf_op jit(solution)/shard_map/pallas_call | solution.py:475
  65.6 1.2 %collective-permute-done.11 = f32[32,128]{1,0:T(8,128)S(1)} collective-permute-done((f32[32,128]{1,0:T(8,128)S(1)}, f32[32,128]{1,0:T(8,128)S(1)}, u32[]{:S(2)}, u32[]{:S(2)}) %collective-permute-start.11) | collective-permute-done | bytes 16416 | tf_op jit(solution)/shard_map/ppermute | solution.py:30
  66.8 1.5 %collective-permute-start.12 = (f32[32,128]{1,0:T(8,128)S(1)}, f32[32,128]{1,0:T(8,128)S(1)}, u32[]{:S(2)}, u32[]{:S(2)}) collective-permute-start(f32[32,128]{1,0:T(8,128)S(1)} %add.14.refs_0_), channel_id=1, source_target_pairs={{0,2},{1,3},{2,0},{3,1},{4,6},{5,7},{6,4},{7,5},{8,10},{9,11},{10,... | collective-permute-start | bytes 49160 | tf_op jit(solution)/shard_map/ppermute | solution.py:30
  68.3 2.2 %collective-permute-done.12.refs_1_ = f32[32,128]{1,0:T(8,128)S(1)} collective-permute-done((f32[32,128]{1,0:T(8,128)S(1)}, f32[32,128]{1,0:T(8,128)S(1)}, u32[]{:S(2)}, u32[]{:S(2)}) %collective-permute-start.12) | collective-permute-done | bytes 16416 | tf_op jit(solution)/shard_map/ppermute | solution.py:30
  70.5 2.9 %shard_map.103 = (f32[4,128]{1,0:T(4,128)S(1)}, f32[32,128]{1,0:T(8,128)}, f32[8,128]{1,0:T(8,128)S(1)}, f32[1,128]{1,0:T(1,128)S(1)}) custom-call(f32[1024,4096]{1,0:T(8,128)S(1)} %get-tuple-element.51.rinv_ref, f32[512,1024]{1,0:T(8,128)S(1)} %copy-done, f32[32,128]{1,0:T(8,128)S(1)} %add.14.refs_0_, f32[32,128]{1,0:T(8,128)S(1)} %collective-permute-done.12.refs_1_, ...), custom_call_target="tpu_custom_call" | custom-call | tf_op jit(solution)/shard_map/pallas_call | solution.py:53
  73.5 1.2 %collective-permute-done.13 = f32[4,128]{1,0:T(4,128)S(1)} collective-permute-done((f32[4,128]{1,0:T(4,128)S(1)}, f32[4,128]{1,0:T(4,128)S(1)}, u32[]{:S(2)}, u32[]{:S(2)}) %collective-permute-start.13) | collective-permute-done | bytes 2080 | tf_op jit(solution)/shard_map/ppermute | solution.py:30
  74.6 1.5 %collective-permute-start.14 = (f32[4,128]{1,0:T(4,128)S(1)}, f32[4,128]{1,0:T(4,128)S(1)}, u32[]{:S(2)}, u32[]{:S(2)}) collective-permute-start(f32[4,128]{1,0:T(4,128)S(1)} %add.15.refs_0_), channel_id=1, source_target_pairs={{0,2},{1,3},{2,0},{3,1},{4,6},{5,7},{6,4},{7,5},{8,10},{9,11},{10,... | collective-permute-start | bytes 6152 | tf_op jit(solution)/shard_map/ppermute | solution.py:30
  76.1 2.1 %collective-permute-done.14.refs_3_.refs_1_ = f32[4,128]{1,0:T(4,128)S(1)} collective-permute-done((f32[4,128]{1,0:T(4,128)S(1)}, f32[4,128]{1,0:T(4,128)S(1)}, u32[]{:S(2)}, u32[]{:S(2)}) %collective-permute-start.14) | collective-permute-done | bytes 2080 | tf_op jit(solution)/shard_map/ppermute | solution.py:30
  78.7 1.1 %collective-permute-start.17 = (f32[128,256]{1,0:T(8,128)S(1)}, f32[128,256]{1,0:T(8,128)S(1)}, u32[]{:S(2)}, u32[]{:S(2)}) collective-permute-start(f32[128,256]{1,0:T(8,128)S(1)} %get-tuple-element.92), channel_id=1, source_target_pairs={{0,8},{4,12},{8,0},{12,4},{16,24},{20,28},{24,16},{28,20},{1,9},{5... | collective-permute-start | bytes 393224 | tf_op jit(solution)/shard_map/ppermute | solution.py:427
  79.8 2.0 %collective-permute-start.18 = (f32[128,256]{1,0:T(8,128)S(1)}, f32[128,256]{1,0:T(8,128)S(1)}, u32[]{:S(2)}, u32[]{:S(2)}) collective-permute-start(f32[128,256]{1,0:T(8,128)S(1)} %get-tuple-element.93), channel_id=1, source_target_pairs={{0,12},{4,8},{8,4},{12,0},{16,28},{20,24},{24,20},{28,16},{1,13},{... | collective-permute-start | bytes 393224 | tf_op jit(solution)/shard_map/ppermute | solution.py:427
  81.9 10.3 %all_to_all.17.parts_ref = f32[8,8,128]{2,1,0:T(8,128)S(1)} all-to-all(f32[8,8,128]{2,1,0:T(8,128)S(1)} %get-tuple-element.86), channel_id=1, replica_groups=mesh['row'=8,'col'=4] {'row'}, dimensions={0} | all-to-all | bytes 65536 | tf_op jit(solution)/shard_map/all_to_all | solution.py:23
  92.2 0.9 shard_map.106
  (38 shorter events, 1.8 us)
Async XLA Ops:
  0.6 29.7 %copy-start.1 = (bf16[256,256]{1,0:T(8,128)(2,1)S(1)}, bf16[256,256]{1,0:T(8,128)(2,1)}, u32[]{:S(2)}) copy-start(bf16[256,256]{1,0:T(8,128)(2,1)} %constant.2.clone.walsh_ref) | copy-start | bytes 393220
  0.6 37.8 %copy-start = (f32[512,1024]{1,0:T(8,128)S(1)}, f32[512,1024]{1,0:T(8,128)}, u32[]{:S(2)}) copy-start(f32[512,1024]{1,0:T(8,128)} %design_ref.9) | copy-start | bytes 6291460
  4.3 24.5 %copy-start.5 = (f32[512,128]{1,0:T(8,128)S(1)}, f32[512,128]{1,0:T(8,128)}, u32[]{:S(2)}) copy-start(f32[512,128]{1,0:T(8,128)} %get-tuple-element.71) | copy-start | bytes 786436
  4.3 25.3 %copy-start.4 = (f32[512,128]{1,0:T(8,128)S(1)}, f32[512,128]{1,0:T(8,128)}, u32[]{:S(2)}) copy-start(f32[512,128]{1,0:T(8,128)} %get-tuple-element.69) | copy-start | bytes 786436
  4.3 26.9 %copy-start.3 = (f32[512,128]{1,0:T(8,128)S(1)}, f32[512,128]{1,0:T(8,128)}, u32[]{:S(2)}) copy-start(f32[512,128]{1,0:T(8,128)} %get-tuple-element.70) | copy-start | bytes 786436
  19.1 12.1 %collective-permute-start.4 = (f32[512,128]{1,0:T(8,128)}, f32[512,128]{1,0:T(8,128)S(1)}, u32[]{:S(2)}, u32[]{:S(2)}) collective-permute-start(f32[512,128]{1,0:T(8,128)} %get-tuple-element.61), channel_id=1, source_target_pairs={{0,4},{4,0},{8,12},{12,8},{16,20},{20,16},{24,28},{28,24},{1,5},{5... | collective-permute-start | bytes 786440 | tf_op jit(solution)/shard_map/ppermute | solution.py:427
  19.3 14.0 %collective-permute-start.5 = (f32[512,128]{1,0:T(8,128)}, f32[512,128]{1,0:T(8,128)S(1)}, u32[]{:S(2)}, u32[]{:S(2)}) collective-permute-start(f32[512,128]{1,0:T(8,128)} %get-tuple-element.62), channel_id=1, source_target_pairs={{0,8},{4,12},{8,0},{12,4},{16,24},{20,28},{24,16},{28,20},{1,9},{5... | collective-permute-start | bytes 786440 | tf_op jit(solution)/shard_map/ppermute | solution.py:427
  20.4 18.0 %collective-permute-start.6 = (f32[512,128]{1,0:T(8,128)}, f32[512,128]{1,0:T(8,128)S(1)}, u32[]{:S(2)}, u32[]{:S(2)}) collective-permute-start(f32[512,128]{1,0:T(8,128)} %get-tuple-element.63), channel_id=1, source_target_pairs={{0,12},{4,8},{8,4},{12,0},{16,28},{20,24},{24,20},{28,16},{1,13},{... | collective-permute-start | bytes 786440 | tf_op jit(solution)/shard_map/ppermute | solution.py:427
  28.8 23.4 %copy-start.2 = (f32[512]{0:T(512)S(1)}, f32[512]{0:T(512)}, u32[]{:S(2)}) copy-start(f32[512]{0:T(512)} %param.11) | copy-start | bytes 6148
  28.8 21.2 %collective-permute-start.10 = (f32[512,128]{1,0:T(8,128)S(1)}, f32[512,128]{1,0:T(8,128)S(1)}, u32[]{:S(2)}, u32[]{:S(2)}) collective-permute-start(f32[512,128]{1,0:T(8,128)S(1)} %copy-done.5), channel_id=1, source_target_pairs={{0,12},{4,8},{8,4},{12,0},{16,28},{20,24},{24,20},{28,16},{1,13},{... | collective-permute-start | bytes 786440 | tf_op jit(solution)/shard_map/ppermute | solution.py:427
  29.6 20.4 %collective-permute-start.8 = (f32[512,128]{1,0:T(8,128)S(1)}, f32[512,128]{1,0:T(8,128)S(1)}, u32[]{:S(2)}, u32[]{:S(2)}) collective-permute-start(f32[512,128]{1,0:T(8,128)S(1)} %copy-done.4), channel_id=1, source_target_pairs={{0,4},{4,0},{8,12},{12,8},{16,20},{20,16},{24,28},{28,24},{1,5},{5... | collective-permute-start | bytes 786440 | tf_op jit(solution)/shard_map/ppermute | solution.py:427
  31.3 18.8 %collective-permute-start.9 = (f32[512,128]{1,0:T(8,128)S(1)}, f32[512,128]{1,0:T(8,128)S(1)}, u32[]{:S(2)}, u32[]{:S(2)}) collective-permute-start(f32[512,128]{1,0:T(8,128)S(1)} %copy-done.3), channel_id=1, source_target_pairs={{0,8},{4,12},{8,0},{12,4},{16,24},{20,28},{24,16},{28,20},{1,9},{5... | collective-permute-start | bytes 786440 | tf_op jit(solution)/shard_map/ppermute | solution.py:427
  39.9 11.2 %collective-permute-start.7 = (f32[1,4,128,128]{3,2,1,0:T(8,128)S(1)}, f32[1,4,128,128]{3,2,1,0:T(8,128)S(1)}, u32[]{:S(2)}, u32[]{:S(2)}) collective-permute-start(f32[1,4,128,128]{3,2,1,0:T(8,128)S(1)} %get-tuple-element.65), channel_id=1, source_target_pairs={{0,16},{4,20},{8,24},{12,28},{16,0},{20,4},{24,8},{28,12},{1,17},{... | collective-permute-start | bytes 786440 | tf_op jit(solution)/shard_map/ppermute | solution.py:427
  40.0 1.2 %collective-permute-start = (f32[32,128]{1,0:T(8,128)S(1)}, f32[32,128]{1,0:T(8,128)S(1)}, u32[]{:S(2)}, u32[]{:S(2)}) collective-permute-start(f32[32,128]{1,0:T(8,128)S(1)} %get-tuple-element.52), channel_id=1, source_target_pairs={{0,1},{1,0},{2,3},{3,2},{4,5},{5,4},{6,7},{7,6},{8,9},{9,8},{10,11... | collective-permute-start | bytes 49160 | tf_op jit(solution)/shard_map/ppermute | solution.py:30
  41.1 3.7 %collective-permute-start.1 = (f32[32,128]{1,0:T(8,128)S(1)}, f32[32,128]{1,0:T(8,128)S(1)}, u32[]{:S(2)}, u32[]{:S(2)}) collective-permute-start(f32[32,128]{1,0:T(8,128)S(1)} %add.12.refs_0_), channel_id=1, source_target_pairs={{0,2},{1,3},{2,0},{3,1},{4,6},{5,7},{6,4},{7,5},{8,10},{9,11},{10,... | collective-permute-start | bytes 49160 | tf_op jit(solution)/shard_map/ppermute | solution.py:30
  47.3 1.2 %collective-permute-start.2 = (f32[4,128]{1,0:T(4,128)S(1)}, f32[4,128]{1,0:T(4,128)S(1)}, u32[]{:S(2)}, u32[]{:S(2)}) collective-permute-start(f32[4,128]{1,0:T(4,128)S(1)} %get-tuple-element.53), channel_id=1, source_target_pairs={{0,1},{1,0},{2,3},{3,2},{4,5},{5,4},{6,7},{7,6},{8,9},{9,8},{10,11... | collective-permute-start | bytes 6152 | tf_op jit(solution)/shard_map/ppermute | solution.py:30
  48.5 3.6 %collective-permute-start.3 = (f32[4,128]{1,0:T(4,128)S(1)}, f32[4,128]{1,0:T(4,128)S(1)}, u32[]{:S(2)}, u32[]{:S(2)}) collective-permute-start(f32[4,128]{1,0:T(4,128)S(1)} %add.13.refs_0_), channel_id=1, source_target_pairs={{0,2},{1,3},{2,0},{3,1},{4,6},{5,7},{6,4},{7,5},{8,10},{9,11},{10,... | collective-permute-start | bytes 6152 | tf_op jit(solution)/shard_map/ppermute | solution.py:30
  63.2 15.0 %collective-permute-start.15 = (f32[1,4,128,128]{3,2,1,0:T(8,128)S(1)}, f32[1,4,128,128]{3,2,1,0:T(8,128)S(1)}, u32[]{:S(2)}, u32[]{:S(2)}) collective-permute-start(f32[1,4,128,128]{3,2,1,0:T(8,128)S(1)} %get-tuple-element.84), channel_id=1, source_target_pairs={{0,16},{4,20},{8,24},{12,28},{16,0},{20,4},{24,8},{28,12},{1,17},{... | collective-permute-start | bytes 786440 | tf_op jit(solution)/shard_map/ppermute | solution.py:427
  65.5 1.2 %collective-permute-start.11 = (f32[32,128]{1,0:T(8,128)S(1)}, f32[32,128]{1,0:T(8,128)S(1)}, u32[]{:S(2)}, u32[]{:S(2)}) collective-permute-start(f32[32,128]{1,0:T(8,128)S(1)} %get-tuple-element.75), channel_id=1, source_target_pairs={{0,1},{1,0},{2,3},{3,2},{4,5},{5,4},{6,7},{7,6},{8,9},{9,8},{10,11... | collective-permute-start | bytes 49160 | tf_op jit(solution)/shard_map/ppermute | solution.py:30
  66.8 3.7 %collective-permute-start.12 = (f32[32,128]{1,0:T(8,128)S(1)}, f32[32,128]{1,0:T(8,128)S(1)}, u32[]{:S(2)}, u32[]{:S(2)}) collective-permute-start(f32[32,128]{1,0:T(8,128)S(1)} %add.14.refs_0_), channel_id=1, source_target_pairs={{0,2},{1,3},{2,0},{3,1},{4,6},{5,7},{6,4},{7,5},{8,10},{9,11},{10,... | collective-permute-start | bytes 49160 | tf_op jit(solution)/shard_map/ppermute | solution.py:30
  73.5 1.2 %collective-permute-start.13 = (f32[4,128]{1,0:T(4,128)S(1)}, f32[4,128]{1,0:T(4,128)S(1)}, u32[]{:S(2)}, u32[]{:S(2)}) collective-permute-start(f32[4,128]{1,0:T(4,128)S(1)} %get-tuple-element.78), channel_id=1, source_target_pairs={{0,1},{1,0},{2,3},{3,2},{4,5},{5,4},{6,7},{7,6},{8,9},{9,8},{10,11... | collective-permute-start | bytes 6152 | tf_op jit(solution)/shard_map/ppermute | solution.py:30
  74.6 3.6 %collective-permute-start.14 = (f32[4,128]{1,0:T(4,128)S(1)}, f32[4,128]{1,0:T(4,128)S(1)}, u32[]{:S(2)}, u32[]{:S(2)}) collective-permute-start(f32[4,128]{1,0:T(4,128)S(1)} %add.15.refs_0_), channel_id=1, source_target_pairs={{0,2},{1,3},{2,0},{3,1},{4,6},{5,7},{6,4},{7,5},{8,10},{9,11},{10,... | collective-permute-start | bytes 6152 | tf_op jit(solution)/shard_map/ppermute | solution.py:30
  78.3 13.9 %collective-permute-start.16 = (f32[128,256]{1,0:T(8,128)S(1)}, f32[128,256]{1,0:T(8,128)S(1)}, u32[]{:S(2)}, u32[]{:S(2)}) collective-permute-start(f32[128,256]{1,0:T(8,128)S(1)} %get-tuple-element.91), channel_id=1, source_target_pairs={{0,4},{4,0},{8,12},{12,8},{16,20},{20,16},{24,28},{28,24},{1,5},{5... | collective-permute-start | bytes 393224 | tf_op jit(solution)/shard_map/ppermute | solution.py:427
  78.7 13.5 %collective-permute-start.17 = (f32[128,256]{1,0:T(8,128)S(1)}, f32[128,256]{1,0:T(8,128)S(1)}, u32[]{:S(2)}, u32[]{:S(2)}) collective-permute-start(f32[128,256]{1,0:T(8,128)S(1)} %get-tuple-element.92), channel_id=1, source_target_pairs={{0,8},{4,12},{8,0},{12,4},{16,24},{20,28},{24,16},{28,20},{1,9},{5... | collective-permute-start | bytes 393224 | tf_op jit(solution)/shard_map/ppermute | solution.py:427
  79.8 12.4 %collective-permute-start.18 = (f32[128,256]{1,0:T(8,128)S(1)}, f32[128,256]{1,0:T(8,128)S(1)}, u32[]{:S(2)}, u32[]{:S(2)}) collective-permute-start(f32[128,256]{1,0:T(8,128)S(1)} %get-tuple-element.93), channel_id=1, source_target_pairs={{0,12},{4,8},{8,4},{12,0},{16,28},{20,24},{24,20},{28,16},{1,13},{... | collective-permute-start | bytes 393224 | tf_op jit(solution)/shard_map/ppermute | solution.py:427

commit v8 on v7

--- a/solution.py
+++ b/solution.py
@@ -165,9 +165,9 @@
     place = lax.axis_index("row") % NEAR
     away = []
     for index, away_ref in enumerate(away_refs):
-        chunk, mask = index // (NEAR - 1), index % (NEAR - 1) + 1
         piece = away_ref.shape[1]
-        column = pl.multiple_of((place ^ mask) * quarter + chunk * piece, LANE)
+        mask = min(index + 1, NEAR - 1)
+        column = pl.multiple_of((place ^ mask) * quarter + (index + 1 - mask) * piece, LANE)
         source = design.at[:, pl.ds(column, piece)]
         away.append(pltpu.make_async_copy(source, away_ref, sems.at[4 + lines + index]))
     for copy in small + large:
@@ -320,7 +320,7 @@
 def sample_body(scale, start, design_ref, parts_ref, mix_ref, order_ref, *refs):
     near, (keep_ref, send_ref, token_ref, both) = refs[: NEAR - 1], refs[NEAR - 1 :]
     token_ref[...] = order_ref[...]
-    rows, piece = near[0].shape
+    rows, piece = near[-1].shape
     quarter = design_ref.shape[1] // NEAR
     groups = mix_ref.shape[0]
     me = lax.axis_index("row")
@@ -331,7 +331,9 @@
         for tile in range(0, piece, LANE):
             column = pl.multiple_of(me % NEAR * quarter + start + tile, LANE)
             here = slice(tile, tile + LANE)
-            values = [design_ref[part, pl.ds(column, LANE)]] + [ref[part, here] for ref in near]
+            there = slice(start + tile, start + tile + LANE)
+            values = [design_ref[part, pl.ds(column, LANE)]] + [ref[part, there] for ref in near[:-1]]
+            values.append(near[-1][part, here])
             values = [value * sign for value, sign in zip(values, signs)]
             apart = 1
             while apart < NEAR:
@@ -409,16 +411,17 @@
     message, *away = pl.pallas_call(
         first_body,
         out_shape=(shape(row_groups, signs_at(width, row_groups) + rounded(lines, 8), LANE),)
-        + (shape(rows, piece),) * (chunks * (NEAR - 1)),
+        + (shape(rows, width // NEAR),) * (NEAR - 2)
+        + (shape(rows, piece),) * chunks,
         in_specs=[HBM] * 5,
-        out_specs=(VMEM,) + (HBM,) * (chunks * (NEAR - 1)),
+        out_specs=(VMEM,) + (HBM,) * (NEAR - 2 + chunks),
         scratch_shapes=[
             pltpu.VMEM((rows, width), F32),
             pltpu.VMEM((lines, LANE), F32),
             pltpu.VMEM((lines, LANE), jnp.int32),
             pltpu.VMEM((row_groups, PAIR), jnp.int32),
             pltpu.VMEM((1, row_groups), jnp.int32),
-            pltpu.SemaphoreType.DMA((4 + lines + chunks * (NEAR - 1),)),
+            pltpu.SemaphoreType.DMA((4 + lines + NEAR - 2 + chunks,)),
         ],
         compiler_params=pltpu.CompilerParams(vmem_limit_bytes=58 << 20),
     )(design, left, bits, picks.reshape(row_groups, PAIR), counts.reshape(1, row_groups))
@@ -440,7 +443,8 @@
             picked,
             mixed,
             order,
-            *near[chunk],
+            *near[: NEAR - 2],
+            near[NEAR - 2 + chunk],
             scratch=[pltpu.VMEM((NEAR, 2, rows, piece), jnp.bfloat16)],
         )
 
@@ -503,20 +507,15 @@
             *(() if last else (design,)),
         )
 
-    def spread(chunk, order):
-        parts = away[chunk * (NEAR - 1) : (chunk + 1) * (NEAR - 1)]
-        parts, _ = lax.optimization_barrier((parts, order))
-        return [swap(part, mask + 1) for mask, part in enumerate(parts)]
-
     betas, alphas, held, joined = [], [], [], []
     message = picked = exchange(message, "row")
-    near = [spread(0, message)]
+    away, _ = lax.optimization_barrier((away, message))
+    near = [swap(part, min(index + 1, NEAR - 1)) for index, part in enumerate(away)]
     for step in range(ITERS):
         last = step + 1 == ITERS
         if step == 0:
             term, beta, here = back(rinv, message, True)
             mixed, token = mix(beta)
-            near += [spread(chunk, beta) for chunk in range(1, chunks)]
         else:
             term, beta = back(here, message, False)
         betas.append(beta)
@@ -527,7 +526,7 @@
         if step == 0:
             parts = []
             for chunk in range(chunks):
-                keep, send, token = sample(chunk, mixed, token if chunk == 0 else alpha)
+                keep, send, token = sample(chunk, mixed, alpha)
                 if chunk < chunks - 1:
                     parts.append((keep, swap(send, row_groups // 2)))
             for part in parts:
@@ -535,7 +534,7 @@
                 joined.append(part)
         images = paired(image, "col")
         if last:
-            quarters, token = trade(joined, keep, come, images[1])
+            quarters, token = trade(joined, keep, come, images[0])
         left, message = turn(images, left, beta, alpha, token, last)
         message = exchange(message, "row")
         if step == 0:

time: 93.5 us -> 94.3 us (level)
  waiting for transfers between devices: 17.2 us -> 19.7 us
  blocking collectives: 36 us -> 34.6 us
    ppermute x11 -> x9, waiting for transfers between devices: 5.07 us -> 10.5 us  [swap(): lax.ppermute(array, 'row', [(i, i ^ mask) for i in range(row_groups)])]
    ppermute x8, waiting for transfers between devices: 12.2 us -> 9.21 us  [paired(): come = lax.ppermute(array, axis, [(i, i ^ mask) for i in range(size)])]
    all_to_all x3, blocking collectives: 36 us -> 34.6 us  [exchange(): return lax.all_to_all(copies, axis, split_axis=0, concat_axis=0, tiled=True)]
    ppermute x11 -> x9, starting transfers between devices: 11.1 us -> 10.3 us  [swap(): lax.ppermute(array, 'row', [(i, i ^ mask) for i in range(row_groups)])]
  transfers between devices with their start and end apart: 19 -> 17, of which waited for: 9 -> 9; matrix products, arithmetic and copies ran while one was open for 0% -> 0% of each run, Pallas kernels for 18% -> 19%
where the time goes in v8:
time: 94.3 us; the launch traced here: 94 us
  blocking collectives  34.6 us (37%)
  Pallas kernels  22.2 us (24%)
  waiting for transfers between devices  19.7 us (21%)
  starting transfers between devices  16.7 us (18%)
    all_to_all x3, blocking collectives, exchange(): return lax.all_to_all(copies, axis, split_axis=0, concat_axis=0, tiled=True)  34.6 us
    pallas_call x10, Pallas kernels, call(): pl.pallas_call(body, out_shape=out_shape, in_specs=[VMEM] * len(operands)...  10.6 us
    ppermute x9, waiting for transfers between devices, swap(): lax.ppermute(array, 'row', [(i, i ^ mask) for i in range(row_groups)])  10.5 us
    ppermute x9, starting transfers between devices, swap(): lax.ppermute(array, 'row', [(i, i ^ mask) for i in range(row_groups)])  10.3 us
    ppermute x8, waiting for transfers between devices, paired(): come = lax.ppermute(array, axis, [(i, i ^ mask) for i in range(size)])  9.21 us
    pallas_call x2, Pallas kernels, back(): pl.pallas_call(functools.partial(back_body, first), out_shape=outs, in_sp...  7.97 us
    ppermute x8, starting transfers between devices, paired(): come = lax.ppermute(array, axis, [(i, i ^ mask) for i in range(size)])  6.4 us
    pallas_call x1, Pallas kernels, shards(): pl.pallas_call(first_body, out_shape=(shape(row_groups, signs_at(width, r...  3.63 us
  transfers between devices with their start and end apart: 17, of which 9 were waited for; matrix products, arithmetic and copies ran while one was open for 0% of the time, Pallas kernels for 19%

profile of v8, /device:TPU:0, one launch (start us, length us, event | category | flops | bytes accessed | tf_op | source)
XLA Modules:
  0.0 94.0 jit_solution(6463630292601010597)
XLA Ops:
  0.7 3.6 %shard_map.94 = (f32[8,32,128]{2,1,0:T(8,128)}, f32[512,256]{1,0:T(8,128)}, f32[512,256]{1,0:T(8,128)}, f32[512,128]{1,0:T(8,128)}, f32[512,128]{1,0:T(8,128)}) custom-call(f32[512,1024]{1,0:T(8,128)} %design_ref.9, f32[4,128]{1,0:T(4,128)} %bitcast.6, s32[4,128]{1,0:T(4,128)} %bitcast.9, s32[8,16]{1,0:T(8,128)} %bitcast.8, s32[1,8]{1,0:T(1,128)} %bitcast.10), custom_call_target="tpu_custom_call" | custom-call | tf_op jit(solution)/shard_map/pallas_call | solution.py:411
  4.3 14.8 %all_to_all.15.parts_ref = f32[8,32,128]{2,1,0:T(8,128)S(1)} all-to-all(f32[8,32,128]{2,1,0:T(8,128)} %get-tuple-element.45), channel_id=1, replica_groups=mesh['row'=8,'col'=4] {'row'}, dimensions={0} | all-to-all | bytes 262144 | tf_op jit(solution)/shard_map/all_to_all | solution.py:23
  19.3 1.1 %collective-permute-start.5 = (f32[512,256]{1,0:T(8,128)}, f32[512,256]{1,0:T(8,128)S(1)}, u32[]{:S(2)}, u32[]{:S(2)}) collective-permute-start(f32[512,256]{1,0:T(8,128)} %get-tuple-element.57), channel_id=1, source_target_pairs={{0,8},{4,12},{8,0},{12,4},{16,24},{20,28},{24,16},{28,20},{1,9},{5... | collective-permute-start | bytes 1572872 | tf_op jit(solution)/shard_map/ppermute | solution.py:430
  20.4 2.2 %collective-permute-start.6 = (f32[512,128]{1,0:T(8,128)}, f32[512,128]{1,0:T(8,128)S(1)}, u32[]{:S(2)}, u32[]{:S(2)}) collective-permute-start(f32[512,128]{1,0:T(8,128)} %get-tuple-element.58), channel_id=1, source_target_pairs={{0,12},{4,8},{8,4},{12,0},{16,28},{20,24},{24,20},{28,16},{1,13},{... | collective-permute-start | bytes 786440 | tf_op jit(solution)/shard_map/ppermute | solution.py:430
  22.6 6.2 %shard_map.95 = (f32[32,128]{1,0:T(8,128)S(1)}, f32[1,128]{1,0:T(1,128)S(1)}, f32[1024,4096]{1,0:T(8,128)S(1)}) custom-call(f32[1024,4096]{1,0:T(8,128)} %rinv_ref.1, f32[8,32,128]{2,1,0:T(8,128)S(1)} %all_to_all.15.parts_ref), custom_call_target="tpu_custom_call" | custom-call | tf_op jit(solution)/shard_map/pallas_call | solution.py:479
  28.8 1.2 %collective-permute-done = f32[32,128]{1,0:T(8,128)S(1)} collective-permute-done((f32[32,128]{1,0:T(8,128)S(1)}, f32[32,128]{1,0:T(8,128)S(1)}, u32[]{:S(2)}, u32[]{:S(2)}) %collective-permute-start) | collective-permute-done | bytes 16416 | tf_op jit(solution)/shard_map/ppermute | solution.py:30
  30.0 1.5 %collective-permute-start.1 = (f32[32,128]{1,0:T(8,128)S(1)}, f32[32,128]{1,0:T(8,128)S(1)}, u32[]{:S(2)}, u32[]{:S(2)}) collective-permute-start(f32[32,128]{1,0:T(8,128)S(1)} %add.12.refs_0_), channel_id=1, source_target_pairs={{0,2},{1,3},{2,0},{3,1},{4,6},{5,7},{6,4},{7,5},{8,10},{9,11},{10,... | collective-permute-start | bytes 49160 | tf_op jit(solution)/shard_map/ppermute | solution.py:30
  31.5 0.7 collective-permute-start.8
  32.2 1.3 %shard_map.97 = (bf16[8,128,512]{2,1,0:T(8,128)(2,1)S(1)}, f32[1,128]{1,0:T(1,128)}) custom-call(f32[8,32,128]{2,1,0:T(8,128)S(1)} %all_to_all.15.parts_ref, bf16[256,256]{1,0:T(8,128)(2,1)S(1)} %copy-done.1, f32[1,128]{1,0:T(1,128)S(1)} %get-tuple-element.49.order_ref.refs_3_.refs_0_), custom_call_target="tpu_custom_call" | custom-call | tf_op jit(solution)/shard_map/pallas_call | solution.py:53
  33.7 2.4 %shard_map.96 = (f32[4,128]{1,0:T(4,128)S(1)}, f32[32,128]{1,0:T(8,128)S(1)}, f32[8,128]{1,0:T(8,128)S(1)}, f32[1,128]{1,0:T(1,128)S(1)}) custom-call(f32[1024,4096]{1,0:T(8,128)S(1)} %get-tuple-element.46.rinv_ref, f32[512,1024]{1,0:T(8,128)S(1)} %copy-done, f32[32,128]{1,0:T(8,128)S(1)} %add.12.refs_0_, f32[32,128]{1,0:T(8,128)S(1)} %collective-permute-done.1.refs_1_), custom_call_target="tpu_custom_call" | custom-call | tf_op jit(solution)/shard_map/pallas_call | solution.py:53
  36.2 6.7 %collective-permute-done.6.refs_2_ = f32[512,128]{1,0:T(8,128)S(1)} collective-permute-done((f32[512,128]{1,0:T(8,128)}, f32[512,128]{1,0:T(8,128)S(1)}, u32[]{:S(2)}, u32[]{:S(2)}) %collective-permute-start.6) | collective-permute-done | bytes 262176 | tf_op jit(solution)/shard_map/ppermute | solution.py:430
  42.9 1.5 %shard_map.98 = (f32[1,4,128,128]{3,2,1,0:T(8,128)S(1)}, f32[1,4,128,128]{3,2,1,0:T(8,128)S(1)}, f32[1,128]{1,0:T(1,128)}) custom-call(f32[512,1024]{1,0:T(8,128)S(1)} %copy-done, f32[8,32,128]{2,1,0:T(8,128)S(1)} %all_to_all.15.parts_ref, bf16[8,128,512]{2,1,0:T(8,128)(2,1)S(1)} %get-tuple-element.51.mix_ref, ...), custom_call_target="tpu_custom_call" | custom-call | tf_op jit(solution)/shard_map/pallas_call | solution.py:53
  44.4 1.2 %collective-permute-done.2 = f32[4,128]{1,0:T(4,128)S(1)} collective-permute-done((f32[4,128]{1,0:T(4,128)S(1)}, f32[4,128]{1,0:T(4,128)S(1)}, u32[]{:S(2)}, u32[]{:S(2)}) %collective-permute-start.2) | collective-permute-done | bytes 2080 | tf_op jit(solution)/shard_map/ppermute | solution.py:30
  45.6 1.8 %collective-permute-start.3 = (f32[4,128]{1,0:T(4,128)S(1)}, f32[4,128]{1,0:T(4,128)S(1)}, u32[]{:S(2)}, u32[]{:S(2)}) collective-permute-start(f32[4,128]{1,0:T(4,128)S(1)} %add.13.refs_0_), channel_id=1, source_target_pairs={{0,2},{1,3},{2,0},{3,1},{4,6},{5,7},{6,4},{7,5},{8,10},{9,11},{10,... | collective-permute-start | bytes 6152 | tf_op jit(solution)/shard_map/ppermute | solution.py:30
  47.4 1.1 %shard_map.99 = (f32[1,4,128,128]{3,2,1,0:T(8,128)S(1)}, f32[1,4,128,128]{3,2,1,0:T(8,128)S(1)}, f32[1,128]{1,0:T(1,128)S(1)}) custom-call(f32[512,1024]{1,0:T(8,128)S(1)} %copy-done, f32[8,32,128]{2,1,0:T(8,128)S(1)} %all_to_all.15.parts_ref, bf16[8,128,512]{2,1,0:T(8,128)(2,1)S(1)} %get-tuple-element.51.mix_ref, ...), custom_call_target="tpu_custom_call" | custom-call | tf_op jit(solution)/shard_map/pallas_call | solution.py:53
  48.5 3.8 %collective-permute-done.7.arrived_ref = f32[1,4,128,128]{3,2,1,0:T(8,128)S(1)} collective-permute-done((f32[1,4,128,128]{3,2,1,0:T(8,128)S(1)}, f32[1,4,128,128]{3,2,1,0:T(8,128)S(1)}, u32[]{:S(2)}, u32[]{:S(2)}) %collective-permute-start.7) | collective-permute-done | bytes 262176 | tf_op jit(solution)/shard_map/ppermute | solution.py:430
  52.4 0.2 shard_map.101
  52.6 10.4 %all_to_all.16.parts_ref = f32[8,16,128]{2,1,0:T(8,128)S(1)} all-to-all(f32[8,16,128]{2,1,0:T(8,128)S(1)} %get-tuple-element.64), channel_id=1, replica_groups=mesh['row'=8,'col'=4] {'row'}, dimensions={0} | all-to-all | bytes 131072 | tf_op jit(solution)/shard_map/all_to_all | solution.py:23
  63.0 2.5 %collective-permute-start.13 = (f32[1,4,128,128]{3,2,1,0:T(8,128)S(1)}, f32[1,4,128,128]{3,2,1,0:T(8,128)S(1)}, u32[]{:S(2)}, u32[]{:S(2)}) collective-permute-start(f32[1,4,128,128]{3,2,1,0:T(8,128)S(1)} %get-tuple-element.74), channel_id=1, source_target_pairs={{0,16},{4,20},{8,24},{12,28},{16,0},{20,4},{24,8},{28,12},{1,17},{... | collective-permute-start | bytes 786440 | tf_op jit(solution)/shard_map/ppermute | solution.py:430
  65.5 1.8 %shard_map.102 = (f32[32,128]{1,0:T(8,128)S(1)}, f32[1,128]{1,0:T(1,128)S(1)}) custom-call(f32[1024,4096]{1,0:T(8,128)S(1)} %get-tuple-element.46.rinv_ref, f32[8,16,128]{2,1,0:T(8,128)S(1)} %all_to_all.16.parts_ref), custom_call_target="tpu_custom_call" | custom-call | tf_op jit(solution)/shard_map/pallas_call | solution.py:479
  67.4 1.2 %collective-permute-done.9 = f32[32,128]{1,0:T(8,128)S(1)} collective-permute-done((f32[32,128]{1,0:T(8,128)S(1)}, f32[32,128]{1,0:T(8,128)S(1)}, u32[]{:S(2)}, u32[]{:S(2)}) %collective-permute-start.9) | collective-permute-done | bytes 16416 | tf_op jit(solution)/shard_map/ppermute | solution.py:30
  68.5 1.5 %collective-permute-start.10 = (f32[32,128]{1,0:T(8,128)S(1)}, f32[32,128]{1,0:T(8,128)S(1)}, u32[]{:S(2)}, u32[]{:S(2)}) collective-permute-start(f32[32,128]{1,0:T(8,128)S(1)} %add.14.refs_0_), channel_id=1, source_target_pairs={{0,2},{1,3},{2,0},{3,1},{4,6},{5,7},{6,4},{7,5},{8,10},{9,11},{10,... | collective-permute-start | bytes 49160 | tf_op jit(solution)/shard_map/ppermute | solution.py:30
  70.0 2.3 %collective-permute-done.10.refs_1_ = f32[32,128]{1,0:T(8,128)S(1)} collective-permute-done((f32[32,128]{1,0:T(8,128)S(1)}, f32[32,128]{1,0:T(8,128)S(1)}, u32[]{:S(2)}, u32[]{:S(2)}) %collective-permute-start.10) | collective-permute-done | bytes 16416 | tf_op jit(solution)/shard_map/ppermute | solution.py:30
  72.3 2.9 %shard_map.103 = (f32[4,128]{1,0:T(4,128)S(1)}, f32[32,128]{1,0:T(8,128)}, f32[8,128]{1,0:T(8,128)S(1)}, f32[1,128]{1,0:T(1,128)S(1)}) custom-call(f32[1024,4096]{1,0:T(8,128)S(1)} %get-tuple-element.46.rinv_ref, f32[512,1024]{1,0:T(8,128)S(1)} %copy-done, f32[32,128]{1,0:T(8,128)S(1)} %add.14.refs_0_, f32[32,128]{1,0:T(8,128)S(1)} %collective-permute-done.10.refs_1_, ...), custom_call_target="tpu_custom_call" | custom-call | tf_op jit(solution)/shard_map/pallas_call | solution.py:53
  75.2 1.2 %collective-permute-done.11 = f32[4,128]{1,0:T(4,128)S(1)} collective-permute-done((f32[4,128]{1,0:T(4,128)S(1)}, f32[4,128]{1,0:T(4,128)S(1)}, u32[]{:S(2)}, u32[]{:S(2)}) %collective-permute-start.11) | collective-permute-done | bytes 2080 | tf_op jit(solution)/shard_map/ppermute | solution.py:30
  76.4 0.5 collective-permute-start.14
  76.9 1.8 %collective-permute-start.15 = (f32[128,256]{1,0:T(8,128)S(1)}, f32[128,256]{1,0:T(8,128)S(1)}, u32[]{:S(2)}, u32[]{:S(2)}) collective-permute-start(f32[128,256]{1,0:T(8,128)S(1)} %get-tuple-element.82), channel_id=1, source_target_pairs={{0,8},{4,12},{8,0},{12,4},{16,24},{20,28},{24,16},{28,20},{1,9},{5... | collective-permute-start | bytes 393224 | tf_op jit(solution)/shard_map/ppermute | solution.py:430
  78.7 1.3 %collective-permute-start.16 = (f32[128,256]{1,0:T(8,128)S(1)}, f32[128,256]{1,0:T(8,128)S(1)}, u32[]{:S(2)}, u32[]{:S(2)}) collective-permute-start(f32[128,256]{1,0:T(8,128)S(1)} %get-tuple-element.83), channel_id=1, source_target_pairs={{0,12},{4,8},{8,4},{12,0},{16,28},{20,24},{24,20},{28,16},{1,13},{... | collective-permute-start | bytes 393224 | tf_op jit(solution)/shard_map/ppermute | solution.py:430
  80.0 1.5 %collective-permute-start.12 = (f32[4,128]{1,0:T(4,128)S(1)}, f32[4,128]{1,0:T(4,128)S(1)}, u32[]{:S(2)}, u32[]{:S(2)}) collective-permute-start(f32[4,128]{1,0:T(4,128)S(1)} %add.15.refs_3_.refs_0_), channel_id=1, source_target_pairs={{0,2},{1,3},{2,0},{3,1},{4,6},{5,7},{6,4},{7,5},{8,10},{9,11},{10,... | collective-permute-start | bytes 6152 | tf_op jit(solution)/shard_map/ppermute | solution.py:30
  81.5 2.1 %collective-permute-done.12.refs_1_ = f32[4,128]{1,0:T(4,128)S(1)} collective-permute-done((f32[4,128]{1,0:T(4,128)S(1)}, f32[4,128]{1,0:T(4,128)S(1)}, u32[]{:S(2)}, u32[]{:S(2)}) %collective-permute-start.12) | collective-permute-done | bytes 2080 | tf_op jit(solution)/shard_map/ppermute | solution.py:30
  83.7 9.4 %all_to_all.17.parts_ref = f32[8,8,128]{2,1,0:T(8,128)S(1)} all-to-all(f32[8,8,128]{2,1,0:T(8,128)S(1)} %get-tuple-element.76), channel_id=1, replica_groups=mesh['row'=8,'col'=4] {'row'}, dimensions={0} | all-to-all | bytes 65536 | tf_op jit(solution)/shard_map/all_to_all | solution.py:23
  93.1 0.9 shard_map.106
  (30 shorter events, 0.8 us)
Async XLA Ops:
  0.6 31.6 %copy-start.1 = (bf16[256,256]{1,0:T(8,128)(2,1)S(1)}, bf16[256,256]{1,0:T(8,128)(2,1)}, u32[]{:S(2)}) copy-start(bf16[256,256]{1,0:T(8,128)(2,1)} %constant.2.clone.walsh_ref) | copy-start | bytes 393220
  0.6 33.1 %copy-start = (f32[512,1024]{1,0:T(8,128)S(1)}, f32[512,1024]{1,0:T(8,128)}, u32[]{:S(2)}) copy-start(f32[512,1024]{1,0:T(8,128)} %design_ref.9) | copy-start | bytes 6291460
  4.3 27.2 %copy-start.3 = (f32[512,128]{1,0:T(8,128)S(1)}, f32[512,128]{1,0:T(8,128)}, u32[]{:S(2)}) copy-start(f32[512,128]{1,0:T(8,128)} %get-tuple-element.61) | copy-start | bytes 786436
  19.1 23.8 %collective-permute-start.4 = (f32[512,256]{1,0:T(8,128)}, f32[512,256]{1,0:T(8,128)S(1)}, u32[]{:S(2)}, u32[]{:S(2)}) collective-permute-start(f32[512,256]{1,0:T(8,128)} %get-tuple-element.56), channel_id=1, source_target_pairs={{0,4},{4,0},{8,12},{12,8},{16,20},{20,16},{24,28},{28,24},{1,5},{5... | collective-permute-start | bytes 1572872 | tf_op jit(solution)/shard_map/ppermute | solution.py:430
  19.3 23.6 %collective-permute-start.5 = (f32[512,256]{1,0:T(8,128)}, f32[512,256]{1,0:T(8,128)S(1)}, u32[]{:S(2)}, u32[]{:S(2)}) collective-permute-start(f32[512,256]{1,0:T(8,128)} %get-tuple-element.57), channel_id=1, source_target_pairs={{0,8},{4,12},{8,0},{12,4},{16,24},{20,28},{24,16},{28,20},{1,9},{5... | collective-permute-start | bytes 1572872 | tf_op jit(solution)/shard_map/ppermute | solution.py:430
  20.4 22.5 %collective-permute-start.6 = (f32[512,128]{1,0:T(8,128)}, f32[512,128]{1,0:T(8,128)S(1)}, u32[]{:S(2)}, u32[]{:S(2)}) collective-permute-start(f32[512,128]{1,0:T(8,128)} %get-tuple-element.58), channel_id=1, source_target_pairs={{0,12},{4,8},{8,4},{12,0},{16,28},{20,24},{24,20},{28,16},{1,13},{... | collective-permute-start | bytes 786440 | tf_op jit(solution)/shard_map/ppermute | solution.py:430
  28.7 23.6 %copy-start.2 = (f32[512]{0:T(512)S(1)}, f32[512]{0:T(512)}, u32[]{:S(2)}) copy-start(f32[512]{0:T(512)} %param.11) | copy-start | bytes 6148
  28.7 1.2 %collective-permute-start = (f32[32,128]{1,0:T(8,128)S(1)}, f32[32,128]{1,0:T(8,128)S(1)}, u32[]{:S(2)}, u32[]{:S(2)}) collective-permute-start(f32[32,128]{1,0:T(8,128)S(1)} %get-tuple-element.47), channel_id=1, source_target_pairs={{0,1},{1,0},{2,3},{3,2},{4,5},{5,4},{6,7},{7,6},{8,9},{9,8},{10,11... | collective-permute-start | bytes 49160 | tf_op jit(solution)/shard_map/ppermute | solution.py:30
  30.0 3.7 %collective-permute-start.1 = (f32[32,128]{1,0:T(8,128)S(1)}, f32[32,128]{1,0:T(8,128)S(1)}, u32[]{:S(2)}, u32[]{:S(2)}) collective-permute-start(f32[32,128]{1,0:T(8,128)S(1)} %add.12.refs_0_), channel_id=1, source_target_pairs={{0,2},{1,3},{2,0},{3,1},{4,6},{5,7},{6,4},{7,5},{8,10},{9,11},{10,... | collective-permute-start | bytes 49160 | tf_op jit(solution)/shard_map/ppermute | solution.py:30
  31.5 15.9 %collective-permute-start.8 = (f32[512,128]{1,0:T(8,128)S(1)}, f32[512,128]{1,0:T(8,128)S(1)}, u32[]{:S(2)}, u32[]{:S(2)}) collective-permute-start(f32[512,128]{1,0:T(8,128)S(1)} %copy-done.3), channel_id=1, source_target_pairs={{0,12},{4,8},{8,4},{12,0},{16,28},{20,24},{24,20},{28,16},{1,13},{... | collective-permute-start | bytes 786440 | tf_op jit(solution)/shard_map/ppermute | solution.py:430
  44.4 7.9 %collective-permute-start.7 = (f32[1,4,128,128]{3,2,1,0:T(8,128)S(1)}, f32[1,4,128,128]{3,2,1,0:T(8,128)S(1)}, u32[]{:S(2)}, u32[]{:S(2)}) collective-permute-start(f32[1,4,128,128]{3,2,1,0:T(8,128)S(1)} %get-tuple-element.60), channel_id=1, source_target_pairs={{0,16},{4,20},{8,24},{12,28},{16,0},{20,4},{24,8},{28,12},{1,17},{... | collective-permute-start | bytes 786440 | tf_op jit(solution)/shard_map/ppermute | solution.py:430
  44.4 1.2 %collective-permute-start.2 = (f32[4,128]{1,0:T(4,128)S(1)}, f32[4,128]{1,0:T(4,128)S(1)}, u32[]{:S(2)}, u32[]{:S(2)}) collective-permute-start(f32[4,128]{1,0:T(4,128)S(1)} %get-tuple-element.48), channel_id=1, source_target_pairs={{0,1},{1,0},{2,3},{3,2},{4,5},{5,4},{6,7},{7,6},{8,9},{9,8},{10,11... | collective-permute-start | bytes 6152 | tf_op jit(solution)/shard_map/ppermute | solution.py:30
  45.6 6.7 %collective-permute-start.3 = (f32[4,128]{1,0:T(4,128)S(1)}, f32[4,128]{1,0:T(4,128)S(1)}, u32[]{:S(2)}, u32[]{:S(2)}) collective-permute-start(f32[4,128]{1,0:T(4,128)S(1)} %add.13.refs_0_), channel_id=1, source_target_pairs={{0,2},{1,3},{2,0},{3,1},{4,6},{5,7},{6,4},{7,5},{8,10},{9,11},{10,... | collective-permute-start | bytes 6152 | tf_op jit(solution)/shard_map/ppermute | solution.py:30
  63.0 13.4 %collective-permute-start.13 = (f32[1,4,128,128]{3,2,1,0:T(8,128)S(1)}, f32[1,4,128,128]{3,2,1,0:T(8,128)S(1)}, u32[]{:S(2)}, u32[]{:S(2)}) collective-permute-start(f32[1,4,128,128]{3,2,1,0:T(8,128)S(1)} %get-tuple-element.74), channel_id=1, source_target_pairs={{0,16},{4,20},{8,24},{12,28},{16,0},{20,4},{24,8},{28,12},{1,17},{... | collective-permute-start | bytes 786440 | tf_op jit(solution)/shard_map/ppermute | solution.py:430
  67.3 1.2 %collective-permute-start.9 = (f32[32,128]{1,0:T(8,128)S(1)}, f32[32,128]{1,0:T(8,128)S(1)}, u32[]{:S(2)}, u32[]{:S(2)}) collective-permute-start(f32[32,128]{1,0:T(8,128)S(1)} %get-tuple-element.65), channel_id=1, source_target_pairs={{0,1},{1,0},{2,3},{3,2},{4,5},{5,4},{6,7},{7,6},{8,9},{9,8},{10,11... | collective-permute-start | bytes 49160 | tf_op jit(solution)/shard_map/ppermute | solution.py:30
  68.5 3.7 %collective-permute-start.10 = (f32[32,128]{1,0:T(8,128)S(1)}, f32[32,128]{1,0:T(8,128)S(1)}, u32[]{:S(2)}, u32[]{:S(2)}) collective-permute-start(f32[32,128]{1,0:T(8,128)S(1)} %add.14.refs_0_), channel_id=1, source_target_pairs={{0,2},{1,3},{2,0},{3,1},{4,6},{5,7},{6,4},{7,5},{8,10},{9,11},{10,... | collective-permute-start | bytes 49160 | tf_op jit(solution)/shard_map/ppermute | solution.py:30
  75.2 1.2 %collective-permute-start.11 = (f32[4,128]{1,0:T(4,128)S(1)}, f32[4,128]{1,0:T(4,128)S(1)}, u32[]{:S(2)}, u32[]{:S(2)}) collective-permute-start(f32[4,128]{1,0:T(4,128)S(1)} %get-tuple-element.68), channel_id=1, source_target_pairs={{0,1},{1,0},{2,3},{3,2},{4,5},{5,4},{6,7},{7,6},{8,9},{9,8},{10,11... | collective-permute-start | bytes 6152 | tf_op jit(solution)/shard_map/ppermute | solution.py:30
  76.4 16.6 %collective-permute-start.14 = (f32[128,256]{1,0:T(8,128)S(1)}, f32[128,256]{1,0:T(8,128)S(1)}, u32[]{:S(2)}, u32[]{:S(2)}) collective-permute-start(f32[128,256]{1,0:T(8,128)S(1)} %get-tuple-element.81), channel_id=1, source_target_pairs={{0,4},{4,0},{8,12},{12,8},{16,20},{20,16},{24,28},{28,24},{1,5},{5... | collective-permute-start | bytes 393224 | tf_op jit(solution)/shard_map/ppermute | solution.py:430
  76.9 16.2 %collective-permute-start.15 = (f32[128,256]{1,0:T(8,128)S(1)}, f32[128,256]{1,0:T(8,128)S(1)}, u32[]{:S(2)}, u32[]{:S(2)}) collective-permute-start(f32[128,256]{1,0:T(8,128)S(1)} %get-tuple-element.82), channel_id=1, source_target_pairs={{0,8},{4,12},{8,0},{12,4},{16,24},{20,28},{24,16},{28,20},{1,9},{5... | collective-permute-start | bytes 393224 | tf_op jit(solution)/shard_map/ppermute | solution.py:430
  78.7 14.4 %collective-permute-start.16 = (f32[128,256]{1,0:T(8,128)S(1)}, f32[128,256]{1,0:T(8,128)S(1)}, u32[]{:S(2)}, u32[]{:S(2)}) collective-permute-start(f32[128,256]{1,0:T(8,128)S(1)} %get-tuple-element.83), channel_id=1, source_target_pairs={{0,12},{4,8},{8,4},{12,0},{16,28},{20,24},{24,20},{28,16},{1,13},{... | collective-permute-start | bytes 393224 | tf_op jit(solution)/shard_map/ppermute | solution.py:430
  80.0 3.6 %collective-permute-start.12 = (f32[4,128]{1,0:T(4,128)S(1)}, f32[4,128]{1,0:T(4,128)S(1)}, u32[]{:S(2)}, u32[]{:S(2)}) collective-permute-start(f32[4,128]{1,0:T(4,128)S(1)} %add.15.refs_3_.refs_0_), channel_id=1, source_target_pairs={{0,2},{1,3},{2,0},{3,1},{4,6},{5,7},{6,4},{7,5},{8,10},{9,11},{10,... | collective-permute-start | bytes 6152 | tf_op jit(solution)/shard_map/ppermute | solution.py:30

commit v9 on v8

--- a/solution.py
+++ b/solution.py
@@ -13,7 +13,6 @@
 ITERS = 2
 LANE = 128
 NEAR = 4
-CHUNKS = 2
 F32 = jnp.float32
 VMEM = pl.BlockSpec(memory_space=pltpu.VMEM)
 HBM = pl.BlockSpec(memory_space=pltpu.HBM)
@@ -136,6 +135,11 @@
     return message_rows(width) + rounded(groups, 8)
 
 
+def columns_traded(width):
+    unit = NEAR * LANE
+    return max(unit, width // 2 // unit * unit)
+
+
 def copy_out(out_ref):
     first = out_ref[0]
     for index in range(1, out_ref.shape[0]):
@@ -150,7 +154,7 @@
     out_ref, away_refs = refs[0], refs[1:-6]
     design, target_here, bits, picks, counts, sems = refs[-6:]
     rows, width = design.shape
-    lines, tiles, quarter = rows // LANE, width // LANE, width // NEAR
+    lines, tiles = rows // LANE, width // LANE
     small = [
         pltpu.make_async_copy(source, place, sems.at[index])
         for index, (source, place) in enumerate(
@@ -166,8 +170,7 @@
     away = []
     for index, away_ref in enumerate(away_refs):
         piece = away_ref.shape[1]
-        mask = min(index + 1, NEAR - 1)
-        column = pl.multiple_of((place ^ mask) * quarter + (index + 1 - mask) * piece, LANE)
+        column = pl.multiple_of(width - NEAR * piece + (place ^ (index + 1)) * piece, LANE)
         source = design.at[:, pl.ds(column, piece)]
         away.append(pltpu.make_async_copy(source, away_ref, sems.at[4 + lines + index]))
     for copy in small + large:
@@ -203,7 +206,7 @@
         copy.wait()
 
 
-def back_body(first, rinv_ref, parts_ref, term_ref, beta_ref, *refs):
+def back_body(first, rinv_ref, parts_ref, order_ref, term_ref, beta_ref, *refs):
     tiles = rinv_ref.shape[0] // LANE
     copies = []
     if first:
@@ -238,7 +241,7 @@
 
 def turn_body(groups, last, *refs):
     left = tree([ref[...] for ref in refs[:groups]])
-    before_ref, beta_ref, alpha_ref, token_ref, *refs = refs[groups:]
+    before_ref, beta_ref, alpha_ref, *refs = refs[groups:]
     left = left - alpha_ref[...] * (before_ref[...] / beta_ref[...])
     square = splat(total(left * left))
     if last:
@@ -254,18 +257,160 @@
     left_ref[...] = left
 
 
+def pieces(value):
+    high = value.astype(jnp.bfloat16)
+    return high, (value - high.astype(F32)).astype(jnp.bfloat16)
+
+
+def weigh(mix, high, low):
+    return jnp.dot(mix, high, preferred_element_type=F32) + jnp.dot(mix, low, preferred_element_type=F32)
+
+
+def for_blocks(groups, step):
+    if groups <= 8:
+        for block in range(groups):
+            step(block, 0)
+    else:
+        lax.fori_loop(0, groups, step, 0)
+
+
+def mix_rows(parts_ref, walsh_ref, width, block, groups, rows):
+    me = lax.axis_index("row")
+    start = picks_at(width)
+    local = lax.broadcasted_iota(jnp.int32, (PAIR, rows), 1).astype(F32)
+    coded = [parts_ref[block, pl.ds(start + (apart ^ me), 1), :] for apart in range(groups)]
+    coded = jnp.concatenate(coded + [jnp.zeros((LANE - groups, LANE), F32)], axis=0).T
+    parity = jnp.int32(0)
+    for bit in range(groups.bit_length() - 1):
+        parity = parity ^ ((block & me) >> bit)
+    sign = (1 - 2 * (parity & 1)).astype(F32)
+    chosen = []
+    for apart in range(groups):
+        match = jnp.broadcast_to(coded[:PAIR, apart : apart + 1], (PAIR, rows)) == local
+        chosen.append(jnp.where(match, sign, 0.0))
+    chosen = jnp.concatenate(chosen, axis=0).astype(jnp.bfloat16)
+    mixed = []
+    for part in range(rows // HB):
+        mix = jnp.dot(chosen[:, part * HB : (part + 1) * HB], walsh_ref[...], preferred_element_type=F32)
+        mixed.append(mix.astype(jnp.bfloat16))
+    return jnp.concatenate(mixed, axis=1)
+
+
+def mix_body(width, parts_ref, walsh_ref, mix_ref, token_ref):
+    token_ref[...] = parts_ref[0, :1, :]
+    groups, _, rows = mix_ref.shape
+
+    def step(block, carry):
+        mix_ref[block] = mix_rows(parts_ref, walsh_ref, width, block, groups, rows)
+        return carry
+
+    for_blocks(groups, step)
+
+
+def share_body(scale, parts_ref, walsh_ref, design_ref, mix_ref, token_ref, out_ref, here, both, share, sems):
+    token_ref[...] = parts_ref[0, :1, :]
+    groups, _, columns = share.shape
+    rows, width = design_ref.shape
+    fetch = pltpu.make_async_copy(design_ref.at[:, pl.ds(0, columns)], here, sems.at[groups])
+    fetch.start()
+    me = lax.axis_index("row")
+
+    def mix(block, carry):
+        mix_ref[block] = mix_rows(parts_ref, walsh_ref, width, block, groups, rows)
+        return carry
+
+    for_blocks(groups, mix)
+    fetch.wait()
+    start = signs_at(width, groups)
+    for line in range(rows // LANE):
+        part = slice(line * LANE, (line + 1) * LANE)
+        sign = across(parts_ref[me, start + line : start + line + 1, :])
+        for tile in range(0, columns, LANE):
+            place = slice(tile, tile + LANE)
+            both[0, part, place], both[1, part, place] = pieces(here[part, place] * sign)
+
+    def out_copy(block):
+        slot = pl.ds(block * PAIR, PAIR)
+        return pltpu.make_async_copy(share.at[:, slot, :], out_ref.at[:, slot, :], sems.at[block])
+
+    def step(block, carry):
+        value = weigh(mix_ref[block], both[0], both[1]) / scale
+        for apart in range(groups):
+            share[apart ^ me, pl.ds(block * PAIR, PAIR), :] = value[apart * PAIR : (apart + 1) * PAIR, :]
+        out_copy(block).start()
+        return carry
+
+    def finish(block, carry):
+        out_copy(block).wait()
+        return carry
+
+    for_blocks(groups, step)
+    for_blocks(groups, finish)
+
+
+def sample_body(scale, design_ref, parts_ref, mix_ref, order_ref, *refs):
+    near, (keep_ref, send_ref, both) = refs[: NEAR - 1], refs[NEAR - 1 :]
+    rows, piece = near[0].shape
+    width = design_ref.shape[1]
+    groups = mix_ref.shape[0]
+    me = lax.axis_index("row")
+    signs_start = signs_at(width, groups)
+    for line in range(rows // LANE):
+        part = slice(line * LANE, (line + 1) * LANE)
+        signs = [across(parts_ref[me ^ mask, signs_start + line : signs_start + line + 1, :]) for mask in range(NEAR)]
+        for tile in range(0, piece, LANE):
+            column = pl.multiple_of(width - NEAR * piece + me % NEAR * piece + tile, LANE)
+            here = slice(tile, tile + LANE)
+            values = [design_ref[part, pl.ds(column, LANE)]] + [ref[part, here] for ref in near]
+            values = [value * sign for value, sign in zip(values, signs)]
+            apart = 1
+            while apart < NEAR:
+                for first in range(NEAR):
+                    if not first & apart:
+                        one, two = values[first], values[first | apart]
+                        values[first], values[first | apart] = one + two, one - two
+                apart *= 2
+            for index, value in enumerate(values):
+                both[index, 0, part, here], both[index, 1, part, here] = pieces(value)
+
+    def step(block, carry):
+        value = weigh(mix_ref[block], both[block % NEAR, 0], both[block % NEAR, 1]) / scale
+        slot = pl.ds(block * PAIR, PAIR)
+        for apart in range(groups):
+            far, low = apart // NEAR, apart % NEAR
+            out_ref = send_ref if far >= groups // NEAR // 2 else keep_ref
+            out_ref[far % (groups // NEAR // 2), low, slot, :] = value[apart * PAIR : (apart + 1) * PAIR, :]
+        return carry
+
+    for_blocks(groups, step)
+
+
+def halve_body(kept_ref, arrived_ref, order_ref, keep_ref, send_ref):
+    half = keep_ref.shape[0]
+    keep_ref[...] = kept_ref[:half] + arrived_ref[:half]
+    send_ref[...] = kept_ref[half:] + arrived_ref[half:]
+
+
+def split_body(kept_ref, arrived_ref, order_ref, *out_refs):
+    for index, out_ref in enumerate(out_refs):
+        out_ref[...] = kept_ref[0, index] + arrived_ref[0, index]
+
+
 def last_body(parts_ref, left_ref, *refs):
-    quarters, sketch_ref, refs = refs[-NEAR - 3 : -3], refs[-1], refs[:-1]
+    basis_ref, solution_ref, sketch_ref = refs[-3:]
+    quarters, summed = refs[3 * ITERS : 3 * ITERS + NEAR], refs[3 * ITERS + NEAR : -3]
     place = lax.axis_index("row") % NEAR
     piece = quarters[0].shape[1]
+    width = sketch_ref.shape[1]
+    for ref in summed:
+        sketch_ref[:, : width - NEAR * piece] = ref[...]
     for mask, part_ref in enumerate(quarters):
         for tile in range(0, piece, LANE):
-            column = pl.multiple_of((place ^ mask) * piece + tile, LANE)
+            column = pl.multiple_of(width - NEAR * piece + (place ^ mask) * piece + tile, LANE)
             sketch_ref[:, pl.ds(column, LANE)] = part_ref[:, tile : tile + LANE]
     betas = [ref[...] for ref in refs[:ITERS]]
     alphas = [ref[...] for ref in refs[ITERS : 2 * ITERS]]
     held = [ref[...] for ref in refs[2 * ITERS : 3 * ITERS]]
-    basis_ref, solution_ref = refs[-2:]
     last = jnp.sqrt(tree([parts_ref[i] for i in range(parts_ref.shape[0])])[:1, :])
     basis_ref[...] = left_ref[...] / last
     betas.append(last)
@@ -286,110 +431,6 @@
     solution_ref[...] = iterate
 
 
-def mix_body(start, parts_ref, walsh_ref, order_ref, out_ref, token_ref):
-    token_ref[...] = order_ref[...]
-    groups, _, rows = out_ref.shape
-    me = lax.axis_index("row")
-    local = lax.broadcasted_iota(jnp.int32, (PAIR, rows), 1).astype(F32)
-
-    def step(block, carry):
-        coded = [parts_ref[block, pl.ds(start + (apart ^ me), 1), :] for apart in range(groups)]
-        coded = jnp.concatenate(coded + [jnp.zeros((LANE - groups, LANE), F32)], axis=0).T
-        parity = jnp.int32(0)
-        for bit in range(groups.bit_length() - 1):
-            parity = parity ^ ((block & me) >> bit)
-        sign = (1 - 2 * (parity & 1)).astype(F32)
-        chosen = []
-        for apart in range(groups):
-            match = jnp.broadcast_to(coded[:PAIR, apart : apart + 1], (PAIR, rows)) == local
-            chosen.append(jnp.where(match, sign, 0.0))
-        chosen = jnp.concatenate(chosen, axis=0).astype(jnp.bfloat16)
-        for part in range(rows // HB):
-            columns = slice(part * HB, (part + 1) * HB)
-            mixed = jnp.dot(chosen[:, columns], walsh_ref[...], preferred_element_type=F32)
-            out_ref[block, :, columns] = mixed.astype(jnp.bfloat16)
-        return carry
-
-    if groups <= 8:
-        for block in range(groups):
-            step(block, 0)
-    else:
-        lax.fori_loop(0, groups, step, 0)
-
-
-def sample_body(scale, start, design_ref, parts_ref, mix_ref, order_ref, *refs):
-    near, (keep_ref, send_ref, token_ref, both) = refs[: NEAR - 1], refs[NEAR - 1 :]
-    token_ref[...] = order_ref[...]
-    rows, piece = near[-1].shape
-    quarter = design_ref.shape[1] // NEAR
-    groups = mix_ref.shape[0]
-    me = lax.axis_index("row")
-    signs_start = signs_at(design_ref.shape[1], groups)
-    for line in range(rows // LANE):
-        part = slice(line * LANE, (line + 1) * LANE)
-        signs = [across(parts_ref[me ^ mask, signs_start + line : signs_start + line + 1, :]) for mask in range(NEAR)]
-        for tile in range(0, piece, LANE):
-            column = pl.multiple_of(me % NEAR * quarter + start + tile, LANE)
-            here = slice(tile, tile + LANE)
-            there = slice(start + tile, start + tile + LANE)
-            values = [design_ref[part, pl.ds(column, LANE)]] + [ref[part, there] for ref in near[:-1]]
-            values.append(near[-1][part, here])
-            values = [value * sign for value, sign in zip(values, signs)]
-            apart = 1
-            while apart < NEAR:
-                for first in range(NEAR):
-                    if not first & apart:
-                        one, two = values[first], values[first | apart]
-                        values[first], values[first | apart] = one + two, one - two
-                apart *= 2
-            for index, value in enumerate(values):
-                high = value.astype(jnp.bfloat16)
-                both[index, 0, part, here] = high
-                both[index, 1, part, here] = (value - high.astype(F32)).astype(jnp.bfloat16)
-
-    def step(block, carry):
-        mix = mix_ref[block]
-        value = jnp.dot(mix, both[block % NEAR, 0], preferred_element_type=F32)
-        value = value + jnp.dot(mix, both[block % NEAR, 1], preferred_element_type=F32)
-        value = value / scale
-        slot = pl.ds(block * PAIR, PAIR)
-        for apart in range(groups):
-            far, low = apart // NEAR, apart % NEAR
-            out_ref = send_ref if far >= groups // NEAR // 2 else keep_ref
-            out_ref[far % (groups // NEAR // 2), low, slot, :] = value[apart * PAIR : (apart + 1) * PAIR, :]
-        return carry
-
-    if groups <= 8:
-        for block in range(groups):
-            step(block, 0)
-    else:
-        lax.fori_loop(0, groups, step, 0)
-
-
-def halve_body(kept_ref, arrived_ref, order_ref, keep_ref, send_ref):
-    half = keep_ref.shape[0]
-    keep_ref[...] = kept_ref[:half] + arrived_ref[:half]
-    send_ref[...] = kept_ref[half:] + arrived_ref[half:]
-
-
-def join_body(kept_ref, arrived_ref, order_ref, out_ref, token_ref):
-    token_ref[...] = order_ref[...]
-    out_ref[...] = kept_ref[0] + arrived_ref[0]
-
-
-def split_body(chunks, *refs):
-    joined, (kept_ref, arrived_ref, order_ref, token_ref, *out_refs) = refs[: chunks - 1], refs[chunks - 1 :]
-    token_ref[...] = order_ref[:1, :]
-    piece = kept_ref.shape[3]
-    for chunk in range(chunks):
-        columns = slice(chunk * piece, (chunk + 1) * piece)
-        for index, out_ref in enumerate(out_refs):
-            if chunk < chunks - 1:
-                out_ref[:, columns] = joined[chunk][index]
-            else:
-                out_ref[:, columns] = kept_ref[0, index] + arrived_ref[0, index]
-
-
 def shape(*dims, dtype=F32):
     return jax.ShapeDtypeStruct(dims, dtype)
 
@@ -403,25 +444,25 @@
     deep = message_rows(width)
     left = target.reshape(lines, LANE)
     bits = sign_bits.reshape(lines, LANE)
-    chunks = min(CHUNKS, width // NEAR // LANE)
-    piece = width // NEAR // chunks
+    piece = columns_traded(width) // NEAR
+    rest = width - NEAR * piece
+    scale = float(np.sqrt(np.float32(rows * row_groups)))
     slots = row_groups * PAIR
     far = row_groups // NEAR
 
     message, *away = pl.pallas_call(
         first_body,
         out_shape=(shape(row_groups, signs_at(width, row_groups) + rounded(lines, 8), LANE),)
-        + (shape(rows, width // NEAR),) * (NEAR - 2)
-        + (shape(rows, piece),) * chunks,
+        + (shape(rows, piece),) * (NEAR - 1),
         in_specs=[HBM] * 5,
-        out_specs=(VMEM,) + (HBM,) * (NEAR - 2 + chunks),
+        out_specs=(VMEM,) + (HBM,) * (NEAR - 1),
         scratch_shapes=[
             pltpu.VMEM((rows, width), F32),
             pltpu.VMEM((lines, LANE), F32),
             pltpu.VMEM((lines, LANE), jnp.int32),
             pltpu.VMEM((row_groups, PAIR), jnp.int32),
             pltpu.VMEM((1, row_groups), jnp.int32),
-            pltpu.SemaphoreType.DMA((4 + lines + NEAR - 2 + chunks,)),
+            pltpu.SemaphoreType.DMA((4 + lines + NEAR - 1,)),
         ],
         compiler_params=pltpu.CompilerParams(vmem_limit_bytes=58 << 20),
     )(design, left, bits, picks.reshape(row_groups, PAIR), counts.reshape(1, row_groups))
@@ -429,22 +470,36 @@
     def swap(array, mask):
         return lax.ppermute(array, "row", [(i, i ^ mask) for i in range(row_groups)])
 
-    def mix(order):
-        signs = jnp.asarray(walsh(HB), jnp.bfloat16)
-        made = (shape(row_groups, slots, rows, dtype=jnp.bfloat16), scalar)
-        return call(functools.partial(mix_body, picks_at(width)), made, picked, signs, order)
-
-    def sample(chunk, mixed, order):
-        scale = float(np.sqrt(np.float32(rows * row_groups)))
+    signs = jnp.asarray(walsh(HB), jnp.bfloat16)
+    made = (shape(row_groups, slots, rows, dtype=jnp.bfloat16), scalar)
+
+    def mix(message):
+        return call(functools.partial(mix_body, width), made, message, signs)
+
+    def share(message):
+        return pl.pallas_call(
+            functools.partial(share_body, scale),
+            out_shape=made + (shape(row_groups, slots, rest),),
+            in_specs=[VMEM, VMEM, HBM],
+            out_specs=(VMEM, VMEM, HBM),
+            scratch_shapes=[
+                pltpu.VMEM((rows, rest), F32),
+                pltpu.VMEM((2, rows, rest), jnp.bfloat16),
+                pltpu.VMEM((row_groups, slots, rest), F32),
+                pltpu.SemaphoreType.DMA((row_groups + 1,)),
+            ],
+            compiler_params=pltpu.CompilerParams(vmem_limit_bytes=57 << 20),
+        )(message, signs, design)
+
+    def sample(mixed, order):
         return call(
-            functools.partial(sample_body, scale, chunk * piece),
-            (shape(far // 2, NEAR, slots, piece),) * 2 + (scalar,),
+            functools.partial(sample_body, scale),
+            (shape(far // 2, NEAR, slots, piece),) * 2,
             design,
             picked,
             mixed,
             order,
-            *near[: NEAR - 2],
-            near[NEAR - 2 + chunk],
+            *near,
             scratch=[pltpu.VMEM((NEAR, 2, rows, piece), jnp.bfloat16)],
         )
 
@@ -457,21 +512,11 @@
             come = swap(send, bit)
         return keep, come
 
-    def join(keep, come, order):
-        keep, come = halve(keep, come, order)
-        return call(join_body, (shape(*keep.shape[1:]), scalar), keep, come, order)
-
-    def trade(joined, keep, come, order):
-        token, mine, *others = call(
-            functools.partial(split_body, chunks),
-            (scalar,) + (shape(slots, width // NEAR),) * NEAR,
-            *joined,
-            *halve(keep, come, order),
-            order,
-        )
-        return [mine] + [swap(part, mask + 1) for mask, part in enumerate(others)], token
-
-    def back(rinv, message, first):
+    def trade(keep, come, order):
+        mine, *others = call(split_body, (shape(slots, piece),) * NEAR, *halve(keep, come, order), order)
+        return [mine] + [swap(part, mask + 1) for mask, part in enumerate(others)]
+
+    def back(rinv, message, order, first):
         outs, scratch = (shape(whole // LANE, LANE), scalar), [pltpu.VMEM((width // LANE, LANE), F32)]
         if first:
             outs += (shape(*rinv.shape),)
@@ -479,11 +524,11 @@
         return pl.pallas_call(
             functools.partial(back_body, first),
             out_shape=outs,
-            in_specs=[HBM if first else VMEM, VMEM],
+            in_specs=[HBM if first else VMEM, VMEM, VMEM],
             out_specs=(VMEM,) * len(outs),
             scratch_shapes=scratch,
             compiler_params=pltpu.CompilerParams(vmem_limit_bytes=(34 if first else 24) << 20),
-            )(rinv, message)
+            )(rinv, message, order)
 
     def forward(terms, *before):
         return call(
@@ -495,7 +540,7 @@
             *before,
         )
 
-    def turn(images, left, beta, alpha, token, last):
+    def turn(images, left, beta, alpha, last):
         return call(
             functools.partial(turn_body, 2, last),
             (shape(lines, LANE), shape(row_groups, 8 if last else deep, LANE)),
@@ -503,43 +548,37 @@
             left,
             beta,
             alpha,
-            token,
             *(() if last else (design,)),
         )
 
-    betas, alphas, held, joined = [], [], [], []
+    betas, alphas, held, summed = [], [], [], []
     message = picked = exchange(message, "row")
     away, _ = lax.optimization_barrier((away, message))
-    near = [swap(part, min(index + 1, NEAR - 1)) for index, part in enumerate(away)]
+    near = [swap(part, mask + 1) for mask, part in enumerate(away)]
+    if rest == 0:
+        mixed, token = mix(message)
+    else:
+        mixed, token, shared = share(message)
+        shared = shared.reshape(row_groups * slots, rest)
+        summed.append(lax.psum_scatter(shared, "row", scatter_dimension=0, tiled=True))
     for step in range(ITERS):
         last = step + 1 == ITERS
         if step == 0:
-            term, beta, here = back(rinv, message, True)
-            mixed, token = mix(beta)
+            term, beta, here = back(rinv, message, token, True)
         else:
-            term, beta = back(here, message, False)
+            term, beta = back(here, message, token, False)
+            quarters = trade(keep, come, beta)
         betas.append(beta)
         terms = paired(term, "col")
+        if step == 0:
+            keep, send = sample(mixed, terms[1])
+            come = swap(send, row_groups // 2)
         image, right, kept, alpha = forward(terms, *(() if step == 0 else (right, beta)))
         alphas.append(alpha)
         held.append(kept)
-        if step == 0:
-            parts = []
-            for chunk in range(chunks):
-                keep, send, token = sample(chunk, mixed, alpha)
-                if chunk < chunks - 1:
-                    parts.append((keep, swap(send, row_groups // 2)))
-            for part in parts:
-                part, token = join(*part, token)
-                joined.append(part)
         images = paired(image, "col")
-        if last:
-            quarters, token = trade(joined, keep, come, images[0])
-        left, message = turn(images, left, beta, alpha, token, last)
+        left, message = turn(images, left, beta, alpha, last)
         message = exchange(message, "row")
-        if step == 0:
-            send, _ = lax.optimization_barrier((send, message))
-            come = swap(send, row_groups // 2)
     basis, answer, sketch = call(
         last_body,
         (shape(lines, LANE), shape(width // LANE, LANE), shape(slots, width)),
@@ -549,6 +588,7 @@
         *alphas,
         *held,
         *quarters,
+        *summed,
     )
     return (sketch, answer.reshape(-1), basis.reshape(-1))
 

time: 94.3 us -> 117 us (1.24)
  between operations: 0.76 us -> 14.2 us
  waiting for transfers between devices: 19.7 us -> 27.3 us
  starting transfers between devices: 16.7 us -> 12.5 us
  Pallas kernels: 22.2 us -> 25.1 us
  local copies, waits for them, and re-layouts: 0.02 us -> 2.53 us
    reduce_scatter x0 -> x1, waiting for transfers between devices: none -> 8.55 us  [shards(): lax.psum_scatter(shared, 'row', scatter_dimension=0, tiled=True)]
    pallas_call x0 -> x1, Pallas kernels: none -> 6.1 us  [share(): pl.pallas_call(functools.partial(share_body, scale), out_shape=made + (sh...]
    ppermute x9 -> x7, waiting for transfers between devices: 10.5 us -> 7.03 us  [swap(): lax.ppermute(array, 'row', [(i, i ^ mask) for i in range(row_groups)])]
    ppermute x9 -> x7, starting transfers between devices: 10.3 us -> 7.18 us  [swap(): lax.ppermute(array, 'row', [(i, i ^ mask) for i in range(row_groups)])]
    pallas_call x10 -> x7, Pallas kernels: 10.6 us -> 7.65 us  [call(): pl.pallas_call(body, out_shape=out_shape, in_specs=[VMEM] * len(operands)...]
    unnamed x8 -> x12, local copies, waits for them, and re-layouts: 0.02 us -> 2.53 us
    ppermute x8, waiting for transfers between devices: 9.21 us -> 11.7 us  [paired(): come = lax.ppermute(array, axis, [(i, i ^ mask) for i in range(size)])]
  transfers between devices with their start and end apart: 17 -> 16, of which waited for: 9 -> 9; matrix products, arithmetic and copies ran while one was open for 0% -> 0% of each run, Pallas kernels for 19% -> 13%
where the time goes in v9:
time: 117 us
  blocking collectives  35.4 us (30%)
  waiting for transfers between devices  27.3 us (23%)
  Pallas kernels  25.1 us (21%)
  between operations  14.2 us (12%)
  starting transfers between devices  12.5 us (11%)
  local copies, waits for them, and re-layouts  2.53 us (2%)
    all_to_all x3, blocking collectives, exchange(): return lax.all_to_all(copies, axis, split_axis=0, concat_axis=0, tiled=True)  35.4 us
    ppermute x8, waiting for transfers between devices, paired(): come = lax.ppermute(array, axis, [(i, i ^ mask) for i in range(size)])  11.7 us
    reduce_scatter x1, waiting for transfers between devices, shards(): lax.psum_scatter(shared, 'row', scatter_dimension=0, tiled=True)  8.55 us
    pallas_call x2, Pallas kernels, back(): pl.pallas_call(functools.partial(back_body, first), out_shape=outs, in_sp...  8 us
    pallas_call x7, Pallas kernels, call(): pl.pallas_call(body, out_shape=out_shape, in_specs=[VMEM] * len(operands)...  7.65 us
    ppermute x7, starting transfers between devices, swap(): lax.ppermute(array, 'row', [(i, i ^ mask) for i in range(row_groups)])  7.18 us
    ppermute x7, waiting for transfers between devices, swap(): lax.ppermute(array, 'row', [(i, i ^ mask) for i in range(row_groups)])  7.03 us
    pallas_call x1, Pallas kernels, share(): pl.pallas_call(functools.partial(share_body, scale), out_shape=made + (sh...  6.1 us
  transfers between devices with their start and end apart: 16, of which 9 were waited for; matrix products, arithmetic and copies ran while one was open for 0% of the time, Pallas kernels for 13%

profile of v9, /device:TPU:0, one launch (start us, length us, event | category | flops | bytes accessed | tf_op | source)
XLA Modules:
  0.0 117.0 jit_solution(17547234214053061814)
XLA Ops:
  7.2 3.3 %shard_map.94 = (f32[8,32,128]{2,1,0:T(8,128)}, f32[512,128]{1,0:T(8,128)}, f32[512,128]{1,0:T(8,128)}, f32[512,128]{1,0:T(8,128)}) custom-call(f32[512,1024]{1,0:T(8,128)} %design_ref.9, f32[4,128]{1,0:T(4,128)} %bitcast.7, s32[4,128]{1,0:T(4,128)} %bitcast.11, s32[8,16]{1,0:T(8,128)} %bitcast.10, s32[1,8]{1,0:T(1,128)} %bitcast.12), custom_call_target="tpu_custom_call" | custom-call | tf_op jit(solution)/shard_map/pallas_call | solution.py:453
  10.6 14.7 %all_to_all.15.parts_ref = f32[8,32,128]{2,1,0:T(8,128)} all-to-all(f32[8,32,128]{2,1,0:T(8,128)} %get-tuple-element.38), channel_id=1, replica_groups=mesh['row'=8,'col'=4] {'row'}, dimensions={0} | all-to-all | bytes 262144 | tf_op jit(solution)/shard_map/all_to_all | solution.py:22
  25.3 6.1 %shard_map.95 = (bf16[8,128,512]{2,1,0:T(8,128)(2,1)}, f32[1,128]{1,0:T(1,128)}, f32[8,128,512]{2,1,0:T(8,128)}) custom-call(f32[8,32,128]{2,1,0:T(8,128)} %all_to_all.15.parts_ref, bf16[256,256]{1,0:T(8,128)(2,1)} %constant.2.clone.walsh_ref, f32[512,1024]{1,0:T(8,128)} %design_ref.9), custom_call_target="tpu_custom_call" | custom-call | tf_op jit(solution)/shard_map/pallas_call | solution.py:480
  31.7 1.1 collective-permute-start.9
  32.8 2.2 %collective-permute-start.10 = (f32[512,128]{1,0:T(8,128)}, f32[512,128]{1,0:T(8,128)S(1)}, u32[]{:S(2)}, u32[]{:S(2)}) collective-permute-start(f32[512,128]{1,0:T(8,128)} %get-tuple-element.62), channel_id=1, source_target_pairs={{0,12},{4,8},{8,4},{12,0},{16,28},{20,24},{24,20},{28,16},{1,13},{... | collective-permute-start | bytes 786440 | tf_op jit(solution)/shard_map/ppermute | solution.py:471
  35.0 0.9 copy-done.1
  35.9 0.7 copy-done.5
  36.6 6.2 %shard_map.96 = (f32[32,128]{1,0:T(8,128)S(1)}, f32[1,128]{1,0:T(1,128)S(1)}, f32[1024,4096]{1,0:T(8,128)S(1)}) custom-call(f32[1024,4096]{1,0:T(8,128)} %rinv_ref.1, f32[8,32,128]{2,1,0:T(8,128)S(1)} %copy-done.1, f32[1,128]{1,0:T(1,128)S(1)} %copy-done.5), custom_call_target="tpu_custom_call" | custom-call | tf_op jit(solution)/shard_map/pallas_call | solution.py:524
  42.9 1.2 %collective-permute-done = f32[32,128]{1,0:T(8,128)S(1)} collective-permute-done((f32[32,128]{1,0:T(8,128)S(1)}, f32[32,128]{1,0:T(8,128)S(1)}, u32[]{:S(2)}, u32[]{:S(2)}) %collective-permute-start) | collective-permute-done | bytes 16416 | tf_op jit(solution)/shard_map/ppermute | solution.py:29
  44.0 1.5 %collective-permute-start.1 = (f32[32,128]{1,0:T(8,128)S(1)}, f32[32,128]{1,0:T(8,128)S(1)}, u32[]{:S(2)}, u32[]{:S(2)}) collective-permute-start(f32[32,128]{1,0:T(8,128)S(1)} %add.14.refs_0_), channel_id=1, source_target_pairs={{0,2},{1,3},{2,0},{3,1},{4,6},{5,7},{6,4},{7,5},{8,10},{9,11},{10,... | collective-permute-start | bytes 49160 | tf_op jit(solution)/shard_map/ppermute | solution.py:29
  45.5 2.2 %collective-permute-done.1.refs_1_.order_ref = f32[32,128]{1,0:T(8,128)S(1)} collective-permute-done((f32[32,128]{1,0:T(8,128)S(1)}, f32[32,128]{1,0:T(8,128)S(1)}, u32[]{:S(2)}, u32[]{:S(2)}) %collective-permute-start.1) | collective-permute-done | bytes 16416 | tf_op jit(solution)/shard_map/ppermute | solution.py:29
  47.8 7.0 %collective-permute-done.10.refs_2_ = f32[512,128]{1,0:T(8,128)S(1)} collective-permute-done((f32[512,128]{1,0:T(8,128)}, f32[512,128]{1,0:T(8,128)S(1)}, u32[]{:S(2)}, u32[]{:S(2)}) %collective-permute-start.10) | collective-permute-done | bytes 262176 | tf_op jit(solution)/shard_map/ppermute | solution.py:471
  54.8 1.1 shard_map.102
  56.0 2.4 %shard_map.97 = (f32[4,128]{1,0:T(4,128)S(1)}, f32[32,128]{1,0:T(8,128)S(1)}, f32[8,128]{1,0:T(8,128)S(1)}, f32[1,128]{1,0:T(1,128)S(1)}) custom-call(f32[1024,4096]{1,0:T(8,128)S(1)} %get-tuple-element.40.rinv_ref, f32[512,1024]{1,0:T(8,128)S(1)} %copy-done, f32[32,128]{1,0:T(8,128)S(1)} %add.14.refs_0_, f32[32,128]{1,0:T(8,128)S(1)} %collective-permute-done.1.refs_1_.order_ref), custom_call_target="tpu_custom_call" | custom-call | tf_op jit(solution)/shard_map/pallas_call | solution.py:52
  58.5 1.1 collective-permute-done.2
  59.6 1.5 %collective-permute-start.3 = (f32[4,128]{1,0:T(4,128)S(1)}, f32[4,128]{1,0:T(4,128)S(1)}, u32[]{:S(2)}, u32[]{:S(2)}) collective-permute-start(f32[4,128]{1,0:T(4,128)S(1)} %add.15.refs_0_), channel_id=1, source_target_pairs={{0,2},{1,3},{2,0},{3,1},{4,6},{5,7},{6,4},{7,5},{8,10},{9,11},{10,... | collective-permute-start | bytes 6152 | tf_op jit(solution)/shard_map/ppermute | solution.py:29
  61.1 2.1 %collective-permute-done.3.refs_1_ = f32[4,128]{1,0:T(4,128)S(1)} collective-permute-done((f32[4,128]{1,0:T(4,128)S(1)}, f32[4,128]{1,0:T(4,128)S(1)}, u32[]{:S(2)}, u32[]{:S(2)}) %collective-permute-start.3) | collective-permute-done | bytes 2080 | tf_op jit(solution)/shard_map/ppermute | solution.py:29
  63.4 11.5 %all_to_all.16.parts_ref = f32[8,16,128]{2,1,0:T(8,128)S(1)} all-to-all(f32[8,16,128]{2,1,0:T(8,128)S(1)} %get-tuple-element.45), channel_id=1, replica_groups=mesh['row'=8,'col'=4] {'row'}, dimensions={0} | all-to-all | bytes 131072 | tf_op jit(solution)/shard_map/all_to_all | solution.py:22
  74.9 1.8 %shard_map.99 = (f32[32,128]{1,0:T(8,128)S(1)}, f32[1,128]{1,0:T(1,128)S(1)}) custom-call(f32[1024,4096]{1,0:T(8,128)S(1)} %get-tuple-element.40.rinv_ref, f32[8,16,128]{2,1,0:T(8,128)S(1)} %all_to_all.16.parts_ref, f32[1,128]{1,0:T(1,128)S(1)} %copy-done.5), custom_call_target="tpu_custom_call" | custom-call | tf_op jit(solution)/shard_map/pallas_call | solution.py:524
  76.8 1.2 %collective-permute-done.4 = f32[32,128]{1,0:T(8,128)S(1)} collective-permute-done((f32[32,128]{1,0:T(8,128)S(1)}, f32[32,128]{1,0:T(8,128)S(1)}, u32[]{:S(2)}, u32[]{:S(2)}) %collective-permute-start.4) | collective-permute-done | bytes 16416 | tf_op jit(solution)/shard_map/ppermute | solution.py:29
  78.0 1.2 %collective-permute-start.5 = (f32[32,128]{1,0:T(8,128)S(1)}, f32[32,128]{1,0:T(8,128)S(1)}, u32[]{:S(2)}, u32[]{:S(2)}) collective-permute-start(f32[32,128]{1,0:T(8,128)S(1)} %add.16.refs_0_), channel_id=1, source_target_pairs={{0,2},{1,3},{2,0},{3,1},{4,6},{5,7},{6,4},{7,5},{8,10},{9,11},{10,... | collective-permute-start | bytes 49160 | tf_op jit(solution)/shard_map/ppermute | solution.py:29
  79.2 0.5 collective-permute-start.12
  79.6 0.8 collective-permute-start.13
  80.5 2.3 %collective-permute-start.14 = (f32[128,128]{1,0:T(8,128)S(1)}, f32[128,128]{1,0:T(8,128)S(1)}, u32[]{:S(2)}, u32[]{:S(2)}) collective-permute-start(f32[128,128]{1,0:T(8,128)S(1)} %get-tuple-element.68), channel_id=1, source_target_pairs={{0,12},{4,8},{8,4},{12,0},{16,28},{20,24},{24,20},{28,16},{1,13},{... | collective-permute-start | bytes 196616 | tf_op jit(solution)/shard_map/ppermute | solution.py:471
  82.7 2.9 %shard_map.100 = (f32[4,128]{1,0:T(4,128)S(1)}, f32[32,128]{1,0:T(8,128)}, f32[8,128]{1,0:T(8,128)S(1)}, f32[1,128]{1,0:T(1,128)S(1)}) custom-call(f32[1024,4096]{1,0:T(8,128)S(1)} %get-tuple-element.40.rinv_ref, f32[512,1024]{1,0:T(8,128)S(1)} %copy-done, f32[32,128]{1,0:T(8,128)S(1)} %add.16.refs_0_, f32[32,128]{1,0:T(8,128)S(1)} %collective-permute-done.5.refs_1_, ...), custom_call_target="tpu_custom_call" | custom-call | tf_op jit(solution)/shard_map/pallas_call | solution.py:52
  85.7 1.2 collective-permute-done.6
  86.8 0.8 collective-permute-start.7
  87.7 2.7 %collective-permute-done.7.refs_1_ = f32[4,128]{1,0:T(4,128)S(1)} collective-permute-done((f32[4,128]{1,0:T(4,128)S(1)}, f32[4,128]{1,0:T(4,128)S(1)}, u32[]{:S(2)}, u32[]{:S(2)}) %collective-permute-start.7) | collective-permute-done | bytes 2080 | tf_op jit(solution)/shard_map/ppermute | solution.py:29
  90.5 9.2 %all_to_all.17.parts_ref = f32[8,8,128]{2,1,0:T(8,128)S(1)} all-to-all(f32[8,8,128]{2,1,0:T(8,128)S(1)} %get-tuple-element.52), channel_id=1, replica_groups=mesh['row'=8,'col'=4] {'row'}, dimensions={0} | all-to-all | bytes 65536 | tf_op jit(solution)/shard_map/all_to_all | solution.py:22
  99.8 8.6 %reduce-scatter.2.cloned.1.call-done.refs_10_ = f32[128,512]{1,0:T(8,128)} async-done(((f32[1024,512]{1,0:T(8,128)}), f32[128,512]{1,0:T(8,128)}) %reduce-scatter.2.cloned.1.call-update) | async-done | bytes 262160 | tf_op jit(solution)/shard_map/reduce_scatter | solution.py:563
  108.3 0.9 copy-done.3
  109.3 0.9 shard_map.104
  (31 shorter events, 1.0 us)
Async XLA Ops:
  7.2 47.6 %copy-start = (f32[512,1024]{1,0:T(8,128)S(1)}, f32[512,1024]{1,0:T(8,128)}, u32[]{:S(2)}) copy-start(f32[512,1024]{1,0:T(8,128)} %design_ref.9) | copy-start | bytes 6291460
  7.2 101.1 %reduce-scatter.2.cloned.1.call-start = ((), (), s32[]{:S(2)}) async-start(), calls=%async_computation.4 | async-start | bytes 2359296 | tf_op jit(solution)/shard_map/reduce_scatter | solution.py:563
  31.4 23.4 %copy-start.2 = (bf16[8,128,512]{2,1,0:T(8,128)(2,1)S(1)}, bf16[8,128,512]{2,1,0:T(8,128)(2,1)}, u32[]{:S(2)}) copy-start(bf16[8,128,512]{2,1,0:T(8,128)(2,1)} %get-tuple-element.56.mix_ref) | copy-start | bytes 3145732
  31.5 16.3 %collective-permute-start.8 = (f32[512,128]{1,0:T(8,128)}, f32[512,128]{1,0:T(8,128)S(1)}, u32[]{:S(2)}, u32[]{:S(2)}) collective-permute-start(f32[512,128]{1,0:T(8,128)} %get-tuple-element.60), channel_id=1, source_target_pairs={{0,4},{4,0},{8,12},{12,8},{16,20},{20,16},{24,28},{28,24},{1,5},{5... | collective-permute-start | bytes 786440 | tf_op jit(solution)/shard_map/ppermute | solution.py:471
  31.7 16.0 %collective-permute-start.9 = (f32[512,128]{1,0:T(8,128)}, f32[512,128]{1,0:T(8,128)S(1)}, u32[]{:S(2)}, u32[]{:S(2)}) collective-permute-start(f32[512,128]{1,0:T(8,128)} %get-tuple-element.61), channel_id=1, source_target_pairs={{0,8},{4,12},{8,0},{12,4},{16,24},{20,28},{24,16},{28,20},{1,9},{5... | collective-permute-start | bytes 786440 | tf_op jit(solution)/shard_map/ppermute | solution.py:471
  32.8 22.0 %collective-permute-start.10 = (f32[512,128]{1,0:T(8,128)}, f32[512,128]{1,0:T(8,128)S(1)}, u32[]{:S(2)}, u32[]{:S(2)}) collective-permute-start(f32[512,128]{1,0:T(8,128)} %get-tuple-element.62), channel_id=1, source_target_pairs={{0,12},{4,8},{8,4},{12,0},{16,28},{20,24},{24,20},{28,16},{1,13},{... | collective-permute-start | bytes 786440 | tf_op jit(solution)/shard_map/ppermute | solution.py:471
  35.0 0.9 copy-start.1
  35.9 0.7 copy-start.5
  36.6 26.6 %copy-start.4 = (f32[512]{0:T(512)S(1)}, f32[512]{0:T(512)}, u32[]{:S(2)}) copy-start(f32[512]{0:T(512)} %param.11) | copy-start | bytes 6148
  42.8 1.2 %collective-permute-start = (f32[32,128]{1,0:T(8,128)S(1)}, f32[32,128]{1,0:T(8,128)S(1)}, u32[]{:S(2)}, u32[]{:S(2)}) collective-permute-start(f32[32,128]{1,0:T(8,128)S(1)} %get-tuple-element.41), channel_id=1, source_target_pairs={{0,1},{1,0},{2,3},{3,2},{4,5},{5,4},{6,7},{7,6},{8,9},{9,8},{10,11... | collective-permute-start | bytes 49160 | tf_op jit(solution)/shard_map/ppermute | solution.py:29
  44.0 3.7 %collective-permute-start.1 = (f32[32,128]{1,0:T(8,128)S(1)}, f32[32,128]{1,0:T(8,128)S(1)}, u32[]{:S(2)}, u32[]{:S(2)}) collective-permute-start(f32[32,128]{1,0:T(8,128)S(1)} %add.14.refs_0_), channel_id=1, source_target_pairs={{0,2},{1,3},{2,0},{3,1},{4,6},{5,7},{6,4},{7,5},{8,10},{9,11},{10,... | collective-permute-start | bytes 49160 | tf_op jit(solution)/shard_map/ppermute | solution.py:29
  55.9 23.3 %collective-permute-start.11 = (f32[1,4,128,128]{3,2,1,0:T(8,128)S(1)}, f32[1,4,128,128]{3,2,1,0:T(8,128)S(1)}, u32[]{:S(2)}, u32[]{:S(2)}) collective-permute-start(f32[1,4,128,128]{3,2,1,0:T(8,128)S(1)} %get-tuple-element.64), channel_id=1, source_target_pairs={{0,16},{4,20},{8,24},{12,28},{16,0},{20,4},{24,8},{28,12},{1,17},{... | collective-permute-start | bytes 786440 | tf_op jit(solution)/shard_map/ppermute | solution.py:471
  58.4 1.2 %collective-permute-start.2 = (f32[4,128]{1,0:T(4,128)S(1)}, f32[4,128]{1,0:T(4,128)S(1)}, u32[]{:S(2)}, u32[]{:S(2)}) collective-permute-start(f32[4,128]{1,0:T(4,128)S(1)} %get-tuple-element.42), channel_id=1, source_target_pairs={{0,1},{1,0},{2,3},{3,2},{4,5},{5,4},{6,7},{7,6},{8,9},{9,8},{10,11... | collective-permute-start | bytes 6152 | tf_op jit(solution)/shard_map/ppermute | solution.py:29
  59.6 3.6 %collective-permute-start.3 = (f32[4,128]{1,0:T(4,128)S(1)}, f32[4,128]{1,0:T(4,128)S(1)}, u32[]{:S(2)}, u32[]{:S(2)}) collective-permute-start(f32[4,128]{1,0:T(4,128)S(1)} %add.15.refs_0_), channel_id=1, source_target_pairs={{0,2},{1,3},{2,0},{3,1},{4,6},{5,7},{6,4},{7,5},{8,10},{9,11},{10,... | collective-permute-start | bytes 6152 | tf_op jit(solution)/shard_map/ppermute | solution.py:29
  76.7 1.2 %collective-permute-start.4 = (f32[32,128]{1,0:T(8,128)S(1)}, f32[32,128]{1,0:T(8,128)S(1)}, u32[]{:S(2)}, u32[]{:S(2)}) collective-permute-start(f32[32,128]{1,0:T(8,128)S(1)} %get-tuple-element.46), channel_id=1, source_target_pairs={{0,1},{1,0},{2,3},{3,2},{4,5},{5,4},{6,7},{7,6},{8,9},{9,8},{10,11... | collective-permute-start | bytes 49160 | tf_op jit(solution)/shard_map/ppermute | solution.py:29
  78.0 4.8 %collective-permute-start.5 = (f32[32,128]{1,0:T(8,128)S(1)}, f32[32,128]{1,0:T(8,128)S(1)}, u32[]{:S(2)}, u32[]{:S(2)}) collective-permute-start(f32[32,128]{1,0:T(8,128)S(1)} %add.16.refs_0_), channel_id=1, source_target_pairs={{0,2},{1,3},{2,0},{3,1},{4,6},{5,7},{6,4},{7,5},{8,10},{9,11},{10,... | collective-permute-start | bytes 49160 | tf_op jit(solution)/shard_map/ppermute | solution.py:29
  79.2 20.6 %collective-permute-start.12 = (f32[128,128]{1,0:T(8,128)S(1)}, f32[128,128]{1,0:T(8,128)S(1)}, u32[]{:S(2)}, u32[]{:S(2)}) collective-permute-start(f32[128,128]{1,0:T(8,128)S(1)} %get-tuple-element.66), channel_id=1, source_target_pairs={{0,4},{4,0},{8,12},{12,8},{16,20},{20,16},{24,28},{28,24},{1,5},{5... | collective-permute-start | bytes 196616 | tf_op jit(solution)/shard_map/ppermute | solution.py:471
  79.6 20.1 %collective-permute-start.13 = (f32[128,128]{1,0:T(8,128)S(1)}, f32[128,128]{1,0:T(8,128)S(1)}, u32[]{:S(2)}, u32[]{:S(2)}) collective-permute-start(f32[128,128]{1,0:T(8,128)S(1)} %get-tuple-element.67), channel_id=1, source_target_pairs={{0,8},{4,12},{8,0},{12,4},{16,24},{20,28},{24,16},{28,20},{1,9},{5... | collective-permute-start | bytes 196616 | tf_op jit(solution)/shard_map/ppermute | solution.py:471
  80.5 19.3 %collective-permute-start.14 = (f32[128,128]{1,0:T(8,128)S(1)}, f32[128,128]{1,0:T(8,128)S(1)}, u32[]{:S(2)}, u32[]{:S(2)}) collective-permute-start(f32[128,128]{1,0:T(8,128)S(1)} %get-tuple-element.68), channel_id=1, source_target_pairs={{0,12},{4,8},{8,4},{12,0},{16,28},{20,24},{24,20},{28,16},{1,13},{... | collective-permute-start | bytes 196616 | tf_op jit(solution)/shard_map/ppermute | solution.py:471
  85.7 1.2 collective-permute-start.6
  86.8 3.6 %collective-permute-start.7 = (f32[4,128]{1,0:T(4,128)S(1)}, f32[4,128]{1,0:T(4,128)S(1)}, u32[]{:S(2)}, u32[]{:S(2)}) collective-permute-start(f32[4,128]{1,0:T(4,128)S(1)} %add.17.refs_0_), channel_id=1, source_target_pairs={{0,2},{1,3},{2,0},{3,1},{4,6},{5,7},{6,4},{7,5},{8,10},{9,11},{10,... | collective-permute-start | bytes 6152 | tf_op jit(solution)/shard_map/ppermute | solution.py:29
  108.3 0.9 copy-start.3
Sparse Core Ops, SparseCore 0:
  31.6 76.6 reduce-scatter.1

commit v10 on v9

--- a/solution.py
+++ b/solution.py
@@ -13,9 +13,11 @@
 ITERS = 2
 LANE = 128
 NEAR = 4
+CHUNKS = 2
 F32 = jnp.float32
 VMEM = pl.BlockSpec(memory_space=pltpu.VMEM)
 HBM = pl.BlockSpec(memory_space=pltpu.HBM)
+ANY = pl.BlockSpec(memory_space=pl.ANY)
 
 
 def exchange(copies, axis):
@@ -128,16 +130,11 @@
 
 
 def picks_at(width):
-    return message_rows(width)
+    return width // LANE + 1
 
 
 def signs_at(width, groups):
-    return message_rows(width) + rounded(groups, 8)
-
-
-def columns_traded(width):
-    unit = NEAR * LANE
-    return max(unit, width // 2 // unit * unit)
+    return picks_at(width) + groups * PAIR // LANE
 
 
 def copy_out(out_ref):
@@ -170,7 +167,8 @@
     away = []
     for index, away_ref in enumerate(away_refs):
         piece = away_ref.shape[1]
-        column = pl.multiple_of(width - NEAR * piece + (place ^ (index + 1)) * piece, LANE)
+        chunk, mask = index // (NEAR - 1), index % (NEAR - 1) + 1
+        column = pl.multiple_of((place ^ mask) * (width // NEAR) + chunk * piece, LANE)
         source = design.at[:, pl.ds(column, piece)]
         away.append(pltpu.make_async_copy(source, away_ref, sems.at[4 + lines + index]))
     for copy in small + large:
@@ -185,7 +183,9 @@
     slot = lax.broadcasted_iota(jnp.int32, picks.shape, 1).astype(F32)
     coded = jnp.where(slot < limit, picks[...].astype(F32), -1.0)
     start = picks_at(width)
-    out_ref[0, start : start + groups, : coded.shape[1]] = coded
+    for owner in range(0, groups, LANE // PAIR):
+        line = jnp.concatenate([coded[i : i + 1, :] for i in range(owner, owner + LANE // PAIR)], axis=1)
+        out_ref[0, start + owner * PAIR // LANE : start + owner * PAIR // LANE + 1, :] = line
     start = signs_at(width, groups)
     out_ref[0, start : start + lines, :] = (2 * bits[...] - 1).astype(F32)
     target = target_here[...]
@@ -206,7 +206,7 @@
         copy.wait()
 
 
-def back_body(first, rinv_ref, parts_ref, order_ref, term_ref, beta_ref, *refs):
+def back_body(first, rinv_ref, parts_ref, term_ref, beta_ref, *refs):
     tiles = rinv_ref.shape[0] // LANE
     copies = []
     if first:
@@ -224,24 +224,25 @@
     left_product_long(scratch, rinv_here, term_ref, copies)
 
 
-def forward_body(groups, first, rinv_ref, design_ref, *refs):
+def forward_body(groups, first, last, rinv_ref, design_ref, *refs):
     right = tree([ref[...] for ref in refs[:groups]])
     refs = refs[groups:]
     if not first:
         before_ref, beta_ref, *refs = refs
         right = right - beta_ref[...] * before_ref[...]
-    image_ref, right_ref, held_ref, alpha_ref = refs
+    image_ref, held_ref, alpha_ref, *right_refs = refs
     alpha = jnp.sqrt(total(right * right))
     alpha_ref[...] = splat(alpha)
     right = right / alpha
-    right_ref[...] = right
+    if not last:
+        right_refs[0][...] = right
     right_product(rinv_ref, right, held_ref)
     right_product(design_ref, held_ref[...], image_ref)
 
 
 def turn_body(groups, last, *refs):
     left = tree([ref[...] for ref in refs[:groups]])
-    before_ref, beta_ref, alpha_ref, *refs = refs[groups:]
+    before_ref, beta_ref, alpha_ref, token_ref, *refs = refs[groups:]
     left = left - alpha_ref[...] * (before_ref[...] / beta_ref[...])
     square = splat(total(left * left))
     if last:
@@ -274,81 +275,34 @@
         lax.fori_loop(0, groups, step, 0)
 
 
-def mix_rows(parts_ref, walsh_ref, width, block, groups, rows):
+def mix_body(width, parts_ref, walsh_ref, mix_ref):
+    groups, _, rows = mix_ref.shape
     me = lax.axis_index("row")
-    start = picks_at(width)
-    local = lax.broadcasted_iota(jnp.int32, (PAIR, rows), 1).astype(F32)
-    coded = [parts_ref[block, pl.ds(start + (apart ^ me), 1), :] for apart in range(groups)]
-    coded = jnp.concatenate(coded + [jnp.zeros((LANE - groups, LANE), F32)], axis=0).T
-    parity = jnp.int32(0)
-    for bit in range(groups.bit_length() - 1):
-        parity = parity ^ ((block & me) >> bit)
-    sign = (1 - 2 * (parity & 1)).astype(F32)
-    chosen = []
-    for apart in range(groups):
-        match = jnp.broadcast_to(coded[:PAIR, apart : apart + 1], (PAIR, rows)) == local
-        chosen.append(jnp.where(match, sign, 0.0))
-    chosen = jnp.concatenate(chosen, axis=0).astype(jnp.bfloat16)
-    mixed = []
-    for part in range(rows // HB):
-        mix = jnp.dot(chosen[:, part * HB : (part + 1) * HB], walsh_ref[...], preferred_element_type=F32)
-        mixed.append(mix.astype(jnp.bfloat16))
-    return jnp.concatenate(mixed, axis=1)
-
-
-def mix_body(width, parts_ref, walsh_ref, mix_ref, token_ref):
-    token_ref[...] = parts_ref[0, :1, :]
-    groups, _, rows = mix_ref.shape
+    local = lax.broadcasted_iota(jnp.int32, (LANE, rows), 1).astype(F32)
+    per = LANE // PAIR
 
     def step(block, carry):
-        mix_ref[block] = mix_rows(parts_ref, walsh_ref, width, block, groups, rows)
+        parity = jnp.int32(0)
+        for bit in range(groups.bit_length() - 1):
+            parity = parity ^ ((block & me) >> bit)
+        sign = (1 - 2 * (parity & 1)).astype(F32)
+        for line in range(groups // per):
+            start = picks_at(width) + line
+            coded = across(parts_ref[block, start : start + 1, :])
+            match = jnp.concatenate([coded] * (rows // LANE), axis=1) == local
+            chosen = jnp.where(match, sign, 0.0).astype(jnp.bfloat16)
+            for part in range(rows // HB):
+                columns = slice(part * HB, (part + 1) * HB)
+                mixed = jnp.dot(chosen[:, columns], walsh_ref[...], preferred_element_type=F32).astype(jnp.bfloat16)
+                for index in range(per):
+                    place = pl.multiple_of(((line * per + index) ^ me) * PAIR, PAIR)
+                    mix_ref[block, pl.ds(place, PAIR), columns] = mixed[index * PAIR : (index + 1) * PAIR, :]
         return carry
 
     for_blocks(groups, step)
 
 
-def share_body(scale, parts_ref, walsh_ref, design_ref, mix_ref, token_ref, out_ref, here, both, share, sems):
-    token_ref[...] = parts_ref[0, :1, :]
-    groups, _, columns = share.shape
-    rows, width = design_ref.shape
-    fetch = pltpu.make_async_copy(design_ref.at[:, pl.ds(0, columns)], here, sems.at[groups])
-    fetch.start()
-    me = lax.axis_index("row")
-
-    def mix(block, carry):
-        mix_ref[block] = mix_rows(parts_ref, walsh_ref, width, block, groups, rows)
-        return carry
-
-    for_blocks(groups, mix)
-    fetch.wait()
-    start = signs_at(width, groups)
-    for line in range(rows // LANE):
-        part = slice(line * LANE, (line + 1) * LANE)
-        sign = across(parts_ref[me, start + line : start + line + 1, :])
-        for tile in range(0, columns, LANE):
-            place = slice(tile, tile + LANE)
-            both[0, part, place], both[1, part, place] = pieces(here[part, place] * sign)
-
-    def out_copy(block):
-        slot = pl.ds(block * PAIR, PAIR)
-        return pltpu.make_async_copy(share.at[:, slot, :], out_ref.at[:, slot, :], sems.at[block])
-
-    def step(block, carry):
-        value = weigh(mix_ref[block], both[0], both[1]) / scale
-        for apart in range(groups):
-            share[apart ^ me, pl.ds(block * PAIR, PAIR), :] = value[apart * PAIR : (apart + 1) * PAIR, :]
-        out_copy(block).start()
-        return carry
-
-    def finish(block, carry):
-        out_copy(block).wait()
-        return carry
-
-    for_blocks(groups, step)
-    for_blocks(groups, finish)
-
-
-def sample_body(scale, design_ref, parts_ref, mix_ref, order_ref, *refs):
+def sample_body(scale, start, design_ref, parts_ref, mix_ref, order_ref, *refs):
     near, (keep_ref, send_ref, both) = refs[: NEAR - 1], refs[NEAR - 1 :]
     rows, piece = near[0].shape
     width = design_ref.shape[1]
@@ -359,7 +313,7 @@
         part = slice(line * LANE, (line + 1) * LANE)
         signs = [across(parts_ref[me ^ mask, signs_start + line : signs_start + line + 1, :]) for mask in range(NEAR)]
         for tile in range(0, piece, LANE):
-            column = pl.multiple_of(width - NEAR * piece + me % NEAR * piece + tile, LANE)
+            column = pl.multiple_of(me % NEAR * (width // NEAR) + start + tile, LANE)
             here = slice(tile, tile + LANE)
             values = [design_ref[part, pl.ds(column, LANE)]] + [ref[part, here] for ref in near]
             values = [value * sign for value, sign in zip(values, signs)]
@@ -391,22 +345,37 @@
     send_ref[...] = kept_ref[half:] + arrived_ref[half:]
 
 
-def split_body(kept_ref, arrived_ref, order_ref, *out_refs):
-    for index, out_ref in enumerate(out_refs):
-        out_ref[...] = kept_ref[0, index] + arrived_ref[0, index]
+def join_body(kept_ref, arrived_ref, order_ref, out_ref, token_ref):
+    token_ref[...] = order_ref[:1, :]
+    out_ref[...] = kept_ref[0] + arrived_ref[0]
+
+
+def touch_body(*refs):
+    order_ref, token_ref = refs[-2:]
+    token_ref[...] = order_ref[:1, :]
+
+
+def split_body(chunks, *refs):
+    joined, (kept_ref, arrived_ref, order_ref, token_ref, *out_refs) = refs[: chunks - 1], refs[chunks - 1 :]
+    token_ref[...] = order_ref[:1, :]
+    piece = kept_ref.shape[3]
+    for chunk in range(chunks):
+        columns = slice(chunk * piece, (chunk + 1) * piece)
+        for index, out_ref in enumerate(out_refs):
+            if chunk < chunks - 1:
+                out_ref[:, columns] = joined[chunk][index]
+            else:
+                out_ref[:, columns] = kept_ref[0, index] + arrived_ref[0, index]
 
 
 def last_body(parts_ref, left_ref, *refs):
     basis_ref, solution_ref, sketch_ref = refs[-3:]
-    quarters, summed = refs[3 * ITERS : 3 * ITERS + NEAR], refs[3 * ITERS + NEAR : -3]
+    quarters = refs[3 * ITERS : 3 * ITERS + NEAR]
     place = lax.axis_index("row") % NEAR
     piece = quarters[0].shape[1]
-    width = sketch_ref.shape[1]
-    for ref in summed:
-        sketch_ref[:, : width - NEAR * piece] = ref[...]
     for mask, part_ref in enumerate(quarters):
         for tile in range(0, piece, LANE):
-            column = pl.multiple_of(width - NEAR * piece + (place ^ mask) * piece + tile, LANE)
+            column = pl.multiple_of((place ^ mask) * piece + tile, LANE)
             sketch_ref[:, pl.ds(column, LANE)] = part_ref[:, tile : tile + LANE]
     betas = [ref[...] for ref in refs[:ITERS]]
     alphas = [ref[...] for ref in refs[ITERS : 2 * ITERS]]
@@ -444,25 +413,25 @@
     deep = message_rows(width)
     left = target.reshape(lines, LANE)
     bits = sign_bits.reshape(lines, LANE)
-    piece = columns_traded(width) // NEAR
-    rest = width - NEAR * piece
+    chunks = min(CHUNKS, width // NEAR // LANE)
+    piece = width // NEAR // chunks
     scale = float(np.sqrt(np.float32(rows * row_groups)))
     slots = row_groups * PAIR
     far = row_groups // NEAR
 
     message, *away = pl.pallas_call(
         first_body,
-        out_shape=(shape(row_groups, signs_at(width, row_groups) + rounded(lines, 8), LANE),)
-        + (shape(rows, piece),) * (NEAR - 1),
+        out_shape=(shape(row_groups, rounded(signs_at(width, row_groups) + lines, 8), LANE),)
+        + (shape(rows, piece),) * (chunks * (NEAR - 1)),
         in_specs=[HBM] * 5,
-        out_specs=(VMEM,) + (HBM,) * (NEAR - 1),
+        out_specs=(VMEM,) + (HBM,) * (chunks * (NEAR - 1)),
         scratch_shapes=[
             pltpu.VMEM((rows, width), F32),
             pltpu.VMEM((lines, LANE), F32),
             pltpu.VMEM((lines, LANE), jnp.int32),
             pltpu.VMEM((row_groups, PAIR), jnp.int32),
             pltpu.VMEM((1, row_groups), jnp.int32),
-            pltpu.SemaphoreType.DMA((4 + lines + NEAR - 1,)),
+            pltpu.SemaphoreType.DMA((4 + lines + chunks * (NEAR - 1),)),
         ],
         compiler_params=pltpu.CompilerParams(vmem_limit_bytes=58 << 20),
     )(design, left, bits, picks.reshape(row_groups, PAIR), counts.reshape(1, row_groups))
@@ -470,38 +439,26 @@
     def swap(array, mask):
         return lax.ppermute(array, "row", [(i, i ^ mask) for i in range(row_groups)])
 
-    signs = jnp.asarray(walsh(HB), jnp.bfloat16)
-    made = (shape(row_groups, slots, rows, dtype=jnp.bfloat16), scalar)
-
     def mix(message):
-        return call(functools.partial(mix_body, width), made, message, signs)
-
-    def share(message):
-        return pl.pallas_call(
-            functools.partial(share_body, scale),
-            out_shape=made + (shape(row_groups, slots, rest),),
-            in_specs=[VMEM, VMEM, HBM],
-            out_specs=(VMEM, VMEM, HBM),
-            scratch_shapes=[
-                pltpu.VMEM((rows, rest), F32),
-                pltpu.VMEM((2, rows, rest), jnp.bfloat16),
-                pltpu.VMEM((row_groups, slots, rest), F32),
-                pltpu.SemaphoreType.DMA((row_groups + 1,)),
-            ],
-            compiler_params=pltpu.CompilerParams(vmem_limit_bytes=57 << 20),
-        )(message, signs, design)
-
-    def sample(mixed, order):
+        made = shape(row_groups, slots, rows, dtype=jnp.bfloat16)
+        return call(functools.partial(mix_body, width), made, message, jnp.asarray(walsh(HB), jnp.bfloat16))
+
+    def sample(chunk, mixed, order):
         return call(
-            functools.partial(sample_body, scale),
+            functools.partial(sample_body, scale, chunk * piece),
             (shape(far // 2, NEAR, slots, piece),) * 2,
             design,
             picked,
             mixed,
             order,
-            *near,
+            *near[chunk],
             scratch=[pltpu.VMEM((NEAR, 2, rows, piece), jnp.bfloat16)],
         )
+
+    def spread(chunk, masks, order):
+        parts = [away[chunk * (NEAR - 1) + mask - 1] for mask in masks]
+        parts, _ = lax.optimization_barrier((parts, order))
+        return [swap(part, mask) for mask, part in zip(masks, parts)]
 
     def halve(keep, come, order):
         bit = row_groups // 2
@@ -512,11 +469,21 @@
             come = swap(send, bit)
         return keep, come
 
-    def trade(keep, come, order):
-        mine, *others = call(split_body, (shape(slots, piece),) * NEAR, *halve(keep, come, order), order)
-        return [mine] + [swap(part, mask + 1) for mask, part in enumerate(others)]
-
-    def back(rinv, message, order, first):
+    def join(keep, come, order):
+        keep, come = halve(keep, come, order)
+        return call(join_body, (shape(*keep.shape[1:]), scalar), keep, come, order)
+
+    def trade(joined, keep, come, order):
+        token, mine, *others = call(
+            functools.partial(split_body, chunks),
+            (scalar,) + (shape(slots, width // NEAR),) * NEAR,
+            *joined,
+            *halve(keep, come, order),
+            order,
+        )
+        return [mine] + [swap(part, mask + 1) for mask, part in enumerate(others)], token
+
+    def back(rinv, message, first):
         outs, scratch = (shape(whole // LANE, LANE), scalar), [pltpu.VMEM((width // LANE, LANE), F32)]
         if first:
             outs += (shape(*rinv.shape),)
@@ -524,23 +491,24 @@
         return pl.pallas_call(
             functools.partial(back_body, first),
             out_shape=outs,
-            in_specs=[HBM if first else VMEM, VMEM, VMEM],
+            in_specs=[HBM if first else VMEM, VMEM],
             out_specs=(VMEM,) * len(outs),
             scratch_shapes=scratch,
             compiler_params=pltpu.CompilerParams(vmem_limit_bytes=(34 if first else 24) << 20),
-            )(rinv, message, order)
-
-    def forward(terms, *before):
+            )(rinv, message)
+
+    def forward(terms, last, *before):
         return call(
-            functools.partial(forward_body, 2, not before),
-            (shape(lines, LANE), shape(whole // LANE, LANE), shape(width // LANE, LANE), scalar),
+            functools.partial(forward_body, len(terms), not before, last),
+            (shape(lines, LANE), shape(width // LANE, LANE), scalar)
+            + (() if last else (shape(whole // LANE, LANE),)),
             here,
             design,
             *terms,
             *before,
         )
 
-    def turn(images, left, beta, alpha, last):
+    def turn(images, left, beta, alpha, token, last):
         return call(
             functools.partial(turn_body, 2, last),
             (shape(lines, LANE), shape(row_groups, 8 if last else deep, LANE)),
@@ -548,37 +516,52 @@
             left,
             beta,
             alpha,
+            token,
             *(() if last else (design,)),
         )
 
-    betas, alphas, held, summed = [], [], [], []
+    betas, alphas, held, joined = [], [], [], []
     message = picked = exchange(message, "row")
-    away, _ = lax.optimization_barrier((away, message))
-    near = [swap(part, mask + 1) for mask, part in enumerate(away)]
-    if rest == 0:
-        mixed, token = mix(message)
-    else:
-        mixed, token, shared = share(message)
-        shared = shared.reshape(row_groups * slots, rest)
-        summed.append(lax.psum_scatter(shared, "row", scatter_dimension=0, tiled=True))
+    near = [spread(0, (1, 2, 3), message)]
+    right = []
     for step in range(ITERS):
         last = step + 1 == ITERS
         if step == 0:
-            term, beta, here = back(rinv, message, token, True)
+            term, beta, here = back(rinv, message, True)
+            mixed = mix(message)
         else:
-            term, beta = back(here, message, token, False)
-            quarters = trade(keep, come, beta)
+            term, beta = back(here, message, False)
         betas.append(beta)
         terms = paired(term, "col")
         if step == 0:
-            keep, send = sample(mixed, terms[1])
+            near += [spread(chunk, (1, 2), terms[1]) for chunk in range(1, chunks)]
+            keep, send = sample(0, mixed, terms[1])
             come = swap(send, row_groups // 2)
-        image, right, kept, alpha = forward(terms, *(() if step == 0 else (right, beta)))
+        elif chunks > 1:
+            keep, send = sample(1, mixed, terms[1])
+            come = swap(send, row_groups // 2)
+        image, kept, alpha, *right = forward(terms, last, *right, *betas[1:])
         alphas.append(alpha)
         held.append(kept)
         images = paired(image, "col")
-        left, message = turn(images, left, beta, alpha, last)
+        token = alpha
+        if chunks > 1 and step == 0:
+            part, token = join(keep, come, alpha)
+            joined.append(part)
+            there = [array for arrays in near[1:] for array in arrays]
+            token = pl.pallas_call(
+                touch_body,
+                out_shape=scalar,
+                in_specs=[ANY] * len(there) + [VMEM],
+                out_specs=VMEM,
+            )(*there, token)
+        if last:
+            quarters, token = trade(joined, keep, come, alpha)
+        left, message = turn(images, left, beta, alpha, token, last)
         message = exchange(message, "row")
+        if step == 0:
+            for chunk in range(1, chunks):
+                near[chunk] += spread(chunk, (3,), message)
     basis, answer, sketch = call(
         last_body,
         (shape(lines, LANE), shape(width // LANE, LANE), shape(slots, width)),
@@ -588,7 +571,6 @@
         *alphas,
         *held,
         *quarters,
-        *summed,
     )
     return (sketch, answer.reshape(-1), basis.reshape(-1))
 

time: 117 us -> 112 us (0.957)
  between operations: 14.2 us -> 0.83 us
  local copies, waits for them, and re-layouts: 2.53 us -> 14.2 us
  waiting for transfers between devices: 27.3 us -> 23.9 us
  Pallas kernels: 25.1 us -> 22.8 us
  starting transfers between devices: 12.5 us -> 14.7 us
    unnamed x12 -> x28, local copies, waits for them, and re-layouts: 2.53 us -> 14.2 us
    reduce_scatter x1 -> x0, waiting for transfers between devices: 8.55 us -> none  [shards(): lax.psum_scatter(shared, 'row', scatter_dimension=0, tiled=True)]
    pallas_call x2, Pallas kernels: 9.44 us -> 4.76 us  [the longest x1 3.59 us: shards(): pl.pallas_call(first_body, out_shape=(shape(row_groups, rounded(signs_at(...]
    ppermute x7 -> x11, waiting for transfers between devices: 7.03 us -> 11.2 us  [swap(): lax.ppermute(array, 'row', [(i, i ^ mask) for i in range(row_groups)])]
    ppermute x7 -> x11, starting transfers between devices: 7.18 us -> 10.5 us  [swap(): lax.ppermute(array, 'row', [(i, i ^ mask) for i in range(row_groups)])]
    pallas_call x7 -> x10, Pallas kernels: 7.65 us -> 9.89 us  [call(): pl.pallas_call(body, out_shape=out_shape, in_specs=[VMEM] * len(operands)...]
  transfers between devices with their start and end apart: 16 -> 19, of which waited for: 9 -> 9; matrix products, arithmetic and copies ran while one was open for 0% -> 0% of each run, Pallas kernels for 13% -> 13%
where the time goes in v10:
time: 112 us
  blocking collectives  35.5 us (32%)
  waiting for transfers between devices  23.9 us (21%)
  Pallas kernels  22.8 us (20%)
  starting transfers between devices  14.7 us (13%)
  local copies, waits for them, and re-layouts  14.2 us (13%)
    all_to_all x3, blocking collectives, exchange(): return lax.all_to_all(copies, axis, split_axis=0, concat_axis=0, tiled=True)  35.5 us
    unnamed x28, local copies, waits for them, and re-layouts  14.2 us
    ppermute x8, waiting for transfers between devices, paired(): come = lax.ppermute(array, axis, [(i, i ^ mask) for i in range(size)])  12.7 us
    ppermute x11, waiting for transfers between devices, swap(): lax.ppermute(array, 'row', [(i, i ^ mask) for i in range(row_groups)])  11.2 us
    ppermute x11, starting transfers between devices, swap(): lax.ppermute(array, 'row', [(i, i ^ mask) for i in range(row_groups)])  10.5 us
    pallas_call x10, Pallas kernels, call(): pl.pallas_call(body, out_shape=out_shape, in_specs=[VMEM] * len(operands)...  9.89 us
    pallas_call x2, Pallas kernels, back(): pl.pallas_call(functools.partial(back_body, first), out_shape=outs, in_sp...  8.11 us
    ppermute x8, starting transfers between devices, paired(): come = lax.ppermute(array, axis, [(i, i ^ mask) for i in range(size)])  4.19 us
  transfers between devices with their start and end apart: 19, of which 9 were waited for; matrix products, arithmetic and copies ran while one was open for 0% of the time, Pallas kernels for 13%

profile of v10, /device:TPU:0, one launch (start us, length us, event | category | flops | bytes accessed | tf_op | source)
XLA Modules:
  0.0 111.8 jit_solution(338523487321765062)
XLA Ops:
  0.7 3.6 %shard_map.94 = (f32[8,16,128]{2,1,0:T(8,128)}, f32[512,128]{1,0:T(8,128)}, f32[512,128]{1,0:T(8,128)}, f32[512,128]{1,0:T(8,128)}, f32[512,128]{1,0:T(8,128)}, /*index=5*/f32[512,128]{1,0:T(8,128)}, f32[512,128]{1,0:T(8,128)}) custom-call(f32[512,1024]{1,0:T(8,128)} %design_ref.9, f32[4,128]{1,0:T(4,128)} %bitcast.6, s32[4,128]{1,0:T(4,128)} %bitcast.9, ...), custom_call_target="tpu_custom_call" | custom-call | tf_op jit(solution)/shard_map/pallas_call | solution.py:422
  4.3 14.3 %all_to_all.15.parts_ref = f32[8,16,128]{2,1,0:T(8,128)S(1)} all-to-all(f32[8,16,128]{2,1,0:T(8,128)} %get-tuple-element.46), channel_id=1, replica_groups=mesh['row'=8,'col'=4] {'row'}, dimensions={0} | all-to-all | bytes 131072 | tf_op jit(solution)/shard_map/all_to_all | solution.py:24
  19.0 0.8 collective-permute-start.7
  19.8 2.3 %collective-permute-start.8 = (f32[512,128]{1,0:T(8,128)}, f32[512,128]{1,0:T(8,128)S(1)}, u32[]{:S(2)}, u32[]{:S(2)}) collective-permute-start(f32[512,128]{1,0:T(8,128)} %get-tuple-element.61), channel_id=1, source_target_pairs={{0,12},{4,8},{8,4},{12,0},{16,28},{20,24},{24,20},{28,16},{1,13},{... | collective-permute-start | bytes 786440 | tf_op jit(solution)/shard_map/ppermute | solution.py:440
  22.1 6.2 %shard_map.95 = (f32[32,128]{1,0:T(8,128)S(1)}, f32[1,128]{1,0:T(1,128)S(1)}, f32[1024,4096]{1,0:T(8,128)S(1)}) custom-call(f32[1024,4096]{1,0:T(8,128)} %rinv_ref.1, f32[8,16,128]{2,1,0:T(8,128)S(1)} %all_to_all.15.parts_ref), custom_call_target="tpu_custom_call" | custom-call | tf_op jit(solution)/shard_map/pallas_call | solution.py:491
  28.4 1.2 %collective-permute-done = f32[32,128]{1,0:T(8,128)S(1)} collective-permute-done((f32[32,128]{1,0:T(8,128)S(1)}, f32[32,128]{1,0:T(8,128)S(1)}, u32[]{:S(2)}, u32[]{:S(2)}) %collective-permute-start) | collective-permute-done | bytes 16416 | tf_op jit(solution)/shard_map/ppermute | solution.py:31
  29.6 1.5 %collective-permute-start.1 = (f32[32,128]{1,0:T(8,128)S(1)}, f32[32,128]{1,0:T(8,128)S(1)}, u32[]{:S(2)}, u32[]{:S(2)}) collective-permute-start(f32[32,128]{1,0:T(8,128)S(1)} %add.12.refs_0_), channel_id=1, source_target_pairs={{0,2},{1,3},{2,0},{3,1},{4,6},{5,7},{6,4},{7,5},{8,10},{9,11},{10,... | collective-permute-start | bytes 49160 | tf_op jit(solution)/shard_map/ppermute | solution.py:31
  31.5 1.8 %collective-permute-done.1.refs_1_.order_ref = f32[32,128]{1,0:T(8,128)S(1)} collective-permute-done((f32[32,128]{1,0:T(8,128)S(1)}, f32[32,128]{1,0:T(8,128)S(1)}, u32[]{:S(2)}, u32[]{:S(2)}) %collective-permute-start.1) | collective-permute-done | bytes 16416 | tf_op jit(solution)/shard_map/ppermute | solution.py:31
  33.3 1.1 shard_map.98
  35.4 1.1 collective-permute-start.5
  36.4 2.5 %shard_map.96 = (f32[4,128]{1,0:T(4,128)S(1)}, f32[8,128]{1,0:T(8,128)S(1)}, f32[1,128]{1,0:T(1,128)S(1)}, f32[32,128]{1,0:T(8,128)S(1)}) custom-call(f32[1024,4096]{1,0:T(8,128)S(1)} %get-tuple-element.47.rinv_ref, f32[512,1024]{1,0:T(8,128)S(1)} %copy-done.3, f32[32,128]{1,0:T(8,128)S(1)} %add.12.refs_0_, ...), custom_call_target="tpu_custom_call" | custom-call | tf_op jit(solution)/shard_map/pallas_call | solution.py:54
  38.9 5.8 %copy-done = f32[1024,4096]{1,0:T(8,128)} copy-done((f32[1024,4096]{1,0:T(8,128)}, f32[1024,4096]{1,0:T(8,128)S(1)}, u32[]{:S(2)}) %copy-start) | copy-done | bytes 16777240
  44.7 1.2 %collective-permute-done.2 = f32[4,128]{1,0:T(4,128)S(1)} collective-permute-done((f32[4,128]{1,0:T(4,128)S(1)}, f32[4,128]{1,0:T(4,128)S(1)}, u32[]{:S(2)}, u32[]{:S(2)}) %collective-permute-start.2) | collective-permute-done | bytes 2080 | tf_op jit(solution)/shard_map/ppermute | solution.py:31
  45.8 1.5 %collective-permute-start.3 = (f32[4,128]{1,0:T(4,128)S(1)}, f32[4,128]{1,0:T(4,128)S(1)}, u32[]{:S(2)}, u32[]{:S(2)}) collective-permute-start(f32[4,128]{1,0:T(4,128)S(1)} %add.13.refs_0_), channel_id=1, source_target_pairs={{0,2},{1,3},{2,0},{3,1},{4,6},{5,7},{6,4},{7,5},{8,10},{9,11},{10,... | collective-permute-start | bytes 6152 | tf_op jit(solution)/shard_map/ppermute | solution.py:31
  48.0 0.7 copy-done.6
  49.3 0.7 copy-done.4
  50.0 1.2 %shard_map.100.refs_5_ = f32[1,128]{1,0:T(1,128)} custom-call(f32[512,128]{1,0:T(8,128)} %copy-done.4, f32[512,128]{1,0:T(8,128)} %collective-permute-done.5.refs_1_, f32[1,128]{1,0:T(1,128)} %copy-done.11), custom_call_target="tpu_custom_call" | custom-call | tf_op jit(solution)/shard_map/pallas_call | solution.py:552
  52.1 11.2 %all_to_all.16.parts_ref = f32[8,16,128]{2,1,0:T(8,128)S(1)} all-to-all(f32[8,16,128]{2,1,0:T(8,128)S(1)} %get-tuple-element.65), channel_id=1, replica_groups=mesh['row'=8,'col'=4] {'row'}, dimensions={0} | all-to-all | bytes 131072 | tf_op jit(solution)/shard_map/all_to_all | solution.py:24
  63.9 5.8 %copy-done.1 = f32[1024,4096]{1,0:T(8,128)S(1)} copy-done((f32[1024,4096]{1,0:T(8,128)S(1)}, f32[1024,4096]{1,0:T(8,128)}, u32[]{:S(2)}) %copy-start.1) | copy-done | bytes 16777240
  69.7 1.9 %shard_map.102 = (f32[32,128]{1,0:T(8,128)S(1)}, f32[1,128]{1,0:T(1,128)S(1)}) custom-call(f32[1024,4096]{1,0:T(8,128)S(1)} %copy-done.1, f32[8,16,128]{2,1,0:T(8,128)S(1)} %all_to_all.16.parts_ref), custom_call_target="tpu_custom_call" | custom-call | tf_op jit(solution)/shard_map/pallas_call | solution.py:491
  71.7 1.2 %collective-permute-done.10 = f32[32,128]{1,0:T(8,128)S(1)} collective-permute-done((f32[32,128]{1,0:T(8,128)S(1)}, f32[32,128]{1,0:T(8,128)S(1)}, u32[]{:S(2)}, u32[]{:S(2)}) %collective-permute-start.10) | collective-permute-done | bytes 16416 | tf_op jit(solution)/shard_map/ppermute | solution.py:31
  73.4 3.2 %collective-permute-done.11.refs_1_.order_ref = f32[32,128]{1,0:T(8,128)S(1)} collective-permute-done((f32[32,128]{1,0:T(8,128)S(1)}, f32[32,128]{1,0:T(8,128)S(1)}, u32[]{:S(2)}, u32[]{:S(2)}) %collective-permute-start.11) | collective-permute-done | bytes 16416 | tf_op jit(solution)/shard_map/ppermute | solution.py:31
  76.6 2.1 %shard_map.104 = (f32[1,4,128,128]{3,2,1,0:T(8,128)S(1)}, f32[1,4,128,128]{3,2,1,0:T(8,128)S(1)}) custom-call(f32[512,1024]{1,0:T(8,128)S(1)} %copy-done.3, f32[8,16,128]{2,1,0:T(8,128)S(1)} %all_to_all.15.parts_ref, bf16[8,128,512]{2,1,0:T(8,128)(2,1)S(1)} %shard_map.97.mix_ref, f32[32,128]{1,0:T(8,128)S(1)} %collective-permute-done.11.refs_1_.order_ref, ...), custom_call_target="tpu_custom_call" | custom-call | tf_op jit(solution)/shard_map/pallas_call | solution.py:54
  78.7 0.8 collective-permute-start.15
  79.5 2.5 %shard_map.103 = (f32[4,128]{1,0:T(4,128)S(1)}, f32[8,128]{1,0:T(8,128)S(1)}, f32[1,128]{1,0:T(1,128)S(1)}) custom-call(f32[1024,4096]{1,0:T(8,128)S(1)} %copy-done.2, f32[512,1024]{1,0:T(8,128)S(1)} %copy-done.3, f32[32,128]{1,0:T(8,128)S(1)} %add.14.refs_0_, f32[32,128]{1,0:T(8,128)S(1)} %collective-permute-done.11.refs_1_.order_ref, ...), custom_call_target="tpu_custom_call" | custom-call | tf_op jit(solution)/shard_map/pallas_call | solution.py:54
  82.0 10.5 %collective-permute-done.15.refs_2_ = f32[1,4,128,128]{3,2,1,0:T(8,128)S(1)} collective-permute-done((f32[1,4,128,128]{3,2,1,0:T(8,128)S(1)}, f32[1,4,128,128]{3,2,1,0:T(8,128)S(1)}, u32[]{:S(2)}, u32[]{:S(2)}) %collective-permute-start.15) | collective-permute-done | bytes 262176 | tf_op jit(solution)/shard_map/ppermute | solution.py:440
  92.6 1.1 collective-permute-start.16
  93.7 2.5 %collective-permute-start.18 = (f32[128,256]{1,0:T(8,128)S(1)}, f32[128,256]{1,0:T(8,128)S(1)}, u32[]{:S(2)}, u32[]{:S(2)}) collective-permute-start(f32[128,256]{1,0:T(8,128)S(1)} %get-tuple-element.85), channel_id=1, source_target_pairs={{0,12},{4,8},{8,4},{12,0},{16,28},{20,24},{24,20},{28,16},{1,13},{... | collective-permute-start | bytes 393224 | tf_op jit(solution)/shard_map/ppermute | solution.py:440
  96.1 1.2 %collective-permute-done.12 = f32[4,128]{1,0:T(4,128)S(1)} collective-permute-done((f32[4,128]{1,0:T(4,128)S(1)}, f32[4,128]{1,0:T(4,128)S(1)}, u32[]{:S(2)}, u32[]{:S(2)}) %collective-permute-start.12) | collective-permute-done | bytes 2080 | tf_op jit(solution)/shard_map/ppermute | solution.py:31
  97.8 3.1 %collective-permute-done.13.refs_1_ = f32[4,128]{1,0:T(4,128)S(1)} collective-permute-done((f32[4,128]{1,0:T(4,128)S(1)}, f32[4,128]{1,0:T(4,128)S(1)}, u32[]{:S(2)}, u32[]{:S(2)}) %collective-permute-start.13) | collective-permute-done | bytes 2080 | tf_op jit(solution)/shard_map/ppermute | solution.py:31
  101.0 9.9 %all_to_all.17.parts_ref = f32[8,8,128]{2,1,0:T(8,128)S(1)} all-to-all(f32[8,8,128]{2,1,0:T(8,128)S(1)} %get-tuple-element.78), channel_id=1, replica_groups=mesh['row'=8,'col'=4] {'row'}, dimensions={0} | all-to-all | bytes 65536 | tf_op jit(solution)/shard_map/all_to_all | solution.py:24
  110.9 0.9 shard_map.107
  (55 shorter events, 6.0 us)
Async XLA Ops:
  0.6 30.4 %copy-start.8 = (bf16[256,256]{1,0:T(8,128)(2,1)S(1)}, bf16[256,256]{1,0:T(8,128)(2,1)}, u32[]{:S(2)}) copy-start(bf16[256,256]{1,0:T(8,128)(2,1)} %constant.2.clone.walsh_ref) | copy-start | bytes 393220
  0.6 32.7 %copy-start.3 = (f32[512,1024]{1,0:T(8,128)S(1)}, f32[512,1024]{1,0:T(8,128)}, u32[]{:S(2)}) copy-start(f32[512,1024]{1,0:T(8,128)} %design_ref.9) | copy-start | bytes 6291460
  4.3 30.7 %copy-start.13 = (f32[512,128]{1,0:T(8,128)S(1)}, f32[512,128]{1,0:T(8,128)}, u32[]{:S(2)}) copy-start(f32[512,128]{1,0:T(8,128)} %get-tuple-element.54) | copy-start | bytes 786436
  4.3 31.1 %copy-start.12 = (f32[512,128]{1,0:T(8,128)S(1)}, f32[512,128]{1,0:T(8,128)}, u32[]{:S(2)}) copy-start(f32[512,128]{1,0:T(8,128)} %get-tuple-element.55) | copy-start | bytes 786436
  18.6 14.7 %collective-permute-start.6 = (f32[512,128]{1,0:T(8,128)}, f32[512,128]{1,0:T(8,128)S(1)}, u32[]{:S(2)}, u32[]{:S(2)}) collective-permute-start(f32[512,128]{1,0:T(8,128)} %get-tuple-element.59), channel_id=1, source_target_pairs={{0,4},{4,0},{8,12},{12,8},{16,20},{20,16},{24,28},{28,24},{1,5},{5... | collective-permute-start | bytes 786440 | tf_op jit(solution)/shard_map/ppermute | solution.py:440
  19.0 14.3 %collective-permute-start.7 = (f32[512,128]{1,0:T(8,128)}, f32[512,128]{1,0:T(8,128)S(1)}, u32[]{:S(2)}, u32[]{:S(2)}) collective-permute-start(f32[512,128]{1,0:T(8,128)} %get-tuple-element.60), channel_id=1, source_target_pairs={{0,8},{4,12},{8,0},{12,4},{16,24},{20,28},{24,16},{28,20},{1,9},{5... | collective-permute-start | bytes 786440 | tf_op jit(solution)/shard_map/ppermute | solution.py:440
  19.8 13.5 %collective-permute-start.8 = (f32[512,128]{1,0:T(8,128)}, f32[512,128]{1,0:T(8,128)S(1)}, u32[]{:S(2)}, u32[]{:S(2)}) collective-permute-start(f32[512,128]{1,0:T(8,128)} %get-tuple-element.61), channel_id=1, source_target_pairs={{0,12},{4,8},{8,4},{12,0},{16,28},{20,24},{24,20},{28,16},{1,13},{... | collective-permute-start | bytes 786440 | tf_op jit(solution)/shard_map/ppermute | solution.py:440
  28.3 22.8 %copy-start.9 = (f32[512]{0:T(512)S(1)}, f32[512]{0:T(512)}, u32[]{:S(2)}) copy-start(f32[512]{0:T(512)} %param.11) | copy-start | bytes 6148
  28.3 1.2 %collective-permute-start = (f32[32,128]{1,0:T(8,128)S(1)}, f32[32,128]{1,0:T(8,128)S(1)}, u32[]{:S(2)}, u32[]{:S(2)}) collective-permute-start(f32[32,128]{1,0:T(8,128)S(1)} %get-tuple-element.48), channel_id=1, source_target_pairs={{0,1},{1,0},{2,3},{3,2},{4,5},{5,4},{6,7},{7,6},{8,9},{9,8},{10,11... | collective-permute-start | bytes 49160 | tf_op jit(solution)/shard_map/ppermute | solution.py:31
  29.6 3.7 %collective-permute-start.1 = (f32[32,128]{1,0:T(8,128)S(1)}, f32[32,128]{1,0:T(8,128)S(1)}, u32[]{:S(2)}, u32[]{:S(2)}) collective-permute-start(f32[32,128]{1,0:T(8,128)S(1)} %add.12.refs_0_), channel_id=1, source_target_pairs={{0,2},{1,3},{2,0},{3,1},{4,6},{5,7},{6,4},{7,5},{8,10},{9,11},{10,... | collective-permute-start | bytes 49160 | tf_op jit(solution)/shard_map/ppermute | solution.py:31
  34.4 13.6 %collective-permute-start.9 = (f32[1,4,128,128]{3,2,1,0:T(8,128)S(1)}, f32[1,4,128,128]{3,2,1,0:T(8,128)S(1)}, u32[]{:S(2)}, u32[]{:S(2)}) collective-permute-start(f32[1,4,128,128]{3,2,1,0:T(8,128)S(1)} %get-tuple-element.63), channel_id=1, source_target_pairs={{0,16},{4,20},{8,24},{12,28},{16,0},{20,4},{24,8},{28,12},{1,17},{... | collective-permute-start | bytes 786440 | tf_op jit(solution)/shard_map/ppermute | solution.py:440
  35.0 14.3 %collective-permute-start.4 = (f32[512,128]{1,0:T(8,128)S(1)}, f32[512,128]{1,0:T(8,128)S(1)}, u32[]{:S(2)}, u32[]{:S(2)}) collective-permute-start(f32[512,128]{1,0:T(8,128)S(1)} %copy-done.13), channel_id=1, source_target_pairs={{0,4},{4,0},{8,12},{12,8},{16,20},{20,16},{24,28},{28,24},{1,5},{5... | collective-permute-start | bytes 786440 | tf_op jit(solution)/shard_map/ppermute | solution.py:440
  35.4 13.9 %collective-permute-start.5 = (f32[512,128]{1,0:T(8,128)S(1)}, f32[512,128]{1,0:T(8,128)}, u32[]{:S(2)}, u32[]{:S(2)}) collective-permute-start(f32[512,128]{1,0:T(8,128)S(1)} %copy-done.12), channel_id=1, source_target_pairs={{0,8},{4,12},{8,0},{12,4},{16,24},{20,28},{24,16},{28,20},{1,9},{5... | collective-permute-start | bytes 786440 | tf_op jit(solution)/shard_map/ppermute | solution.py:440
  38.9 5.8 %copy-start = (f32[1024,4096]{1,0:T(8,128)}, f32[1024,4096]{1,0:T(8,128)S(1)}, u32[]{:S(2)}) copy-start(f32[1024,4096]{1,0:T(8,128)S(1)} %get-tuple-element.47.rinv_ref) | copy-start | bytes 50331652
  44.7 1.2 %collective-permute-start.2 = (f32[4,128]{1,0:T(4,128)S(1)}, f32[4,128]{1,0:T(4,128)S(1)}, u32[]{:S(2)}, u32[]{:S(2)}) collective-permute-start(f32[4,128]{1,0:T(4,128)S(1)} %get-tuple-element.49), channel_id=1, source_target_pairs={{0,1},{1,0},{2,3},{3,2},{4,5},{5,4},{6,7},{7,6},{8,9},{9,8},{10,11... | collective-permute-start | bytes 6152 | tf_op jit(solution)/shard_map/ppermute | solution.py:31
  45.8 5.3 %collective-permute-start.3 = (f32[4,128]{1,0:T(4,128)S(1)}, f32[4,128]{1,0:T(4,128)S(1)}, u32[]{:S(2)}, u32[]{:S(2)}) collective-permute-start(f32[4,128]{1,0:T(4,128)S(1)} %add.13.refs_0_), channel_id=1, source_target_pairs={{0,2},{1,3},{2,0},{3,1},{4,6},{5,7},{6,4},{7,5},{8,10},{9,11},{10,... | collective-permute-start | bytes 6152 | tf_op jit(solution)/shard_map/ppermute | solution.py:31
  48.0 0.7 copy-start.6
  49.3 0.7 copy-start.4
  51.1 25.5 %copy-start.5 = (f32[512,128]{1,0:T(8,128)S(1)}, f32[512,128]{1,0:T(8,128)}, u32[]{:S(2)}) copy-start(f32[512,128]{1,0:T(8,128)} %copy-done.4) | copy-start | bytes 786436
  51.1 0.7 copy-start.10
  63.3 13.3 %collective-permute-start.14 = (f32[512,128]{1,0:T(8,128)}, f32[512,128]{1,0:T(8,128)S(1)}, u32[]{:S(2)}, u32[]{:S(2)}) collective-permute-start(f32[512,128]{1,0:T(8,128)} %get-tuple-element.74), channel_id=1, source_target_pairs={{0,12},{4,8},{8,4},{12,0},{16,28},{20,24},{24,20},{28,16},{1,13},{... | collective-permute-start | bytes 786440 | tf_op jit(solution)/shard_map/ppermute | solution.py:440
  63.9 5.8 %copy-start.1 = (f32[1024,4096]{1,0:T(8,128)S(1)}, f32[1024,4096]{1,0:T(8,128)}, u32[]{:S(2)}) copy-start(f32[1024,4096]{1,0:T(8,128)} %copy-done) | copy-start | bytes 50331652
  69.7 9.8 %copy-start.2 = (f32[1024,4096]{1,0:T(8,128)S(1)}, f32[1024,4096]{1,0:T(8,128)}, u32[]{:S(2)}) copy-start(f32[1024,4096]{1,0:T(8,128)} %copy-done) | copy-start | bytes 50331652
  69.7 22.8 %copy-start.7 = (f32[4,128,128]{2,1,0:T(8,128)S(1)}, f32[4,128,128]{2,1,0:T(8,128)}, u32[]{:S(2)}) copy-start(f32[4,128,128]{2,1,0:T(8,128)} %copy-done.6) | copy-start | bytes 786436
  71.6 1.2 %collective-permute-start.10 = (f32[32,128]{1,0:T(8,128)S(1)}, f32[32,128]{1,0:T(8,128)S(1)}, u32[]{:S(2)}, u32[]{:S(2)}) collective-permute-start(f32[32,128]{1,0:T(8,128)S(1)} %get-tuple-element.66), channel_id=1, source_target_pairs={{0,1},{1,0},{2,3},{3,2},{4,5},{5,4},{6,7},{7,6},{8,9},{9,8},{10,11... | collective-permute-start | bytes 49160 | tf_op jit(solution)/shard_map/ppermute | solution.py:31
  72.9 3.7 %collective-permute-start.11 = (f32[32,128]{1,0:T(8,128)S(1)}, f32[32,128]{1,0:T(8,128)S(1)}, u32[]{:S(2)}, u32[]{:S(2)}) collective-permute-start(f32[32,128]{1,0:T(8,128)S(1)} %add.14.refs_0_), channel_id=1, source_target_pairs={{0,2},{1,3},{2,0},{3,1},{4,6},{5,7},{6,4},{7,5},{8,10},{9,11},{10,... | collective-permute-start | bytes 49160 | tf_op jit(solution)/shard_map/ppermute | solution.py:31
  78.7 13.8 %collective-permute-start.15 = (f32[1,4,128,128]{3,2,1,0:T(8,128)S(1)}, f32[1,4,128,128]{3,2,1,0:T(8,128)S(1)}, u32[]{:S(2)}, u32[]{:S(2)}) collective-permute-start(f32[1,4,128,128]{3,2,1,0:T(8,128)S(1)} %get-tuple-element.76), channel_id=1, source_target_pairs={{0,16},{4,20},{8,24},{12,28},{16,0},{20,4},{24,8},{28,12},{1,17},{... | collective-permute-start | bytes 786440 | tf_op jit(solution)/shard_map/ppermute | solution.py:440
  92.6 18.3 %collective-permute-start.16 = (f32[128,256]{1,0:T(8,128)S(1)}, f32[128,256]{1,0:T(8,128)S(1)}, u32[]{:S(2)}, u32[]{:S(2)}) collective-permute-start(f32[128,256]{1,0:T(8,128)S(1)} %get-tuple-element.83), channel_id=1, source_target_pairs={{0,4},{4,0},{8,12},{12,8},{16,20},{20,16},{24,28},{28,24},{1,5},{5... | collective-permute-start | bytes 393224 | tf_op jit(solution)/shard_map/ppermute | solution.py:440
  93.7 17.2 %collective-permute-start.17 = (f32[128,256]{1,0:T(8,128)S(1)}, f32[128,256]{1,0:T(8,128)S(1)}, u32[]{:S(2)}, u32[]{:S(2)}) collective-permute-start(f32[128,256]{1,0:T(8,128)S(1)} %get-tuple-element.84), channel_id=1, source_target_pairs={{0,8},{4,12},{8,0},{12,4},{16,24},{20,28},{24,16},{28,20},{1,9},{5... | collective-permute-start | bytes 393224 | tf_op jit(solution)/shard_map/ppermute | solution.py:440
  93.7 17.2 %collective-permute-start.18 = (f32[128,256]{1,0:T(8,128)S(1)}, f32[128,256]{1,0:T(8,128)S(1)}, u32[]{:S(2)}, u32[]{:S(2)}) collective-permute-start(f32[128,256]{1,0:T(8,128)S(1)} %get-tuple-element.85), channel_id=1, source_target_pairs={{0,12},{4,8},{8,4},{12,0},{16,28},{20,24},{24,20},{28,16},{1,13},{... | collective-permute-start | bytes 393224 | tf_op jit(solution)/shard_map/ppermute | solution.py:440
  96.1 1.2 %collective-permute-start.12 = (f32[4,128]{1,0:T(4,128)S(1)}, f32[4,128]{1,0:T(4,128)S(1)}, u32[]{:S(2)}, u32[]{:S(2)}) collective-permute-start(f32[4,128]{1,0:T(4,128)S(1)} %get-tuple-element.69), channel_id=1, source_target_pairs={{0,1},{1,0},{2,3},{3,2},{4,5},{5,4},{6,7},{7,6},{8,9},{9,8},{10,11... | collective-permute-start | bytes 6152 | tf_op jit(solution)/shard_map/ppermute | solution.py:31
  97.3 3.6 %collective-permute-start.13 = (f32[4,128]{1,0:T(4,128)S(1)}, f32[4,128]{1,0:T(4,128)S(1)}, u32[]{:S(2)}, u32[]{:S(2)}) collective-permute-start(f32[4,128]{1,0:T(4,128)S(1)} %add.15.refs_0_), channel_id=1, source_target_pairs={{0,2},{1,3},{2,0},{3,1},{4,6},{5,7},{6,4},{7,5},{8,10},{9,11},{10,... | collective-permute-start | bytes 6152 | tf_op jit(solution)/shard_map/ppermute | solution.py:31
  (1 other events, 0.5 us)

commit v11 on v10

--- a/solution.py
+++ b/solution.py
@@ -33,6 +33,13 @@
         if mask == size:
             return [array, come]
         array = array + come
+
+
+def direct(array, axis):
+    size = lax.axis_size(axis)
+    return [array] + [
+        lax.ppermute(array, axis, [(i, i ^ mask) for i in range(size)]) for mask in range(1, size)
+    ]
 
 
 def tree(values):
@@ -356,8 +363,7 @@
 
 
 def split_body(chunks, *refs):
-    joined, (kept_ref, arrived_ref, order_ref, token_ref, *out_refs) = refs[: chunks - 1], refs[chunks - 1 :]
-    token_ref[...] = order_ref[:1, :]
+    joined, (kept_ref, arrived_ref, order_ref, *out_refs) = refs[: chunks - 1], refs[chunks - 1 :]
     piece = kept_ref.shape[3]
     for chunk in range(chunks):
         columns = slice(chunk * piece, (chunk + 1) * piece)
@@ -368,15 +374,18 @@
                 out_ref[:, columns] = kept_ref[0, index] + arrived_ref[0, index]
 
 
-def last_body(parts_ref, left_ref, *refs):
-    basis_ref, solution_ref, sketch_ref = refs[-3:]
-    quarters = refs[3 * ITERS : 3 * ITERS + NEAR]
+def assemble_body(*refs):
+    quarters, sketch_ref = refs[:-1], refs[-1]
     place = lax.axis_index("row") % NEAR
     piece = quarters[0].shape[1]
     for mask, part_ref in enumerate(quarters):
         for tile in range(0, piece, LANE):
             column = pl.multiple_of((place ^ mask) * piece + tile, LANE)
             sketch_ref[:, pl.ds(column, LANE)] = part_ref[:, tile : tile + LANE]
+
+
+def last_body(parts_ref, left_ref, *refs):
+    basis_ref, solution_ref = refs[-2:]
     betas = [ref[...] for ref in refs[:ITERS]]
     alphas = [ref[...] for ref in refs[ITERS : 2 * ITERS]]
     held = [ref[...] for ref in refs[2 * ITERS : 3 * ITERS]]
@@ -474,14 +483,14 @@
         return call(join_body, (shape(*keep.shape[1:]), scalar), keep, come, order)
 
     def trade(joined, keep, come, order):
-        token, mine, *others = call(
+        mine, *others = call(
             functools.partial(split_body, chunks),
-            (scalar,) + (shape(slots, width // NEAR),) * NEAR,
+            (shape(slots, width // NEAR),) * NEAR,
             *joined,
             *halve(keep, come, order),
             order,
         )
-        return [mine] + [swap(part, mask + 1) for mask, part in enumerate(others)], token
+        return [mine] + [swap(part, mask + 1) for mask, part in enumerate(others)]
 
     def back(rinv, message, first):
         outs, scratch = (shape(whole // LANE, LANE), scalar), [pltpu.VMEM((width // LANE, LANE), F32)]
@@ -510,7 +519,7 @@
 
     def turn(images, left, beta, alpha, token, last):
         return call(
-            functools.partial(turn_body, 2, last),
+            functools.partial(turn_body, len(images), last),
             (shape(lines, LANE), shape(row_groups, 8 if last else deep, LANE)),
             *images,
             left,
@@ -532,18 +541,19 @@
         else:
             term, beta = back(here, message, False)
         betas.append(beta)
-        terms = paired(term, "col")
+        spare = chunks > 1 and step > 0
+        terms = direct(term, "col") if spare else paired(term, "col")
         if step == 0:
             near += [spread(chunk, (1, 2), terms[1]) for chunk in range(1, chunks)]
             keep, send = sample(0, mixed, terms[1])
             come = swap(send, row_groups // 2)
-        elif chunks > 1:
-            keep, send = sample(1, mixed, terms[1])
-            come = swap(send, row_groups // 2)
         image, kept, alpha, *right = forward(terms, last, *right, *betas[1:])
         alphas.append(alpha)
         held.append(kept)
-        images = paired(image, "col")
+        if spare:
+            keep, send = sample(1, mixed, alpha)
+            come = swap(send, row_groups // 2)
+        images = direct(image, "col") if spare else paired(image, "col")
         token = alpha
         if chunks > 1 and step == 0:
             part, token = join(keep, come, alpha)
@@ -554,24 +564,23 @@
                 out_shape=scalar,
                 in_specs=[ANY] * len(there) + [VMEM],
                 out_specs=VMEM,
+                compiler_params=pltpu.CompilerParams(vmem_limit_bytes=2 << 20),
             )(*there, token)
-        if last:
-            quarters, token = trade(joined, keep, come, alpha)
         left, message = turn(images, left, beta, alpha, token, last)
         message = exchange(message, "row")
         if step == 0:
             for chunk in range(1, chunks):
                 near[chunk] += spread(chunk, (3,), message)
-    basis, answer, sketch = call(
+    basis, answer = call(
         last_body,
-        (shape(lines, LANE), shape(width // LANE, LANE), shape(slots, width)),
+        (shape(lines, LANE), shape(width // LANE, LANE)),
         message,
         left,
         *betas,
         *alphas,
         *held,
-        *quarters,
     )
+    sketch = call(assemble_body, shape(slots, width), *trade(joined, keep, come, message))
     return (sketch, answer.reshape(-1), basis.reshape(-1))
 
 

time: 112 us -> 95.3 us (0.85)
  local copies, waits for them, and re-layouts: 14.2 us -> 0.03 us
  waiting for transfers between devices: 23.9 us -> 19.4 us
  starting transfers between devices: 14.7 us -> 17.6 us
  Pallas kernels: 22.8 us -> 21 us
    unnamed x28 -> x12, local copies, waits for them, and re-layouts: 14.2 us -> 0.03 us
    ppermute x8 -> x4, waiting for transfers between devices: 12.7 us -> 4.07 us  [paired(): come = lax.ppermute(array, axis, [(i, i ^ mask) for i in range(size)])]
    ppermute x0 -> x6, waiting for transfers between devices: none -> 4.05 us  [direct(): lax.ppermute(array, axis, [(i, i ^ mask) for i in range(size)])]
    ppermute x0 -> x6, starting transfers between devices: none -> 3.95 us  [direct(): lax.ppermute(array, axis, [(i, i ^ mask) for i in range(size)])]
    pallas_call x1, Pallas kernels: 1.17 us -> 0.01 us  [shards(): pl.pallas_call(touch_body, out_shape=scalar, in_specs=[ANY] * len(there)...]
    ppermute x8 -> x4, starting transfers between devices: 4.19 us -> 3.12 us  [paired(): come = lax.ppermute(array, axis, [(i, i ^ mask) for i in range(size)])]
    pallas_call x10 -> x11, Pallas kernels: 9.89 us -> 9.41 us  [call(): pl.pallas_call(body, out_shape=out_shape, in_specs=[VMEM] * len(operands)...]
  transfers between devices with their start and end apart: 19 -> 21, of which waited for: 9 -> 11; matrix products, arithmetic and copies ran while one was open for 0% -> 0% of each run, Pallas kernels for 13% -> 15%
where the time goes in v11:
time: 95.3 us; the launch traced here: 95 us
  blocking collectives  36.1 us (38%)
  Pallas kernels  21 us (22%)
  waiting for transfers between devices  19.4 us (20%)
  starting transfers between devices  17.6 us (18%)
    all_to_all x3, blocking collectives, exchange(): return lax.all_to_all(copies, axis, split_axis=0, concat_axis=0, tiled=True)  36.1 us
    ppermute x11, waiting for transfers between devices, swap(): lax.ppermute(array, 'row', [(i, i ^ mask) for i in range(row_groups)])  11.3 us
    ppermute x11, starting transfers between devices, swap(): lax.ppermute(array, 'row', [(i, i ^ mask) for i in range(row_groups)])  10.5 us
    pallas_call x11, Pallas kernels, call(): pl.pallas_call(body, out_shape=out_shape, in_specs=[VMEM] * len(operands)...  9.41 us
    pallas_call x2, Pallas kernels, back(): pl.pallas_call(functools.partial(back_body, first), out_shape=outs, in_sp...  7.97 us
    ppermute x4, waiting for transfers between devices, paired(): come = lax.ppermute(array, axis, [(i, i ^ mask) for i in range(size)])  4.07 us
    ppermute x6, waiting for transfers between devices, direct(): lax.ppermute(array, axis, [(i, i ^ mask) for i in range(size)])  4.05 us
    ppermute x6, starting transfers between devices, direct(): lax.ppermute(array, axis, [(i, i ^ mask) for i in range(size)])  3.95 us
  transfers between devices with their start and end apart: 21, of which 11 were waited for; matrix products, arithmetic and copies ran while one was open for 0% of the time, Pallas kernels for 15%

profile of v11, /device:TPU:0, one launch (start us, length us, event | category | flops | bytes accessed | tf_op | source)
XLA Modules:
  0.0 95.0 jit_solution(4449634241295882730)
XLA Ops:
  0.7 3.6 %shard_map.94 = (f32[8,16,128]{2,1,0:T(8,128)}, f32[512,128]{1,0:T(8,128)}, f32[512,128]{1,0:T(8,128)}, f32[512,128]{1,0:T(8,128)}, f32[512,128]{1,0:T(8,128)}, /*index=5*/f32[512,128]{1,0:T(8,128)}, f32[512,128]{1,0:T(8,128)}) custom-call(f32[512,1024]{1,0:T(8,128)} %design_ref.9, f32[4,128]{1,0:T(4,128)} %bitcast.6, s32[4,128]{1,0:T(4,128)} %bitcast.9, ...), custom_call_target="tpu_custom_call" | custom-call | tf_op jit(solution)/shard_map/pallas_call | solution.py:431
  4.3 14.3 %all_to_all.15.parts_ref = f32[8,16,128]{2,1,0:T(8,128)S(1)} all-to-all(f32[8,16,128]{2,1,0:T(8,128)} %get-tuple-element.44), channel_id=1, replica_groups=mesh['row'=8,'col'=4] {'row'}, dimensions={0} | all-to-all | bytes 131072 | tf_op jit(solution)/shard_map/all_to_all | solution.py:24
  19.0 0.8 collective-permute-start.3
  19.8 2.3 %collective-permute-start.4 = (f32[512,128]{1,0:T(8,128)}, f32[512,128]{1,0:T(8,128)S(1)}, u32[]{:S(2)}, u32[]{:S(2)}) collective-permute-start(f32[512,128]{1,0:T(8,128)} %get-tuple-element.51), channel_id=1, source_target_pairs={{0,12},{4,8},{8,4},{12,0},{16,28},{20,24},{24,20},{28,16},{1,13},{... | collective-permute-start | bytes 786440 | tf_op jit(solution)/shard_map/ppermute | solution.py:449
  22.1 6.2 %shard_map.96 = (f32[32,128]{1,0:T(8,128)S(1)}, f32[1,128]{1,0:T(1,128)S(1)}, f32[1024,4096]{1,0:T(8,128)S(1)}) custom-call(f32[1024,4096]{1,0:T(8,128)} %rinv_ref.1, f32[8,16,128]{2,1,0:T(8,128)S(1)} %all_to_all.15.parts_ref), custom_call_target="tpu_custom_call" | custom-call | tf_op jit(solution)/shard_map/pallas_call | solution.py:500
  28.4 1.2 %collective-permute-done = f32[32,128]{1,0:T(8,128)S(1)} collective-permute-done((f32[32,128]{1,0:T(8,128)S(1)}, f32[32,128]{1,0:T(8,128)S(1)}, u32[]{:S(2)}, u32[]{:S(2)}) %collective-permute-start) | collective-permute-done | bytes 16416 | tf_op jit(solution)/shard_map/ppermute | solution.py:31
  29.6 1.5 %collective-permute-start.1 = (f32[32,128]{1,0:T(8,128)S(1)}, f32[32,128]{1,0:T(8,128)S(1)}, u32[]{:S(2)}, u32[]{:S(2)}) collective-permute-start(f32[32,128]{1,0:T(8,128)S(1)} %add.6.refs_0_), channel_id=1, source_target_pairs={{0,2},{1,3},{2,0},{3,1},{4,6},{5,7},{6,4},{7,5},{8,10},{9,11},{10,... | collective-permute-start | bytes 49160 | tf_op jit(solution)/shard_map/ppermute | solution.py:31
  31.5 1.8 %collective-permute-done.1.order_ref.refs_1_ = f32[32,128]{1,0:T(8,128)S(1)} collective-permute-done((f32[32,128]{1,0:T(8,128)S(1)}, f32[32,128]{1,0:T(8,128)S(1)}, u32[]{:S(2)}, u32[]{:S(2)}) %collective-permute-start.1) | collective-permute-done | bytes 16416 | tf_op jit(solution)/shard_map/ppermute | solution.py:31
  33.3 1.1 %shard_map.97 = (f32[1,4,128,128]{3,2,1,0:T(8,128)S(1)}, f32[1,4,128,128]{3,2,1,0:T(8,128)S(1)}) custom-call(f32[512,1024]{1,0:T(8,128)S(1)} %copy-done, f32[8,16,128]{2,1,0:T(8,128)S(1)} %all_to_all.15.parts_ref, bf16[8,128,512]{2,1,0:T(8,128)(2,1)S(1)} %shard_map.95.mix_ref, f32[32,128]{1,0:T(8,128)S(1)} %collective-permute-done.1.order_ref.refs_1_, ...), custom_call_target="tpu_custom_call" | custom-call | tf_op jit(solution)/shard_map/pallas_call | solution.py:61
  35.3 1.1 %collective-permute-start.9 = (f32[512,128]{1,0:T(8,128)S(1)}, f32[512,128]{1,0:T(8,128)S(1)}, u32[]{:S(2)}, u32[]{:S(2)}) collective-permute-start(f32[512,128]{1,0:T(8,128)S(1)} %copy-done.4), channel_id=1, source_target_pairs={{0,8},{4,12},{8,0},{12,4},{16,24},{20,28},{24,16},{28,20},{1,9},{5... | collective-permute-start | bytes 786440 | tf_op jit(solution)/shard_map/ppermute | solution.py:449
  36.4 2.4 %shard_map.98 = (f32[4,128]{1,0:T(4,128)S(1)}, f32[8,128]{1,0:T(8,128)S(1)}, f32[1,128]{1,0:T(1,128)S(1)}, f32[32,128]{1,0:T(8,128)S(1)}) custom-call(f32[1024,4096]{1,0:T(8,128)S(1)} %get-tuple-element.54.rinv_ref, f32[512,1024]{1,0:T(8,128)S(1)} %copy-done, f32[32,128]{1,0:T(8,128)S(1)} %add.6.refs_0_, f32[32,128]{1,0:T(8,128)S(1)} %collective-permute-done.1.order_ref.refs_1_), custom_call_target="tpu_custom_call" | custom-call | tf_op jit(solution)/shard_map/pallas_call | solution.py:61
  38.9 1.1 %collective-permute-done.6 = f32[4,128]{1,0:T(4,128)S(1)} collective-permute-done((f32[4,128]{1,0:T(4,128)S(1)}, f32[4,128]{1,0:T(4,128)S(1)}, u32[]{:S(2)}, u32[]{:S(2)}) %collective-permute-start.6) | collective-permute-done | bytes 2080 | tf_op jit(solution)/shard_map/ppermute | solution.py:31
  40.1 1.5 %collective-permute-start.7 = (f32[4,128]{1,0:T(4,128)S(1)}, f32[4,128]{1,0:T(4,128)S(1)}, u32[]{:S(2)}, u32[]{:S(2)}) collective-permute-start(f32[4,128]{1,0:T(4,128)S(1)} %add.7.refs_0_), channel_id=1, source_target_pairs={{0,2},{1,3},{2,0},{3,1},{4,6},{5,7},{6,4},{7,5},{8,10},{9,11},{10,... | collective-permute-start | bytes 6152 | tf_op jit(solution)/shard_map/ppermute | solution.py:31
  41.6 6.4 %collective-permute-done.5.arrived_ref = f32[1,4,128,128]{3,2,1,0:T(8,128)S(1)} collective-permute-done((f32[1,4,128,128]{3,2,1,0:T(8,128)S(1)}, f32[1,4,128,128]{3,2,1,0:T(8,128)S(1)}, u32[]{:S(2)}, u32[]{:S(2)}) %collective-permute-start.5) | collective-permute-done | bytes 262176 | tf_op jit(solution)/shard_map/ppermute | solution.py:449
  48.3 10.4 %all_to_all.16.parts_ref = f32[8,16,128]{2,1,0:T(8,128)S(1)} all-to-all(f32[8,16,128]{2,1,0:T(8,128)S(1)} %get-tuple-element.64), channel_id=1, replica_groups=mesh['row'=8,'col'=4] {'row'}, dimensions={0} | all-to-all | bytes 131072 | tf_op jit(solution)/shard_map/all_to_all | solution.py:24
  58.7 0.7 collective-permute-start.13
  59.3 1.8 %shard_map.102 = (f32[32,128]{1,0:T(8,128)S(1)}, f32[1,128]{1,0:T(1,128)S(1)}) custom-call(f32[1024,4096]{1,0:T(8,128)S(1)} %get-tuple-element.54.rinv_ref, f32[8,16,128]{2,1,0:T(8,128)S(1)} %all_to_all.16.parts_ref), custom_call_target="tpu_custom_call" | custom-call | tf_op jit(solution)/shard_map/pallas_call | solution.py:500
  61.2 1.6 %collective-permute-start.11 = (f32[32,128]{1,0:T(8,128)S(1)}, f32[32,128]{1,0:T(8,128)S(1)}, u32[]{:S(2)}, u32[]{:S(2)}) collective-permute-start(f32[32,128]{1,0:T(8,128)S(1)} %get-tuple-element.65.refs_0_), channel_id=1, source_target_pairs={{0,2},{1,3},{2,0},{3,1},{4,6},{5,7},{6,4},{7,5},{8,10},{9,11},{10,... | collective-permute-start | bytes 49160 | tf_op jit(solution)/shard_map/ppermute | solution.py:41
  63.1 1.4 %collective-permute-done.12.refs_3_ = f32[32,128]{1,0:T(8,128)S(1)} collective-permute-done((f32[32,128]{1,0:T(8,128)S(1)}, f32[32,128]{1,0:T(8,128)S(1)}, u32[]{:S(2)}, u32[]{:S(2)}) %collective-permute-start.12) | collective-permute-done | bytes 16416 | tf_op jit(solution)/shard_map/ppermute | solution.py:41
  65.0 2.4 %shard_map.103 = (f32[4,128]{1,0:T(4,128)S(1)}, f32[8,128]{1,0:T(8,128)S(1)}, f32[1,128]{1,0:T(1,128)S(1)}) custom-call(f32[1024,4096]{1,0:T(8,128)S(1)} %get-tuple-element.54.rinv_ref, f32[512,1024]{1,0:T(8,128)S(1)} %copy-done, f32[32,128]{1,0:T(8,128)S(1)} %get-tuple-element.65.refs_0_, f32[32,128]{1,0:T(8,128)S(1)} %collective-permute-done.10.refs_1_, ...), custom_call_target="tpu_custom_call" | custom-call | tf_op jit(solution)/shard_map/pallas_call | solution.py:61
  67.5 1.1 %shard_map.104 = (f32[1,4,128,128]{3,2,1,0:T(8,128)S(1)}, f32[1,4,128,128]{3,2,1,0:T(8,128)S(1)}) custom-call(f32[512,1024]{1,0:T(8,128)S(1)} %copy-done, f32[8,16,128]{2,1,0:T(8,128)S(1)} %all_to_all.15.parts_ref, bf16[8,128,512]{2,1,0:T(8,128)(2,1)S(1)} %shard_map.95.mix_ref, f32[1,128]{1,0:T(1,128)S(1)} %get-tuple-element.68.order_ref.refs_6_.refs_7_.refs_3_, ...), custom_call_target="tpu_custom_call" | custom-call | tf_op jit(solution)/shard_map/pallas_call | solution.py:61
  68.6 0.8 collective-permute-start.14
  69.9 1.5 %collective-permute-start.16 = (f32[4,128]{1,0:T(4,128)S(1)}, f32[4,128]{1,0:T(4,128)S(1)}, u32[]{:S(2)}, u32[]{:S(2)}) collective-permute-start(f32[4,128]{1,0:T(4,128)S(1)} %get-tuple-element.73.refs_0_), channel_id=1, source_target_pairs={{0,2},{1,3},{2,0},{3,1},{4,6},{5,7},{6,4},{7,5},{8,10},{9,11},{10,... | collective-permute-start | bytes 6152 | tf_op jit(solution)/shard_map/ppermute | solution.py:41
  71.4 1.0 %collective-permute-done.17.refs_3_ = f32[4,128]{1,0:T(4,128)S(1)} collective-permute-done((f32[4,128]{1,0:T(4,128)S(1)}, f32[4,128]{1,0:T(4,128)S(1)}, u32[]{:S(2)}, u32[]{:S(2)}) %collective-permute-start.17) | collective-permute-done | bytes 2080 | tf_op jit(solution)/shard_map/ppermute | solution.py:41
  72.4 1.1 %collective-permute-done.16.refs_2_ = f32[4,128]{1,0:T(4,128)S(1)} collective-permute-done((f32[4,128]{1,0:T(4,128)S(1)}, f32[4,128]{1,0:T(4,128)S(1)}, u32[]{:S(2)}, u32[]{:S(2)}) %collective-permute-start.16) | collective-permute-done | bytes 2080 | tf_op jit(solution)/shard_map/ppermute | solution.py:41
  73.6 11.4 %all_to_all.17.refs_3_.parts_ref = f32[8,8,128]{2,1,0:T(8,128)S(1)} all-to-all(f32[8,8,128]{2,1,0:T(8,128)S(1)} %get-tuple-element.75), channel_id=1, replica_groups=mesh['row'=8,'col'=4] {'row'}, dimensions={0} | all-to-all | bytes 65536 | tf_op jit(solution)/shard_map/all_to_all | solution.py:24
  85.0 1.3 %collective-permute-start.18 = (f32[128,256]{1,0:T(8,128)S(1)}, f32[128,256]{1,0:T(8,128)S(1)}, u32[]{:S(2)}, u32[]{:S(2)}) collective-permute-start(f32[128,256]{1,0:T(8,128)S(1)} %get-tuple-element.77), channel_id=1, source_target_pairs={{0,4},{4,0},{8,12},{12,8},{16,20},{20,16},{24,28},{28,24},{1,5},{5... | collective-permute-start | bytes 393224 | tf_op jit(solution)/shard_map/ppermute | solution.py:449
  86.8 1.8 %collective-permute-start.20 = (f32[128,256]{1,0:T(8,128)S(1)}, f32[128,256]{1,0:T(8,128)S(1)}, u32[]{:S(2)}, u32[]{:S(2)}) collective-permute-start(f32[128,256]{1,0:T(8,128)S(1)} %get-tuple-element.79), channel_id=1, source_target_pairs={{0,12},{4,8},{8,4},{12,0},{16,28},{20,24},{24,20},{28,16},{1,13},{... | collective-permute-start | bytes 393224 | tf_op jit(solution)/shard_map/ppermute | solution.py:449
  89.2 1.4 %collective-permute-done.18.refs_1_ = f32[128,256]{1,0:T(8,128)S(1)} collective-permute-done((f32[128,256]{1,0:T(8,128)S(1)}, f32[128,256]{1,0:T(8,128)S(1)}, u32[]{:S(2)}, u32[]{:S(2)}) %collective-permute-start.18) | collective-permute-done | bytes 131104 | tf_op jit(solution)/shard_map/ppermute | solution.py:449
  90.6 1.7 %collective-permute-done.19.refs_2_ = f32[128,256]{1,0:T(8,128)S(1)} collective-permute-done((f32[128,256]{1,0:T(8,128)S(1)}, f32[128,256]{1,0:T(8,128)S(1)}, u32[]{:S(2)}, u32[]{:S(2)}) %collective-permute-start.19) | collective-permute-done | bytes 131104 | tf_op jit(solution)/shard_map/ppermute | solution.py:449
  92.3 1.8 %collective-permute-done.20.refs_3_ = f32[128,256]{1,0:T(8,128)S(1)} collective-permute-done((f32[128,256]{1,0:T(8,128)S(1)}, f32[128,256]{1,0:T(8,128)S(1)}, u32[]{:S(2)}, u32[]{:S(2)}) %collective-permute-start.20) | collective-permute-done | bytes 131104 | tf_op jit(solution)/shard_map/ppermute | solution.py:449
  94.1 0.9 shard_map.107
  (42 shorter events, 5.0 us)
Async XLA Ops:
  0.6 30.4 %copy-start.1 = (bf16[256,256]{1,0:T(8,128)(2,1)S(1)}, bf16[256,256]{1,0:T(8,128)(2,1)}, u32[]{:S(2)}) copy-start(bf16[256,256]{1,0:T(8,128)(2,1)} %constant.2.clone.walsh_ref) | copy-start | bytes 393220
  0.6 32.7 %copy-start = (f32[512,1024]{1,0:T(8,128)S(1)}, f32[512,1024]{1,0:T(8,128)}, u32[]{:S(2)}) copy-start(f32[512,1024]{1,0:T(8,128)} %design_ref.9) | copy-start | bytes 6291460
  4.3 30.7 %copy-start.5 = (f32[512,128]{1,0:T(8,128)S(1)}, f32[512,128]{1,0:T(8,128)}, u32[]{:S(2)}) copy-start(f32[512,128]{1,0:T(8,128)} %get-tuple-element.61) | copy-start | bytes 786436
  4.3 31.1 %copy-start.4 = (f32[512,128]{1,0:T(8,128)S(1)}, f32[512,128]{1,0:T(8,128)}, u32[]{:S(2)}) copy-start(f32[512,128]{1,0:T(8,128)} %get-tuple-element.62) | copy-start | bytes 786436
  18.6 14.7 %collective-permute-start.2 = (f32[512,128]{1,0:T(8,128)}, f32[512,128]{1,0:T(8,128)S(1)}, u32[]{:S(2)}, u32[]{:S(2)}) collective-permute-start(f32[512,128]{1,0:T(8,128)} %get-tuple-element.49), channel_id=1, source_target_pairs={{0,4},{4,0},{8,12},{12,8},{16,20},{20,16},{24,28},{28,24},{1,5},{5... | collective-permute-start | bytes 786440 | tf_op jit(solution)/shard_map/ppermute | solution.py:449
  19.0 14.3 %collective-permute-start.3 = (f32[512,128]{1,0:T(8,128)}, f32[512,128]{1,0:T(8,128)S(1)}, u32[]{:S(2)}, u32[]{:S(2)}) collective-permute-start(f32[512,128]{1,0:T(8,128)} %get-tuple-element.50), channel_id=1, source_target_pairs={{0,8},{4,12},{8,0},{12,4},{16,24},{20,28},{24,16},{28,20},{1,9},{5... | collective-permute-start | bytes 786440 | tf_op jit(solution)/shard_map/ppermute | solution.py:449
  19.8 13.5 %collective-permute-start.4 = (f32[512,128]{1,0:T(8,128)}, f32[512,128]{1,0:T(8,128)S(1)}, u32[]{:S(2)}, u32[]{:S(2)}) collective-permute-start(f32[512,128]{1,0:T(8,128)} %get-tuple-element.51), channel_id=1, source_target_pairs={{0,12},{4,8},{8,4},{12,0},{16,28},{20,24},{24,20},{28,16},{1,13},{... | collective-permute-start | bytes 786440 | tf_op jit(solution)/shard_map/ppermute | solution.py:449
  28.3 19.8 %copy-start.2 = (f32[512]{0:T(512)S(1)}, f32[512]{0:T(512)}, u32[]{:S(2)}) copy-start(f32[512]{0:T(512)} %param.11) | copy-start | bytes 6148
  28.3 30.4 %copy-start.3 = (f32[512,128]{1,0:T(8,128)S(1)}, f32[512,128]{1,0:T(8,128)}, u32[]{:S(2)}) copy-start(f32[512,128]{1,0:T(8,128)} %get-tuple-element.70) | copy-start | bytes 786436
  28.3 1.2 %collective-permute-start = (f32[32,128]{1,0:T(8,128)S(1)}, f32[32,128]{1,0:T(8,128)S(1)}, u32[]{:S(2)}, u32[]{:S(2)}) collective-permute-start(f32[32,128]{1,0:T(8,128)S(1)} %get-tuple-element.45), channel_id=1, source_target_pairs={{0,1},{1,0},{2,3},{3,2},{4,5},{5,4},{6,7},{7,6},{8,9},{9,8},{10,11... | collective-permute-start | bytes 49160 | tf_op jit(solution)/shard_map/ppermute | solution.py:31
  29.6 3.7 %collective-permute-start.1 = (f32[32,128]{1,0:T(8,128)S(1)}, f32[32,128]{1,0:T(8,128)S(1)}, u32[]{:S(2)}, u32[]{:S(2)}) collective-permute-start(f32[32,128]{1,0:T(8,128)S(1)} %add.6.refs_0_), channel_id=1, source_target_pairs={{0,2},{1,3},{2,0},{3,1},{4,6},{5,7},{6,4},{7,5},{8,10},{9,11},{10,... | collective-permute-start | bytes 49160 | tf_op jit(solution)/shard_map/ppermute | solution.py:31
  34.4 13.6 %collective-permute-start.5 = (f32[1,4,128,128]{3,2,1,0:T(8,128)S(1)}, f32[1,4,128,128]{3,2,1,0:T(8,128)S(1)}, u32[]{:S(2)}, u32[]{:S(2)}) collective-permute-start(f32[1,4,128,128]{3,2,1,0:T(8,128)S(1)} %get-tuple-element.53), channel_id=1, source_target_pairs={{0,16},{4,20},{8,24},{12,28},{16,0},{20,4},{24,8},{28,12},{1,17},{... | collective-permute-start | bytes 786440 | tf_op jit(solution)/shard_map/ppermute | solution.py:449
  35.0 13.1 %collective-permute-start.8 = (f32[512,128]{1,0:T(8,128)S(1)}, f32[512,128]{1,0:T(8,128)S(1)}, u32[]{:S(2)}, u32[]{:S(2)}) collective-permute-start(f32[512,128]{1,0:T(8,128)S(1)} %copy-done.5), channel_id=1, source_target_pairs={{0,4},{4,0},{8,12},{12,8},{16,20},{20,16},{24,28},{28,24},{1,5},{5... | collective-permute-start | bytes 786440 | tf_op jit(solution)/shard_map/ppermute | solution.py:449
  35.3 12.7 %collective-permute-start.9 = (f32[512,128]{1,0:T(8,128)S(1)}, f32[512,128]{1,0:T(8,128)S(1)}, u32[]{:S(2)}, u32[]{:S(2)}) collective-permute-start(f32[512,128]{1,0:T(8,128)S(1)} %copy-done.4), channel_id=1, source_target_pairs={{0,8},{4,12},{8,0},{12,4},{16,24},{20,28},{24,16},{28,20},{1,9},{5... | collective-permute-start | bytes 786440 | tf_op jit(solution)/shard_map/ppermute | solution.py:449
  38.9 1.2 %collective-permute-start.6 = (f32[4,128]{1,0:T(4,128)S(1)}, f32[4,128]{1,0:T(4,128)S(1)}, u32[]{:S(2)}, u32[]{:S(2)}) collective-permute-start(f32[4,128]{1,0:T(4,128)S(1)} %get-tuple-element.57), channel_id=1, source_target_pairs={{0,1},{1,0},{2,3},{3,2},{4,5},{5,4},{6,7},{7,6},{8,9},{9,8},{10,11... | collective-permute-start | bytes 6152 | tf_op jit(solution)/shard_map/ppermute | solution.py:31
  40.1 8.0 %collective-permute-start.7 = (f32[4,128]{1,0:T(4,128)S(1)}, f32[4,128]{1,0:T(4,128)S(1)}, u32[]{:S(2)}, u32[]{:S(2)}) collective-permute-start(f32[4,128]{1,0:T(4,128)S(1)} %add.7.refs_0_), channel_id=1, source_target_pairs={{0,2},{1,3},{2,0},{3,1},{4,6},{5,7},{6,4},{7,5},{8,10},{9,11},{10,... | collective-permute-start | bytes 6152 | tf_op jit(solution)/shard_map/ppermute | solution.py:31
  58.7 8.8 %collective-permute-start.13 = (f32[512,128]{1,0:T(8,128)S(1)}, f32[512,128]{1,0:T(8,128)S(1)}, u32[]{:S(2)}, u32[]{:S(2)}) collective-permute-start(f32[512,128]{1,0:T(8,128)S(1)} %copy-done.3), channel_id=1, source_target_pairs={{0,12},{4,8},{8,4},{12,0},{16,28},{20,24},{24,20},{28,16},{1,13},{... | collective-permute-start | bytes 786440 | tf_op jit(solution)/shard_map/ppermute | solution.py:449
  61.1 3.4 %collective-permute-start.12 = (f32[32,128]{1,0:T(8,128)S(1)}, f32[32,128]{1,0:T(8,128)S(1)}, u32[]{:S(2)}, u32[]{:S(2)}) collective-permute-start(f32[32,128]{1,0:T(8,128)S(1)} %get-tuple-element.65.refs_0_), channel_id=1, source_target_pairs={{0,3},{1,2},{2,1},{3,0},{4,7},{5,6},{6,5},{7,4},{8,11},{9,10},{10,... | collective-permute-start | bytes 49160 | tf_op jit(solution)/shard_map/ppermute | solution.py:41
  61.2 3.8 %collective-permute-start.11 = (f32[32,128]{1,0:T(8,128)S(1)}, f32[32,128]{1,0:T(8,128)S(1)}, u32[]{:S(2)}, u32[]{:S(2)}) collective-permute-start(f32[32,128]{1,0:T(8,128)S(1)} %get-tuple-element.65.refs_0_), channel_id=1, source_target_pairs={{0,2},{1,3},{2,0},{3,1},{4,6},{5,7},{6,4},{7,5},{8,10},{9,11},{10,... | collective-permute-start | bytes 49160 | tf_op jit(solution)/shard_map/ppermute | solution.py:41
  62.8 2.3 %collective-permute-start.10 = (f32[32,128]{1,0:T(8,128)S(1)}, f32[32,128]{1,0:T(8,128)S(1)}, u32[]{:S(2)}, u32[]{:S(2)}) collective-permute-start(f32[32,128]{1,0:T(8,128)S(1)} %get-tuple-element.65.refs_0_), channel_id=1, source_target_pairs={{0,1},{1,0},{2,3},{3,2},{4,5},{5,4},{6,7},{7,6},{8,9},{9,8},{10,11... | collective-permute-start | bytes 49160 | tf_op jit(solution)/shard_map/ppermute | solution.py:41
  68.6 16.4 %collective-permute-start.14 = (f32[1,4,128,128]{3,2,1,0:T(8,128)S(1)}, f32[1,4,128,128]{3,2,1,0:T(8,128)S(1)}, u32[]{:S(2)}, u32[]{:S(2)}) collective-permute-start(f32[1,4,128,128]{3,2,1,0:T(8,128)S(1)} %get-tuple-element.72), channel_id=1, source_target_pairs={{0,16},{4,20},{8,24},{12,28},{16,0},{20,4},{24,8},{28,12},{1,17},{... | collective-permute-start | bytes 786440 | tf_op jit(solution)/shard_map/ppermute | solution.py:449
  69.4 3.0 %collective-permute-start.17 = (f32[4,128]{1,0:T(4,128)S(1)}, f32[4,128]{1,0:T(4,128)S(1)}, u32[]{:S(2)}, u32[]{:S(2)}) collective-permute-start(f32[4,128]{1,0:T(4,128)S(1)} %get-tuple-element.73.refs_0_), channel_id=1, source_target_pairs={{0,3},{1,2},{2,1},{3,0},{4,7},{5,6},{6,5},{7,4},{8,11},{9,10},{10,... | collective-permute-start | bytes 6152 | tf_op jit(solution)/shard_map/ppermute | solution.py:41
  69.9 3.6 %collective-permute-start.16 = (f32[4,128]{1,0:T(4,128)S(1)}, f32[4,128]{1,0:T(4,128)S(1)}, u32[]{:S(2)}, u32[]{:S(2)}) collective-permute-start(f32[4,128]{1,0:T(4,128)S(1)} %get-tuple-element.73.refs_0_), channel_id=1, source_target_pairs={{0,2},{1,3},{2,0},{3,1},{4,6},{5,7},{6,4},{7,5},{8,10},{9,11},{10,... | collective-permute-start | bytes 6152 | tf_op jit(solution)/shard_map/ppermute | solution.py:41
  71.4 2.1 %collective-permute-start.15 = (f32[4,128]{1,0:T(4,128)S(1)}, f32[4,128]{1,0:T(4,128)S(1)}, u32[]{:S(2)}, u32[]{:S(2)}) collective-permute-start(f32[4,128]{1,0:T(4,128)S(1)} %get-tuple-element.73.refs_0_), channel_id=1, source_target_pairs={{0,1},{1,0},{2,3},{3,2},{4,5},{5,4},{6,7},{7,6},{8,9},{9,8},{10,11... | collective-permute-start | bytes 6152 | tf_op jit(solution)/shard_map/ppermute | solution.py:41
  85.0 5.6 %collective-permute-start.18 = (f32[128,256]{1,0:T(8,128)S(1)}, f32[128,256]{1,0:T(8,128)S(1)}, u32[]{:S(2)}, u32[]{:S(2)}) collective-permute-start(f32[128,256]{1,0:T(8,128)S(1)} %get-tuple-element.77), channel_id=1, source_target_pairs={{0,4},{4,0},{8,12},{12,8},{16,20},{20,16},{24,28},{28,24},{1,5},{5... | collective-permute-start | bytes 393224 | tf_op jit(solution)/shard_map/ppermute | solution.py:449
  86.3 6.0 %collective-permute-start.19 = (f32[128,256]{1,0:T(8,128)S(1)}, f32[128,256]{1,0:T(8,128)S(1)}, u32[]{:S(2)}, u32[]{:S(2)}) collective-permute-start(f32[128,256]{1,0:T(8,128)S(1)} %get-tuple-element.78), channel_id=1, source_target_pairs={{0,8},{4,12},{8,0},{12,4},{16,24},{20,28},{24,16},{28,20},{1,9},{5... | collective-permute-start | bytes 393224 | tf_op jit(solution)/shard_map/ppermute | solution.py:449
  86.8 7.3 %collective-permute-start.20 = (f32[128,256]{1,0:T(8,128)S(1)}, f32[128,256]{1,0:T(8,128)S(1)}, u32[]{:S(2)}, u32[]{:S(2)}) collective-permute-start(f32[128,256]{1,0:T(8,128)S(1)} %get-tuple-element.79), channel_id=1, source_target_pairs={{0,12},{4,8},{8,4},{12,0},{16,28},{20,24},{24,20},{28,16},{1,13},{... | collective-permute-start | bytes 393224 | tf_op jit(solution)/shard_map/ppermute | solution.py:449

commit v12 on v11

--- a/solution.py
+++ b/solution.py
@@ -17,7 +17,6 @@
 F32 = jnp.float32
 VMEM = pl.BlockSpec(memory_space=pltpu.VMEM)
 HBM = pl.BlockSpec(memory_space=pltpu.HBM)
-ANY = pl.BlockSpec(memory_space=pl.ANY)
 
 
 def exchange(copies, axis):
@@ -154,7 +153,7 @@
     return jnp.broadcast_to(row, (LANE, LANE)).T
 
 
-def first_body(design_ref, target_ref, bits_ref, picks_ref, counts_ref, *refs):
+def first_body(sent, design_ref, target_ref, bits_ref, picks_ref, counts_ref, *refs):
     out_ref, away_refs = refs[0], refs[1:-6]
     design, target_here, bits, picks, counts, sems = refs[-6:]
     rows, width = design.shape
@@ -174,8 +173,8 @@
     away = []
     for index, away_ref in enumerate(away_refs):
         piece = away_ref.shape[1]
-        chunk, mask = index // (NEAR - 1), index % (NEAR - 1) + 1
-        column = pl.multiple_of((place ^ mask) * (width // NEAR) + chunk * piece, LANE)
+        mask, start = sent[index]
+        column = pl.multiple_of((place ^ mask) * (width // NEAR) + start, LANE)
         source = design.at[:, pl.ds(column, piece)]
         away.append(pltpu.make_async_copy(source, away_ref, sems.at[4 + lines + index]))
     for copy in small + large:
@@ -231,7 +230,7 @@
     left_product_long(scratch, rinv_here, term_ref, copies)
 
 
-def forward_body(groups, first, last, rinv_ref, design_ref, *refs):
+def forward_body(groups, first, last, rinv_ref, design_ref, token_ref, *refs):
     right = tree([ref[...] for ref in refs[:groups]])
     refs = refs[groups:]
     if not first:
@@ -249,7 +248,7 @@
 
 def turn_body(groups, last, *refs):
     left = tree([ref[...] for ref in refs[:groups]])
-    before_ref, beta_ref, alpha_ref, token_ref, *refs = refs[groups:]
+    before_ref, beta_ref, alpha_ref, *refs = refs[groups:]
     left = left - alpha_ref[...] * (before_ref[...] / beta_ref[...])
     square = splat(total(left * left))
     if last:
@@ -310,8 +309,9 @@
 
 
 def sample_body(scale, start, design_ref, parts_ref, mix_ref, order_ref, *refs):
-    near, (keep_ref, send_ref, both) = refs[: NEAR - 1], refs[NEAR - 1 :]
-    rows, piece = near[0].shape
+    near, (keep_ref, send_ref, token_ref, both) = refs[: NEAR - 1], refs[NEAR - 1 :]
+    token_ref[...] = order_ref[:1, :]
+    rows, piece = near[-1].shape
     width = design_ref.shape[1]
     groups = mix_ref.shape[0]
     me = lax.axis_index("row")
@@ -322,7 +322,9 @@
         for tile in range(0, piece, LANE):
             column = pl.multiple_of(me % NEAR * (width // NEAR) + start + tile, LANE)
             here = slice(tile, tile + LANE)
-            values = [design_ref[part, pl.ds(column, LANE)]] + [ref[part, here] for ref in near]
+            there = slice(start + tile, start + tile + LANE)
+            values = [design_ref[part, pl.ds(column, LANE)], near[0][part, there]]
+            values += [ref[part, here] for ref in near[1:]]
             values = [value * sign for value, sign in zip(values, signs)]
             apart = 1
             while apart < NEAR:
@@ -357,13 +359,9 @@
     out_ref[...] = kept_ref[0] + arrived_ref[0]
 
 
-def touch_body(*refs):
-    order_ref, token_ref = refs[-2:]
+def split_body(chunks, *refs):
+    joined, (kept_ref, arrived_ref, order_ref, token_ref, *out_refs) = refs[: chunks - 1], refs[chunks - 1 :]
     token_ref[...] = order_ref[:1, :]
-
-
-def split_body(chunks, *refs):
-    joined, (kept_ref, arrived_ref, order_ref, *out_refs) = refs[: chunks - 1], refs[chunks - 1 :]
     piece = kept_ref.shape[3]
     for chunk in range(chunks):
         columns = slice(chunk * piece, (chunk + 1) * piece)
@@ -428,19 +426,22 @@
     slots = row_groups * PAIR
     far = row_groups // NEAR
 
+    sent = [(1, 0)] + [(mask, chunk * piece) for mask in range(2, NEAR) for chunk in range(chunks)]
+    sizes = [piece * chunks] + [piece] * (chunks * (NEAR - 2))
+
     message, *away = pl.pallas_call(
-        first_body,
+        functools.partial(first_body, sent),
         out_shape=(shape(row_groups, rounded(signs_at(width, row_groups) + lines, 8), LANE),)
-        + (shape(rows, piece),) * (chunks * (NEAR - 1)),
+        + tuple(shape(rows, size) for size in sizes),
         in_specs=[HBM] * 5,
-        out_specs=(VMEM,) + (HBM,) * (chunks * (NEAR - 1)),
+        out_specs=(VMEM,) + (HBM,) * len(sent),
         scratch_shapes=[
             pltpu.VMEM((rows, width), F32),
             pltpu.VMEM((lines, LANE), F32),
             pltpu.VMEM((lines, LANE), jnp.int32),
             pltpu.VMEM((row_groups, PAIR), jnp.int32),
             pltpu.VMEM((1, row_groups), jnp.int32),
-            pltpu.SemaphoreType.DMA((4 + lines + chunks * (NEAR - 1),)),
+            pltpu.SemaphoreType.DMA((4 + lines + len(sent),)),
         ],
         compiler_params=pltpu.CompilerParams(vmem_limit_bytes=58 << 20),
     )(design, left, bits, picks.reshape(row_groups, PAIR), counts.reshape(1, row_groups))
@@ -455,19 +456,18 @@
     def sample(chunk, mixed, order):
         return call(
             functools.partial(sample_body, scale, chunk * piece),
-            (shape(far // 2, NEAR, slots, piece),) * 2,
+            (shape(far // 2, NEAR, slots, piece),) * 2 + (scalar,),
             design,
             picked,
             mixed,
             order,
-            *near[chunk],
+            *(near[index] for index, (mask, start) in enumerate(sent) if mask == 1 or start == chunk * piece),
             scratch=[pltpu.VMEM((NEAR, 2, rows, piece), jnp.bfloat16)],
         )
 
-    def spread(chunk, masks, order):
-        parts = [away[chunk * (NEAR - 1) + mask - 1] for mask in masks]
-        parts, _ = lax.optimization_barrier((parts, order))
-        return [swap(part, mask) for mask, part in zip(masks, parts)]
+    def spread(indices, order):
+        parts, _ = lax.optimization_barrier(([away[index] for index in indices], order))
+        return [swap(part, sent[index][0]) for index, part in zip(indices, parts)]
 
     def halve(keep, come, order):
         bit = row_groups // 2
@@ -483,14 +483,14 @@
         return call(join_body, (shape(*keep.shape[1:]), scalar), keep, come, order)
 
     def trade(joined, keep, come, order):
-        mine, *others = call(
+        token, mine, *others = call(
             functools.partial(split_body, chunks),
-            (shape(slots, width // NEAR),) * NEAR,
+            (scalar,) + (shape(slots, width // NEAR),) * NEAR,
             *joined,
             *halve(keep, come, order),
             order,
         )
-        return [mine] + [swap(part, mask + 1) for mask, part in enumerate(others)]
+        return [mine] + [swap(part, mask + 1) for mask, part in enumerate(others)], token
 
     def back(rinv, message, first):
         outs, scratch = (shape(whole // LANE, LANE), scalar), [pltpu.VMEM((width // LANE, LANE), F32)]
@@ -506,18 +506,19 @@
             compiler_params=pltpu.CompilerParams(vmem_limit_bytes=(34 if first else 24) << 20),
             )(rinv, message)
 
-    def forward(terms, last, *before):
+    def forward(terms, token, last, *before):
         return call(
             functools.partial(forward_body, len(terms), not before, last),
             (shape(lines, LANE), shape(width // LANE, LANE), scalar)
             + (() if last else (shape(whole // LANE, LANE),)),
             here,
             design,
+            token,
             *terms,
             *before,
         )
 
-    def turn(images, left, beta, alpha, token, last):
+    def turn(images, left, beta, alpha, last):
         return call(
             functools.partial(turn_body, len(images), last),
             (shape(lines, LANE), shape(row_groups, 8 if last else deep, LANE)),
@@ -525,14 +526,13 @@
             left,
             beta,
             alpha,
-            token,
             *(() if last else (design,)),
         )
 
-    betas, alphas, held, joined = [], [], [], []
+    betas, alphas, held, joined, right = [], [], [], [], []
     message = picked = exchange(message, "row")
-    near = [spread(0, (1, 2, 3), message)]
-    right = []
+    late = len(sent) - 1 if chunks > 1 else len(sent)
+    near = spread(range(late), message)
     for step in range(ITERS):
         last = step + 1 == ITERS
         if step == 0:
@@ -540,37 +540,28 @@
             mixed = mix(message)
         else:
             term, beta = back(here, message, False)
+            token = beta
+            if chunks > 1:
+                part, token = join(keep, come, beta)
+                joined.append(part)
+                keep, send, token = sample(1, mixed, token)
+                come = swap(send, row_groups // 2)
         betas.append(beta)
         spare = chunks > 1 and step > 0
         terms = direct(term, "col") if spare else paired(term, "col")
         if step == 0:
-            near += [spread(chunk, (1, 2), terms[1]) for chunk in range(1, chunks)]
-            keep, send = sample(0, mixed, terms[1])
+            near += spread(range(late, len(sent)), terms[1])
+            keep, send, token = sample(0, mixed, terms[1])
             come = swap(send, row_groups // 2)
-        image, kept, alpha, *right = forward(terms, last, *right, *betas[1:])
+        image, kept, alpha, *right = forward(terms, token, last, *right, *betas[1:])
         alphas.append(alpha)
         held.append(kept)
-        if spare:
-            keep, send = sample(1, mixed, alpha)
-            come = swap(send, row_groups // 2)
         images = direct(image, "col") if spare else paired(image, "col")
-        token = alpha
-        if chunks > 1 and step == 0:
-            part, token = join(keep, come, alpha)
-            joined.append(part)
-            there = [array for arrays in near[1:] for array in arrays]
-            token = pl.pallas_call(
-                touch_body,
-                out_shape=scalar,
-                in_specs=[ANY] * len(there) + [VMEM],
-                out_specs=VMEM,
-                compiler_params=pltpu.CompilerParams(vmem_limit_bytes=2 << 20),
-            )(*there, token)
-        left, message = turn(images, left, beta, alpha, token, last)
+        left, message = turn(images, left, beta, alpha, last)
+        if last:
+            quarters, token = trade(joined, keep, come, left)
+            message, _ = lax.optimization_barrier((message, token))
         message = exchange(message, "row")
-        if step == 0:
-            for chunk in range(1, chunks):
-                near[chunk] += spread(chunk, (3,), message)
     basis, answer = call(
         last_body,
         (shape(lines, LANE), shape(width // LANE, LANE)),
@@ -580,7 +571,7 @@
         *alphas,
         *held,
     )
-    sketch = call(assemble_body, shape(slots, width), *trade(joined, keep, come, message))
+    sketch = call(assemble_body, shape(slots, width), *quarters)
     return (sketch, answer.reshape(-1), basis.reshape(-1))
 
 

time: 95.3 us -> 89.2 us (0.936)
  waiting for transfers between devices: 19.4 us -> 14.6 us
  starting transfers between devices: 17.6 us -> 16.6 us
    ppermute x11 -> x10, waiting for transfers between devices: 11.3 us -> 4.58 us  [swap(): lax.ppermute(array, 'row', [(i, i ^ mask) for i in range(row_groups)])]
    ppermute x4, waiting for transfers between devices: 4.07 us -> 5.94 us  [paired(): come = lax.ppermute(array, axis, [(i, i ^ mask) for i in range(size)])]
    ppermute x11 -> x10, starting transfers between devices: 10.5 us -> 9.48 us  [swap(): lax.ppermute(array, 'row', [(i, i ^ mask) for i in range(row_groups)])]
    pallas_call x2 -> x1, Pallas kernels: 3.61 us -> 3.61 us  [shards(): pl.pallas_call(functools.partial(first_body, sent), out_shape=(shape(row_...]
  transfers between devices with their start and end apart: 21 -> 20, of which waited for: 11 -> 10; matrix products, arithmetic and copies ran while one was open for 0% -> 0% of each run, Pallas kernels for 15% -> 18%
where the time goes in v12:
time: 89.2 us; the launch traced here: 88.9 us
  blocking collectives  35.2 us (39%)
  Pallas kernels  21.8 us (24%)
  starting transfers between devices  16.6 us (19%)
  waiting for transfers between devices  14.6 us (16%)
    all_to_all x3, blocking collectives, exchange(): return lax.all_to_all(copies, axis, split_axis=0, concat_axis=0, tiled=True)  35.2 us
    pallas_call x11, Pallas kernels, call(): pl.pallas_call(body, out_shape=out_shape, in_specs=[VMEM] * len(operands)...  10 us
    ppermute x10, starting transfers between devices, swap(): lax.ppermute(array, 'row', [(i, i ^ mask) for i in range(row_groups)])  9.48 us
    pallas_call x2, Pallas kernels, back(): pl.pallas_call(functools.partial(back_body, first), out_shape=outs, in_sp...  8.15 us
    ppermute x4, waiting for transfers between devices, paired(): come = lax.ppermute(array, axis, [(i, i ^ mask) for i in range(size)])  5.94 us
    ppermute x10, waiting for transfers between devices, swap(): lax.ppermute(array, 'row', [(i, i ^ mask) for i in range(row_groups)])  4.58 us
    ppermute x6, waiting for transfers between devices, direct(): lax.ppermute(array, axis, [(i, i ^ mask) for i in range(size)])  4.03 us
    ppermute x6, starting transfers between devices, direct(): lax.ppermute(array, axis, [(i, i ^ mask) for i in range(size)])  4 us
  transfers between devices with their start and end apart: 20, of which 10 were waited for; matrix products, arithmetic and copies ran while one was open for 0% of the time, Pallas kernels for 18%

profile of v12, /device:TPU:0, one launch (start us, length us, event | category | flops | bytes accessed | tf_op | source)
XLA Modules:
  0.0 88.9 jit_solution(2485447527435596167)
XLA Ops:
  0.7 3.6 %shard_map.94 = (f32[8,16,128]{2,1,0:T(8,128)}, f32[512,256]{1,0:T(8,128)}, f32[512,128]{1,0:T(8,128)}, f32[512,128]{1,0:T(8,128)}, f32[512,128]{1,0:T(8,128)}, /*index=5*/f32[512,128]{1,0:T(8,128)}) custom-call(f32[512,1024]{1,0:T(8,128)} %design_ref.9, f32[4,128]{1,0:T(4,128)} %bitcast.6, s32[4,128]{1,0:T(4,128)} %bitcast.9, s32[8,16]{1,0:T(8,128)} %bitcast.8, ...), custom_call_target="tpu_custom_call" | custom-call | tf_op jit(solution)/shard_map/pallas_call | solution.py:432
  4.3 14.3 %all_to_all.15.parts_ref = f32[8,16,128]{2,1,0:T(8,128)S(1)} all-to-all(f32[8,16,128]{2,1,0:T(8,128)} %get-tuple-element.44), channel_id=1, replica_groups=mesh['row'=8,'col'=4] {'row'}, dimensions={0} | all-to-all | bytes 131072 | tf_op jit(solution)/shard_map/all_to_all | solution.py:23
  19.0 0.8 collective-permute-start.3
  19.8 2.3 %collective-permute-start.4 = (f32[512,128]{1,0:T(8,128)}, f32[512,128]{1,0:T(8,128)S(1)}, u32[]{:S(2)}, u32[]{:S(2)}) collective-permute-start(f32[512,128]{1,0:T(8,128)} %get-tuple-element.52), channel_id=1, source_target_pairs={{0,12},{4,8},{8,4},{12,0},{16,28},{20,24},{24,20},{28,16},{1,13},{... | collective-permute-start | bytes 786440 | tf_op jit(solution)/shard_map/ppermute | solution.py:450
  22.1 6.2 %shard_map.96 = (f32[32,128]{1,0:T(8,128)S(1)}, f32[1,128]{1,0:T(1,128)S(1)}, f32[1024,4096]{1,0:T(8,128)S(1)}) custom-call(f32[1024,4096]{1,0:T(8,128)} %rinv_ref.1, f32[8,16,128]{2,1,0:T(8,128)S(1)} %all_to_all.15.parts_ref), custom_call_target="tpu_custom_call" | custom-call | tf_op jit(solution)/shard_map/pallas_call | solution.py:500
  28.4 1.2 %collective-permute-done = f32[32,128]{1,0:T(8,128)S(1)} collective-permute-done((f32[32,128]{1,0:T(8,128)S(1)}, f32[32,128]{1,0:T(8,128)S(1)}, u32[]{:S(2)}, u32[]{:S(2)}) %collective-permute-start) | collective-permute-done | bytes 16416 | tf_op jit(solution)/shard_map/ppermute | solution.py:30
  29.6 1.5 %collective-permute-start.1 = (f32[32,128]{1,0:T(8,128)S(1)}, f32[32,128]{1,0:T(8,128)S(1)}, u32[]{:S(2)}, u32[]{:S(2)}) collective-permute-start(f32[32,128]{1,0:T(8,128)S(1)} %add.6.refs_0_), channel_id=1, source_target_pairs={{0,2},{1,3},{2,0},{3,1},{4,6},{5,7},{6,4},{7,5},{8,10},{9,11},{10,... | collective-permute-start | bytes 49160 | tf_op jit(solution)/shard_map/ppermute | solution.py:30
  31.8 1.5 %collective-permute-done.1.order_ref.refs_1_ = f32[32,128]{1,0:T(8,128)S(1)} collective-permute-done((f32[32,128]{1,0:T(8,128)S(1)}, f32[32,128]{1,0:T(8,128)S(1)}, u32[]{:S(2)}, u32[]{:S(2)}) %collective-permute-start.1) | collective-permute-done | bytes 16416 | tf_op jit(solution)/shard_map/ppermute | solution.py:30
  33.3 3.4 %collective-permute-done.2.refs_0_ = f32[512,256]{1,0:T(8,128)S(1)} collective-permute-done((f32[512,256]{1,0:T(8,128)}, f32[512,256]{1,0:T(8,128)S(1)}, u32[]{:S(2)}, u32[]{:S(2)}) %collective-permute-start.2) | collective-permute-done | bytes 524320 | tf_op jit(solution)/shard_map/ppermute | solution.py:450
  36.7 1.1 %shard_map.97 = (f32[1,4,128,128]{3,2,1,0:T(8,128)S(1)}, f32[1,4,128,128]{3,2,1,0:T(8,128)S(1)}, f32[1,128]{1,0:T(1,128)S(1)}) custom-call(f32[512,1024]{1,0:T(8,128)S(1)} %copy-done, f32[8,16,128]{2,1,0:T(8,128)S(1)} %all_to_all.15.parts_ref, bf16[8,128,512]{2,1,0:T(8,128)(2,1)S(1)} %shard_map.95.mix_ref, ...), custom_call_target="tpu_custom_call" | custom-call | tf_op jit(solution)/shard_map/pallas_call | solution.py:60
  37.8 0.8 collective-permute-start.5
  38.6 0.9 %collective-permute-start.9 = (f32[512,128]{1,0:T(8,128)S(1)}, f32[512,128]{1,0:T(8,128)S(1)}, u32[]{:S(2)}, u32[]{:S(2)}) collective-permute-start(f32[512,128]{1,0:T(8,128)S(1)} %copy-done.3), channel_id=1, source_target_pairs={{0,12},{4,8},{8,4},{12,0},{16,28},{20,24},{24,20},{28,16},{1,13},{... | collective-permute-start | bytes 786440 | tf_op jit(solution)/shard_map/ppermute | solution.py:450
  39.5 2.5 %shard_map.98 = (f32[4,128]{1,0:T(4,128)S(1)}, f32[8,128]{1,0:T(8,128)S(1)}, f32[1,128]{1,0:T(1,128)S(1)}, f32[32,128]{1,0:T(8,128)S(1)}) custom-call(f32[1024,4096]{1,0:T(8,128)S(1)} %get-tuple-element.55.rinv_ref, f32[512,1024]{1,0:T(8,128)S(1)} %copy-done, f32[1,128]{1,0:T(1,128)S(1)} %get-tuple-element.56.token_ref, f32[32,128]{1,0:T(8,128)S(1)} %add.6.refs_0_, ...), custom_call_target="tpu_custom_call" | custom-call | tf_op jit(solution)/shard_map/pallas_call | solution.py:60
  42.1 1.1 %collective-permute-done.6 = f32[4,128]{1,0:T(4,128)S(1)} collective-permute-done((f32[4,128]{1,0:T(4,128)S(1)}, f32[4,128]{1,0:T(4,128)S(1)}, u32[]{:S(2)}, u32[]{:S(2)}) %collective-permute-start.6) | collective-permute-done | bytes 2080 | tf_op jit(solution)/shard_map/ppermute | solution.py:30
  43.2 1.5 %collective-permute-start.7 = (f32[4,128]{1,0:T(4,128)S(1)}, f32[4,128]{1,0:T(4,128)S(1)}, u32[]{:S(2)}, u32[]{:S(2)}) collective-permute-start(f32[4,128]{1,0:T(4,128)S(1)} %add.7.refs_0_), channel_id=1, source_target_pairs={{0,2},{1,3},{2,0},{3,1},{4,6},{5,7},{6,4},{7,5},{8,10},{9,11},{10,... | collective-permute-start | bytes 6152 | tf_op jit(solution)/shard_map/ppermute | solution.py:30
  44.7 2.1 %collective-permute-done.7.refs_1_ = f32[4,128]{1,0:T(4,128)S(1)} collective-permute-done((f32[4,128]{1,0:T(4,128)S(1)}, f32[4,128]{1,0:T(4,128)S(1)}, u32[]{:S(2)}, u32[]{:S(2)}) %collective-permute-start.7) | collective-permute-done | bytes 2080 | tf_op jit(solution)/shard_map/ppermute | solution.py:30
  47.0 11.6 %all_to_all.16.parts_ref = f32[8,16,128]{2,1,0:T(8,128)S(1)} all-to-all(f32[8,16,128]{2,1,0:T(8,128)S(1)} %get-tuple-element.60), channel_id=1, replica_groups=mesh['row'=8,'col'=4] {'row'}, dimensions={0} | all-to-all | bytes 131072 | tf_op jit(solution)/shard_map/all_to_all | solution.py:23
  58.6 2.0 %shard_map.100 = (f32[32,128]{1,0:T(8,128)S(1)}, f32[1,128]{1,0:T(1,128)S(1)}) custom-call(f32[1024,4096]{1,0:T(8,128)S(1)} %get-tuple-element.55.rinv_ref, f32[8,16,128]{2,1,0:T(8,128)S(1)} %all_to_all.16.parts_ref), custom_call_target="tpu_custom_call" | custom-call | tf_op jit(solution)/shard_map/pallas_call | solution.py:500
  60.7 1.1 %shard_map.102 = (f32[1,4,128,128]{3,2,1,0:T(8,128)S(1)}, f32[1,4,128,128]{3,2,1,0:T(8,128)S(1)}, f32[1,128]{1,0:T(1,128)S(1)}) custom-call(f32[512,1024]{1,0:T(8,128)S(1)} %copy-done, f32[8,16,128]{2,1,0:T(8,128)S(1)} %all_to_all.15.parts_ref, bf16[8,128,512]{2,1,0:T(8,128)(2,1)S(1)} %shard_map.95.mix_ref, f32[1,128]{1,0:T(1,128)S(1)} %get-tuple-element.63.order_ref, ...), custom_call_target="tpu_custom_call" | custom-call | tf_op jit(solution)/shard_map/pallas_call | solution.py:60
  62.3 1.5 %collective-permute-start.12 = (f32[32,128]{1,0:T(8,128)S(1)}, f32[32,128]{1,0:T(8,128)S(1)}, u32[]{:S(2)}, u32[]{:S(2)}) collective-permute-start(f32[32,128]{1,0:T(8,128)S(1)} %get-tuple-element.70.refs_0_), channel_id=1, source_target_pairs={{0,2},{1,3},{2,0},{3,1},{4,6},{5,7},{6,4},{7,5},{8,10},{9,11},{10,... | collective-permute-start | bytes 49160 | tf_op jit(solution)/shard_map/ppermute | solution.py:40
  64.2 1.4 %collective-permute-done.13.refs_3_ = f32[32,128]{1,0:T(8,128)S(1)} collective-permute-done((f32[32,128]{1,0:T(8,128)S(1)}, f32[32,128]{1,0:T(8,128)S(1)}, u32[]{:S(2)}, u32[]{:S(2)}) %collective-permute-start.13) | collective-permute-done | bytes 16416 | tf_op jit(solution)/shard_map/ppermute | solution.py:40
  66.1 2.5 %shard_map.103 = (f32[4,128]{1,0:T(4,128)S(1)}, f32[8,128]{1,0:T(8,128)S(1)}, f32[1,128]{1,0:T(1,128)S(1)}) custom-call(f32[1024,4096]{1,0:T(8,128)S(1)} %get-tuple-element.55.rinv_ref, f32[512,1024]{1,0:T(8,128)S(1)} %copy-done, f32[1,128]{1,0:T(1,128)S(1)} %get-tuple-element.69.token_ref, f32[32,128]{1,0:T(8,128)S(1)} %get-tuple-element.70.refs_0_, ...), custom_call_target="tpu_custom_call" | custom-call | tf_op jit(solution)/shard_map/pallas_call | solution.py:60
  68.6 0.7 collective-permute-start.16
  69.2 1.5 %collective-permute-start.15 = (f32[4,128]{1,0:T(4,128)S(1)}, f32[4,128]{1,0:T(4,128)S(1)}, u32[]{:S(2)}, u32[]{:S(2)}) collective-permute-start(f32[4,128]{1,0:T(4,128)S(1)} %get-tuple-element.72.refs_0_), channel_id=1, source_target_pairs={{0,2},{1,3},{2,0},{3,1},{4,6},{5,7},{6,4},{7,5},{8,10},{9,11},{10,... | collective-permute-start | bytes 6152 | tf_op jit(solution)/shard_map/ppermute | solution.py:40
  70.7 0.9 %collective-permute-done.16.refs_3_ = f32[4,128]{1,0:T(4,128)S(1)} collective-permute-done((f32[4,128]{1,0:T(4,128)S(1)}, f32[4,128]{1,0:T(4,128)S(1)}, u32[]{:S(2)}, u32[]{:S(2)}) %collective-permute-start.16) | collective-permute-done | bytes 2080 | tf_op jit(solution)/shard_map/ppermute | solution.py:40
  71.6 1.2 %collective-permute-done.15.refs_2_ = f32[4,128]{1,0:T(4,128)S(1)} collective-permute-done((f32[4,128]{1,0:T(4,128)S(1)}, f32[4,128]{1,0:T(4,128)S(1)}, u32[]{:S(2)}, u32[]{:S(2)}) %collective-permute-start.15) | collective-permute-done | bytes 2080 | tf_op jit(solution)/shard_map/ppermute | solution.py:40
  72.9 1.2 %collective-permute-done.10.refs_2_ = f32[1,4,128,128]{3,2,1,0:T(8,128)S(1)} collective-permute-done((f32[1,4,128,128]{3,2,1,0:T(8,128)S(1)}, f32[1,4,128,128]{3,2,1,0:T(8,128)S(1)}, u32[]{:S(2)}, u32[]{:S(2)}) %collective-permute-start.10) | collective-permute-done | bytes 262176 | tf_op jit(solution)/shard_map/ppermute | solution.py:450
  74.7 0.8 collective-permute-start.17
  75.5 2.6 %collective-permute-start.19 = (f32[128,256]{1,0:T(8,128)S(1)}, f32[128,256]{1,0:T(8,128)S(1)}, u32[]{:S(2)}, u32[]{:S(2)}) collective-permute-start(f32[128,256]{1,0:T(8,128)S(1)} %get-tuple-element.79), channel_id=1, source_target_pairs={{0,12},{4,8},{8,4},{12,0},{16,28},{20,24},{24,20},{28,16},{1,13},{... | collective-permute-start | bytes 393224 | tf_op jit(solution)/shard_map/ppermute | solution.py:450
  78.1 9.3 %all_to_all.17.parts_ref = f32[8,8,128]{2,1,0:T(8,128)S(1)} all-to-all(f32[8,8,128]{2,1,0:T(8,128)S(1)} %get-tuple-element.80), channel_id=1, replica_groups=mesh['row'=8,'col'=4] {'row'}, dimensions={0} | all-to-all | bytes 65536 | tf_op jit(solution)/shard_map/all_to_all | solution.py:23
  87.4 0.6 shard_map.107
  88.1 0.9 shard_map.106
  (37 shorter events, 3.6 us)
Async XLA Ops:
  0.6 30.6 %copy-start.1 = (bf16[256,256]{1,0:T(8,128)(2,1)S(1)}, bf16[256,256]{1,0:T(8,128)(2,1)}, u32[]{:S(2)}) copy-start(bf16[256,256]{1,0:T(8,128)(2,1)} %constant.2.clone.walsh_ref) | copy-start | bytes 393220
  0.6 36.0 %copy-start = (f32[512,1024]{1,0:T(8,128)S(1)}, f32[512,1024]{1,0:T(8,128)}, u32[]{:S(2)}) copy-start(f32[512,1024]{1,0:T(8,128)} %design_ref.9) | copy-start | bytes 6291460
  4.3 26.8 %copy-start.4 = (f32[512,128]{1,0:T(8,128)S(1)}, f32[512,128]{1,0:T(8,128)}, u32[]{:S(2)}) copy-start(f32[512,128]{1,0:T(8,128)} %get-tuple-element.64) | copy-start | bytes 786436
  4.3 34.3 %copy-start.3 = (f32[512,128]{1,0:T(8,128)S(1)}, f32[512,128]{1,0:T(8,128)}, u32[]{:S(2)}) copy-start(f32[512,128]{1,0:T(8,128)} %get-tuple-element.66) | copy-start | bytes 786436
  18.6 28.2 %copy-start.2 = (f32[512]{0:T(512)S(1)}, f32[512]{0:T(512)}, u32[]{:S(2)}) copy-start(f32[512]{0:T(512)} %param.11) | copy-start | bytes 6148
  18.6 18.1 %collective-permute-start.2 = (f32[512,256]{1,0:T(8,128)}, f32[512,256]{1,0:T(8,128)S(1)}, u32[]{:S(2)}, u32[]{:S(2)}) collective-permute-start(f32[512,256]{1,0:T(8,128)} %get-tuple-element.50), channel_id=1, source_target_pairs={{0,4},{4,0},{8,12},{12,8},{16,20},{20,16},{24,28},{28,24},{1,5},{5... | collective-permute-start | bytes 1572872 | tf_op jit(solution)/shard_map/ppermute | solution.py:450
  19.0 14.3 %collective-permute-start.3 = (f32[512,128]{1,0:T(8,128)}, f32[512,128]{1,0:T(8,128)S(1)}, u32[]{:S(2)}, u32[]{:S(2)}) collective-permute-start(f32[512,128]{1,0:T(8,128)} %get-tuple-element.51), channel_id=1, source_target_pairs={{0,8},{4,12},{8,0},{12,4},{16,24},{20,28},{24,16},{28,20},{1,9},{5... | collective-permute-start | bytes 786440 | tf_op jit(solution)/shard_map/ppermute | solution.py:450
  19.8 13.5 %collective-permute-start.4 = (f32[512,128]{1,0:T(8,128)}, f32[512,128]{1,0:T(8,128)S(1)}, u32[]{:S(2)}, u32[]{:S(2)}) collective-permute-start(f32[512,128]{1,0:T(8,128)} %get-tuple-element.52), channel_id=1, source_target_pairs={{0,12},{4,8},{8,4},{12,0},{16,28},{20,24},{24,20},{28,16},{1,13},{... | collective-permute-start | bytes 786440 | tf_op jit(solution)/shard_map/ppermute | solution.py:450
  28.3 1.2 %collective-permute-start = (f32[32,128]{1,0:T(8,128)S(1)}, f32[32,128]{1,0:T(8,128)S(1)}, u32[]{:S(2)}, u32[]{:S(2)}) collective-permute-start(f32[32,128]{1,0:T(8,128)S(1)} %get-tuple-element.45), channel_id=1, source_target_pairs={{0,1},{1,0},{2,3},{3,2},{4,5},{5,4},{6,7},{7,6},{8,9},{9,8},{10,11... | collective-permute-start | bytes 49160 | tf_op jit(solution)/shard_map/ppermute | solution.py:30
  29.6 3.7 %collective-permute-start.1 = (f32[32,128]{1,0:T(8,128)S(1)}, f32[32,128]{1,0:T(8,128)S(1)}, u32[]{:S(2)}, u32[]{:S(2)}) collective-permute-start(f32[32,128]{1,0:T(8,128)S(1)} %add.6.refs_0_), channel_id=1, source_target_pairs={{0,2},{1,3},{2,0},{3,1},{4,6},{5,7},{6,4},{7,5},{8,10},{9,11},{10,... | collective-permute-start | bytes 49160 | tf_op jit(solution)/shard_map/ppermute | solution.py:30
  31.0 29.6 %collective-permute-start.8 = (f32[512,128]{1,0:T(8,128)S(1)}, f32[512,128]{1,0:T(8,128)S(1)}, u32[]{:S(2)}, u32[]{:S(2)}) collective-permute-start(f32[512,128]{1,0:T(8,128)S(1)} %copy-done.4), channel_id=1, source_target_pairs={{0,8},{4,12},{8,0},{12,4},{16,24},{20,28},{24,16},{28,20},{1,9},{5... | collective-permute-start | bytes 786440 | tf_op jit(solution)/shard_map/ppermute | solution.py:450
  37.8 22.8 %collective-permute-start.5 = (f32[1,4,128,128]{3,2,1,0:T(8,128)S(1)}, f32[1,4,128,128]{3,2,1,0:T(8,128)S(1)}, u32[]{:S(2)}, u32[]{:S(2)}) collective-permute-start(f32[1,4,128,128]{3,2,1,0:T(8,128)S(1)} %get-tuple-element.54), channel_id=1, source_target_pairs={{0,16},{4,20},{8,24},{12,28},{16,0},{20,4},{24,8},{28,12},{1,17},{... | collective-permute-start | bytes 786440 | tf_op jit(solution)/shard_map/ppermute | solution.py:450
  38.6 22.0 %collective-permute-start.9 = (f32[512,128]{1,0:T(8,128)S(1)}, f32[512,128]{1,0:T(8,128)S(1)}, u32[]{:S(2)}, u32[]{:S(2)}) collective-permute-start(f32[512,128]{1,0:T(8,128)S(1)} %copy-done.3), channel_id=1, source_target_pairs={{0,12},{4,8},{8,4},{12,0},{16,28},{20,24},{24,20},{28,16},{1,13},{... | collective-permute-start | bytes 786440 | tf_op jit(solution)/shard_map/ppermute | solution.py:450
  42.0 1.2 %collective-permute-start.6 = (f32[4,128]{1,0:T(4,128)S(1)}, f32[4,128]{1,0:T(4,128)S(1)}, u32[]{:S(2)}, u32[]{:S(2)}) collective-permute-start(f32[4,128]{1,0:T(4,128)S(1)} %get-tuple-element.57), channel_id=1, source_target_pairs={{0,1},{1,0},{2,3},{3,2},{4,5},{5,4},{6,7},{7,6},{8,9},{9,8},{10,11... | collective-permute-start | bytes 6152 | tf_op jit(solution)/shard_map/ppermute | solution.py:30
  43.2 3.6 %collective-permute-start.7 = (f32[4,128]{1,0:T(4,128)S(1)}, f32[4,128]{1,0:T(4,128)S(1)}, u32[]{:S(2)}, u32[]{:S(2)}) collective-permute-start(f32[4,128]{1,0:T(4,128)S(1)} %add.7.refs_0_), channel_id=1, source_target_pairs={{0,2},{1,3},{2,0},{3,1},{4,6},{5,7},{6,4},{7,5},{8,10},{9,11},{10,... | collective-permute-start | bytes 6152 | tf_op jit(solution)/shard_map/ppermute | solution.py:30
  61.8 12.3 %collective-permute-start.10 = (f32[1,4,128,128]{3,2,1,0:T(8,128)S(1)}, f32[1,4,128,128]{3,2,1,0:T(8,128)S(1)}, u32[]{:S(2)}, u32[]{:S(2)}) collective-permute-start(f32[1,4,128,128]{3,2,1,0:T(8,128)S(1)} %get-tuple-element.68), channel_id=1, source_target_pairs={{0,16},{4,20},{8,24},{12,28},{16,0},{20,4},{24,8},{28,12},{1,17},{... | collective-permute-start | bytes 786440 | tf_op jit(solution)/shard_map/ppermute | solution.py:450
  62.3 3.3 %collective-permute-start.13 = (f32[32,128]{1,0:T(8,128)S(1)}, f32[32,128]{1,0:T(8,128)S(1)}, u32[]{:S(2)}, u32[]{:S(2)}) collective-permute-start(f32[32,128]{1,0:T(8,128)S(1)} %get-tuple-element.70.refs_0_), channel_id=1, source_target_pairs={{0,3},{1,2},{2,1},{3,0},{4,7},{5,6},{6,5},{7,4},{8,11},{9,10},{10,... | collective-permute-start | bytes 49160 | tf_op jit(solution)/shard_map/ppermute | solution.py:40
  62.3 3.8 %collective-permute-start.12 = (f32[32,128]{1,0:T(8,128)S(1)}, f32[32,128]{1,0:T(8,128)S(1)}, u32[]{:S(2)}, u32[]{:S(2)}) collective-permute-start(f32[32,128]{1,0:T(8,128)S(1)} %get-tuple-element.70.refs_0_), channel_id=1, source_target_pairs={{0,2},{1,3},{2,0},{3,1},{4,6},{5,7},{6,4},{7,5},{8,10},{9,11},{10,... | collective-permute-start | bytes 49160 | tf_op jit(solution)/shard_map/ppermute | solution.py:40
  63.8 2.2 %collective-permute-start.11 = (f32[32,128]{1,0:T(8,128)S(1)}, f32[32,128]{1,0:T(8,128)S(1)}, u32[]{:S(2)}, u32[]{:S(2)}) collective-permute-start(f32[32,128]{1,0:T(8,128)S(1)} %get-tuple-element.70.refs_0_), channel_id=1, source_target_pairs={{0,1},{1,0},{2,3},{3,2},{4,5},{5,4},{6,7},{7,6},{8,9},{9,8},{10,11... | collective-permute-start | bytes 49160 | tf_op jit(solution)/shard_map/ppermute | solution.py:40
  68.6 3.1 %collective-permute-start.16 = (f32[4,128]{1,0:T(4,128)S(1)}, f32[4,128]{1,0:T(4,128)S(1)}, u32[]{:S(2)}, u32[]{:S(2)}) collective-permute-start(f32[4,128]{1,0:T(4,128)S(1)} %get-tuple-element.72.refs_0_), channel_id=1, source_target_pairs={{0,3},{1,2},{2,1},{3,0},{4,7},{5,6},{6,5},{7,4},{8,11},{9,10},{10,... | collective-permute-start | bytes 6152 | tf_op jit(solution)/shard_map/ppermute | solution.py:40
  69.2 3.6 %collective-permute-start.15 = (f32[4,128]{1,0:T(4,128)S(1)}, f32[4,128]{1,0:T(4,128)S(1)}, u32[]{:S(2)}, u32[]{:S(2)}) collective-permute-start(f32[4,128]{1,0:T(4,128)S(1)} %get-tuple-element.72.refs_0_), channel_id=1, source_target_pairs={{0,2},{1,3},{2,0},{3,1},{4,6},{5,7},{6,4},{7,5},{8,10},{9,11},{10,... | collective-permute-start | bytes 6152 | tf_op jit(solution)/shard_map/ppermute | solution.py:40
  70.7 2.1 %collective-permute-start.14 = (f32[4,128]{1,0:T(4,128)S(1)}, f32[4,128]{1,0:T(4,128)S(1)}, u32[]{:S(2)}, u32[]{:S(2)}) collective-permute-start(f32[4,128]{1,0:T(4,128)S(1)} %get-tuple-element.72.refs_0_), channel_id=1, source_target_pairs={{0,1},{1,0},{2,3},{3,2},{4,5},{5,4},{6,7},{7,6},{8,9},{9,8},{10,11... | collective-permute-start | bytes 6152 | tf_op jit(solution)/shard_map/ppermute | solution.py:40
  74.7 13.4 %collective-permute-start.17 = (f32[128,256]{1,0:T(8,128)S(1)}, f32[128,256]{1,0:T(8,128)S(1)}, u32[]{:S(2)}, u32[]{:S(2)}) collective-permute-start(f32[128,256]{1,0:T(8,128)S(1)} %get-tuple-element.77), channel_id=1, source_target_pairs={{0,4},{4,0},{8,12},{12,8},{16,20},{20,16},{24,28},{28,24},{1,5},{5... | collective-permute-start | bytes 393224 | tf_op jit(solution)/shard_map/ppermute | solution.py:450
  75.5 12.6 %collective-permute-start.18 = (f32[128,256]{1,0:T(8,128)S(1)}, f32[128,256]{1,0:T(8,128)S(1)}, u32[]{:S(2)}, u32[]{:S(2)}) collective-permute-start(f32[128,256]{1,0:T(8,128)S(1)} %get-tuple-element.78), channel_id=1, source_target_pairs={{0,8},{4,12},{8,0},{12,4},{16,24},{20,28},{24,16},{28,20},{1,9},{5... | collective-permute-start | bytes 393224 | tf_op jit(solution)/shard_map/ppermute | solution.py:450
  75.5 12.6 %collective-permute-start.19 = (f32[128,256]{1,0:T(8,128)S(1)}, f32[128,256]{1,0:T(8,128)S(1)}, u32[]{:S(2)}, u32[]{:S(2)}) collective-permute-start(f32[128,256]{1,0:T(8,128)S(1)} %get-tuple-element.79), channel_id=1, source_target_pairs={{0,12},{4,8},{8,4},{12,0},{16,28},{20,24},{24,20},{28,16},{1,13},{... | collective-permute-start | bytes 393224 | tf_op jit(solution)/shard_map/ppermute | solution.py:450

commit v13 on v12

--- a/solution.py
+++ b/solution.py
@@ -252,8 +252,15 @@
     left = left - alpha_ref[...] * (before_ref[...] / beta_ref[...])
     square = splat(total(left * left))
     if last:
-        left_ref, out_ref = refs
+        *parts, left_ref, out_ref = refs[: -NEAR]
+        out_refs = refs[-NEAR:]
         out_ref[...] = jnp.broadcast_to(square, out_ref.shape)
+        *joined, kept_ref, arrived_ref = parts
+        piece = kept_ref.shape[3]
+        for index, rows_ref in enumerate(out_refs):
+            for chunk, part_ref in enumerate(joined):
+                rows_ref[:, chunk * piece : (chunk + 1) * piece] = part_ref[index]
+            rows_ref[:, len(joined) * piece :] = kept_ref[0, index] + arrived_ref[0, index]
     else:
         design_ref, left_ref, out_ref = refs
         tiles = design_ref.shape[1] // LANE
@@ -359,31 +366,15 @@
     out_ref[...] = kept_ref[0] + arrived_ref[0]
 
 
-def split_body(chunks, *refs):
-    joined, (kept_ref, arrived_ref, order_ref, token_ref, *out_refs) = refs[: chunks - 1], refs[chunks - 1 :]
-    token_ref[...] = order_ref[:1, :]
-    piece = kept_ref.shape[3]
-    for chunk in range(chunks):
-        columns = slice(chunk * piece, (chunk + 1) * piece)
-        for index, out_ref in enumerate(out_refs):
-            if chunk < chunks - 1:
-                out_ref[:, columns] = joined[chunk][index]
-            else:
-                out_ref[:, columns] = kept_ref[0, index] + arrived_ref[0, index]
-
-
-def assemble_body(*refs):
-    quarters, sketch_ref = refs[:-1], refs[-1]
+def last_body(parts_ref, left_ref, *refs):
+    basis_ref, solution_ref, sketch_ref = refs[-3:]
+    quarters = refs[3 * ITERS : 3 * ITERS + NEAR]
     place = lax.axis_index("row") % NEAR
     piece = quarters[0].shape[1]
     for mask, part_ref in enumerate(quarters):
         for tile in range(0, piece, LANE):
             column = pl.multiple_of((place ^ mask) * piece + tile, LANE)
             sketch_ref[:, pl.ds(column, LANE)] = part_ref[:, tile : tile + LANE]
-
-
-def last_body(parts_ref, left_ref, *refs):
-    basis_ref, solution_ref = refs[-2:]
     betas = [ref[...] for ref in refs[:ITERS]]
     alphas = [ref[...] for ref in refs[ITERS : 2 * ITERS]]
     held = [ref[...] for ref in refs[2 * ITERS : 3 * ITERS]]
@@ -482,16 +473,6 @@
         keep, come = halve(keep, come, order)
         return call(join_body, (shape(*keep.shape[1:]), scalar), keep, come, order)
 
-    def trade(joined, keep, come, order):
-        token, mine, *others = call(
-            functools.partial(split_body, chunks),
-            (scalar,) + (shape(slots, width // NEAR),) * NEAR,
-            *joined,
-            *halve(keep, come, order),
-            order,
-        )
-        return [mine] + [swap(part, mask + 1) for mask, part in enumerate(others)], token
-
     def back(rinv, message, first):
         outs, scratch = (shape(whole // LANE, LANE), scalar), [pltpu.VMEM((width // LANE, LANE), F32)]
         if first:
@@ -518,15 +499,16 @@
             *before,
         )
 
-    def turn(images, left, beta, alpha, last):
+    def turn(images, left, beta, alpha, parts):
         return call(
-            functools.partial(turn_body, len(images), last),
-            (shape(lines, LANE), shape(row_groups, 8 if last else deep, LANE)),
+            functools.partial(turn_body, len(images), bool(parts)),
+            (shape(lines, LANE), shape(row_groups, 8 if parts else deep, LANE))
+            + (shape(slots, width // NEAR),) * (NEAR if parts else 0),
             *images,
             left,
             beta,
             alpha,
-            *(() if last else (design,)),
+            *(parts or (design,)),
         )
 
     betas, alphas, held, joined, right = [], [], [], [], []
@@ -557,21 +539,21 @@
         alphas.append(alpha)
         held.append(kept)
         images = direct(image, "col") if spare else paired(image, "col")
-        left, message = turn(images, left, beta, alpha, last)
-        if last:
-            quarters, token = trade(joined, keep, come, left)
-            message, _ = lax.optimization_barrier((message, token))
+        parts = (*joined, *halve(keep, come, beta)) if last else ()
+        left, message, *quarters = turn(images, left, beta, alpha, parts)
         message = exchange(message, "row")
-    basis, answer = call(
+    mine, *others = quarters
+    basis, answer, sketch = call(
         last_body,
-        (shape(lines, LANE), shape(width // LANE, LANE)),
+        (shape(lines, LANE), shape(width // LANE, LANE), shape(slots, width)),
         message,
         left,
         *betas,
         *alphas,
         *held,
+        mine,
+        *(swap(part, mask + 1) for mask, part in enumerate(others)),
     )
-    sketch = call(assemble_body, shape(slots, width), *quarters)
     return (sketch, answer.reshape(-1), basis.reshape(-1))
 
 

time: 89.2 us -> 88.2 us (0.989)
  Pallas kernels: 21.8 us -> 20.6 us
    pallas_call x11 -> x9, Pallas kernels: 10 us -> 8.86 us  [call(): pl.pallas_call(body, out_shape=out_shape, in_specs=[VMEM] * len(operands)...]
  transfers between devices with their start and end apart: 20 -> 20, of which waited for: 10 -> 10; matrix products, arithmetic and copies ran while one was open for 0% -> 0% of each run, Pallas kernels for 18% -> 17%
where the time goes in v13:
time: 88.2 us; the launch traced here: 87.8 us
  blocking collectives  35.1 us (40%)
  Pallas kernels  20.6 us (23%)
  starting transfers between devices  16.6 us (19%)
  waiting for transfers between devices  14.7 us (17%)
    all_to_all x3, blocking collectives, exchange(): return lax.all_to_all(copies, axis, split_axis=0, concat_axis=0, tiled=True)  35.1 us
    ppermute x10, starting transfers between devices, swap(): lax.ppermute(array, 'row', [(i, i ^ mask) for i in range(row_groups)])  9.51 us
    pallas_call x9, Pallas kernels, call(): pl.pallas_call(body, out_shape=out_shape, in_specs=[VMEM] * len(operands)...  8.86 us
    pallas_call x2, Pallas kernels, back(): pl.pallas_call(functools.partial(back_body, first), out_shape=outs, in_sp...  8.15 us
    ppermute x4, waiting for transfers between devices, paired(): come = lax.ppermute(array, axis, [(i, i ^ mask) for i in range(size)])  5.94 us
    ppermute x10, waiting for transfers between devices, swap(): lax.ppermute(array, 'row', [(i, i ^ mask) for i in range(row_groups)])  4.68 us
    ppermute x6, waiting for transfers between devices, direct(): lax.ppermute(array, axis, [(i, i ^ mask) for i in range(size)])  4.03 us
    ppermute x6, starting transfers between devices, direct(): lax.ppermute(array, axis, [(i, i ^ mask) for i in range(size)])  4 us
  transfers between devices with their start and end apart: 20, of which 10 were waited for; matrix products, arithmetic and copies ran while one was open for 0% of the time, Pallas kernels for 17%

profile of v13, /device:TPU:0, one launch (start us, length us, event | category | flops | bytes accessed | tf_op | source)
XLA Modules:
  0.0 87.8 jit_solution(5277405191944637219)
XLA Ops:
  0.7 3.6 %shard_map.94 = (f32[8,16,128]{2,1,0:T(8,128)}, f32[512,256]{1,0:T(8,128)}, f32[512,128]{1,0:T(8,128)}, f32[512,128]{1,0:T(8,128)}, f32[512,128]{1,0:T(8,128)}, /*index=5*/f32[512,128]{1,0:T(8,128)}) custom-call(f32[512,1024]{1,0:T(8,128)} %design_ref.9, f32[4,128]{1,0:T(4,128)} %bitcast.6, s32[4,128]{1,0:T(4,128)} %bitcast.9, s32[8,16]{1,0:T(8,128)} %bitcast.8, ...), custom_call_target="tpu_custom_call" | custom-call | tf_op jit(solution)/shard_map/pallas_call | solution.py:423
  4.3 14.3 %all_to_all.15.parts_ref = f32[8,16,128]{2,1,0:T(8,128)S(1)} all-to-all(f32[8,16,128]{2,1,0:T(8,128)} %get-tuple-element.45), channel_id=1, replica_groups=mesh['row'=8,'col'=4] {'row'}, dimensions={0} | all-to-all | bytes 131072 | tf_op jit(solution)/shard_map/all_to_all | solution.py:23
  19.0 0.8 collective-permute-start.3
  19.8 2.3 %collective-permute-start.4 = (f32[512,128]{1,0:T(8,128)}, f32[512,128]{1,0:T(8,128)S(1)}, u32[]{:S(2)}, u32[]{:S(2)}) collective-permute-start(f32[512,128]{1,0:T(8,128)} %get-tuple-element.54), channel_id=1, source_target_pairs={{0,12},{4,8},{8,4},{12,0},{16,28},{20,24},{24,20},{28,16},{1,13},{... | collective-permute-start | bytes 786440 | tf_op jit(solution)/shard_map/ppermute | solution.py:441
  22.1 6.2 %shard_map.95 = (f32[32,128]{1,0:T(8,128)S(1)}, f32[1,128]{1,0:T(1,128)S(1)}, f32[1024,4096]{1,0:T(8,128)S(1)}) custom-call(f32[1024,4096]{1,0:T(8,128)} %rinv_ref.1, f32[8,16,128]{2,1,0:T(8,128)S(1)} %all_to_all.15.parts_ref), custom_call_target="tpu_custom_call" | custom-call | tf_op jit(solution)/shard_map/pallas_call | solution.py:481
  28.4 1.2 %collective-permute-done = f32[32,128]{1,0:T(8,128)S(1)} collective-permute-done((f32[32,128]{1,0:T(8,128)S(1)}, f32[32,128]{1,0:T(8,128)S(1)}, u32[]{:S(2)}, u32[]{:S(2)}) %collective-permute-start) | collective-permute-done | bytes 16416 | tf_op jit(solution)/shard_map/ppermute | solution.py:30
  29.6 1.5 %collective-permute-start.1 = (f32[32,128]{1,0:T(8,128)S(1)}, f32[32,128]{1,0:T(8,128)S(1)}, u32[]{:S(2)}, u32[]{:S(2)}) collective-permute-start(f32[32,128]{1,0:T(8,128)S(1)} %add.6.refs_0_), channel_id=1, source_target_pairs={{0,2},{1,3},{2,0},{3,1},{4,6},{5,7},{6,4},{7,5},{8,10},{9,11},{10,... | collective-permute-start | bytes 49160 | tf_op jit(solution)/shard_map/ppermute | solution.py:30
  31.8 1.5 %collective-permute-done.1.order_ref.refs_1_ = f32[32,128]{1,0:T(8,128)S(1)} collective-permute-done((f32[32,128]{1,0:T(8,128)S(1)}, f32[32,128]{1,0:T(8,128)S(1)}, u32[]{:S(2)}, u32[]{:S(2)}) %collective-permute-start.1) | collective-permute-done | bytes 16416 | tf_op jit(solution)/shard_map/ppermute | solution.py:30
  33.3 3.4 %collective-permute-done.2.refs_0_ = f32[512,256]{1,0:T(8,128)S(1)} collective-permute-done((f32[512,256]{1,0:T(8,128)}, f32[512,256]{1,0:T(8,128)S(1)}, u32[]{:S(2)}, u32[]{:S(2)}) %collective-permute-start.2) | collective-permute-done | bytes 524320 | tf_op jit(solution)/shard_map/ppermute | solution.py:441
  36.7 1.1 %shard_map.97 = (f32[1,4,128,128]{3,2,1,0:T(8,128)S(1)}, f32[1,4,128,128]{3,2,1,0:T(8,128)S(1)}, f32[1,128]{1,0:T(1,128)S(1)}) custom-call(f32[512,1024]{1,0:T(8,128)S(1)} %copy-done, f32[8,16,128]{2,1,0:T(8,128)S(1)} %all_to_all.15.parts_ref, bf16[8,128,512]{2,1,0:T(8,128)(2,1)S(1)} %shard_map.96.mix_ref, ...), custom_call_target="tpu_custom_call" | custom-call | tf_op jit(solution)/shard_map/pallas_call | solution.py:60
  37.8 0.8 collective-permute-start.5
  38.6 0.9 %collective-permute-start.9 = (f32[512,128]{1,0:T(8,128)S(1)}, f32[512,128]{1,0:T(8,128)S(1)}, u32[]{:S(2)}, u32[]{:S(2)}) collective-permute-start(f32[512,128]{1,0:T(8,128)S(1)} %copy-done.3), channel_id=1, source_target_pairs={{0,12},{4,8},{8,4},{12,0},{16,28},{20,24},{24,20},{28,16},{1,13},{... | collective-permute-start | bytes 786440 | tf_op jit(solution)/shard_map/ppermute | solution.py:441
  39.5 2.5 %shard_map.98 = (f32[4,128]{1,0:T(4,128)S(1)}, f32[8,128]{1,0:T(8,128)S(1)}, f32[1,128]{1,0:T(1,128)S(1)}, f32[32,128]{1,0:T(8,128)S(1)}) custom-call(f32[1024,4096]{1,0:T(8,128)S(1)} %get-tuple-element.46.rinv_ref, f32[512,1024]{1,0:T(8,128)S(1)} %copy-done, f32[1,128]{1,0:T(1,128)S(1)} %get-tuple-element.57.token_ref, f32[32,128]{1,0:T(8,128)S(1)} %add.6.refs_0_, ...), custom_call_target="tpu_custom_call" | custom-call | tf_op jit(solution)/shard_map/pallas_call | solution.py:60
  42.1 1.1 %collective-permute-done.6 = f32[4,128]{1,0:T(4,128)S(1)} collective-permute-done((f32[4,128]{1,0:T(4,128)S(1)}, f32[4,128]{1,0:T(4,128)S(1)}, u32[]{:S(2)}, u32[]{:S(2)}) %collective-permute-start.6) | collective-permute-done | bytes 2080 | tf_op jit(solution)/shard_map/ppermute | solution.py:30
  43.2 1.5 %collective-permute-start.7 = (f32[4,128]{1,0:T(4,128)S(1)}, f32[4,128]{1,0:T(4,128)S(1)}, u32[]{:S(2)}, u32[]{:S(2)}) collective-permute-start(f32[4,128]{1,0:T(4,128)S(1)} %add.7.refs_0_), channel_id=1, source_target_pairs={{0,2},{1,3},{2,0},{3,1},{4,6},{5,7},{6,4},{7,5},{8,10},{9,11},{10,... | collective-permute-start | bytes 6152 | tf_op jit(solution)/shard_map/ppermute | solution.py:30
  44.7 2.1 %collective-permute-done.7.refs_1_ = f32[4,128]{1,0:T(4,128)S(1)} collective-permute-done((f32[4,128]{1,0:T(4,128)S(1)}, f32[4,128]{1,0:T(4,128)S(1)}, u32[]{:S(2)}, u32[]{:S(2)}) %collective-permute-start.7) | collective-permute-done | bytes 2080 | tf_op jit(solution)/shard_map/ppermute | solution.py:30
  47.0 11.6 %all_to_all.16.parts_ref = f32[8,16,128]{2,1,0:T(8,128)S(1)} all-to-all(f32[8,16,128]{2,1,0:T(8,128)S(1)} %get-tuple-element.61), channel_id=1, replica_groups=mesh['row'=8,'col'=4] {'row'}, dimensions={0} | all-to-all | bytes 131072 | tf_op jit(solution)/shard_map/all_to_all | solution.py:23
  58.6 2.0 %shard_map.100 = (f32[32,128]{1,0:T(8,128)S(1)}, f32[1,128]{1,0:T(1,128)S(1)}) custom-call(f32[1024,4096]{1,0:T(8,128)S(1)} %get-tuple-element.46.rinv_ref, f32[8,16,128]{2,1,0:T(8,128)S(1)} %all_to_all.16.parts_ref), custom_call_target="tpu_custom_call" | custom-call | tf_op jit(solution)/shard_map/pallas_call | solution.py:481
  60.7 1.1 %shard_map.102 = (f32[1,4,128,128]{3,2,1,0:T(8,128)S(1)}, f32[1,4,128,128]{3,2,1,0:T(8,128)S(1)}, f32[1,128]{1,0:T(1,128)S(1)}) custom-call(f32[512,1024]{1,0:T(8,128)S(1)} %copy-done, f32[8,16,128]{2,1,0:T(8,128)S(1)} %all_to_all.15.parts_ref, bf16[8,128,512]{2,1,0:T(8,128)(2,1)S(1)} %shard_map.96.mix_ref, f32[1,128]{1,0:T(1,128)S(1)} %get-tuple-element.63.order_ref, ...), custom_call_target="tpu_custom_call" | custom-call | tf_op jit(solution)/shard_map/pallas_call | solution.py:60
  61.8 0.5 collective-permute-start.16
  62.3 1.5 %collective-permute-start.11 = (f32[32,128]{1,0:T(8,128)S(1)}, f32[32,128]{1,0:T(8,128)S(1)}, u32[]{:S(2)}, u32[]{:S(2)}) collective-permute-start(f32[32,128]{1,0:T(8,128)S(1)} %get-tuple-element.68.refs_0_), channel_id=1, source_target_pairs={{0,2},{1,3},{2,0},{3,1},{4,6},{5,7},{6,4},{7,5},{8,10},{9,11},{10,... | collective-permute-start | bytes 49160 | tf_op jit(solution)/shard_map/ppermute | solution.py:40
  64.2 1.4 %collective-permute-done.12.refs_3_ = f32[32,128]{1,0:T(8,128)S(1)} collective-permute-done((f32[32,128]{1,0:T(8,128)S(1)}, f32[32,128]{1,0:T(8,128)S(1)}, u32[]{:S(2)}, u32[]{:S(2)}) %collective-permute-start.12) | collective-permute-done | bytes 16416 | tf_op jit(solution)/shard_map/ppermute | solution.py:40
  66.1 2.5 %shard_map.103 = (f32[4,128]{1,0:T(4,128)S(1)}, f32[8,128]{1,0:T(8,128)S(1)}, f32[1,128]{1,0:T(1,128)S(1)}) custom-call(f32[1024,4096]{1,0:T(8,128)S(1)} %get-tuple-element.46.rinv_ref, f32[512,1024]{1,0:T(8,128)S(1)} %copy-done, f32[1,128]{1,0:T(1,128)S(1)} %get-tuple-element.67.token_ref, f32[32,128]{1,0:T(8,128)S(1)} %get-tuple-element.68.refs_0_, ...), custom_call_target="tpu_custom_call" | custom-call | tf_op jit(solution)/shard_map/pallas_call | solution.py:60
  68.6 0.7 collective-permute-start.15
  69.2 1.5 %collective-permute-start.14 = (f32[4,128]{1,0:T(4,128)S(1)}, f32[4,128]{1,0:T(4,128)S(1)}, u32[]{:S(2)}, u32[]{:S(2)}) collective-permute-start(f32[4,128]{1,0:T(4,128)S(1)} %get-tuple-element.70.refs_0_), channel_id=1, source_target_pairs={{0,2},{1,3},{2,0},{3,1},{4,6},{5,7},{6,4},{7,5},{8,10},{9,11},{10,... | collective-permute-start | bytes 6152 | tf_op jit(solution)/shard_map/ppermute | solution.py:40
  70.7 0.9 %collective-permute-done.15.refs_3_ = f32[4,128]{1,0:T(4,128)S(1)} collective-permute-done((f32[4,128]{1,0:T(4,128)S(1)}, f32[4,128]{1,0:T(4,128)S(1)}, u32[]{:S(2)}, u32[]{:S(2)}) %collective-permute-start.15) | collective-permute-done | bytes 2080 | tf_op jit(solution)/shard_map/ppermute | solution.py:40
  71.6 1.2 %collective-permute-done.14.refs_2_ = f32[4,128]{1,0:T(4,128)S(1)} collective-permute-done((f32[4,128]{1,0:T(4,128)S(1)}, f32[4,128]{1,0:T(4,128)S(1)}, u32[]{:S(2)}, u32[]{:S(2)}) %collective-permute-start.14) | collective-permute-done | bytes 2080 | tf_op jit(solution)/shard_map/ppermute | solution.py:40
  72.8 1.3 %collective-permute-done.16.refs_9_ = f32[1,4,128,128]{3,2,1,0:T(8,128)S(1)} collective-permute-done((f32[1,4,128,128]{3,2,1,0:T(8,128)S(1)}, f32[1,4,128,128]{3,2,1,0:T(8,128)S(1)}, u32[]{:S(2)}, u32[]{:S(2)}) %collective-permute-start.16) | collective-permute-done | bytes 262176 | tf_op jit(solution)/shard_map/ppermute | solution.py:441
  74.2 0.9 collective-permute-start.17
  75.1 2.6 %collective-permute-start.19 = (f32[128,256]{1,0:T(8,128)S(1)}, f32[128,256]{1,0:T(8,128)S(1)}, u32[]{:S(2)}, u32[]{:S(2)}) collective-permute-start(f32[128,256]{1,0:T(8,128)S(1)} %get-tuple-element.83), channel_id=1, source_target_pairs={{0,12},{4,8},{8,4},{12,0},{16,28},{20,24},{24,20},{28,16},{1,13},{... | collective-permute-start | bytes 393224 | tf_op jit(solution)/shard_map/ppermute | solution.py:441
  77.7 9.2 %all_to_all.17.parts_ref = f32[8,8,128]{2,1,0:T(8,128)S(1)} all-to-all(f32[8,8,128]{2,1,0:T(8,128)S(1)} %get-tuple-element.76), channel_id=1, replica_groups=mesh['row'=8,'col'=4] {'row'}, dimensions={0} | all-to-all | bytes 65536 | tf_op jit(solution)/shard_map/all_to_all | solution.py:23
  86.9 0.9 %shard_map.105 = (f32[4,128]{1,0:T(4,128)}, f32[8,128]{1,0:T(8,128)}, f32[128,1024]{1,0:T(8,128)}) custom-call(f32[8,8,128]{2,1,0:T(8,128)S(1)} %all_to_all.17.parts_ref, f32[4,128]{1,0:T(4,128)S(1)} %get-tuple-element.77.left_ref, f32[1,128]{1,0:T(1,128)S(1)} %get-tuple-element.59.refs_3_.refs_0_, f32[1,128]{1,0:T(1,128)S(1)} %get-tuple-element.62.order_ref.refs_5_.refs_1_, ...), custom_call_target="tpu_custom_call" | custom-call | tf_op jit(solution)/shard_map/pallas_call | solution.py:60
  (35 shorter events, 2.5 us)
Async XLA Ops:
  0.6 30.6 %copy-start.1 = (bf16[256,256]{1,0:T(8,128)(2,1)S(1)}, bf16[256,256]{1,0:T(8,128)(2,1)}, u32[]{:S(2)}) copy-start(bf16[256,256]{1,0:T(8,128)(2,1)} %constant.2.clone.walsh_ref) | copy-start | bytes 393220
  0.6 36.0 %copy-start = (f32[512,1024]{1,0:T(8,128)S(1)}, f32[512,1024]{1,0:T(8,128)}, u32[]{:S(2)}) copy-start(f32[512,1024]{1,0:T(8,128)} %design_ref.9) | copy-start | bytes 6291460
  4.3 26.8 %copy-start.4 = (f32[512,128]{1,0:T(8,128)S(1)}, f32[512,128]{1,0:T(8,128)}, u32[]{:S(2)}) copy-start(f32[512,128]{1,0:T(8,128)} %get-tuple-element.64) | copy-start | bytes 786436
  4.3 34.3 %copy-start.3 = (f32[512,128]{1,0:T(8,128)S(1)}, f32[512,128]{1,0:T(8,128)}, u32[]{:S(2)}) copy-start(f32[512,128]{1,0:T(8,128)} %get-tuple-element.66) | copy-start | bytes 786436
  18.6 28.2 %copy-start.2 = (f32[512]{0:T(512)S(1)}, f32[512]{0:T(512)}, u32[]{:S(2)}) copy-start(f32[512]{0:T(512)} %param.11) | copy-start | bytes 6148
  18.6 18.1 %collective-permute-start.2 = (f32[512,256]{1,0:T(8,128)}, f32[512,256]{1,0:T(8,128)S(1)}, u32[]{:S(2)}, u32[]{:S(2)}) collective-permute-start(f32[512,256]{1,0:T(8,128)} %get-tuple-element.52), channel_id=1, source_target_pairs={{0,4},{4,0},{8,12},{12,8},{16,20},{20,16},{24,28},{28,24},{1,5},{5... | collective-permute-start | bytes 1572872 | tf_op jit(solution)/shard_map/ppermute | solution.py:441
  19.0 14.3 %collective-permute-start.3 = (f32[512,128]{1,0:T(8,128)}, f32[512,128]{1,0:T(8,128)S(1)}, u32[]{:S(2)}, u32[]{:S(2)}) collective-permute-start(f32[512,128]{1,0:T(8,128)} %get-tuple-element.53), channel_id=1, source_target_pairs={{0,8},{4,12},{8,0},{12,4},{16,24},{20,28},{24,16},{28,20},{1,9},{5... | collective-permute-start | bytes 786440 | tf_op jit(solution)/shard_map/ppermute | solution.py:441
  19.8 13.5 %collective-permute-start.4 = (f32[512,128]{1,0:T(8,128)}, f32[512,128]{1,0:T(8,128)S(1)}, u32[]{:S(2)}, u32[]{:S(2)}) collective-permute-start(f32[512,128]{1,0:T(8,128)} %get-tuple-element.54), channel_id=1, source_target_pairs={{0,12},{4,8},{8,4},{12,0},{16,28},{20,24},{24,20},{28,16},{1,13},{... | collective-permute-start | bytes 786440 | tf_op jit(solution)/shard_map/ppermute | solution.py:441
  28.3 1.2 %collective-permute-start = (f32[32,128]{1,0:T(8,128)S(1)}, f32[32,128]{1,0:T(8,128)S(1)}, u32[]{:S(2)}, u32[]{:S(2)}) collective-permute-start(f32[32,128]{1,0:T(8,128)S(1)} %get-tuple-element.47), channel_id=1, source_target_pairs={{0,1},{1,0},{2,3},{3,2},{4,5},{5,4},{6,7},{7,6},{8,9},{9,8},{10,11... | collective-permute-start | bytes 49160 | tf_op jit(solution)/shard_map/ppermute | solution.py:30
  29.6 3.7 %collective-permute-start.1 = (f32[32,128]{1,0:T(8,128)S(1)}, f32[32,128]{1,0:T(8,128)S(1)}, u32[]{:S(2)}, u32[]{:S(2)}) collective-permute-start(f32[32,128]{1,0:T(8,128)S(1)} %add.6.refs_0_), channel_id=1, source_target_pairs={{0,2},{1,3},{2,0},{3,1},{4,6},{5,7},{6,4},{7,5},{8,10},{9,11},{10,... | collective-permute-start | bytes 49160 | tf_op jit(solution)/shard_map/ppermute | solution.py:30
  31.1 29.6 %collective-permute-start.8 = (f32[512,128]{1,0:T(8,128)S(1)}, f32[512,128]{1,0:T(8,128)S(1)}, u32[]{:S(2)}, u32[]{:S(2)}) collective-permute-start(f32[512,128]{1,0:T(8,128)S(1)} %copy-done.4), channel_id=1, source_target_pairs={{0,8},{4,12},{8,0},{12,4},{16,24},{20,28},{24,16},{28,20},{1,9},{5... | collective-permute-start | bytes 786440 | tf_op jit(solution)/shard_map/ppermute | solution.py:441
  37.8 22.8 %collective-permute-start.5 = (f32[1,4,128,128]{3,2,1,0:T(8,128)S(1)}, f32[1,4,128,128]{3,2,1,0:T(8,128)S(1)}, u32[]{:S(2)}, u32[]{:S(2)}) collective-permute-start(f32[1,4,128,128]{3,2,1,0:T(8,128)S(1)} %get-tuple-element.56), channel_id=1, source_target_pairs={{0,16},{4,20},{8,24},{12,28},{16,0},{20,4},{24,8},{28,12},{1,17},{... | collective-permute-start | bytes 786440 | tf_op jit(solution)/shard_map/ppermute | solution.py:441
  38.6 22.1 %collective-permute-start.9 = (f32[512,128]{1,0:T(8,128)S(1)}, f32[512,128]{1,0:T(8,128)S(1)}, u32[]{:S(2)}, u32[]{:S(2)}) collective-permute-start(f32[512,128]{1,0:T(8,128)S(1)} %copy-done.3), channel_id=1, source_target_pairs={{0,12},{4,8},{8,4},{12,0},{16,28},{20,24},{24,20},{28,16},{1,13},{... | collective-permute-start | bytes 786440 | tf_op jit(solution)/shard_map/ppermute | solution.py:441
  42.0 1.2 %collective-permute-start.6 = (f32[4,128]{1,0:T(4,128)S(1)}, f32[4,128]{1,0:T(4,128)S(1)}, u32[]{:S(2)}, u32[]{:S(2)}) collective-permute-start(f32[4,128]{1,0:T(4,128)S(1)} %get-tuple-element.58), channel_id=1, source_target_pairs={{0,1},{1,0},{2,3},{3,2},{4,5},{5,4},{6,7},{7,6},{8,9},{9,8},{10,11... | collective-permute-start | bytes 6152 | tf_op jit(solution)/shard_map/ppermute | solution.py:30
  43.2 3.6 %collective-permute-start.7 = (f32[4,128]{1,0:T(4,128)S(1)}, f32[4,128]{1,0:T(4,128)S(1)}, u32[]{:S(2)}, u32[]{:S(2)}) collective-permute-start(f32[4,128]{1,0:T(4,128)S(1)} %add.7.refs_0_), channel_id=1, source_target_pairs={{0,2},{1,3},{2,0},{3,1},{4,6},{5,7},{6,4},{7,5},{8,10},{9,11},{10,... | collective-permute-start | bytes 6152 | tf_op jit(solution)/shard_map/ppermute | solution.py:30
  61.8 12.3 %collective-permute-start.16 = (f32[1,4,128,128]{3,2,1,0:T(8,128)S(1)}, f32[1,4,128,128]{3,2,1,0:T(8,128)S(1)}, u32[]{:S(2)}, u32[]{:S(2)}) collective-permute-start(f32[1,4,128,128]{3,2,1,0:T(8,128)S(1)} %get-tuple-element.75), channel_id=1, source_target_pairs={{0,16},{4,20},{8,24},{12,28},{16,0},{20,4},{24,8},{28,12},{1,17},{... | collective-permute-start | bytes 786440 | tf_op jit(solution)/shard_map/ppermute | solution.py:441
  62.3 3.3 %collective-permute-start.12 = (f32[32,128]{1,0:T(8,128)S(1)}, f32[32,128]{1,0:T(8,128)S(1)}, u32[]{:S(2)}, u32[]{:S(2)}) collective-permute-start(f32[32,128]{1,0:T(8,128)S(1)} %get-tuple-element.68.refs_0_), channel_id=1, source_target_pairs={{0,3},{1,2},{2,1},{3,0},{4,7},{5,6},{6,5},{7,4},{8,11},{9,10},{10,... | collective-permute-start | bytes 49160 | tf_op jit(solution)/shard_map/ppermute | solution.py:40
  62.3 3.8 %collective-permute-start.11 = (f32[32,128]{1,0:T(8,128)S(1)}, f32[32,128]{1,0:T(8,128)S(1)}, u32[]{:S(2)}, u32[]{:S(2)}) collective-permute-start(f32[32,128]{1,0:T(8,128)S(1)} %get-tuple-element.68.refs_0_), channel_id=1, source_target_pairs={{0,2},{1,3},{2,0},{3,1},{4,6},{5,7},{6,4},{7,5},{8,10},{9,11},{10,... | collective-permute-start | bytes 49160 | tf_op jit(solution)/shard_map/ppermute | solution.py:40
  63.8 2.2 %collective-permute-start.10 = (f32[32,128]{1,0:T(8,128)S(1)}, f32[32,128]{1,0:T(8,128)S(1)}, u32[]{:S(2)}, u32[]{:S(2)}) collective-permute-start(f32[32,128]{1,0:T(8,128)S(1)} %get-tuple-element.68.refs_0_), channel_id=1, source_target_pairs={{0,1},{1,0},{2,3},{3,2},{4,5},{5,4},{6,7},{7,6},{8,9},{9,8},{10,11... | collective-permute-start | bytes 49160 | tf_op jit(solution)/shard_map/ppermute | solution.py:40
  68.6 3.1 %collective-permute-start.15 = (f32[4,128]{1,0:T(4,128)S(1)}, f32[4,128]{1,0:T(4,128)S(1)}, u32[]{:S(2)}, u32[]{:S(2)}) collective-permute-start(f32[4,128]{1,0:T(4,128)S(1)} %get-tuple-element.70.refs_0_), channel_id=1, source_target_pairs={{0,3},{1,2},{2,1},{3,0},{4,7},{5,6},{6,5},{7,4},{8,11},{9,10},{10,... | collective-permute-start | bytes 6152 | tf_op jit(solution)/shard_map/ppermute | solution.py:40
  69.2 3.6 %collective-permute-start.14 = (f32[4,128]{1,0:T(4,128)S(1)}, f32[4,128]{1,0:T(4,128)S(1)}, u32[]{:S(2)}, u32[]{:S(2)}) collective-permute-start(f32[4,128]{1,0:T(4,128)S(1)} %get-tuple-element.70.refs_0_), channel_id=1, source_target_pairs={{0,2},{1,3},{2,0},{3,1},{4,6},{5,7},{6,4},{7,5},{8,10},{9,11},{10,... | collective-permute-start | bytes 6152 | tf_op jit(solution)/shard_map/ppermute | solution.py:40
  70.7 2.1 %collective-permute-start.13 = (f32[4,128]{1,0:T(4,128)S(1)}, f32[4,128]{1,0:T(4,128)S(1)}, u32[]{:S(2)}, u32[]{:S(2)}) collective-permute-start(f32[4,128]{1,0:T(4,128)S(1)} %get-tuple-element.70.refs_0_), channel_id=1, source_target_pairs={{0,1},{1,0},{2,3},{3,2},{4,5},{5,4},{6,7},{7,6},{8,9},{9,8},{10,11... | collective-permute-start | bytes 6152 | tf_op jit(solution)/shard_map/ppermute | solution.py:40
  74.2 12.7 %collective-permute-start.17 = (f32[128,256]{1,0:T(8,128)S(1)}, f32[128,256]{1,0:T(8,128)S(1)}, u32[]{:S(2)}, u32[]{:S(2)}) collective-permute-start(f32[128,256]{1,0:T(8,128)S(1)} %get-tuple-element.81), channel_id=1, source_target_pairs={{0,4},{4,0},{8,12},{12,8},{16,20},{20,16},{24,28},{28,24},{1,5},{5... | collective-permute-start | bytes 393224 | tf_op jit(solution)/shard_map/ppermute | solution.py:441
  75.1 11.9 %collective-permute-start.18 = (f32[128,256]{1,0:T(8,128)S(1)}, f32[128,256]{1,0:T(8,128)S(1)}, u32[]{:S(2)}, u32[]{:S(2)}) collective-permute-start(f32[128,256]{1,0:T(8,128)S(1)} %get-tuple-element.82), channel_id=1, source_target_pairs={{0,8},{4,12},{8,0},{12,4},{16,24},{20,28},{24,16},{28,20},{1,9},{5... | collective-permute-start | bytes 393224 | tf_op jit(solution)/shard_map/ppermute | solution.py:441
  75.1 11.9 %collective-permute-start.19 = (f32[128,256]{1,0:T(8,128)S(1)}, f32[128,256]{1,0:T(8,128)S(1)}, u32[]{:S(2)}, u32[]{:S(2)}) collective-permute-start(f32[128,256]{1,0:T(8,128)S(1)} %get-tuple-element.83), channel_id=1, source_target_pairs={{0,12},{4,8},{8,4},{12,0},{16,28},{20,24},{24,20},{28,16},{1,13},{... | collective-permute-start | bytes 393224 | tf_op jit(solution)/shard_map/ppermute | solution.py:441

commit v14 on v13

--- a/solution.py
+++ b/solution.py
@@ -17,6 +17,7 @@
 F32 = jnp.float32
 VMEM = pl.BlockSpec(memory_space=pltpu.VMEM)
 HBM = pl.BlockSpec(memory_space=pltpu.HBM)
+ANY = pl.BlockSpec(memory_space=pl.ANY)
 
 
 def exchange(copies, axis):
@@ -212,7 +213,7 @@
         copy.wait()
 
 
-def back_body(first, rinv_ref, parts_ref, term_ref, beta_ref, *refs):
+def back_body(first, rinv_ref, parts_ref, order_ref, term_ref, beta_ref, *refs):
     tiles = rinv_ref.shape[0] // LANE
     copies = []
     if first:
@@ -329,9 +330,7 @@
         for tile in range(0, piece, LANE):
             column = pl.multiple_of(me % NEAR * (width // NEAR) + start + tile, LANE)
             here = slice(tile, tile + LANE)
-            there = slice(start + tile, start + tile + LANE)
-            values = [design_ref[part, pl.ds(column, LANE)], near[0][part, there]]
-            values += [ref[part, here] for ref in near[1:]]
+            values = [design_ref[part, pl.ds(column, LANE)]] + [ref[part, here] for ref in near]
             values = [value * sign for value, sign in zip(values, signs)]
             apart = 1
             while apart < NEAR:
@@ -364,6 +363,11 @@
 def join_body(kept_ref, arrived_ref, order_ref, out_ref, token_ref):
     token_ref[...] = order_ref[:1, :]
     out_ref[...] = kept_ref[0] + arrived_ref[0]
+
+
+def touch_body(*refs):
+    order_ref, token_ref = refs[-2:]
+    token_ref[...] = order_ref[0, :1, :]
 
 
 def last_body(parts_ref, left_ref, *refs):
@@ -417,13 +421,12 @@
     slots = row_groups * PAIR
     far = row_groups // NEAR
 
-    sent = [(1, 0)] + [(mask, chunk * piece) for mask in range(2, NEAR) for chunk in range(chunks)]
-    sizes = [piece * chunks] + [piece] * (chunks * (NEAR - 2))
+    sent = [(mask, chunk * piece) for chunk in range(chunks) for mask in range(1, NEAR)]
 
     message, *away = pl.pallas_call(
         functools.partial(first_body, sent),
         out_shape=(shape(row_groups, rounded(signs_at(width, row_groups) + lines, 8), LANE),)
-        + tuple(shape(rows, size) for size in sizes),
+        + (shape(rows, piece),) * len(sent),
         in_specs=[HBM] * 5,
         out_specs=(VMEM,) + (HBM,) * len(sent),
         scratch_shapes=[
@@ -452,12 +455,14 @@
             picked,
             mixed,
             order,
-            *(near[index] for index, (mask, start) in enumerate(sent) if mask == 1 or start == chunk * piece),
+            *near[chunk * (NEAR - 1) : (chunk + 1) * (NEAR - 1)],
             scratch=[pltpu.VMEM((NEAR, 2, rows, piece), jnp.bfloat16)],
         )
 
     def spread(indices, order):
-        parts, _ = lax.optimization_barrier(([away[index] for index in indices], order))
+        parts = [away[index] for index in indices]
+        if order is not None:
+            parts, _ = lax.optimization_barrier((parts, order))
         return [swap(part, sent[index][0]) for index, part in zip(indices, parts)]
 
     def halve(keep, come, order):
@@ -473,7 +478,7 @@
         keep, come = halve(keep, come, order)
         return call(join_body, (shape(*keep.shape[1:]), scalar), keep, come, order)
 
-    def back(rinv, message, first):
+    def back(rinv, message, order, first):
         outs, scratch = (shape(whole // LANE, LANE), scalar), [pltpu.VMEM((width // LANE, LANE), F32)]
         if first:
             outs += (shape(*rinv.shape),)
@@ -481,11 +486,11 @@
         return pl.pallas_call(
             functools.partial(back_body, first),
             out_shape=outs,
-            in_specs=[HBM if first else VMEM, VMEM],
+            in_specs=[HBM if first else VMEM, VMEM, VMEM],
             out_specs=(VMEM,) * len(outs),
             scratch_shapes=scratch,
             compiler_params=pltpu.CompilerParams(vmem_limit_bytes=(34 if first else 24) << 20),
-            )(rinv, message)
+            )(rinv, message, order)
 
     def forward(terms, token, last, *before):
         return call(
@@ -512,16 +517,24 @@
         )
 
     betas, alphas, held, joined, right = [], [], [], [], []
+    near = spread(range(NEAR - 2), None)
     message = picked = exchange(message, "row")
-    late = len(sent) - 1 if chunks > 1 else len(sent)
-    near = spread(range(late), message)
+    token = pl.pallas_call(
+        touch_body,
+        out_shape=scalar,
+        in_specs=[ANY] * len(near) + [VMEM],
+        out_specs=VMEM,
+        compiler_params=pltpu.CompilerParams(vmem_limit_bytes=2 << 20),
+    )(*near, message)
+    late = len(sent) - (chunks > 1)
+    near += spread(range(NEAR - 2, late), message)
     for step in range(ITERS):
         last = step + 1 == ITERS
         if step == 0:
-            term, beta, here = back(rinv, message, True)
+            term, beta, here = back(rinv, message, token, True)
             mixed = mix(message)
         else:
-            term, beta = back(here, message, False)
+            term, beta = back(here, message, alpha, False)
             token = beta
             if chunks > 1:
                 part, token = join(keep, come, beta)
@@ -533,7 +546,7 @@
         terms = direct(term, "col") if spare else paired(term, "col")
         if step == 0:
             near += spread(range(late, len(sent)), terms[1])
-            keep, send, token = sample(0, mixed, terms[1])
+            keep, send, token = sample(0, mixed, beta)
             come = swap(send, row_groups // 2)
         image, kept, alpha, *right = forward(terms, token, last, *right, *betas[1:])
         alphas.append(alpha)

time: 88.2 us -> 86.4 us (0.980)
  blocking collectives: 35.1 us -> 18.6 us
  starting transfers between devices: 16.6 us -> 27.4 us
  waiting for transfers between devices: 14.7 us -> 18.5 us
    all_to_all x3 -> x2, blocking collectives: 35.1 us -> 18.6 us  [exchange(): return lax.all_to_all(copies, axis, split_axis=0, concat_axis=0, tiled=True)]
    all_to_all x0 -> x1, starting transfers between devices: none -> 7.42 us  [exchange(): return lax.all_to_all(copies, axis, split_axis=0, concat_axis=0, tiled=True)]
    ppermute x10 -> x11, starting transfers between devices: 9.51 us -> 14.1 us  [swap(): lax.ppermute(array, 'row', [(i, i ^ mask) for i in range(row_groups)])]
    all_to_all x0 -> x1, waiting for transfers between devices: none -> 3.84 us  [exchange(): return lax.all_to_all(copies, axis, split_axis=0, concat_axis=0, tiled=True)]
    ppermute x4, starting transfers between devices: 3.12 us -> 2.17 us  [paired(): come = lax.ppermute(array, axis, [(i, i ^ mask) for i in range(size)])]
    ppermute x10 -> x11, waiting for transfers between devices: 4.68 us -> 5.09 us  [swap(): lax.ppermute(array, 'row', [(i, i ^ mask) for i in range(row_groups)])]
  transfers between devices with their start and end apart: 20 -> 22, of which waited for: 10 -> 11; matrix products, arithmetic and copies ran while one was open for 0% -> 0% of each run, Pallas kernels for 17% -> 17%
where the time goes in v14:
time: 86.4 us; the launch traced here: 86 us
  starting transfers between devices  27.4 us (32%)
  Pallas kernels  20.6 us (24%)
  blocking collectives  18.6 us (22%)
  waiting for transfers between devices  18.5 us (21%)
    all_to_all x2, blocking collectives, exchange(): return lax.all_to_all(copies, axis, split_axis=0, concat_axis=0, tiled=True)  18.6 us
    ppermute x11, starting transfers between devices, swap(): lax.ppermute(array, 'row', [(i, i ^ mask) for i in range(row_groups)])  14.1 us
    pallas_call x9, Pallas kernels, call(): pl.pallas_call(body, out_shape=out_shape, in_specs=[VMEM] * len(operands)...  8.87 us
    pallas_call x2, Pallas kernels, back(): pl.pallas_call(functools.partial(back_body, first), out_shape=outs, in_sp...  8.16 us
    all_to_all x1, starting transfers between devices, exchange(): return lax.all_to_all(copies, axis, split_axis=0, concat_axis=0, tiled=True)  7.42 us
    ppermute x4, waiting for transfers between devices, paired(): come = lax.ppermute(array, axis, [(i, i ^ mask) for i in range(size)])  5.36 us
    ppermute x11, waiting for transfers between devices, swap(): lax.ppermute(array, 'row', [(i, i ^ mask) for i in range(row_groups)])  5.09 us
    ppermute x6, waiting for transfers between devices, direct(): lax.ppermute(array, axis, [(i, i ^ mask) for i in range(size)])  4.21 us
  transfers between devices with their start and end apart: 22, of which 11 were waited for; matrix products, arithmetic and copies ran while one was open for 0% of the time, Pallas kernels for 17%

profile of v14, /device:TPU:0, one launch (start us, length us, event | category | flops | bytes accessed | tf_op | source)
XLA Modules:
  0.0 86.0 jit_solution(3173617577936834650)
XLA Ops:
  0.7 3.6 %shard_map.94 = (f32[8,16,128]{2,1,0:T(8,128)}, f32[512,128]{1,0:T(8,128)}, f32[512,128]{1,0:T(8,128)}, f32[512,128]{1,0:T(8,128)}, f32[512,128]{1,0:T(8,128)}, /*index=5*/f32[512,128]{1,0:T(8,128)}, f32[512,128]{1,0:T(8,128)}) custom-call(f32[512,1024]{1,0:T(8,128)} %design_ref.9, f32[4,128]{1,0:T(4,128)} %bitcast.6, s32[4,128]{1,0:T(4,128)} %bitcast.9, ...), custom_call_target="tpu_custom_call" | custom-call | tf_op jit(solution)/shard_map/pallas_call | solution.py:426
  4.3 7.4 %all-to-all-start = ((f32[8,16,128]{2,1,0:T(8,128)}), f32[8,16,128]{2,1,0:T(8,128)S(1)}, u32[]{:S(2)}, u32[]{:S(2)}) async-start(f32[8,16,128]{2,1,0:T(8,128)} %get-tuple-element.45), calls=%async_computation | async-start | bytes 131072 | tf_op jit(solution)/shard_map/all_to_all | solution.py:24
  11.7 2.0 %collective-permute-start = (f32[512,128]{1,0:T(8,128)}, f32[512,128]{1,0:T(8,128)S(1)}, u32[]{:S(2)}, u32[]{:S(2)}) collective-permute-start(f32[512,128]{1,0:T(8,128)} %get-tuple-element.46), channel_id=1, source_target_pairs={{0,4},{4,0},{8,12},{12,8},{16,20},{20,16},{24,28},{28,24},{1,5},{5... | collective-permute-start | bytes 786440 | tf_op jit(solution)/shard_map/ppermute | solution.py:444
  13.7 1.5 %collective-permute-start.1 = (f32[512,128]{1,0:T(8,128)}, f32[512,128]{1,0:T(8,128)S(1)}, u32[]{:S(2)}, u32[]{:S(2)}) collective-permute-start(f32[512,128]{1,0:T(8,128)} %get-tuple-element.47), channel_id=1, source_target_pairs={{0,8},{4,12},{8,0},{12,4},{16,24},{20,28},{24,16},{28,20},{1,9},{5... | collective-permute-start | bytes 786440 | tf_op jit(solution)/shard_map/ppermute | solution.py:444
  15.2 3.8 %all-to-all-done.refs_2_.parts_ref = f32[8,16,128]{2,1,0:T(8,128)S(1)} async-done(((f32[8,16,128]{2,1,0:T(8,128)}), f32[8,16,128]{2,1,0:T(8,128)S(1)}, u32[]{:S(2)}, u32[]{:S(2)}) %all-to-all-start) | async-done | bytes 65568 | tf_op jit(solution)/shard_map/all_to_all | solution.py:24
  19.0 0.7 collective-permute-start.2
  20.4 2.9 %collective-permute-done.1.refs_1_ = f32[512,128]{1,0:T(8,128)S(1)} collective-permute-done((f32[512,128]{1,0:T(8,128)}, f32[512,128]{1,0:T(8,128)S(1)}, u32[]{:S(2)}, u32[]{:S(2)}) %collective-permute-start.1) | collective-permute-done | bytes 262176 | tf_op jit(solution)/shard_map/ppermute | solution.py:444
  23.3 6.2 %shard_map.96 = (f32[32,128]{1,0:T(8,128)S(1)}, f32[1,128]{1,0:T(1,128)S(1)}, f32[1024,4096]{1,0:T(8,128)S(1)}) custom-call(f32[1024,4096]{1,0:T(8,128)} %rinv_ref.1, f32[8,16,128]{2,1,0:T(8,128)S(1)} %all-to-all-done.refs_2_.parts_ref, f32[1,128]{1,0:T(1,128)S(1)} %shard_map.95.order_ref), custom_call_target="tpu_custom_call" | custom-call | tf_op jit(solution)/shard_map/pallas_call | solution.py:486
  29.6 1.2 %collective-permute-done.4 = f32[32,128]{1,0:T(8,128)S(1)} collective-permute-done((f32[32,128]{1,0:T(8,128)S(1)}, f32[32,128]{1,0:T(8,128)S(1)}, u32[]{:S(2)}, u32[]{:S(2)}) %collective-permute-start.4) | collective-permute-done | bytes 16416 | tf_op jit(solution)/shard_map/ppermute | solution.py:31
  30.8 1.5 %collective-permute-start.5 = (f32[32,128]{1,0:T(8,128)S(1)}, f32[32,128]{1,0:T(8,128)S(1)}, u32[]{:S(2)}, u32[]{:S(2)}) collective-permute-start(f32[32,128]{1,0:T(8,128)S(1)} %add.6.refs_0_), channel_id=1, source_target_pairs={{0,2},{1,3},{2,0},{3,1},{4,6},{5,7},{6,4},{7,5},{8,10},{9,11},{10,... | collective-permute-start | bytes 49160 | tf_op jit(solution)/shard_map/ppermute | solution.py:31
  32.3 1.9 %collective-permute-start.9 = (f32[512,128]{1,0:T(8,128)S(1)}, f32[512,128]{1,0:T(8,128)S(1)}, u32[]{:S(2)}, u32[]{:S(2)}) collective-permute-start(f32[512,128]{1,0:T(8,128)S(1)} %copy-done.4), channel_id=1, source_target_pairs={{0,8},{4,12},{8,0},{12,4},{16,24},{20,28},{24,16},{28,20},{1,9},{5... | collective-permute-start | bytes 786440 | tf_op jit(solution)/shard_map/ppermute | solution.py:444
  34.7 1.1 %shard_map.98 = (f32[1,4,128,128]{3,2,1,0:T(8,128)S(1)}, f32[1,4,128,128]{3,2,1,0:T(8,128)S(1)}, f32[1,128]{1,0:T(1,128)S(1)}) custom-call(f32[512,1024]{1,0:T(8,128)S(1)} %copy-done, f32[8,16,128]{2,1,0:T(8,128)S(1)} %all-to-all-done.refs_2_.parts_ref, bf16[8,128,512]{2,1,0:T(8,128)(2,1)S(1)} %shard_map.97.mix_ref, ...), custom_call_target="tpu_custom_call" | custom-call | tf_op jit(solution)/shard_map/pallas_call | solution.py:61
  35.8 2.4 %collective-permute-start.3 = (f32[1,4,128,128]{3,2,1,0:T(8,128)S(1)}, f32[1,4,128,128]{3,2,1,0:T(8,128)S(1)}, u32[]{:S(2)}, u32[]{:S(2)}) collective-permute-start(f32[1,4,128,128]{3,2,1,0:T(8,128)S(1)} %get-tuple-element.55), channel_id=1, source_target_pairs={{0,16},{4,20},{8,24},{12,28},{16,0},{20,4},{24,8},{28,12},{1,17},{... | collective-permute-start | bytes 786440 | tf_op jit(solution)/shard_map/ppermute | solution.py:444
  38.2 1.5 %collective-permute-start.10 = (f32[512,128]{1,0:T(8,128)S(1)}, f32[512,128]{1,0:T(8,128)S(1)}, u32[]{:S(2)}, u32[]{:S(2)}) collective-permute-start(f32[512,128]{1,0:T(8,128)S(1)} %copy-done.3), channel_id=1, source_target_pairs={{0,12},{4,8},{8,4},{12,0},{16,28},{20,24},{24,20},{28,16},{1,13},{... | collective-permute-start | bytes 786440 | tf_op jit(solution)/shard_map/ppermute | solution.py:444
  39.7 2.5 %shard_map.99 = (f32[4,128]{1,0:T(4,128)S(1)}, f32[8,128]{1,0:T(8,128)S(1)}, f32[1,128]{1,0:T(1,128)S(1)}, f32[32,128]{1,0:T(8,128)S(1)}) custom-call(f32[1024,4096]{1,0:T(8,128)S(1)} %get-tuple-element.48.rinv_ref, f32[512,1024]{1,0:T(8,128)S(1)} %copy-done, f32[1,128]{1,0:T(1,128)S(1)} %get-tuple-element.56.token_ref, f32[32,128]{1,0:T(8,128)S(1)} %add.6.refs_0_, ...), custom_call_target="tpu_custom_call" | custom-call | tf_op jit(solution)/shard_map/pallas_call | solution.py:61
  42.2 1.1 %collective-permute-done.6 = f32[4,128]{1,0:T(4,128)S(1)} collective-permute-done((f32[4,128]{1,0:T(4,128)S(1)}, f32[4,128]{1,0:T(4,128)S(1)}, u32[]{:S(2)}, u32[]{:S(2)}) %collective-permute-start.6) | collective-permute-done | bytes 2080 | tf_op jit(solution)/shard_map/ppermute | solution.py:31
  43.9 3.0 %collective-permute-done.7.refs_1_ = f32[4,128]{1,0:T(4,128)S(1)} collective-permute-done((f32[4,128]{1,0:T(4,128)S(1)}, f32[4,128]{1,0:T(4,128)S(1)}, u32[]{:S(2)}, u32[]{:S(2)}) %collective-permute-start.7) | collective-permute-done | bytes 2080 | tf_op jit(solution)/shard_map/ppermute | solution.py:31
  47.2 9.4 %all_to_all.15.parts_ref = f32[8,16,128]{2,1,0:T(8,128)S(1)} all-to-all(f32[8,16,128]{2,1,0:T(8,128)S(1)} %get-tuple-element.60), channel_id=1, replica_groups=mesh['row'=8,'col'=4] {'row'}, dimensions={0} | all-to-all | bytes 131072 | tf_op jit(solution)/shard_map/all_to_all | solution.py:24
  56.6 2.0 %shard_map.101 = (f32[32,128]{1,0:T(8,128)S(1)}, f32[1,128]{1,0:T(1,128)S(1)}) custom-call(f32[1024,4096]{1,0:T(8,128)S(1)} %get-tuple-element.48.rinv_ref, f32[8,16,128]{2,1,0:T(8,128)S(1)} %all_to_all.15.parts_ref, f32[1,128]{1,0:T(1,128)S(1)} %get-tuple-element.59.refs_4_.order_ref.refs_2_), custom_call_target="tpu_custom_call" | custom-call | tf_op jit(solution)/shard_map/pallas_call | solution.py:486
  58.7 1.1 %shard_map.103 = (f32[1,4,128,128]{3,2,1,0:T(8,128)S(1)}, f32[1,4,128,128]{3,2,1,0:T(8,128)S(1)}, f32[1,128]{1,0:T(1,128)S(1)}) custom-call(f32[512,1024]{1,0:T(8,128)S(1)} %copy-done, f32[8,16,128]{2,1,0:T(8,128)S(1)} %all-to-all-done.refs_2_.parts_ref, bf16[8,128,512]{2,1,0:T(8,128)(2,1)S(1)} %shard_map.97.mix_ref, ...), custom_call_target="tpu_custom_call" | custom-call | tf_op jit(solution)/shard_map/pallas_call | solution.py:61
  60.9 1.3 %collective-permute-start.11 = (f32[32,128]{1,0:T(8,128)S(1)}, f32[32,128]{1,0:T(8,128)S(1)}, u32[]{:S(2)}, u32[]{:S(2)}) collective-permute-start(f32[32,128]{1,0:T(8,128)S(1)} %get-tuple-element.68.refs_0_), channel_id=1, source_target_pairs={{0,1},{1,0},{2,3},{3,2},{4,5},{5,4},{6,7},{7,6},{8,9},{9,8},{10,11... | collective-permute-start | bytes 49160 | tf_op jit(solution)/shard_map/ppermute | solution.py:41
  62.2 1.3 %collective-permute-done.13.refs_3_ = f32[32,128]{1,0:T(8,128)S(1)} collective-permute-done((f32[32,128]{1,0:T(8,128)S(1)}, f32[32,128]{1,0:T(8,128)S(1)}, u32[]{:S(2)}, u32[]{:S(2)}) %collective-permute-start.13) | collective-permute-done | bytes 16416 | tf_op jit(solution)/shard_map/ppermute | solution.py:41
  64.1 2.5 %shard_map.104 = (f32[4,128]{1,0:T(4,128)S(1)}, f32[8,128]{1,0:T(8,128)S(1)}, f32[1,128]{1,0:T(1,128)S(1)}) custom-call(f32[1024,4096]{1,0:T(8,128)S(1)} %get-tuple-element.48.rinv_ref, f32[512,1024]{1,0:T(8,128)S(1)} %copy-done, f32[1,128]{1,0:T(1,128)S(1)} %get-tuple-element.67.token_ref, f32[32,128]{1,0:T(8,128)S(1)} %get-tuple-element.68.refs_0_, ...), custom_call_target="tpu_custom_call" | custom-call | tf_op jit(solution)/shard_map/pallas_call | solution.py:61
  66.6 0.6 collective-permute-start.16
  67.8 0.7 collective-permute-start.14
  68.5 1.1 %collective-permute-done.16.refs_3_ = f32[4,128]{1,0:T(4,128)S(1)} collective-permute-done((f32[4,128]{1,0:T(4,128)S(1)}, f32[4,128]{1,0:T(4,128)S(1)}, u32[]{:S(2)}, u32[]{:S(2)}) %collective-permute-start.16) | collective-permute-done | bytes 2080 | tf_op jit(solution)/shard_map/ppermute | solution.py:41
  69.7 1.2 %collective-permute-done.15.refs_2_ = f32[4,128]{1,0:T(4,128)S(1)} collective-permute-done((f32[4,128]{1,0:T(4,128)S(1)}, f32[4,128]{1,0:T(4,128)S(1)}, u32[]{:S(2)}, u32[]{:S(2)}) %collective-permute-start.15) | collective-permute-done | bytes 2080 | tf_op jit(solution)/shard_map/ppermute | solution.py:41
  70.8 1.5 %collective-permute-done.17.refs_9_ = f32[1,4,128,128]{3,2,1,0:T(8,128)S(1)} collective-permute-done((f32[1,4,128,128]{3,2,1,0:T(8,128)S(1)}, f32[1,4,128,128]{3,2,1,0:T(8,128)S(1)}, u32[]{:S(2)}, u32[]{:S(2)}) %collective-permute-start.17) | collective-permute-done | bytes 262176 | tf_op jit(solution)/shard_map/ppermute | solution.py:444
  72.4 0.8 collective-permute-start.18
  73.2 2.7 %collective-permute-start.20 = (f32[128,256]{1,0:T(8,128)S(1)}, f32[128,256]{1,0:T(8,128)S(1)}, u32[]{:S(2)}, u32[]{:S(2)}) collective-permute-start(f32[128,256]{1,0:T(8,128)S(1)} %get-tuple-element.83), channel_id=1, source_target_pairs={{0,12},{4,8},{8,4},{12,0},{16,28},{20,24},{24,20},{28,16},{1,13},{... | collective-permute-start | bytes 393224 | tf_op jit(solution)/shard_map/ppermute | solution.py:444
  76.0 9.2 %all_to_all.16.parts_ref = f32[8,8,128]{2,1,0:T(8,128)S(1)} all-to-all(f32[8,8,128]{2,1,0:T(8,128)S(1)} %get-tuple-element.76), channel_id=1, replica_groups=mesh['row'=8,'col'=4] {'row'}, dimensions={0} | all-to-all | bytes 65536 | tf_op jit(solution)/shard_map/all_to_all | solution.py:24
  85.1 0.9 %shard_map.106 = (f32[4,128]{1,0:T(4,128)}, f32[8,128]{1,0:T(8,128)}, f32[128,1024]{1,0:T(8,128)}) custom-call(f32[8,8,128]{2,1,0:T(8,128)S(1)} %all_to_all.16.parts_ref, f32[4,128]{1,0:T(4,128)S(1)} %get-tuple-element.77.left_ref, f32[1,128]{1,0:T(1,128)S(1)} %get-tuple-element.49.order_ref.refs_3_.refs_0_, ...), custom_call_target="tpu_custom_call" | custom-call | tf_op jit(solution)/shard_map/pallas_call | solution.py:61
  (41 shorter events, 4.5 us)
Async XLA Ops:
  0.6 33.5 %copy-start.1 = (bf16[256,256]{1,0:T(8,128)(2,1)S(1)}, bf16[256,256]{1,0:T(8,128)(2,1)}, u32[]{:S(2)}) copy-start(bf16[256,256]{1,0:T(8,128)(2,1)} %constant.2.clone.walsh_ref) | copy-start | bytes 393220
  0.6 34.0 %copy-start = (f32[512,1024]{1,0:T(8,128)S(1)}, f32[512,1024]{1,0:T(8,128)}, u32[]{:S(2)}) copy-start(f32[512,1024]{1,0:T(8,128)} %design_ref.9) | copy-start | bytes 6291460
  4.3 28.0 %copy-start.4 = (f32[512,128]{1,0:T(8,128)S(1)}, f32[512,128]{1,0:T(8,128)}, u32[]{:S(2)}) copy-start(f32[512,128]{1,0:T(8,128)} %get-tuple-element.64) | copy-start | bytes 786436
  4.3 33.9 %copy-start.3 = (f32[512,128]{1,0:T(8,128)S(1)}, f32[512,128]{1,0:T(8,128)}, u32[]{:S(2)}) copy-start(f32[512,128]{1,0:T(8,128)} %get-tuple-element.66) | copy-start | bytes 786436
  4.3 14.8 %all-to-all-start = ((f32[8,16,128]{2,1,0:T(8,128)}), f32[8,16,128]{2,1,0:T(8,128)S(1)}, u32[]{:S(2)}, u32[]{:S(2)}) async-start(f32[8,16,128]{2,1,0:T(8,128)} %get-tuple-element.45), calls=%async_computation | async-start | bytes 131072 | tf_op jit(solution)/shard_map/all_to_all | solution.py:24
  11.7 8.7 %collective-permute-start = (f32[512,128]{1,0:T(8,128)}, f32[512,128]{1,0:T(8,128)S(1)}, u32[]{:S(2)}, u32[]{:S(2)}) collective-permute-start(f32[512,128]{1,0:T(8,128)} %get-tuple-element.46), channel_id=1, source_target_pairs={{0,4},{4,0},{8,12},{12,8},{16,20},{20,16},{24,28},{28,24},{1,5},{5... | collective-permute-start | bytes 786440 | tf_op jit(solution)/shard_map/ppermute | solution.py:444
  13.7 9.6 %collective-permute-start.1 = (f32[512,128]{1,0:T(8,128)}, f32[512,128]{1,0:T(8,128)S(1)}, u32[]{:S(2)}, u32[]{:S(2)}) collective-permute-start(f32[512,128]{1,0:T(8,128)} %get-tuple-element.47), channel_id=1, source_target_pairs={{0,8},{4,12},{8,0},{12,4},{16,24},{20,28},{24,16},{28,20},{1,9},{5... | collective-permute-start | bytes 786440 | tf_op jit(solution)/shard_map/ppermute | solution.py:444
  19.0 13.2 %copy-start.5 = (f32[512,128]{1,0:T(8,128)S(1)}, f32[512,128]{1,0:T(8,128)}, u32[]{:S(2)}) copy-start(f32[512,128]{1,0:T(8,128)} %get-tuple-element.63) | copy-start | bytes 786436
  19.0 15.6 %collective-permute-start.2 = (f32[512,128]{1,0:T(8,128)}, f32[512,128]{1,0:T(8,128)S(1)}, u32[]{:S(2)}, u32[]{:S(2)}) collective-permute-start(f32[512,128]{1,0:T(8,128)} %get-tuple-element.53), channel_id=1, source_target_pairs={{0,12},{4,8},{8,4},{12,0},{16,28},{20,24},{24,20},{28,16},{1,13},{... | collective-permute-start | bytes 786440 | tf_op jit(solution)/shard_map/ppermute | solution.py:444
  23.3 23.6 %copy-start.2 = (f32[512]{0:T(512)S(1)}, f32[512]{0:T(512)}, u32[]{:S(2)}) copy-start(f32[512]{0:T(512)} %param.11) | copy-start | bytes 6148
  29.5 1.2 %collective-permute-start.4 = (f32[32,128]{1,0:T(8,128)S(1)}, f32[32,128]{1,0:T(8,128)S(1)}, u32[]{:S(2)}, u32[]{:S(2)}) collective-permute-start(f32[32,128]{1,0:T(8,128)S(1)} %get-tuple-element.57), channel_id=1, source_target_pairs={{0,1},{1,0},{2,3},{3,2},{4,5},{5,4},{6,7},{7,6},{8,9},{9,8},{10,11... | collective-permute-start | bytes 49160 | tf_op jit(solution)/shard_map/ppermute | solution.py:31
  30.8 7.4 %collective-permute-start.5 = (f32[32,128]{1,0:T(8,128)S(1)}, f32[32,128]{1,0:T(8,128)S(1)}, u32[]{:S(2)}, u32[]{:S(2)}) collective-permute-start(f32[32,128]{1,0:T(8,128)S(1)} %add.6.refs_0_), channel_id=1, source_target_pairs={{0,2},{1,3},{2,0},{3,1},{4,6},{5,7},{6,4},{7,5},{8,10},{9,11},{10,... | collective-permute-start | bytes 49160 | tf_op jit(solution)/shard_map/ppermute | solution.py:31
  32.3 26.4 %collective-permute-start.8 = (f32[512,128]{1,0:T(8,128)S(1)}, f32[512,128]{1,0:T(8,128)S(1)}, u32[]{:S(2)}, u32[]{:S(2)}) collective-permute-start(f32[512,128]{1,0:T(8,128)S(1)} %copy-done.5), channel_id=1, source_target_pairs={{0,4},{4,0},{8,12},{12,8},{16,20},{20,16},{24,28},{28,24},{1,5},{5... | collective-permute-start | bytes 786440 | tf_op jit(solution)/shard_map/ppermute | solution.py:444
  32.3 26.4 %collective-permute-start.9 = (f32[512,128]{1,0:T(8,128)S(1)}, f32[512,128]{1,0:T(8,128)S(1)}, u32[]{:S(2)}, u32[]{:S(2)}) collective-permute-start(f32[512,128]{1,0:T(8,128)S(1)} %copy-done.4), channel_id=1, source_target_pairs={{0,8},{4,12},{8,0},{12,4},{16,24},{20,28},{24,16},{28,20},{1,9},{5... | collective-permute-start | bytes 786440 | tf_op jit(solution)/shard_map/ppermute | solution.py:444
  35.8 22.8 %collective-permute-start.3 = (f32[1,4,128,128]{3,2,1,0:T(8,128)S(1)}, f32[1,4,128,128]{3,2,1,0:T(8,128)S(1)}, u32[]{:S(2)}, u32[]{:S(2)}) collective-permute-start(f32[1,4,128,128]{3,2,1,0:T(8,128)S(1)} %get-tuple-element.55), channel_id=1, source_target_pairs={{0,16},{4,20},{8,24},{12,28},{16,0},{20,4},{24,8},{28,12},{1,17},{... | collective-permute-start | bytes 786440 | tf_op jit(solution)/shard_map/ppermute | solution.py:444
  38.2 20.5 %collective-permute-start.10 = (f32[512,128]{1,0:T(8,128)S(1)}, f32[512,128]{1,0:T(8,128)S(1)}, u32[]{:S(2)}, u32[]{:S(2)}) collective-permute-start(f32[512,128]{1,0:T(8,128)S(1)} %copy-done.3), channel_id=1, source_target_pairs={{0,12},{4,8},{8,4},{12,0},{16,28},{20,24},{24,20},{28,16},{1,13},{... | collective-permute-start | bytes 786440 | tf_op jit(solution)/shard_map/ppermute | solution.py:444
  42.1 1.2 %collective-permute-start.6 = (f32[4,128]{1,0:T(4,128)S(1)}, f32[4,128]{1,0:T(4,128)S(1)}, u32[]{:S(2)}, u32[]{:S(2)}) collective-permute-start(f32[4,128]{1,0:T(4,128)S(1)} %get-tuple-element.58), channel_id=1, source_target_pairs={{0,1},{1,0},{2,3},{3,2},{4,5},{5,4},{6,7},{7,6},{8,9},{9,8},{10,11... | collective-permute-start | bytes 6152 | tf_op jit(solution)/shard_map/ppermute | solution.py:31
  43.4 3.6 %collective-permute-start.7 = (f32[4,128]{1,0:T(4,128)S(1)}, f32[4,128]{1,0:T(4,128)S(1)}, u32[]{:S(2)}, u32[]{:S(2)}) collective-permute-start(f32[4,128]{1,0:T(4,128)S(1)} %add.7.refs_0_), channel_id=1, source_target_pairs={{0,2},{1,3},{2,0},{3,1},{4,6},{5,7},{6,4},{7,5},{8,10},{9,11},{10,... | collective-permute-start | bytes 6152 | tf_op jit(solution)/shard_map/ppermute | solution.py:31
  59.8 12.6 %collective-permute-start.17 = (f32[1,4,128,128]{3,2,1,0:T(8,128)S(1)}, f32[1,4,128,128]{3,2,1,0:T(8,128)S(1)}, u32[]{:S(2)}, u32[]{:S(2)}) collective-permute-start(f32[1,4,128,128]{3,2,1,0:T(8,128)S(1)} %get-tuple-element.75), channel_id=1, source_target_pairs={{0,16},{4,20},{8,24},{12,28},{16,0},{20,4},{24,8},{28,12},{1,17},{... | collective-permute-start | bytes 786440 | tf_op jit(solution)/shard_map/ppermute | solution.py:444
  60.3 3.2 %collective-permute-start.13 = (f32[32,128]{1,0:T(8,128)S(1)}, f32[32,128]{1,0:T(8,128)S(1)}, u32[]{:S(2)}, u32[]{:S(2)}) collective-permute-start(f32[32,128]{1,0:T(8,128)S(1)} %get-tuple-element.68.refs_0_), channel_id=1, source_target_pairs={{0,3},{1,2},{2,1},{3,0},{4,7},{5,6},{6,5},{7,4},{8,11},{9,10},{10,... | collective-permute-start | bytes 49160 | tf_op jit(solution)/shard_map/ppermute | solution.py:41
  60.3 3.8 %collective-permute-start.12 = (f32[32,128]{1,0:T(8,128)S(1)}, f32[32,128]{1,0:T(8,128)S(1)}, u32[]{:S(2)}, u32[]{:S(2)}) collective-permute-start(f32[32,128]{1,0:T(8,128)S(1)} %get-tuple-element.68.refs_0_), channel_id=1, source_target_pairs={{0,2},{1,3},{2,0},{3,1},{4,6},{5,7},{6,4},{7,5},{8,10},{9,11},{10,... | collective-permute-start | bytes 49160 | tf_op jit(solution)/shard_map/ppermute | solution.py:41
  60.9 3.2 %collective-permute-start.11 = (f32[32,128]{1,0:T(8,128)S(1)}, f32[32,128]{1,0:T(8,128)S(1)}, u32[]{:S(2)}, u32[]{:S(2)}) collective-permute-start(f32[32,128]{1,0:T(8,128)S(1)} %get-tuple-element.68.refs_0_), channel_id=1, source_target_pairs={{0,1},{1,0},{2,3},{3,2},{4,5},{5,4},{6,7},{7,6},{8,9},{9,8},{10,11... | collective-permute-start | bytes 49160 | tf_op jit(solution)/shard_map/ppermute | solution.py:41
  66.6 3.1 %collective-permute-start.16 = (f32[4,128]{1,0:T(4,128)S(1)}, f32[4,128]{1,0:T(4,128)S(1)}, u32[]{:S(2)}, u32[]{:S(2)}) collective-permute-start(f32[4,128]{1,0:T(4,128)S(1)} %get-tuple-element.70.refs_0_), channel_id=1, source_target_pairs={{0,3},{1,2},{2,1},{3,0},{4,7},{5,6},{6,5},{7,4},{8,11},{9,10},{10,... | collective-permute-start | bytes 6152 | tf_op jit(solution)/shard_map/ppermute | solution.py:41
  67.2 3.6 %collective-permute-start.15 = (f32[4,128]{1,0:T(4,128)S(1)}, f32[4,128]{1,0:T(4,128)S(1)}, u32[]{:S(2)}, u32[]{:S(2)}) collective-permute-start(f32[4,128]{1,0:T(4,128)S(1)} %get-tuple-element.70.refs_0_), channel_id=1, source_target_pairs={{0,2},{1,3},{2,0},{3,1},{4,6},{5,7},{6,4},{7,5},{8,10},{9,11},{10,... | collective-permute-start | bytes 6152 | tf_op jit(solution)/shard_map/ppermute | solution.py:41
  67.8 3.0 %collective-permute-start.14 = (f32[4,128]{1,0:T(4,128)S(1)}, f32[4,128]{1,0:T(4,128)S(1)}, u32[]{:S(2)}, u32[]{:S(2)}) collective-permute-start(f32[4,128]{1,0:T(4,128)S(1)} %get-tuple-element.70.refs_0_), channel_id=1, source_target_pairs={{0,1},{1,0},{2,3},{3,2},{4,5},{5,4},{6,7},{7,6},{8,9},{9,8},{10,11... | collective-permute-start | bytes 6152 | tf_op jit(solution)/shard_map/ppermute | solution.py:41
  72.4 12.7 %collective-permute-start.18 = (f32[128,256]{1,0:T(8,128)S(1)}, f32[128,256]{1,0:T(8,128)S(1)}, u32[]{:S(2)}, u32[]{:S(2)}) collective-permute-start(f32[128,256]{1,0:T(8,128)S(1)} %get-tuple-element.81), channel_id=1, source_target_pairs={{0,4},{4,0},{8,12},{12,8},{16,20},{20,16},{24,28},{28,24},{1,5},{5... | collective-permute-start | bytes 393224 | tf_op jit(solution)/shard_map/ppermute | solution.py:444
  73.2 11.9 %collective-permute-start.19 = (f32[128,256]{1,0:T(8,128)S(1)}, f32[128,256]{1,0:T(8,128)S(1)}, u32[]{:S(2)}, u32[]{:S(2)}) collective-permute-start(f32[128,256]{1,0:T(8,128)S(1)} %get-tuple-element.82), channel_id=1, source_target_pairs={{0,8},{4,12},{8,0},{12,4},{16,24},{20,28},{24,16},{28,20},{1,9},{5... | collective-permute-start | bytes 393224 | tf_op jit(solution)/shard_map/ppermute | solution.py:444
  73.2 11.9 %collective-permute-start.20 = (f32[128,256]{1,0:T(8,128)S(1)}, f32[128,256]{1,0:T(8,128)S(1)}, u32[]{:S(2)}, u32[]{:S(2)}) collective-permute-start(f32[128,256]{1,0:T(8,128)S(1)} %get-tuple-element.83), channel_id=1, source_target_pairs={{0,12},{4,8},{8,4},{12,0},{16,28},{20,24},{24,20},{28,16},{1,13},{... | collective-permute-start | bytes 393224 | tf_op jit(solution)/shard_map/ppermute | solution.py:444

commit v15 on v14

--- a/solution.py
+++ b/solution.py
@@ -253,15 +253,8 @@
     left = left - alpha_ref[...] * (before_ref[...] / beta_ref[...])
     square = splat(total(left * left))
     if last:
-        *parts, left_ref, out_ref = refs[: -NEAR]
-        out_refs = refs[-NEAR:]
+        left_ref, out_ref = refs
         out_ref[...] = jnp.broadcast_to(square, out_ref.shape)
-        *joined, kept_ref, arrived_ref = parts
-        piece = kept_ref.shape[3]
-        for index, rows_ref in enumerate(out_refs):
-            for chunk, part_ref in enumerate(joined):
-                rows_ref[:, chunk * piece : (chunk + 1) * piece] = part_ref[index]
-            rows_ref[:, len(joined) * piece :] = kept_ref[0, index] + arrived_ref[0, index]
     else:
         design_ref, left_ref, out_ref = refs
         tiles = design_ref.shape[1] // LANE
@@ -363,6 +356,15 @@
 def join_body(kept_ref, arrived_ref, order_ref, out_ref, token_ref):
     token_ref[...] = order_ref[:1, :]
     out_ref[...] = kept_ref[0] + arrived_ref[0]
+
+
+def split_body(*refs):
+    *joined, kept_ref, arrived_ref, order_ref = refs[:-NEAR]
+    piece = kept_ref.shape[3]
+    for index, rows_ref in enumerate(refs[-NEAR:]):
+        for chunk, part_ref in enumerate(joined):
+            rows_ref[:, chunk * piece : (chunk + 1) * piece] = part_ref[index]
+        rows_ref[:, len(joined) * piece :] = kept_ref[0, index] + arrived_ref[0, index]
 
 
 def touch_body(*refs):
@@ -504,20 +506,19 @@
             *before,
         )
 
-    def turn(images, left, beta, alpha, parts):
+    def turn(images, left, beta, alpha, last):
         return call(
-            functools.partial(turn_body, len(images), bool(parts)),
-            (shape(lines, LANE), shape(row_groups, 8 if parts else deep, LANE))
-            + (shape(slots, width // NEAR),) * (NEAR if parts else 0),
+            functools.partial(turn_body, len(images), last),
+            (shape(lines, LANE), shape(row_groups, 8 if last else deep, LANE)),
             *images,
             left,
             beta,
             alpha,
-            *(parts or (design,)),
+            *(() if last else (design,)),
         )
 
     betas, alphas, held, joined, right = [], [], [], [], []
-    near = spread(range(NEAR - 2), None)
+    near = spread(range(1), None)
     message = picked = exchange(message, "row")
     token = pl.pallas_call(
         touch_body,
@@ -527,7 +528,7 @@
         compiler_params=pltpu.CompilerParams(vmem_limit_bytes=2 << 20),
     )(*near, message)
     late = len(sent) - (chunks > 1)
-    near += spread(range(NEAR - 2, late), message)
+    near += spread(range(1, late), message)
     for step in range(ITERS):
         last = step + 1 == ITERS
         if step == 0:
@@ -552,10 +553,10 @@
         alphas.append(alpha)
         held.append(kept)
         images = direct(image, "col") if spare else paired(image, "col")
-        parts = (*joined, *halve(keep, come, beta)) if last else ()
-        left, message, *quarters = turn(images, left, beta, alpha, parts)
+        left, message = turn(images, left, beta, alpha, last)
         message = exchange(message, "row")
-    mine, *others = quarters
+    quarters = (shape(slots, width // NEAR),) * NEAR
+    mine, *others = call(split_body, quarters, *joined, *halve(keep, come, beta), left)
     basis, answer, sketch = call(
         last_body,
         (shape(lines, LANE), shape(width // LANE, LANE), shape(slots, width)),

time: 86.4 us -> 84.3 us (0.976)
  waiting for transfers between devices: 18.5 us -> 15.8 us
    ppermute x11, waiting for transfers between devices: 5.09 us -> 1.23 us  [swap(): lax.ppermute(array, 'row', [(i, i ^ mask) for i in range(row_groups)])]
    all_to_all x1, waiting for transfers between devices: 3.84 us -> 4.99 us  [exchange(): return lax.all_to_all(copies, axis, split_axis=0, concat_axis=0, tiled=True)]
    pallas_call x9 -> x10, Pallas kernels: 8.87 us -> 8.91 us  [call(): pl.pallas_call(body, out_shape=out_shape, in_specs=[VMEM] * len(operands)...]
  transfers between devices with their start and end apart: 22 -> 22, of which waited for: 11 -> 9; matrix products, arithmetic and copies ran while one was open for 0% -> 0% of each run, Pallas kernels for 17% -> 18%
where the time goes in v15:
time: 84.3 us; the launch traced here: 84 us
  starting transfers between devices  27.2 us (32%)
  Pallas kernels  20.7 us (25%)
  blocking collectives  19.4 us (23%)
  waiting for transfers between devices  15.8 us (19%)
    all_to_all x2, blocking collectives, exchange(): return lax.all_to_all(copies, axis, split_axis=0, concat_axis=0, tiled=True)  19.4 us
    ppermute x11, starting transfers between devices, swap(): lax.ppermute(array, 'row', [(i, i ^ mask) for i in range(row_groups)])  13.8 us
    pallas_call x10, Pallas kernels, call(): pl.pallas_call(body, out_shape=out_shape, in_specs=[VMEM] * len(operands)...  8.91 us
    pallas_call x2, Pallas kernels, back(): pl.pallas_call(functools.partial(back_body, first), out_shape=outs, in_sp...  8.16 us
    all_to_all x1, starting transfers between devices, exchange(): return lax.all_to_all(copies, axis, split_axis=0, concat_axis=0, tiled=True)  7.42 us
    ppermute x4, waiting for transfers between devices, paired(): come = lax.ppermute(array, axis, [(i, i ^ mask) for i in range(size)])  5.37 us
    all_to_all x1, waiting for transfers between devices, exchange(): return lax.all_to_all(copies, axis, split_axis=0, concat_axis=0, tiled=True)  4.99 us
    ppermute x6, waiting for transfers between devices, direct(): lax.ppermute(array, axis, [(i, i ^ mask) for i in range(size)])  4.21 us
  transfers between devices with their start and end apart: 22, of which 9 were waited for; matrix products, arithmetic and copies ran while one was open for 0% of the time, Pallas kernels for 18%

profile of v15, /device:TPU:0, one launch (start us, length us, event | category | flops | bytes accessed | tf_op | source)
XLA Modules:
  0.0 84.0 jit_solution(6970986302770613557)
XLA Ops:
  0.7 3.6 %shard_map.94 = (f32[8,16,128]{2,1,0:T(8,128)}, f32[512,128]{1,0:T(8,128)}, f32[512,128]{1,0:T(8,128)}, f32[512,128]{1,0:T(8,128)}, f32[512,128]{1,0:T(8,128)}, /*index=5*/f32[512,128]{1,0:T(8,128)}, f32[512,128]{1,0:T(8,128)}) custom-call(f32[512,1024]{1,0:T(8,128)} %design_ref.9, f32[4,128]{1,0:T(4,128)} %bitcast.6, s32[4,128]{1,0:T(4,128)} %bitcast.9, ...), custom_call_target="tpu_custom_call" | custom-call | tf_op jit(solution)/shard_map/pallas_call | solution.py:428
  4.3 7.4 %all-to-all-start = ((f32[8,16,128]{2,1,0:T(8,128)}), f32[8,16,128]{2,1,0:T(8,128)S(1)}, u32[]{:S(2)}, u32[]{:S(2)}) async-start(f32[8,16,128]{2,1,0:T(8,128)} %get-tuple-element.46), calls=%async_computation | async-start | bytes 131072 | tf_op jit(solution)/shard_map/all_to_all | solution.py:24
  11.7 2.0 %collective-permute-start = (f32[512,128]{1,0:T(8,128)}, f32[512,128]{1,0:T(8,128)S(1)}, u32[]{:S(2)}, u32[]{:S(2)}) collective-permute-start(f32[512,128]{1,0:T(8,128)} %get-tuple-element.47), channel_id=1, source_target_pairs={{0,4},{4,0},{8,12},{12,8},{16,20},{20,16},{24,28},{28,24},{1,5},{5... | collective-permute-start | bytes 786440 | tf_op jit(solution)/shard_map/ppermute | solution.py:446
  13.7 5.0 %all-to-all-done.refs_1_.parts_ref = f32[8,16,128]{2,1,0:T(8,128)S(1)} async-done(((f32[8,16,128]{2,1,0:T(8,128)}), f32[8,16,128]{2,1,0:T(8,128)S(1)}, u32[]{:S(2)}, u32[]{:S(2)}) %all-to-all-start) | async-done | bytes 65568 | tf_op jit(solution)/shard_map/all_to_all | solution.py:24
  18.9 1.6 %collective-permute-start.2 = (f32[512,128]{1,0:T(8,128)}, f32[512,128]{1,0:T(8,128)S(1)}, u32[]{:S(2)}, u32[]{:S(2)}) collective-permute-start(f32[512,128]{1,0:T(8,128)} %get-tuple-element.55), channel_id=1, source_target_pairs={{0,12},{4,8},{8,4},{12,0},{16,28},{20,24},{24,20},{28,16},{1,13},{... | collective-permute-start | bytes 786440 | tf_op jit(solution)/shard_map/ppermute | solution.py:446
  20.5 6.2 %shard_map.96 = (f32[32,128]{1,0:T(8,128)S(1)}, f32[1,128]{1,0:T(1,128)S(1)}, f32[1024,4096]{1,0:T(8,128)S(1)}) custom-call(f32[1024,4096]{1,0:T(8,128)} %rinv_ref.1, f32[8,16,128]{2,1,0:T(8,128)S(1)} %all-to-all-done.refs_1_.parts_ref, f32[1,128]{1,0:T(1,128)S(1)} %shard_map.95.order_ref), custom_call_target="tpu_custom_call" | custom-call | tf_op jit(solution)/shard_map/pallas_call | solution.py:488
  26.8 1.2 %collective-permute-done.4 = f32[32,128]{1,0:T(8,128)S(1)} collective-permute-done((f32[32,128]{1,0:T(8,128)S(1)}, f32[32,128]{1,0:T(8,128)S(1)}, u32[]{:S(2)}, u32[]{:S(2)}) %collective-permute-start.4) | collective-permute-done | bytes 16416 | tf_op jit(solution)/shard_map/ppermute | solution.py:31
  28.0 1.5 %collective-permute-start.5 = (f32[32,128]{1,0:T(8,128)S(1)}, f32[32,128]{1,0:T(8,128)S(1)}, u32[]{:S(2)}, u32[]{:S(2)}) collective-permute-start(f32[32,128]{1,0:T(8,128)S(1)} %add.6.refs_0_), channel_id=1, source_target_pairs={{0,2},{1,3},{2,0},{3,1},{4,6},{5,7},{6,4},{7,5},{8,10},{9,11},{10,... | collective-permute-start | bytes 49160 | tf_op jit(solution)/shard_map/ppermute | solution.py:31
  29.4 1.7 %collective-permute-start.8 = (f32[512,128]{1,0:T(8,128)S(1)}, f32[512,128]{1,0:T(8,128)S(1)}, u32[]{:S(2)}, u32[]{:S(2)}) collective-permute-start(f32[512,128]{1,0:T(8,128)S(1)} %copy-done.5), channel_id=1, source_target_pairs={{0,4},{4,0},{8,12},{12,8},{16,20},{20,16},{24,28},{28,24},{1,5},{5... | collective-permute-start | bytes 786440 | tf_op jit(solution)/shard_map/ppermute | solution.py:446
  31.2 1.0 %collective-permute-start.9 = (f32[512,128]{1,0:T(8,128)S(1)}, f32[512,128]{1,0:T(8,128)S(1)}, u32[]{:S(2)}, u32[]{:S(2)}) collective-permute-start(f32[512,128]{1,0:T(8,128)S(1)} %copy-done.4), channel_id=1, source_target_pairs={{0,8},{4,12},{8,0},{12,4},{16,24},{20,28},{24,16},{28,20},{1,9},{5... | collective-permute-start | bytes 786440 | tf_op jit(solution)/shard_map/ppermute | solution.py:446
  32.7 1.1 %shard_map.98 = (f32[1,4,128,128]{3,2,1,0:T(8,128)S(1)}, f32[1,4,128,128]{3,2,1,0:T(8,128)S(1)}, f32[1,128]{1,0:T(1,128)S(1)}) custom-call(f32[512,1024]{1,0:T(8,128)S(1)} %copy-done, f32[8,16,128]{2,1,0:T(8,128)S(1)} %all-to-all-done.refs_1_.parts_ref, bf16[8,128,512]{2,1,0:T(8,128)(2,1)S(1)} %shard_map.97.mix_ref, ...), custom_call_target="tpu_custom_call" | custom-call | tf_op jit(solution)/shard_map/pallas_call | solution.py:61
  33.8 2.4 %collective-permute-start.3 = (f32[1,4,128,128]{3,2,1,0:T(8,128)S(1)}, f32[1,4,128,128]{3,2,1,0:T(8,128)S(1)}, u32[]{:S(2)}, u32[]{:S(2)}) collective-permute-start(f32[1,4,128,128]{3,2,1,0:T(8,128)S(1)} %get-tuple-element.57), channel_id=1, source_target_pairs={{0,16},{4,20},{8,24},{12,28},{16,0},{20,4},{24,8},{28,12},{1,17},{... | collective-permute-start | bytes 786440 | tf_op jit(solution)/shard_map/ppermute | solution.py:446
  36.2 0.8 collective-permute-start.10
  37.0 2.5 %shard_map.99 = (f32[4,128]{1,0:T(4,128)S(1)}, f32[8,128]{1,0:T(8,128)S(1)}, f32[1,128]{1,0:T(1,128)S(1)}, f32[32,128]{1,0:T(8,128)S(1)}) custom-call(f32[1024,4096]{1,0:T(8,128)S(1)} %get-tuple-element.48.rinv_ref, f32[512,1024]{1,0:T(8,128)S(1)} %copy-done, f32[1,128]{1,0:T(1,128)S(1)} %get-tuple-element.58.token_ref, f32[32,128]{1,0:T(8,128)S(1)} %add.6.refs_0_, ...), custom_call_target="tpu_custom_call" | custom-call | tf_op jit(solution)/shard_map/pallas_call | solution.py:61
  39.5 1.1 %collective-permute-done.6 = f32[4,128]{1,0:T(4,128)S(1)} collective-permute-done((f32[4,128]{1,0:T(4,128)S(1)}, f32[4,128]{1,0:T(4,128)S(1)}, u32[]{:S(2)}, u32[]{:S(2)}) %collective-permute-start.6) | collective-permute-done | bytes 2080 | tf_op jit(solution)/shard_map/ppermute | solution.py:31
  41.2 3.1 %collective-permute-done.7.refs_1_ = f32[4,128]{1,0:T(4,128)S(1)} collective-permute-done((f32[4,128]{1,0:T(4,128)S(1)}, f32[4,128]{1,0:T(4,128)S(1)}, u32[]{:S(2)}, u32[]{:S(2)}) %collective-permute-start.7) | collective-permute-done | bytes 2080 | tf_op jit(solution)/shard_map/ppermute | solution.py:31
  44.5 10.2 %all_to_all.15.parts_ref = f32[8,16,128]{2,1,0:T(8,128)S(1)} all-to-all(f32[8,16,128]{2,1,0:T(8,128)S(1)} %get-tuple-element.62), channel_id=1, replica_groups=mesh['row'=8,'col'=4] {'row'}, dimensions={0} | all-to-all | bytes 131072 | tf_op jit(solution)/shard_map/all_to_all | solution.py:24
  54.7 2.0 %shard_map.101 = (f32[32,128]{1,0:T(8,128)S(1)}, f32[1,128]{1,0:T(1,128)S(1)}) custom-call(f32[1024,4096]{1,0:T(8,128)S(1)} %get-tuple-element.48.rinv_ref, f32[8,16,128]{2,1,0:T(8,128)S(1)} %all_to_all.15.parts_ref, f32[1,128]{1,0:T(1,128)S(1)} %get-tuple-element.61.refs_4_.order_ref.refs_2_), custom_call_target="tpu_custom_call" | custom-call | tf_op jit(solution)/shard_map/pallas_call | solution.py:488
  56.7 1.1 %shard_map.103 = (f32[1,4,128,128]{3,2,1,0:T(8,128)S(1)}, f32[1,4,128,128]{3,2,1,0:T(8,128)S(1)}, f32[1,128]{1,0:T(1,128)S(1)}) custom-call(f32[512,1024]{1,0:T(8,128)S(1)} %copy-done, f32[8,16,128]{2,1,0:T(8,128)S(1)} %all-to-all-done.refs_1_.parts_ref, bf16[8,128,512]{2,1,0:T(8,128)(2,1)S(1)} %shard_map.97.mix_ref, ...), custom_call_target="tpu_custom_call" | custom-call | tf_op jit(solution)/shard_map/pallas_call | solution.py:61
  58.9 1.3 %collective-permute-start.11 = (f32[32,128]{1,0:T(8,128)S(1)}, f32[32,128]{1,0:T(8,128)S(1)}, u32[]{:S(2)}, u32[]{:S(2)}) collective-permute-start(f32[32,128]{1,0:T(8,128)S(1)} %get-tuple-element.70.refs_0_), channel_id=1, source_target_pairs={{0,1},{1,0},{2,3},{3,2},{4,5},{5,4},{6,7},{7,6},{8,9},{9,8},{10,11... | collective-permute-start | bytes 49160 | tf_op jit(solution)/shard_map/ppermute | solution.py:41
  60.2 1.3 %collective-permute-done.13.refs_3_ = f32[32,128]{1,0:T(8,128)S(1)} collective-permute-done((f32[32,128]{1,0:T(8,128)S(1)}, f32[32,128]{1,0:T(8,128)S(1)}, u32[]{:S(2)}, u32[]{:S(2)}) %collective-permute-start.13) | collective-permute-done | bytes 16416 | tf_op jit(solution)/shard_map/ppermute | solution.py:41
  61.5 0.6 collective-permute-done.12.refs_2_
  62.1 2.5 %shard_map.104 = (f32[4,128]{1,0:T(4,128)S(1)}, f32[8,128]{1,0:T(8,128)S(1)}, f32[1,128]{1,0:T(1,128)S(1)}) custom-call(f32[1024,4096]{1,0:T(8,128)S(1)} %get-tuple-element.48.rinv_ref, f32[512,1024]{1,0:T(8,128)S(1)} %copy-done, f32[1,128]{1,0:T(1,128)S(1)} %get-tuple-element.69.token_ref, f32[32,128]{1,0:T(8,128)S(1)} %get-tuple-element.70.refs_0_, ...), custom_call_target="tpu_custom_call" | custom-call | tf_op jit(solution)/shard_map/pallas_call | solution.py:61
  64.6 0.6 collective-permute-start.16
  65.8 0.7 collective-permute-start.14
  66.6 1.1 %collective-permute-done.16.refs_3_ = f32[4,128]{1,0:T(4,128)S(1)} collective-permute-done((f32[4,128]{1,0:T(4,128)S(1)}, f32[4,128]{1,0:T(4,128)S(1)}, u32[]{:S(2)}, u32[]{:S(2)}) %collective-permute-start.16) | collective-permute-done | bytes 2080 | tf_op jit(solution)/shard_map/ppermute | solution.py:41
  67.7 1.2 %collective-permute-done.15.refs_2_ = f32[4,128]{1,0:T(4,128)S(1)} collective-permute-done((f32[4,128]{1,0:T(4,128)S(1)}, f32[4,128]{1,0:T(4,128)S(1)}, u32[]{:S(2)}, u32[]{:S(2)}) %collective-permute-start.15) | collective-permute-done | bytes 2080 | tf_op jit(solution)/shard_map/ppermute | solution.py:41
  69.0 1.2 %collective-permute-done.17.refs_2_ = f32[1,4,128,128]{3,2,1,0:T(8,128)S(1)} collective-permute-done((f32[1,4,128,128]{3,2,1,0:T(8,128)S(1)}, f32[1,4,128,128]{3,2,1,0:T(8,128)S(1)}, u32[]{:S(2)}, u32[]{:S(2)}) %collective-permute-start.17) | collective-permute-done | bytes 262176 | tf_op jit(solution)/shard_map/ppermute | solution.py:446
  70.2 1.0 %collective-permute-start.18 = (f32[128,256]{1,0:T(8,128)S(1)}, f32[128,256]{1,0:T(8,128)S(1)}, u32[]{:S(2)}, u32[]{:S(2)}) collective-permute-start(f32[128,256]{1,0:T(8,128)S(1)} %get-tuple-element.83), channel_id=1, source_target_pairs={{0,4},{4,0},{8,12},{12,8},{16,20},{20,16},{24,28},{28,24},{1,5},{5... | collective-permute-start | bytes 393224 | tf_op jit(solution)/shard_map/ppermute | solution.py:446
  71.2 2.5 %collective-permute-start.20 = (f32[128,256]{1,0:T(8,128)S(1)}, f32[128,256]{1,0:T(8,128)S(1)}, u32[]{:S(2)}, u32[]{:S(2)}) collective-permute-start(f32[128,256]{1,0:T(8,128)S(1)} %get-tuple-element.85), channel_id=1, source_target_pairs={{0,12},{4,8},{8,4},{12,0},{16,28},{20,24},{24,20},{28,16},{1,13},{... | collective-permute-start | bytes 393224 | tf_op jit(solution)/shard_map/ppermute | solution.py:446
  73.8 9.3 %all_to_all.16.parts_ref = f32[8,8,128]{2,1,0:T(8,128)S(1)} all-to-all(f32[8,8,128]{2,1,0:T(8,128)S(1)} %get-tuple-element.75), channel_id=1, replica_groups=mesh['row'=8,'col'=4] {'row'}, dimensions={0} | all-to-all | bytes 65536 | tf_op jit(solution)/shard_map/all_to_all | solution.py:24
  83.1 0.9 %shard_map.107 = (f32[4,128]{1,0:T(4,128)}, f32[8,128]{1,0:T(8,128)}, f32[128,1024]{1,0:T(8,128)}) custom-call(f32[8,8,128]{2,1,0:T(8,128)S(1)} %all_to_all.16.parts_ref, f32[4,128]{1,0:T(4,128)S(1)} %get-tuple-element.76.refs_3_.left_ref, f32[1,128]{1,0:T(1,128)S(1)} %get-tuple-element.49.order_ref.refs_3_.refs_0_, ...), custom_call_target="tpu_custom_call" | custom-call | tf_op jit(solution)/shard_map/pallas_call | solution.py:61
  (42 shorter events, 3.5 us)
Async XLA Ops:
  0.6 31.6 %copy-start.1 = (bf16[256,256]{1,0:T(8,128)(2,1)S(1)}, bf16[256,256]{1,0:T(8,128)(2,1)}, u32[]{:S(2)}) copy-start(bf16[256,256]{1,0:T(8,128)(2,1)} %constant.2.clone.walsh_ref) | copy-start | bytes 393220
  0.6 32.1 %copy-start = (f32[512,1024]{1,0:T(8,128)S(1)}, f32[512,1024]{1,0:T(8,128)}, u32[]{:S(2)}) copy-start(f32[512,1024]{1,0:T(8,128)} %design_ref.9) | copy-start | bytes 6291460
  4.3 25.2 %copy-start.5 = (f32[512,128]{1,0:T(8,128)S(1)}, f32[512,128]{1,0:T(8,128)}, u32[]{:S(2)}) copy-start(f32[512,128]{1,0:T(8,128)} %get-tuple-element.65) | copy-start | bytes 786436
  4.3 26.9 %copy-start.4 = (f32[512,128]{1,0:T(8,128)S(1)}, f32[512,128]{1,0:T(8,128)}, u32[]{:S(2)}) copy-start(f32[512,128]{1,0:T(8,128)} %get-tuple-element.66) | copy-start | bytes 786436
  4.3 31.9 %copy-start.3 = (f32[512,128]{1,0:T(8,128)S(1)}, f32[512,128]{1,0:T(8,128)}, u32[]{:S(2)}) copy-start(f32[512,128]{1,0:T(8,128)} %get-tuple-element.68) | copy-start | bytes 786436
  4.3 14.4 %all-to-all-start = ((f32[8,16,128]{2,1,0:T(8,128)}), f32[8,16,128]{2,1,0:T(8,128)S(1)}, u32[]{:S(2)}, u32[]{:S(2)}) async-start(f32[8,16,128]{2,1,0:T(8,128)} %get-tuple-element.46), calls=%async_computation | async-start | bytes 131072 | tf_op jit(solution)/shard_map/all_to_all | solution.py:24
  11.7 8.8 %collective-permute-start = (f32[512,128]{1,0:T(8,128)}, f32[512,128]{1,0:T(8,128)S(1)}, u32[]{:S(2)}, u32[]{:S(2)}) collective-permute-start(f32[512,128]{1,0:T(8,128)} %get-tuple-element.47), channel_id=1, source_target_pairs={{0,4},{4,0},{8,12},{12,8},{16,20},{20,16},{24,28},{28,24},{1,5},{5... | collective-permute-start | bytes 786440 | tf_op jit(solution)/shard_map/ppermute | solution.py:446
  18.7 14.0 %collective-permute-start.1 = (f32[512,128]{1,0:T(8,128)}, f32[512,128]{1,0:T(8,128)S(1)}, u32[]{:S(2)}, u32[]{:S(2)}) collective-permute-start(f32[512,128]{1,0:T(8,128)} %get-tuple-element.54), channel_id=1, source_target_pairs={{0,8},{4,12},{8,0},{12,4},{16,24},{20,28},{24,16},{28,20},{1,9},{5... | collective-permute-start | bytes 786440 | tf_op jit(solution)/shard_map/ppermute | solution.py:446
  18.9 13.8 %collective-permute-start.2 = (f32[512,128]{1,0:T(8,128)}, f32[512,128]{1,0:T(8,128)S(1)}, u32[]{:S(2)}, u32[]{:S(2)}) collective-permute-start(f32[512,128]{1,0:T(8,128)} %get-tuple-element.55), channel_id=1, source_target_pairs={{0,12},{4,8},{8,4},{12,0},{16,28},{20,24},{24,20},{28,16},{1,13},{... | collective-permute-start | bytes 786440 | tf_op jit(solution)/shard_map/ppermute | solution.py:446
  20.5 23.8 %copy-start.2 = (f32[512]{0:T(512)S(1)}, f32[512]{0:T(512)}, u32[]{:S(2)}) copy-start(f32[512]{0:T(512)} %param.11) | copy-start | bytes 6148
  26.7 1.2 %collective-permute-start.4 = (f32[32,128]{1,0:T(8,128)S(1)}, f32[32,128]{1,0:T(8,128)S(1)}, u32[]{:S(2)}, u32[]{:S(2)}) collective-permute-start(f32[32,128]{1,0:T(8,128)S(1)} %get-tuple-element.59), channel_id=1, source_target_pairs={{0,1},{1,0},{2,3},{3,2},{4,5},{5,4},{6,7},{7,6},{8,9},{9,8},{10,11... | collective-permute-start | bytes 49160 | tf_op jit(solution)/shard_map/ppermute | solution.py:31
  28.0 8.2 %collective-permute-start.5 = (f32[32,128]{1,0:T(8,128)S(1)}, f32[32,128]{1,0:T(8,128)S(1)}, u32[]{:S(2)}, u32[]{:S(2)}) collective-permute-start(f32[32,128]{1,0:T(8,128)S(1)} %add.6.refs_0_), channel_id=1, source_target_pairs={{0,2},{1,3},{2,0},{3,1},{4,6},{5,7},{6,4},{7,5},{8,10},{9,11},{10,... | collective-permute-start | bytes 49160 | tf_op jit(solution)/shard_map/ppermute | solution.py:31
  29.4 27.3 %collective-permute-start.8 = (f32[512,128]{1,0:T(8,128)S(1)}, f32[512,128]{1,0:T(8,128)S(1)}, u32[]{:S(2)}, u32[]{:S(2)}) collective-permute-start(f32[512,128]{1,0:T(8,128)S(1)} %copy-done.5), channel_id=1, source_target_pairs={{0,4},{4,0},{8,12},{12,8},{16,20},{20,16},{24,28},{28,24},{1,5},{5... | collective-permute-start | bytes 786440 | tf_op jit(solution)/shard_map/ppermute | solution.py:446
  31.2 25.5 %collective-permute-start.9 = (f32[512,128]{1,0:T(8,128)S(1)}, f32[512,128]{1,0:T(8,128)S(1)}, u32[]{:S(2)}, u32[]{:S(2)}) collective-permute-start(f32[512,128]{1,0:T(8,128)S(1)} %copy-done.4), channel_id=1, source_target_pairs={{0,8},{4,12},{8,0},{12,4},{16,24},{20,28},{24,16},{28,20},{1,9},{5... | collective-permute-start | bytes 786440 | tf_op jit(solution)/shard_map/ppermute | solution.py:446
  33.8 22.8 %collective-permute-start.3 = (f32[1,4,128,128]{3,2,1,0:T(8,128)S(1)}, f32[1,4,128,128]{3,2,1,0:T(8,128)S(1)}, u32[]{:S(2)}, u32[]{:S(2)}) collective-permute-start(f32[1,4,128,128]{3,2,1,0:T(8,128)S(1)} %get-tuple-element.57), channel_id=1, source_target_pairs={{0,16},{4,20},{8,24},{12,28},{16,0},{20,4},{24,8},{28,12},{1,17},{... | collective-permute-start | bytes 786440 | tf_op jit(solution)/shard_map/ppermute | solution.py:446
  36.2 20.5 %collective-permute-start.10 = (f32[512,128]{1,0:T(8,128)S(1)}, f32[512,128]{1,0:T(8,128)S(1)}, u32[]{:S(2)}, u32[]{:S(2)}) collective-permute-start(f32[512,128]{1,0:T(8,128)S(1)} %copy-done.3), channel_id=1, source_target_pairs={{0,12},{4,8},{8,4},{12,0},{16,28},{20,24},{24,20},{28,16},{1,13},{... | collective-permute-start | bytes 786440 | tf_op jit(solution)/shard_map/ppermute | solution.py:446
  39.5 1.2 %collective-permute-start.6 = (f32[4,128]{1,0:T(4,128)S(1)}, f32[4,128]{1,0:T(4,128)S(1)}, u32[]{:S(2)}, u32[]{:S(2)}) collective-permute-start(f32[4,128]{1,0:T(4,128)S(1)} %get-tuple-element.60), channel_id=1, source_target_pairs={{0,1},{1,0},{2,3},{3,2},{4,5},{5,4},{6,7},{7,6},{8,9},{9,8},{10,11... | collective-permute-start | bytes 6152 | tf_op jit(solution)/shard_map/ppermute | solution.py:31
  40.7 3.6 %collective-permute-start.7 = (f32[4,128]{1,0:T(4,128)S(1)}, f32[4,128]{1,0:T(4,128)S(1)}, u32[]{:S(2)}, u32[]{:S(2)}) collective-permute-start(f32[4,128]{1,0:T(4,128)S(1)} %add.7.refs_0_), channel_id=1, source_target_pairs={{0,2},{1,3},{2,0},{3,1},{4,6},{5,7},{6,4},{7,5},{8,10},{9,11},{10,... | collective-permute-start | bytes 6152 | tf_op jit(solution)/shard_map/ppermute | solution.py:31
  57.8 12.3 %collective-permute-start.17 = (f32[1,4,128,128]{3,2,1,0:T(8,128)S(1)}, f32[1,4,128,128]{3,2,1,0:T(8,128)S(1)}, u32[]{:S(2)}, u32[]{:S(2)}) collective-permute-start(f32[1,4,128,128]{3,2,1,0:T(8,128)S(1)} %get-tuple-element.81), channel_id=1, source_target_pairs={{0,16},{4,20},{8,24},{12,28},{16,0},{20,4},{24,8},{28,12},{1,17},{... | collective-permute-start | bytes 786440 | tf_op jit(solution)/shard_map/ppermute | solution.py:446
  58.4 3.2 %collective-permute-start.13 = (f32[32,128]{1,0:T(8,128)S(1)}, f32[32,128]{1,0:T(8,128)S(1)}, u32[]{:S(2)}, u32[]{:S(2)}) collective-permute-start(f32[32,128]{1,0:T(8,128)S(1)} %get-tuple-element.70.refs_0_), channel_id=1, source_target_pairs={{0,3},{1,2},{2,1},{3,0},{4,7},{5,6},{6,5},{7,4},{8,11},{9,10},{10,... | collective-permute-start | bytes 49160 | tf_op jit(solution)/shard_map/ppermute | solution.py:41
  58.4 3.8 %collective-permute-start.12 = (f32[32,128]{1,0:T(8,128)S(1)}, f32[32,128]{1,0:T(8,128)S(1)}, u32[]{:S(2)}, u32[]{:S(2)}) collective-permute-start(f32[32,128]{1,0:T(8,128)S(1)} %get-tuple-element.70.refs_0_), channel_id=1, source_target_pairs={{0,2},{1,3},{2,0},{3,1},{4,6},{5,7},{6,4},{7,5},{8,10},{9,11},{10,... | collective-permute-start | bytes 49160 | tf_op jit(solution)/shard_map/ppermute | solution.py:41
  58.9 3.2 %collective-permute-start.11 = (f32[32,128]{1,0:T(8,128)S(1)}, f32[32,128]{1,0:T(8,128)S(1)}, u32[]{:S(2)}, u32[]{:S(2)}) collective-permute-start(f32[32,128]{1,0:T(8,128)S(1)} %get-tuple-element.70.refs_0_), channel_id=1, source_target_pairs={{0,1},{1,0},{2,3},{3,2},{4,5},{5,4},{6,7},{7,6},{8,9},{9,8},{10,11... | collective-permute-start | bytes 49160 | tf_op jit(solution)/shard_map/ppermute | solution.py:41
  64.6 3.1 %collective-permute-start.16 = (f32[4,128]{1,0:T(4,128)S(1)}, f32[4,128]{1,0:T(4,128)S(1)}, u32[]{:S(2)}, u32[]{:S(2)}) collective-permute-start(f32[4,128]{1,0:T(4,128)S(1)} %get-tuple-element.72.refs_0_), channel_id=1, source_target_pairs={{0,3},{1,2},{2,1},{3,0},{4,7},{5,6},{6,5},{7,4},{8,11},{9,10},{10,... | collective-permute-start | bytes 6152 | tf_op jit(solution)/shard_map/ppermute | solution.py:41
  65.3 3.6 %collective-permute-start.15 = (f32[4,128]{1,0:T(4,128)S(1)}, f32[4,128]{1,0:T(4,128)S(1)}, u32[]{:S(2)}, u32[]{:S(2)}) collective-permute-start(f32[4,128]{1,0:T(4,128)S(1)} %get-tuple-element.72.refs_0_), channel_id=1, source_target_pairs={{0,2},{1,3},{2,0},{3,1},{4,6},{5,7},{6,4},{7,5},{8,10},{9,11},{10,... | collective-permute-start | bytes 6152 | tf_op jit(solution)/shard_map/ppermute | solution.py:41
  65.8 3.0 %collective-permute-start.14 = (f32[4,128]{1,0:T(4,128)S(1)}, f32[4,128]{1,0:T(4,128)S(1)}, u32[]{:S(2)}, u32[]{:S(2)}) collective-permute-start(f32[4,128]{1,0:T(4,128)S(1)} %get-tuple-element.72.refs_0_), channel_id=1, source_target_pairs={{0,1},{1,0},{2,3},{3,2},{4,5},{5,4},{6,7},{7,6},{8,9},{9,8},{10,11... | collective-permute-start | bytes 6152 | tf_op jit(solution)/shard_map/ppermute | solution.py:41
  70.2 12.8 %collective-permute-start.18 = (f32[128,256]{1,0:T(8,128)S(1)}, f32[128,256]{1,0:T(8,128)S(1)}, u32[]{:S(2)}, u32[]{:S(2)}) collective-permute-start(f32[128,256]{1,0:T(8,128)S(1)} %get-tuple-element.83), channel_id=1, source_target_pairs={{0,4},{4,0},{8,12},{12,8},{16,20},{20,16},{24,28},{28,24},{1,5},{5... | collective-permute-start | bytes 393224 | tf_op jit(solution)/shard_map/ppermute | solution.py:446
  71.2 11.8 %collective-permute-start.19 = (f32[128,256]{1,0:T(8,128)S(1)}, f32[128,256]{1,0:T(8,128)S(1)}, u32[]{:S(2)}, u32[]{:S(2)}) collective-permute-start(f32[128,256]{1,0:T(8,128)S(1)} %get-tuple-element.84), channel_id=1, source_target_pairs={{0,8},{4,12},{8,0},{12,4},{16,24},{20,28},{24,16},{28,20},{1,9},{5... | collective-permute-start | bytes 393224 | tf_op jit(solution)/shard_map/ppermute | solution.py:446
  71.2 11.8 %collective-permute-start.20 = (f32[128,256]{1,0:T(8,128)S(1)}, f32[128,256]{1,0:T(8,128)S(1)}, u32[]{:S(2)}, u32[]{:S(2)}) collective-permute-start(f32[128,256]{1,0:T(8,128)S(1)} %get-tuple-element.85), channel_id=1, source_target_pairs={{0,12},{4,8},{8,4},{12,0},{16,28},{20,24},{24,20},{28,16},{1,13},{... | collective-permute-start | bytes 393224 | tf_op jit(solution)/shard_map/ppermute | solution.py:446

commit v16 on v15

--- a/solution.py
+++ b/solution.py
@@ -92,24 +92,16 @@
         out_ref[tile : tile + 1, :] = jnp.sum(sums[tile], axis=0, keepdims=True)
 
 
-def left_product_long(vector_ref, matrix_ref, out_ref, copies=()):
+def left_product_upper(vector_ref, matrix_ref, out_ref, copies=()):
     blocks, tiles = matrix_ref.shape[0] // LANE, matrix_ref.shape[1] // LANE
-
-    def step(block, sums):
-        weight = across(vector_ref[pl.ds(block, 1), :])
-        rows = pl.ds(pl.multiple_of(block * LANE, LANE), LANE)
-        return tuple(
-            sums[tile] + fold_rows(matrix_ref[rows, tile * LANE : (tile + 1) * LANE] * weight)
-            for tile in range(tiles)
-        )
-
-    sums = tuple(jnp.zeros((8, LANE), F32) for _ in range(tiles))
-    if copies:
-        for block, copy in enumerate(copies):
-            copy.wait()
-            sums = step(block, sums)
-    else:
-        sums = lax.fori_loop(0, blocks, step, sums)
+    sums = [jnp.zeros((8, LANE), F32) for _ in range(tiles)]
+    for block in range(blocks):
+        if copies:
+            copies[block].wait()
+        weight = across(vector_ref[block : block + 1, :])
+        for tile in range(block, tiles):
+            part = matrix_ref[block * LANE : (block + 1) * LANE, tile * LANE : (tile + 1) * LANE]
+            sums[tile] = sums[tile] + fold_rows(part * weight)
     for tile in range(tiles):
         out_ref[tile : tile + 1, :] = jnp.sum(sums[tile], axis=0, keepdims=True)
 
@@ -126,6 +118,16 @@
         return carry
 
     lax.fori_loop(0, blocks, step, 0)
+
+
+def right_product_upper(matrix_ref, vector, out_ref):
+    blocks, tiles = matrix_ref.shape[0] // LANE, matrix_ref.shape[1] // LANE
+    for block in range(blocks):
+        rows = slice(block * LANE, (block + 1) * LANE)
+        sums = jnp.zeros((LANE, LANE), F32)
+        for tile in range(block, tiles):
+            sums = sums + matrix_ref[rows, tile * LANE : (tile + 1) * LANE] * vector[tile : tile + 1, :]
+        out_ref[block : block + 1, :] = jnp.sum(fold_rows(sums.T), axis=0, keepdims=True)
 
 
 def rounded(count, unit):
@@ -176,8 +178,9 @@
         piece = away_ref.shape[1]
         mask, start = sent[index]
         column = pl.multiple_of((place ^ mask) * (width // NEAR) + start, LANE)
-        source = design.at[:, pl.ds(column, piece)]
-        away.append(pltpu.make_async_copy(source, away_ref, sems.at[4 + lines + index]))
+        for line, part in enumerate(parts):
+            source = design.at[part, pl.ds(column, piece)]
+            away.append(pltpu.make_async_copy(source, away_ref.at[part, :], sems.at[4 + lines * (index + 1) + line]))
     for copy in small + large:
         copy.start()
     for copy in small:
@@ -201,9 +204,8 @@
     for line, part in enumerate(parts):
         weight = across(target[line : line + 1, :])
         large[line].wait()
-        if line == lines - 1:
-            for copy in away:
-                copy.start()
+        for copy in away[line::lines]:
+            copy.start()
         for tile in range(tiles):
             sums[tile] = sums[tile] + fold_rows(design[part, tile * LANE : (tile + 1) * LANE] * weight)
     for tile in range(tiles):
@@ -213,14 +215,14 @@
         copy.wait()
 
 
-def back_body(first, rinv_ref, parts_ref, order_ref, term_ref, beta_ref, *refs):
+def back_body(first, rinv_ref, parts_ref, term_ref, beta_ref, *refs):
     tiles = rinv_ref.shape[0] // LANE
     copies = []
     if first:
         rinv_here, scratch, sems = refs
         for block in range(tiles):
-            part = slice(block * LANE, (block + 1) * LANE)
-            copies.append(pltpu.make_async_copy(rinv_ref.at[part, :], rinv_here.at[part, :], sems.at[block]))
+            part, right = slice(block * LANE, (block + 1) * LANE), slice(block * LANE, rinv_ref.shape[1])
+            copies.append(pltpu.make_async_copy(rinv_ref.at[part, right], rinv_here.at[part, right], sems.at[block]))
             copies[-1].start()
     else:
         rinv_here, (scratch,) = rinv_ref, refs
@@ -228,7 +230,7 @@
     beta = jnp.sqrt(summed[tiles : tiles + 1, :])
     beta_ref[...] = beta
     scratch[...] = summed[:tiles, :] / beta
-    left_product_long(scratch, rinv_here, term_ref, copies)
+    left_product_upper(scratch, rinv_here, term_ref, copies)
 
 
 def forward_body(groups, first, last, rinv_ref, design_ref, token_ref, *refs):
@@ -243,7 +245,7 @@
     right = right / alpha
     if not last:
         right_refs[0][...] = right
-    right_product(rinv_ref, right, held_ref)
+    right_product_upper(rinv_ref, right, held_ref)
     right_product(design_ref, held_ref[...], image_ref)
 
 
@@ -367,9 +369,8 @@
         rows_ref[:, len(joined) * piece :] = kept_ref[0, index] + arrived_ref[0, index]
 
 
-def touch_body(*refs):
-    order_ref, token_ref = refs[-2:]
-    token_ref[...] = order_ref[0, :1, :]
+def pass_body(*refs):
+    refs[-1][...] = refs[-2][...]
 
 
 def last_body(parts_ref, left_ref, *refs):
@@ -437,7 +438,7 @@
             pltpu.VMEM((lines, LANE), jnp.int32),
             pltpu.VMEM((row_groups, PAIR), jnp.int32),
             pltpu.VMEM((1, row_groups), jnp.int32),
-            pltpu.SemaphoreType.DMA((4 + lines + len(sent),)),
+            pltpu.SemaphoreType.DMA((4 + lines * (1 + len(sent)),)),
         ],
         compiler_params=pltpu.CompilerParams(vmem_limit_bytes=58 << 20),
     )(design, left, bits, picks.reshape(row_groups, PAIR), counts.reshape(1, row_groups))
@@ -480,7 +481,7 @@
         keep, come = halve(keep, come, order)
         return call(join_body, (shape(*keep.shape[1:]), scalar), keep, come, order)
 
-    def back(rinv, message, order, first):
+    def back(rinv, message, first):
         outs, scratch = (shape(whole // LANE, LANE), scalar), [pltpu.VMEM((width // LANE, LANE), F32)]
         if first:
             outs += (shape(*rinv.shape),)
@@ -488,11 +489,11 @@
         return pl.pallas_call(
             functools.partial(back_body, first),
             out_shape=outs,
-            in_specs=[HBM if first else VMEM, VMEM, VMEM],
+            in_specs=[HBM if first else VMEM, VMEM],
             out_specs=(VMEM,) * len(outs),
             scratch_shapes=scratch,
             compiler_params=pltpu.CompilerParams(vmem_limit_bytes=(34 if first else 24) << 20),
-            )(rinv, message, order)
+            )(rinv, message)
 
     def forward(terms, token, last, *before):
         return call(
@@ -520,22 +521,22 @@
     betas, alphas, held, joined, right = [], [], [], [], []
     near = spread(range(1), None)
     message = picked = exchange(message, "row")
-    token = pl.pallas_call(
-        touch_body,
-        out_shape=scalar,
-        in_specs=[ANY] * len(near) + [VMEM],
-        out_specs=VMEM,
-        compiler_params=pltpu.CompilerParams(vmem_limit_bytes=2 << 20),
-    )(*near, message)
     late = len(sent) - (chunks > 1)
     near += spread(range(1, late), message)
     for step in range(ITERS):
         last = step + 1 == ITERS
         if step == 0:
-            term, beta, here = back(rinv, message, token, True)
+            term, beta, here = back(rinv, message, True)
+            term = pl.pallas_call(
+                pass_body,
+                out_shape=shape(*term.shape),
+                in_specs=[ANY, VMEM],
+                out_specs=VMEM,
+                compiler_params=pltpu.CompilerParams(vmem_limit_bytes=2 << 20),
+            )(near[0], term)
             mixed = mix(message)
         else:
-            term, beta = back(here, message, alpha, False)
+            term, beta = back(here, message, False)
             token = beta
             if chunks > 1:
                 part, token = join(keep, come, beta)

time: 84.3 us -> 81.5 us (0.967)
  Pallas kernels: 20.7 us -> 17.8 us
  blocking collectives: 19.4 us -> 20.6 us
  starting transfers between devices: 27.2 us -> 26.2 us
    ppermute x11, starting transfers between devices: 13.8 us -> 11.9 us  [swap(): lax.ppermute(array, 'row', [(i, i ^ mask) for i in range(row_groups)])]
    pallas_call x10, Pallas kernels: 8.91 us -> 7.41 us  [call(): pl.pallas_call(body, out_shape=out_shape, in_specs=[VMEM] * len(operands)...]
    all_to_all x2, blocking collectives: 19.4 us -> 20.6 us  [exchange(): return lax.all_to_all(copies, axis, split_axis=0, concat_axis=0, tiled=True)]
    pallas_call x2, Pallas kernels: 8.16 us -> 6.99 us  [back(): pl.pallas_call(functools.partial(back_body, first), out_shape=outs, in_sp...]
  transfers between devices with their start and end apart: 22 -> 22, of which waited for: 9 -> 9; matrix products, arithmetic and copies ran while one was open for 0% -> 0% of each run, Pallas kernels for 18% -> 15%
where the time goes in v16:
time: 81.5 us; the launch traced here: 81.1 us
  starting transfers between devices  26.2 us (32%)
  blocking collectives  20.6 us (25%)
  Pallas kernels  17.8 us (22%)
  waiting for transfers between devices  15.7 us (19%)
  between operations  0.85 us (1%)
    all_to_all x2, blocking collectives, exchange(): return lax.all_to_all(copies, axis, split_axis=0, concat_axis=0, tiled=True)  20.6 us
    ppermute x11, starting transfers between devices, swap(): lax.ppermute(array, 'row', [(i, i ^ mask) for i in range(row_groups)])  11.9 us
    all_to_all x1, starting transfers between devices, exchange(): return lax.all_to_all(copies, axis, split_axis=0, concat_axis=0, tiled=True)  7.42 us
    pallas_call x10, Pallas kernels, call(): pl.pallas_call(body, out_shape=out_shape, in_specs=[VMEM] * len(operands)...  7.41 us
    pallas_call x2, Pallas kernels, back(): pl.pallas_call(functools.partial(back_body, first), out_shape=outs, in_sp...  6.99 us
    all_to_all x1, waiting for transfers between devices, exchange(): return lax.all_to_all(copies, axis, split_axis=0, concat_axis=0, tiled=True)  4.99 us
    ppermute x4, waiting for transfers between devices, paired(): come = lax.ppermute(array, axis, [(i, i ^ mask) for i in range(size)])  4.53 us
    ppermute x6, waiting for transfers between devices, direct(): lax.ppermute(array, axis, [(i, i ^ mask) for i in range(size)])  4.45 us
  transfers between devices with their start and end apart: 22, of which 9 were waited for; matrix products, arithmetic and copies ran while one was open for 0% of the time, Pallas kernels for 15%

profile of v16, /device:TPU:0, one launch (start us, length us, event | category | flops | bytes accessed | tf_op | source)
XLA Modules:
  0.0 81.1 jit_solution(5690508534318977268)
XLA Ops:
  0.7 3.4 %shard_map.94 = (f32[8,16,128]{2,1,0:T(8,128)}, f32[512,128]{1,0:T(8,128)}, f32[512,128]{1,0:T(8,128)}, f32[512,128]{1,0:T(8,128)}, f32[512,128]{1,0:T(8,128)}, /*index=5*/f32[512,128]{1,0:T(8,128)}, f32[512,128]{1,0:T(8,128)}) custom-call(f32[512,1024]{1,0:T(8,128)} %design_ref.9, f32[4,128]{1,0:T(4,128)} %bitcast.6, s32[4,128]{1,0:T(4,128)} %bitcast.9, ...), custom_call_target="tpu_custom_call" | custom-call | tf_op jit(solution)/shard_map/pallas_call | solution.py:429
  4.1 7.4 %all-to-all-start = ((f32[8,16,128]{2,1,0:T(8,128)}), f32[8,16,128]{2,1,0:T(8,128)S(1)}, u32[]{:S(2)}, u32[]{:S(2)}) async-start(f32[8,16,128]{2,1,0:T(8,128)} %get-tuple-element.46), calls=%async_computation | async-start | bytes 131072 | tf_op jit(solution)/shard_map/all_to_all | solution.py:24
  11.5 2.0 %collective-permute-start = (f32[512,128]{1,0:T(8,128)}, f32[512,128]{1,0:T(8,128)S(1)}, u32[]{:S(2)}, u32[]{:S(2)}) collective-permute-start(f32[512,128]{1,0:T(8,128)} %get-tuple-element.49), channel_id=1, source_target_pairs={{0,4},{4,0},{8,12},{12,8},{16,20},{20,16},{24,28},{28,24},{1,5},{5... | collective-permute-start | bytes 786440 | tf_op jit(solution)/shard_map/ppermute | solution.py:447
  13.5 5.0 %all-to-all-done.parts_ref = f32[8,16,128]{2,1,0:T(8,128)S(1)} async-done(((f32[8,16,128]{2,1,0:T(8,128)}), f32[8,16,128]{2,1,0:T(8,128)S(1)}, u32[]{:S(2)}, u32[]{:S(2)}) %all-to-all-start) | async-done | bytes 65568 | tf_op jit(solution)/shard_map/all_to_all | solution.py:24
  18.7 1.6 %collective-permute-start.2 = (f32[512,128]{1,0:T(8,128)}, f32[512,128]{1,0:T(8,128)S(1)}, u32[]{:S(2)}, u32[]{:S(2)}) collective-permute-start(f32[512,128]{1,0:T(8,128)} %get-tuple-element.55), channel_id=1, source_target_pairs={{0,12},{4,8},{8,4},{12,0},{16,28},{20,24},{24,20},{28,16},{1,13},{... | collective-permute-start | bytes 786440 | tf_op jit(solution)/shard_map/ppermute | solution.py:447
  20.3 5.6 %shard_map.95 = (f32[32,128]{1,0:T(8,128)S(1)}, f32[1,128]{1,0:T(1,128)S(1)}, f32[1024,4096]{1,0:T(8,128)S(1)}) custom-call(f32[1024,4096]{1,0:T(8,128)} %rinv_ref.1, f32[8,16,128]{2,1,0:T(8,128)S(1)} %all-to-all-done.parts_ref), custom_call_target="tpu_custom_call" | custom-call | tf_op jit(solution)/shard_map/pallas_call | solution.py:489
  26.0 1.2 %collective-permute-done.4 = f32[32,128]{1,0:T(8,128)S(1)} collective-permute-done((f32[32,128]{1,0:T(8,128)S(1)}, f32[32,128]{1,0:T(8,128)S(1)}, u32[]{:S(2)}, u32[]{:S(2)}) %collective-permute-start.4) | collective-permute-done | bytes 16416 | tf_op jit(solution)/shard_map/ppermute | solution.py:31
  27.1 1.5 %collective-permute-start.5 = (f32[32,128]{1,0:T(8,128)S(1)}, f32[32,128]{1,0:T(8,128)S(1)}, u32[]{:S(2)}, u32[]{:S(2)}) collective-permute-start(f32[32,128]{1,0:T(8,128)S(1)} %add.6.refs_0_), channel_id=1, source_target_pairs={{0,2},{1,3},{2,0},{3,1},{4,6},{5,7},{6,4},{7,5},{8,10},{9,11},{10,... | collective-permute-start | bytes 49160 | tf_op jit(solution)/shard_map/ppermute | solution.py:31
  28.6 1.7 %collective-permute-start.8 = (f32[512,128]{1,0:T(8,128)S(1)}, f32[512,128]{1,0:T(8,128)S(1)}, u32[]{:S(2)}, u32[]{:S(2)}) collective-permute-start(f32[512,128]{1,0:T(8,128)S(1)} %copy-done.5), channel_id=1, source_target_pairs={{0,4},{4,0},{8,12},{12,8},{16,20},{20,16},{24,28},{28,24},{1,5},{5... | collective-permute-start | bytes 786440 | tf_op jit(solution)/shard_map/ppermute | solution.py:447
  31.1 1.1 %shard_map.97 = (f32[1,4,128,128]{3,2,1,0:T(8,128)S(1)}, f32[1,4,128,128]{3,2,1,0:T(8,128)S(1)}, f32[1,128]{1,0:T(1,128)S(1)}) custom-call(f32[512,1024]{1,0:T(8,128)S(1)} %copy-done, f32[8,16,128]{2,1,0:T(8,128)S(1)} %all-to-all-done.parts_ref, bf16[8,128,512]{2,1,0:T(8,128)(2,1)S(1)} %shard_map.96.mix_ref, ...), custom_call_target="tpu_custom_call" | custom-call | tf_op jit(solution)/shard_map/pallas_call | solution.py:61
  32.2 0.9 %collective-permute-start.3 = (f32[1,4,128,128]{3,2,1,0:T(8,128)S(1)}, f32[1,4,128,128]{3,2,1,0:T(8,128)S(1)}, u32[]{:S(2)}, u32[]{:S(2)}) collective-permute-start(f32[1,4,128,128]{3,2,1,0:T(8,128)S(1)} %get-tuple-element.57), channel_id=1, source_target_pairs={{0,16},{4,20},{8,24},{12,28},{16,0},{20,4},{24,8},{28,12},{1,17},{... | collective-permute-start | bytes 786440 | tf_op jit(solution)/shard_map/ppermute | solution.py:447
  33.1 1.2 %collective-permute-start.10 = (f32[512,128]{1,0:T(8,128)S(1)}, f32[512,128]{1,0:T(8,128)S(1)}, u32[]{:S(2)}, u32[]{:S(2)}) collective-permute-start(f32[512,128]{1,0:T(8,128)S(1)} %copy-done.3), channel_id=1, source_target_pairs={{0,12},{4,8},{8,4},{12,0},{16,28},{20,24},{24,20},{28,16},{1,13},{... | collective-permute-start | bytes 786440 | tf_op jit(solution)/shard_map/ppermute | solution.py:447
  34.3 1.7 %shard_map.99 = (f32[4,128]{1,0:T(4,128)S(1)}, f32[8,128]{1,0:T(8,128)S(1)}, f32[1,128]{1,0:T(1,128)S(1)}, f32[32,128]{1,0:T(8,128)S(1)}) custom-call(f32[1024,4096]{1,0:T(8,128)S(1)} %get-tuple-element.47.rinv_ref, f32[512,1024]{1,0:T(8,128)S(1)} %copy-done, f32[1,128]{1,0:T(1,128)S(1)} %get-tuple-element.58.token_ref, f32[32,128]{1,0:T(8,128)S(1)} %add.6.refs_0_, ...), custom_call_target="tpu_custom_call" | custom-call | tf_op jit(solution)/shard_map/pallas_call | solution.py:61
  36.1 1.1 %collective-permute-done.6 = f32[4,128]{1,0:T(4,128)S(1)} collective-permute-done((f32[4,128]{1,0:T(4,128)S(1)}, f32[4,128]{1,0:T(4,128)S(1)}, u32[]{:S(2)}, u32[]{:S(2)}) %collective-permute-start.6) | collective-permute-done | bytes 2080 | tf_op jit(solution)/shard_map/ppermute | solution.py:31
  37.2 1.4 %collective-permute-start.7 = (f32[4,128]{1,0:T(4,128)S(1)}, f32[4,128]{1,0:T(4,128)S(1)}, u32[]{:S(2)}, u32[]{:S(2)}) collective-permute-start(f32[4,128]{1,0:T(4,128)S(1)} %add.7.refs_0_), channel_id=1, source_target_pairs={{0,2},{1,3},{2,0},{3,1},{4,6},{5,7},{6,4},{7,5},{8,10},{9,11},{10,... | collective-permute-start | bytes 6152 | tf_op jit(solution)/shard_map/ppermute | solution.py:31
  38.6 2.2 %collective-permute-done.7.refs_1_ = f32[4,128]{1,0:T(4,128)S(1)} collective-permute-done((f32[4,128]{1,0:T(4,128)S(1)}, f32[4,128]{1,0:T(4,128)S(1)}, u32[]{:S(2)}, u32[]{:S(2)}) %collective-permute-start.7) | collective-permute-done | bytes 2080 | tf_op jit(solution)/shard_map/ppermute | solution.py:31
  41.1 11.6 %all_to_all.15.parts_ref = f32[8,16,128]{2,1,0:T(8,128)S(1)} all-to-all(f32[8,16,128]{2,1,0:T(8,128)S(1)} %get-tuple-element.62), channel_id=1, replica_groups=mesh['row'=8,'col'=4] {'row'}, dimensions={0} | all-to-all | bytes 131072 | tf_op jit(solution)/shard_map/all_to_all | solution.py:24
  52.6 1.4 %shard_map.101 = (f32[32,128]{1,0:T(8,128)S(1)}, f32[1,128]{1,0:T(1,128)S(1)}) custom-call(f32[1024,4096]{1,0:T(8,128)S(1)} %get-tuple-element.47.rinv_ref, f32[8,16,128]{2,1,0:T(8,128)S(1)} %all_to_all.15.parts_ref), custom_call_target="tpu_custom_call" | custom-call | tf_op jit(solution)/shard_map/pallas_call | solution.py:489
  54.1 1.1 %shard_map.103 = (f32[1,4,128,128]{3,2,1,0:T(8,128)S(1)}, f32[1,4,128,128]{3,2,1,0:T(8,128)S(1)}, f32[1,128]{1,0:T(1,128)S(1)}) custom-call(f32[512,1024]{1,0:T(8,128)S(1)} %copy-done, f32[8,16,128]{2,1,0:T(8,128)S(1)} %all-to-all-done.parts_ref, bf16[8,128,512]{2,1,0:T(8,128)(2,1)S(1)} %shard_map.96.mix_ref, f32[1,128]{1,0:T(1,128)S(1)} %get-tuple-element.64.order_ref, ...), custom_call_target="tpu_custom_call" | custom-call | tf_op jit(solution)/shard_map/pallas_call | solution.py:61
  55.8 1.1 %collective-permute-start.12 = (f32[32,128]{1,0:T(8,128)S(1)}, f32[32,128]{1,0:T(8,128)S(1)}, u32[]{:S(2)}, u32[]{:S(2)}) collective-permute-start(f32[32,128]{1,0:T(8,128)S(1)} %get-tuple-element.70.refs_0_), channel_id=1, source_target_pairs={{0,2},{1,3},{2,0},{3,1},{4,6},{5,7},{6,4},{7,5},{8,10},{9,11},{10,... | collective-permute-start | bytes 49160 | tf_op jit(solution)/shard_map/ppermute | solution.py:41
  56.9 0.8 collective-permute-start.11
  57.6 1.3 %collective-permute-done.13.refs_3_ = f32[32,128]{1,0:T(8,128)S(1)} collective-permute-done((f32[32,128]{1,0:T(8,128)S(1)}, f32[32,128]{1,0:T(8,128)S(1)}, u32[]{:S(2)}, u32[]{:S(2)}) %collective-permute-start.13) | collective-permute-done | bytes 16416 | tf_op jit(solution)/shard_map/ppermute | solution.py:41
  59.6 1.7 %shard_map.104 = (f32[4,128]{1,0:T(4,128)S(1)}, f32[8,128]{1,0:T(8,128)S(1)}, f32[1,128]{1,0:T(1,128)S(1)}) custom-call(f32[1024,4096]{1,0:T(8,128)S(1)} %get-tuple-element.47.rinv_ref, f32[512,1024]{1,0:T(8,128)S(1)} %copy-done, f32[1,128]{1,0:T(1,128)S(1)} %get-tuple-element.69.token_ref, f32[32,128]{1,0:T(8,128)S(1)} %get-tuple-element.70.refs_0_, ...), custom_call_target="tpu_custom_call" | custom-call | tf_op jit(solution)/shard_map/pallas_call | solution.py:61
  61.3 0.9 %collective-permute-start.16 = (f32[4,128]{1,0:T(4,128)S(1)}, f32[4,128]{1,0:T(4,128)S(1)}, u32[]{:S(2)}, u32[]{:S(2)}) collective-permute-start(f32[4,128]{1,0:T(4,128)S(1)} %get-tuple-element.72.refs_0_), channel_id=1, source_target_pairs={{0,3},{1,2},{2,1},{3,0},{4,7},{5,6},{6,5},{7,4},{8,11},{9,10},{10,... | collective-permute-start | bytes 6152 | tf_op jit(solution)/shard_map/ppermute | solution.py:41
  62.2 0.9 %collective-permute-start.15 = (f32[4,128]{1,0:T(4,128)S(1)}, f32[4,128]{1,0:T(4,128)S(1)}, u32[]{:S(2)}, u32[]{:S(2)}) collective-permute-start(f32[4,128]{1,0:T(4,128)S(1)} %get-tuple-element.72.refs_0_), channel_id=1, source_target_pairs={{0,2},{1,3},{2,0},{3,1},{4,6},{5,7},{6,4},{7,5},{8,10},{9,11},{10,... | collective-permute-start | bytes 6152 | tf_op jit(solution)/shard_map/ppermute | solution.py:41
  63.3 1.1 %collective-permute-done.16.refs_3_ = f32[4,128]{1,0:T(4,128)S(1)} collective-permute-done((f32[4,128]{1,0:T(4,128)S(1)}, f32[4,128]{1,0:T(4,128)S(1)}, u32[]{:S(2)}, u32[]{:S(2)}) %collective-permute-start.16) | collective-permute-done | bytes 2080 | tf_op jit(solution)/shard_map/ppermute | solution.py:41
  64.4 1.4 %collective-permute-done.15.refs_2_ = f32[4,128]{1,0:T(4,128)S(1)} collective-permute-done((f32[4,128]{1,0:T(4,128)S(1)}, f32[4,128]{1,0:T(4,128)S(1)}, u32[]{:S(2)}, u32[]{:S(2)}) %collective-permute-start.15) | collective-permute-done | bytes 2080 | tf_op jit(solution)/shard_map/ppermute | solution.py:41
  65.9 1.7 %collective-permute-done.17.refs_2_ = f32[1,4,128,128]{3,2,1,0:T(8,128)S(1)} collective-permute-done((f32[1,4,128,128]{3,2,1,0:T(8,128)S(1)}, f32[1,4,128,128]{3,2,1,0:T(8,128)S(1)}, u32[]{:S(2)}, u32[]{:S(2)}) %collective-permute-start.17) | collective-permute-done | bytes 262176 | tf_op jit(solution)/shard_map/ppermute | solution.py:447
  67.6 0.9 %collective-permute-start.18 = (f32[128,256]{1,0:T(8,128)S(1)}, f32[128,256]{1,0:T(8,128)S(1)}, u32[]{:S(2)}, u32[]{:S(2)}) collective-permute-start(f32[128,256]{1,0:T(8,128)S(1)} %get-tuple-element.83), channel_id=1, source_target_pairs={{0,4},{4,0},{8,12},{12,8},{16,20},{20,16},{24,28},{28,24},{1,5},{5... | collective-permute-start | bytes 393224 | tf_op jit(solution)/shard_map/ppermute | solution.py:447
  68.5 2.6 %collective-permute-start.20 = (f32[128,256]{1,0:T(8,128)S(1)}, f32[128,256]{1,0:T(8,128)S(1)}, u32[]{:S(2)}, u32[]{:S(2)}) collective-permute-start(f32[128,256]{1,0:T(8,128)S(1)} %get-tuple-element.85), channel_id=1, source_target_pairs={{0,12},{4,8},{8,4},{12,0},{16,28},{20,24},{24,20},{28,16},{1,13},{... | collective-permute-start | bytes 393224 | tf_op jit(solution)/shard_map/ppermute | solution.py:447
  71.2 9.0 %all_to_all.16.parts_ref = f32[8,8,128]{2,1,0:T(8,128)S(1)} all-to-all(f32[8,8,128]{2,1,0:T(8,128)S(1)} %get-tuple-element.75), channel_id=1, replica_groups=mesh['row'=8,'col'=4] {'row'}, dimensions={0} | all-to-all | bytes 65536 | tf_op jit(solution)/shard_map/all_to_all | solution.py:24
  80.2 0.9 %shard_map.107 = (f32[4,128]{1,0:T(4,128)}, f32[8,128]{1,0:T(8,128)}, f32[128,1024]{1,0:T(8,128)}) custom-call(f32[8,8,128]{2,1,0:T(8,128)S(1)} %all_to_all.16.parts_ref, f32[4,128]{1,0:T(4,128)S(1)} %get-tuple-element.76.refs_3_.left_ref, f32[1,128]{1,0:T(1,128)S(1)} %get-tuple-element.48.order_ref.refs_3_.refs_0_, ...), custom_call_target="tpu_custom_call" | custom-call | tf_op jit(solution)/shard_map/pallas_call | solution.py:61
  (42 shorter events, 2.8 us)
Async XLA Ops:
  0.6 29.9 %copy-start.1 = (bf16[256,256]{1,0:T(8,128)(2,1)S(1)}, bf16[256,256]{1,0:T(8,128)(2,1)}, u32[]{:S(2)}) copy-start(bf16[256,256]{1,0:T(8,128)(2,1)} %constant.2.clone.walsh_ref) | copy-start | bytes 393220
  0.6 30.4 %copy-start = (f32[512,1024]{1,0:T(8,128)S(1)}, f32[512,1024]{1,0:T(8,128)}, u32[]{:S(2)}) copy-start(f32[512,1024]{1,0:T(8,128)} %design_ref.9) | copy-start | bytes 6291460
  4.0 24.6 %copy-start.5 = (f32[512,128]{1,0:T(8,128)S(1)}, f32[512,128]{1,0:T(8,128)}, u32[]{:S(2)}) copy-start(f32[512,128]{1,0:T(8,128)} %get-tuple-element.65) | copy-start | bytes 786436
  4.0 26.3 %copy-start.4 = (f32[512,128]{1,0:T(8,128)S(1)}, f32[512,128]{1,0:T(8,128)}, u32[]{:S(2)}) copy-start(f32[512,128]{1,0:T(8,128)} %get-tuple-element.66) | copy-start | bytes 786436
  4.1 29.1 %copy-start.3 = (f32[512,128]{1,0:T(8,128)S(1)}, f32[512,128]{1,0:T(8,128)}, u32[]{:S(2)}) copy-start(f32[512,128]{1,0:T(8,128)} %get-tuple-element.68) | copy-start | bytes 786436
  4.1 14.4 %all-to-all-start = ((f32[8,16,128]{2,1,0:T(8,128)}), f32[8,16,128]{2,1,0:T(8,128)S(1)}, u32[]{:S(2)}, u32[]{:S(2)}) async-start(f32[8,16,128]{2,1,0:T(8,128)} %get-tuple-element.46), calls=%async_computation | async-start | bytes 131072 | tf_op jit(solution)/shard_map/all_to_all | solution.py:24
  11.5 14.4 %collective-permute-start = (f32[512,128]{1,0:T(8,128)}, f32[512,128]{1,0:T(8,128)S(1)}, u32[]{:S(2)}, u32[]{:S(2)}) collective-permute-start(f32[512,128]{1,0:T(8,128)} %get-tuple-element.49), channel_id=1, source_target_pairs={{0,4},{4,0},{8,12},{12,8},{16,20},{20,16},{24,28},{28,24},{1,5},{5... | collective-permute-start | bytes 786440 | tf_op jit(solution)/shard_map/ppermute | solution.py:447
  18.5 22.3 %copy-start.2 = (f32[512]{0:T(512)S(1)}, f32[512]{0:T(512)}, u32[]{:S(2)}) copy-start(f32[512]{0:T(512)} %param.11) | copy-start | bytes 6148
  18.5 12.6 %collective-permute-start.1 = (f32[512,128]{1,0:T(8,128)}, f32[512,128]{1,0:T(8,128)S(1)}, u32[]{:S(2)}, u32[]{:S(2)}) collective-permute-start(f32[512,128]{1,0:T(8,128)} %get-tuple-element.54), channel_id=1, source_target_pairs={{0,8},{4,12},{8,0},{12,4},{16,24},{20,28},{24,16},{28,20},{1,9},{5... | collective-permute-start | bytes 786440 | tf_op jit(solution)/shard_map/ppermute | solution.py:447
  18.7 12.4 %collective-permute-start.2 = (f32[512,128]{1,0:T(8,128)}, f32[512,128]{1,0:T(8,128)S(1)}, u32[]{:S(2)}, u32[]{:S(2)}) collective-permute-start(f32[512,128]{1,0:T(8,128)} %get-tuple-element.55), channel_id=1, source_target_pairs={{0,12},{4,8},{8,4},{12,0},{16,28},{20,24},{24,20},{28,16},{1,13},{... | collective-permute-start | bytes 786440 | tf_op jit(solution)/shard_map/ppermute | solution.py:447
  25.9 1.2 %collective-permute-start.4 = (f32[32,128]{1,0:T(8,128)S(1)}, f32[32,128]{1,0:T(8,128)S(1)}, u32[]{:S(2)}, u32[]{:S(2)}) collective-permute-start(f32[32,128]{1,0:T(8,128)S(1)} %shard_map.98), channel_id=1, source_target_pairs={{0,1},{1,0},{2,3},{3,2},{4,5},{5,4},{6,7},{7,6},{8,9},{9,8},{10,11... | collective-permute-start | bytes 49160 | tf_op jit(solution)/shard_map/ppermute | solution.py:31
  27.1 6.0 %collective-permute-start.5 = (f32[32,128]{1,0:T(8,128)S(1)}, f32[32,128]{1,0:T(8,128)S(1)}, u32[]{:S(2)}, u32[]{:S(2)}) collective-permute-start(f32[32,128]{1,0:T(8,128)S(1)} %add.6.refs_0_), channel_id=1, source_target_pairs={{0,2},{1,3},{2,0},{3,1},{4,6},{5,7},{6,4},{7,5},{8,10},{9,11},{10,... | collective-permute-start | bytes 49160 | tf_op jit(solution)/shard_map/ppermute | solution.py:31
  28.6 25.5 %collective-permute-start.8 = (f32[512,128]{1,0:T(8,128)S(1)}, f32[512,128]{1,0:T(8,128)S(1)}, u32[]{:S(2)}, u32[]{:S(2)}) collective-permute-start(f32[512,128]{1,0:T(8,128)S(1)} %copy-done.5), channel_id=1, source_target_pairs={{0,4},{4,0},{8,12},{12,8},{16,20},{20,16},{24,28},{28,24},{1,5},{5... | collective-permute-start | bytes 786440 | tf_op jit(solution)/shard_map/ppermute | solution.py:447
  30.4 23.8 %collective-permute-start.9 = (f32[512,128]{1,0:T(8,128)S(1)}, f32[512,128]{1,0:T(8,128)S(1)}, u32[]{:S(2)}, u32[]{:S(2)}) collective-permute-start(f32[512,128]{1,0:T(8,128)S(1)} %copy-done.4), channel_id=1, source_target_pairs={{0,8},{4,12},{8,0},{12,4},{16,24},{20,28},{24,16},{28,20},{1,9},{5... | collective-permute-start | bytes 786440 | tf_op jit(solution)/shard_map/ppermute | solution.py:447
  32.2 21.9 %collective-permute-start.3 = (f32[1,4,128,128]{3,2,1,0:T(8,128)S(1)}, f32[1,4,128,128]{3,2,1,0:T(8,128)S(1)}, u32[]{:S(2)}, u32[]{:S(2)}) collective-permute-start(f32[1,4,128,128]{3,2,1,0:T(8,128)S(1)} %get-tuple-element.57), channel_id=1, source_target_pairs={{0,16},{4,20},{8,24},{12,28},{16,0},{20,4},{24,8},{28,12},{1,17},{... | collective-permute-start | bytes 786440 | tf_op jit(solution)/shard_map/ppermute | solution.py:447
  33.1 21.0 %collective-permute-start.10 = (f32[512,128]{1,0:T(8,128)S(1)}, f32[512,128]{1,0:T(8,128)S(1)}, u32[]{:S(2)}, u32[]{:S(2)}) collective-permute-start(f32[512,128]{1,0:T(8,128)S(1)} %copy-done.3), channel_id=1, source_target_pairs={{0,12},{4,8},{8,4},{12,0},{16,28},{20,24},{24,20},{28,16},{1,13},{... | collective-permute-start | bytes 786440 | tf_op jit(solution)/shard_map/ppermute | solution.py:447
  36.0 1.2 %collective-permute-start.6 = (f32[4,128]{1,0:T(4,128)S(1)}, f32[4,128]{1,0:T(4,128)S(1)}, u32[]{:S(2)}, u32[]{:S(2)}) collective-permute-start(f32[4,128]{1,0:T(4,128)S(1)} %get-tuple-element.60), channel_id=1, source_target_pairs={{0,1},{1,0},{2,3},{3,2},{4,5},{5,4},{6,7},{7,6},{8,9},{9,8},{10,11... | collective-permute-start | bytes 6152 | tf_op jit(solution)/shard_map/ppermute | solution.py:31
  37.2 3.6 %collective-permute-start.7 = (f32[4,128]{1,0:T(4,128)S(1)}, f32[4,128]{1,0:T(4,128)S(1)}, u32[]{:S(2)}, u32[]{:S(2)}) collective-permute-start(f32[4,128]{1,0:T(4,128)S(1)} %add.7.refs_0_), channel_id=1, source_target_pairs={{0,2},{1,3},{2,0},{3,1},{4,6},{5,7},{6,4},{7,5},{8,10},{9,11},{10,... | collective-permute-start | bytes 6152 | tf_op jit(solution)/shard_map/ppermute | solution.py:31
  55.2 12.3 %collective-permute-start.17 = (f32[1,4,128,128]{3,2,1,0:T(8,128)S(1)}, f32[1,4,128,128]{3,2,1,0:T(8,128)S(1)}, u32[]{:S(2)}, u32[]{:S(2)}) collective-permute-start(f32[1,4,128,128]{3,2,1,0:T(8,128)S(1)} %get-tuple-element.81), channel_id=1, source_target_pairs={{0,16},{4,20},{8,24},{12,28},{16,0},{20,4},{24,8},{28,12},{1,17},{... | collective-permute-start | bytes 786440 | tf_op jit(solution)/shard_map/ppermute | solution.py:447
  55.8 3.2 %collective-permute-start.13 = (f32[32,128]{1,0:T(8,128)S(1)}, f32[32,128]{1,0:T(8,128)S(1)}, u32[]{:S(2)}, u32[]{:S(2)}) collective-permute-start(f32[32,128]{1,0:T(8,128)S(1)} %get-tuple-element.70.refs_0_), channel_id=1, source_target_pairs={{0,3},{1,2},{2,1},{3,0},{4,7},{5,6},{6,5},{7,4},{8,11},{9,10},{10,... | collective-permute-start | bytes 49160 | tf_op jit(solution)/shard_map/ppermute | solution.py:41
  55.8 3.8 %collective-permute-start.12 = (f32[32,128]{1,0:T(8,128)S(1)}, f32[32,128]{1,0:T(8,128)S(1)}, u32[]{:S(2)}, u32[]{:S(2)}) collective-permute-start(f32[32,128]{1,0:T(8,128)S(1)} %get-tuple-element.70.refs_0_), channel_id=1, source_target_pairs={{0,2},{1,3},{2,0},{3,1},{4,6},{5,7},{6,4},{7,5},{8,10},{9,11},{10,... | collective-permute-start | bytes 49160 | tf_op jit(solution)/shard_map/ppermute | solution.py:41
  56.9 2.7 %collective-permute-start.11 = (f32[32,128]{1,0:T(8,128)S(1)}, f32[32,128]{1,0:T(8,128)S(1)}, u32[]{:S(2)}, u32[]{:S(2)}) collective-permute-start(f32[32,128]{1,0:T(8,128)S(1)} %get-tuple-element.70.refs_0_), channel_id=1, source_target_pairs={{0,1},{1,0},{2,3},{3,2},{4,5},{5,4},{6,7},{7,6},{8,9},{9,8},{10,11... | collective-permute-start | bytes 49160 | tf_op jit(solution)/shard_map/ppermute | solution.py:41
  61.3 3.1 %collective-permute-start.16 = (f32[4,128]{1,0:T(4,128)S(1)}, f32[4,128]{1,0:T(4,128)S(1)}, u32[]{:S(2)}, u32[]{:S(2)}) collective-permute-start(f32[4,128]{1,0:T(4,128)S(1)} %get-tuple-element.72.refs_0_), channel_id=1, source_target_pairs={{0,3},{1,2},{2,1},{3,0},{4,7},{5,6},{6,5},{7,4},{8,11},{9,10},{10,... | collective-permute-start | bytes 6152 | tf_op jit(solution)/shard_map/ppermute | solution.py:41
  62.2 3.6 %collective-permute-start.15 = (f32[4,128]{1,0:T(4,128)S(1)}, f32[4,128]{1,0:T(4,128)S(1)}, u32[]{:S(2)}, u32[]{:S(2)}) collective-permute-start(f32[4,128]{1,0:T(4,128)S(1)} %get-tuple-element.72.refs_0_), channel_id=1, source_target_pairs={{0,2},{1,3},{2,0},{3,1},{4,6},{5,7},{6,4},{7,5},{8,10},{9,11},{10,... | collective-permute-start | bytes 6152 | tf_op jit(solution)/shard_map/ppermute | solution.py:41
  63.1 2.7 %collective-permute-start.14 = (f32[4,128]{1,0:T(4,128)S(1)}, f32[4,128]{1,0:T(4,128)S(1)}, u32[]{:S(2)}, u32[]{:S(2)}) collective-permute-start(f32[4,128]{1,0:T(4,128)S(1)} %get-tuple-element.72.refs_0_), channel_id=1, source_target_pairs={{0,1},{1,0},{2,3},{3,2},{4,5},{5,4},{6,7},{7,6},{8,9},{9,8},{10,11... | collective-permute-start | bytes 6152 | tf_op jit(solution)/shard_map/ppermute | solution.py:41
  67.6 12.6 %collective-permute-start.18 = (f32[128,256]{1,0:T(8,128)S(1)}, f32[128,256]{1,0:T(8,128)S(1)}, u32[]{:S(2)}, u32[]{:S(2)}) collective-permute-start(f32[128,256]{1,0:T(8,128)S(1)} %get-tuple-element.83), channel_id=1, source_target_pairs={{0,4},{4,0},{8,12},{12,8},{16,20},{20,16},{24,28},{28,24},{1,5},{5... | collective-permute-start | bytes 393224 | tf_op jit(solution)/shard_map/ppermute | solution.py:447
  68.5 11.7 %collective-permute-start.19 = (f32[128,256]{1,0:T(8,128)S(1)}, f32[128,256]{1,0:T(8,128)S(1)}, u32[]{:S(2)}, u32[]{:S(2)}) collective-permute-start(f32[128,256]{1,0:T(8,128)S(1)} %get-tuple-element.84), channel_id=1, source_target_pairs={{0,8},{4,12},{8,0},{12,4},{16,24},{20,28},{24,16},{28,20},{1,9},{5... | collective-permute-start | bytes 393224 | tf_op jit(solution)/shard_map/ppermute | solution.py:447
  68.5 11.7 %collective-permute-start.20 = (f32[128,256]{1,0:T(8,128)S(1)}, f32[128,256]{1,0:T(8,128)S(1)}, u32[]{:S(2)}, u32[]{:S(2)}) collective-permute-start(f32[128,256]{1,0:T(8,128)S(1)} %get-tuple-element.85), channel_id=1, source_target_pairs={{0,12},{4,8},{8,4},{12,0},{16,28},{20,24},{24,20},{28,16},{1,13},{... | collective-permute-start | bytes 393224 | tf_op jit(solution)/shard_map/ppermute | solution.py:447

commit v17 on v16

--- a/solution.py
+++ b/solution.py
@@ -313,7 +313,7 @@
 
 def sample_body(scale, start, design_ref, parts_ref, mix_ref, order_ref, *refs):
     near, (keep_ref, send_ref, token_ref, both) = refs[: NEAR - 1], refs[NEAR - 1 :]
-    token_ref[...] = order_ref[:1, :]
+    token_ref[...] = first_row(order_ref)
     rows, piece = near[-1].shape
     width = design_ref.shape[1]
     groups = mix_ref.shape[0]
@@ -355,8 +355,12 @@
     send_ref[...] = kept_ref[half:] + arrived_ref[half:]
 
 
+def first_row(ref):
+    return ref[:1, :] if len(ref.shape) == 2 else ref[0, :1, :]
+
+
 def join_body(kept_ref, arrived_ref, order_ref, out_ref, token_ref):
-    token_ref[...] = order_ref[:1, :]
+    token_ref[...] = first_row(order_ref)
     out_ref[...] = kept_ref[0] + arrived_ref[0]
 
 
@@ -519,10 +523,10 @@
         )
 
     betas, alphas, held, joined, right = [], [], [], [], []
-    near = spread(range(1), None)
+    near = spread(range(NEAR - 2), None)
     message = picked = exchange(message, "row")
     late = len(sent) - (chunks > 1)
-    near += spread(range(1, late), message)
+    near += spread(range(NEAR - 2, late), message)
     for step in range(ITERS):
         last = step + 1 == ITERS
         if step == 0:
@@ -530,16 +534,16 @@
             term = pl.pallas_call(
                 pass_body,
                 out_shape=shape(*term.shape),
-                in_specs=[ANY, VMEM],
+                in_specs=[ANY] * (NEAR - 2) + [VMEM],
                 out_specs=VMEM,
                 compiler_params=pltpu.CompilerParams(vmem_limit_bytes=2 << 20),
-            )(near[0], term)
+            )(*near[: NEAR - 2], term)
             mixed = mix(message)
         else:
             term, beta = back(here, message, False)
             token = beta
             if chunks > 1:
-                part, token = join(keep, come, beta)
+                part, token = join(keep, come, message)
                 joined.append(part)
                 keep, send, token = sample(1, mixed, token)
                 come = swap(send, row_groups // 2)

time: 81.5 us -> 80.9 us (level)
  waiting for transfers between devices: 15.7 us -> 13.7 us
  blocking collectives: 20.6 us -> 22.5 us
    all_to_all x2, blocking collectives: 20.6 us -> 22.5 us  [exchange(): return lax.all_to_all(copies, axis, split_axis=0, concat_axis=0, tiled=True)]
    ppermute x11, waiting for transfers between devices: 1.71 us -> 0.52 us  [swap(): lax.ppermute(array, 'row', [(i, i ^ mask) for i in range(row_groups)])]
    all_to_all x1, waiting for transfers between devices: 4.99 us -> 3.84 us  [exchange(): return lax.all_to_all(copies, axis, split_axis=0, concat_axis=0, tiled=True)]
where the time goes in v17:
time: 80.9 us; the launch traced here: 80.5 us
  starting transfers between devices  25.6 us (32%)
  blocking collectives  22.5 us (28%)
  Pallas kernels  17.8 us (22%)
  waiting for transfers between devices  13.7 us (17%)
  between operations  0.84 us (1%)
    all_to_all x2, blocking collectives, exchange(): return lax.all_to_all(copies, axis, split_axis=0, concat_axis=0, tiled=True)  22.5 us
    ppermute x11, starting transfers between devices, swap(): lax.ppermute(array, 'row', [(i, i ^ mask) for i in range(row_groups)])  12 us
    pallas_call x10, Pallas kernels, call(): pl.pallas_call(body, out_shape=out_shape, in_specs=[VMEM] * len(operands)...  7.46 us
    all_to_all x1, starting transfers between devices, exchange(): return lax.all_to_all(copies, axis, split_axis=0, concat_axis=0, tiled=True)  7.42 us
    pallas_call x2, Pallas kernels, back(): pl.pallas_call(functools.partial(back_body, first), out_shape=outs, in_sp...  6.99 us
    ppermute x4, waiting for transfers between devices, paired(): come = lax.ppermute(array, axis, [(i, i ^ mask) for i in range(size)])  5.19 us
    ppermute x6, waiting for transfers between devices, direct(): lax.ppermute(array, axis, [(i, i ^ mask) for i in range(size)])  4.2 us
    ppermute x6, starting transfers between devices, direct(): lax.ppermute(array, axis, [(i, i ^ mask) for i in range(size)])  3.85 us
  transfers between devices with their start and end apart: 22, of which 9 were waited for; matrix products, arithmetic and copies ran while one was open for 0% of the time, Pallas kernels for 15%

profile of v17, /device:TPU:0, one launch (start us, length us, event | category | flops | bytes accessed | tf_op | source)
XLA Modules:
  0.0 80.5 jit_solution(15738978155923843651)
XLA Ops:
  0.7 3.4 %shard_map.94 = (f32[8,16,128]{2,1,0:T(8,128)}, f32[512,128]{1,0:T(8,128)}, f32[512,128]{1,0:T(8,128)}, f32[512,128]{1,0:T(8,128)}, f32[512,128]{1,0:T(8,128)}, /*index=5*/f32[512,128]{1,0:T(8,128)}, f32[512,128]{1,0:T(8,128)}) custom-call(f32[512,1024]{1,0:T(8,128)} %design_ref.9, f32[4,128]{1,0:T(4,128)} %bitcast.6, s32[4,128]{1,0:T(4,128)} %bitcast.9, ...), custom_call_target="tpu_custom_call" | custom-call | tf_op jit(solution)/shard_map/pallas_call | solution.py:433
  4.1 7.4 %all-to-all-start = ((f32[8,16,128]{2,1,0:T(8,128)}), f32[8,16,128]{2,1,0:T(8,128)S(1)}, u32[]{:S(2)}, u32[]{:S(2)}) async-start(f32[8,16,128]{2,1,0:T(8,128)} %get-tuple-element.45), calls=%async_computation | async-start | bytes 131072 | tf_op jit(solution)/shard_map/all_to_all | solution.py:24
  11.5 2.0 %collective-permute-start = (f32[512,128]{1,0:T(8,128)}, f32[512,128]{1,0:T(8,128)S(1)}, u32[]{:S(2)}, u32[]{:S(2)}) collective-permute-start(f32[512,128]{1,0:T(8,128)} %get-tuple-element.48), channel_id=1, source_target_pairs={{0,4},{4,0},{8,12},{12,8},{16,20},{20,16},{24,28},{28,24},{1,5},{5... | collective-permute-start | bytes 786440 | tf_op jit(solution)/shard_map/ppermute | solution.py:451
  13.5 1.5 %collective-permute-start.1 = (f32[512,128]{1,0:T(8,128)}, f32[512,128]{1,0:T(8,128)S(1)}, u32[]{:S(2)}, u32[]{:S(2)}) collective-permute-start(f32[512,128]{1,0:T(8,128)} %get-tuple-element.49), channel_id=1, source_target_pairs={{0,8},{4,12},{8,0},{12,4},{16,24},{20,28},{24,16},{28,20},{1,9},{5... | collective-permute-start | bytes 786440 | tf_op jit(solution)/shard_map/ppermute | solution.py:451
  15.0 3.8 %all-to-all-done.parts_ref = f32[8,16,128]{2,1,0:T(8,128)S(1)} async-done(((f32[8,16,128]{2,1,0:T(8,128)}), f32[8,16,128]{2,1,0:T(8,128)S(1)}, u32[]{:S(2)}, u32[]{:S(2)}) %all-to-all-start) | async-done | bytes 65568 | tf_op jit(solution)/shard_map/all_to_all | solution.py:24
  18.8 0.7 collective-permute-start.2
  19.5 5.6 %shard_map.95 = (f32[32,128]{1,0:T(8,128)S(1)}, f32[1,128]{1,0:T(1,128)S(1)}, f32[1024,4096]{1,0:T(8,128)S(1)}) custom-call(f32[1024,4096]{1,0:T(8,128)} %rinv_ref.1, f32[8,16,128]{2,1,0:T(8,128)S(1)} %all-to-all-done.parts_ref), custom_call_target="tpu_custom_call" | custom-call | tf_op jit(solution)/shard_map/pallas_call | solution.py:493
  25.2 1.2 %collective-permute-done.4 = f32[32,128]{1,0:T(8,128)S(1)} collective-permute-done((f32[32,128]{1,0:T(8,128)S(1)}, f32[32,128]{1,0:T(8,128)S(1)}, u32[]{:S(2)}, u32[]{:S(2)}) %collective-permute-start.4) | collective-permute-done | bytes 16416 | tf_op jit(solution)/shard_map/ppermute | solution.py:31
  26.4 1.5 %collective-permute-start.5 = (f32[32,128]{1,0:T(8,128)S(1)}, f32[32,128]{1,0:T(8,128)S(1)}, u32[]{:S(2)}, u32[]{:S(2)}) collective-permute-start(f32[32,128]{1,0:T(8,128)S(1)} %add.6.refs_0_), channel_id=1, source_target_pairs={{0,2},{1,3},{2,0},{3,1},{4,6},{5,7},{6,4},{7,5},{8,10},{9,11},{10,... | collective-permute-start | bytes 49160 | tf_op jit(solution)/shard_map/ppermute | solution.py:31
  27.9 0.6 collective-permute-start.8
  28.5 2.1 %collective-permute-start.9 = (f32[512,128]{1,0:T(8,128)S(1)}, f32[512,128]{1,0:T(8,128)S(1)}, u32[]{:S(2)}, u32[]{:S(2)}) collective-permute-start(f32[512,128]{1,0:T(8,128)S(1)} %copy-done.4), channel_id=1, source_target_pairs={{0,8},{4,12},{8,0},{12,4},{16,24},{20,28},{24,16},{28,20},{1,9},{5... | collective-permute-start | bytes 786440 | tf_op jit(solution)/shard_map/ppermute | solution.py:451
  31.2 1.1 %shard_map.97 = (f32[1,4,128,128]{3,2,1,0:T(8,128)S(1)}, f32[1,4,128,128]{3,2,1,0:T(8,128)S(1)}, f32[1,128]{1,0:T(1,128)S(1)}) custom-call(f32[512,1024]{1,0:T(8,128)S(1)} %copy-done, f32[8,16,128]{2,1,0:T(8,128)S(1)} %all-to-all-done.parts_ref, bf16[8,128,512]{2,1,0:T(8,128)(2,1)S(1)} %shard_map.96.mix_ref, ...), custom_call_target="tpu_custom_call" | custom-call | tf_op jit(solution)/shard_map/pallas_call | solution.py:61
  33.2 1.7 %shard_map.99 = (f32[4,128]{1,0:T(4,128)S(1)}, f32[8,128]{1,0:T(8,128)S(1)}, f32[1,128]{1,0:T(1,128)S(1)}, f32[32,128]{1,0:T(8,128)S(1)}) custom-call(f32[1024,4096]{1,0:T(8,128)S(1)} %get-tuple-element.46.rinv_ref, f32[512,1024]{1,0:T(8,128)S(1)} %copy-done, f32[1,128]{1,0:T(1,128)S(1)} %get-tuple-element.56.token_ref, f32[32,128]{1,0:T(8,128)S(1)} %add.6.refs_0_, ...), custom_call_target="tpu_custom_call" | custom-call | tf_op jit(solution)/shard_map/pallas_call | solution.py:61
  35.0 1.1 %collective-permute-done.6 = f32[4,128]{1,0:T(4,128)S(1)} collective-permute-done((f32[4,128]{1,0:T(4,128)S(1)}, f32[4,128]{1,0:T(4,128)S(1)}, u32[]{:S(2)}, u32[]{:S(2)}) %collective-permute-start.6) | collective-permute-done | bytes 2080 | tf_op jit(solution)/shard_map/ppermute | solution.py:31
  36.2 0.7 collective-permute-start.7
  36.9 2.9 %collective-permute-done.7.refs_1_ = f32[4,128]{1,0:T(4,128)S(1)} collective-permute-done((f32[4,128]{1,0:T(4,128)S(1)}, f32[4,128]{1,0:T(4,128)S(1)}, u32[]{:S(2)}, u32[]{:S(2)}) %collective-permute-start.7) | collective-permute-done | bytes 2080 | tf_op jit(solution)/shard_map/ppermute | solution.py:31
  40.0 12.4 %all_to_all.15.order_ref.parts_ref = f32[8,16,128]{2,1,0:T(8,128)S(1)} all-to-all(f32[8,16,128]{2,1,0:T(8,128)S(1)} %get-tuple-element.60), channel_id=1, replica_groups=mesh['row'=8,'col'=4] {'row'}, dimensions={0} | all-to-all | bytes 131072 | tf_op jit(solution)/shard_map/all_to_all | solution.py:24
  52.5 1.1 %shard_map.102 = (f32[1,4,128,128]{3,2,1,0:T(8,128)S(1)}, f32[1,4,128,128]{3,2,1,0:T(8,128)S(1)}, f32[1,128]{1,0:T(1,128)S(1)}) custom-call(f32[512,1024]{1,0:T(8,128)S(1)} %copy-done, f32[8,16,128]{2,1,0:T(8,128)S(1)} %all-to-all-done.parts_ref, bf16[8,128,512]{2,1,0:T(8,128)(2,1)S(1)} %shard_map.96.mix_ref, f32[1,128]{1,0:T(1,128)S(1)} %get-tuple-element.61.order_ref, ...), custom_call_target="tpu_custom_call" | custom-call | tf_op jit(solution)/shard_map/pallas_call | solution.py:61
  54.1 1.4 %shard_map.103 = (f32[32,128]{1,0:T(8,128)S(1)}, f32[1,128]{1,0:T(1,128)S(1)}) custom-call(f32[1024,4096]{1,0:T(8,128)S(1)} %get-tuple-element.46.rinv_ref, f32[8,16,128]{2,1,0:T(8,128)S(1)} %all_to_all.15.order_ref.parts_ref), custom_call_target="tpu_custom_call" | custom-call | tf_op jit(solution)/shard_map/pallas_call | solution.py:493
  55.6 0.6 collective-permute-start.12
  56.2 1.2 %collective-permute-start.11 = (f32[32,128]{1,0:T(8,128)S(1)}, f32[32,128]{1,0:T(8,128)S(1)}, u32[]{:S(2)}, u32[]{:S(2)}) collective-permute-start(f32[32,128]{1,0:T(8,128)S(1)} %get-tuple-element.67.refs_0_), channel_id=1, source_target_pairs={{0,1},{1,0},{2,3},{3,2},{4,5},{5,4},{6,7},{7,6},{8,9},{9,8},{10,11... | collective-permute-start | bytes 49160 | tf_op jit(solution)/shard_map/ppermute | solution.py:41
  57.5 1.3 %collective-permute-done.13.refs_3_ = f32[32,128]{1,0:T(8,128)S(1)} collective-permute-done((f32[32,128]{1,0:T(8,128)S(1)}, f32[32,128]{1,0:T(8,128)S(1)}, u32[]{:S(2)}, u32[]{:S(2)}) %collective-permute-start.13) | collective-permute-done | bytes 16416 | tf_op jit(solution)/shard_map/ppermute | solution.py:41
  58.8 0.7 collective-permute-done.12.refs_2_
  59.4 1.7 %shard_map.104 = (f32[4,128]{1,0:T(4,128)S(1)}, f32[8,128]{1,0:T(8,128)S(1)}, f32[1,128]{1,0:T(1,128)S(1)}) custom-call(f32[1024,4096]{1,0:T(8,128)S(1)} %get-tuple-element.46.rinv_ref, f32[512,1024]{1,0:T(8,128)S(1)} %copy-done, f32[1,128]{1,0:T(1,128)S(1)} %get-tuple-element.66.token_ref, f32[32,128]{1,0:T(8,128)S(1)} %get-tuple-element.67.refs_0_, ...), custom_call_target="tpu_custom_call" | custom-call | tf_op jit(solution)/shard_map/pallas_call | solution.py:61
  61.2 0.6 collective-permute-start.16
  62.3 0.8 collective-permute-start.14
  63.1 1.1 %collective-permute-done.16.refs_3_ = f32[4,128]{1,0:T(4,128)S(1)} collective-permute-done((f32[4,128]{1,0:T(4,128)S(1)}, f32[4,128]{1,0:T(4,128)S(1)}, u32[]{:S(2)}, u32[]{:S(2)}) %collective-permute-start.16) | collective-permute-done | bytes 2080 | tf_op jit(solution)/shard_map/ppermute | solution.py:41
  64.3 1.1 %collective-permute-done.15.refs_2_ = f32[4,128]{1,0:T(4,128)S(1)} collective-permute-done((f32[4,128]{1,0:T(4,128)S(1)}, f32[4,128]{1,0:T(4,128)S(1)}, u32[]{:S(2)}, u32[]{:S(2)}) %collective-permute-start.15) | collective-permute-done | bytes 2080 | tf_op jit(solution)/shard_map/ppermute | solution.py:41
  66.0 0.9 %collective-permute-start.18 = (f32[128,256]{1,0:T(8,128)S(1)}, f32[128,256]{1,0:T(8,128)S(1)}, u32[]{:S(2)}, u32[]{:S(2)}) collective-permute-start(f32[128,256]{1,0:T(8,128)S(1)} %get-tuple-element.81), channel_id=1, source_target_pairs={{0,4},{4,0},{8,12},{12,8},{16,20},{20,16},{24,28},{28,24},{1,5},{5... | collective-permute-start | bytes 393224 | tf_op jit(solution)/shard_map/ppermute | solution.py:451
  67.3 2.2 %collective-permute-start.20 = (f32[128,256]{1,0:T(8,128)S(1)}, f32[128,256]{1,0:T(8,128)S(1)}, u32[]{:S(2)}, u32[]{:S(2)}) collective-permute-start(f32[128,256]{1,0:T(8,128)S(1)} %get-tuple-element.83), channel_id=1, source_target_pairs={{0,12},{4,8},{8,4},{12,0},{16,28},{20,24},{24,20},{28,16},{1,13},{... | collective-permute-start | bytes 393224 | tf_op jit(solution)/shard_map/ppermute | solution.py:451
  69.5 10.1 %all_to_all.16.parts_ref = f32[8,8,128]{2,1,0:T(8,128)S(1)} all-to-all(f32[8,8,128]{2,1,0:T(8,128)S(1)} %get-tuple-element.73), channel_id=1, replica_groups=mesh['row'=8,'col'=4] {'row'}, dimensions={0} | all-to-all | bytes 65536 | tf_op jit(solution)/shard_map/all_to_all | solution.py:24
  79.6 0.9 %shard_map.107 = (f32[4,128]{1,0:T(4,128)}, f32[8,128]{1,0:T(8,128)}, f32[128,1024]{1,0:T(8,128)}) custom-call(f32[8,8,128]{2,1,0:T(8,128)S(1)} %all_to_all.16.parts_ref, f32[4,128]{1,0:T(4,128)S(1)} %get-tuple-element.74.refs_3_.left_ref, f32[1,128]{1,0:T(1,128)S(1)} %get-tuple-element.47.order_ref.refs_3_.refs_0_, ...), custom_call_target="tpu_custom_call" | custom-call | tf_op jit(solution)/shard_map/pallas_call | solution.py:61
  (42 shorter events, 4.1 us)
Async XLA Ops:
  0.6 30.0 %copy-start.1 = (bf16[256,256]{1,0:T(8,128)(2,1)S(1)}, bf16[256,256]{1,0:T(8,128)(2,1)}, u32[]{:S(2)}) copy-start(bf16[256,256]{1,0:T(8,128)(2,1)} %constant.2.clone.walsh_ref) | copy-start | bytes 393220
  0.6 30.5 %copy-start = (f32[512,1024]{1,0:T(8,128)S(1)}, f32[512,1024]{1,0:T(8,128)}, u32[]{:S(2)}) copy-start(f32[512,1024]{1,0:T(8,128)} %design_ref.9) | copy-start | bytes 6291460
  4.0 24.5 %copy-start.4 = (f32[512,128]{1,0:T(8,128)S(1)}, f32[512,128]{1,0:T(8,128)}, u32[]{:S(2)}) copy-start(f32[512,128]{1,0:T(8,128)} %get-tuple-element.63) | copy-start | bytes 786436
  4.0 28.7 %copy-start.3 = (f32[512,128]{1,0:T(8,128)S(1)}, f32[512,128]{1,0:T(8,128)}, u32[]{:S(2)}) copy-start(f32[512,128]{1,0:T(8,128)} %get-tuple-element.65) | copy-start | bytes 786436
  4.1 14.8 %all-to-all-start = ((f32[8,16,128]{2,1,0:T(8,128)}), f32[8,16,128]{2,1,0:T(8,128)S(1)}, u32[]{:S(2)}, u32[]{:S(2)}) async-start(f32[8,16,128]{2,1,0:T(8,128)} %get-tuple-element.45), calls=%async_computation | async-start | bytes 131072 | tf_op jit(solution)/shard_map/all_to_all | solution.py:24
  11.5 13.7 %collective-permute-start = (f32[512,128]{1,0:T(8,128)}, f32[512,128]{1,0:T(8,128)S(1)}, u32[]{:S(2)}, u32[]{:S(2)}) collective-permute-start(f32[512,128]{1,0:T(8,128)} %get-tuple-element.48), channel_id=1, source_target_pairs={{0,4},{4,0},{8,12},{12,8},{16,20},{20,16},{24,28},{28,24},{1,5},{5... | collective-permute-start | bytes 786440 | tf_op jit(solution)/shard_map/ppermute | solution.py:451
  13.5 11.6 %collective-permute-start.1 = (f32[512,128]{1,0:T(8,128)}, f32[512,128]{1,0:T(8,128)S(1)}, u32[]{:S(2)}, u32[]{:S(2)}) collective-permute-start(f32[512,128]{1,0:T(8,128)} %get-tuple-element.49), channel_id=1, source_target_pairs={{0,8},{4,12},{8,0},{12,4},{16,24},{20,28},{24,16},{28,20},{1,9},{5... | collective-permute-start | bytes 786440 | tf_op jit(solution)/shard_map/ppermute | solution.py:451
  18.8 9.1 %copy-start.5 = (f32[512,128]{1,0:T(8,128)S(1)}, f32[512,128]{1,0:T(8,128)}, u32[]{:S(2)}) copy-start(f32[512,128]{1,0:T(8,128)} %get-tuple-element.62) | copy-start | bytes 786436
  18.8 21.0 %copy-start.2 = (f32[512]{0:T(512)S(1)}, f32[512]{0:T(512)}, u32[]{:S(2)}) copy-start(f32[512]{0:T(512)} %param.11) | copy-start | bytes 6148
  18.8 12.4 %collective-permute-start.2 = (f32[512,128]{1,0:T(8,128)}, f32[512,128]{1,0:T(8,128)S(1)}, u32[]{:S(2)}, u32[]{:S(2)}) collective-permute-start(f32[512,128]{1,0:T(8,128)} %get-tuple-element.53), channel_id=1, source_target_pairs={{0,12},{4,8},{8,4},{12,0},{16,28},{20,24},{24,20},{28,16},{1,13},{... | collective-permute-start | bytes 786440 | tf_op jit(solution)/shard_map/ppermute | solution.py:451
  25.2 1.2 %collective-permute-start.4 = (f32[32,128]{1,0:T(8,128)S(1)}, f32[32,128]{1,0:T(8,128)S(1)}, u32[]{:S(2)}, u32[]{:S(2)}) collective-permute-start(f32[32,128]{1,0:T(8,128)S(1)} %shard_map.98), channel_id=1, source_target_pairs={{0,1},{1,0},{2,3},{3,2},{4,5},{5,4},{6,7},{7,6},{8,9},{9,8},{10,11... | collective-permute-start | bytes 49160 | tf_op jit(solution)/shard_map/ppermute | solution.py:31
  26.4 6.3 %collective-permute-start.5 = (f32[32,128]{1,0:T(8,128)S(1)}, f32[32,128]{1,0:T(8,128)S(1)}, u32[]{:S(2)}, u32[]{:S(2)}) collective-permute-start(f32[32,128]{1,0:T(8,128)S(1)} %add.6.refs_0_), channel_id=1, source_target_pairs={{0,2},{1,3},{2,0},{3,1},{4,6},{5,7},{6,4},{7,5},{8,10},{9,11},{10,... | collective-permute-start | bytes 49160 | tf_op jit(solution)/shard_map/ppermute | solution.py:31
  27.9 24.5 %collective-permute-start.8 = (f32[512,128]{1,0:T(8,128)S(1)}, f32[512,128]{1,0:T(8,128)S(1)}, u32[]{:S(2)}, u32[]{:S(2)}) collective-permute-start(f32[512,128]{1,0:T(8,128)S(1)} %copy-done.5), channel_id=1, source_target_pairs={{0,4},{4,0},{8,12},{12,8},{16,20},{20,16},{24,28},{28,24},{1,5},{5... | collective-permute-start | bytes 786440 | tf_op jit(solution)/shard_map/ppermute | solution.py:451
  28.5 23.9 %collective-permute-start.9 = (f32[512,128]{1,0:T(8,128)S(1)}, f32[512,128]{1,0:T(8,128)S(1)}, u32[]{:S(2)}, u32[]{:S(2)}) collective-permute-start(f32[512,128]{1,0:T(8,128)S(1)} %copy-done.4), channel_id=1, source_target_pairs={{0,8},{4,12},{8,0},{12,4},{16,24},{20,28},{24,16},{28,20},{1,9},{5... | collective-permute-start | bytes 786440 | tf_op jit(solution)/shard_map/ppermute | solution.py:451
  32.3 20.1 %collective-permute-start.3 = (f32[1,4,128,128]{3,2,1,0:T(8,128)S(1)}, f32[1,4,128,128]{3,2,1,0:T(8,128)S(1)}, u32[]{:S(2)}, u32[]{:S(2)}) collective-permute-start(f32[1,4,128,128]{3,2,1,0:T(8,128)S(1)} %get-tuple-element.55), channel_id=1, source_target_pairs={{0,16},{4,20},{8,24},{12,28},{16,0},{20,4},{24,8},{28,12},{1,17},{... | collective-permute-start | bytes 786440 | tf_op jit(solution)/shard_map/ppermute | solution.py:451
  32.8 19.7 %collective-permute-start.10 = (f32[512,128]{1,0:T(8,128)S(1)}, f32[512,128]{1,0:T(8,128)S(1)}, u32[]{:S(2)}, u32[]{:S(2)}) collective-permute-start(f32[512,128]{1,0:T(8,128)S(1)} %copy-done.3), channel_id=1, source_target_pairs={{0,12},{4,8},{8,4},{12,0},{16,28},{20,24},{24,20},{28,16},{1,13},{... | collective-permute-start | bytes 786440 | tf_op jit(solution)/shard_map/ppermute | solution.py:451
  34.9 1.2 %collective-permute-start.6 = (f32[4,128]{1,0:T(4,128)S(1)}, f32[4,128]{1,0:T(4,128)S(1)}, u32[]{:S(2)}, u32[]{:S(2)}) collective-permute-start(f32[4,128]{1,0:T(4,128)S(1)} %get-tuple-element.58), channel_id=1, source_target_pairs={{0,1},{1,0},{2,3},{3,2},{4,5},{5,4},{6,7},{7,6},{8,9},{9,8},{10,11... | collective-permute-start | bytes 6152 | tf_op jit(solution)/shard_map/ppermute | solution.py:31
  36.2 3.6 %collective-permute-start.7 = (f32[4,128]{1,0:T(4,128)S(1)}, f32[4,128]{1,0:T(4,128)S(1)}, u32[]{:S(2)}, u32[]{:S(2)}) collective-permute-start(f32[4,128]{1,0:T(4,128)S(1)} %add.7.refs_0_), channel_id=1, source_target_pairs={{0,2},{1,3},{2,0},{3,1},{4,6},{5,7},{6,4},{7,5},{8,10},{9,11},{10,... | collective-permute-start | bytes 6152 | tf_op jit(solution)/shard_map/ppermute | solution.py:31
  53.6 12.3 %collective-permute-start.17 = (f32[1,4,128,128]{3,2,1,0:T(8,128)S(1)}, f32[1,4,128,128]{3,2,1,0:T(8,128)S(1)}, u32[]{:S(2)}, u32[]{:S(2)}) collective-permute-start(f32[1,4,128,128]{3,2,1,0:T(8,128)S(1)} %get-tuple-element.79), channel_id=1, source_target_pairs={{0,16},{4,20},{8,24},{12,28},{16,0},{20,4},{24,8},{28,12},{1,17},{... | collective-permute-start | bytes 786440 | tf_op jit(solution)/shard_map/ppermute | solution.py:451
  55.6 3.2 %collective-permute-start.13 = (f32[32,128]{1,0:T(8,128)S(1)}, f32[32,128]{1,0:T(8,128)S(1)}, u32[]{:S(2)}, u32[]{:S(2)}) collective-permute-start(f32[32,128]{1,0:T(8,128)S(1)} %get-tuple-element.67.refs_0_), channel_id=1, source_target_pairs={{0,3},{1,2},{2,1},{3,0},{4,7},{5,6},{6,5},{7,4},{8,11},{9,10},{10,... | collective-permute-start | bytes 49160 | tf_op jit(solution)/shard_map/ppermute | solution.py:41
  55.6 3.8 %collective-permute-start.12 = (f32[32,128]{1,0:T(8,128)S(1)}, f32[32,128]{1,0:T(8,128)S(1)}, u32[]{:S(2)}, u32[]{:S(2)}) collective-permute-start(f32[32,128]{1,0:T(8,128)S(1)} %get-tuple-element.67.refs_0_), channel_id=1, source_target_pairs={{0,2},{1,3},{2,0},{3,1},{4,6},{5,7},{6,4},{7,5},{8,10},{9,11},{10,... | collective-permute-start | bytes 49160 | tf_op jit(solution)/shard_map/ppermute | solution.py:41
  56.2 3.2 %collective-permute-start.11 = (f32[32,128]{1,0:T(8,128)S(1)}, f32[32,128]{1,0:T(8,128)S(1)}, u32[]{:S(2)}, u32[]{:S(2)}) collective-permute-start(f32[32,128]{1,0:T(8,128)S(1)} %get-tuple-element.67.refs_0_), channel_id=1, source_target_pairs={{0,1},{1,0},{2,3},{3,2},{4,5},{5,4},{6,7},{7,6},{8,9},{9,8},{10,11... | collective-permute-start | bytes 49160 | tf_op jit(solution)/shard_map/ppermute | solution.py:41
  61.2 3.1 %collective-permute-start.16 = (f32[4,128]{1,0:T(4,128)S(1)}, f32[4,128]{1,0:T(4,128)S(1)}, u32[]{:S(2)}, u32[]{:S(2)}) collective-permute-start(f32[4,128]{1,0:T(4,128)S(1)} %get-tuple-element.70.refs_0_), channel_id=1, source_target_pairs={{0,3},{1,2},{2,1},{3,0},{4,7},{5,6},{6,5},{7,4},{8,11},{9,10},{10,... | collective-permute-start | bytes 6152 | tf_op jit(solution)/shard_map/ppermute | solution.py:41
  61.8 3.6 %collective-permute-start.15 = (f32[4,128]{1,0:T(4,128)S(1)}, f32[4,128]{1,0:T(4,128)S(1)}, u32[]{:S(2)}, u32[]{:S(2)}) collective-permute-start(f32[4,128]{1,0:T(4,128)S(1)} %get-tuple-element.70.refs_0_), channel_id=1, source_target_pairs={{0,2},{1,3},{2,0},{3,1},{4,6},{5,7},{6,4},{7,5},{8,10},{9,11},{10,... | collective-permute-start | bytes 6152 | tf_op jit(solution)/shard_map/ppermute | solution.py:41
  62.3 3.0 %collective-permute-start.14 = (f32[4,128]{1,0:T(4,128)S(1)}, f32[4,128]{1,0:T(4,128)S(1)}, u32[]{:S(2)}, u32[]{:S(2)}) collective-permute-start(f32[4,128]{1,0:T(4,128)S(1)} %get-tuple-element.70.refs_0_), channel_id=1, source_target_pairs={{0,1},{1,0},{2,3},{3,2},{4,5},{5,4},{6,7},{7,6},{8,9},{9,8},{10,11... | collective-permute-start | bytes 6152 | tf_op jit(solution)/shard_map/ppermute | solution.py:41
  66.0 13.6 %collective-permute-start.18 = (f32[128,256]{1,0:T(8,128)S(1)}, f32[128,256]{1,0:T(8,128)S(1)}, u32[]{:S(2)}, u32[]{:S(2)}) collective-permute-start(f32[128,256]{1,0:T(8,128)S(1)} %get-tuple-element.81), channel_id=1, source_target_pairs={{0,4},{4,0},{8,12},{12,8},{16,20},{20,16},{24,28},{28,24},{1,5},{5... | collective-permute-start | bytes 393224 | tf_op jit(solution)/shard_map/ppermute | solution.py:451
  66.9 12.7 %collective-permute-start.19 = (f32[128,256]{1,0:T(8,128)S(1)}, f32[128,256]{1,0:T(8,128)S(1)}, u32[]{:S(2)}, u32[]{:S(2)}) collective-permute-start(f32[128,256]{1,0:T(8,128)S(1)} %get-tuple-element.82), channel_id=1, source_target_pairs={{0,8},{4,12},{8,0},{12,4},{16,24},{20,28},{24,16},{28,20},{1,9},{5... | collective-permute-start | bytes 393224 | tf_op jit(solution)/shard_map/ppermute | solution.py:451
  67.3 12.3 %collective-permute-start.20 = (f32[128,256]{1,0:T(8,128)S(1)}, f32[128,256]{1,0:T(8,128)S(1)}, u32[]{:S(2)}, u32[]{:S(2)}) collective-permute-start(f32[128,256]{1,0:T(8,128)S(1)} %get-tuple-element.83), channel_id=1, source_target_pairs={{0,12},{4,8},{8,4},{12,0},{16,28},{20,24},{24,20},{28,16},{1,13},{... | collective-permute-start | bytes 393224 | tf_op jit(solution)/shard_map/ppermute | solution.py:451

commit v18 on v17

--- a/solution.py
+++ b/solution.py
@@ -377,15 +377,18 @@
     refs[-1][...] = refs[-2][...]
 
 
-def last_body(parts_ref, left_ref, *refs):
-    basis_ref, solution_ref, sketch_ref = refs[-3:]
-    quarters = refs[3 * ITERS : 3 * ITERS + NEAR]
+def assemble_body(token_ref, *refs):
+    quarters, sketch_ref = refs[:-1], refs[-1]
     place = lax.axis_index("row") % NEAR
     piece = quarters[0].shape[1]
     for mask, part_ref in enumerate(quarters):
         for tile in range(0, piece, LANE):
             column = pl.multiple_of((place ^ mask) * piece + tile, LANE)
             sketch_ref[:, pl.ds(column, LANE)] = part_ref[:, tile : tile + LANE]
+
+
+def last_body(parts_ref, left_ref, *refs):
+    basis_ref, solution_ref, token_ref = refs[-3:]
     betas = [ref[...] for ref in refs[:ITERS]]
     alphas = [ref[...] for ref in refs[ITERS : 2 * ITERS]]
     held = [ref[...] for ref in refs[2 * ITERS : 3 * ITERS]]
@@ -407,6 +410,7 @@
             search = held[step + 1] - sine * alpha / rho * search
             rhobar = -cosine * alpha
     solution_ref[...] = iterate
+    token_ref[...] = last
 
 
 def shape(*dims, dtype=F32):
@@ -562,17 +566,16 @@
         message = exchange(message, "row")
     quarters = (shape(slots, width // NEAR),) * NEAR
     mine, *others = call(split_body, quarters, *joined, *halve(keep, come, beta), left)
-    basis, answer, sketch = call(
+    basis, answer, token = pl.pallas_call(
         last_body,
-        (shape(lines, LANE), shape(width // LANE, LANE), shape(slots, width)),
-        message,
-        left,
-        *betas,
-        *alphas,
-        *held,
-        mine,
-        *(swap(part, mask + 1) for mask, part in enumerate(others)),
-    )
+        out_shape=(shape(lines, LANE), shape(width // LANE, LANE), scalar),
+        in_specs=[VMEM] * (2 + 3 * ITERS),
+        out_specs=(VMEM,) * 3,
+        compiler_params=pltpu.CompilerParams(vmem_limit_bytes=4 << 20),
+        cost_estimate=pl.CostEstimate(flops=0, bytes_accessed=16000 << 10, transcendentals=0),
+    )(message, left, *betas, *alphas, *held)
+    others = [swap(part, mask + 1) for mask, part in enumerate(others)]
+    sketch = call(assemble_body, shape(slots, width), token, mine, *others)
     return (sketch, answer.reshape(-1), basis.reshape(-1))
 
 

time: 80.9 us -> 81.5 us (level)
  transfers between devices with their start and end apart: 22 -> 22, of which waited for: 9 -> 9; matrix products, arithmetic and copies ran while one was open for 0% -> 0% of each run, Pallas kernels for 15% -> 16%
where the time goes in v18:
time: 81.5 us; the launch traced here: 81.1 us
  starting transfers between devices  25.6 us (31%)
  blocking collectives  22.5 us (28%)
  Pallas kernels  18.4 us (23%)
  waiting for transfers between devices  13.7 us (17%)
  between operations  0.84 us (1%)
    all_to_all x2, blocking collectives, exchange(): return lax.all_to_all(copies, axis, split_axis=0, concat_axis=0, tiled=True)  22.5 us
    ppermute x11, starting transfers between devices, swap(): lax.ppermute(array, 'row', [(i, i ^ mask) for i in range(row_groups)])  12 us
    all_to_all x1, starting transfers between devices, exchange(): return lax.all_to_all(copies, axis, split_axis=0, concat_axis=0, tiled=True)  7.42 us
    pallas_call x10, Pallas kernels, call(): pl.pallas_call(body, out_shape=out_shape, in_specs=[VMEM] * len(operands)...  7.42 us
    pallas_call x2, Pallas kernels, back(): pl.pallas_call(functools.partial(back_body, first), out_shape=outs, in_sp...  6.99 us
    ppermute x4, waiting for transfers between devices, paired(): come = lax.ppermute(array, axis, [(i, i ^ mask) for i in range(size)])  5.19 us
    ppermute x6, waiting for transfers between devices, direct(): lax.ppermute(array, axis, [(i, i ^ mask) for i in range(size)])  4.2 us
    ppermute x6, starting transfers between devices, direct(): lax.ppermute(array, axis, [(i, i ^ mask) for i in range(size)])  3.85 us
  transfers between devices with their start and end apart: 22, of which 9 were waited for; matrix products, arithmetic and copies ran while one was open for 0% of the time, Pallas kernels for 16%

profile of v18, /device:TPU:0, one launch (start us, length us, event | category | flops | bytes accessed | tf_op | source)
XLA Modules:
  0.0 81.1 jit_solution(12178986488687477282)
XLA Ops:
  0.7 3.4 %shard_map.94 = (f32[8,16,128]{2,1,0:T(8,128)}, f32[512,128]{1,0:T(8,128)}, f32[512,128]{1,0:T(8,128)}, f32[512,128]{1,0:T(8,128)}, f32[512,128]{1,0:T(8,128)}, /*index=5*/f32[512,128]{1,0:T(8,128)}, f32[512,128]{1,0:T(8,128)}) custom-call(f32[512,1024]{1,0:T(8,128)} %design_ref.9, f32[4,128]{1,0:T(4,128)} %bitcast.6, s32[4,128]{1,0:T(4,128)} %bitcast.9, ...), custom_call_target="tpu_custom_call" | custom-call | tf_op jit(solution)/shard_map/pallas_call | solution.py:437
  4.1 7.4 %all-to-all-start = ((f32[8,16,128]{2,1,0:T(8,128)}), f32[8,16,128]{2,1,0:T(8,128)S(1)}, u32[]{:S(2)}, u32[]{:S(2)}) async-start(f32[8,16,128]{2,1,0:T(8,128)} %get-tuple-element.45), calls=%async_computation | async-start | bytes 131072 | tf_op jit(solution)/shard_map/all_to_all | solution.py:24
  11.5 2.0 %collective-permute-start = (f32[512,128]{1,0:T(8,128)}, f32[512,128]{1,0:T(8,128)S(1)}, u32[]{:S(2)}, u32[]{:S(2)}) collective-permute-start(f32[512,128]{1,0:T(8,128)} %get-tuple-element.48), channel_id=1, source_target_pairs={{0,4},{4,0},{8,12},{12,8},{16,20},{20,16},{24,28},{28,24},{1,5},{5... | collective-permute-start | bytes 786440 | tf_op jit(solution)/shard_map/ppermute | solution.py:455
  13.5 1.5 %collective-permute-start.1 = (f32[512,128]{1,0:T(8,128)}, f32[512,128]{1,0:T(8,128)S(1)}, u32[]{:S(2)}, u32[]{:S(2)}) collective-permute-start(f32[512,128]{1,0:T(8,128)} %get-tuple-element.49), channel_id=1, source_target_pairs={{0,8},{4,12},{8,0},{12,4},{16,24},{20,28},{24,16},{28,20},{1,9},{5... | collective-permute-start | bytes 786440 | tf_op jit(solution)/shard_map/ppermute | solution.py:455
  15.0 3.8 %all-to-all-done.parts_ref = f32[8,16,128]{2,1,0:T(8,128)S(1)} async-done(((f32[8,16,128]{2,1,0:T(8,128)}), f32[8,16,128]{2,1,0:T(8,128)S(1)}, u32[]{:S(2)}, u32[]{:S(2)}) %all-to-all-start) | async-done | bytes 65568 | tf_op jit(solution)/shard_map/all_to_all | solution.py:24
  18.8 0.7 collective-permute-start.2
  19.5 5.6 %shard_map.95 = (f32[32,128]{1,0:T(8,128)S(1)}, f32[1,128]{1,0:T(1,128)S(1)}, f32[1024,4096]{1,0:T(8,128)S(1)}) custom-call(f32[1024,4096]{1,0:T(8,128)} %rinv_ref.1, f32[8,16,128]{2,1,0:T(8,128)S(1)} %all-to-all-done.parts_ref), custom_call_target="tpu_custom_call" | custom-call | tf_op jit(solution)/shard_map/pallas_call | solution.py:497
  25.2 1.2 %collective-permute-done.4 = f32[32,128]{1,0:T(8,128)S(1)} collective-permute-done((f32[32,128]{1,0:T(8,128)S(1)}, f32[32,128]{1,0:T(8,128)S(1)}, u32[]{:S(2)}, u32[]{:S(2)}) %collective-permute-start.4) | collective-permute-done | bytes 16416 | tf_op jit(solution)/shard_map/ppermute | solution.py:31
  26.4 1.5 %collective-permute-start.5 = (f32[32,128]{1,0:T(8,128)S(1)}, f32[32,128]{1,0:T(8,128)S(1)}, u32[]{:S(2)}, u32[]{:S(2)}) collective-permute-start(f32[32,128]{1,0:T(8,128)S(1)} %add.6.refs_0_), channel_id=1, source_target_pairs={{0,2},{1,3},{2,0},{3,1},{4,6},{5,7},{6,4},{7,5},{8,10},{9,11},{10,... | collective-permute-start | bytes 49160 | tf_op jit(solution)/shard_map/ppermute | solution.py:31
  27.9 0.6 collective-permute-start.8
  28.5 2.1 %collective-permute-start.9 = (f32[512,128]{1,0:T(8,128)S(1)}, f32[512,128]{1,0:T(8,128)S(1)}, u32[]{:S(2)}, u32[]{:S(2)}) collective-permute-start(f32[512,128]{1,0:T(8,128)S(1)} %copy-done.4), channel_id=1, source_target_pairs={{0,8},{4,12},{8,0},{12,4},{16,24},{20,28},{24,16},{28,20},{1,9},{5... | collective-permute-start | bytes 786440 | tf_op jit(solution)/shard_map/ppermute | solution.py:455
  31.2 1.1 %shard_map.97 = (f32[1,4,128,128]{3,2,1,0:T(8,128)S(1)}, f32[1,4,128,128]{3,2,1,0:T(8,128)S(1)}, f32[1,128]{1,0:T(1,128)S(1)}) custom-call(f32[512,1024]{1,0:T(8,128)S(1)} %copy-done, f32[8,16,128]{2,1,0:T(8,128)S(1)} %all-to-all-done.parts_ref, bf16[8,128,512]{2,1,0:T(8,128)(2,1)S(1)} %shard_map.96.mix_ref, ...), custom_call_target="tpu_custom_call" | custom-call | tf_op jit(solution)/shard_map/pallas_call | solution.py:61
  33.2 1.7 %shard_map.99 = (f32[4,128]{1,0:T(4,128)S(1)}, f32[8,128]{1,0:T(8,128)S(1)}, f32[1,128]{1,0:T(1,128)S(1)}, f32[32,128]{1,0:T(8,128)S(1)}) custom-call(f32[1024,4096]{1,0:T(8,128)S(1)} %get-tuple-element.46.rinv_ref, f32[512,1024]{1,0:T(8,128)S(1)} %copy-done, f32[1,128]{1,0:T(1,128)S(1)} %get-tuple-element.56.token_ref, f32[32,128]{1,0:T(8,128)S(1)} %add.6.refs_0_, ...), custom_call_target="tpu_custom_call" | custom-call | tf_op jit(solution)/shard_map/pallas_call | solution.py:61
  35.0 1.1 %collective-permute-done.6 = f32[4,128]{1,0:T(4,128)S(1)} collective-permute-done((f32[4,128]{1,0:T(4,128)S(1)}, f32[4,128]{1,0:T(4,128)S(1)}, u32[]{:S(2)}, u32[]{:S(2)}) %collective-permute-start.6) | collective-permute-done | bytes 2080 | tf_op jit(solution)/shard_map/ppermute | solution.py:31
  36.2 0.7 collective-permute-start.7
  36.9 2.9 %collective-permute-done.7.refs_1_ = f32[4,128]{1,0:T(4,128)S(1)} collective-permute-done((f32[4,128]{1,0:T(4,128)S(1)}, f32[4,128]{1,0:T(4,128)S(1)}, u32[]{:S(2)}, u32[]{:S(2)}) %collective-permute-start.7) | collective-permute-done | bytes 2080 | tf_op jit(solution)/shard_map/ppermute | solution.py:31
  40.0 12.4 %all_to_all.15.order_ref.parts_ref = f32[8,16,128]{2,1,0:T(8,128)S(1)} all-to-all(f32[8,16,128]{2,1,0:T(8,128)S(1)} %get-tuple-element.60), channel_id=1, replica_groups=mesh['row'=8,'col'=4] {'row'}, dimensions={0} | all-to-all | bytes 131072 | tf_op jit(solution)/shard_map/all_to_all | solution.py:24
  52.5 1.1 %shard_map.102 = (f32[1,4,128,128]{3,2,1,0:T(8,128)S(1)}, f32[1,4,128,128]{3,2,1,0:T(8,128)S(1)}, f32[1,128]{1,0:T(1,128)S(1)}) custom-call(f32[512,1024]{1,0:T(8,128)S(1)} %copy-done, f32[8,16,128]{2,1,0:T(8,128)S(1)} %all-to-all-done.parts_ref, bf16[8,128,512]{2,1,0:T(8,128)(2,1)S(1)} %shard_map.96.mix_ref, f32[1,128]{1,0:T(1,128)S(1)} %get-tuple-element.61.order_ref, ...), custom_call_target="tpu_custom_call" | custom-call | tf_op jit(solution)/shard_map/pallas_call | solution.py:61
  54.1 1.4 %shard_map.103 = (f32[32,128]{1,0:T(8,128)S(1)}, f32[1,128]{1,0:T(1,128)S(1)}) custom-call(f32[1024,4096]{1,0:T(8,128)S(1)} %get-tuple-element.46.rinv_ref, f32[8,16,128]{2,1,0:T(8,128)S(1)} %all_to_all.15.order_ref.parts_ref), custom_call_target="tpu_custom_call" | custom-call | tf_op jit(solution)/shard_map/pallas_call | solution.py:497
  55.6 0.6 collective-permute-start.12
  56.2 1.2 %collective-permute-start.11 = (f32[32,128]{1,0:T(8,128)S(1)}, f32[32,128]{1,0:T(8,128)S(1)}, u32[]{:S(2)}, u32[]{:S(2)}) collective-permute-start(f32[32,128]{1,0:T(8,128)S(1)} %get-tuple-element.67.refs_0_), channel_id=1, source_target_pairs={{0,1},{1,0},{2,3},{3,2},{4,5},{5,4},{6,7},{7,6},{8,9},{9,8},{10,11... | collective-permute-start | bytes 49160 | tf_op jit(solution)/shard_map/ppermute | solution.py:41
  57.5 1.3 %collective-permute-done.13.refs_3_ = f32[32,128]{1,0:T(8,128)S(1)} collective-permute-done((f32[32,128]{1,0:T(8,128)S(1)}, f32[32,128]{1,0:T(8,128)S(1)}, u32[]{:S(2)}, u32[]{:S(2)}) %collective-permute-start.13) | collective-permute-done | bytes 16416 | tf_op jit(solution)/shard_map/ppermute | solution.py:41
  58.8 0.7 collective-permute-done.12.refs_2_
  59.4 1.7 %shard_map.104 = (f32[4,128]{1,0:T(4,128)S(1)}, f32[8,128]{1,0:T(8,128)S(1)}, f32[1,128]{1,0:T(1,128)S(1)}) custom-call(f32[1024,4096]{1,0:T(8,128)S(1)} %get-tuple-element.46.rinv_ref, f32[512,1024]{1,0:T(8,128)S(1)} %copy-done, f32[1,128]{1,0:T(1,128)S(1)} %get-tuple-element.66.token_ref, f32[32,128]{1,0:T(8,128)S(1)} %get-tuple-element.67.refs_0_, ...), custom_call_target="tpu_custom_call" | custom-call | tf_op jit(solution)/shard_map/pallas_call | solution.py:61
  62.3 0.8 collective-permute-start.14
  63.1 1.1 %collective-permute-done.16.refs_3_ = f32[4,128]{1,0:T(4,128)S(1)} collective-permute-done((f32[4,128]{1,0:T(4,128)S(1)}, f32[4,128]{1,0:T(4,128)S(1)}, u32[]{:S(2)}, u32[]{:S(2)}) %collective-permute-start.16) | collective-permute-done | bytes 2080 | tf_op jit(solution)/shard_map/ppermute | solution.py:41
  64.3 1.1 %collective-permute-done.15.refs_2_ = f32[4,128]{1,0:T(4,128)S(1)} collective-permute-done((f32[4,128]{1,0:T(4,128)S(1)}, f32[4,128]{1,0:T(4,128)S(1)}, u32[]{:S(2)}, u32[]{:S(2)}) %collective-permute-start.15) | collective-permute-done | bytes 2080 | tf_op jit(solution)/shard_map/ppermute | solution.py:41
  66.0 0.9 %collective-permute-start.18 = (f32[128,256]{1,0:T(8,128)S(1)}, f32[128,256]{1,0:T(8,128)S(1)}, u32[]{:S(2)}, u32[]{:S(2)}) collective-permute-start(f32[128,256]{1,0:T(8,128)S(1)} %get-tuple-element.82), channel_id=1, source_target_pairs={{0,4},{4,0},{8,12},{12,8},{16,20},{20,16},{24,28},{28,24},{1,5},{5... | collective-permute-start | bytes 393224 | tf_op jit(solution)/shard_map/ppermute | solution.py:455
  67.3 2.2 %collective-permute-start.20 = (f32[128,256]{1,0:T(8,128)S(1)}, f32[128,256]{1,0:T(8,128)S(1)}, u32[]{:S(2)}, u32[]{:S(2)}) collective-permute-start(f32[128,256]{1,0:T(8,128)S(1)} %get-tuple-element.84), channel_id=1, source_target_pairs={{0,12},{4,8},{8,4},{12,0},{16,28},{20,24},{24,20},{28,16},{1,13},{... | collective-permute-start | bytes 393224 | tf_op jit(solution)/shard_map/ppermute | solution.py:455
  69.5 10.1 %all_to_all.16.parts_ref = f32[8,8,128]{2,1,0:T(8,128)S(1)} all-to-all(f32[8,8,128]{2,1,0:T(8,128)S(1)} %get-tuple-element.73), channel_id=1, replica_groups=mesh['row'=8,'col'=4] {'row'}, dimensions={0} | all-to-all | bytes 65536 | tf_op jit(solution)/shard_map/all_to_all | solution.py:24
  79.6 0.6 shard_map.106
  80.3 0.9 %shard_map.108 = f32[128,1024]{1,0:T(8,128)} custom-call(f32[1,128]{1,0:T(1,128)S(1)} %get-tuple-element.77.token_ref, f32[128,256]{1,0:T(8,128)S(1)} %get-tuple-element.81.refs_0_, f32[128,256]{1,0:T(8,128)S(1)} %collective-permute-done.18.refs_1_, f32[128,256]{1,0:T(8,128)S(1)} %collective-permute-done.19.refs_2_, ...), custom_call_target="tpu_custom_call" | custom-call | tf_op jit(solution)/shard_map/pallas_call | solution.py:61
  (43 shorter events, 4.7 us)
Async XLA Ops:
  0.6 30.0 %copy-start.1 = (bf16[256,256]{1,0:T(8,128)(2,1)S(1)}, bf16[256,256]{1,0:T(8,128)(2,1)}, u32[]{:S(2)}) copy-start(bf16[256,256]{1,0:T(8,128)(2,1)} %constant.2.clone.walsh_ref) | copy-start | bytes 393220
  0.6 30.5 %copy-start = (f32[512,1024]{1,0:T(8,128)S(1)}, f32[512,1024]{1,0:T(8,128)}, u32[]{:S(2)}) copy-start(f32[512,1024]{1,0:T(8,128)} %design_ref.9) | copy-start | bytes 6291460
  4.0 24.5 %copy-start.4 = (f32[512,128]{1,0:T(8,128)S(1)}, f32[512,128]{1,0:T(8,128)}, u32[]{:S(2)}) copy-start(f32[512,128]{1,0:T(8,128)} %get-tuple-element.63) | copy-start | bytes 786436
  4.0 28.7 %copy-start.3 = (f32[512,128]{1,0:T(8,128)S(1)}, f32[512,128]{1,0:T(8,128)}, u32[]{:S(2)}) copy-start(f32[512,128]{1,0:T(8,128)} %get-tuple-element.65) | copy-start | bytes 786436
  4.1 14.8 %all-to-all-start = ((f32[8,16,128]{2,1,0:T(8,128)}), f32[8,16,128]{2,1,0:T(8,128)S(1)}, u32[]{:S(2)}, u32[]{:S(2)}) async-start(f32[8,16,128]{2,1,0:T(8,128)} %get-tuple-element.45), calls=%async_computation | async-start | bytes 131072 | tf_op jit(solution)/shard_map/all_to_all | solution.py:24
  11.5 13.7 %collective-permute-start = (f32[512,128]{1,0:T(8,128)}, f32[512,128]{1,0:T(8,128)S(1)}, u32[]{:S(2)}, u32[]{:S(2)}) collective-permute-start(f32[512,128]{1,0:T(8,128)} %get-tuple-element.48), channel_id=1, source_target_pairs={{0,4},{4,0},{8,12},{12,8},{16,20},{20,16},{24,28},{28,24},{1,5},{5... | collective-permute-start | bytes 786440 | tf_op jit(solution)/shard_map/ppermute | solution.py:455
  13.5 11.6 %collective-permute-start.1 = (f32[512,128]{1,0:T(8,128)}, f32[512,128]{1,0:T(8,128)S(1)}, u32[]{:S(2)}, u32[]{:S(2)}) collective-permute-start(f32[512,128]{1,0:T(8,128)} %get-tuple-element.49), channel_id=1, source_target_pairs={{0,8},{4,12},{8,0},{12,4},{16,24},{20,28},{24,16},{28,20},{1,9},{5... | collective-permute-start | bytes 786440 | tf_op jit(solution)/shard_map/ppermute | solution.py:455
  18.8 9.1 %copy-start.5 = (f32[512,128]{1,0:T(8,128)S(1)}, f32[512,128]{1,0:T(8,128)}, u32[]{:S(2)}) copy-start(f32[512,128]{1,0:T(8,128)} %get-tuple-element.62) | copy-start | bytes 786436
  18.8 21.0 %copy-start.2 = (f32[512]{0:T(512)S(1)}, f32[512]{0:T(512)}, u32[]{:S(2)}) copy-start(f32[512]{0:T(512)} %param.11) | copy-start | bytes 6148
  18.8 12.4 %collective-permute-start.2 = (f32[512,128]{1,0:T(8,128)}, f32[512,128]{1,0:T(8,128)S(1)}, u32[]{:S(2)}, u32[]{:S(2)}) collective-permute-start(f32[512,128]{1,0:T(8,128)} %get-tuple-element.53), channel_id=1, source_target_pairs={{0,12},{4,8},{8,4},{12,0},{16,28},{20,24},{24,20},{28,16},{1,13},{... | collective-permute-start | bytes 786440 | tf_op jit(solution)/shard_map/ppermute | solution.py:455
  25.2 1.2 %collective-permute-start.4 = (f32[32,128]{1,0:T(8,128)S(1)}, f32[32,128]{1,0:T(8,128)S(1)}, u32[]{:S(2)}, u32[]{:S(2)}) collective-permute-start(f32[32,128]{1,0:T(8,128)S(1)} %shard_map.98), channel_id=1, source_target_pairs={{0,1},{1,0},{2,3},{3,2},{4,5},{5,4},{6,7},{7,6},{8,9},{9,8},{10,11... | collective-permute-start | bytes 49160 | tf_op jit(solution)/shard_map/ppermute | solution.py:31
  26.4 6.3 %collective-permute-start.5 = (f32[32,128]{1,0:T(8,128)S(1)}, f32[32,128]{1,0:T(8,128)S(1)}, u32[]{:S(2)}, u32[]{:S(2)}) collective-permute-start(f32[32,128]{1,0:T(8,128)S(1)} %add.6.refs_0_), channel_id=1, source_target_pairs={{0,2},{1,3},{2,0},{3,1},{4,6},{5,7},{6,4},{7,5},{8,10},{9,11},{10,... | collective-permute-start | bytes 49160 | tf_op jit(solution)/shard_map/ppermute | solution.py:31
  27.9 24.5 %collective-permute-start.8 = (f32[512,128]{1,0:T(8,128)S(1)}, f32[512,128]{1,0:T(8,128)S(1)}, u32[]{:S(2)}, u32[]{:S(2)}) collective-permute-start(f32[512,128]{1,0:T(8,128)S(1)} %copy-done.5), channel_id=1, source_target_pairs={{0,4},{4,0},{8,12},{12,8},{16,20},{20,16},{24,28},{28,24},{1,5},{5... | collective-permute-start | bytes 786440 | tf_op jit(solution)/shard_map/ppermute | solution.py:455
  28.5 23.9 %collective-permute-start.9 = (f32[512,128]{1,0:T(8,128)S(1)}, f32[512,128]{1,0:T(8,128)S(1)}, u32[]{:S(2)}, u32[]{:S(2)}) collective-permute-start(f32[512,128]{1,0:T(8,128)S(1)} %copy-done.4), channel_id=1, source_target_pairs={{0,8},{4,12},{8,0},{12,4},{16,24},{20,28},{24,16},{28,20},{1,9},{5... | collective-permute-start | bytes 786440 | tf_op jit(solution)/shard_map/ppermute | solution.py:455
  32.3 20.1 %collective-permute-start.3 = (f32[1,4,128,128]{3,2,1,0:T(8,128)S(1)}, f32[1,4,128,128]{3,2,1,0:T(8,128)S(1)}, u32[]{:S(2)}, u32[]{:S(2)}) collective-permute-start(f32[1,4,128,128]{3,2,1,0:T(8,128)S(1)} %get-tuple-element.55), channel_id=1, source_target_pairs={{0,16},{4,20},{8,24},{12,28},{16,0},{20,4},{24,8},{28,12},{1,17},{... | collective-permute-start | bytes 786440 | tf_op jit(solution)/shard_map/ppermute | solution.py:455
  32.8 19.7 %collective-permute-start.10 = (f32[512,128]{1,0:T(8,128)S(1)}, f32[512,128]{1,0:T(8,128)S(1)}, u32[]{:S(2)}, u32[]{:S(2)}) collective-permute-start(f32[512,128]{1,0:T(8,128)S(1)} %copy-done.3), channel_id=1, source_target_pairs={{0,12},{4,8},{8,4},{12,0},{16,28},{20,24},{24,20},{28,16},{1,13},{... | collective-permute-start | bytes 786440 | tf_op jit(solution)/shard_map/ppermute | solution.py:455
  34.9 1.2 %collective-permute-start.6 = (f32[4,128]{1,0:T(4,128)S(1)}, f32[4,128]{1,0:T(4,128)S(1)}, u32[]{:S(2)}, u32[]{:S(2)}) collective-permute-start(f32[4,128]{1,0:T(4,128)S(1)} %get-tuple-element.58), channel_id=1, source_target_pairs={{0,1},{1,0},{2,3},{3,2},{4,5},{5,4},{6,7},{7,6},{8,9},{9,8},{10,11... | collective-permute-start | bytes 6152 | tf_op jit(solution)/shard_map/ppermute | solution.py:31
  36.2 3.6 %collective-permute-start.7 = (f32[4,128]{1,0:T(4,128)S(1)}, f32[4,128]{1,0:T(4,128)S(1)}, u32[]{:S(2)}, u32[]{:S(2)}) collective-permute-start(f32[4,128]{1,0:T(4,128)S(1)} %add.7.refs_0_), channel_id=1, source_target_pairs={{0,2},{1,3},{2,0},{3,1},{4,6},{5,7},{6,4},{7,5},{8,10},{9,11},{10,... | collective-permute-start | bytes 6152 | tf_op jit(solution)/shard_map/ppermute | solution.py:31
  53.6 12.3 %collective-permute-start.17 = (f32[1,4,128,128]{3,2,1,0:T(8,128)S(1)}, f32[1,4,128,128]{3,2,1,0:T(8,128)S(1)}, u32[]{:S(2)}, u32[]{:S(2)}) collective-permute-start(f32[1,4,128,128]{3,2,1,0:T(8,128)S(1)} %get-tuple-element.80), channel_id=1, source_target_pairs={{0,16},{4,20},{8,24},{12,28},{16,0},{20,4},{24,8},{28,12},{1,17},{... | collective-permute-start | bytes 786440 | tf_op jit(solution)/shard_map/ppermute | solution.py:455
  55.6 3.2 %collective-permute-start.13 = (f32[32,128]{1,0:T(8,128)S(1)}, f32[32,128]{1,0:T(8,128)S(1)}, u32[]{:S(2)}, u32[]{:S(2)}) collective-permute-start(f32[32,128]{1,0:T(8,128)S(1)} %get-tuple-element.67.refs_0_), channel_id=1, source_target_pairs={{0,3},{1,2},{2,1},{3,0},{4,7},{5,6},{6,5},{7,4},{8,11},{9,10},{10,... | collective-permute-start | bytes 49160 | tf_op jit(solution)/shard_map/ppermute | solution.py:41
  55.6 3.8 %collective-permute-start.12 = (f32[32,128]{1,0:T(8,128)S(1)}, f32[32,128]{1,0:T(8,128)S(1)}, u32[]{:S(2)}, u32[]{:S(2)}) collective-permute-start(f32[32,128]{1,0:T(8,128)S(1)} %get-tuple-element.67.refs_0_), channel_id=1, source_target_pairs={{0,2},{1,3},{2,0},{3,1},{4,6},{5,7},{6,4},{7,5},{8,10},{9,11},{10,... | collective-permute-start | bytes 49160 | tf_op jit(solution)/shard_map/ppermute | solution.py:41
  56.2 3.2 %collective-permute-start.11 = (f32[32,128]{1,0:T(8,128)S(1)}, f32[32,128]{1,0:T(8,128)S(1)}, u32[]{:S(2)}, u32[]{:S(2)}) collective-permute-start(f32[32,128]{1,0:T(8,128)S(1)} %get-tuple-element.67.refs_0_), channel_id=1, source_target_pairs={{0,1},{1,0},{2,3},{3,2},{4,5},{5,4},{6,7},{7,6},{8,9},{9,8},{10,11... | collective-permute-start | bytes 49160 | tf_op jit(solution)/shard_map/ppermute | solution.py:41
  61.2 3.1 %collective-permute-start.16 = (f32[4,128]{1,0:T(4,128)S(1)}, f32[4,128]{1,0:T(4,128)S(1)}, u32[]{:S(2)}, u32[]{:S(2)}) collective-permute-start(f32[4,128]{1,0:T(4,128)S(1)} %get-tuple-element.70.refs_0_), channel_id=1, source_target_pairs={{0,3},{1,2},{2,1},{3,0},{4,7},{5,6},{6,5},{7,4},{8,11},{9,10},{10,... | collective-permute-start | bytes 6152 | tf_op jit(solution)/shard_map/ppermute | solution.py:41
  61.8 3.6 %collective-permute-start.15 = (f32[4,128]{1,0:T(4,128)S(1)}, f32[4,128]{1,0:T(4,128)S(1)}, u32[]{:S(2)}, u32[]{:S(2)}) collective-permute-start(f32[4,128]{1,0:T(4,128)S(1)} %get-tuple-element.70.refs_0_), channel_id=1, source_target_pairs={{0,2},{1,3},{2,0},{3,1},{4,6},{5,7},{6,4},{7,5},{8,10},{9,11},{10,... | collective-permute-start | bytes 6152 | tf_op jit(solution)/shard_map/ppermute | solution.py:41
  62.3 3.0 %collective-permute-start.14 = (f32[4,128]{1,0:T(4,128)S(1)}, f32[4,128]{1,0:T(4,128)S(1)}, u32[]{:S(2)}, u32[]{:S(2)}) collective-permute-start(f32[4,128]{1,0:T(4,128)S(1)} %get-tuple-element.70.refs_0_), channel_id=1, source_target_pairs={{0,1},{1,0},{2,3},{3,2},{4,5},{5,4},{6,7},{7,6},{8,9},{9,8},{10,11... | collective-permute-start | bytes 6152 | tf_op jit(solution)/shard_map/ppermute | solution.py:41
  66.0 14.3 %collective-permute-start.18 = (f32[128,256]{1,0:T(8,128)S(1)}, f32[128,256]{1,0:T(8,128)S(1)}, u32[]{:S(2)}, u32[]{:S(2)}) collective-permute-start(f32[128,256]{1,0:T(8,128)S(1)} %get-tuple-element.82), channel_id=1, source_target_pairs={{0,4},{4,0},{8,12},{12,8},{16,20},{20,16},{24,28},{28,24},{1,5},{5... | collective-permute-start | bytes 393224 | tf_op jit(solution)/shard_map/ppermute | solution.py:455
  66.9 13.4 %collective-permute-start.19 = (f32[128,256]{1,0:T(8,128)S(1)}, f32[128,256]{1,0:T(8,128)S(1)}, u32[]{:S(2)}, u32[]{:S(2)}) collective-permute-start(f32[128,256]{1,0:T(8,128)S(1)} %get-tuple-element.83), channel_id=1, source_target_pairs={{0,8},{4,12},{8,0},{12,4},{16,24},{20,28},{24,16},{28,20},{1,9},{5... | collective-permute-start | bytes 393224 | tf_op jit(solution)/shard_map/ppermute | solution.py:455
  67.3 12.9 %collective-permute-start.20 = (f32[128,256]{1,0:T(8,128)S(1)}, f32[128,256]{1,0:T(8,128)S(1)}, u32[]{:S(2)}, u32[]{:S(2)}) collective-permute-start(f32[128,256]{1,0:T(8,128)S(1)} %get-tuple-element.84), channel_id=1, source_target_pairs={{0,12},{4,8},{8,4},{12,0},{16,28},{20,24},{24,20},{28,16},{1,13},{... | collective-permute-start | bytes 393224 | tf_op jit(solution)/shard_map/ppermute | solution.py:455

commit v19 on v17

--- a/solution.py
+++ b/solution.py
@@ -49,12 +49,10 @@
 
 
 def walsh(size):
-    index = np.arange(size)
-    common = index[:, None] & index[None, :]
-    parity = np.zeros((size, size), np.int64)
-    for shift in range(size.bit_length()):
-        parity ^= (common >> shift) & 1
-    return (1 - 2 * parity).astype(np.float32)
+    parity = lax.broadcasted_iota(jnp.int32, (size, size), 0) & lax.broadcasted_iota(jnp.int32, (size, size), 1)
+    for shift in (4, 2, 1):
+        parity = parity ^ (parity >> shift)
+    return (1 - 2 * (parity & 1)).astype(F32).astype(jnp.bfloat16)
 
 
 def call(body, out_shape, *operands, scratch=()):
@@ -215,7 +213,11 @@
         copy.wait()
 
 
-def back_body(first, rinv_ref, parts_ref, term_ref, beta_ref, *refs):
+def back_body(first, rinv_ref, parts_ref, *refs):
+    if first:
+        term_ref, beta_ref, mix_ref, *refs, walsh_ref = refs
+    else:
+        term_ref, beta_ref, *refs = refs
     tiles = rinv_ref.shape[0] // LANE
     copies = []
     if first:
@@ -224,6 +226,8 @@
             part, right = slice(block * LANE, (block + 1) * LANE), slice(block * LANE, rinv_ref.shape[1])
             copies.append(pltpu.make_async_copy(rinv_ref.at[part, right], rinv_here.at[part, right], sems.at[block]))
             copies[-1].start()
+        walsh_ref[...] = walsh(HB)
+        mix_body(rinv_ref.shape[0], parts_ref, walsh_ref, mix_ref)
     else:
         rinv_here, (scratch,) = rinv_ref, refs
     summed = tree([parts_ref[i, : tiles + 1, :] for i in range(parts_ref.shape[0])])
@@ -378,14 +382,15 @@
 
 
 def last_body(parts_ref, left_ref, *refs):
-    basis_ref, solution_ref, sketch_ref = refs[-3:]
+    basis_ref, solution_ref, sketch_ref, sems = refs[-4:]
     quarters = refs[3 * ITERS : 3 * ITERS + NEAR]
     place = lax.axis_index("row") % NEAR
     piece = quarters[0].shape[1]
+    copies = []
     for mask, part_ref in enumerate(quarters):
-        for tile in range(0, piece, LANE):
-            column = pl.multiple_of((place ^ mask) * piece + tile, LANE)
-            sketch_ref[:, pl.ds(column, LANE)] = part_ref[:, tile : tile + LANE]
+        columns = pl.ds(pl.multiple_of((place ^ mask) * piece, LANE), piece)
+        copies.append(pltpu.make_async_copy(part_ref, sketch_ref.at[:, columns], sems.at[mask]))
+        copies[-1].start()
     betas = [ref[...] for ref in refs[:ITERS]]
     alphas = [ref[...] for ref in refs[ITERS : 2 * ITERS]]
     held = [ref[...] for ref in refs[2 * ITERS : 3 * ITERS]]
@@ -407,6 +412,8 @@
             search = held[step + 1] - sine * alpha / rho * search
             rhobar = -cosine * alpha
     solution_ref[...] = iterate
+    for copy in copies:
+        copy.wait()
 
 
 def shape(*dims, dtype=F32):
@@ -450,10 +457,6 @@
     def swap(array, mask):
         return lax.ppermute(array, "row", [(i, i ^ mask) for i in range(row_groups)])
 
-    def mix(message):
-        made = shape(row_groups, slots, rows, dtype=jnp.bfloat16)
-        return call(functools.partial(mix_body, width), made, message, jnp.asarray(walsh(HB), jnp.bfloat16))
-
     def sample(chunk, mixed, order):
         return call(
             functools.partial(sample_body, scale, chunk * piece),
@@ -487,17 +490,19 @@
 
     def back(rinv, message, first):
         outs, scratch = (shape(whole // LANE, LANE), scalar), [pltpu.VMEM((width // LANE, LANE), F32)]
+        operands = (rinv, message)
         if first:
-            outs += (shape(*rinv.shape),)
+            outs += (shape(row_groups, slots, rows, dtype=jnp.bfloat16), shape(*rinv.shape))
             scratch += [pltpu.SemaphoreType.DMA((width // LANE,))]
+            scratch += [pltpu.VMEM((HB, HB), jnp.bfloat16)]
         return pl.pallas_call(
             functools.partial(back_body, first),
             out_shape=outs,
-            in_specs=[HBM if first else VMEM, VMEM],
+            in_specs=[HBM if first else VMEM] + [VMEM] * (len(operands) - 1),
             out_specs=(VMEM,) * len(outs),
             scratch_shapes=scratch,
             compiler_params=pltpu.CompilerParams(vmem_limit_bytes=(34 if first else 24) << 20),
-            )(rinv, message)
+        )(*operands)
 
     def forward(terms, token, last, *before):
         return call(
@@ -530,7 +535,7 @@
     for step in range(ITERS):
         last = step + 1 == ITERS
         if step == 0:
-            term, beta, here = back(rinv, message, True)
+            term, beta, mixed, here = back(rinv, message, True)
             term = pl.pallas_call(
                 pass_body,
                 out_shape=shape(*term.shape),
@@ -538,7 +543,6 @@
                 out_specs=VMEM,
                 compiler_params=pltpu.CompilerParams(vmem_limit_bytes=2 << 20),
             )(*near[: NEAR - 2], term)
-            mixed = mix(message)
         else:
             term, beta = back(here, message, False)
             token = beta
@@ -562,17 +566,15 @@
         message = exchange(message, "row")
     quarters = (shape(slots, width // NEAR),) * NEAR
     mine, *others = call(split_body, quarters, *joined, *halve(keep, come, beta), left)
-    basis, answer, sketch = call(
+    quarters = [mine] + [swap(part, mask + 1) for mask, part in enumerate(others)]
+    basis, answer, sketch = pl.pallas_call(
         last_body,
-        (shape(lines, LANE), shape(width // LANE, LANE), shape(slots, width)),
-        message,
-        left,
-        *betas,
-        *alphas,
-        *held,
-        mine,
-        *(swap(part, mask + 1) for mask, part in enumerate(others)),
-    )
+        out_shape=(shape(lines, LANE), shape(width // LANE, LANE), shape(slots, width)),
+        in_specs=[VMEM] * (2 + 3 * ITERS + NEAR),
+        out_specs=(VMEM, VMEM, HBM),
+        scratch_shapes=[pltpu.SemaphoreType.DMA((NEAR,))],
+        compiler_params=pltpu.CompilerParams(vmem_limit_bytes=24 << 20),
+    )(message, left, *betas, *alphas, *held, *quarters)
     return (sketch, answer.reshape(-1), basis.reshape(-1))
 
 

time: 80.9 us -> 80.9 us (level)
    pallas_call x0 -> x1, Pallas kernels: none -> 1.43 us  [shards(): pl.pallas_call(last_body, out_shape=(shape(lines, LANE), shape(width // L...]
    pallas_call x10 -> x8, Pallas kernels: 7.46 us -> 6.06 us  [call(): pl.pallas_call(body, out_shape=out_shape, in_specs=[VMEM] * len(operands)...]
where the time goes in v19:
time: 80.9 us; the launch traced here: 80.5 us
  starting transfers between devices  26 us (32%)
  blocking collectives  22.1 us (27%)
  Pallas kernels  18.1 us (22%)
  waiting for transfers between devices  13.4 us (17%)
  between operations  0.81 us (1%)
    all_to_all x2, blocking collectives, exchange(): return lax.all_to_all(copies, axis, split_axis=0, concat_axis=0, tiled=True)  22.1 us
    ppermute x11, starting transfers between devices, swap(): lax.ppermute(array, 'row', [(i, i ^ mask) for i in range(row_groups)])  12 us
    all_to_all x1, starting transfers between devices, exchange(): return lax.all_to_all(copies, axis, split_axis=0, concat_axis=0, tiled=True)  7.42 us
    pallas_call x2, Pallas kernels, back(): pl.pallas_call(functools.partial(back_body, first), out_shape=outs, in_sp...  7.29 us
    pallas_call x8, Pallas kernels, call(): pl.pallas_call(body, out_shape=out_shape, in_specs=[VMEM] * len(operands)...  6.06 us
    ppermute x4, waiting for transfers between devices, paired(): come = lax.ppermute(array, axis, [(i, i ^ mask) for i in range(size)])  4.75 us
    ppermute x6, waiting for transfers between devices, direct(): lax.ppermute(array, axis, [(i, i ^ mask) for i in range(size)])  4.2 us
    ppermute x6, starting transfers between devices, direct(): lax.ppermute(array, axis, [(i, i ^ mask) for i in range(size)])  3.85 us
  transfers between devices with their start and end apart: 22, of which 9 were waited for; matrix products, arithmetic and copies ran while one was open for 0% of the time, Pallas kernels for 15%

profile of v19, /device:TPU:0, one launch (start us, length us, event | category | flops | bytes accessed | tf_op | source)
XLA Modules:
  0.0 80.5 jit_solution(9728568972084428947)
XLA Ops:
  0.6 3.4 %shard_map.85 = (f32[8,16,128]{2,1,0:T(8,128)}, f32[512,128]{1,0:T(8,128)}, f32[512,128]{1,0:T(8,128)}, f32[512,128]{1,0:T(8,128)}, f32[512,128]{1,0:T(8,128)}, /*index=5*/f32[512,128]{1,0:T(8,128)}, f32[512,128]{1,0:T(8,128)}) custom-call(f32[512,1024]{1,0:T(8,128)} %design_ref.9, f32[4,128]{1,0:T(4,128)} %bitcast.6, s32[4,128]{1,0:T(4,128)} %bitcast.9, ...), custom_call_target="tpu_custom_call" | custom-call | tf_op jit(solution)/shard_map/pallas_call | solution.py:440
  4.0 7.4 %all-to-all-start = ((f32[8,16,128]{2,1,0:T(8,128)}), f32[8,16,128]{2,1,0:T(8,128)S(1)}, u32[]{:S(2)}, u32[]{:S(2)}) async-start(f32[8,16,128]{2,1,0:T(8,128)} %get-tuple-element.46), calls=%async_computation | async-start | bytes 131072 | tf_op jit(solution)/shard_map/all_to_all | solution.py:24
  11.5 2.0 %collective-permute-start = (f32[512,128]{1,0:T(8,128)}, f32[512,128]{1,0:T(8,128)S(1)}, u32[]{:S(2)}, u32[]{:S(2)}) collective-permute-start(f32[512,128]{1,0:T(8,128)} %get-tuple-element.50), channel_id=1, source_target_pairs={{0,4},{4,0},{8,12},{12,8},{16,20},{20,16},{24,28},{28,24},{1,5},{5... | collective-permute-start | bytes 786440 | tf_op jit(solution)/shard_map/ppermute | solution.py:458
  13.5 1.5 %collective-permute-start.1 = (f32[512,128]{1,0:T(8,128)}, f32[512,128]{1,0:T(8,128)S(1)}, u32[]{:S(2)}, u32[]{:S(2)}) collective-permute-start(f32[512,128]{1,0:T(8,128)} %get-tuple-element.51), channel_id=1, source_target_pairs={{0,8},{4,12},{8,0},{12,4},{16,24},{20,28},{24,16},{28,20},{1,9},{5... | collective-permute-start | bytes 786440 | tf_op jit(solution)/shard_map/ppermute | solution.py:458
  14.9 3.8 %all-to-all-done.parts_ref = f32[8,16,128]{2,1,0:T(8,128)S(1)} async-done(((f32[8,16,128]{2,1,0:T(8,128)}), f32[8,16,128]{2,1,0:T(8,128)S(1)}, u32[]{:S(2)}, u32[]{:S(2)}) %all-to-all-start) | async-done | bytes 65568 | tf_op jit(solution)/shard_map/all_to_all | solution.py:24
  18.8 0.7 collective-permute-start.2
  19.5 5.9 %shard_map.86 = (f32[32,128]{1,0:T(8,128)S(1)}, f32[1,128]{1,0:T(1,128)S(1)}, bf16[8,128,512]{2,1,0:T(8,128)(2,1)S(1)}, f32[1024,4096]{1,0:T(8,128)S(1)}) custom-call(f32[1024,4096]{1,0:T(8,128)} %rinv_ref.1, f32[8,16,128]{2,1,0:T(8,128)S(1)} %all-to-all-done.parts_ref), custom_call_target="tpu_custom_call" | custom-call | tf_op jit(solution)/shard_map/pallas_call | solution.py:498
  25.5 1.2 %collective-permute-done.4 = f32[32,128]{1,0:T(8,128)S(1)} collective-permute-done((f32[32,128]{1,0:T(8,128)S(1)}, f32[32,128]{1,0:T(8,128)S(1)}, u32[]{:S(2)}, u32[]{:S(2)}) %collective-permute-start.4) | collective-permute-done | bytes 16416 | tf_op jit(solution)/shard_map/ppermute | solution.py:31
  26.7 1.5 %collective-permute-start.5 = (f32[32,128]{1,0:T(8,128)S(1)}, f32[32,128]{1,0:T(8,128)S(1)}, u32[]{:S(2)}, u32[]{:S(2)}) collective-permute-start(f32[32,128]{1,0:T(8,128)S(1)} %add.6.refs_0_), channel_id=1, source_target_pairs={{0,2},{1,3},{2,0},{3,1},{4,6},{5,7},{6,4},{7,5},{8,10},{9,11},{10,... | collective-permute-start | bytes 49160 | tf_op jit(solution)/shard_map/ppermute | solution.py:31
  28.2 0.6 collective-permute-start.8
  28.8 2.1 %collective-permute-start.9 = (f32[512,128]{1,0:T(8,128)S(1)}, f32[512,128]{1,0:T(8,128)S(1)}, u32[]{:S(2)}, u32[]{:S(2)}) collective-permute-start(f32[512,128]{1,0:T(8,128)S(1)} %copy-done.3), channel_id=1, source_target_pairs={{0,8},{4,12},{8,0},{12,4},{16,24},{20,28},{24,16},{28,20},{1,9},{5... | collective-permute-start | bytes 786440 | tf_op jit(solution)/shard_map/ppermute | solution.py:458
  31.0 1.1 %shard_map.87 = (f32[1,4,128,128]{3,2,1,0:T(8,128)S(1)}, f32[1,4,128,128]{3,2,1,0:T(8,128)S(1)}, f32[1,128]{1,0:T(1,128)S(1)}) custom-call(f32[512,1024]{1,0:T(8,128)S(1)} %copy-done, f32[8,16,128]{2,1,0:T(8,128)S(1)} %all-to-all-done.parts_ref, bf16[8,128,512]{2,1,0:T(8,128)(2,1)S(1)} %get-tuple-element.48.mix_ref, ...), custom_call_target="tpu_custom_call" | custom-call | tf_op jit(solution)/shard_map/pallas_call | solution.py:59
  33.0 1.7 %shard_map.89 = (f32[4,128]{1,0:T(4,128)S(1)}, f32[8,128]{1,0:T(8,128)S(1)}, f32[1,128]{1,0:T(1,128)S(1)}, f32[32,128]{1,0:T(8,128)S(1)}) custom-call(f32[1024,4096]{1,0:T(8,128)S(1)} %get-tuple-element.47.rinv_ref, f32[512,1024]{1,0:T(8,128)S(1)} %copy-done, f32[1,128]{1,0:T(1,128)S(1)} %get-tuple-element.58.token_ref, f32[32,128]{1,0:T(8,128)S(1)} %add.6.refs_0_, ...), custom_call_target="tpu_custom_call" | custom-call | tf_op jit(solution)/shard_map/pallas_call | solution.py:59
  34.8 1.1 %collective-permute-done.6 = f32[4,128]{1,0:T(4,128)S(1)} collective-permute-done((f32[4,128]{1,0:T(4,128)S(1)}, f32[4,128]{1,0:T(4,128)S(1)}, u32[]{:S(2)}, u32[]{:S(2)}) %collective-permute-start.6) | collective-permute-done | bytes 2080 | tf_op jit(solution)/shard_map/ppermute | solution.py:31
  35.9 1.2 %collective-permute-start.7 = (f32[4,128]{1,0:T(4,128)S(1)}, f32[4,128]{1,0:T(4,128)S(1)}, u32[]{:S(2)}, u32[]{:S(2)}) collective-permute-start(f32[4,128]{1,0:T(4,128)S(1)} %add.7.refs_0_), channel_id=1, source_target_pairs={{0,2},{1,3},{2,0},{3,1},{4,6},{5,7},{6,4},{7,5},{8,10},{9,11},{10,... | collective-permute-start | bytes 6152 | tf_op jit(solution)/shard_map/ppermute | solution.py:31
  37.1 2.4 %collective-permute-done.7.refs_1_ = f32[4,128]{1,0:T(4,128)S(1)} collective-permute-done((f32[4,128]{1,0:T(4,128)S(1)}, f32[4,128]{1,0:T(4,128)S(1)}, u32[]{:S(2)}, u32[]{:S(2)}) %collective-permute-start.7) | collective-permute-done | bytes 2080 | tf_op jit(solution)/shard_map/ppermute | solution.py:31
  39.7 12.4 %all_to_all.15.order_ref.parts_ref = f32[8,16,128]{2,1,0:T(8,128)S(1)} all-to-all(f32[8,16,128]{2,1,0:T(8,128)S(1)} %get-tuple-element.62), channel_id=1, replica_groups=mesh['row'=8,'col'=4] {'row'}, dimensions={0} | all-to-all | bytes 131072 | tf_op jit(solution)/shard_map/all_to_all | solution.py:24
  52.2 1.1 %shard_map.92 = (f32[1,4,128,128]{3,2,1,0:T(8,128)S(1)}, f32[1,4,128,128]{3,2,1,0:T(8,128)S(1)}, f32[1,128]{1,0:T(1,128)S(1)}) custom-call(f32[512,1024]{1,0:T(8,128)S(1)} %copy-done, f32[8,16,128]{2,1,0:T(8,128)S(1)} %all-to-all-done.parts_ref, bf16[8,128,512]{2,1,0:T(8,128)(2,1)S(1)} %get-tuple-element.48.mix_ref, ...), custom_call_target="tpu_custom_call" | custom-call | tf_op jit(solution)/shard_map/pallas_call | solution.py:59
  53.9 1.4 %shard_map.93 = (f32[32,128]{1,0:T(8,128)S(1)}, f32[1,128]{1,0:T(1,128)S(1)}) custom-call(f32[1024,4096]{1,0:T(8,128)S(1)} %get-tuple-element.47.rinv_ref, f32[8,16,128]{2,1,0:T(8,128)S(1)} %all_to_all.15.order_ref.parts_ref), custom_call_target="tpu_custom_call" | custom-call | tf_op jit(solution)/shard_map/pallas_call | solution.py:498
  55.4 0.6 collective-permute-start.12
  56.0 1.3 %collective-permute-start.11 = (f32[32,128]{1,0:T(8,128)S(1)}, f32[32,128]{1,0:T(8,128)S(1)}, u32[]{:S(2)}, u32[]{:S(2)}) collective-permute-start(f32[32,128]{1,0:T(8,128)S(1)} %get-tuple-element.69.refs_0_), channel_id=1, source_target_pairs={{0,1},{1,0},{2,3},{3,2},{4,5},{5,4},{6,7},{7,6},{8,9},{9,8},{10,11... | collective-permute-start | bytes 49160 | tf_op jit(solution)/shard_map/ppermute | solution.py:41
  57.2 1.3 %collective-permute-done.13.refs_3_ = f32[32,128]{1,0:T(8,128)S(1)} collective-permute-done((f32[32,128]{1,0:T(8,128)S(1)}, f32[32,128]{1,0:T(8,128)S(1)}, u32[]{:S(2)}, u32[]{:S(2)}) %collective-permute-start.13) | collective-permute-done | bytes 16416 | tf_op jit(solution)/shard_map/ppermute | solution.py:41
  58.5 0.7 collective-permute-done.12.refs_2_
  59.2 1.7 %shard_map.94 = (f32[4,128]{1,0:T(4,128)S(1)}, f32[8,128]{1,0:T(8,128)S(1)}, f32[1,128]{1,0:T(1,128)S(1)}) custom-call(f32[1024,4096]{1,0:T(8,128)S(1)} %get-tuple-element.47.rinv_ref, f32[512,1024]{1,0:T(8,128)S(1)} %copy-done, f32[1,128]{1,0:T(1,128)S(1)} %get-tuple-element.68.token_ref, f32[32,128]{1,0:T(8,128)S(1)} %get-tuple-element.69.refs_0_, ...), custom_call_target="tpu_custom_call" | custom-call | tf_op jit(solution)/shard_map/pallas_call | solution.py:59
  62.1 0.8 collective-permute-start.14
  62.9 1.1 %collective-permute-done.16.refs_3_ = f32[4,128]{1,0:T(4,128)S(1)} collective-permute-done((f32[4,128]{1,0:T(4,128)S(1)}, f32[4,128]{1,0:T(4,128)S(1)}, u32[]{:S(2)}, u32[]{:S(2)}) %collective-permute-start.16) | collective-permute-done | bytes 2080 | tf_op jit(solution)/shard_map/ppermute | solution.py:41
  64.0 1.1 %collective-permute-done.15.refs_2_ = f32[4,128]{1,0:T(4,128)S(1)} collective-permute-done((f32[4,128]{1,0:T(4,128)S(1)}, f32[4,128]{1,0:T(4,128)S(1)}, u32[]{:S(2)}, u32[]{:S(2)}) %collective-permute-start.15) | collective-permute-done | bytes 2080 | tf_op jit(solution)/shard_map/ppermute | solution.py:41
  65.8 0.8 %collective-permute-start.18 = (f32[128,256]{1,0:T(8,128)S(1)}, f32[128,256]{1,0:T(8,128)S(1)}, u32[]{:S(2)}, u32[]{:S(2)}) collective-permute-start(f32[128,256]{1,0:T(8,128)S(1)} %get-tuple-element.83), channel_id=1, source_target_pairs={{0,4},{4,0},{8,12},{12,8},{16,20},{20,16},{24,28},{28,24},{1,5},{5... | collective-permute-start | bytes 393224 | tf_op jit(solution)/shard_map/ppermute | solution.py:458
  66.7 0.8 %collective-permute-start.19 = (f32[128,256]{1,0:T(8,128)S(1)}, f32[128,256]{1,0:T(8,128)S(1)}, u32[]{:S(2)}, u32[]{:S(2)}) collective-permute-start(f32[128,256]{1,0:T(8,128)S(1)} %get-tuple-element.84), channel_id=1, source_target_pairs={{0,8},{4,12},{8,0},{12,4},{16,24},{20,28},{24,16},{28,20},{1,9},{5... | collective-permute-start | bytes 393224 | tf_op jit(solution)/shard_map/ppermute | solution.py:458
  67.5 1.9 %collective-permute-start.20 = (f32[128,256]{1,0:T(8,128)S(1)}, f32[128,256]{1,0:T(8,128)S(1)}, u32[]{:S(2)}, u32[]{:S(2)}) collective-permute-start(f32[128,256]{1,0:T(8,128)S(1)} %get-tuple-element.85), channel_id=1, source_target_pairs={{0,12},{4,8},{8,4},{12,0},{16,28},{20,24},{24,20},{28,16},{1,13},{... | collective-permute-start | bytes 393224 | tf_op jit(solution)/shard_map/ppermute | solution.py:458
  69.4 9.7 %all_to_all.16.parts_ref = f32[8,8,128]{2,1,0:T(8,128)S(1)} all-to-all(f32[8,8,128]{2,1,0:T(8,128)S(1)} %get-tuple-element.75), channel_id=1, replica_groups=mesh['row'=8,'col'=4] {'row'}, dimensions={0} | all-to-all | bytes 65536 | tf_op jit(solution)/shard_map/all_to_all | solution.py:24
  79.1 1.4 %shard_map.97 = (f32[4,128]{1,0:T(4,128)}, f32[8,128]{1,0:T(8,128)}, f32[128,1024]{1,0:T(8,128)}) custom-call(f32[8,8,128]{2,1,0:T(8,128)S(1)} %all_to_all.16.parts_ref, f32[4,128]{1,0:T(4,128)S(1)} %get-tuple-element.76.refs_3_.left_ref, f32[1,128]{1,0:T(1,128)S(1)} %get-tuple-element.49.order_ref.refs_3_.refs_0_, ...), custom_call_target="tpu_custom_call" | custom-call | tf_op jit(solution)/shard_map/pallas_call | solution.py:570
  (39 shorter events, 3.9 us)
Async XLA Ops:
  0.6 30.3 %copy-start = (f32[512,1024]{1,0:T(8,128)S(1)}, f32[512,1024]{1,0:T(8,128)}, u32[]{:S(2)}) copy-start(f32[512,1024]{1,0:T(8,128)} %design_ref.9) | copy-start | bytes 6291460
  4.0 24.2 %copy-start.4 = (f32[512,128]{1,0:T(8,128)S(1)}, f32[512,128]{1,0:T(8,128)}, u32[]{:S(2)}) copy-start(f32[512,128]{1,0:T(8,128)} %get-tuple-element.64) | copy-start | bytes 786436
  4.0 24.8 %copy-start.3 = (f32[512,128]{1,0:T(8,128)S(1)}, f32[512,128]{1,0:T(8,128)}, u32[]{:S(2)}) copy-start(f32[512,128]{1,0:T(8,128)} %get-tuple-element.65) | copy-start | bytes 786436
  4.0 28.5 %copy-start.2 = (f32[512,128]{1,0:T(8,128)S(1)}, f32[512,128]{1,0:T(8,128)}, u32[]{:S(2)}) copy-start(f32[512,128]{1,0:T(8,128)} %get-tuple-element.67) | copy-start | bytes 786436
  4.0 14.8 %all-to-all-start = ((f32[8,16,128]{2,1,0:T(8,128)}), f32[8,16,128]{2,1,0:T(8,128)S(1)}, u32[]{:S(2)}, u32[]{:S(2)}) async-start(f32[8,16,128]{2,1,0:T(8,128)} %get-tuple-element.46), calls=%async_computation | async-start | bytes 131072 | tf_op jit(solution)/shard_map/all_to_all | solution.py:24
  11.5 14.0 %collective-permute-start = (f32[512,128]{1,0:T(8,128)}, f32[512,128]{1,0:T(8,128)S(1)}, u32[]{:S(2)}, u32[]{:S(2)}) collective-permute-start(f32[512,128]{1,0:T(8,128)} %get-tuple-element.50), channel_id=1, source_target_pairs={{0,4},{4,0},{8,12},{12,8},{16,20},{20,16},{24,28},{28,24},{1,5},{5... | collective-permute-start | bytes 786440 | tf_op jit(solution)/shard_map/ppermute | solution.py:458
  13.5 11.9 %collective-permute-start.1 = (f32[512,128]{1,0:T(8,128)}, f32[512,128]{1,0:T(8,128)S(1)}, u32[]{:S(2)}, u32[]{:S(2)}) collective-permute-start(f32[512,128]{1,0:T(8,128)} %get-tuple-element.51), channel_id=1, source_target_pairs={{0,8},{4,12},{8,0},{12,4},{16,24},{20,28},{24,16},{28,20},{1,9},{5... | collective-permute-start | bytes 786440 | tf_op jit(solution)/shard_map/ppermute | solution.py:458
  18.8 20.7 %copy-start.1 = (f32[512]{0:T(512)S(1)}, f32[512]{0:T(512)}, u32[]{:S(2)}) copy-start(f32[512]{0:T(512)} %param.10) | copy-start | bytes 6148
  18.8 12.2 %collective-permute-start.2 = (f32[512,128]{1,0:T(8,128)}, f32[512,128]{1,0:T(8,128)S(1)}, u32[]{:S(2)}, u32[]{:S(2)}) collective-permute-start(f32[512,128]{1,0:T(8,128)} %get-tuple-element.55), channel_id=1, source_target_pairs={{0,12},{4,8},{8,4},{12,0},{16,28},{20,24},{24,20},{28,16},{1,13},{... | collective-permute-start | bytes 786440 | tf_op jit(solution)/shard_map/ppermute | solution.py:458
  25.4 1.2 %collective-permute-start.4 = (f32[32,128]{1,0:T(8,128)S(1)}, f32[32,128]{1,0:T(8,128)S(1)}, u32[]{:S(2)}, u32[]{:S(2)}) collective-permute-start(f32[32,128]{1,0:T(8,128)S(1)} %shard_map.88), channel_id=1, source_target_pairs={{0,1},{1,0},{2,3},{3,2},{4,5},{5,4},{6,7},{7,6},{8,9},{9,8},{10,11... | collective-permute-start | bytes 49160 | tf_op jit(solution)/shard_map/ppermute | solution.py:31
  26.7 5.8 %collective-permute-start.5 = (f32[32,128]{1,0:T(8,128)S(1)}, f32[32,128]{1,0:T(8,128)S(1)}, u32[]{:S(2)}, u32[]{:S(2)}) collective-permute-start(f32[32,128]{1,0:T(8,128)S(1)} %add.6.refs_0_), channel_id=1, source_target_pairs={{0,2},{1,3},{2,0},{3,1},{4,6},{5,7},{6,4},{7,5},{8,10},{9,11},{10,... | collective-permute-start | bytes 49160 | tf_op jit(solution)/shard_map/ppermute | solution.py:31
  28.2 24.0 %collective-permute-start.8 = (f32[512,128]{1,0:T(8,128)S(1)}, f32[512,128]{1,0:T(8,128)S(1)}, u32[]{:S(2)}, u32[]{:S(2)}) collective-permute-start(f32[512,128]{1,0:T(8,128)S(1)} %copy-done.4), channel_id=1, source_target_pairs={{0,4},{4,0},{8,12},{12,8},{16,20},{20,16},{24,28},{28,24},{1,5},{5... | collective-permute-start | bytes 786440 | tf_op jit(solution)/shard_map/ppermute | solution.py:458
  28.8 23.4 %collective-permute-start.9 = (f32[512,128]{1,0:T(8,128)S(1)}, f32[512,128]{1,0:T(8,128)S(1)}, u32[]{:S(2)}, u32[]{:S(2)}) collective-permute-start(f32[512,128]{1,0:T(8,128)S(1)} %copy-done.3), channel_id=1, source_target_pairs={{0,8},{4,12},{8,0},{12,4},{16,24},{20,28},{24,16},{28,20},{1,9},{5... | collective-permute-start | bytes 786440 | tf_op jit(solution)/shard_map/ppermute | solution.py:458
  32.1 20.1 %collective-permute-start.3 = (f32[1,4,128,128]{3,2,1,0:T(8,128)S(1)}, f32[1,4,128,128]{3,2,1,0:T(8,128)S(1)}, u32[]{:S(2)}, u32[]{:S(2)}) collective-permute-start(f32[1,4,128,128]{3,2,1,0:T(8,128)S(1)} %get-tuple-element.57), channel_id=1, source_target_pairs={{0,16},{4,20},{8,24},{12,28},{16,0},{20,4},{24,8},{28,12},{1,17},{... | collective-permute-start | bytes 786440 | tf_op jit(solution)/shard_map/ppermute | solution.py:458
  32.5 19.7 %collective-permute-start.10 = (f32[512,128]{1,0:T(8,128)S(1)}, f32[512,128]{1,0:T(8,128)S(1)}, u32[]{:S(2)}, u32[]{:S(2)}) collective-permute-start(f32[512,128]{1,0:T(8,128)S(1)} %copy-done.2), channel_id=1, source_target_pairs={{0,12},{4,8},{8,4},{12,0},{16,28},{20,24},{24,20},{28,16},{1,13},{... | collective-permute-start | bytes 786440 | tf_op jit(solution)/shard_map/ppermute | solution.py:458
  34.7 1.2 %collective-permute-start.6 = (f32[4,128]{1,0:T(4,128)S(1)}, f32[4,128]{1,0:T(4,128)S(1)}, u32[]{:S(2)}, u32[]{:S(2)}) collective-permute-start(f32[4,128]{1,0:T(4,128)S(1)} %get-tuple-element.60), channel_id=1, source_target_pairs={{0,1},{1,0},{2,3},{3,2},{4,5},{5,4},{6,7},{7,6},{8,9},{9,8},{10,11... | collective-permute-start | bytes 6152 | tf_op jit(solution)/shard_map/ppermute | solution.py:31
  35.9 3.6 %collective-permute-start.7 = (f32[4,128]{1,0:T(4,128)S(1)}, f32[4,128]{1,0:T(4,128)S(1)}, u32[]{:S(2)}, u32[]{:S(2)}) collective-permute-start(f32[4,128]{1,0:T(4,128)S(1)} %add.7.refs_0_), channel_id=1, source_target_pairs={{0,2},{1,3},{2,0},{3,1},{4,6},{5,7},{6,4},{7,5},{8,10},{9,11},{10,... | collective-permute-start | bytes 6152 | tf_op jit(solution)/shard_map/ppermute | solution.py:31
  53.4 12.4 %collective-permute-start.17 = (f32[1,4,128,128]{3,2,1,0:T(8,128)S(1)}, f32[1,4,128,128]{3,2,1,0:T(8,128)S(1)}, u32[]{:S(2)}, u32[]{:S(2)}) collective-permute-start(f32[1,4,128,128]{3,2,1,0:T(8,128)S(1)} %get-tuple-element.81), channel_id=1, source_target_pairs={{0,16},{4,20},{8,24},{12,28},{16,0},{20,4},{24,8},{28,12},{1,17},{... | collective-permute-start | bytes 786440 | tf_op jit(solution)/shard_map/ppermute | solution.py:458
  55.3 3.2 %collective-permute-start.13 = (f32[32,128]{1,0:T(8,128)S(1)}, f32[32,128]{1,0:T(8,128)S(1)}, u32[]{:S(2)}, u32[]{:S(2)}) collective-permute-start(f32[32,128]{1,0:T(8,128)S(1)} %get-tuple-element.69.refs_0_), channel_id=1, source_target_pairs={{0,3},{1,2},{2,1},{3,0},{4,7},{5,6},{6,5},{7,4},{8,11},{9,10},{10,... | collective-permute-start | bytes 49160 | tf_op jit(solution)/shard_map/ppermute | solution.py:41
  55.4 3.8 %collective-permute-start.12 = (f32[32,128]{1,0:T(8,128)S(1)}, f32[32,128]{1,0:T(8,128)S(1)}, u32[]{:S(2)}, u32[]{:S(2)}) collective-permute-start(f32[32,128]{1,0:T(8,128)S(1)} %get-tuple-element.69.refs_0_), channel_id=1, source_target_pairs={{0,2},{1,3},{2,0},{3,1},{4,6},{5,7},{6,4},{7,5},{8,10},{9,11},{10,... | collective-permute-start | bytes 49160 | tf_op jit(solution)/shard_map/ppermute | solution.py:41
  56.0 3.2 %collective-permute-start.11 = (f32[32,128]{1,0:T(8,128)S(1)}, f32[32,128]{1,0:T(8,128)S(1)}, u32[]{:S(2)}, u32[]{:S(2)}) collective-permute-start(f32[32,128]{1,0:T(8,128)S(1)} %get-tuple-element.69.refs_0_), channel_id=1, source_target_pairs={{0,1},{1,0},{2,3},{3,2},{4,5},{5,4},{6,7},{7,6},{8,9},{9,8},{10,11... | collective-permute-start | bytes 49160 | tf_op jit(solution)/shard_map/ppermute | solution.py:41
  60.9 3.1 %collective-permute-start.16 = (f32[4,128]{1,0:T(4,128)S(1)}, f32[4,128]{1,0:T(4,128)S(1)}, u32[]{:S(2)}, u32[]{:S(2)}) collective-permute-start(f32[4,128]{1,0:T(4,128)S(1)} %get-tuple-element.72.refs_0_), channel_id=1, source_target_pairs={{0,3},{1,2},{2,1},{3,0},{4,7},{5,6},{6,5},{7,4},{8,11},{9,10},{10,... | collective-permute-start | bytes 6152 | tf_op jit(solution)/shard_map/ppermute | solution.py:41
  61.5 3.6 %collective-permute-start.15 = (f32[4,128]{1,0:T(4,128)S(1)}, f32[4,128]{1,0:T(4,128)S(1)}, u32[]{:S(2)}, u32[]{:S(2)}) collective-permute-start(f32[4,128]{1,0:T(4,128)S(1)} %get-tuple-element.72.refs_0_), channel_id=1, source_target_pairs={{0,2},{1,3},{2,0},{3,1},{4,6},{5,7},{6,4},{7,5},{8,10},{9,11},{10,... | collective-permute-start | bytes 6152 | tf_op jit(solution)/shard_map/ppermute | solution.py:41
  62.1 3.0 %collective-permute-start.14 = (f32[4,128]{1,0:T(4,128)S(1)}, f32[4,128]{1,0:T(4,128)S(1)}, u32[]{:S(2)}, u32[]{:S(2)}) collective-permute-start(f32[4,128]{1,0:T(4,128)S(1)} %get-tuple-element.72.refs_0_), channel_id=1, source_target_pairs={{0,1},{1,0},{2,3},{3,2},{4,5},{5,4},{6,7},{7,6},{8,9},{9,8},{10,11... | collective-permute-start | bytes 6152 | tf_op jit(solution)/shard_map/ppermute | solution.py:41
  65.8 13.3 %collective-permute-start.18 = (f32[128,256]{1,0:T(8,128)S(1)}, f32[128,256]{1,0:T(8,128)S(1)}, u32[]{:S(2)}, u32[]{:S(2)}) collective-permute-start(f32[128,256]{1,0:T(8,128)S(1)} %get-tuple-element.83), channel_id=1, source_target_pairs={{0,4},{4,0},{8,12},{12,8},{16,20},{20,16},{24,28},{28,24},{1,5},{5... | collective-permute-start | bytes 393224 | tf_op jit(solution)/shard_map/ppermute | solution.py:458
  66.7 12.5 %collective-permute-start.19 = (f32[128,256]{1,0:T(8,128)S(1)}, f32[128,256]{1,0:T(8,128)S(1)}, u32[]{:S(2)}, u32[]{:S(2)}) collective-permute-start(f32[128,256]{1,0:T(8,128)S(1)} %get-tuple-element.84), channel_id=1, source_target_pairs={{0,8},{4,12},{8,0},{12,4},{16,24},{20,28},{24,16},{28,20},{1,9},{5... | collective-permute-start | bytes 393224 | tf_op jit(solution)/shard_map/ppermute | solution.py:458
  67.5 11.6 %collective-permute-start.20 = (f32[128,256]{1,0:T(8,128)S(1)}, f32[128,256]{1,0:T(8,128)S(1)}, u32[]{:S(2)}, u32[]{:S(2)}) collective-permute-start(f32[128,256]{1,0:T(8,128)S(1)} %get-tuple-element.85), channel_id=1, source_target_pairs={{0,12},{4,8},{8,4},{12,0},{16,28},{20,24},{24,20},{28,16},{1,13},{... | collective-permute-start | bytes 393224 | tf_op jit(solution)/shard_map/ppermute | solution.py:458

commit v20 on v19

--- a/solution.py
+++ b/solution.py
@@ -382,15 +382,14 @@
 
 
 def last_body(parts_ref, left_ref, *refs):
-    basis_ref, solution_ref, sketch_ref, sems = refs[-4:]
+    basis_ref, solution_ref, sketch_ref = refs[-3:]
     quarters = refs[3 * ITERS : 3 * ITERS + NEAR]
     place = lax.axis_index("row") % NEAR
     piece = quarters[0].shape[1]
-    copies = []
     for mask, part_ref in enumerate(quarters):
-        columns = pl.ds(pl.multiple_of((place ^ mask) * piece, LANE), piece)
-        copies.append(pltpu.make_async_copy(part_ref, sketch_ref.at[:, columns], sems.at[mask]))
-        copies[-1].start()
+        for tile in range(0, piece, LANE):
+            column = pl.multiple_of((place ^ mask) * piece + tile, LANE)
+            sketch_ref[:, pl.ds(column, LANE)] = part_ref[:, tile : tile + LANE]
     betas = [ref[...] for ref in refs[:ITERS]]
     alphas = [ref[...] for ref in refs[ITERS : 2 * ITERS]]
     held = [ref[...] for ref in refs[2 * ITERS : 3 * ITERS]]
@@ -412,8 +411,6 @@
             search = held[step + 1] - sine * alpha / rho * search
             rhobar = -cosine * alpha
     solution_ref[...] = iterate
-    for copy in copies:
-        copy.wait()
 
 
 def shape(*dims, dtype=F32):
@@ -528,10 +525,10 @@
         )
 
     betas, alphas, held, joined, right = [], [], [], [], []
-    near = spread(range(NEAR - 2), None)
+    near = spread(range(NEAR - 1), None)
     message = picked = exchange(message, "row")
     late = len(sent) - (chunks > 1)
-    near += spread(range(NEAR - 2, late), message)
+    near += spread(range(NEAR - 1, late), message)
     for step in range(ITERS):
         last = step + 1 == ITERS
         if step == 0:
@@ -539,10 +536,10 @@
             term = pl.pallas_call(
                 pass_body,
                 out_shape=shape(*term.shape),
-                in_specs=[ANY] * (NEAR - 2) + [VMEM],
+                in_specs=[ANY] * (NEAR - 1) + [VMEM],
                 out_specs=VMEM,
                 compiler_params=pltpu.CompilerParams(vmem_limit_bytes=2 << 20),
-            )(*near[: NEAR - 2], term)
+            )(*near[: NEAR - 1], term)
         else:
             term, beta = back(here, message, False)
             token = beta
@@ -566,15 +563,17 @@
         message = exchange(message, "row")
     quarters = (shape(slots, width // NEAR),) * NEAR
     mine, *others = call(split_body, quarters, *joined, *halve(keep, come, beta), left)
-    quarters = [mine] + [swap(part, mask + 1) for mask, part in enumerate(others)]
-    basis, answer, sketch = pl.pallas_call(
+    basis, answer, sketch = call(
         last_body,
-        out_shape=(shape(lines, LANE), shape(width // LANE, LANE), shape(slots, width)),
-        in_specs=[VMEM] * (2 + 3 * ITERS + NEAR),
-        out_specs=(VMEM, VMEM, HBM),
-        scratch_shapes=[pltpu.SemaphoreType.DMA((NEAR,))],
-        compiler_params=pltpu.CompilerParams(vmem_limit_bytes=24 << 20),
-    )(message, left, *betas, *alphas, *held, *quarters)
+        (shape(lines, LANE), shape(width // LANE, LANE), shape(slots, width)),
+        message,
+        left,
+        *betas,
+        *alphas,
+        *held,
+        mine,
+        *(swap(part, mask + 1) for mask, part in enumerate(others)),
+    )
     return (sketch, answer.reshape(-1), basis.reshape(-1))
 
 

time: 80.9 us -> 83.7 us (1.035)
  blocking collectives: 22.1 us -> 35.7 us
  starting transfers between devices: 26 us -> 18.9 us
  waiting for transfers between devices: 13.4 us -> 10.4 us
    all_to_all x2 -> x3, blocking collectives: 22.1 us -> 35.7 us  [exchange(): return lax.all_to_all(copies, axis, split_axis=0, concat_axis=0, tiled=True)]
    all_to_all x1 -> x0, starting transfers between devices: 7.42 us -> none  [exchange(): return lax.all_to_all(copies, axis, split_axis=0, concat_axis=0, tiled=True)]
    all_to_all x1 -> x0, waiting for transfers between devices: 3.84 us -> none  [exchange(): return lax.all_to_all(copies, axis, split_axis=0, concat_axis=0, tiled=True)]
    pallas_call x1 -> x0, Pallas kernels: 1.43 us -> none  [shards(): pl.pallas_call(last_body, out_shape=(shape(lines, LANE), shape(width // L...]
    pallas_call x8 -> x9, Pallas kernels: 6.06 us -> 6.97 us  [call(): pl.pallas_call(body, out_shape=out_shape, in_specs=[VMEM] * len(operands)...]
    ppermute x11, starting transfers between devices: 12 us -> 12.9 us  [swap(): lax.ppermute(array, 'row', [(i, i ^ mask) for i in range(row_groups)])]
  transfers between devices with their start and end apart: 22 -> 21, of which waited for: 9 -> 8; matrix products, arithmetic and copies ran while one was open for 0% -> 0% of each run, Pallas kernels for 15% -> 15%
where the time goes in v20:
time: 83.7 us; the launch traced here: 83.5 us
  blocking collectives  35.7 us (43%)
  starting transfers between devices  18.9 us (23%)
  Pallas kernels  17.6 us (21%)
  waiting for transfers between devices  10.4 us (12%)
    all_to_all x3, blocking collectives, exchange(): return lax.all_to_all(copies, axis, split_axis=0, concat_axis=0, tiled=True)  35.7 us
    ppermute x11, starting transfers between devices, swap(): lax.ppermute(array, 'row', [(i, i ^ mask) for i in range(row_groups)])  12.9 us
    pallas_call x2, Pallas kernels, back(): pl.pallas_call(functools.partial(back_body, first), out_shape=outs, in_sp...  7.28 us
    pallas_call x9, Pallas kernels, call(): pl.pallas_call(body, out_shape=out_shape, in_specs=[VMEM] * len(operands)...  6.97 us
    ppermute x4, waiting for transfers between devices, paired(): come = lax.ppermute(array, axis, [(i, i ^ mask) for i in range(size)])  5.36 us
    ppermute x6, waiting for transfers between devices, direct(): lax.ppermute(array, axis, [(i, i ^ mask) for i in range(size)])  4.2 us
    ppermute x6, starting transfers between devices, direct(): lax.ppermute(array, axis, [(i, i ^ mask) for i in range(size)])  3.85 us
    pallas_call x1, Pallas kernels, shards(): pl.pallas_call(functools.partial(first_body, sent), out_shape=(shape(row_...  3.34 us
  transfers between devices with their start and end apart: 21, of which 8 were waited for; matrix products, arithmetic and copies ran while one was open for 0% of the time, Pallas kernels for 15%

profile of v20, /device:TPU:0, one launch (start us, length us, event | category | flops | bytes accessed | tf_op | source)
XLA Modules:
  0.0 83.5 jit_solution(4533175091198931944)
XLA Ops:
  0.6 3.3 %shard_map.85 = (f32[8,16,128]{2,1,0:T(8,128)}, f32[512,128]{1,0:T(8,128)}, f32[512,128]{1,0:T(8,128)}, f32[512,128]{1,0:T(8,128)}, f32[512,128]{1,0:T(8,128)}, /*index=5*/f32[512,128]{1,0:T(8,128)}, f32[512,128]{1,0:T(8,128)}) custom-call(f32[512,1024]{1,0:T(8,128)} %design_ref.9, f32[4,128]{1,0:T(4,128)} %bitcast.6, s32[4,128]{1,0:T(4,128)} %bitcast.9, ...), custom_call_target="tpu_custom_call" | custom-call | tf_op jit(solution)/shard_map/pallas_call | solution.py:437
  4.0 3.0 %collective-permute-start = (f32[512,128]{1,0:T(8,128)}, f32[512,128]{1,0:T(8,128)S(1)}, u32[]{:S(2)}, u32[]{:S(2)}) collective-permute-start(f32[512,128]{1,0:T(8,128)} %get-tuple-element.49), channel_id=1, source_target_pairs={{0,4},{4,0},{8,12},{12,8},{16,20},{20,16},{24,28},{28,24},{1,5},{5... | collective-permute-start | bytes 786440 | tf_op jit(solution)/shard_map/ppermute | solution.py:455
  7.1 1.6 %collective-permute-start.1 = (f32[512,128]{1,0:T(8,128)}, f32[512,128]{1,0:T(8,128)S(1)}, u32[]{:S(2)}, u32[]{:S(2)}) collective-permute-start(f32[512,128]{1,0:T(8,128)} %get-tuple-element.50), channel_id=1, source_target_pairs={{0,8},{4,12},{8,0},{12,4},{16,24},{20,28},{24,16},{28,20},{1,9},{5... | collective-permute-start | bytes 786440 | tf_op jit(solution)/shard_map/ppermute | solution.py:455
  8.6 15.0 %all_to_all.15.parts_ref = f32[8,16,128]{2,1,0:T(8,128)S(1)} all-to-all(f32[8,16,128]{2,1,0:T(8,128)} %get-tuple-element.45), channel_id=1, replica_groups=mesh['row'=8,'col'=4] {'row'}, dimensions={0} | all-to-all | bytes 131072 | tf_op jit(solution)/shard_map/all_to_all | solution.py:24
  23.6 5.9 %shard_map.86 = (f32[32,128]{1,0:T(8,128)S(1)}, f32[1,128]{1,0:T(1,128)S(1)}, bf16[8,128,512]{2,1,0:T(8,128)(2,1)S(1)}, f32[1024,4096]{1,0:T(8,128)S(1)}) custom-call(f32[1024,4096]{1,0:T(8,128)} %rinv_ref.1, f32[8,16,128]{2,1,0:T(8,128)S(1)} %all_to_all.15.parts_ref), custom_call_target="tpu_custom_call" | custom-call | tf_op jit(solution)/shard_map/pallas_call | solution.py:495
  29.6 1.2 %collective-permute-done.4 = f32[32,128]{1,0:T(8,128)S(1)} collective-permute-done((f32[32,128]{1,0:T(8,128)S(1)}, f32[32,128]{1,0:T(8,128)S(1)}, u32[]{:S(2)}, u32[]{:S(2)}) %collective-permute-start.4) | collective-permute-done | bytes 16416 | tf_op jit(solution)/shard_map/ppermute | solution.py:31
  30.8 1.5 %collective-permute-start.5 = (f32[32,128]{1,0:T(8,128)S(1)}, f32[32,128]{1,0:T(8,128)S(1)}, u32[]{:S(2)}, u32[]{:S(2)}) collective-permute-start(f32[32,128]{1,0:T(8,128)S(1)} %add.6.refs_0_), channel_id=1, source_target_pairs={{0,2},{1,3},{2,0},{3,1},{4,6},{5,7},{6,4},{7,5},{8,10},{9,11},{10,... | collective-permute-start | bytes 49160 | tf_op jit(solution)/shard_map/ppermute | solution.py:31
  32.3 1.3 %collective-permute-start.8 = (f32[512,128]{1,0:T(8,128)S(1)}, f32[512,128]{1,0:T(8,128)S(1)}, u32[]{:S(2)}, u32[]{:S(2)}) collective-permute-start(f32[512,128]{1,0:T(8,128)S(1)} %copy-done.4), channel_id=1, source_target_pairs={{0,4},{4,0},{8,12},{12,8},{16,20},{20,16},{24,28},{28,24},{1,5},{5... | collective-permute-start | bytes 786440 | tf_op jit(solution)/shard_map/ppermute | solution.py:455
  33.6 0.8 collective-permute-start.9
  34.4 1.1 %shard_map.87 = (f32[1,4,128,128]{3,2,1,0:T(8,128)S(1)}, f32[1,4,128,128]{3,2,1,0:T(8,128)S(1)}, f32[1,128]{1,0:T(1,128)S(1)}) custom-call(f32[512,1024]{1,0:T(8,128)S(1)} %copy-done, f32[8,16,128]{2,1,0:T(8,128)S(1)} %all_to_all.15.parts_ref, bf16[8,128,512]{2,1,0:T(8,128)(2,1)S(1)} %get-tuple-element.47.mix_ref, ...), custom_call_target="tpu_custom_call" | custom-call | tf_op jit(solution)/shard_map/pallas_call | solution.py:59
  35.5 1.6 %collective-permute-start.3 = (f32[1,4,128,128]{3,2,1,0:T(8,128)S(1)}, f32[1,4,128,128]{3,2,1,0:T(8,128)S(1)}, u32[]{:S(2)}, u32[]{:S(2)}) collective-permute-start(f32[1,4,128,128]{3,2,1,0:T(8,128)S(1)} %get-tuple-element.53), channel_id=1, source_target_pairs={{0,16},{4,20},{8,24},{12,28},{16,0},{20,4},{24,8},{28,12},{1,17},{... | collective-permute-start | bytes 786440 | tf_op jit(solution)/shard_map/ppermute | solution.py:455
  37.5 1.7 %shard_map.89 = (f32[4,128]{1,0:T(4,128)S(1)}, f32[8,128]{1,0:T(8,128)S(1)}, f32[1,128]{1,0:T(1,128)S(1)}, f32[32,128]{1,0:T(8,128)S(1)}) custom-call(f32[1024,4096]{1,0:T(8,128)S(1)} %get-tuple-element.46.rinv_ref, f32[512,1024]{1,0:T(8,128)S(1)} %copy-done, f32[1,128]{1,0:T(1,128)S(1)} %get-tuple-element.54.token_ref, f32[32,128]{1,0:T(8,128)S(1)} %add.6.refs_0_, ...), custom_call_target="tpu_custom_call" | custom-call | tf_op jit(solution)/shard_map/pallas_call | solution.py:59
  39.3 1.1 %collective-permute-done.6 = f32[4,128]{1,0:T(4,128)S(1)} collective-permute-done((f32[4,128]{1,0:T(4,128)S(1)}, f32[4,128]{1,0:T(4,128)S(1)}, u32[]{:S(2)}, u32[]{:S(2)}) %collective-permute-start.6) | collective-permute-done | bytes 2080 | tf_op jit(solution)/shard_map/ppermute | solution.py:31
  41.0 3.0 %collective-permute-done.7.refs_1_ = f32[4,128]{1,0:T(4,128)S(1)} collective-permute-done((f32[4,128]{1,0:T(4,128)S(1)}, f32[4,128]{1,0:T(4,128)S(1)}, u32[]{:S(2)}, u32[]{:S(2)}) %collective-permute-start.7) | collective-permute-done | bytes 2080 | tf_op jit(solution)/shard_map/ppermute | solution.py:31
  44.3 11.3 %all_to_all.16.order_ref.parts_ref = f32[8,16,128]{2,1,0:T(8,128)S(1)} all-to-all(f32[8,16,128]{2,1,0:T(8,128)S(1)} %get-tuple-element.58), channel_id=1, replica_groups=mesh['row'=8,'col'=4] {'row'}, dimensions={0} | all-to-all | bytes 131072 | tf_op jit(solution)/shard_map/all_to_all | solution.py:24
  55.7 1.1 %shard_map.92 = (f32[1,4,128,128]{3,2,1,0:T(8,128)S(1)}, f32[1,4,128,128]{3,2,1,0:T(8,128)S(1)}, f32[1,128]{1,0:T(1,128)S(1)}) custom-call(f32[512,1024]{1,0:T(8,128)S(1)} %copy-done, f32[8,16,128]{2,1,0:T(8,128)S(1)} %all_to_all.15.parts_ref, bf16[8,128,512]{2,1,0:T(8,128)(2,1)S(1)} %get-tuple-element.47.mix_ref, f32[1,128]{1,0:T(1,128)S(1)} %get-tuple-element.59.order_ref, ...), custom_call_target="tpu_custom_call" | custom-call | tf_op jit(solution)/shard_map/pallas_call | solution.py:59
  57.3 1.4 %shard_map.93 = (f32[32,128]{1,0:T(8,128)S(1)}, f32[1,128]{1,0:T(1,128)S(1)}) custom-call(f32[1024,4096]{1,0:T(8,128)S(1)} %get-tuple-element.46.rinv_ref, f32[8,16,128]{2,1,0:T(8,128)S(1)} %all_to_all.16.order_ref.parts_ref), custom_call_target="tpu_custom_call" | custom-call | tf_op jit(solution)/shard_map/pallas_call | solution.py:495
  58.8 0.6 collective-permute-start.12
  59.4 1.3 %collective-permute-start.11 = (f32[32,128]{1,0:T(8,128)S(1)}, f32[32,128]{1,0:T(8,128)S(1)}, u32[]{:S(2)}, u32[]{:S(2)}) collective-permute-start(f32[32,128]{1,0:T(8,128)S(1)} %get-tuple-element.67.refs_0_), channel_id=1, source_target_pairs={{0,1},{1,0},{2,3},{3,2},{4,5},{5,4},{6,7},{7,6},{8,9},{9,8},{10,11... | collective-permute-start | bytes 49160 | tf_op jit(solution)/shard_map/ppermute | solution.py:41
  60.7 1.3 %collective-permute-done.13.refs_3_ = f32[32,128]{1,0:T(8,128)S(1)} collective-permute-done((f32[32,128]{1,0:T(8,128)S(1)}, f32[32,128]{1,0:T(8,128)S(1)}, u32[]{:S(2)}, u32[]{:S(2)}) %collective-permute-start.13) | collective-permute-done | bytes 16416 | tf_op jit(solution)/shard_map/ppermute | solution.py:41
  62.0 0.7 collective-permute-done.12.refs_2_
  62.7 1.7 %shard_map.94 = (f32[4,128]{1,0:T(4,128)S(1)}, f32[8,128]{1,0:T(8,128)S(1)}, f32[1,128]{1,0:T(1,128)S(1)}) custom-call(f32[1024,4096]{1,0:T(8,128)S(1)} %get-tuple-element.46.rinv_ref, f32[512,1024]{1,0:T(8,128)S(1)} %copy-done, f32[1,128]{1,0:T(1,128)S(1)} %get-tuple-element.66.token_ref, f32[32,128]{1,0:T(8,128)S(1)} %get-tuple-element.67.refs_0_, ...), custom_call_target="tpu_custom_call" | custom-call | tf_op jit(solution)/shard_map/pallas_call | solution.py:59
  64.4 0.6 collective-permute-start.16
  65.5 0.8 collective-permute-start.14
  66.3 1.1 %collective-permute-done.16.refs_3_ = f32[4,128]{1,0:T(4,128)S(1)} collective-permute-done((f32[4,128]{1,0:T(4,128)S(1)}, f32[4,128]{1,0:T(4,128)S(1)}, u32[]{:S(2)}, u32[]{:S(2)}) %collective-permute-start.16) | collective-permute-done | bytes 2080 | tf_op jit(solution)/shard_map/ppermute | solution.py:41
  67.5 1.1 %collective-permute-done.15.refs_2_ = f32[4,128]{1,0:T(4,128)S(1)} collective-permute-done((f32[4,128]{1,0:T(4,128)S(1)}, f32[4,128]{1,0:T(4,128)S(1)}, u32[]{:S(2)}, u32[]{:S(2)}) %collective-permute-start.15) | collective-permute-done | bytes 2080 | tf_op jit(solution)/shard_map/ppermute | solution.py:41
  68.6 0.8 collective-permute-done.17.refs_2_
  69.5 0.7 collective-permute-start.18
  70.2 0.7 collective-permute-start.19
  70.9 2.2 %collective-permute-start.20 = (f32[128,256]{1,0:T(8,128)S(1)}, f32[128,256]{1,0:T(8,128)S(1)}, u32[]{:S(2)}, u32[]{:S(2)}) collective-permute-start(f32[128,256]{1,0:T(8,128)S(1)} %get-tuple-element.83), channel_id=1, source_target_pairs={{0,12},{4,8},{8,4},{12,0},{16,28},{20,24},{24,20},{28,16},{1,13},{... | collective-permute-start | bytes 393224 | tf_op jit(solution)/shard_map/ppermute | solution.py:455
  73.1 9.5 %all_to_all.17.parts_ref = f32[8,8,128]{2,1,0:T(8,128)S(1)} all-to-all(f32[8,8,128]{2,1,0:T(8,128)S(1)} %get-tuple-element.73), channel_id=1, replica_groups=mesh['row'=8,'col'=4] {'row'}, dimensions={0} | all-to-all | bytes 65536 | tf_op jit(solution)/shard_map/all_to_all | solution.py:24
  82.6 0.9 %shard_map.97 = (f32[4,128]{1,0:T(4,128)}, f32[8,128]{1,0:T(8,128)}, f32[128,1024]{1,0:T(8,128)}) custom-call(f32[8,8,128]{2,1,0:T(8,128)S(1)} %all_to_all.17.parts_ref, f32[4,128]{1,0:T(4,128)S(1)} %get-tuple-element.74.refs_3_.left_ref, f32[1,128]{1,0:T(1,128)S(1)} %get-tuple-element.48.order_ref.refs_3_.refs_0_, ...), custom_call_target="tpu_custom_call" | custom-call | tf_op jit(solution)/shard_map/pallas_call | solution.py:59
  (38 shorter events, 2.8 us)
Async XLA Ops:
  0.6 33.8 %copy-start = (f32[512,1024]{1,0:T(8,128)S(1)}, f32[512,1024]{1,0:T(8,128)}, u32[]{:S(2)}) copy-start(f32[512,1024]{1,0:T(8,128)} %design_ref.9) | copy-start | bytes 6291460
  4.0 28.3 %copy-start.4 = (f32[512,128]{1,0:T(8,128)S(1)}, f32[512,128]{1,0:T(8,128)}, u32[]{:S(2)}) copy-start(f32[512,128]{1,0:T(8,128)} %get-tuple-element.62) | copy-start | bytes 786436
  4.0 29.6 %copy-start.3 = (f32[512,128]{1,0:T(8,128)S(1)}, f32[512,128]{1,0:T(8,128)}, u32[]{:S(2)}) copy-start(f32[512,128]{1,0:T(8,128)} %get-tuple-element.63) | copy-start | bytes 786436
  4.0 33.1 %copy-start.2 = (f32[512,128]{1,0:T(8,128)S(1)}, f32[512,128]{1,0:T(8,128)}, u32[]{:S(2)}) copy-start(f32[512,128]{1,0:T(8,128)} %get-tuple-element.65) | copy-start | bytes 786436
  4.0 25.5 %collective-permute-start = (f32[512,128]{1,0:T(8,128)}, f32[512,128]{1,0:T(8,128)S(1)}, u32[]{:S(2)}, u32[]{:S(2)}) collective-permute-start(f32[512,128]{1,0:T(8,128)} %get-tuple-element.49), channel_id=1, source_target_pairs={{0,4},{4,0},{8,12},{12,8},{16,20},{20,16},{24,28},{28,24},{1,5},{5... | collective-permute-start | bytes 786440 | tf_op jit(solution)/shard_map/ppermute | solution.py:455
  7.1 22.4 %collective-permute-start.1 = (f32[512,128]{1,0:T(8,128)}, f32[512,128]{1,0:T(8,128)S(1)}, u32[]{:S(2)}, u32[]{:S(2)}) collective-permute-start(f32[512,128]{1,0:T(8,128)} %get-tuple-element.50), channel_id=1, source_target_pairs={{0,8},{4,12},{8,0},{12,4},{16,24},{20,28},{24,16},{28,20},{1,9},{5... | collective-permute-start | bytes 786440 | tf_op jit(solution)/shard_map/ppermute | solution.py:455
  8.6 20.9 %collective-permute-start.2 = (f32[512,128]{1,0:T(8,128)}, f32[512,128]{1,0:T(8,128)S(1)}, u32[]{:S(2)}, u32[]{:S(2)}) collective-permute-start(f32[512,128]{1,0:T(8,128)} %get-tuple-element.51), channel_id=1, source_target_pairs={{0,12},{4,8},{8,4},{12,0},{16,28},{20,24},{24,20},{28,16},{1,13},{... | collective-permute-start | bytes 786440 | tf_op jit(solution)/shard_map/ppermute | solution.py:455
  23.6 20.5 %copy-start.1 = (f32[512]{0:T(512)S(1)}, f32[512]{0:T(512)}, u32[]{:S(2)}) copy-start(f32[512]{0:T(512)} %param.10) | copy-start | bytes 6148
  29.5 1.2 %collective-permute-start.4 = (f32[32,128]{1,0:T(8,128)S(1)}, f32[32,128]{1,0:T(8,128)S(1)}, u32[]{:S(2)}, u32[]{:S(2)}) collective-permute-start(f32[32,128]{1,0:T(8,128)S(1)} %shard_map.88), channel_id=1, source_target_pairs={{0,1},{1,0},{2,3},{3,2},{4,5},{5,4},{6,7},{7,6},{8,9},{9,8},{10,11... | collective-permute-start | bytes 49160 | tf_op jit(solution)/shard_map/ppermute | solution.py:31
  30.8 6.3 %collective-permute-start.5 = (f32[32,128]{1,0:T(8,128)S(1)}, f32[32,128]{1,0:T(8,128)S(1)}, u32[]{:S(2)}, u32[]{:S(2)}) collective-permute-start(f32[32,128]{1,0:T(8,128)S(1)} %add.6.refs_0_), channel_id=1, source_target_pairs={{0,2},{1,3},{2,0},{3,1},{4,6},{5,7},{6,4},{7,5},{8,10},{9,11},{10,... | collective-permute-start | bytes 49160 | tf_op jit(solution)/shard_map/ppermute | solution.py:31
  32.3 23.4 %collective-permute-start.8 = (f32[512,128]{1,0:T(8,128)S(1)}, f32[512,128]{1,0:T(8,128)S(1)}, u32[]{:S(2)}, u32[]{:S(2)}) collective-permute-start(f32[512,128]{1,0:T(8,128)S(1)} %copy-done.4), channel_id=1, source_target_pairs={{0,4},{4,0},{8,12},{12,8},{16,20},{20,16},{24,28},{28,24},{1,5},{5... | collective-permute-start | bytes 786440 | tf_op jit(solution)/shard_map/ppermute | solution.py:455
  33.6 22.1 %collective-permute-start.9 = (f32[512,128]{1,0:T(8,128)S(1)}, f32[512,128]{1,0:T(8,128)S(1)}, u32[]{:S(2)}, u32[]{:S(2)}) collective-permute-start(f32[512,128]{1,0:T(8,128)S(1)} %copy-done.3), channel_id=1, source_target_pairs={{0,8},{4,12},{8,0},{12,4},{16,24},{20,28},{24,16},{28,20},{1,9},{5... | collective-permute-start | bytes 786440 | tf_op jit(solution)/shard_map/ppermute | solution.py:455
  35.5 20.1 %collective-permute-start.3 = (f32[1,4,128,128]{3,2,1,0:T(8,128)S(1)}, f32[1,4,128,128]{3,2,1,0:T(8,128)S(1)}, u32[]{:S(2)}, u32[]{:S(2)}) collective-permute-start(f32[1,4,128,128]{3,2,1,0:T(8,128)S(1)} %get-tuple-element.53), channel_id=1, source_target_pairs={{0,16},{4,20},{8,24},{12,28},{16,0},{20,4},{24,8},{28,12},{1,17},{... | collective-permute-start | bytes 786440 | tf_op jit(solution)/shard_map/ppermute | solution.py:455
  37.1 18.6 %collective-permute-start.10 = (f32[512,128]{1,0:T(8,128)S(1)}, f32[512,128]{1,0:T(8,128)S(1)}, u32[]{:S(2)}, u32[]{:S(2)}) collective-permute-start(f32[512,128]{1,0:T(8,128)S(1)} %copy-done.2), channel_id=1, source_target_pairs={{0,12},{4,8},{8,4},{12,0},{16,28},{20,24},{24,20},{28,16},{1,13},{... | collective-permute-start | bytes 786440 | tf_op jit(solution)/shard_map/ppermute | solution.py:455
  39.3 1.2 %collective-permute-start.6 = (f32[4,128]{1,0:T(4,128)S(1)}, f32[4,128]{1,0:T(4,128)S(1)}, u32[]{:S(2)}, u32[]{:S(2)}) collective-permute-start(f32[4,128]{1,0:T(4,128)S(1)} %get-tuple-element.56), channel_id=1, source_target_pairs={{0,1},{1,0},{2,3},{3,2},{4,5},{5,4},{6,7},{7,6},{8,9},{9,8},{10,11... | collective-permute-start | bytes 6152 | tf_op jit(solution)/shard_map/ppermute | solution.py:31
  40.5 3.6 %collective-permute-start.7 = (f32[4,128]{1,0:T(4,128)S(1)}, f32[4,128]{1,0:T(4,128)S(1)}, u32[]{:S(2)}, u32[]{:S(2)}) collective-permute-start(f32[4,128]{1,0:T(4,128)S(1)} %add.7.refs_0_), channel_id=1, source_target_pairs={{0,2},{1,3},{2,0},{3,1},{4,6},{5,7},{6,4},{7,5},{8,10},{9,11},{10,... | collective-permute-start | bytes 6152 | tf_op jit(solution)/shard_map/ppermute | solution.py:31
  56.8 12.7 %collective-permute-start.17 = (f32[1,4,128,128]{3,2,1,0:T(8,128)S(1)}, f32[1,4,128,128]{3,2,1,0:T(8,128)S(1)}, u32[]{:S(2)}, u32[]{:S(2)}) collective-permute-start(f32[1,4,128,128]{3,2,1,0:T(8,128)S(1)} %get-tuple-element.79), channel_id=1, source_target_pairs={{0,16},{4,20},{8,24},{12,28},{16,0},{20,4},{24,8},{28,12},{1,17},{... | collective-permute-start | bytes 786440 | tf_op jit(solution)/shard_map/ppermute | solution.py:455
  58.8 3.2 %collective-permute-start.13 = (f32[32,128]{1,0:T(8,128)S(1)}, f32[32,128]{1,0:T(8,128)S(1)}, u32[]{:S(2)}, u32[]{:S(2)}) collective-permute-start(f32[32,128]{1,0:T(8,128)S(1)} %get-tuple-element.67.refs_0_), channel_id=1, source_target_pairs={{0,3},{1,2},{2,1},{3,0},{4,7},{5,6},{6,5},{7,4},{8,11},{9,10},{10,... | collective-permute-start | bytes 49160 | tf_op jit(solution)/shard_map/ppermute | solution.py:41
  58.8 3.8 %collective-permute-start.12 = (f32[32,128]{1,0:T(8,128)S(1)}, f32[32,128]{1,0:T(8,128)S(1)}, u32[]{:S(2)}, u32[]{:S(2)}) collective-permute-start(f32[32,128]{1,0:T(8,128)S(1)} %get-tuple-element.67.refs_0_), channel_id=1, source_target_pairs={{0,2},{1,3},{2,0},{3,1},{4,6},{5,7},{6,4},{7,5},{8,10},{9,11},{10,... | collective-permute-start | bytes 49160 | tf_op jit(solution)/shard_map/ppermute | solution.py:41
  59.4 3.2 %collective-permute-start.11 = (f32[32,128]{1,0:T(8,128)S(1)}, f32[32,128]{1,0:T(8,128)S(1)}, u32[]{:S(2)}, u32[]{:S(2)}) collective-permute-start(f32[32,128]{1,0:T(8,128)S(1)} %get-tuple-element.67.refs_0_), channel_id=1, source_target_pairs={{0,1},{1,0},{2,3},{3,2},{4,5},{5,4},{6,7},{7,6},{8,9},{9,8},{10,11... | collective-permute-start | bytes 49160 | tf_op jit(solution)/shard_map/ppermute | solution.py:41
  64.4 3.1 %collective-permute-start.16 = (f32[4,128]{1,0:T(4,128)S(1)}, f32[4,128]{1,0:T(4,128)S(1)}, u32[]{:S(2)}, u32[]{:S(2)}) collective-permute-start(f32[4,128]{1,0:T(4,128)S(1)} %get-tuple-element.70.refs_0_), channel_id=1, source_target_pairs={{0,3},{1,2},{2,1},{3,0},{4,7},{5,6},{6,5},{7,4},{8,11},{9,10},{10,... | collective-permute-start | bytes 6152 | tf_op jit(solution)/shard_map/ppermute | solution.py:41
  65.0 3.6 %collective-permute-start.15 = (f32[4,128]{1,0:T(4,128)S(1)}, f32[4,128]{1,0:T(4,128)S(1)}, u32[]{:S(2)}, u32[]{:S(2)}) collective-permute-start(f32[4,128]{1,0:T(4,128)S(1)} %get-tuple-element.70.refs_0_), channel_id=1, source_target_pairs={{0,2},{1,3},{2,0},{3,1},{4,6},{5,7},{6,4},{7,5},{8,10},{9,11},{10,... | collective-permute-start | bytes 6152 | tf_op jit(solution)/shard_map/ppermute | solution.py:41
  65.5 3.0 %collective-permute-start.14 = (f32[4,128]{1,0:T(4,128)S(1)}, f32[4,128]{1,0:T(4,128)S(1)}, u32[]{:S(2)}, u32[]{:S(2)}) collective-permute-start(f32[4,128]{1,0:T(4,128)S(1)} %get-tuple-element.70.refs_0_), channel_id=1, source_target_pairs={{0,1},{1,0},{2,3},{3,2},{4,5},{5,4},{6,7},{7,6},{8,9},{9,8},{10,11... | collective-permute-start | bytes 6152 | tf_op jit(solution)/shard_map/ppermute | solution.py:41
  69.5 13.0 %collective-permute-start.18 = (f32[128,256]{1,0:T(8,128)S(1)}, f32[128,256]{1,0:T(8,128)S(1)}, u32[]{:S(2)}, u32[]{:S(2)}) collective-permute-start(f32[128,256]{1,0:T(8,128)S(1)} %get-tuple-element.81), channel_id=1, source_target_pairs={{0,4},{4,0},{8,12},{12,8},{16,20},{20,16},{24,28},{28,24},{1,5},{5... | collective-permute-start | bytes 393224 | tf_op jit(solution)/shard_map/ppermute | solution.py:455
  70.2 12.3 %collective-permute-start.19 = (f32[128,256]{1,0:T(8,128)S(1)}, f32[128,256]{1,0:T(8,128)S(1)}, u32[]{:S(2)}, u32[]{:S(2)}) collective-permute-start(f32[128,256]{1,0:T(8,128)S(1)} %get-tuple-element.82), channel_id=1, source_target_pairs={{0,8},{4,12},{8,0},{12,4},{16,24},{20,28},{24,16},{28,20},{1,9},{5... | collective-permute-start | bytes 393224 | tf_op jit(solution)/shard_map/ppermute | solution.py:455
  70.9 11.6 %collective-permute-start.20 = (f32[128,256]{1,0:T(8,128)S(1)}, f32[128,256]{1,0:T(8,128)S(1)}, u32[]{:S(2)}, u32[]{:S(2)}) collective-permute-start(f32[128,256]{1,0:T(8,128)S(1)} %get-tuple-element.83), channel_id=1, source_target_pairs={{0,12},{4,8},{8,4},{12,0},{16,28},{20,24},{24,20},{28,16},{1,13},{... | collective-permute-start | bytes 393224 | tf_op jit(solution)/shard_map/ppermute | solution.py:455

commit v21 on v20

--- a/solution.py
+++ b/solution.py
@@ -525,10 +525,10 @@
         )
 
     betas, alphas, held, joined, right = [], [], [], [], []
-    near = spread(range(NEAR - 1), None)
+    near = spread(range(NEAR - 2), None)
     message = picked = exchange(message, "row")
     late = len(sent) - (chunks > 1)
-    near += spread(range(NEAR - 1, late), message)
+    near += spread(range(NEAR - 2, late), message)
     for step in range(ITERS):
         last = step + 1 == ITERS
         if step == 0:
@@ -536,10 +536,10 @@
             term = pl.pallas_call(
                 pass_body,
                 out_shape=shape(*term.shape),
-                in_specs=[ANY] * (NEAR - 1) + [VMEM],
+                in_specs=[ANY] * (NEAR - 2) + [VMEM],
                 out_specs=VMEM,
                 compiler_params=pltpu.CompilerParams(vmem_limit_bytes=2 << 20),
-            )(*near[: NEAR - 1], term)
+            )(*near[: NEAR - 2], term)
         else:
             term, beta = back(here, message, False)
             token = beta

time: 83.7 us -> 80.3 us (0.959)
  blocking collectives: 35.7 us -> 22.1 us
  starting transfers between devices: 18.9 us -> 26 us
  waiting for transfers between devices: 10.4 us -> 13.4 us
    all_to_all x3 -> x2, blocking collectives: 35.7 us -> 22.1 us  [exchange(): return lax.all_to_all(copies, axis, split_axis=0, concat_axis=0, tiled=True)]
    all_to_all x0 -> x1, starting transfers between devices: none -> 7.42 us  [exchange(): return lax.all_to_all(copies, axis, split_axis=0, concat_axis=0, tiled=True)]
    all_to_all x0 -> x1, waiting for transfers between devices: none -> 3.84 us  [exchange(): return lax.all_to_all(copies, axis, split_axis=0, concat_axis=0, tiled=True)]
    ppermute x11, starting transfers between devices: 12.9 us -> 12 us  [swap(): lax.ppermute(array, 'row', [(i, i ^ mask) for i in range(row_groups)])]
  transfers between devices with their start and end apart: 21 -> 22, of which waited for: 8 -> 9; matrix products, arithmetic and copies ran while one was open for 0% -> 0% of each run, Pallas kernels for 15% -> 15%
where the time goes in v21:
time: 80.3 us; the launch traced here: 80 us
  starting transfers between devices  26 us (32%)
  blocking collectives  22.1 us (28%)
  Pallas kernels  17.6 us (22%)
  waiting for transfers between devices  13.4 us (17%)
  between operations  0.81 us (1%)
    all_to_all x2, blocking collectives, exchange(): return lax.all_to_all(copies, axis, split_axis=0, concat_axis=0, tiled=True)  22.1 us
    ppermute x11, starting transfers between devices, swap(): lax.ppermute(array, 'row', [(i, i ^ mask) for i in range(row_groups)])  12 us
    all_to_all x1, starting transfers between devices, exchange(): return lax.all_to_all(copies, axis, split_axis=0, concat_axis=0, tiled=True)  7.42 us
    pallas_call x2, Pallas kernels, back(): pl.pallas_call(functools.partial(back_body, first), out_shape=outs, in_sp...  7.29 us
    pallas_call x9, Pallas kernels, call(): pl.pallas_call(body, out_shape=out_shape, in_specs=[VMEM] * len(operands)...  6.97 us
    ppermute x4, waiting for transfers between devices, paired(): come = lax.ppermute(array, axis, [(i, i ^ mask) for i in range(size)])  4.75 us
    ppermute x6, waiting for transfers between devices, direct(): lax.ppermute(array, axis, [(i, i ^ mask) for i in range(size)])  4.2 us
    ppermute x6, starting transfers between devices, direct(): lax.ppermute(array, axis, [(i, i ^ mask) for i in range(size)])  3.85 us
  transfers between devices with their start and end apart: 22, of which 9 were waited for; matrix products, arithmetic and copies ran while one was open for 0% of the time, Pallas kernels for 15%

profile of v21, /device:TPU:0, one launch (start us, length us, event | category | flops | bytes accessed | tf_op | source)
XLA Modules:
  0.0 80.0 jit_solution(6805294748339450759)
XLA Ops:
  0.6 3.4 %shard_map.85 = (f32[8,16,128]{2,1,0:T(8,128)}, f32[512,128]{1,0:T(8,128)}, f32[512,128]{1,0:T(8,128)}, f32[512,128]{1,0:T(8,128)}, f32[512,128]{1,0:T(8,128)}, /*index=5*/f32[512,128]{1,0:T(8,128)}, f32[512,128]{1,0:T(8,128)}) custom-call(f32[512,1024]{1,0:T(8,128)} %design_ref.9, f32[4,128]{1,0:T(4,128)} %bitcast.6, s32[4,128]{1,0:T(4,128)} %bitcast.9, ...), custom_call_target="tpu_custom_call" | custom-call | tf_op jit(solution)/shard_map/pallas_call | solution.py:437
  4.0 7.4 %all-to-all-start = ((f32[8,16,128]{2,1,0:T(8,128)}), f32[8,16,128]{2,1,0:T(8,128)S(1)}, u32[]{:S(2)}, u32[]{:S(2)}) async-start(f32[8,16,128]{2,1,0:T(8,128)} %get-tuple-element.46), calls=%async_computation | async-start | bytes 131072 | tf_op jit(solution)/shard_map/all_to_all | solution.py:24
  11.5 2.0 %collective-permute-start = (f32[512,128]{1,0:T(8,128)}, f32[512,128]{1,0:T(8,128)S(1)}, u32[]{:S(2)}, u32[]{:S(2)}) collective-permute-start(f32[512,128]{1,0:T(8,128)} %get-tuple-element.50), channel_id=1, source_target_pairs={{0,4},{4,0},{8,12},{12,8},{16,20},{20,16},{24,28},{28,24},{1,5},{5... | collective-permute-start | bytes 786440 | tf_op jit(solution)/shard_map/ppermute | solution.py:455
  13.5 1.5 %collective-permute-start.1 = (f32[512,128]{1,0:T(8,128)}, f32[512,128]{1,0:T(8,128)S(1)}, u32[]{:S(2)}, u32[]{:S(2)}) collective-permute-start(f32[512,128]{1,0:T(8,128)} %get-tuple-element.51), channel_id=1, source_target_pairs={{0,8},{4,12},{8,0},{12,4},{16,24},{20,28},{24,16},{28,20},{1,9},{5... | collective-permute-start | bytes 786440 | tf_op jit(solution)/shard_map/ppermute | solution.py:455
  14.9 3.8 %all-to-all-done.parts_ref = f32[8,16,128]{2,1,0:T(8,128)S(1)} async-done(((f32[8,16,128]{2,1,0:T(8,128)}), f32[8,16,128]{2,1,0:T(8,128)S(1)}, u32[]{:S(2)}, u32[]{:S(2)}) %all-to-all-start) | async-done | bytes 65568 | tf_op jit(solution)/shard_map/all_to_all | solution.py:24
  18.8 0.7 collective-permute-start.2
  19.5 5.9 %shard_map.86 = (f32[32,128]{1,0:T(8,128)S(1)}, f32[1,128]{1,0:T(1,128)S(1)}, bf16[8,128,512]{2,1,0:T(8,128)(2,1)S(1)}, f32[1024,4096]{1,0:T(8,128)S(1)}) custom-call(f32[1024,4096]{1,0:T(8,128)} %rinv_ref.1, f32[8,16,128]{2,1,0:T(8,128)S(1)} %all-to-all-done.parts_ref), custom_call_target="tpu_custom_call" | custom-call | tf_op jit(solution)/shard_map/pallas_call | solution.py:495
  25.5 1.2 %collective-permute-done.4 = f32[32,128]{1,0:T(8,128)S(1)} collective-permute-done((f32[32,128]{1,0:T(8,128)S(1)}, f32[32,128]{1,0:T(8,128)S(1)}, u32[]{:S(2)}, u32[]{:S(2)}) %collective-permute-start.4) | collective-permute-done | bytes 16416 | tf_op jit(solution)/shard_map/ppermute | solution.py:31
  26.7 1.5 %collective-permute-start.5 = (f32[32,128]{1,0:T(8,128)S(1)}, f32[32,128]{1,0:T(8,128)S(1)}, u32[]{:S(2)}, u32[]{:S(2)}) collective-permute-start(f32[32,128]{1,0:T(8,128)S(1)} %add.6.refs_0_), channel_id=1, source_target_pairs={{0,2},{1,3},{2,0},{3,1},{4,6},{5,7},{6,4},{7,5},{8,10},{9,11},{10,... | collective-permute-start | bytes 49160 | tf_op jit(solution)/shard_map/ppermute | solution.py:31
  28.2 0.6 collective-permute-start.8
  28.8 2.1 %collective-permute-start.9 = (f32[512,128]{1,0:T(8,128)S(1)}, f32[512,128]{1,0:T(8,128)S(1)}, u32[]{:S(2)}, u32[]{:S(2)}) collective-permute-start(f32[512,128]{1,0:T(8,128)S(1)} %copy-done.3), channel_id=1, source_target_pairs={{0,8},{4,12},{8,0},{12,4},{16,24},{20,28},{24,16},{28,20},{1,9},{5... | collective-permute-start | bytes 786440 | tf_op jit(solution)/shard_map/ppermute | solution.py:455
  31.0 1.1 %shard_map.87 = (f32[1,4,128,128]{3,2,1,0:T(8,128)S(1)}, f32[1,4,128,128]{3,2,1,0:T(8,128)S(1)}, f32[1,128]{1,0:T(1,128)S(1)}) custom-call(f32[512,1024]{1,0:T(8,128)S(1)} %copy-done, f32[8,16,128]{2,1,0:T(8,128)S(1)} %all-to-all-done.parts_ref, bf16[8,128,512]{2,1,0:T(8,128)(2,1)S(1)} %get-tuple-element.48.mix_ref, ...), custom_call_target="tpu_custom_call" | custom-call | tf_op jit(solution)/shard_map/pallas_call | solution.py:59
  33.0 1.7 %shard_map.89 = (f32[4,128]{1,0:T(4,128)S(1)}, f32[8,128]{1,0:T(8,128)S(1)}, f32[1,128]{1,0:T(1,128)S(1)}, f32[32,128]{1,0:T(8,128)S(1)}) custom-call(f32[1024,4096]{1,0:T(8,128)S(1)} %get-tuple-element.47.rinv_ref, f32[512,1024]{1,0:T(8,128)S(1)} %copy-done, f32[1,128]{1,0:T(1,128)S(1)} %get-tuple-element.58.token_ref, f32[32,128]{1,0:T(8,128)S(1)} %add.6.refs_0_, ...), custom_call_target="tpu_custom_call" | custom-call | tf_op jit(solution)/shard_map/pallas_call | solution.py:59
  34.8 1.1 %collective-permute-done.6 = f32[4,128]{1,0:T(4,128)S(1)} collective-permute-done((f32[4,128]{1,0:T(4,128)S(1)}, f32[4,128]{1,0:T(4,128)S(1)}, u32[]{:S(2)}, u32[]{:S(2)}) %collective-permute-start.6) | collective-permute-done | bytes 2080 | tf_op jit(solution)/shard_map/ppermute | solution.py:31
  35.9 1.2 %collective-permute-start.7 = (f32[4,128]{1,0:T(4,128)S(1)}, f32[4,128]{1,0:T(4,128)S(1)}, u32[]{:S(2)}, u32[]{:S(2)}) collective-permute-start(f32[4,128]{1,0:T(4,128)S(1)} %add.7.refs_0_), channel_id=1, source_target_pairs={{0,2},{1,3},{2,0},{3,1},{4,6},{5,7},{6,4},{7,5},{8,10},{9,11},{10,... | collective-permute-start | bytes 6152 | tf_op jit(solution)/shard_map/ppermute | solution.py:31
  37.1 2.4 %collective-permute-done.7.refs_1_ = f32[4,128]{1,0:T(4,128)S(1)} collective-permute-done((f32[4,128]{1,0:T(4,128)S(1)}, f32[4,128]{1,0:T(4,128)S(1)}, u32[]{:S(2)}, u32[]{:S(2)}) %collective-permute-start.7) | collective-permute-done | bytes 2080 | tf_op jit(solution)/shard_map/ppermute | solution.py:31
  39.7 12.4 %all_to_all.15.order_ref.parts_ref = f32[8,16,128]{2,1,0:T(8,128)S(1)} all-to-all(f32[8,16,128]{2,1,0:T(8,128)S(1)} %get-tuple-element.62), channel_id=1, replica_groups=mesh['row'=8,'col'=4] {'row'}, dimensions={0} | all-to-all | bytes 131072 | tf_op jit(solution)/shard_map/all_to_all | solution.py:24
  52.2 1.1 %shard_map.92 = (f32[1,4,128,128]{3,2,1,0:T(8,128)S(1)}, f32[1,4,128,128]{3,2,1,0:T(8,128)S(1)}, f32[1,128]{1,0:T(1,128)S(1)}) custom-call(f32[512,1024]{1,0:T(8,128)S(1)} %copy-done, f32[8,16,128]{2,1,0:T(8,128)S(1)} %all-to-all-done.parts_ref, bf16[8,128,512]{2,1,0:T(8,128)(2,1)S(1)} %get-tuple-element.48.mix_ref, ...), custom_call_target="tpu_custom_call" | custom-call | tf_op jit(solution)/shard_map/pallas_call | solution.py:59
  53.9 1.4 %shard_map.93 = (f32[32,128]{1,0:T(8,128)S(1)}, f32[1,128]{1,0:T(1,128)S(1)}) custom-call(f32[1024,4096]{1,0:T(8,128)S(1)} %get-tuple-element.47.rinv_ref, f32[8,16,128]{2,1,0:T(8,128)S(1)} %all_to_all.15.order_ref.parts_ref), custom_call_target="tpu_custom_call" | custom-call | tf_op jit(solution)/shard_map/pallas_call | solution.py:495
  55.4 0.6 collective-permute-start.12
  56.0 1.3 %collective-permute-start.11 = (f32[32,128]{1,0:T(8,128)S(1)}, f32[32,128]{1,0:T(8,128)S(1)}, u32[]{:S(2)}, u32[]{:S(2)}) collective-permute-start(f32[32,128]{1,0:T(8,128)S(1)} %get-tuple-element.69.refs_0_), channel_id=1, source_target_pairs={{0,1},{1,0},{2,3},{3,2},{4,5},{5,4},{6,7},{7,6},{8,9},{9,8},{10,11... | collective-permute-start | bytes 49160 | tf_op jit(solution)/shard_map/ppermute | solution.py:41
  57.2 1.3 %collective-permute-done.13.refs_3_ = f32[32,128]{1,0:T(8,128)S(1)} collective-permute-done((f32[32,128]{1,0:T(8,128)S(1)}, f32[32,128]{1,0:T(8,128)S(1)}, u32[]{:S(2)}, u32[]{:S(2)}) %collective-permute-start.13) | collective-permute-done | bytes 16416 | tf_op jit(solution)/shard_map/ppermute | solution.py:41
  58.5 0.7 collective-permute-done.12.refs_2_
  59.2 1.7 %shard_map.94 = (f32[4,128]{1,0:T(4,128)S(1)}, f32[8,128]{1,0:T(8,128)S(1)}, f32[1,128]{1,0:T(1,128)S(1)}) custom-call(f32[1024,4096]{1,0:T(8,128)S(1)} %get-tuple-element.47.rinv_ref, f32[512,1024]{1,0:T(8,128)S(1)} %copy-done, f32[1,128]{1,0:T(1,128)S(1)} %get-tuple-element.68.token_ref, f32[32,128]{1,0:T(8,128)S(1)} %get-tuple-element.69.refs_0_, ...), custom_call_target="tpu_custom_call" | custom-call | tf_op jit(solution)/shard_map/pallas_call | solution.py:59
  62.1 0.8 collective-permute-start.14
  62.9 1.1 %collective-permute-done.16.refs_3_ = f32[4,128]{1,0:T(4,128)S(1)} collective-permute-done((f32[4,128]{1,0:T(4,128)S(1)}, f32[4,128]{1,0:T(4,128)S(1)}, u32[]{:S(2)}, u32[]{:S(2)}) %collective-permute-start.16) | collective-permute-done | bytes 2080 | tf_op jit(solution)/shard_map/ppermute | solution.py:41
  64.0 1.1 %collective-permute-done.15.refs_2_ = f32[4,128]{1,0:T(4,128)S(1)} collective-permute-done((f32[4,128]{1,0:T(4,128)S(1)}, f32[4,128]{1,0:T(4,128)S(1)}, u32[]{:S(2)}, u32[]{:S(2)}) %collective-permute-start.15) | collective-permute-done | bytes 2080 | tf_op jit(solution)/shard_map/ppermute | solution.py:41
  65.8 0.8 %collective-permute-start.18 = (f32[128,256]{1,0:T(8,128)S(1)}, f32[128,256]{1,0:T(8,128)S(1)}, u32[]{:S(2)}, u32[]{:S(2)}) collective-permute-start(f32[128,256]{1,0:T(8,128)S(1)} %get-tuple-element.83), channel_id=1, source_target_pairs={{0,4},{4,0},{8,12},{12,8},{16,20},{20,16},{24,28},{28,24},{1,5},{5... | collective-permute-start | bytes 393224 | tf_op jit(solution)/shard_map/ppermute | solution.py:455
  66.7 0.8 %collective-permute-start.19 = (f32[128,256]{1,0:T(8,128)S(1)}, f32[128,256]{1,0:T(8,128)S(1)}, u32[]{:S(2)}, u32[]{:S(2)}) collective-permute-start(f32[128,256]{1,0:T(8,128)S(1)} %get-tuple-element.84), channel_id=1, source_target_pairs={{0,8},{4,12},{8,0},{12,4},{16,24},{20,28},{24,16},{28,20},{1,9},{5... | collective-permute-start | bytes 393224 | tf_op jit(solution)/shard_map/ppermute | solution.py:455
  67.5 1.9 %collective-permute-start.20 = (f32[128,256]{1,0:T(8,128)S(1)}, f32[128,256]{1,0:T(8,128)S(1)}, u32[]{:S(2)}, u32[]{:S(2)}) collective-permute-start(f32[128,256]{1,0:T(8,128)S(1)} %get-tuple-element.85), channel_id=1, source_target_pairs={{0,12},{4,8},{8,4},{12,0},{16,28},{20,24},{24,20},{28,16},{1,13},{... | collective-permute-start | bytes 393224 | tf_op jit(solution)/shard_map/ppermute | solution.py:455
  69.4 9.7 %all_to_all.16.parts_ref = f32[8,8,128]{2,1,0:T(8,128)S(1)} all-to-all(f32[8,8,128]{2,1,0:T(8,128)S(1)} %get-tuple-element.75), channel_id=1, replica_groups=mesh['row'=8,'col'=4] {'row'}, dimensions={0} | all-to-all | bytes 65536 | tf_op jit(solution)/shard_map/all_to_all | solution.py:24
  79.1 0.9 %shard_map.97 = (f32[4,128]{1,0:T(4,128)}, f32[8,128]{1,0:T(8,128)}, f32[128,1024]{1,0:T(8,128)}) custom-call(f32[8,8,128]{2,1,0:T(8,128)S(1)} %all_to_all.16.parts_ref, f32[4,128]{1,0:T(4,128)S(1)} %get-tuple-element.76.refs_3_.left_ref, f32[1,128]{1,0:T(1,128)S(1)} %get-tuple-element.49.order_ref.refs_3_.refs_0_, ...), custom_call_target="tpu_custom_call" | custom-call | tf_op jit(solution)/shard_map/pallas_call | solution.py:59
  (39 shorter events, 3.9 us)
Async XLA Ops:
  0.6 30.3 %copy-start = (f32[512,1024]{1,0:T(8,128)S(1)}, f32[512,1024]{1,0:T(8,128)}, u32[]{:S(2)}) copy-start(f32[512,1024]{1,0:T(8,128)} %design_ref.9) | copy-start | bytes 6291460
  4.0 24.2 %copy-start.4 = (f32[512,128]{1,0:T(8,128)S(1)}, f32[512,128]{1,0:T(8,128)}, u32[]{:S(2)}) copy-start(f32[512,128]{1,0:T(8,128)} %get-tuple-element.64) | copy-start | bytes 786436
  4.0 24.8 %copy-start.3 = (f32[512,128]{1,0:T(8,128)S(1)}, f32[512,128]{1,0:T(8,128)}, u32[]{:S(2)}) copy-start(f32[512,128]{1,0:T(8,128)} %get-tuple-element.65) | copy-start | bytes 786436
  4.0 28.5 %copy-start.2 = (f32[512,128]{1,0:T(8,128)S(1)}, f32[512,128]{1,0:T(8,128)}, u32[]{:S(2)}) copy-start(f32[512,128]{1,0:T(8,128)} %get-tuple-element.67) | copy-start | bytes 786436
  4.0 14.8 %all-to-all-start = ((f32[8,16,128]{2,1,0:T(8,128)}), f32[8,16,128]{2,1,0:T(8,128)S(1)}, u32[]{:S(2)}, u32[]{:S(2)}) async-start(f32[8,16,128]{2,1,0:T(8,128)} %get-tuple-element.46), calls=%async_computation | async-start | bytes 131072 | tf_op jit(solution)/shard_map/all_to_all | solution.py:24
  11.5 14.0 %collective-permute-start = (f32[512,128]{1,0:T(8,128)}, f32[512,128]{1,0:T(8,128)S(1)}, u32[]{:S(2)}, u32[]{:S(2)}) collective-permute-start(f32[512,128]{1,0:T(8,128)} %get-tuple-element.50), channel_id=1, source_target_pairs={{0,4},{4,0},{8,12},{12,8},{16,20},{20,16},{24,28},{28,24},{1,5},{5... | collective-permute-start | bytes 786440 | tf_op jit(solution)/shard_map/ppermute | solution.py:455
  13.5 11.9 %collective-permute-start.1 = (f32[512,128]{1,0:T(8,128)}, f32[512,128]{1,0:T(8,128)S(1)}, u32[]{:S(2)}, u32[]{:S(2)}) collective-permute-start(f32[512,128]{1,0:T(8,128)} %get-tuple-element.51), channel_id=1, source_target_pairs={{0,8},{4,12},{8,0},{12,4},{16,24},{20,28},{24,16},{28,20},{1,9},{5... | collective-permute-start | bytes 786440 | tf_op jit(solution)/shard_map/ppermute | solution.py:455
  18.8 20.7 %copy-start.1 = (f32[512]{0:T(512)S(1)}, f32[512]{0:T(512)}, u32[]{:S(2)}) copy-start(f32[512]{0:T(512)} %param.10) | copy-start | bytes 6148
  18.8 12.2 %collective-permute-start.2 = (f32[512,128]{1,0:T(8,128)}, f32[512,128]{1,0:T(8,128)S(1)}, u32[]{:S(2)}, u32[]{:S(2)}) collective-permute-start(f32[512,128]{1,0:T(8,128)} %get-tuple-element.55), channel_id=1, source_target_pairs={{0,12},{4,8},{8,4},{12,0},{16,28},{20,24},{24,20},{28,16},{1,13},{... | collective-permute-start | bytes 786440 | tf_op jit(solution)/shard_map/ppermute | solution.py:455
  25.4 1.2 %collective-permute-start.4 = (f32[32,128]{1,0:T(8,128)S(1)}, f32[32,128]{1,0:T(8,128)S(1)}, u32[]{:S(2)}, u32[]{:S(2)}) collective-permute-start(f32[32,128]{1,0:T(8,128)S(1)} %shard_map.88), channel_id=1, source_target_pairs={{0,1},{1,0},{2,3},{3,2},{4,5},{5,4},{6,7},{7,6},{8,9},{9,8},{10,11... | collective-permute-start | bytes 49160 | tf_op jit(solution)/shard_map/ppermute | solution.py:31
  26.7 5.8 %collective-permute-start.5 = (f32[32,128]{1,0:T(8,128)S(1)}, f32[32,128]{1,0:T(8,128)S(1)}, u32[]{:S(2)}, u32[]{:S(2)}) collective-permute-start(f32[32,128]{1,0:T(8,128)S(1)} %add.6.refs_0_), channel_id=1, source_target_pairs={{0,2},{1,3},{2,0},{3,1},{4,6},{5,7},{6,4},{7,5},{8,10},{9,11},{10,... | collective-permute-start | bytes 49160 | tf_op jit(solution)/shard_map/ppermute | solution.py:31
  28.2 24.0 %collective-permute-start.8 = (f32[512,128]{1,0:T(8,128)S(1)}, f32[512,128]{1,0:T(8,128)S(1)}, u32[]{:S(2)}, u32[]{:S(2)}) collective-permute-start(f32[512,128]{1,0:T(8,128)S(1)} %copy-done.4), channel_id=1, source_target_pairs={{0,4},{4,0},{8,12},{12,8},{16,20},{20,16},{24,28},{28,24},{1,5},{5... | collective-permute-start | bytes 786440 | tf_op jit(solution)/shard_map/ppermute | solution.py:455
  28.8 23.4 %collective-permute-start.9 = (f32[512,128]{1,0:T(8,128)S(1)}, f32[512,128]{1,0:T(8,128)S(1)}, u32[]{:S(2)}, u32[]{:S(2)}) collective-permute-start(f32[512,128]{1,0:T(8,128)S(1)} %copy-done.3), channel_id=1, source_target_pairs={{0,8},{4,12},{8,0},{12,4},{16,24},{20,28},{24,16},{28,20},{1,9},{5... | collective-permute-start | bytes 786440 | tf_op jit(solution)/shard_map/ppermute | solution.py:455
  32.1 20.1 %collective-permute-start.3 = (f32[1,4,128,128]{3,2,1,0:T(8,128)S(1)}, f32[1,4,128,128]{3,2,1,0:T(8,128)S(1)}, u32[]{:S(2)}, u32[]{:S(2)}) collective-permute-start(f32[1,4,128,128]{3,2,1,0:T(8,128)S(1)} %get-tuple-element.57), channel_id=1, source_target_pairs={{0,16},{4,20},{8,24},{12,28},{16,0},{20,4},{24,8},{28,12},{1,17},{... | collective-permute-start | bytes 786440 | tf_op jit(solution)/shard_map/ppermute | solution.py:455
  32.5 19.7 %collective-permute-start.10 = (f32[512,128]{1,0:T(8,128)S(1)}, f32[512,128]{1,0:T(8,128)S(1)}, u32[]{:S(2)}, u32[]{:S(2)}) collective-permute-start(f32[512,128]{1,0:T(8,128)S(1)} %copy-done.2), channel_id=1, source_target_pairs={{0,12},{4,8},{8,4},{12,0},{16,28},{20,24},{24,20},{28,16},{1,13},{... | collective-permute-start | bytes 786440 | tf_op jit(solution)/shard_map/ppermute | solution.py:455
  34.7 1.2 %collective-permute-start.6 = (f32[4,128]{1,0:T(4,128)S(1)}, f32[4,128]{1,0:T(4,128)S(1)}, u32[]{:S(2)}, u32[]{:S(2)}) collective-permute-start(f32[4,128]{1,0:T(4,128)S(1)} %get-tuple-element.60), channel_id=1, source_target_pairs={{0,1},{1,0},{2,3},{3,2},{4,5},{5,4},{6,7},{7,6},{8,9},{9,8},{10,11... | collective-permute-start | bytes 6152 | tf_op jit(solution)/shard_map/ppermute | solution.py:31
  35.9 3.6 %collective-permute-start.7 = (f32[4,128]{1,0:T(4,128)S(1)}, f32[4,128]{1,0:T(4,128)S(1)}, u32[]{:S(2)}, u32[]{:S(2)}) collective-permute-start(f32[4,128]{1,0:T(4,128)S(1)} %add.7.refs_0_), channel_id=1, source_target_pairs={{0,2},{1,3},{2,0},{3,1},{4,6},{5,7},{6,4},{7,5},{8,10},{9,11},{10,... | collective-permute-start | bytes 6152 | tf_op jit(solution)/shard_map/ppermute | solution.py:31
  53.4 12.4 %collective-permute-start.17 = (f32[1,4,128,128]{3,2,1,0:T(8,128)S(1)}, f32[1,4,128,128]{3,2,1,0:T(8,128)S(1)}, u32[]{:S(2)}, u32[]{:S(2)}) collective-permute-start(f32[1,4,128,128]{3,2,1,0:T(8,128)S(1)} %get-tuple-element.81), channel_id=1, source_target_pairs={{0,16},{4,20},{8,24},{12,28},{16,0},{20,4},{24,8},{28,12},{1,17},{... | collective-permute-start | bytes 786440 | tf_op jit(solution)/shard_map/ppermute | solution.py:455
  55.3 3.2 %collective-permute-start.13 = (f32[32,128]{1,0:T(8,128)S(1)}, f32[32,128]{1,0:T(8,128)S(1)}, u32[]{:S(2)}, u32[]{:S(2)}) collective-permute-start(f32[32,128]{1,0:T(8,128)S(1)} %get-tuple-element.69.refs_0_), channel_id=1, source_target_pairs={{0,3},{1,2},{2,1},{3,0},{4,7},{5,6},{6,5},{7,4},{8,11},{9,10},{10,... | collective-permute-start | bytes 49160 | tf_op jit(solution)/shard_map/ppermute | solution.py:41
  55.4 3.8 %collective-permute-start.12 = (f32[32,128]{1,0:T(8,128)S(1)}, f32[32,128]{1,0:T(8,128)S(1)}, u32[]{:S(2)}, u32[]{:S(2)}) collective-permute-start(f32[32,128]{1,0:T(8,128)S(1)} %get-tuple-element.69.refs_0_), channel_id=1, source_target_pairs={{0,2},{1,3},{2,0},{3,1},{4,6},{5,7},{6,4},{7,5},{8,10},{9,11},{10,... | collective-permute-start | bytes 49160 | tf_op jit(solution)/shard_map/ppermute | solution.py:41
  56.0 3.2 %collective-permute-start.11 = (f32[32,128]{1,0:T(8,128)S(1)}, f32[32,128]{1,0:T(8,128)S(1)}, u32[]{:S(2)}, u32[]{:S(2)}) collective-permute-start(f32[32,128]{1,0:T(8,128)S(1)} %get-tuple-element.69.refs_0_), channel_id=1, source_target_pairs={{0,1},{1,0},{2,3},{3,2},{4,5},{5,4},{6,7},{7,6},{8,9},{9,8},{10,11... | collective-permute-start | bytes 49160 | tf_op jit(solution)/shard_map/ppermute | solution.py:41
  60.9 3.1 %collective-permute-start.16 = (f32[4,128]{1,0:T(4,128)S(1)}, f32[4,128]{1,0:T(4,128)S(1)}, u32[]{:S(2)}, u32[]{:S(2)}) collective-permute-start(f32[4,128]{1,0:T(4,128)S(1)} %get-tuple-element.72.refs_0_), channel_id=1, source_target_pairs={{0,3},{1,2},{2,1},{3,0},{4,7},{5,6},{6,5},{7,4},{8,11},{9,10},{10,... | collective-permute-start | bytes 6152 | tf_op jit(solution)/shard_map/ppermute | solution.py:41
  61.5 3.6 %collective-permute-start.15 = (f32[4,128]{1,0:T(4,128)S(1)}, f32[4,128]{1,0:T(4,128)S(1)}, u32[]{:S(2)}, u32[]{:S(2)}) collective-permute-start(f32[4,128]{1,0:T(4,128)S(1)} %get-tuple-element.72.refs_0_), channel_id=1, source_target_pairs={{0,2},{1,3},{2,0},{3,1},{4,6},{5,7},{6,4},{7,5},{8,10},{9,11},{10,... | collective-permute-start | bytes 6152 | tf_op jit(solution)/shard_map/ppermute | solution.py:41
  62.1 3.0 %collective-permute-start.14 = (f32[4,128]{1,0:T(4,128)S(1)}, f32[4,128]{1,0:T(4,128)S(1)}, u32[]{:S(2)}, u32[]{:S(2)}) collective-permute-start(f32[4,128]{1,0:T(4,128)S(1)} %get-tuple-element.72.refs_0_), channel_id=1, source_target_pairs={{0,1},{1,0},{2,3},{3,2},{4,5},{5,4},{6,7},{7,6},{8,9},{9,8},{10,11... | collective-permute-start | bytes 6152 | tf_op jit(solution)/shard_map/ppermute | solution.py:41
  65.8 13.3 %collective-permute-start.18 = (f32[128,256]{1,0:T(8,128)S(1)}, f32[128,256]{1,0:T(8,128)S(1)}, u32[]{:S(2)}, u32[]{:S(2)}) collective-permute-start(f32[128,256]{1,0:T(8,128)S(1)} %get-tuple-element.83), channel_id=1, source_target_pairs={{0,4},{4,0},{8,12},{12,8},{16,20},{20,16},{24,28},{28,24},{1,5},{5... | collective-permute-start | bytes 393224 | tf_op jit(solution)/shard_map/ppermute | solution.py:455
  66.7 12.5 %collective-permute-start.19 = (f32[128,256]{1,0:T(8,128)S(1)}, f32[128,256]{1,0:T(8,128)S(1)}, u32[]{:S(2)}, u32[]{:S(2)}) collective-permute-start(f32[128,256]{1,0:T(8,128)S(1)} %get-tuple-element.84), channel_id=1, source_target_pairs={{0,8},{4,12},{8,0},{12,4},{16,24},{20,28},{24,16},{28,20},{1,9},{5... | collective-permute-start | bytes 393224 | tf_op jit(solution)/shard_map/ppermute | solution.py:455
  67.5 11.6 %collective-permute-start.20 = (f32[128,256]{1,0:T(8,128)S(1)}, f32[128,256]{1,0:T(8,128)S(1)}, u32[]{:S(2)}, u32[]{:S(2)}) collective-permute-start(f32[128,256]{1,0:T(8,128)S(1)} %get-tuple-element.85), channel_id=1, source_target_pairs={{0,12},{4,8},{8,4},{12,0},{16,28},{20,24},{24,20},{28,16},{1,13},{... | collective-permute-start | bytes 393224 | tf_op jit(solution)/shard_map/ppermute | solution.py:455

commit v22 on v21

--- a/solution.py
+++ b/solution.py
@@ -524,6 +524,15 @@
             *(() if last else (design,)),
         )
 
+    def after(arrays, value):
+        return pl.pallas_call(
+            pass_body,
+            out_shape=shape(*value.shape),
+            in_specs=[ANY] * len(arrays) + [VMEM],
+            out_specs=VMEM,
+            compiler_params=pltpu.CompilerParams(vmem_limit_bytes=2 << 20),
+        )(*arrays, value)
+
     betas, alphas, held, joined, right = [], [], [], [], []
     near = spread(range(NEAR - 2), None)
     message = picked = exchange(message, "row")
@@ -533,13 +542,7 @@
         last = step + 1 == ITERS
         if step == 0:
             term, beta, mixed, here = back(rinv, message, True)
-            term = pl.pallas_call(
-                pass_body,
-                out_shape=shape(*term.shape),
-                in_specs=[ANY] * (NEAR - 2) + [VMEM],
-                out_specs=VMEM,
-                compiler_params=pltpu.CompilerParams(vmem_limit_bytes=2 << 20),
-            )(*near[: NEAR - 2], term)
+            term = after(near[: NEAR - 2], term)
         else:
             term, beta = back(here, message, False)
             token = beta
@@ -553,7 +556,7 @@
         terms = direct(term, "col") if spare else paired(term, "col")
         if step == 0:
             near += spread(range(late, len(sent)), terms[1])
-            keep, send, token = sample(0, mixed, beta)
+            keep, send, token = sample(0, mixed, after([near[NEAR - 2], *near[NEAR:late]], beta) if chunks > 1 else beta)
             come = swap(send, row_groups // 2)
         image, kept, alpha, *right = forward(terms, token, last, *right, *betas[1:])
         alphas.append(alpha)

time: 80.3 us -> 82.3 us (1.025)
  starting transfers between devices: 26 us -> 29.3 us
  blocking collectives: 22.1 us -> 19.5 us
  waiting for transfers between devices: 13.4 us -> 14.7 us
    ppermute x11, starting transfers between devices: 12 us -> 14.8 us  [swap(): lax.ppermute(array, 'row', [(i, i ^ mask) for i in range(row_groups)])]
    all_to_all x2, blocking collectives: 22.1 us -> 19.5 us  [exchange(): return lax.all_to_all(copies, axis, split_axis=0, concat_axis=0, tiled=True)]
    ppermute x11, waiting for transfers between devices: 0.61 us -> 2.32 us  [swap(): lax.ppermute(array, 'row', [(i, i ^ mask) for i in range(row_groups)])]
  transfers between devices with their start and end apart: 22 -> 22, of which waited for: 9 -> 10; matrix products, arithmetic and copies ran while one was open for 0% -> 0% of each run, Pallas kernels for 15% -> 15%
where the time goes in v22:
time: 82.3 us; the launch traced here: 82 us
  starting transfers between devices  29.3 us (36%)
  blocking collectives  19.5 us (24%)
  Pallas kernels  17.6 us (21%)
  waiting for transfers between devices  14.7 us (18%)
    all_to_all x2, blocking collectives, exchange(): return lax.all_to_all(copies, axis, split_axis=0, concat_axis=0, tiled=True)  19.5 us
    ppermute x11, starting transfers between devices, swap(): lax.ppermute(array, 'row', [(i, i ^ mask) for i in range(row_groups)])  14.8 us
    all_to_all x1, starting transfers between devices, exchange(): return lax.all_to_all(copies, axis, split_axis=0, concat_axis=0, tiled=True)  7.42 us
    pallas_call x2, Pallas kernels, back(): pl.pallas_call(functools.partial(back_body, first), out_shape=outs, in_sp...  7.28 us
    pallas_call x9, Pallas kernels, call(): pl.pallas_call(body, out_shape=out_shape, in_specs=[VMEM] * len(operands)...  6.97 us
    ppermute x4, waiting for transfers between devices, paired(): come = lax.ppermute(array, axis, [(i, i ^ mask) for i in range(size)])  4.41 us
    ppermute x6, waiting for transfers between devices, direct(): lax.ppermute(array, axis, [(i, i ^ mask) for i in range(size)])  4.09 us
    ppermute x6, starting transfers between devices, direct(): lax.ppermute(array, axis, [(i, i ^ mask) for i in range(size)])  3.99 us
  transfers between devices with their start and end apart: 22, of which 10 were waited for; matrix products, arithmetic and copies ran while one was open for 0% of the time, Pallas kernels for 15%

profile of v22, /device:TPU:0, one launch (start us, length us, event | category | flops | bytes accessed | tf_op | source)
XLA Modules:
  0.0 82.0 jit_solution(6715472701294306679)
XLA Ops:
  0.6 3.4 %shard_map.85 = (f32[8,16,128]{2,1,0:T(8,128)}, f32[512,128]{1,0:T(8,128)}, f32[512,128]{1,0:T(8,128)}, f32[512,128]{1,0:T(8,128)}, f32[512,128]{1,0:T(8,128)}, /*index=5*/f32[512,128]{1,0:T(8,128)}, f32[512,128]{1,0:T(8,128)}) custom-call(f32[512,1024]{1,0:T(8,128)} %design_ref.9, f32[4,128]{1,0:T(4,128)} %bitcast.6, s32[4,128]{1,0:T(4,128)} %bitcast.9, ...), custom_call_target="tpu_custom_call" | custom-call | tf_op jit(solution)/shard_map/pallas_call | solution.py:437
  4.0 7.4 %all-to-all-start = ((f32[8,16,128]{2,1,0:T(8,128)}), f32[8,16,128]{2,1,0:T(8,128)S(1)}, u32[]{:S(2)}, u32[]{:S(2)}) async-start(f32[8,16,128]{2,1,0:T(8,128)} %get-tuple-element.46), calls=%async_computation | async-start | bytes 131072 | tf_op jit(solution)/shard_map/all_to_all | solution.py:24
  11.5 2.0 %collective-permute-start.2 = (f32[512,128]{1,0:T(8,128)}, f32[512,128]{1,0:T(8,128)S(1)}, u32[]{:S(2)}, u32[]{:S(2)}) collective-permute-start(f32[512,128]{1,0:T(8,128)} %get-tuple-element.55), channel_id=1, source_target_pairs={{0,4},{4,0},{8,12},{12,8},{16,20},{20,16},{24,28},{28,24},{1,5},{5... | collective-permute-start | bytes 786440 | tf_op jit(solution)/shard_map/ppermute | solution.py:455
  13.5 1.5 %collective-permute-start.3 = (f32[512,128]{1,0:T(8,128)}, f32[512,128]{1,0:T(8,128)S(1)}, u32[]{:S(2)}, u32[]{:S(2)}) collective-permute-start(f32[512,128]{1,0:T(8,128)} %get-tuple-element.56), channel_id=1, source_target_pairs={{0,8},{4,12},{8,0},{12,4},{16,24},{20,28},{24,16},{28,20},{1,9},{5... | collective-permute-start | bytes 786440 | tf_op jit(solution)/shard_map/ppermute | solution.py:455
  15.0 3.8 %all-to-all-done.parts_ref = f32[8,16,128]{2,1,0:T(8,128)S(1)} async-done(((f32[8,16,128]{2,1,0:T(8,128)}), f32[8,16,128]{2,1,0:T(8,128)S(1)}, u32[]{:S(2)}, u32[]{:S(2)}) %all-to-all-start) | async-done | bytes 65568 | tf_op jit(solution)/shard_map/all_to_all | solution.py:24
  18.8 0.7 collective-permute-start
  19.5 0.9 %collective-permute-start.1 = (f32[512,128]{1,0:T(8,128)}, f32[512,128]{1,0:T(8,128)S(1)}, u32[]{:S(2)}, u32[]{:S(2)}) collective-permute-start(f32[512,128]{1,0:T(8,128)} %get-tuple-element.53), channel_id=1, source_target_pairs={{0,8},{4,12},{8,0},{12,4},{16,24},{20,28},{24,16},{28,20},{1,9},{5... | collective-permute-start | bytes 786440 | tf_op jit(solution)/shard_map/ppermute | solution.py:455
  20.5 5.9 %shard_map.86 = (f32[32,128]{1,0:T(8,128)S(1)}, f32[1,128]{1,0:T(1,128)S(1)}, bf16[8,128,512]{2,1,0:T(8,128)(2,1)S(1)}, f32[1024,4096]{1,0:T(8,128)S(1)}) custom-call(f32[1024,4096]{1,0:T(8,128)} %rinv_ref.1, f32[8,16,128]{2,1,0:T(8,128)S(1)} %all-to-all-done.parts_ref), custom_call_target="tpu_custom_call" | custom-call | tf_op jit(solution)/shard_map/pallas_call | solution.py:495
  26.5 1.2 %collective-permute-done.5 = f32[32,128]{1,0:T(8,128)S(1)} collective-permute-done((f32[32,128]{1,0:T(8,128)S(1)}, f32[32,128]{1,0:T(8,128)S(1)}, u32[]{:S(2)}, u32[]{:S(2)}) %collective-permute-start.5) | collective-permute-done | bytes 16416 | tf_op jit(solution)/shard_map/ppermute | solution.py:31
  27.6 1.5 %collective-permute-start.6 = (f32[32,128]{1,0:T(8,128)S(1)}, f32[32,128]{1,0:T(8,128)S(1)}, u32[]{:S(2)}, u32[]{:S(2)}) collective-permute-start(f32[32,128]{1,0:T(8,128)S(1)} %add.6.refs_0_), channel_id=1, source_target_pairs={{0,2},{1,3},{2,0},{3,1},{4,6},{5,7},{6,4},{7,5},{8,10},{9,11},{10,... | collective-permute-start | bytes 49160 | tf_op jit(solution)/shard_map/ppermute | solution.py:31
  29.1 1.8 %collective-permute-start.9 = (f32[512,128]{1,0:T(8,128)S(1)}, f32[512,128]{1,0:T(8,128)S(1)}, u32[]{:S(2)}, u32[]{:S(2)}) collective-permute-start(f32[512,128]{1,0:T(8,128)S(1)} %copy-done.3), channel_id=1, source_target_pairs={{0,4},{4,0},{8,12},{12,8},{16,20},{20,16},{24,28},{28,24},{1,5},{5... | collective-permute-start | bytes 786440 | tf_op jit(solution)/shard_map/ppermute | solution.py:455
  30.9 1.8 %collective-permute-done.1.refs_1_ = f32[512,128]{1,0:T(8,128)S(1)} collective-permute-done((f32[512,128]{1,0:T(8,128)}, f32[512,128]{1,0:T(8,128)S(1)}, u32[]{:S(2)}, u32[]{:S(2)}) %collective-permute-start.1) | collective-permute-done | bytes 262176 | tf_op jit(solution)/shard_map/ppermute | solution.py:455
  32.8 1.1 %shard_map.88 = (f32[1,4,128,128]{3,2,1,0:T(8,128)S(1)}, f32[1,4,128,128]{3,2,1,0:T(8,128)S(1)}, f32[1,128]{1,0:T(1,128)S(1)}) custom-call(f32[512,1024]{1,0:T(8,128)S(1)} %copy-done, f32[8,16,128]{2,1,0:T(8,128)S(1)} %all-to-all-done.parts_ref, bf16[8,128,512]{2,1,0:T(8,128)(2,1)S(1)} %get-tuple-element.48.mix_ref, f32[1,128]{1,0:T(1,128)S(1)} %shard_map.87.order_ref, ...), custom_call_target="tpu_custom_call" | custom-call | tf_op jit(solution)/shard_map/pallas_call | solution.py:59
  33.9 2.3 %collective-permute-start.4 = (f32[1,4,128,128]{3,2,1,0:T(8,128)S(1)}, f32[1,4,128,128]{3,2,1,0:T(8,128)S(1)}, u32[]{:S(2)}, u32[]{:S(2)}) collective-permute-start(f32[1,4,128,128]{3,2,1,0:T(8,128)S(1)} %get-tuple-element.58), channel_id=1, source_target_pairs={{0,16},{4,20},{8,24},{12,28},{16,0},{20,4},{24,8},{28,12},{1,17},{... | collective-permute-start | bytes 786440 | tf_op jit(solution)/shard_map/ppermute | solution.py:455
  36.2 1.5 %collective-permute-start.10 = (f32[512,128]{1,0:T(8,128)S(1)}, f32[512,128]{1,0:T(8,128)S(1)}, u32[]{:S(2)}, u32[]{:S(2)}) collective-permute-start(f32[512,128]{1,0:T(8,128)S(1)} %copy-done.2), channel_id=1, source_target_pairs={{0,12},{4,8},{8,4},{12,0},{16,28},{20,24},{24,20},{28,16},{1,13},{... | collective-permute-start | bytes 786440 | tf_op jit(solution)/shard_map/ppermute | solution.py:455
  37.6 1.7 %shard_map.90 = (f32[4,128]{1,0:T(4,128)S(1)}, f32[8,128]{1,0:T(8,128)S(1)}, f32[1,128]{1,0:T(1,128)S(1)}, f32[32,128]{1,0:T(8,128)S(1)}) custom-call(f32[1024,4096]{1,0:T(8,128)S(1)} %get-tuple-element.47.rinv_ref, f32[512,1024]{1,0:T(8,128)S(1)} %copy-done, f32[1,128]{1,0:T(1,128)S(1)} %get-tuple-element.59.token_ref, f32[32,128]{1,0:T(8,128)S(1)} %add.6.refs_0_, ...), custom_call_target="tpu_custom_call" | custom-call | tf_op jit(solution)/shard_map/pallas_call | solution.py:59
  39.4 1.1 %collective-permute-done.7 = f32[4,128]{1,0:T(4,128)S(1)} collective-permute-done((f32[4,128]{1,0:T(4,128)S(1)}, f32[4,128]{1,0:T(4,128)S(1)}, u32[]{:S(2)}, u32[]{:S(2)}) %collective-permute-start.7) | collective-permute-done | bytes 2080 | tf_op jit(solution)/shard_map/ppermute | solution.py:31
  40.6 1.5 %collective-permute-start.8 = (f32[4,128]{1,0:T(4,128)S(1)}, f32[4,128]{1,0:T(4,128)S(1)}, u32[]{:S(2)}, u32[]{:S(2)}) collective-permute-start(f32[4,128]{1,0:T(4,128)S(1)} %add.7.refs_0_), channel_id=1, source_target_pairs={{0,2},{1,3},{2,0},{3,1},{4,6},{5,7},{6,4},{7,5},{8,10},{9,11},{10,... | collective-permute-start | bytes 6152 | tf_op jit(solution)/shard_map/ppermute | solution.py:31
  42.1 2.1 %collective-permute-done.8.refs_1_ = f32[4,128]{1,0:T(4,128)S(1)} collective-permute-done((f32[4,128]{1,0:T(4,128)S(1)}, f32[4,128]{1,0:T(4,128)S(1)}, u32[]{:S(2)}, u32[]{:S(2)}) %collective-permute-start.8) | collective-permute-done | bytes 2080 | tf_op jit(solution)/shard_map/ppermute | solution.py:31
  44.4 9.6 %all_to_all.15.order_ref.parts_ref = f32[8,16,128]{2,1,0:T(8,128)S(1)} all-to-all(f32[8,16,128]{2,1,0:T(8,128)S(1)} %get-tuple-element.63), channel_id=1, replica_groups=mesh['row'=8,'col'=4] {'row'}, dimensions={0} | all-to-all | bytes 131072 | tf_op jit(solution)/shard_map/all_to_all | solution.py:24
  54.1 1.1 %shard_map.93 = (f32[1,4,128,128]{3,2,1,0:T(8,128)S(1)}, f32[1,4,128,128]{3,2,1,0:T(8,128)S(1)}, f32[1,128]{1,0:T(1,128)S(1)}) custom-call(f32[512,1024]{1,0:T(8,128)S(1)} %copy-done, f32[8,16,128]{2,1,0:T(8,128)S(1)} %all-to-all-done.parts_ref, bf16[8,128,512]{2,1,0:T(8,128)(2,1)S(1)} %get-tuple-element.48.mix_ref, ...), custom_call_target="tpu_custom_call" | custom-call | tf_op jit(solution)/shard_map/pallas_call | solution.py:59
  55.7 1.4 %shard_map.94 = (f32[32,128]{1,0:T(8,128)S(1)}, f32[1,128]{1,0:T(1,128)S(1)}) custom-call(f32[1024,4096]{1,0:T(8,128)S(1)} %get-tuple-element.47.rinv_ref, f32[8,16,128]{2,1,0:T(8,128)S(1)} %all_to_all.15.order_ref.parts_ref), custom_call_target="tpu_custom_call" | custom-call | tf_op jit(solution)/shard_map/pallas_call | solution.py:495
  57.2 1.6 %collective-permute-start.12 = (f32[32,128]{1,0:T(8,128)S(1)}, f32[32,128]{1,0:T(8,128)S(1)}, u32[]{:S(2)}, u32[]{:S(2)}) collective-permute-start(f32[32,128]{1,0:T(8,128)S(1)} %get-tuple-element.69.refs_0_), channel_id=1, source_target_pairs={{0,2},{1,3},{2,0},{3,1},{4,6},{5,7},{6,4},{7,5},{8,10},{9,11},{10,... | collective-permute-start | bytes 49160 | tf_op jit(solution)/shard_map/ppermute | solution.py:41
  59.1 1.4 %collective-permute-done.13.refs_3_ = f32[32,128]{1,0:T(8,128)S(1)} collective-permute-done((f32[32,128]{1,0:T(8,128)S(1)}, f32[32,128]{1,0:T(8,128)S(1)}, u32[]{:S(2)}, u32[]{:S(2)}) %collective-permute-start.13) | collective-permute-done | bytes 16416 | tf_op jit(solution)/shard_map/ppermute | solution.py:41
  61.0 1.7 %shard_map.95 = (f32[4,128]{1,0:T(4,128)S(1)}, f32[8,128]{1,0:T(8,128)S(1)}, f32[1,128]{1,0:T(1,128)S(1)}) custom-call(f32[1024,4096]{1,0:T(8,128)S(1)} %get-tuple-element.47.rinv_ref, f32[512,1024]{1,0:T(8,128)S(1)} %copy-done, f32[1,128]{1,0:T(1,128)S(1)} %get-tuple-element.68.token_ref, f32[32,128]{1,0:T(8,128)S(1)} %get-tuple-element.69.refs_0_, ...), custom_call_target="tpu_custom_call" | custom-call | tf_op jit(solution)/shard_map/pallas_call | solution.py:59
  63.4 1.5 %collective-permute-start.15 = (f32[4,128]{1,0:T(4,128)S(1)}, f32[4,128]{1,0:T(4,128)S(1)}, u32[]{:S(2)}, u32[]{:S(2)}) collective-permute-start(f32[4,128]{1,0:T(4,128)S(1)} %get-tuple-element.72.refs_0_), channel_id=1, source_target_pairs={{0,2},{1,3},{2,0},{3,1},{4,6},{5,7},{6,4},{7,5},{8,10},{9,11},{10,... | collective-permute-start | bytes 6152 | tf_op jit(solution)/shard_map/ppermute | solution.py:41
  64.8 1.0 %collective-permute-done.16.refs_3_ = f32[4,128]{1,0:T(4,128)S(1)} collective-permute-done((f32[4,128]{1,0:T(4,128)S(1)}, f32[4,128]{1,0:T(4,128)S(1)}, u32[]{:S(2)}, u32[]{:S(2)}) %collective-permute-start.16) | collective-permute-done | bytes 2080 | tf_op jit(solution)/shard_map/ppermute | solution.py:41
  65.9 1.1 %collective-permute-done.15.refs_2_ = f32[4,128]{1,0:T(4,128)S(1)} collective-permute-done((f32[4,128]{1,0:T(4,128)S(1)}, f32[4,128]{1,0:T(4,128)S(1)}, u32[]{:S(2)}, u32[]{:S(2)}) %collective-permute-start.15) | collective-permute-done | bytes 2080 | tf_op jit(solution)/shard_map/ppermute | solution.py:41
  67.6 0.9 %collective-permute-start.18 = (f32[128,256]{1,0:T(8,128)S(1)}, f32[128,256]{1,0:T(8,128)S(1)}, u32[]{:S(2)}, u32[]{:S(2)}) collective-permute-start(f32[128,256]{1,0:T(8,128)S(1)} %get-tuple-element.83), channel_id=1, source_target_pairs={{0,4},{4,0},{8,12},{12,8},{16,20},{20,16},{24,28},{28,24},{1,5},{5... | collective-permute-start | bytes 393224 | tf_op jit(solution)/shard_map/ppermute | solution.py:455
  68.9 2.2 %collective-permute-start.20 = (f32[128,256]{1,0:T(8,128)S(1)}, f32[128,256]{1,0:T(8,128)S(1)}, u32[]{:S(2)}, u32[]{:S(2)}) collective-permute-start(f32[128,256]{1,0:T(8,128)S(1)} %get-tuple-element.85), channel_id=1, source_target_pairs={{0,12},{4,8},{8,4},{12,0},{16,28},{20,24},{24,20},{28,16},{1,13},{... | collective-permute-start | bytes 393224 | tf_op jit(solution)/shard_map/ppermute | solution.py:455
  71.1 9.9 %all_to_all.16.parts_ref = f32[8,8,128]{2,1,0:T(8,128)S(1)} all-to-all(f32[8,8,128]{2,1,0:T(8,128)S(1)} %get-tuple-element.75), channel_id=1, replica_groups=mesh['row'=8,'col'=4] {'row'}, dimensions={0} | all-to-all | bytes 65536 | tf_op jit(solution)/shard_map/all_to_all | solution.py:24
  81.1 0.9 %shard_map.98 = (f32[4,128]{1,0:T(4,128)}, f32[8,128]{1,0:T(8,128)}, f32[128,1024]{1,0:T(8,128)}) custom-call(f32[8,8,128]{2,1,0:T(8,128)S(1)} %all_to_all.16.parts_ref, f32[4,128]{1,0:T(4,128)S(1)} %get-tuple-element.76.refs_3_.left_ref, f32[1,128]{1,0:T(1,128)S(1)} %get-tuple-element.54.refs_2_.refs_3_.refs_0_, ...), custom_call_target="tpu_custom_call" | custom-call | tf_op jit(solution)/shard_map/pallas_call | solution.py:59
  (38 shorter events, 3.6 us)
Async XLA Ops:
  0.6 32.2 %copy-start = (f32[512,1024]{1,0:T(8,128)S(1)}, f32[512,1024]{1,0:T(8,128)}, u32[]{:S(2)}) copy-start(f32[512,1024]{1,0:T(8,128)} %design_ref.9) | copy-start | bytes 6291460
  4.0 25.1 %copy-start.3 = (f32[512,128]{1,0:T(8,128)S(1)}, f32[512,128]{1,0:T(8,128)}, u32[]{:S(2)}) copy-start(f32[512,128]{1,0:T(8,128)} %get-tuple-element.65) | copy-start | bytes 786436
  4.0 32.1 %copy-start.2 = (f32[512,128]{1,0:T(8,128)S(1)}, f32[512,128]{1,0:T(8,128)}, u32[]{:S(2)}) copy-start(f32[512,128]{1,0:T(8,128)} %get-tuple-element.67) | copy-start | bytes 786436
  4.0 14.8 %all-to-all-start = ((f32[8,16,128]{2,1,0:T(8,128)}), f32[8,16,128]{2,1,0:T(8,128)S(1)}, u32[]{:S(2)}, u32[]{:S(2)}) async-start(f32[8,16,128]{2,1,0:T(8,128)} %get-tuple-element.46), calls=%async_computation | async-start | bytes 131072 | tf_op jit(solution)/shard_map/all_to_all | solution.py:24
  11.5 14.9 %collective-permute-start.2 = (f32[512,128]{1,0:T(8,128)}, f32[512,128]{1,0:T(8,128)S(1)}, u32[]{:S(2)}, u32[]{:S(2)}) collective-permute-start(f32[512,128]{1,0:T(8,128)} %get-tuple-element.55), channel_id=1, source_target_pairs={{0,4},{4,0},{8,12},{12,8},{16,20},{20,16},{24,28},{28,24},{1,5},{5... | collective-permute-start | bytes 786440 | tf_op jit(solution)/shard_map/ppermute | solution.py:455
  13.5 12.9 %collective-permute-start.3 = (f32[512,128]{1,0:T(8,128)}, f32[512,128]{1,0:T(8,128)S(1)}, u32[]{:S(2)}, u32[]{:S(2)}) collective-permute-start(f32[512,128]{1,0:T(8,128)} %get-tuple-element.56), channel_id=1, source_target_pairs={{0,8},{4,12},{8,0},{12,4},{16,24},{20,28},{24,16},{28,20},{1,9},{5... | collective-permute-start | bytes 786440 | tf_op jit(solution)/shard_map/ppermute | solution.py:455
  18.8 25.4 %copy-start.1 = (f32[512]{0:T(512)S(1)}, f32[512]{0:T(512)}, u32[]{:S(2)}) copy-start(f32[512]{0:T(512)} %param.10) | copy-start | bytes 6148
  18.8 12.2 %collective-permute-start = (f32[512,128]{1,0:T(8,128)}, f32[512,128]{1,0:T(8,128)S(1)}, u32[]{:S(2)}, u32[]{:S(2)}) collective-permute-start(f32[512,128]{1,0:T(8,128)} %get-tuple-element.52), channel_id=1, source_target_pairs={{0,12},{4,8},{8,4},{12,0},{16,28},{20,24},{24,20},{28,16},{1,13},{... | collective-permute-start | bytes 786440 | tf_op jit(solution)/shard_map/ppermute | solution.py:455
  19.5 13.3 %collective-permute-start.1 = (f32[512,128]{1,0:T(8,128)}, f32[512,128]{1,0:T(8,128)S(1)}, u32[]{:S(2)}, u32[]{:S(2)}) collective-permute-start(f32[512,128]{1,0:T(8,128)} %get-tuple-element.53), channel_id=1, source_target_pairs={{0,8},{4,12},{8,0},{12,4},{16,24},{20,28},{24,16},{28,20},{1,9},{5... | collective-permute-start | bytes 786440 | tf_op jit(solution)/shard_map/ppermute | solution.py:455
  26.4 1.2 %collective-permute-start.5 = (f32[32,128]{1,0:T(8,128)S(1)}, f32[32,128]{1,0:T(8,128)S(1)}, u32[]{:S(2)}, u32[]{:S(2)}) collective-permute-start(f32[32,128]{1,0:T(8,128)S(1)} %shard_map.89), channel_id=1, source_target_pairs={{0,1},{1,0},{2,3},{3,2},{4,5},{5,4},{6,7},{7,6},{8,9},{9,8},{10,11... | collective-permute-start | bytes 49160 | tf_op jit(solution)/shard_map/ppermute | solution.py:31
  27.6 8.5 %collective-permute-start.6 = (f32[32,128]{1,0:T(8,128)S(1)}, f32[32,128]{1,0:T(8,128)S(1)}, u32[]{:S(2)}, u32[]{:S(2)}) collective-permute-start(f32[32,128]{1,0:T(8,128)S(1)} %add.6.refs_0_), channel_id=1, source_target_pairs={{0,2},{1,3},{2,0},{3,1},{4,6},{5,7},{6,4},{7,5},{8,10},{9,11},{10,... | collective-permute-start | bytes 49160 | tf_op jit(solution)/shard_map/ppermute | solution.py:31
  29.1 24.9 %collective-permute-start.9 = (f32[512,128]{1,0:T(8,128)S(1)}, f32[512,128]{1,0:T(8,128)S(1)}, u32[]{:S(2)}, u32[]{:S(2)}) collective-permute-start(f32[512,128]{1,0:T(8,128)S(1)} %copy-done.3), channel_id=1, source_target_pairs={{0,4},{4,0},{8,12},{12,8},{16,20},{20,16},{24,28},{28,24},{1,5},{5... | collective-permute-start | bytes 786440 | tf_op jit(solution)/shard_map/ppermute | solution.py:455
  33.9 20.1 %collective-permute-start.4 = (f32[1,4,128,128]{3,2,1,0:T(8,128)S(1)}, f32[1,4,128,128]{3,2,1,0:T(8,128)S(1)}, u32[]{:S(2)}, u32[]{:S(2)}) collective-permute-start(f32[1,4,128,128]{3,2,1,0:T(8,128)S(1)} %get-tuple-element.58), channel_id=1, source_target_pairs={{0,16},{4,20},{8,24},{12,28},{16,0},{20,4},{24,8},{28,12},{1,17},{... | collective-permute-start | bytes 786440 | tf_op jit(solution)/shard_map/ppermute | solution.py:455
  36.2 17.9 %collective-permute-start.10 = (f32[512,128]{1,0:T(8,128)S(1)}, f32[512,128]{1,0:T(8,128)S(1)}, u32[]{:S(2)}, u32[]{:S(2)}) collective-permute-start(f32[512,128]{1,0:T(8,128)S(1)} %copy-done.2), channel_id=1, source_target_pairs={{0,12},{4,8},{8,4},{12,0},{16,28},{20,24},{24,20},{28,16},{1,13},{... | collective-permute-start | bytes 786440 | tf_op jit(solution)/shard_map/ppermute | solution.py:455
  39.4 1.2 %collective-permute-start.7 = (f32[4,128]{1,0:T(4,128)S(1)}, f32[4,128]{1,0:T(4,128)S(1)}, u32[]{:S(2)}, u32[]{:S(2)}) collective-permute-start(f32[4,128]{1,0:T(4,128)S(1)} %get-tuple-element.61), channel_id=1, source_target_pairs={{0,1},{1,0},{2,3},{3,2},{4,5},{5,4},{6,7},{7,6},{8,9},{9,8},{10,11... | collective-permute-start | bytes 6152 | tf_op jit(solution)/shard_map/ppermute | solution.py:31
  40.6 3.6 %collective-permute-start.8 = (f32[4,128]{1,0:T(4,128)S(1)}, f32[4,128]{1,0:T(4,128)S(1)}, u32[]{:S(2)}, u32[]{:S(2)}) collective-permute-start(f32[4,128]{1,0:T(4,128)S(1)} %add.7.refs_0_), channel_id=1, source_target_pairs={{0,2},{1,3},{2,0},{3,1},{4,6},{5,7},{6,4},{7,5},{8,10},{9,11},{10,... | collective-permute-start | bytes 6152 | tf_op jit(solution)/shard_map/ppermute | solution.py:31
  55.2 12.3 %collective-permute-start.17 = (f32[1,4,128,128]{3,2,1,0:T(8,128)S(1)}, f32[1,4,128,128]{3,2,1,0:T(8,128)S(1)}, u32[]{:S(2)}, u32[]{:S(2)}) collective-permute-start(f32[1,4,128,128]{3,2,1,0:T(8,128)S(1)} %get-tuple-element.81), channel_id=1, source_target_pairs={{0,16},{4,20},{8,24},{12,28},{16,0},{20,4},{24,8},{28,12},{1,17},{... | collective-permute-start | bytes 786440 | tf_op jit(solution)/shard_map/ppermute | solution.py:455
  57.1 3.4 %collective-permute-start.13 = (f32[32,128]{1,0:T(8,128)S(1)}, f32[32,128]{1,0:T(8,128)S(1)}, u32[]{:S(2)}, u32[]{:S(2)}) collective-permute-start(f32[32,128]{1,0:T(8,128)S(1)} %get-tuple-element.69.refs_0_), channel_id=1, source_target_pairs={{0,3},{1,2},{2,1},{3,0},{4,7},{5,6},{6,5},{7,4},{8,11},{9,10},{10,... | collective-permute-start | bytes 49160 | tf_op jit(solution)/shard_map/ppermute | solution.py:41
  57.2 3.8 %collective-permute-start.12 = (f32[32,128]{1,0:T(8,128)S(1)}, f32[32,128]{1,0:T(8,128)S(1)}, u32[]{:S(2)}, u32[]{:S(2)}) collective-permute-start(f32[32,128]{1,0:T(8,128)S(1)} %get-tuple-element.69.refs_0_), channel_id=1, source_target_pairs={{0,2},{1,3},{2,0},{3,1},{4,6},{5,7},{6,4},{7,5},{8,10},{9,11},{10,... | collective-permute-start | bytes 49160 | tf_op jit(solution)/shard_map/ppermute | solution.py:41
  58.8 2.3 %collective-permute-start.11 = (f32[32,128]{1,0:T(8,128)S(1)}, f32[32,128]{1,0:T(8,128)S(1)}, u32[]{:S(2)}, u32[]{:S(2)}) collective-permute-start(f32[32,128]{1,0:T(8,128)S(1)} %get-tuple-element.69.refs_0_), channel_id=1, source_target_pairs={{0,1},{1,0},{2,3},{3,2},{4,5},{5,4},{6,7},{7,6},{8,9},{9,8},{10,11... | collective-permute-start | bytes 49160 | tf_op jit(solution)/shard_map/ppermute | solution.py:41
  62.8 3.1 %collective-permute-start.16 = (f32[4,128]{1,0:T(4,128)S(1)}, f32[4,128]{1,0:T(4,128)S(1)}, u32[]{:S(2)}, u32[]{:S(2)}) collective-permute-start(f32[4,128]{1,0:T(4,128)S(1)} %get-tuple-element.72.refs_0_), channel_id=1, source_target_pairs={{0,3},{1,2},{2,1},{3,0},{4,7},{5,6},{6,5},{7,4},{8,11},{9,10},{10,... | collective-permute-start | bytes 6152 | tf_op jit(solution)/shard_map/ppermute | solution.py:41
  63.4 3.6 %collective-permute-start.15 = (f32[4,128]{1,0:T(4,128)S(1)}, f32[4,128]{1,0:T(4,128)S(1)}, u32[]{:S(2)}, u32[]{:S(2)}) collective-permute-start(f32[4,128]{1,0:T(4,128)S(1)} %get-tuple-element.72.refs_0_), channel_id=1, source_target_pairs={{0,2},{1,3},{2,0},{3,1},{4,6},{5,7},{6,4},{7,5},{8,10},{9,11},{10,... | collective-permute-start | bytes 6152 | tf_op jit(solution)/shard_map/ppermute | solution.py:41
  64.8 2.1 %collective-permute-start.14 = (f32[4,128]{1,0:T(4,128)S(1)}, f32[4,128]{1,0:T(4,128)S(1)}, u32[]{:S(2)}, u32[]{:S(2)}) collective-permute-start(f32[4,128]{1,0:T(4,128)S(1)} %get-tuple-element.72.refs_0_), channel_id=1, source_target_pairs={{0,1},{1,0},{2,3},{3,2},{4,5},{5,4},{6,7},{7,6},{8,9},{9,8},{10,11... | collective-permute-start | bytes 6152 | tf_op jit(solution)/shard_map/ppermute | solution.py:41
  67.6 13.5 %collective-permute-start.18 = (f32[128,256]{1,0:T(8,128)S(1)}, f32[128,256]{1,0:T(8,128)S(1)}, u32[]{:S(2)}, u32[]{:S(2)}) collective-permute-start(f32[128,256]{1,0:T(8,128)S(1)} %get-tuple-element.83), channel_id=1, source_target_pairs={{0,4},{4,0},{8,12},{12,8},{16,20},{20,16},{24,28},{28,24},{1,5},{5... | collective-permute-start | bytes 393224 | tf_op jit(solution)/shard_map/ppermute | solution.py:455
  68.5 12.6 %collective-permute-start.19 = (f32[128,256]{1,0:T(8,128)S(1)}, f32[128,256]{1,0:T(8,128)S(1)}, u32[]{:S(2)}, u32[]{:S(2)}) collective-permute-start(f32[128,256]{1,0:T(8,128)S(1)} %get-tuple-element.84), channel_id=1, source_target_pairs={{0,8},{4,12},{8,0},{12,4},{16,24},{20,28},{24,16},{28,20},{1,9},{5... | collective-permute-start | bytes 393224 | tf_op jit(solution)/shard_map/ppermute | solution.py:455
  68.9 12.1 %collective-permute-start.20 = (f32[128,256]{1,0:T(8,128)S(1)}, f32[128,256]{1,0:T(8,128)S(1)}, u32[]{:S(2)}, u32[]{:S(2)}) collective-permute-start(f32[128,256]{1,0:T(8,128)S(1)} %get-tuple-element.85), channel_id=1, source_target_pairs={{0,12},{4,8},{8,4},{12,0},{16,28},{20,24},{24,20},{28,16},{1,13},{... | collective-permute-start | bytes 393224 | tf_op jit(solution)/shard_map/ppermute | solution.py:455

commit v23 on v22

--- a/solution.py
+++ b/solution.py
@@ -556,11 +556,13 @@
         terms = direct(term, "col") if spare else paired(term, "col")
         if step == 0:
             near += spread(range(late, len(sent)), terms[1])
-            keep, send, token = sample(0, mixed, after([near[NEAR - 2], *near[NEAR:late]], beta) if chunks > 1 else beta)
+            keep, send, token = sample(0, mixed, beta)
             come = swap(send, row_groups // 2)
         image, kept, alpha, *right = forward(terms, token, last, *right, *betas[1:])
         alphas.append(alpha)
         held.append(kept)
+        if step == 0 and chunks > 1:
+            image = after(near[NEAR:late], image)
         images = direct(image, "col") if spare else paired(image, "col")
         left, message = turn(images, left, beta, alpha, last)
         message = exchange(message, "row")

time: 82.3 us -> 80.6 us (0.979)
  waiting for transfers between devices: 14.7 us -> 13 us
  blocking collectives: 19.5 us -> 21 us
  starting transfers between devices: 29.3 us -> 27.9 us
    ppermute x11, waiting for transfers between devices: 2.32 us -> 0.52 us  [swap(): lax.ppermute(array, 'row', [(i, i ^ mask) for i in range(row_groups)])]
    all_to_all x2, blocking collectives: 19.5 us -> 21 us  [exchange(): return lax.all_to_all(copies, axis, split_axis=0, concat_axis=0, tiled=True)]
    ppermute x11, starting transfers between devices: 14.8 us -> 13.5 us  [swap(): lax.ppermute(array, 'row', [(i, i ^ mask) for i in range(row_groups)])]
  transfers between devices with their start and end apart: 22 -> 22, of which waited for: 10 -> 9; matrix products, arithmetic and copies ran while one was open for 0% -> 0% of each run, Pallas kernels for 15% -> 15%
where the time goes in v23:
time: 80.6 us; the launch traced here: 80.3 us
  starting transfers between devices  27.9 us (35%)
  blocking collectives  21 us (26%)
  Pallas kernels  17.6 us (22%)
  waiting for transfers between devices  13 us (16%)
  between operations  0.81 us (1%)
    all_to_all x2, blocking collectives, exchange(): return lax.all_to_all(copies, axis, split_axis=0, concat_axis=0, tiled=True)  21 us
    ppermute x11, starting transfers between devices, swap(): lax.ppermute(array, 'row', [(i, i ^ mask) for i in range(row_groups)])  13.5 us
    all_to_all x1, starting transfers between devices, exchange(): return lax.all_to_all(copies, axis, split_axis=0, concat_axis=0, tiled=True)  7.42 us
    pallas_call x2, Pallas kernels, back(): pl.pallas_call(functools.partial(back_body, first), out_shape=outs, in_sp...  7.28 us
    pallas_call x9, Pallas kernels, call(): pl.pallas_call(body, out_shape=out_shape, in_specs=[VMEM] * len(operands)...  6.97 us
    ppermute x4, waiting for transfers between devices, paired(): come = lax.ppermute(array, axis, [(i, i ^ mask) for i in range(size)])  4.41 us
    ppermute x6, waiting for transfers between devices, direct(): lax.ppermute(array, axis, [(i, i ^ mask) for i in range(size)])  4.2 us
    ppermute x6, starting transfers between devices, direct(): lax.ppermute(array, axis, [(i, i ^ mask) for i in range(size)])  3.85 us
  transfers between devices with their start and end apart: 22, of which 9 were waited for; matrix products, arithmetic and copies ran while one was open for 0% of the time, Pallas kernels for 15%

profile of v23, /device:TPU:0, one launch (start us, length us, event | category | flops | bytes accessed | tf_op | source)
XLA Modules:
  0.0 80.3 jit_solution(13859260034518172147)
XLA Ops:
  0.6 3.4 %shard_map.85 = (f32[8,16,128]{2,1,0:T(8,128)}, f32[512,128]{1,0:T(8,128)}, f32[512,128]{1,0:T(8,128)}, f32[512,128]{1,0:T(8,128)}, f32[512,128]{1,0:T(8,128)}, /*index=5*/f32[512,128]{1,0:T(8,128)}, f32[512,128]{1,0:T(8,128)}) custom-call(f32[512,1024]{1,0:T(8,128)} %design_ref.9, f32[4,128]{1,0:T(4,128)} %bitcast.6, s32[4,128]{1,0:T(4,128)} %bitcast.9, ...), custom_call_target="tpu_custom_call" | custom-call | tf_op jit(solution)/shard_map/pallas_call | solution.py:437
  4.0 7.4 %all-to-all-start = ((f32[8,16,128]{2,1,0:T(8,128)}), f32[8,16,128]{2,1,0:T(8,128)S(1)}, u32[]{:S(2)}, u32[]{:S(2)}) async-start(f32[8,16,128]{2,1,0:T(8,128)} %get-tuple-element.46), calls=%async_computation | async-start | bytes 131072 | tf_op jit(solution)/shard_map/all_to_all | solution.py:24
  11.5 2.0 %collective-permute-start = (f32[512,128]{1,0:T(8,128)}, f32[512,128]{1,0:T(8,128)S(1)}, u32[]{:S(2)}, u32[]{:S(2)}) collective-permute-start(f32[512,128]{1,0:T(8,128)} %get-tuple-element.50), channel_id=1, source_target_pairs={{0,4},{4,0},{8,12},{12,8},{16,20},{20,16},{24,28},{28,24},{1,5},{5... | collective-permute-start | bytes 786440 | tf_op jit(solution)/shard_map/ppermute | solution.py:455
  13.5 1.5 %collective-permute-start.1 = (f32[512,128]{1,0:T(8,128)}, f32[512,128]{1,0:T(8,128)S(1)}, u32[]{:S(2)}, u32[]{:S(2)}) collective-permute-start(f32[512,128]{1,0:T(8,128)} %get-tuple-element.51), channel_id=1, source_target_pairs={{0,8},{4,12},{8,0},{12,4},{16,24},{20,28},{24,16},{28,20},{1,9},{5... | collective-permute-start | bytes 786440 | tf_op jit(solution)/shard_map/ppermute | solution.py:455
  15.0 3.8 %all-to-all-done.parts_ref = f32[8,16,128]{2,1,0:T(8,128)S(1)} async-done(((f32[8,16,128]{2,1,0:T(8,128)}), f32[8,16,128]{2,1,0:T(8,128)S(1)}, u32[]{:S(2)}, u32[]{:S(2)}) %all-to-all-start) | async-done | bytes 65568 | tf_op jit(solution)/shard_map/all_to_all | solution.py:24
  18.8 0.7 collective-permute-start.2
  19.5 0.9 %collective-permute-start.4 = (f32[512,128]{1,0:T(8,128)}, f32[512,128]{1,0:T(8,128)S(1)}, u32[]{:S(2)}, u32[]{:S(2)}) collective-permute-start(f32[512,128]{1,0:T(8,128)} %get-tuple-element.58), channel_id=1, source_target_pairs={{0,8},{4,12},{8,0},{12,4},{16,24},{20,28},{24,16},{28,20},{1,9},{5... | collective-permute-start | bytes 786440 | tf_op jit(solution)/shard_map/ppermute | solution.py:455
  20.5 5.9 %shard_map.86 = (f32[32,128]{1,0:T(8,128)S(1)}, f32[1,128]{1,0:T(1,128)S(1)}, bf16[8,128,512]{2,1,0:T(8,128)(2,1)S(1)}, f32[1024,4096]{1,0:T(8,128)S(1)}) custom-call(f32[1024,4096]{1,0:T(8,128)} %rinv_ref.1, f32[8,16,128]{2,1,0:T(8,128)S(1)} %all-to-all-done.parts_ref), custom_call_target="tpu_custom_call" | custom-call | tf_op jit(solution)/shard_map/pallas_call | solution.py:495
  26.5 1.2 %collective-permute-done.5 = f32[32,128]{1,0:T(8,128)S(1)} collective-permute-done((f32[32,128]{1,0:T(8,128)S(1)}, f32[32,128]{1,0:T(8,128)S(1)}, u32[]{:S(2)}, u32[]{:S(2)}) %collective-permute-start.5) | collective-permute-done | bytes 16416 | tf_op jit(solution)/shard_map/ppermute | solution.py:31
  27.6 1.5 %collective-permute-start.6 = (f32[32,128]{1,0:T(8,128)S(1)}, f32[32,128]{1,0:T(8,128)S(1)}, u32[]{:S(2)}, u32[]{:S(2)}) collective-permute-start(f32[32,128]{1,0:T(8,128)S(1)} %add.6.refs_0_), channel_id=1, source_target_pairs={{0,2},{1,3},{2,0},{3,1},{4,6},{5,7},{6,4},{7,5},{8,10},{9,11},{10,... | collective-permute-start | bytes 49160 | tf_op jit(solution)/shard_map/ppermute | solution.py:31
  29.1 1.8 %collective-permute-start.9 = (f32[512,128]{1,0:T(8,128)S(1)}, f32[512,128]{1,0:T(8,128)S(1)}, u32[]{:S(2)}, u32[]{:S(2)}) collective-permute-start(f32[512,128]{1,0:T(8,128)S(1)} %copy-done.3), channel_id=1, source_target_pairs={{0,4},{4,0},{8,12},{12,8},{16,20},{20,16},{24,28},{28,24},{1,5},{5... | collective-permute-start | bytes 786440 | tf_op jit(solution)/shard_map/ppermute | solution.py:455
  31.0 1.1 %shard_map.87 = (f32[1,4,128,128]{3,2,1,0:T(8,128)S(1)}, f32[1,4,128,128]{3,2,1,0:T(8,128)S(1)}, f32[1,128]{1,0:T(1,128)S(1)}) custom-call(f32[512,1024]{1,0:T(8,128)S(1)} %copy-done, f32[8,16,128]{2,1,0:T(8,128)S(1)} %all-to-all-done.parts_ref, bf16[8,128,512]{2,1,0:T(8,128)(2,1)S(1)} %get-tuple-element.48.mix_ref, ...), custom_call_target="tpu_custom_call" | custom-call | tf_op jit(solution)/shard_map/pallas_call | solution.py:59
  32.5 2.0 %collective-permute-start.10 = (f32[512,128]{1,0:T(8,128)S(1)}, f32[512,128]{1,0:T(8,128)S(1)}, u32[]{:S(2)}, u32[]{:S(2)}) collective-permute-start(f32[512,128]{1,0:T(8,128)S(1)} %copy-done.2), channel_id=1, source_target_pairs={{0,12},{4,8},{8,4},{12,0},{16,28},{20,24},{24,20},{28,16},{1,13},{... | collective-permute-start | bytes 786440 | tf_op jit(solution)/shard_map/ppermute | solution.py:455
  34.5 1.7 %shard_map.89 = (f32[4,128]{1,0:T(4,128)S(1)}, f32[8,128]{1,0:T(8,128)S(1)}, f32[1,128]{1,0:T(1,128)S(1)}, f32[32,128]{1,0:T(8,128)S(1)}) custom-call(f32[1024,4096]{1,0:T(8,128)S(1)} %get-tuple-element.47.rinv_ref, f32[512,1024]{1,0:T(8,128)S(1)} %copy-done, f32[1,128]{1,0:T(1,128)S(1)} %get-tuple-element.59.token_ref, f32[32,128]{1,0:T(8,128)S(1)} %add.6.refs_0_, ...), custom_call_target="tpu_custom_call" | custom-call | tf_op jit(solution)/shard_map/pallas_call | solution.py:59
  36.3 1.1 %collective-permute-done.7 = f32[4,128]{1,0:T(4,128)S(1)} collective-permute-done((f32[4,128]{1,0:T(4,128)S(1)}, f32[4,128]{1,0:T(4,128)S(1)}, u32[]{:S(2)}, u32[]{:S(2)}) %collective-permute-start.7) | collective-permute-done | bytes 2080 | tf_op jit(solution)/shard_map/ppermute | solution.py:31
  37.4 1.5 %collective-permute-start.8 = (f32[4,128]{1,0:T(4,128)S(1)}, f32[4,128]{1,0:T(4,128)S(1)}, u32[]{:S(2)}, u32[]{:S(2)}) collective-permute-start(f32[4,128]{1,0:T(4,128)S(1)} %add.7.refs_0_), channel_id=1, source_target_pairs={{0,2},{1,3},{2,0},{3,1},{4,6},{5,7},{6,4},{7,5},{8,10},{9,11},{10,... | collective-permute-start | bytes 6152 | tf_op jit(solution)/shard_map/ppermute | solution.py:31
  38.9 2.1 %collective-permute-done.8.refs_1_ = f32[4,128]{1,0:T(4,128)S(1)} collective-permute-done((f32[4,128]{1,0:T(4,128)S(1)}, f32[4,128]{1,0:T(4,128)S(1)}, u32[]{:S(2)}, u32[]{:S(2)}) %collective-permute-start.8) | collective-permute-done | bytes 2080 | tf_op jit(solution)/shard_map/ppermute | solution.py:31
  41.3 10.9 %all_to_all.15.order_ref.parts_ref = f32[8,16,128]{2,1,0:T(8,128)S(1)} all-to-all(f32[8,16,128]{2,1,0:T(8,128)S(1)} %get-tuple-element.63), channel_id=1, replica_groups=mesh['row'=8,'col'=4] {'row'}, dimensions={0} | all-to-all | bytes 131072 | tf_op jit(solution)/shard_map/all_to_all | solution.py:24
  52.2 1.1 %shard_map.93 = (f32[1,4,128,128]{3,2,1,0:T(8,128)S(1)}, f32[1,4,128,128]{3,2,1,0:T(8,128)S(1)}, f32[1,128]{1,0:T(1,128)S(1)}) custom-call(f32[512,1024]{1,0:T(8,128)S(1)} %copy-done, f32[8,16,128]{2,1,0:T(8,128)S(1)} %all-to-all-done.parts_ref, bf16[8,128,512]{2,1,0:T(8,128)(2,1)S(1)} %get-tuple-element.48.mix_ref, ...), custom_call_target="tpu_custom_call" | custom-call | tf_op jit(solution)/shard_map/pallas_call | solution.py:59
  53.9 1.4 %shard_map.94 = (f32[32,128]{1,0:T(8,128)S(1)}, f32[1,128]{1,0:T(1,128)S(1)}) custom-call(f32[1024,4096]{1,0:T(8,128)S(1)} %get-tuple-element.47.rinv_ref, f32[8,16,128]{2,1,0:T(8,128)S(1)} %all_to_all.15.order_ref.parts_ref), custom_call_target="tpu_custom_call" | custom-call | tf_op jit(solution)/shard_map/pallas_call | solution.py:495
  55.4 0.6 collective-permute-start.12
  56.0 1.2 %collective-permute-start.11 = (f32[32,128]{1,0:T(8,128)S(1)}, f32[32,128]{1,0:T(8,128)S(1)}, u32[]{:S(2)}, u32[]{:S(2)}) collective-permute-start(f32[32,128]{1,0:T(8,128)S(1)} %get-tuple-element.69.refs_0_), channel_id=1, source_target_pairs={{0,1},{1,0},{2,3},{3,2},{4,5},{5,4},{6,7},{7,6},{8,9},{9,8},{10,11... | collective-permute-start | bytes 49160 | tf_op jit(solution)/shard_map/ppermute | solution.py:41
  57.3 1.3 %collective-permute-done.13.refs_3_ = f32[32,128]{1,0:T(8,128)S(1)} collective-permute-done((f32[32,128]{1,0:T(8,128)S(1)}, f32[32,128]{1,0:T(8,128)S(1)}, u32[]{:S(2)}, u32[]{:S(2)}) %collective-permute-start.13) | collective-permute-done | bytes 16416 | tf_op jit(solution)/shard_map/ppermute | solution.py:41
  58.6 0.7 collective-permute-done.12.refs_2_
  59.2 1.7 %shard_map.95 = (f32[4,128]{1,0:T(4,128)S(1)}, f32[8,128]{1,0:T(8,128)S(1)}, f32[1,128]{1,0:T(1,128)S(1)}) custom-call(f32[1024,4096]{1,0:T(8,128)S(1)} %get-tuple-element.47.rinv_ref, f32[512,1024]{1,0:T(8,128)S(1)} %copy-done, f32[1,128]{1,0:T(1,128)S(1)} %get-tuple-element.68.token_ref, f32[32,128]{1,0:T(8,128)S(1)} %get-tuple-element.69.refs_0_, ...), custom_call_target="tpu_custom_call" | custom-call | tf_op jit(solution)/shard_map/pallas_call | solution.py:59
  62.1 0.8 collective-permute-start.14
  62.9 1.1 %collective-permute-done.16.refs_3_ = f32[4,128]{1,0:T(4,128)S(1)} collective-permute-done((f32[4,128]{1,0:T(4,128)S(1)}, f32[4,128]{1,0:T(4,128)S(1)}, u32[]{:S(2)}, u32[]{:S(2)}) %collective-permute-start.16) | collective-permute-done | bytes 2080 | tf_op jit(solution)/shard_map/ppermute | solution.py:41
  64.0 1.1 %collective-permute-done.15.refs_2_ = f32[4,128]{1,0:T(4,128)S(1)} collective-permute-done((f32[4,128]{1,0:T(4,128)S(1)}, f32[4,128]{1,0:T(4,128)S(1)}, u32[]{:S(2)}, u32[]{:S(2)}) %collective-permute-start.15) | collective-permute-done | bytes 2080 | tf_op jit(solution)/shard_map/ppermute | solution.py:41
  65.7 0.9 %collective-permute-start.18 = (f32[128,256]{1,0:T(8,128)S(1)}, f32[128,256]{1,0:T(8,128)S(1)}, u32[]{:S(2)}, u32[]{:S(2)}) collective-permute-start(f32[128,256]{1,0:T(8,128)S(1)} %get-tuple-element.83), channel_id=1, source_target_pairs={{0,4},{4,0},{8,12},{12,8},{16,20},{20,16},{24,28},{28,24},{1,5},{5... | collective-permute-start | bytes 393224 | tf_op jit(solution)/shard_map/ppermute | solution.py:455
  67.1 2.2 %collective-permute-start.20 = (f32[128,256]{1,0:T(8,128)S(1)}, f32[128,256]{1,0:T(8,128)S(1)}, u32[]{:S(2)}, u32[]{:S(2)}) collective-permute-start(f32[128,256]{1,0:T(8,128)S(1)} %get-tuple-element.85), channel_id=1, source_target_pairs={{0,12},{4,8},{8,4},{12,0},{16,28},{20,24},{24,20},{28,16},{1,13},{... | collective-permute-start | bytes 393224 | tf_op jit(solution)/shard_map/ppermute | solution.py:455
  69.3 10.1 %all_to_all.16.parts_ref = f32[8,8,128]{2,1,0:T(8,128)S(1)} all-to-all(f32[8,8,128]{2,1,0:T(8,128)S(1)} %get-tuple-element.75), channel_id=1, replica_groups=mesh['row'=8,'col'=4] {'row'}, dimensions={0} | all-to-all | bytes 65536 | tf_op jit(solution)/shard_map/all_to_all | solution.py:24
  79.4 0.9 %shard_map.98 = (f32[4,128]{1,0:T(4,128)}, f32[8,128]{1,0:T(8,128)}, f32[128,1024]{1,0:T(8,128)}) custom-call(f32[8,8,128]{2,1,0:T(8,128)S(1)} %all_to_all.16.parts_ref, f32[4,128]{1,0:T(4,128)S(1)} %get-tuple-element.76.refs_3_.left_ref, f32[1,128]{1,0:T(1,128)S(1)} %get-tuple-element.49.order_ref.refs_3_.refs_0_, ...), custom_call_target="tpu_custom_call" | custom-call | tf_op jit(solution)/shard_map/pallas_call | solution.py:59
  (38 shorter events, 3.8 us)
Async XLA Ops:
  0.6 30.3 %copy-start = (f32[512,1024]{1,0:T(8,128)S(1)}, f32[512,1024]{1,0:T(8,128)}, u32[]{:S(2)}) copy-start(f32[512,1024]{1,0:T(8,128)} %design_ref.9) | copy-start | bytes 6291460
  4.0 25.1 %copy-start.3 = (f32[512,128]{1,0:T(8,128)S(1)}, f32[512,128]{1,0:T(8,128)}, u32[]{:S(2)}) copy-start(f32[512,128]{1,0:T(8,128)} %get-tuple-element.65) | copy-start | bytes 786436
  4.0 28.5 %copy-start.2 = (f32[512,128]{1,0:T(8,128)S(1)}, f32[512,128]{1,0:T(8,128)}, u32[]{:S(2)}) copy-start(f32[512,128]{1,0:T(8,128)} %get-tuple-element.67) | copy-start | bytes 786436
  4.0 14.8 %all-to-all-start = ((f32[8,16,128]{2,1,0:T(8,128)}), f32[8,16,128]{2,1,0:T(8,128)S(1)}, u32[]{:S(2)}, u32[]{:S(2)}) async-start(f32[8,16,128]{2,1,0:T(8,128)} %get-tuple-element.46), calls=%async_computation | async-start | bytes 131072 | tf_op jit(solution)/shard_map/all_to_all | solution.py:24
  11.5 14.9 %collective-permute-start = (f32[512,128]{1,0:T(8,128)}, f32[512,128]{1,0:T(8,128)S(1)}, u32[]{:S(2)}, u32[]{:S(2)}) collective-permute-start(f32[512,128]{1,0:T(8,128)} %get-tuple-element.50), channel_id=1, source_target_pairs={{0,4},{4,0},{8,12},{12,8},{16,20},{20,16},{24,28},{28,24},{1,5},{5... | collective-permute-start | bytes 786440 | tf_op jit(solution)/shard_map/ppermute | solution.py:455
  13.5 12.9 %collective-permute-start.1 = (f32[512,128]{1,0:T(8,128)}, f32[512,128]{1,0:T(8,128)S(1)}, u32[]{:S(2)}, u32[]{:S(2)}) collective-permute-start(f32[512,128]{1,0:T(8,128)} %get-tuple-element.51), channel_id=1, source_target_pairs={{0,8},{4,12},{8,0},{12,4},{16,24},{20,28},{24,16},{28,20},{1,9},{5... | collective-permute-start | bytes 786440 | tf_op jit(solution)/shard_map/ppermute | solution.py:455
  18.8 22.2 %copy-start.1 = (f32[512]{0:T(512)S(1)}, f32[512]{0:T(512)}, u32[]{:S(2)}) copy-start(f32[512]{0:T(512)} %param.10) | copy-start | bytes 6148
  18.8 12.2 %collective-permute-start.2 = (f32[512,128]{1,0:T(8,128)}, f32[512,128]{1,0:T(8,128)S(1)}, u32[]{:S(2)}, u32[]{:S(2)}) collective-permute-start(f32[512,128]{1,0:T(8,128)} %get-tuple-element.55), channel_id=1, source_target_pairs={{0,12},{4,8},{8,4},{12,0},{16,28},{20,24},{24,20},{28,16},{1,13},{... | collective-permute-start | bytes 786440 | tf_op jit(solution)/shard_map/ppermute | solution.py:455
  19.5 16.7 %collective-permute-start.4 = (f32[512,128]{1,0:T(8,128)}, f32[512,128]{1,0:T(8,128)S(1)}, u32[]{:S(2)}, u32[]{:S(2)}) collective-permute-start(f32[512,128]{1,0:T(8,128)} %get-tuple-element.58), channel_id=1, source_target_pairs={{0,8},{4,12},{8,0},{12,4},{16,24},{20,28},{24,16},{28,20},{1,9},{5... | collective-permute-start | bytes 786440 | tf_op jit(solution)/shard_map/ppermute | solution.py:455
  26.4 1.2 %collective-permute-start.5 = (f32[32,128]{1,0:T(8,128)S(1)}, f32[32,128]{1,0:T(8,128)S(1)}, u32[]{:S(2)}, u32[]{:S(2)}) collective-permute-start(f32[32,128]{1,0:T(8,128)S(1)} %shard_map.88), channel_id=1, source_target_pairs={{0,1},{1,0},{2,3},{3,2},{4,5},{5,4},{6,7},{7,6},{8,9},{9,8},{10,11... | collective-permute-start | bytes 49160 | tf_op jit(solution)/shard_map/ppermute | solution.py:31
  27.6 4.9 %collective-permute-start.6 = (f32[32,128]{1,0:T(8,128)S(1)}, f32[32,128]{1,0:T(8,128)S(1)}, u32[]{:S(2)}, u32[]{:S(2)}) collective-permute-start(f32[32,128]{1,0:T(8,128)S(1)} %add.6.refs_0_), channel_id=1, source_target_pairs={{0,2},{1,3},{2,0},{3,1},{4,6},{5,7},{6,4},{7,5},{8,10},{9,11},{10,... | collective-permute-start | bytes 49160 | tf_op jit(solution)/shard_map/ppermute | solution.py:31
  29.1 23.1 %collective-permute-start.9 = (f32[512,128]{1,0:T(8,128)S(1)}, f32[512,128]{1,0:T(8,128)S(1)}, u32[]{:S(2)}, u32[]{:S(2)}) collective-permute-start(f32[512,128]{1,0:T(8,128)S(1)} %copy-done.3), channel_id=1, source_target_pairs={{0,4},{4,0},{8,12},{12,8},{16,20},{20,16},{24,28},{28,24},{1,5},{5... | collective-permute-start | bytes 786440 | tf_op jit(solution)/shard_map/ppermute | solution.py:455
  32.1 20.1 %collective-permute-start.3 = (f32[1,4,128,128]{3,2,1,0:T(8,128)S(1)}, f32[1,4,128,128]{3,2,1,0:T(8,128)S(1)}, u32[]{:S(2)}, u32[]{:S(2)}) collective-permute-start(f32[1,4,128,128]{3,2,1,0:T(8,128)S(1)} %get-tuple-element.57), channel_id=1, source_target_pairs={{0,16},{4,20},{8,24},{12,28},{16,0},{20,4},{24,8},{28,12},{1,17},{... | collective-permute-start | bytes 786440 | tf_op jit(solution)/shard_map/ppermute | solution.py:455
  32.5 19.7 %collective-permute-start.10 = (f32[512,128]{1,0:T(8,128)S(1)}, f32[512,128]{1,0:T(8,128)S(1)}, u32[]{:S(2)}, u32[]{:S(2)}) collective-permute-start(f32[512,128]{1,0:T(8,128)S(1)} %copy-done.2), channel_id=1, source_target_pairs={{0,12},{4,8},{8,4},{12,0},{16,28},{20,24},{24,20},{28,16},{1,13},{... | collective-permute-start | bytes 786440 | tf_op jit(solution)/shard_map/ppermute | solution.py:455
  36.2 1.2 %collective-permute-start.7 = (f32[4,128]{1,0:T(4,128)S(1)}, f32[4,128]{1,0:T(4,128)S(1)}, u32[]{:S(2)}, u32[]{:S(2)}) collective-permute-start(f32[4,128]{1,0:T(4,128)S(1)} %shard_map.90), channel_id=1, source_target_pairs={{0,1},{1,0},{2,3},{3,2},{4,5},{5,4},{6,7},{7,6},{8,9},{9,8},{10,11... | collective-permute-start | bytes 6152 | tf_op jit(solution)/shard_map/ppermute | solution.py:31
  37.4 3.6 %collective-permute-start.8 = (f32[4,128]{1,0:T(4,128)S(1)}, f32[4,128]{1,0:T(4,128)S(1)}, u32[]{:S(2)}, u32[]{:S(2)}) collective-permute-start(f32[4,128]{1,0:T(4,128)S(1)} %add.7.refs_0_), channel_id=1, source_target_pairs={{0,2},{1,3},{2,0},{3,1},{4,6},{5,7},{6,4},{7,5},{8,10},{9,11},{10,... | collective-permute-start | bytes 6152 | tf_op jit(solution)/shard_map/ppermute | solution.py:31
  53.4 12.3 %collective-permute-start.17 = (f32[1,4,128,128]{3,2,1,0:T(8,128)S(1)}, f32[1,4,128,128]{3,2,1,0:T(8,128)S(1)}, u32[]{:S(2)}, u32[]{:S(2)}) collective-permute-start(f32[1,4,128,128]{3,2,1,0:T(8,128)S(1)} %get-tuple-element.81), channel_id=1, source_target_pairs={{0,16},{4,20},{8,24},{12,28},{16,0},{20,4},{24,8},{28,12},{1,17},{... | collective-permute-start | bytes 786440 | tf_op jit(solution)/shard_map/ppermute | solution.py:455
  55.3 3.2 %collective-permute-start.13 = (f32[32,128]{1,0:T(8,128)S(1)}, f32[32,128]{1,0:T(8,128)S(1)}, u32[]{:S(2)}, u32[]{:S(2)}) collective-permute-start(f32[32,128]{1,0:T(8,128)S(1)} %get-tuple-element.69.refs_0_), channel_id=1, source_target_pairs={{0,3},{1,2},{2,1},{3,0},{4,7},{5,6},{6,5},{7,4},{8,11},{9,10},{10,... | collective-permute-start | bytes 49160 | tf_op jit(solution)/shard_map/ppermute | solution.py:41
  55.4 3.8 %collective-permute-start.12 = (f32[32,128]{1,0:T(8,128)S(1)}, f32[32,128]{1,0:T(8,128)S(1)}, u32[]{:S(2)}, u32[]{:S(2)}) collective-permute-start(f32[32,128]{1,0:T(8,128)S(1)} %get-tuple-element.69.refs_0_), channel_id=1, source_target_pairs={{0,2},{1,3},{2,0},{3,1},{4,6},{5,7},{6,4},{7,5},{8,10},{9,11},{10,... | collective-permute-start | bytes 49160 | tf_op jit(solution)/shard_map/ppermute | solution.py:41
  56.0 3.2 %collective-permute-start.11 = (f32[32,128]{1,0:T(8,128)S(1)}, f32[32,128]{1,0:T(8,128)S(1)}, u32[]{:S(2)}, u32[]{:S(2)}) collective-permute-start(f32[32,128]{1,0:T(8,128)S(1)} %get-tuple-element.69.refs_0_), channel_id=1, source_target_pairs={{0,1},{1,0},{2,3},{3,2},{4,5},{5,4},{6,7},{7,6},{8,9},{9,8},{10,11... | collective-permute-start | bytes 49160 | tf_op jit(solution)/shard_map/ppermute | solution.py:41
  60.9 3.1 %collective-permute-start.16 = (f32[4,128]{1,0:T(4,128)S(1)}, f32[4,128]{1,0:T(4,128)S(1)}, u32[]{:S(2)}, u32[]{:S(2)}) collective-permute-start(f32[4,128]{1,0:T(4,128)S(1)} %get-tuple-element.72.refs_0_), channel_id=1, source_target_pairs={{0,3},{1,2},{2,1},{3,0},{4,7},{5,6},{6,5},{7,4},{8,11},{9,10},{10,... | collective-permute-start | bytes 6152 | tf_op jit(solution)/shard_map/ppermute | solution.py:41
  61.5 3.6 %collective-permute-start.15 = (f32[4,128]{1,0:T(4,128)S(1)}, f32[4,128]{1,0:T(4,128)S(1)}, u32[]{:S(2)}, u32[]{:S(2)}) collective-permute-start(f32[4,128]{1,0:T(4,128)S(1)} %get-tuple-element.72.refs_0_), channel_id=1, source_target_pairs={{0,2},{1,3},{2,0},{3,1},{4,6},{5,7},{6,4},{7,5},{8,10},{9,11},{10,... | collective-permute-start | bytes 6152 | tf_op jit(solution)/shard_map/ppermute | solution.py:41
  62.1 3.0 %collective-permute-start.14 = (f32[4,128]{1,0:T(4,128)S(1)}, f32[4,128]{1,0:T(4,128)S(1)}, u32[]{:S(2)}, u32[]{:S(2)}) collective-permute-start(f32[4,128]{1,0:T(4,128)S(1)} %get-tuple-element.72.refs_0_), channel_id=1, source_target_pairs={{0,1},{1,0},{2,3},{3,2},{4,5},{5,4},{6,7},{7,6},{8,9},{9,8},{10,11... | collective-permute-start | bytes 6152 | tf_op jit(solution)/shard_map/ppermute | solution.py:41
  65.7 13.7 %collective-permute-start.18 = (f32[128,256]{1,0:T(8,128)S(1)}, f32[128,256]{1,0:T(8,128)S(1)}, u32[]{:S(2)}, u32[]{:S(2)}) collective-permute-start(f32[128,256]{1,0:T(8,128)S(1)} %get-tuple-element.83), channel_id=1, source_target_pairs={{0,4},{4,0},{8,12},{12,8},{16,20},{20,16},{24,28},{28,24},{1,5},{5... | collective-permute-start | bytes 393224 | tf_op jit(solution)/shard_map/ppermute | solution.py:455
  66.7 12.7 %collective-permute-start.19 = (f32[128,256]{1,0:T(8,128)S(1)}, f32[128,256]{1,0:T(8,128)S(1)}, u32[]{:S(2)}, u32[]{:S(2)}) collective-permute-start(f32[128,256]{1,0:T(8,128)S(1)} %get-tuple-element.84), channel_id=1, source_target_pairs={{0,8},{4,12},{8,0},{12,4},{16,24},{20,28},{24,16},{28,20},{1,9},{5... | collective-permute-start | bytes 393224 | tf_op jit(solution)/shard_map/ppermute | solution.py:455
  67.1 12.3 %collective-permute-start.20 = (f32[128,256]{1,0:T(8,128)S(1)}, f32[128,256]{1,0:T(8,128)S(1)}, u32[]{:S(2)}, u32[]{:S(2)}) collective-permute-start(f32[128,256]{1,0:T(8,128)S(1)} %get-tuple-element.85), channel_id=1, source_target_pairs={{0,12},{4,8},{8,4},{12,0},{16,28},{20,24},{24,20},{28,16},{1,13},{... | collective-permute-start | bytes 393224 | tf_op jit(solution)/shard_map/ppermute | solution.py:455
